TPU v7x, 32 devices: a whole 2x2x4 slice. The times are simulated.
32 devices in a mesh: fsdp: 4 (over x, core), seq: 8 (over z, y).
Axes of the slice: x: 2, y: 2, z: 4, core: 2. Of those that a mesh axis runs over, the one named last changes fastest.
Arguments:
- layer_input: bfloat16 [2, 4096, 2048], P(None, ('fsdp', 'seq')), may hold values from -6 to 6
- cotangent: bfloat16 [2, 4096, 2048], P(None, ('fsdp', 'seq')), may hold values from -6 to 6
- segments: int32 [2, 4096], P(None, 'fsdp'), may hold values from 0 to 31, as said below
- routes: int32 [2, 4096, 8], P(None, ('fsdp', 'seq')), may hold values from 0 to 31, all different within a row; in each aligned block of 128 rows (0 to 127, 128 to 255, ..., all dimensions but the last counted through in order) at most 48 rows name the same one
- route_weights: float32 [2, 4096, 8], P(None, ('fsdp', 'seq')), may hold values from 0.1 to 0.3
- gain_attention: bfloat16 [2048], P('fsdp'), may hold values from 0.5 to 1.5
- gain_experts: bfloat16 [2048], P('fsdp'), may hold values from 0.5 to 1.5
- query_proj: bfloat16 [2048, 2048], P('fsdp'), may hold values from -0.125 to 0.125
- key_proj: bfloat16 [2048, 2048], P('fsdp'), may hold values from -0.125 to 0.125
- value_proj: bfloat16 [2048, 2048], P('fsdp'), may hold values from -0.125 to 0.125
- output_proj: bfloat16 [2048, 2048], P('fsdp'), may hold values from -1 to 1
- head_gains: bfloat16 [2, 128], replicated, may hold values from 0.5 to 1.5
- expert_gate: bfloat16 [32, 2048, 1024], P('seq', 'fsdp'), may hold values from -0.125 to 0.125
- expert_up: bfloat16 [32, 2048, 1024], P('seq', 'fsdp'), may hold values from -0.125 to 0.125
- expert_down: bfloat16 [32, 2048, 1024], P('seq', 'fsdp'), may hold values from -0.375 to 0.375
Outputs:
- layer_output: bfloat16 [2, 4096, 2048], P(None, ('fsdp', 'seq'))
- input_grad: float32 [2, 4096, 2048], P(None, ('fsdp', 'seq'))
- grad_gain_attention: float32 [2048], P(('fsdp', 'seq'))
- grad_gain_experts: float32 [2048], P(('fsdp', 'seq'))
- grad_query: float32 [2048, 2048], P(('fsdp', 'seq'))
- grad_key: float32 [2048, 2048], P(('fsdp', 'seq'))
- grad_value: float32 [2048, 2048], P(('fsdp', 'seq'))
- grad_output: float32 [2048, 2048], P(('fsdp', 'seq'))
- grad_head_gains: float32 [2, 128], replicated
- grad_expert_gate: float32 [32, 2048, 1024], P('seq', 'fsdp')
- grad_expert_up: float32 [32, 2048, 1024], P('seq', 'fsdp')
- grad_expert_down: float32 [32, 2048, 1024], P('seq', 'fsdp')
Inputs may be any that keep to these rules, and one draw needn't show every extreme that they name: `routes`: in each aligned block of 128 rows (one device's tokens of one micro-batch) no expert is named more than 48 times, and some expert exactly that often; a row names 8 different experts. `segments`: numbers never fall along a micro-batch; each document lies inside one 1024-token sequence, which holds 2 to 4 documents of 204 tokens or more, the last sequence exactly 4; sequence j of all (micro-batches first) numbers its documents 4 * j, 4 * j + 1 and so on.
All inputs are finite; a program needn't handle non-finite values.
Results may differ from a plain program's by a relative error of at most 0.015.
Values may be sent and summed in bfloat16 or wider, within the bound.
No kernel may reach another device: no remote copies, remote signals or barrier semaphores. Data moves between devices by JAX's collectives and lax.ppermute only.
A program may use at most 448 MiB of HBM per device.

v0:
```python
import math

import jax
import jax.numpy as jnp
from jax import lax
from jax.sharding import PartitionSpec as P

D = 2048
H = 16
HD = 128
FFE = 1024
TOP = 8
SEQ_LEN = 1024


eps = 1e-06
rope_base = 10000.0
masked_score = -1e30


def rms_scale(values):
    return lax.rsqrt(jnp.mean(values * values, axis=-1, keepdims=True) + eps)


def rope_tables(length, width):
    middle = width // 2
    frequency = jnp.exp(-jnp.log(rope_base) * (2.0 * jnp.arange(middle, dtype=jnp.float32) / width))
    angles = jnp.arange(length, dtype=jnp.float32)[:, None] * frequency[None, :]
    return (jnp.cos(angles), jnp.sin(angles))


def rotate(values, cosine, sine_tab):
    middle = values.shape[-1] // 2
    first_half = values[..., :middle]
    second_half = values[..., middle:]
    cos_b = cosine[:, None, :]
    sin_b = sine_tab[:, None, :]
    return jnp.concatenate(
        [first_half * cos_b - second_half * sin_b, second_half * cos_b + first_half * sin_b],
        axis=-1,
    )


def norm_rotate(raw, gain, cosine, sine_tab):
    values = raw.astype(jnp.float32)
    inverse = rms_scale(values)
    normed = values * inverse
    turned = rotate(normed * gain, cosine, sine_tab)
    return (turned.astype(jnp.bfloat16), normed, inverse)


def norm_rotate_back(grad_turned, normed, inverse, gain, cosine, sine_tab):
    grad_scaled = rotate(grad_turned, cosine, -sine_tab)
    grad_gain = jnp.sum(grad_scaled * normed, axis=(0, 1, 2))
    grad_normed = grad_scaled * gain
    grad_raw = inverse * (
        grad_normed - normed * jnp.mean(grad_normed * normed, axis=-1, keepdims=True)
    )
    return (grad_raw, grad_gain)


def token_norm_back(grad_scaled, normed, inverse, gain):
    grad_gain = jnp.sum(grad_scaled * normed, axis=0)
    grad_normed = grad_scaled * gain
    grad_raw = inverse * (
        grad_normed - normed * jnp.mean(grad_normed * normed, axis=-1, keepdims=True)
    )
    return (grad_raw, grad_gain)


def masked_scores(queries, key_rows, segment):
    scaling = 1.0 / math.sqrt(queries.shape[-1])
    scores = (
        jnp.einsum("qhd,khd->hqk", queries, key_rows, preferred_element_type=jnp.float32) * scaling
    )
    allowed = (segment[:, None] == segment[None, :])[None, :, :]
    return jnp.where(allowed, scores, masked_score)


def attend_block(packed):
    queries, key_rows, value_rows, segment = packed
    scores = masked_scores(queries, key_rows, segment)
    row_top = jnp.max(scores, axis=-1, keepdims=True)
    powered = jnp.exp(scores - row_top)
    totals = jnp.sum(powered, axis=-1, keepdims=True)
    probabilities = (powered / totals).astype(jnp.bfloat16)
    attended = jnp.einsum(
        "hqk,khd->qhd", probabilities, value_rows, preferred_element_type=jnp.float32
    )
    return (attended, (row_top + jnp.log(totals))[..., 0])


def attend_back(packed):
    queries, key_rows, value_rows, segment, log_total, grad_out = packed
    scaling = 1.0 / math.sqrt(queries.shape[-1])
    scores = masked_scores(queries, key_rows, segment)
    probabilities = jnp.exp(scores - log_total[..., None])
    grad_probs = jnp.einsum(
        "qhd,khd->hqk", grad_out, value_rows, preferred_element_type=jnp.float32
    )
    centre = jnp.sum(probabilities * grad_probs, axis=-1, keepdims=True)
    grad_scores = (probabilities * (grad_probs - centre)).astype(jnp.bfloat16)
    grad_query = (
        jnp.einsum("hqk,khd->qhd", grad_scores, key_rows, preferred_element_type=jnp.float32)
        * scaling
    )
    grad_key = (
        jnp.einsum("hqk,qhd->khd", grad_scores, queries, preferred_element_type=jnp.float32)
        * scaling
    )
    grad_value = jnp.einsum(
        "hqk,qhd->khd",
        probabilities.astype(jnp.bfloat16),
        grad_out,
        preferred_element_type=jnp.float32,
    )
    return (grad_query, grad_key, grad_value)


def empty_sums(local_experts, column_width):
    square = jnp.zeros((D, D), jnp.float32)
    columns = jnp.zeros((D, column_width), jnp.float32)
    vector = jnp.zeros((D,), jnp.float32)
    bank = jnp.zeros((local_experts, D, FFE), jnp.float32)
    return (
        vector,
        vector,
        columns,
        columns,
        columns,
        square,
        jnp.zeros((2, HD), jnp.float32),
        bank,
        bank,
        bank,
    )


def reduce_grads(sums):
    token_side = tuple(
        (
            lax.psum_scatter(sums[0], ("fsdp", "seq"), scatter_dimension=0, tiled=True),
            lax.psum_scatter(sums[1], ("fsdp", "seq"), scatter_dimension=0, tiled=True),
            lax.psum_scatter(sums[2], ("fsdp", "seq"), scatter_dimension=0, tiled=True),
            lax.psum_scatter(sums[3], ("fsdp", "seq"), scatter_dimension=0, tiled=True),
            lax.psum_scatter(sums[4], ("fsdp", "seq"), scatter_dimension=0, tiled=True),
            lax.psum_scatter(sums[5], ("fsdp", "seq"), scatter_dimension=0, tiled=True),
        )
    )
    head_side = lax.psum(sums[6], ("fsdp", "seq"))
    expert_side = (
        lax.psum_scatter(
            sums[7].astype(jnp.bfloat16), "fsdp", scatter_dimension=1, tiled=True
        ).astype(jnp.float32),
        lax.psum_scatter(
            sums[8].astype(jnp.bfloat16), "fsdp", scatter_dimension=1, tiled=True
        ).astype(jnp.float32),
        lax.psum_scatter(
            sums[9].astype(jnp.bfloat16), "fsdp", scatter_dimension=1, tiled=True
        ).astype(jnp.float32),
    )
    return tuple(token_side) + (head_side,) + tuple(expert_side)


def gather_weights(
    gain_attention,
    gain_experts,
    query_proj,
    key_proj,
    value_proj,
    output_proj,
    head_gains,
    expert_gate,
    expert_up,
    expert_down,
):
    gain_full_one, gain_full_two, w_query, w_key, w_value, w_output = (
        lax.all_gather(gain_attention, "fsdp", axis=0, tiled=True),
        lax.all_gather(gain_experts, "fsdp", axis=0, tiled=True),
        lax.all_gather(query_proj, "fsdp", axis=0, tiled=True),
        lax.all_gather(key_proj, "fsdp", axis=0, tiled=True),
        lax.all_gather(value_proj, "fsdp", axis=0, tiled=True),
        lax.all_gather(output_proj, "fsdp", axis=0, tiled=True),
    )
    w_gate, w_up, w_down = (
        lax.all_gather(expert_gate, "fsdp", axis=1, tiled=True),
        lax.all_gather(expert_up, "fsdp", axis=1, tiled=True),
        lax.all_gather(expert_down, "fsdp", axis=1, tiled=True),
    )
    return (
        gain_full_one.astype(jnp.float32),
        gain_full_two.astype(jnp.float32),
        w_query,
        w_key,
        w_value,
        w_output,
        head_gains.astype(jnp.float32),
        w_gate,
        w_up,
        w_down,
    )


def one_micro(x_in, grad_seed, segment, my_routes, my_weights, weights, sums):
    gain_one, gain_two, w_query, w_key, w_value, w_output, head_gain, w_gate, w_up, w_down = weights
    rows = x_in.shape[0]
    seq_count = lax.axis_size("seq")
    heads_local = H // seq_count
    local_experts = w_gate.shape[0]
    experts = local_experts * seq_count
    capacity = min(rows, 3 * rows * TOP // (2 * experts))
    group = rows * seq_count
    seqs_here = group // SEQ_LEN
    block_shape = (seqs_here, SEQ_LEN, heads_local, HD)
    cosine, sine_tab = rope_tables(SEQ_LEN, HD)
    x_rows = x_in.astype(jnp.float32)
    inv_one = rms_scale(x_rows)
    normed_one = x_rows * inv_one
    h_one = (normed_one * gain_one).astype(jnp.bfloat16)
    q_rows = (
        jnp.dot(h_one, w_query, preferred_element_type=jnp.float32)
        .astype(jnp.bfloat16)
        .reshape(rows, H, HD)
    )
    k_rows = (
        jnp.dot(h_one, w_key, preferred_element_type=jnp.float32)
        .astype(jnp.bfloat16)
        .reshape(rows, H, HD)
    )
    v_rows = (
        jnp.dot(h_one, w_value, preferred_element_type=jnp.float32)
        .astype(jnp.bfloat16)
        .reshape(rows, H, HD)
    )
    q_heads, k_heads, v_heads = (
        lax.all_to_all(q_rows, "seq", split_axis=1, concat_axis=0, tiled=True),
        lax.all_to_all(k_rows, "seq", split_axis=1, concat_axis=0, tiled=True),
        lax.all_to_all(v_rows, "seq", split_axis=1, concat_axis=0, tiled=True),
    )
    q_turn, q_normed, q_inverse = norm_rotate(
        q_heads.reshape(block_shape), head_gain[0], cosine, sine_tab
    )
    k_turn, k_normed, k_inverse = norm_rotate(
        k_heads.reshape(block_shape), head_gain[1], cosine, sine_tab
    )
    v_block = v_heads.reshape(block_shape)
    seg_block = segment.reshape(seqs_here, SEQ_LEN)
    attended, log_total = lax.map(attend_block, (q_turn, k_turn, v_block, seg_block))
    o_send = attended.astype(jnp.bfloat16).reshape(group, heads_local, HD)
    o_rows = lax.all_to_all(o_send, "seq", split_axis=0, concat_axis=1, tiled=True).reshape(rows, D)
    middle = x_rows + jnp.dot(o_rows, w_output, preferred_element_type=jnp.float32)
    inv_two = rms_scale(middle)
    normed_two = middle * inv_two
    h_two = (normed_two * gain_two).astype(jnp.bfloat16)
    flat_ids = my_routes.reshape(-1)
    onehot = (flat_ids[:, None] == jnp.arange(experts)[None, :]).astype(jnp.int32)
    slot_of = jnp.sum((jnp.cumsum(onehot, axis=0) - onehot) * onehot, axis=1)
    target = flat_ids * capacity + slot_of
    token_of = jnp.arange(rows * TOP) // TOP
    buffer_shape = (seq_count, local_experts, capacity, D)
    outgoing = jnp.zeros((experts * capacity, D), jnp.bfloat16).at[target].set(h_two[token_of])
    received = lax.all_to_all(
        outgoing.reshape(buffer_shape), "seq", split_axis=0, concat_axis=0, tiled=True
    )
    gate_act = jnp.einsum("secd,edf->secf", received, w_gate, preferred_element_type=jnp.float32)
    up_act = jnp.einsum("secd,edf->secf", received, w_up, preferred_element_type=jnp.float32)
    gate_sig = jax.nn.sigmoid(gate_act)
    gate_silu = gate_act * gate_sig
    hidden = (gate_silu * up_act).astype(jnp.bfloat16)
    expert_out = jnp.einsum(
        "secf,edf->secd", hidden, w_down, preferred_element_type=jnp.float32
    ).astype(jnp.bfloat16)
    returned = lax.all_to_all(expert_out, "seq", split_axis=0, concat_axis=0, tiled=True).reshape(
        experts * capacity, D
    )
    picked = returned[target].astype(jnp.float32).reshape(rows, TOP, D)
    out_rows = (middle + jnp.sum(picked * my_weights[:, :, None], axis=1)).astype(jnp.bfloat16)
    grad_top = grad_seed.astype(jnp.float32)
    grad_pick = (
        (grad_top[:, None, :] * my_weights[:, :, None]).astype(jnp.bfloat16).reshape(rows * TOP, D)
    )
    grad_send = jnp.zeros((experts * capacity, D), jnp.bfloat16).at[target].set(grad_pick)
    grad_recv = lax.all_to_all(
        grad_send.reshape(buffer_shape), "seq", split_axis=0, concat_axis=0, tiled=True
    )
    grad_hidden = jnp.einsum(
        "secd,edf->secf", grad_recv, w_down, preferred_element_type=jnp.float32
    )
    new_down = sums[9] + jnp.einsum(
        "secd,secf->edf", grad_recv, hidden, preferred_element_type=jnp.float32
    )
    grad_gate_act = (grad_hidden * up_act * gate_sig * (1.0 + gate_act * (1.0 - gate_sig))).astype(
        jnp.bfloat16
    )
    grad_up_act = (grad_hidden * gate_silu).astype(jnp.bfloat16)
    new_gate = sums[7] + jnp.einsum(
        "secd,secf->edf", received, grad_gate_act, preferred_element_type=jnp.float32
    )
    new_up = sums[8] + jnp.einsum(
        "secd,secf->edf", received, grad_up_act, preferred_element_type=jnp.float32
    )
    grad_rows_exp = jnp.einsum(
        "secf,edf->secd", grad_gate_act, w_gate, preferred_element_type=jnp.float32
    )
    grad_rows_exp = grad_rows_exp + jnp.einsum(
        "secf,edf->secd", grad_up_act, w_up, preferred_element_type=jnp.float32
    )
    grad_back = lax.all_to_all(
        grad_rows_exp.astype(jnp.bfloat16), "seq", split_axis=0, concat_axis=0, tiled=True
    ).reshape(experts * capacity, D)
    grad_h_two = jnp.sum(grad_back[target].astype(jnp.float32).reshape(rows, TOP, D), axis=1)
    grad_norm_two, grad_gain_two = token_norm_back(grad_h_two, normed_two, inv_two, gain_two)
    grad_middle = grad_top + grad_norm_two
    grad_attn = grad_middle.astype(jnp.bfloat16)
    grad_output = jnp.einsum("td,te->de", o_rows, grad_attn, preferred_element_type=jnp.float32)
    grad_o = (
        jnp.einsum("te,de->td", grad_attn, w_output, preferred_element_type=jnp.float32)
        .astype(jnp.bfloat16)
        .reshape(rows, H, HD)
    )
    grad_o_heads = lax.all_to_all(grad_o, "seq", split_axis=1, concat_axis=0, tiled=True).reshape(
        block_shape
    )
    grad_q_turn, grad_k_turn, grad_v_block = lax.map(
        attend_back, (q_turn, k_turn, v_block, seg_block, log_total, grad_o_heads)
    )
    grad_q_raw, grad_q_gain = norm_rotate_back(
        grad_q_turn, q_normed, q_inverse, head_gain[0], cosine, sine_tab
    )
    grad_k_raw, grad_k_gain = norm_rotate_back(
        grad_k_turn, k_normed, k_inverse, head_gain[1], cosine, sine_tab
    )
    head_shape = (group, heads_local, HD)
    send_q = grad_q_raw.astype(jnp.bfloat16).reshape(head_shape)
    send_k = grad_k_raw.astype(jnp.bfloat16).reshape(head_shape)
    send_v = grad_v_block.astype(jnp.bfloat16).reshape(head_shape)
    grad_q_rows, grad_k_rows, grad_v_rows = (
        lax.all_to_all(send_q, "seq", split_axis=0, concat_axis=1, tiled=True),
        lax.all_to_all(send_k, "seq", split_axis=0, concat_axis=1, tiled=True),
        lax.all_to_all(send_v, "seq", split_axis=0, concat_axis=1, tiled=True),
    )
    grad_q_rows = grad_q_rows.reshape(rows, D)
    grad_k_rows = grad_k_rows.reshape(rows, D)
    grad_v_rows = grad_v_rows.reshape(rows, D)
    grad_query = jnp.einsum("td,te->de", h_one, grad_q_rows, preferred_element_type=jnp.float32)
    grad_key = jnp.einsum("td,te->de", h_one, grad_k_rows, preferred_element_type=jnp.float32)
    grad_value = jnp.einsum("td,te->de", h_one, grad_v_rows, preferred_element_type=jnp.float32)
    grad_h_one = jnp.einsum("te,de->td", grad_q_rows, w_query, preferred_element_type=jnp.float32)
    grad_h_one = grad_h_one + jnp.einsum(
        "te,de->td", grad_k_rows, w_key, preferred_element_type=jnp.float32
    )
    grad_h_one = grad_h_one + jnp.einsum(
        "te,de->td", grad_v_rows, w_value, preferred_element_type=jnp.float32
    )
    grad_norm_one, grad_gain_one = token_norm_back(grad_h_one, normed_one, inv_one, gain_one)
    grad_rows_in = grad_middle + grad_norm_one
    new_sums = (
        sums[0] + grad_gain_one,
        sums[1] + grad_gain_two,
        sums[2] + grad_query,
        sums[3] + grad_key,
        sums[4] + grad_value,
        sums[5] + grad_output,
        sums[6] + jnp.stack([grad_q_gain, grad_k_gain]),
        new_gate,
        new_up,
        new_down,
    )
    return (out_rows, grad_rows_in, new_sums)


def body(
    layer_input,
    cotangent,
    segments,
    routes,
    route_weights,
    gain_attention,
    gain_experts,
    query_proj,
    key_proj,
    value_proj,
    output_proj,
    head_gains,
    expert_gate,
    expert_up,
    expert_down,
):
    local_experts = expert_gate.shape[0]
    column_width = D
    sums = empty_sums(local_experts, column_width)
    reduced = None
    outputs = []
    grads_in = []
    for batch_index in range(layer_input.shape[0]):
        weights = gather_weights(
            gain_attention,
            gain_experts,
            query_proj,
            key_proj,
            value_proj,
            output_proj,
            head_gains,
            expert_gate,
            expert_up,
            expert_down,
        )
        out_rows, grad_rows_in, sums = one_micro(
            layer_input[batch_index],
            cotangent[batch_index],
            segments[batch_index],
            routes[batch_index],
            route_weights[batch_index],
            weights,
            sums,
        )
        outputs.append(out_rows)
        grads_in.append(grad_rows_in)
    reduced = reduce_grads(sums)
    layer_output = jnp.stack(outputs)
    input_grad = jnp.stack(grads_in)
    return (
        layer_output,
        input_grad,
        reduced[0],
        reduced[1],
        reduced[2],
        reduced[3],
        reduced[4],
        reduced[5],
        reduced[6],
        reduced[7],
        reduced[8],
        reduced[9],
    )


def solution(mesh):
    placed = (
        P(None, ("fsdp", "seq"), None),
        P(None, ("fsdp", "seq"), None),
        P(None, "fsdp"),
        P(None, ("fsdp", "seq"), None),
        P(None, ("fsdp", "seq"), None),
        P("fsdp"),
        P("fsdp"),
        P("fsdp", None),
        P("fsdp", None),
        P("fsdp", None),
        P("fsdp", None),
        P(),
        P("seq", "fsdp", None),
        P("seq", "fsdp", None),
        P("seq", "fsdp", None),
    )
    return jax.shard_map(
        body,
        mesh=mesh,
        in_specs=placed,
        out_specs=(
            P(None, ("fsdp", "seq"), None),
            P(None, ("fsdp", "seq"), None),
            P(("fsdp", "seq")),
            P(("fsdp", "seq")),
            P(("fsdp", "seq"), None),
            P(("fsdp", "seq"), None),
            P(("fsdp", "seq"), None),
            P(("fsdp", "seq"), None),
            P(),
            P("seq", "fsdp", None),
            P("seq", "fsdp", None),
            P("seq", "fsdp", None),
        ),
        check_vma=False,
    )
```

profile of v0, /device:TPU:0, one launch (start us, length us, event | category | flops | bytes accessed | tf_op | source)
XLA Modules:
  0.0 3199.7 jit_solution(11871708037983290398)
XLA Ops:
  12.8 9.0 reduce-window.14
  28.7 42.0 %all-gather.10.cloned.1.call-done = bf16[2048,2048]{1,0:T(8,128)(2,1)} async-done(((bf16[512,2048]{1,0:T(8,128)(2,1)}), bf16[2048,2048]{1,0:T(8,128)(2,1)}) %all-gather.10.cloned.1.call-update) | async-done | bytes 8388624 | tf_op jit(solution)/shard_map/all_gather | solution.py:182
  81.9 48.6 %all-gather.12.cloned.1.call-done = bf16[2048,2048]{1,0:T(8,128)(2,1)} async-done(((bf16[512,2048]{1,0:T(8,128)(2,1)}), bf16[2048,2048]{1,0:T(8,128)(2,1)}) %all-gather.12.cloned.1.call-update) | async-done | bytes 8388624 | tf_op jit(solution)/shard_map/all_gather | solution.py:180
  161.9 28.6 all-gather.14.cloned.1.call-done
  227.1 9.1 all-to-all-done.8
  283.7 24.1 scatter_custom_fusion
  317.2 11.0 scatter_custom_fusion.2
  328.1 124.8 %all-to-all-done.4 = bf16[8,4,48,2048]{3,2,1,0:T(8,128)(2,1)} async-done(((bf16[8,4,48,2048]{3,2,1,0:T(8,128)(2,1)}), bf16[8,4,48,2048]{3,2,1,0:T(8,128)(2,1)}, u32[]{:S(2)}, u32[]{:S(2)}) %all-to-all-start.4) | async-done | bytes 6291488 | tf_op jit(solution)/shard_map/all_to_all | solution.py:262
  470.8 18.2 fusion.17
  489.0 15.4 fusion.25
  504.4 91.1 %all-to-all-done.12 = bf16[8,4,48,2048]{3,2,1,0:T(8,128)(2,1)} async-done(((bf16[8,4,48,2048]{3,2,1,0:T(8,128)(2,1)}), bf16[8,4,48,2048]{3,2,1,0:T(8,128)(2,1)}, u32[]{:S(2)}, u32[]{:S(2)}) %all-to-all-start.12) | async-done | bytes 6291488 | tf_op jit(solution)/shard_map/all_to_all | solution.py:283
  599.4 18.4 fusion.43
  617.7 13.9 fusion.13
  631.7 15.8 fusion.35
  660.7 9.0 reduce-window.16
  676.3 121.6 %all-to-all-done.13 = bf16[8,4,48,2048]{3,2,1,0:T(8,128)(2,1)} async-done(((bf16[8,4,48,2048]{3,2,1,0:T(8,128)(2,1)}), bf16[8,4,48,2048]{3,2,1,0:T(8,128)(2,1)}, u32[]{:S(2)}, u32[]{:S(2)}) %all-to-all-start.13) | async-done | bytes 6291488 | tf_op jit(solution)/shard_map/all_to_all | solution.py:308
  797.9 12.4 gather_fusion.2
  816.4 24.3 scatter_custom_fusion.1
  845.8 10.6 scatter_custom_fusion.3
  856.4 126.5 %all-to-all-done.10 = bf16[8,4,48,2048]{3,2,1,0:T(8,128)(2,1)} async-done(((bf16[8,4,48,2048]{3,2,1,0:T(8,128)(2,1)}), bf16[8,4,48,2048]{3,2,1,0:T(8,128)(2,1)}, u32[]{:S(2)}, u32[]{:S(2)}) %all-to-all-start.10) | async-done | bytes 6291488 | tf_op jit(solution)/shard_map/all_to_all | solution.py:262
  988.2 18.2 fusion.96
  1006.4 15.2 fusion.15
  1021.6 15.2 fusion.23
  1036.8 88.3 %all-to-all-done.18 = bf16[8,4,48,2048]{3,2,1,0:T(8,128)(2,1)} async-done(((bf16[8,4,48,2048]{3,2,1,0:T(8,128)(2,1)}), bf16[8,4,48,2048]{3,2,1,0:T(8,128)(2,1)}, u32[]{:S(2)}, u32[]{:S(2)}) %all-to-all-start.18) | async-done | bytes 6291488 | tf_op jit(solution)/shard_map/all_to_all | solution.py:283
  1125.1 18.3 fusion.39
  1143.4 22.4 fusion.2
  1167.7 24.2 fusion.93
  1191.9 21.6 fusion.1
  1215.4 24.4 convert_bitcast_fusion.1
  1239.7 6.6 copy.232
  1251.2 18.7 fusion.90
  1269.8 21.5 fusion
  1291.3 15.1 fusion.11
  1306.4 20.5 fusion.36
  1327.0 6.5 copy.284
  1333.5 55.6 %all-to-all-done.5 = bf16[8,4,48,2048]{3,2,1,0:T(8,128)(2,1)} async-done(((bf16[8,4,48,2048]{3,2,1,0:T(8,128)(2,1)}), bf16[8,4,48,2048]{3,2,1,0:T(8,128)(2,1)}, u32[]{:S(2)}, u32[]{:S(2)}) %all-to-all-start.5) | async-done | bytes 6291488 | tf_op jit(solution)/shard_map/all_to_all | solution.py:273
  1393.9 24.4 convert_bitcast_fusion
  1418.3 6.7 copy.251
  1425.1 106.1 %all-to-all-done.19 = bf16[8,4,48,2048]{3,2,1,0:T(8,128)(2,1)} async-done(((bf16[8,4,48,2048]{3,2,1,0:T(8,128)(2,1)}), bf16[8,4,48,2048]{3,2,1,0:T(8,128)(2,1)}, u32[]{:S(2)}, u32[]{:S(2)}) %all-to-all-start.19) | async-done | bytes 6291488 | tf_op jit(solution)/shard_map/all_to_all | solution.py:308
  1536.2 12.8 gather_fusion
  1549.0 7.4 fusion.28
  1556.5 12.4 gather_fusion.3
  1568.9 104.3 %all-to-all-done.11 = bf16[8,4,48,2048]{3,2,1,0:T(8,128)(2,1)} async-done(((bf16[8,4,48,2048]{3,2,1,0:T(8,128)(2,1)}), bf16[8,4,48,2048]{3,2,1,0:T(8,128)(2,1)}, u32[]{:S(2)}, u32[]{:S(2)}) %all-to-all-start.11) | async-done | bytes 6291488 | tf_op jit(solution)/shard_map/all_to_all | solution.py:273
  1673.2 12.7 gather_fusion.1
  1700.7 8.4 convolution_add_fusion
  1727.4 10.9 all-to-all-done.14
  1744.3 21.0 all-to-all-done.20
  1802.6 17.4 all-to-all-done.21
  1824.0 19.0 all-to-all-done.15
  1846.0 8.4 convolution_add_fusion.3
  1870.6 16.2 all-to-all-done.22
  1890.9 16.9 all-to-all-done.16
  1910.6 8.4 convolution_add_fusion.2
  1936.7 13.1 all-to-all-done.23
  1954.1 18.2 all-to-all-done.17
  1975.2 8.3 convolution_add_fusion.1
  2016.2 43.8 %all-reduce.2 = (f32[2048]{0:T(1024)S(1)}, f32[2048]{0:T(1024)S(1)}, f32[2,128]{1,0:T(2,128)}) all-reduce(f32[2048]{0:T(1024)S(1)} %add.338, f32[2048]{0:T(1024)S(1)} %add.339, f32[2,128]{1,0:T(2,128)S(1)} %maximum_add_fusion), channel_id=2, replica_groups=mesh['fsdp'=4,'seq'=8] {'fsdp','seq'}, use_global_device_ids=true, to_apply=%region_38.39.clone | all-reduce | flops 4352 | bytes 34816
  2064.8 6.7 convert_element_type.582
  2071.5 6.7 convert_element_type.584
  2078.1 6.7 convert_element_type.586
  2084.8 27.5 reduce-scatter.14.cloned.1.call-done
  2112.3 360.2 %reduce-scatter.8.cloned.1.call-done = f32[64,2048]{1,0:T(8,128)} async-done(((f32[2048,2048]{1,0:T(8,128)}), f32[64,2048]{1,0:T(8,128)}) %reduce-scatter.8.cloned.1.call-update) | async-done | bytes 524304 | tf_op jit(solution)/shard_map/reduce_scatter | solution.py:144
  2472.5 360.3 %reduce-scatter.10.cloned.1.call-done = f32[64,2048]{1,0:T(8,128)} async-done(((f32[2048,2048]{1,0:T(8,128)}), f32[64,2048]{1,0:T(8,128)}) %reduce-scatter.10.cloned.1.call-update) | async-done | bytes 524304 | tf_op jit(solution)/shard_map/reduce_scatter | solution.py:145
  2832.8 360.2 %reduce-scatter.12.cloned.1.call-done = f32[64,2048]{1,0:T(8,128)} async-done(((f32[2048,2048]{1,0:T(8,128)}), f32[64,2048]{1,0:T(8,128)}) %reduce-scatter.12.cloned.1.call-update) | async-done | bytes 524304 | tf_op jit(solution)/shard_map/reduce_scatter | solution.py:146
  (521 shorter events, 391.6 us)
Async XLA Ops:
  7.2 63.5 %all-gather.10.cloned.1.call-start = ((), (), s32[]{:S(2)}) async-start(), calls=%async_computation.31 | async-start | bytes 10485760 | tf_op jit(solution)/shard_map/all_gather | solution.py:182
  7.9 122.6 %all-gather.12.cloned.1.call-start = ((), (), s32[]{:S(2)}) async-start(), calls=%async_computation.32 | async-start | bytes 10485760 | tf_op jit(solution)/shard_map/all_gather | solution.py:180
  8.7 181.7 %all-gather.14.cloned.1.call-start = ((), (), s32[]{:S(2)}) async-start(), calls=%async_computation.33 | async-start | bytes 10485760 | tf_op jit(solution)/shard_map/all_gather | solution.py:181
  9.4 269.2 %all-gather.16.cloned.1.call-start = ((), (), s32[]{:S(2)}) async-start(), calls=%async_computation.34 | async-start | bytes 10485760 | tf_op jit(solution)/shard_map/all_gather | solution.py:183
  10.0 460.8 %all-gather.20.cloned.1.call-start = ((), (), s32[]{:S(2)}) async-start(), calls=%async_computation.36 | async-start | bytes 20971520 | tf_op jit(solution)/shard_map/all_gather | solution.py:187
  10.6 478.4 %all-gather.18.cloned.1.call-start = ((), (), s32[]{:S(2)}) async-start(), calls=%async_computation.35 | async-start | bytes 20971520 | tf_op jit(solution)/shard_map/all_gather | solution.py:186
  11.2 588.2 %all-gather.22.cloned.1.call-start = ((), (), s32[]{:S(2)}) async-start(), calls=%async_computation.37 | async-start | bytes 20971520 | tf_op jit(solution)/shard_map/all_gather | solution.py:188
  28.3 234.8 %copy-start.14 = (f32[4,1,512]{2,1,0:T(1,128)}, f32[4,1,512]{2,1,0:T(1,128)S(1)}, u32[]{:S(2)}) copy-start(f32[4,1,512]{2,1,0:T(1,128)S(1)} %convert_element_type.627) | copy-start | bytes 24580
  28.6 161.8 %copy-start.76 = (f32[128]{0:T(128)}, f32[128]{0:T(128)S(1)}, u32[]{:S(2)}) copy-start(f32[128]{0:T(128)S(1)} %get-tuple-element.229) | copy-start | bytes 1540
  28.6 234.5 %copy-start.74 = (f32[128]{0:T(128)}, f32[128]{0:T(128)S(1)}, u32[]{:S(2)}) copy-start(f32[128]{0:T(128)S(1)} %get-tuple-element.228) | copy-start | bytes 1540
  76.3 59.9 %all-to-all-start = ((bf16[128,16,128]{2,0,1:T(8,128)(2,1)}), bf16[128,16,128]{2,0,1:T(8,128)(2,1)S(1)}, u32[]{:S(2)}, u32[]{:S(2)}) async-start(bf16[128,16,128]{2,0,1:T(8,128)(2,1)} %bitcast.635), calls=%async_computation | async-start | bytes 1048576 | tf_op jit(solution)/shard_map/all_to_all | solution.py:238
  81.8 157.7 %copy-start.113 = (f32[128]{0:T(128)}, f32[128]{0:T(128)S(1)}, u32[]{:S(2)}) copy-start(f32[128]{0:T(128)S(1)} %get-tuple-element.198) | copy-start | bytes 1540
  81.8 159.9 %copy-start.111 = (f32[128]{0:T(128)}, f32[128]{0:T(128)S(1)}, u32[]{:S(2)}) copy-start(f32[128]{0:T(128)S(1)} %get-tuple-element.199) | copy-start | bytes 1540
  136.2 20.4 all-to-all-start.1
  156.6 56.2 %copy-start.27 = (bf16[128,16,128]{2,0,1:T(8,128)(2,1)}, bf16[128,16,128]{2,0,1:T(8,128)(2,1)S(1)}, u32[]{:S(2)}) copy-start(bf16[128,16,128]{2,0,1:T(8,128)(2,1)S(1)} %all-to-all-done.1) | copy-start | bytes 1572868
  156.6 39.5 %all-to-all-start.7 = ((bf16[128,16,128]{2,0,1:T(8,128)(2,1)}), bf16[128,16,128]{2,0,1:T(8,128)(2,1)S(1)}, u32[]{:S(2)}, u32[]{:S(2)}) async-start(bf16[128,16,128]{2,0,1:T(8,128)(2,1)} %bitcast.631), calls=%async_computation.7 | async-start | bytes 1048576 | tf_op jit(solution)/shard_map/all_to_all | solution.py:236
  196.8 20.4 all-to-all-start.2
  210.2 29.3 copy-start.23
  217.3 18.9 all-to-all-start.8
  253.9 18.2 all-to-all-start.3
  263.0 552.4 %copy-start.72 = (f32[4,1,512]{2,1,0:T(1,128)}, f32[4,1,512]{2,1,0:T(1,128)S(1)}, u32[]{:S(2)}) copy-start(f32[4,1,512]{2,1,0:T(1,128)S(1)} %convert_element_type.628) | copy-start | bytes 24580
  272.1 35.7 %all-to-all-start.6 = ((bf16[128,16,128]{2,0,1:T(8,128)(2,1)}), bf16[128,16,128]{2,0,1:T(8,128)(2,1)S(1)}, u32[]{:S(2)}, u32[]{:S(2)}) async-start(bf16[128,16,128]{2,0,1:T(8,128)(2,1)} %bitcast.632), calls=%async_computation.6 | async-start | bytes 1048576 | tf_op jit(solution)/shard_map/all_to_all | solution.py:238
  283.5 531.9 %copy-start.8 = (f32[128,2048]{1,0:T(8,128)}, f32[128,2048]{1,0:T(8,128)S(1)}, u32[]{:S(2)}) copy-start(f32[128,2048]{1,0:T(8,128)S(1)} %get-tuple-element.218) | copy-start | bytes 3145732
  283.5 531.9 %copy-start.115 = (f32[128]{0:T(128)}, f32[128]{0:T(128)S(1)}, u32[]{:S(2)}) copy-start(f32[128]{0:T(128)S(1)} %add_rsqrt_fusion.6) | copy-start | bytes 1540
  308.6 144.3 %all-to-all-start.4 = ((bf16[8,4,48,2048]{3,2,1,0:T(8,128)(2,1)}), bf16[8,4,48,2048]{3,2,1,0:T(8,128)(2,1)}, u32[]{:S(2)}, u32[]{:S(2)}) async-start(bf16[8,4,48,2048]{3,2,1,0:T(8,128)(2,1)} %bitcast.643), calls=%async_computation.4 | async-start | bytes 12582912 | tf_op jit(solution)/shard_map/all_to_all | solution.py:262
  452.9 142.6 %all-to-all-start.12 = ((bf16[8,4,48,2048]{3,2,1,0:T(8,128)(2,1)}), bf16[8,4,48,2048]{3,2,1,0:T(8,128)(2,1)}, u32[]{:S(2)}, u32[]{:S(2)}) async-start(bf16[8,4,48,2048]{3,2,1,0:T(8,128)(2,1)} %bitcast.642), calls=%async_computation.12 | async-start | bytes 12582912 | tf_op jit(solution)/shard_map/all_to_all | solution.py:283
  595.5 58.4 %all-to-all-start.9 = ((bf16[1024,2,128]{2,1,0:T(2,128)(2,1)}), bf16[1024,2,128]{2,1,0:T(2,128)(2,1)S(1)}, u32[]{:S(2)}, u32[]{:S(2)}) async-start(bf16[1024,2,128]{2,1,0:T(2,128)(2,1)} %copy.241), calls=%async_computation.9 | async-start | bytes 1048576 | tf_op jit(solution)/shard_map/all_to_all | solution.py:250
  653.9 144.0 %all-to-all-start.13 = ((bf16[8,4,48,2048]{3,2,1,0:T(8,128)(2,1)}), bf16[8,4,48,2048]{3,2,1,0:T(8,128)(2,1)}, u32[]{:S(2)}, u32[]{:S(2)}) async-start(bf16[8,4,48,2048]{3,2,1,0:T(8,128)(2,1)} %copy.255), calls=%async_computation.13 | async-start | bytes 12582912 | tf_op jit(solution)/shard_map/all_to_all | solution.py:308
  670.2 127.7 %copy-start.86 = (s32[1024]{0:T(1024)}, s32[1024]{0:T(1024)S(1)}, u32[]{:S(2)}) copy-start(s32[1024]{0:T(1024)S(1)} %broadcast_clamp_fusion.1) | copy-start | bytes 12292
  670.3 175.5 %copy-start.102 = (s32[1024,1]{0,1:T(1,128)}, s32[1024,1]{0,1:T(1,128)S(1)}, u32[]{:S(2)}) copy-start(s32[1024,1]{0,1:T(1,128)S(1)} %compare_select_fusion) | copy-start | bytes 12292
  676.3 139.2 %copy-start.11 = (f32[128,2048]{1,0:T(8,128)}, f32[128,2048]{1,0:T(8,128)S(1)}, u32[]{:S(2)}) copy-start(f32[128,2048]{1,0:T(8,128)S(1)} %get-tuple-element.222) | copy-start | bytes 3145732
  676.3 139.1 %copy-start.117 = (f32[128]{0:T(128)}, f32[128]{0:T(128)S(1)}, u32[]{:S(2)}) copy-start(f32[128]{0:T(128)S(1)} %add_rsqrt_fusion.4) | copy-start | bytes 1540
  840.7 142.2 %all-to-all-start.10 = ((bf16[8,4,48,2048]{3,2,1,0:T(8,128)(2,1)}), bf16[8,4,48,2048]{3,2,1,0:T(8,128)(2,1)}, u32[]{:S(2)}, u32[]{:S(2)}) async-start(bf16[8,4,48,2048]{3,2,1,0:T(8,128)(2,1)} %bitcast.645), calls=%async_computation.10 | async-start | bytes 12582912 | tf_op jit(solution)/shard_map/all_to_all | solution.py:262
  982.9 142.3 %all-to-all-start.18 = ((bf16[8,4,48,2048]{3,2,1,0:T(8,128)(2,1)}), bf16[8,4,48,2048]{3,2,1,0:T(8,128)(2,1)}, u32[]{:S(2)}, u32[]{:S(2)}) async-start(bf16[8,4,48,2048]{3,2,1,0:T(8,128)(2,1)} %bitcast.644), calls=%async_computation.18 | async-start | bytes 12582912 | tf_op jit(solution)/shard_map/all_to_all | solution.py:283
  988.0 1076.9 %reduce-scatter.16.cloned.1.call-start = ((), (), s32[]{:S(2)}) async-start(), calls=%async_computation.42 | async-start | bytes 20971520 | tf_op jit(solution)/shard_map/reduce_scatter | solution.py:152
  1165.8 905.7 %reduce-scatter.18.cloned.1.call-start = ((), (), s32[]{:S(2)}) async-start(), calls=%async_computation.43 | async-start | bytes 20971520 | tf_op jit(solution)/shard_map/reduce_scatter | solution.py:155
  1246.4 142.7 %all-to-all-start.5 = ((bf16[8,4,48,2048]{3,2,1,0:T(8,128)(2,1)}), bf16[8,4,48,2048]{3,2,1,0:T(8,128)(2,1)}, u32[]{:S(2)}, u32[]{:S(2)}) async-start(bf16[8,4,48,2048]{3,2,1,0:T(8,128)(2,1)} %copy.232), calls=%async_computation.5 | async-start | bytes 12582912 | tf_op jit(solution)/shard_map/all_to_all | solution.py:273
  1251.1 827.0 %reduce-scatter.20.cloned.1.call-start = ((), (), s32[]{:S(2)}) async-start(), calls=%async_computation.44 | async-start | bytes 20971520 | tf_op jit(solution)/shard_map/reduce_scatter | solution.py:158
  1333.5 60.4 %copy-start.128 = (bf16[8,4,48,1024]{3,2,0,1:T(8,128)(2,1)S(1)}, bf16[8,4,48,1024]{3,2,0,1:T(8,128)(2,1)}, u32[]{:S(2)}) copy-start(bf16[8,4,48,1024]{3,2,0,1:T(8,128)(2,1)} %get-tuple-element.141) | copy-start | bytes 9437188
  1389.1 142.0 %all-to-all-start.19 = ((bf16[8,4,48,2048]{3,2,1,0:T(8,128)(2,1)}), bf16[8,4,48,2048]{3,2,1,0:T(8,128)(2,1)}, u32[]{:S(2)}, u32[]{:S(2)}) async-start(bf16[8,4,48,2048]{3,2,1,0:T(8,128)(2,1)} %copy.284), calls=%async_computation.19 | async-start | bytes 12582912 | tf_op jit(solution)/shard_map/all_to_all | solution.py:308
  1425.1 110.9 %copy-start.107 = (f32[128,8]{0,1:T(8,128)S(1)}, f32[128,8]{0,1:T(8,128)}, u32[]{:S(2)}) copy-start(f32[128,8]{0,1:T(8,128)} %get-tuple-element.186) | copy-start | bytes 12292
  1425.1 111.0 %copy-start.106 = (f32[128,8]{0,1:T(8,128)S(1)}, f32[128,8]{0,1:T(8,128)}, u32[]{:S(2)}) copy-start(f32[128,8]{0,1:T(8,128)} %get-tuple-element.185) | copy-start | bytes 12292
  1425.1 111.1 %copy-start.103 = (s32[1024,1]{0,1:T(1,128)S(1)}, s32[1024,1]{0,1:T(1,128)}, u32[]{:S(2)}) copy-start(s32[1024,1]{0,1:T(1,128)} %copy-done.102) | copy-start | bytes 12292
  1425.1 111.1 %copy-start.87 = (s32[1024]{0:T(1024)S(1)}, s32[1024]{0:T(1024)}, u32[]{:S(2)}) copy-start(s32[1024]{0:T(1024)} %copy-done.86) | copy-start | bytes 12292
  1531.2 142.0 %all-to-all-start.11 = ((bf16[8,4,48,2048]{3,2,1,0:T(8,128)(2,1)}), bf16[8,4,48,2048]{3,2,1,0:T(8,128)(2,1)}, u32[]{:S(2)}, u32[]{:S(2)}) async-start(bf16[8,4,48,2048]{3,2,1,0:T(8,128)(2,1)} %copy.251), calls=%async_computation.11 | async-start | bytes 12582912 | tf_op jit(solution)/shard_map/all_to_all | solution.py:273
  1535.9 576.4 %reduce-scatter.14.cloned.1.call-start = ((), (), s32[]{:S(2)}) async-start(), calls=%async_computation.41 | async-start | bytes 17301504 | tf_op jit(solution)/shard_map/reduce_scatter | solution.py:147
  1716.3 22.0 all-to-all-start.14
  1720.1 45.3 %copy-start.55 = (bf16[1024,2,128]{0,2,1:T(8,128)(2,1)S(1)}, bf16[1024,2,128]{0,2,1:T(8,128)(2,1)}, u32[]{:S(2)}) copy-start(bf16[1024,2,128]{0,2,1:T(8,128)(2,1)} %copy-done.54) | copy-start | bytes 1572868
  1738.3 27.0 all-to-all-start.20
  1744.3 33.5 %copy-start.41 = (bf16[128,8,2,128]{3,0,1,2:T(8,128)(2,1)}, bf16[128,8,2,128]{3,0,1,2:T(8,128)(2,1)S(1)}, u32[]{:S(2)}) copy-start(bf16[128,8,2,128]{3,0,1,2:T(8,128)(2,1)S(1)} %copy.257) | copy-start | bytes 1572868
  1792.7 50.7 %copy-start.1 = (bf16[2,128,2048]{2,1,0:T(8,128)(2,1)S(1)}, bf16[2,128,2048]{2,1,0:T(8,128)(2,1)}, u32[]{:S(2)}) copy-start(bf16[2,128,2048]{2,1,0:T(8,128)(2,1)} %param.15) | copy-start | bytes 3145732
  1792.7 50.7 %copy-start.15 = (f32[4,1,512]{2,1,0:T(1,128)S(1)}, f32[4,1,512]{2,1,0:T(1,128)}, u32[]{:S(2)}) copy-start(f32[4,1,512]{2,1,0:T(1,128)} %copy-done.14) | copy-start | bytes 24580
  1792.7 50.7 %copy-start.77 = (f32[128]{0:T(128)S(1)}, f32[128]{0:T(128)}, u32[]{:S(2)}) copy-start(f32[128]{0:T(128)} %copy-done.76) | copy-start | bytes 1540
  1796.7 23.2 all-to-all-start.21
  1819.9 23.1 all-to-all-start.15
  1823.4 649.1 %reduce-scatter.8.cloned.1.call-start = ((), (), s32[]{:S(2)}) async-start(), calls=%async_computation.38 | async-start | bytes 17301504 | tf_op jit(solution)/shard_map/reduce_scatter | solution.py:144
  1864.7 22.1 all-to-all-start.22
  1886.8 21.0 all-to-all-start.16
  1890.3 942.5 %reduce-scatter.10.cloned.1.call-start = ((), (), s32[]{:S(2)}) async-start(), calls=%async_computation.39 | async-start | bytes 17301504 | tf_op jit(solution)/shard_map/reduce_scatter | solution.py:145
  1926.2 23.7 all-to-all-start.23
  1949.8 22.5 all-to-all-start.17
  1953.3 1239.7 %reduce-scatter.12.cloned.1.call-start = ((), (), s32[]{:S(2)}) async-start(), calls=%async_computation.40 | async-start | bytes 17301504 | tf_op jit(solution)/shard_map/reduce_scatter | solution.py:146
  2012.0 49.1 %copy-start.5 = (f32[128,2048]{1,0:T(8,128)S(1)}, f32[128,2048]{1,0:T(8,128)}, u32[]{:S(2)}) copy-start(f32[128,2048]{1,0:T(8,128)} %copy-done.4) | copy-start | bytes 3145732
  2012.0 49.1 %copy-start.7 = (f32[128,2048]{1,0:T(8,128)S(1)}, f32[128,2048]{1,0:T(8,128)}, u32[]{:S(2)}) copy-start(f32[128,2048]{1,0:T(8,128)} %copy-done.6) | copy-start | bytes 3145732
  (109 other events, 783.0 us)
Sparse Core Ops, SparseCore 0:
  9.6 61.0 all-gather.9
  72.2 58.2 all-gather.11
  132.1 58.2 all-gather.13
  191.8 58.2 all-gather.15
  251.6 105.9 all-gather.19
  358.9 105.9 all-gather.17
  466.4 105.9 all-gather.21
  1165.9 124.2 reduce-scatter.15
  1292.9 126.0 reduce-scatter.17
  1421.5 126.0 reduce-scatter.19
  1709.2 403.0 reduce-scatter.13
  2115.2 357.3 reduce-scatter.7
  2475.5 357.2 reduce-scatter.9
  2835.6 357.3 reduce-scatter.11
where the time goes:
time: 3210 us; the launch traced here: 3200 us
  waiting for transfers between devices  2200 us (69%)
  matrix products  500 us (16%)
  local copies, waits for them, and re-layouts  170 us (5%)
  other arithmetic  143 us (4%)
  starting transfers between devices  112 us (3%)
  blocking collectives  55.1 us (2%)
    reduce_scatter x1, waiting for transfers between devices, reduce_grads(): lax.psum_scatter(sums[3], ('fsdp', 'seq'), scatter_dimension=0, tiled=True)  360 us
    reduce_scatter x1, waiting for transfers between devices, reduce_grads(): lax.psum_scatter(sums[4], ('fsdp', 'seq'), scatter_dimension=0, tiled=True)  360 us
    reduce_scatter x1, waiting for transfers between devices, reduce_grads(): lax.psum_scatter(sums[2], ('fsdp', 'seq'), scatter_dimension=0, tiled=True)  360 us
    all_to_all x2, waiting for transfers between devices, one_micro(): lax.all_to_all(outgoing.reshape(buffer_shape), 'seq', split_axis=0, conca...  251 us
    all_to_all x2, waiting for transfers between devices, one_micro(): lax.all_to_all(grad_rows_exp.astype(jnp.bfloat16), 'seq', split_axis=0, c...  228 us
    all_to_all x2, waiting for transfers between devices, one_micro(): lax.all_to_all(grad_send.reshape(buffer_shape), 'seq', split_axis=0, conc...  179 us
    all_to_all x2, waiting for transfers between devices, one_micro(): lax.all_to_all(expert_out, 'seq', split_axis=0, concat_axis=0, tiled=True)  160 us
  transfers between devices with their start and end apart: 38, of which 27 were waited for; matrix products, arithmetic and copies ran while one was open for 22% of the time, Pallas kernels for 0%

commit v1 on v0

v1 whole, which is shorter than its diff:
```python
import math

import jax
import jax.numpy as jnp
from jax import lax
from jax.sharding import PartitionSpec as P

D = 2048
H = 16
HD = 128
FFE = 1024
TOP = 8
SEQ_LEN = 1024

eps = 1e-06
rope_base = 10000.0
masked_score = -1e30
f32 = jnp.float32
bf16 = jnp.bfloat16


def shift(value, axis, outer, inner, by_outer, by_inner):
    pairs = []
    for a in range(outer):
        for b in range(inner):
            there = ((a + by_outer) % outer) * inner + (b + by_inner) % inner
            pairs.append((a * inner + b, there))
    return lax.ppermute(value, axis, pairs)


def sizes(axis):
    count = lax.axis_size(axis)
    return (count // 2, 2) if axis == "fsdp" else (4, count // 4)


def ring_gather(value, axis):
    outer, inner = sizes(axis)
    blocks = []
    for a in range(outer):
        if a:
            value = shift(value, axis, outer, inner, 1, 0)
        moved = value
        blocks.append(moved)
        for b in range(1, inner):
            moved = shift(moved, axis, outer, inner, 0, 1)
            blocks.append(moved)
    return blocks


def ring_scatter(parts, axis):
    outer, inner = sizes(axis)
    reduced = [None] * outer
    for a in list(range(1, outer)) + [0]:
        total = parts[a * inner + 1 % inner]
        for b in range(2, inner + 1):
            moved = shift(total, axis, outer, inner, 0, 1)
            total = (moved.astype(f32) + parts[a * inner + b % inner].astype(f32)).astype(bf16)
        reduced[a] = total
    total = reduced[1 % outer]
    for a in range(2, outer + 1):
        moved = shift(total, axis, outer, inner, 1, 0)
        total = moved.astype(f32) + reduced[a % outer].astype(f32)
        if a < outer:
            total = total.astype(bf16)
    return total


def relative_order(axis):
    outer, inner = sizes(axis)
    me = lax.axis_index(axis)
    a, b = me // inner, me % inner
    k = jnp.arange(outer * inner)
    return ((a - k // inner) % outer) * inner + (b - k % inner) % inner


def rms_scale(values):
    return lax.rsqrt(jnp.mean(values * values, axis=-1, keepdims=True) + eps)


def rotate(values, cosine, sine_tab):
    middle = values.shape[-1] // 2
    first_half = values[..., :middle]
    second_half = values[..., middle:]
    cos_b = cosine[:, None, :]
    sin_b = sine_tab[:, None, :]
    return jnp.concatenate(
        [first_half * cos_b - second_half * sin_b, second_half * cos_b + first_half * sin_b],
        axis=-1,
    )


def norm_rotate(raw, gain, cosine, sine_tab):
    values = raw.astype(f32)
    inverse = rms_scale(values)
    normed = values * inverse
    turned = rotate(normed * gain, cosine, sine_tab)
    return (turned.astype(bf16), normed, inverse)


def norm_rotate_back(grad_turned, normed, inverse, gain, cosine, sine_tab):
    grad_scaled = rotate(grad_turned, cosine, -sine_tab)
    grad_gain = jnp.sum(grad_scaled * normed, axis=(0, 1, 2))
    grad_normed = grad_scaled * gain
    grad_raw = inverse * (
        grad_normed - normed * jnp.mean(grad_normed * normed, axis=-1, keepdims=True)
    )
    return (grad_raw, grad_gain)


def token_norm_back(grad_scaled, normed, inverse, gain):
    grad_gain = jnp.sum(grad_scaled * normed, axis=0)
    grad_normed = grad_scaled * gain
    grad_raw = inverse * (
        grad_normed - normed * jnp.mean(grad_normed * normed, axis=-1, keepdims=True)
    )
    return (grad_raw, grad_gain)


def masked_scores(queries, key_rows, segment):
    scaling = 1.0 / math.sqrt(queries.shape[-1])
    scores = jnp.einsum("mqhd,mkhd->mhqk", queries, key_rows, preferred_element_type=f32) * scaling
    allowed = (segment[:, :, None] == segment[:, None, :])[:, None, :, :]
    return jnp.where(allowed, scores, masked_score)


def attend(queries, key_rows, value_rows, segment):
    scores = masked_scores(queries, key_rows, segment)
    row_top = jnp.max(scores, axis=-1, keepdims=True)
    powered = jnp.exp(scores - row_top)
    totals = jnp.sum(powered, axis=-1, keepdims=True)
    probabilities = (powered / totals).astype(bf16)
    attended = jnp.einsum("mhqk,mkhd->mqhd", probabilities, value_rows, preferred_element_type=f32)
    return (attended, row_top + jnp.log(totals))


def attend_back(queries, key_rows, value_rows, segment, log_total, grad_out):
    scaling = 1.0 / math.sqrt(queries.shape[-1])
    scores = masked_scores(queries, key_rows, segment)
    probabilities = jnp.exp(scores - log_total)
    grad_probs = jnp.einsum("mqhd,mkhd->mhqk", grad_out, value_rows, preferred_element_type=f32)
    centre = jnp.sum(probabilities * grad_probs, axis=-1, keepdims=True)
    grad_scores = (probabilities * (grad_probs - centre)).astype(bf16)
    grad_query = (
        jnp.einsum("mhqk,mkhd->mqhd", grad_scores, key_rows, preferred_element_type=f32) * scaling
    )
    grad_key = (
        jnp.einsum("mhqk,mqhd->mkhd", grad_scores, queries, preferred_element_type=f32) * scaling
    )
    grad_value = jnp.einsum(
        "mhqk,mqhd->mkhd", probabilities.astype(bf16), grad_out, preferred_element_type=f32
    )
    return (grad_query, grad_key, grad_value)


def body(
    layer_input,
    cotangent,
    segments,
    routes,
    route_weights,
    gain_attention,
    gain_experts,
    query_proj,
    key_proj,
    value_proj,
    output_proj,
    head_gains,
    expert_gate,
    expert_up,
    expert_down,
):
    micro, rows, _ = layer_input.shape
    nf, ns = lax.axis_size("fsdp"), lax.axis_size("seq")
    seq_index = lax.axis_index("seq")
    fsdp_order = relative_order("fsdp")
    seq_order = relative_order("seq")
    tokens = micro * rows
    group = rows * ns
    heads_local = H // ns
    width = heads_local * HD
    local_experts = expert_gate.shape[0]
    experts = local_experts * ns
    capacity = ns * min(rows, 3 * rows * TOP // (2 * experts))
    head_gain = head_gains.astype(f32)

    def to_relative(value):
        cut = value.reshape(value.shape[:-1] + (nf, D // nf))
        return jnp.take(cut, fsdp_order, axis=-2).reshape(value.shape)

    inverse_order = jnp.argsort(fsdp_order)

    def from_relative(value):
        cut = value.reshape(value.shape[:-1] + (nf, D // nf))
        return jnp.take(cut, inverse_order, axis=-2).reshape(value.shape)

    def gather_tokens(value):
        return jnp.concatenate(ring_gather(value, "seq"), axis=1)

    def scatter_tokens(value):
        cut = value.reshape(micro, ns, rows, value.shape[-1])
        return ring_scatter([cut[:, k] for k in range(ns)], "seq")

    columns = [
        lax.dynamic_slice_in_dim(w, seq_index * width, width, axis=1)
        for w in (query_proj, key_proj, value_proj)
    ]
    w_qkv = jnp.concatenate(ring_gather(jnp.concatenate(columns, axis=1), "fsdp"), axis=0)
    gains = lax.all_gather(
        jnp.stack([gain_attention, gain_experts]), "fsdp", axis=1, tiled=True
    ).astype(f32)
    w_output = jnp.concatenate(ring_gather(output_proj, "fsdp"), axis=0)
    w_down = jnp.concatenate(ring_gather(expert_down, "fsdp"), axis=1)
    w_gate = jnp.concatenate(ring_gather(expert_gate, "fsdp"), axis=1)
    w_up = jnp.concatenate(ring_gather(expert_up, "fsdp"), axis=1)

    x_rows = layer_input.astype(f32)
    inv_one = rms_scale(x_rows)
    normed_one = x_rows * inv_one
    h_one = gather_tokens(to_relative((normed_one * gains[0]).astype(bf16)))
    qkv = jnp.einsum("mtd,de->mte", h_one, w_qkv, preferred_element_type=f32).astype(bf16)
    heads_shape = (micro, group, heads_local, HD)
    q_raw = qkv[..., :width].reshape(heads_shape)
    k_raw = qkv[..., width : 2 * width].reshape(heads_shape)
    v_heads = qkv[..., 2 * width :].reshape(heads_shape)

    places = (seq_order[:, None] * rows + jnp.arange(rows)[None, :]).reshape(-1)
    frequency = jnp.exp(
        -jnp.log(rope_base) * (2.0 * jnp.arange(HD // 2, dtype=f32) / HD)
    )
    angles = places.astype(f32)[:, None] * frequency[None, :]
    cosine, sine_tab = jnp.cos(angles), jnp.sin(angles)
    segment = jnp.take(segments.reshape(micro, ns, rows), seq_order, axis=1).reshape(micro, group)

    q_turn, q_normed, q_inverse = norm_rotate(q_raw, head_gain[0], cosine, sine_tab)
    k_turn, k_normed, k_inverse = norm_rotate(k_raw, head_gain[1], cosine, sine_tab)
    attended, log_total = attend(q_turn, k_turn, v_heads, segment)

    inverse_seq = jnp.argsort(seq_order)

    def to_blocks(value):
        cut = value.reshape(micro, ns, rows, value.shape[-1])
        return jnp.take(jnp.moveaxis(cut, 1, 0), inverse_seq, axis=0)

    o_heads = to_blocks(attended.astype(bf16).reshape(micro, group, width))
    o_back = lax.all_to_all(o_heads, "seq", split_axis=0, concat_axis=0, tiled=True)
    o_rows = jnp.moveaxis(o_back, 0, 2).reshape(tokens, D)
    o_all = lax.all_gather(o_heads.reshape(group * micro, width), "seq", axis=1, tiled=True)

    middle = x_rows.reshape(tokens, D) + jnp.dot(
        to_relative(o_rows), w_output, preferred_element_type=f32
    )
    inv_two = rms_scale(middle)
    normed_two = middle * inv_two
    h_two = gather_tokens(
        to_relative((normed_two * gains[1]).astype(bf16)).reshape(micro, rows, D)
    )

    packed = jnp.concatenate([routes.astype(f32), route_weights], axis=-1)
    packed = gather_tokens(packed)
    route_all, weight_all = packed[..., :TOP].astype(jnp.int32), packed[..., TOP:]
    mine = seq_index * local_experts + jnp.arange(local_experts)
    hit = route_all[:, :, None, :] == mine[None, None, :, None]
    chosen = jnp.any(hit, axis=-1)
    weight_of = jnp.sum(jnp.where(hit, weight_all[:, :, None, :], 0.0), axis=-1)
    block = 128
    counted = chosen.reshape(micro, group // block, block, local_experts).astype(f32)
    below = jnp.tril(jnp.ones((block, block), f32), -1)
    inside = jnp.einsum("ab,mkbe->mkae", below, counted)
    sums = jnp.sum(counted, axis=2)
    before = jnp.cumsum(sums, axis=1) - sums
    slot = (inside + before[:, :, None, :]).reshape(micro, group, local_experts).astype(jnp.int32)
    slot = jnp.where(chosen, slot, -1)
    slot_t = jnp.transpose(slot, (2, 0, 1))
    weight_t = jnp.transpose(weight_of, (2, 0, 1))
    onehot = slot_t[:, :, None, :] == jnp.arange(capacity)[None, None, :, None]
    weight_slot = jnp.sum(jnp.where(onehot, weight_t[:, :, None, :], 0.0), axis=-1)
    pick = onehot.astype(bf16)

    def dispatch(value):
        return jnp.einsum("emct,mtd->emcd", pick, value, preferred_element_type=f32)

    def combine(value):
        return jnp.einsum("emct,emcd->mtd", pick, value, preferred_element_type=f32).astype(bf16)

    grad_top = cotangent.astype(f32)
    g_all = gather_tokens(to_relative(cotangent))
    grad_rows = (dispatch(g_all) * weight_slot[..., None]).astype(bf16)
    grad_hidden = jnp.einsum("emcd,edf->emcf", grad_rows, w_down, preferred_element_type=f32)

    taken = dispatch(h_two).astype(bf16)
    gate_act = jnp.einsum("emcd,edf->emcf", taken, w_gate, preferred_element_type=f32)
    up_act = jnp.einsum("emcd,edf->emcf", taken, w_up, preferred_element_type=f32)
    gate_sig = jax.nn.sigmoid(gate_act)
    gate_silu = gate_act * gate_sig
    hidden = (gate_silu * up_act).astype(bf16)
    grad_gate_act = (grad_hidden * up_act * gate_sig * (1.0 + gate_act * (1.0 - gate_sig))).astype(
        bf16
    )
    grad_up_act = (grad_hidden * gate_silu).astype(bf16)
    grad_taken = jnp.einsum(
        "emcf,edf->emcd", grad_gate_act, w_gate, preferred_element_type=f32
    ) + jnp.einsum("emcf,edf->emcd", grad_up_act, w_up, preferred_element_type=f32)
    grad_h_two = from_relative(scatter_tokens(combine(grad_taken.astype(bf16))))

    def bank_grad(left, right):
        whole = jnp.einsum("emcd,emcf->edf", left, right, preferred_element_type=f32).astype(bf16)
        cut = whole.reshape(local_experts, nf, D // nf, FFE)
        return ring_scatter([cut[:, k] for k in range(nf)], "fsdp")

    grad_down = bank_grad(grad_rows, hidden)
    grad_gate = bank_grad(taken, grad_gate_act)
    grad_up = bank_grad(taken, grad_up_act)

    expert_out = jnp.einsum("emcf,edf->emcd", hidden, w_down, preferred_element_type=f32)
    mixed = from_relative(
        scatter_tokens(combine((expert_out * weight_slot[..., None]).astype(bf16)))
    )
    layer_output = (middle.reshape(micro, rows, D) + mixed).astype(bf16)

    grad_norm_two, grad_gain_two = token_norm_back(
        grad_h_two.reshape(tokens, D), normed_two, inv_two, gains[1]
    )
    grad_middle = grad_top.reshape(tokens, D) + grad_norm_two
    grad_attn = grad_middle.astype(bf16)
    grad_o = from_relative(
        jnp.einsum("te,de->td", grad_attn, w_output, preferred_element_type=f32).astype(bf16)
    )

    def to_heads(value):
        cut = value.reshape(micro, rows, ns, width)
        return lax.all_to_all(
            jnp.moveaxis(cut, 2, 0), "seq", split_axis=0, concat_axis=0, tiled=True
        )

    do_blocks = to_heads(grad_o)
    grad_attn_columns = to_heads(grad_attn).reshape(micro * group, width)
    do_heads = jnp.moveaxis(jnp.take(do_blocks, seq_order, axis=0), 0, 1).reshape(heads_shape)
    grad_q_turn, grad_k_turn, grad_v = attend_back(
        q_turn, k_turn, v_heads, segment, log_total, do_heads
    )
    grad_q, grad_q_gain = norm_rotate_back(
        grad_q_turn, q_normed, q_inverse, head_gain[0], cosine, sine_tab
    )
    grad_k, grad_k_gain = norm_rotate_back(
        grad_k_turn, k_normed, k_inverse, head_gain[1], cosine, sine_tab
    )
    grad_qkv = jnp.concatenate(
        [g.astype(bf16).reshape(micro, group, width) for g in (grad_q, grad_k, grad_v)], axis=-1
    )
    grad_h_one = from_relative(
        scatter_tokens(
            jnp.einsum("mte,de->mtd", grad_qkv, w_qkv, preferred_element_type=f32).astype(bf16)
        )
    )
    grad_norm_one, grad_gain_one = token_norm_back(
        grad_h_one.reshape(tokens, D), normed_one.reshape(tokens, D), inv_one.reshape(tokens, 1), gains[0]
    )
    input_grad = (grad_middle + grad_norm_one).reshape(micro, rows, D)

    from_qkv = jnp.einsum("mtd,mte->de", h_one, grad_qkv, preferred_element_type=f32)
    from_out = jnp.einsum("td,te->de", o_all, grad_attn_columns, preferred_element_type=f32)
    from_out = jnp.take(from_out.reshape(nf, D // nf, width), fsdp_order, axis=0).reshape(D, width)
    whole = jnp.concatenate([from_qkv, from_out], axis=1).astype(bf16)
    cut = whole.reshape(nf, D // nf, 4 * width)
    owned = ring_scatter([cut[k] for k in range(nf)], "fsdp").astype(bf16)
    owned = owned.reshape(ns, D // (nf * ns), 4 * width)
    owned = lax.all_to_all(owned, "seq", split_axis=0, concat_axis=0, tiled=True)
    owned = jnp.moveaxis(owned.reshape(ns, -1, 4, width), 0, 2).astype(f32)
    grad_query, grad_key, grad_value, grad_output = (
        owned[:, k].reshape(-1, D) for k in range(4)
    )

    vectors = lax.psum(
        jnp.concatenate([grad_gain_one, grad_gain_two, grad_q_gain, grad_k_gain]), ("fsdp", "seq")
    )
    share = D // (nf * ns)
    start = (lax.axis_index("fsdp") * ns + seq_index) * share
    grad_gain_attention = lax.dynamic_slice_in_dim(vectors, start, share)
    grad_gain_experts = lax.dynamic_slice_in_dim(vectors, D + start, share)
    grad_head_gains = vectors[2 * D :].reshape(2, HD)
    return (
        layer_output,
        input_grad,
        grad_gain_attention,
        grad_gain_experts,
        grad_query,
        grad_key,
        grad_value,
        grad_output,
        grad_head_gains,
        grad_gate,
        grad_up,
        grad_down,
    )


def solution(mesh):
    placed = (
        P(None, ("fsdp", "seq"), None),
        P(None, ("fsdp", "seq"), None),
        P(None, "fsdp"),
        P(None, ("fsdp", "seq"), None),
        P(None, ("fsdp", "seq"), None),
        P("fsdp"),
        P("fsdp"),
        P("fsdp", None),
        P("fsdp", None),
        P("fsdp", None),
        P("fsdp", None),
        P(),
        P("seq", "fsdp", None),
        P("seq", "fsdp", None),
        P("seq", "fsdp", None),
    )
    return jax.shard_map(
        body,
        mesh=mesh,
        in_specs=placed,
        out_specs=(
            P(None, ("fsdp", "seq"), None),
            P(None, ("fsdp", "seq"), None),
            P(("fsdp", "seq")),
            P(("fsdp", "seq")),
            P(("fsdp", "seq"), None),
            P(("fsdp", "seq"), None),
            P(("fsdp", "seq"), None),
            P(("fsdp", "seq"), None),
            P(),
            P("seq", "fsdp", None),
            P("seq", "fsdp", None),
            P("seq", "fsdp", None),
        ),
        check_vma=False,
    )
```

time: 3210 us -> 1440 us (0.45)
  waiting for transfers between devices: 2200 us -> 421 us
  matrix products: 500 us -> 365 us
  local copies, waits for them, and re-layouts: 170 us -> 301 us
  other arithmetic: 143 us -> 185 us
    reduce_scatter x7 -> x0, waiting for transfers between devices: 1110 us -> none  [the longest x1 360 us: reduce_grads(): lax.psum_scatter(sums[3], ('fsdp', 'seq'), scatter_dimension=0, tiled=True)]
    all_to_all x24 -> x4, waiting for transfers between devices: 972 us -> 0.01 us  [the longest x2 0.01 us: to_heads(): lax.all_to_all(jnp.moveaxis(cut, 2, 0), 'seq', split_axis=0, concat_axis=...]
    ppermute x0 -> x76, waiting for transfers between devices: none -> 421 us  [shift(): return lax.ppermute(value, axis, pairs)]
    dot_general x54 -> x26, matrix products: 500 us -> 365 us  [the longest x3 60.2 us: bank_grad(): jnp.einsum('emcd,emcf->edf', left, right, preferred_element_type=f32)]
    unnamed x274 -> x300, local copies, waits for them, and re-layouts: 13.8 us -> 147 us
    all_gather x7 -> x1, waiting for transfers between devices: 119 us -> 0.01 us  [body(): lax.all_gather(o_heads.reshape(group * micro, width), 'seq', axis=1, tile...]
    all_to_all x24 -> x4, starting transfers between devices: 110 us -> 20.7 us  [the longest x2 10.6 us: to_heads(): lax.all_to_all(jnp.moveaxis(cut, 2, 0), 'seq', split_axis=0, concat_axis=...]
    ppermute x0 -> x76, starting transfers between devices: none -> 70.5 us  [shift(): return lax.ppermute(value, axis, pairs)]
  transfers between devices with their start and end apart: 38 -> 81, of which waited for: 27 -> 27; matrix products, arithmetic and copies ran while one was open for 22% -> 57% of each run, Pallas kernels for 0% -> 0%
where the time goes in v1:
time: 1440 us; the launch traced here: 1430 us
  waiting for transfers between devices  421 us (29%)
  matrix products  365 us (25%)
  local copies, waits for them, and re-layouts  301 us (21%)
  other arithmetic  185 us (13%)
  starting transfers between devices  91.2 us (6%)
  blocking collectives  46.5 us (3%)
  between operations  16.1 us (1%)
    ppermute x76, waiting for transfers between devices, shift(): return lax.ppermute(value, axis, pairs)  421 us
    unnamed x300, local copies, waits for them, and re-layouts  147 us
    ppermute x76, starting transfers between devices, shift(): return lax.ppermute(value, axis, pairs)  70.5 us
    dot_general x3, matrix products, bank_grad(): jnp.einsum('emcd,emcf->edf', left, right, preferred_element_type=f32)  60.2 us
    add x6, other arithmetic, ring_scatter(): total = moved.astype(f32) + reduced[a % outer].astype(f32)  41.6 us
    psum x1, blocking collectives, body(): lax.psum(jnp.concatenate([grad_gain_one, grad_gain_two, grad_q_gain, grad...  40.3 us
    dot_general x2, matrix products, combine(): jnp.einsum('emct,emcd->mtd', pick, value, preferred_element_type=f32)  36.5 us
    dot_general x2, matrix products, dispatch(): return jnp.einsum('emct,mtd->emcd', pick, value, preferred_element_type=f32)  34.6 us
  transfers between devices with their start and end apart: 81, of which 27 were waited for; matrix products, arithmetic and copies ran while one was open for 57% of the time, Pallas kernels for 0%

profile of v1, /device:TPU:0, one launch (start us, length us, event | category | flops | bytes accessed | tf_op | source)
XLA Modules:
  0.0 1425.4 jit_solution(10694750832812037592)
XLA Ops:
  11.4 6.1 all_gather.6
  74.3 4.7 constant_dynamic-update-slice_fusion.35
  119.6 34.6 %collective-permute-done.3 = bf16[2,128,2048]{2,1,0:T(8,128)(2,1)S(1)} collective-permute-done((bf16[2,128,2048]{2,1,0:T(8,128)(2,1)}, bf16[2,128,2048]{2,1,0:T(8,128)(2,1)S(1)}, u32[]{:S(2)}, u32[]{:S(2)}) %collective-permute-start.3) | collective-permute-done | bytes 1048608 | tf_op jit(solution)/shard_map/ppermute | solution.py:28
  165.9 10.7 collective-permute-done.5
  189.0 13.5 collective-permute-done.6
  206.6 11.9 collective-permute-start.48
  218.4 14.0 convolution_convert_fusion.2
  244.6 7.9 fusion.142
  252.6 8.0 fusion.13
  262.8 7.6 fusion.74
  273.3 5.3 all-to-all-start
  278.7 13.1 collective-permute-done.47
  292.4 25.5 %collective-permute-done.49 = bf16[2,128,2048]{1,2,0:T(8,128)(2,1)} collective-permute-done((bf16[2,128,2048]{1,2,0:T(8,128)(2,1)}, bf16[2,128,2048]{1,2,0:T(8,128)(2,1)}, u32[]{:S(2)}, u32[]{:S(2)}) %collective-permute-start.49) | collective-permute-done | bytes 1048608 | tf_op jit(solution)/shard_map/ppermute | solution.py:28
  342.7 6.9 multiply_reduce_fusion.6
  357.9 56.2 %collective-permute-done.28 = bf16[4,512,1024]{2,1,0:T(8,128)(2,1)} collective-permute-done((bf16[4,512,1024]{2,1,0:T(8,128)(2,1)}, bf16[4,512,1024]{2,1,0:T(8,128)(2,1)}, u32[]{:S(2)}, u32[]{:S(2)}) %collective-permute-start.28) | collective-permute-done | bytes 4194336 | tf_op jit(solution)/shard_map/ppermute | solution.py:28
  414.1 80.4 %collective-permute-done.34 = bf16[4,512,1024]{2,1,0:T(8,128)(2,1)} collective-permute-done((bf16[4,512,1024]{2,1,0:T(8,128)(2,1)}, bf16[4,512,1024]{2,1,0:T(8,128)(2,1)}, u32[]{:S(2)}, u32[]{:S(2)}) %collective-permute-start.34) | collective-permute-done | bytes 4194336 | tf_op jit(solution)/shard_map/ppermute | solution.py:28
  494.5 18.2 %fusion = bf16[4,2,384,2048]{3,2,0,1:T(8,128)(2,1)} fusion(f32[4,2,384]{2,0,1:T(4,128)S(1)} %select_reduce_fusion, bf16[2,1024,2048]{1,2,0:T(8,128)(2,1)} %constant_dynamic-update-slice_fusion.40, s32[4,2,1024]{2,0,1:T(4,128)S(1)} %select_bitcast_fusion.9), kind=kOutput, calls=%fused_computation.16 | convolution fusion | flops 12900630528 | bytes 21016576 | tf_op jit(solution)/shard_map/emct,mtd->emcd/dot_general | solution.py:280
  529.0 4.8 constant_dynamic-update-slice_fusion.29
  544.2 5.7 collective-permute-done.23
  556.3 7.2 collective-permute-done.22
  568.5 8.2 collective-permute-done.25
  582.8 4.8 constant_dynamic-update-slice_fusion.28
  587.6 4.8 constant_dynamic-update-slice_fusion.36
  594.4 15.7 %collective-permute-done.26 = bf16[2,128,2048]{1,2,0:T(8,128)(2,1)S(1)} collective-permute-done((bf16[2,128,2048]{1,2,0:T(8,128)(2,1)}, bf16[2,128,2048]{1,2,0:T(8,128)(2,1)S(1)}, u32[]{:S(2)}, u32[]{:S(2)}) %collective-permute-start.26) | collective-permute-done | bytes 1048608 | tf_op jit(solution)/shard_map/ppermute | solution.py:28
  610.4 16.4 %convert_bitcast_fusion = bf16[4,2,384,2048]{2,3,0,1:T(8,128)(2,1)} fusion(bf16[2,1024,2048]{1,2,0:T(8,128)(2,1)S(1)} %constant_dynamic-update-slice_fusion.20, s32[4,2,1024]{2,0,1:T(4,128)S(1)} %select_bitcast_fusion.9), kind=kOutput, calls=%fused_computation.51 | convolution fusion | flops 12894339072 | bytes 21004288 | tf_op jit(solution)/shard_map/emct,mtd->emcd/dot_general | solution.py:280
  626.8 22.8 %fusion.3 = f32[4,2,384,1024]{3,2,1,0:T(8,128)} fusion(bf16[4,2048,1024]{2,1,0:T(8,128)(2,1)} %constant_dynamic-update-slice_fusion.32, bf16[4,2,384,2048]{2,3,0,1:T(8,128)(2,1)} %convert_bitcast_fusion), kind=kOutput, calls=%fused_computation.21 | convolution fusion | flops 12884901888 | bytes 41943040 | tf_op jit(solution)/shard_map/emcd,edf->emcf/dot_general | solution.py:292
  649.6 22.9 %fusion.5 = f32[4,2,384,1024]{3,2,1,0:T(8,128)} fusion(bf16[4,2048,1024]{2,1,0:T(8,128)(2,1)} %constant_dynamic-update-slice_fusion.28, bf16[4,2,384,2048]{2,3,0,1:T(8,128)(2,1)} %convert_bitcast_fusion), kind=kOutput, calls=%fused_computation.23 | convolution fusion | flops 12884901888 | bytes 41943040 | tf_op jit(solution)/shard_map/emcd,edf->emcf/dot_general | solution.py:291
  672.4 30.4 %multiply_convert_fusion.3 = (bf16[4,2,384,1024]{3,2,1,0:T(8,128)(2,1)}, bf16[4,2,384,1024]{3,2,1,0:T(8,128)(2,1)}, bf16[4,2,384,1024]{3,2,1,0:T(8,128)(2,1)}) fusion(f32[4,2,384,1024]{3,2,1,0:T(8,128)} %fusion.5, f32[4,2,384,1024]{3,2,1,0:T(8,128)} %fusion.3, bf16[4,2048,1024]{2,1,0:T(8,128)(2,1)} %constant_dynamic-update-slice_fusion.36, ...), kind=kOutput, calls=%fused_computation.44 | convolution fusion | flops 12932087808 | bytes 73400320 | tf_op jit(solution)/shard_map/emcd,edf->emcf/dot_general | solution.py:288
  702.9 19.6 %multiply_convert_fusion.13 = bf16[4,2,384,2048]{3,2,0,1:T(8,128)(2,1)} fusion(f32[4,2,384]{2,0,1:T(4,128)S(1)} %select_reduce_fusion, bf16[4,2048,1024]{2,1,0:T(8,128)(2,1)} %constant_dynamic-update-slice_fusion.36, bf16[4,2,384,1024]{3,2,1,0:T(8,128)(2,1)} %get-tuple-element.74), kind=kOutput, calls=%fused_computation.18.clone.clone.clone.clone.2 | convolution fusion | flops 12897484800 | bytes 35663872 | tf_op jit(solution)/shard_map/emcf,edf->emcd/dot_general | solution.py:314
  722.5 16.6 %bitcast_convert_fusion.4 = bf16[2,1024,2048]{2,1,0:T(8,128)(2,1)S(1)} fusion(s32[4,2,1024]{2,0,1:T(4,128)S(1)} %select_bitcast_fusion.9, bf16[4,2,384,2048]{3,2,0,1:T(8,128)(2,1)} %multiply_convert_fusion.13), kind=kOutput, calls=%fused_computation.26 | convolution fusion | flops 12892241920 | bytes 21004288 | tf_op jit(solution)/shard_map/emct,emcd->mtd/dot_general | solution.py:283
  743.5 21.8 %fusion.9 = f32[4,2,384,2048]{3,2,0,1:T(8,128)} fusion(bf16[4,2048,1024]{2,1,0:T(8,128)(2,1)} %constant_dynamic-update-slice_fusion.32, bf16[4,2,384,1024]{3,2,1,0:T(8,128)(2,1)} %get-tuple-element.72), kind=kOutput, calls=%fused_computation.29 | convolution fusion | flops 12884901888 | bytes 48234496 | tf_op jit(solution)/shard_map/emcf,edf->emcd/dot_general | solution.py:302
  765.3 22.0 %fusion.11 = f32[4,2,384,2048]{3,2,0,1:T(8,128)} fusion(bf16[4,2048,1024]{2,1,0:T(8,128)(2,1)} %constant_dynamic-update-slice_fusion.28, bf16[4,2,384,1024]{3,2,1,0:T(8,128)(2,1)} %get-tuple-element.73), kind=kOutput, calls=%fused_computation.31 | convolution fusion | flops 12884901888 | bytes 48234496 | tf_op jit(solution)/shard_map/emcf,edf->emcd/dot_general | solution.py:300
  787.3 19.9 %bitcast_convert_fusion.3 = bf16[2,1024,2048]{2,1,0:T(8,128)(2,1)S(1)} fusion(f32[4,2,384,2048]{3,2,0,1:T(8,128)} %fusion.11, f32[4,2,384,2048]{3,2,0,1:T(8,128)} %fusion.9, s32[4,2,1024]{2,0,1:T(4,128)S(1)} %select_bitcast_fusion.9), kind=kOutput, calls=%fused_computation.25 | convolution fusion | flops 12904824832 | bytes 58753024 | tf_op jit(solution)/shard_map/emct,emcd->mtd/dot_general | solution.py:283
  814.1 19.6 %bitcast_convert_fusion = bf16[4,2048,1024]{2,1,0:T(8,128)(2,1)} fusion(bf16[4,2,384,2048]{3,2,0,1:T(8,128)(2,1)} %fusion, bf16[4,2,384,1024]{3,2,1,0:T(8,128)(2,1)} %get-tuple-element.74), kind=kOutput, calls=%fused_computation.12 | convolution fusion | flops 12893290496 | bytes 35651584 | tf_op jit(solution)/shard_map/emcd,emcf->edf/dot_general | solution.py:306
  852.2 20.5 %bitcast_convert_fusion.1 = bf16[4,2048,1024]{2,1,0:T(8,128)(2,1)} fusion(bf16[4,2,384,2048]{2,3,0,1:T(8,128)(2,1)} %convert_bitcast_fusion, bf16[4,2,384,1024]{3,2,1,0:T(8,128)(2,1)} %get-tuple-element.72), kind=kOutput, calls=%fused_computation.13 | convolution fusion | flops 12893290496 | bytes 35651584 | tf_op jit(solution)/shard_map/emcd,emcf->edf/dot_general | solution.py:306
  886.1 10.5 collective-permute-done.51
  900.4 20.1 %bitcast_convert_fusion.2 = bf16[4,2048,1024]{2,1,0:T(8,128)(2,1)} fusion(bf16[4,2,384,2048]{2,3,0,1:T(8,128)(2,1)} %convert_bitcast_fusion, bf16[4,2,384,1024]{3,2,1,0:T(8,128)(2,1)} %get-tuple-element.73), kind=kOutput, calls=%fused_computation.14 | convolution fusion | flops 12893290496 | bytes 35651584 | tf_op jit(solution)/shard_map/emcd,emcf->edf/dot_general | solution.py:306
  932.5 9.0 collective-permute-done.53
  945.4 6.1 slice_bitcast_fusion.1
  954.1 9.9 collective-permute-done.41
  972.3 10.0 collective-permute-done.55
  1013.0 6.2 slice_bitcast_fusion.5
  1019.7 6.0 slice_bitcast_fusion.9
  1025.7 7.6 fusion.27
  1042.4 6.4 all-to-all-start.2
  1052.2 11.1 multiply_reduce_fusion
  1063.3 12.6 multiply_convert_fusion.1
  1101.7 9.5 fusion.75
  1111.3 11.0 convolution_convert_fusion
  1122.3 5.7 fusion.136
  1132.2 7.6 fusion.29
  1140.3 7.6 fusion.31
  1161.5 11.4 bitcast_convert_fusion.5
  1180.8 4.9 collective-permute-done.58
  1189.8 11.1 convert_add_fusion.6
  1200.8 12.2 copy.488
  1214.1 6.0 fusion.143
  1224.4 13.2 collective-permute-done.60
  1240.8 11.1 convert_add_fusion.7
  1255.1 68.4 %collective-permute-done.68 = bf16[4,512,1024]{2,1,0:T(8,128)(2,1)} collective-permute-done((bf16[4,512,1024]{2,1,0:T(8,128)(2,1)}, bf16[4,512,1024]{2,1,0:T(8,128)(2,1)}, u32[]{:S(2)}, u32[]{:S(2)}) %collective-permute-start.68) | collective-permute-done | bytes 4194336 | tf_op jit(solution)/shard_map/ppermute | solution.py:28
  1323.5 11.1 convert_add_fusion.8
  1347.6 4.8 all-to-all-start.3
  1360.9 40.3 %psum.7 = f32[4352]{0:T(1024)S(1)} all-reduce(f32[4352]{0:T(1024)S(1)} %pad_maximum_fusion.13), channel_id=1, replica_groups=mesh['fsdp'=4,'seq'=8] {'fsdp','seq'}, use_global_device_ids=true, to_apply=%region_24.29 | all-reduce | flops 4352 | bytes 34816 | tf_op jit(solution)/shard_map/psum | solution.py:373
  1404.5 4.9 fusion.68
  (611 shorter events, 445.0 us)
Async XLA Ops:
  35.8 83.2 %collective-permute-start = (bf16[2,128,2048]{2,1,0:T(8,128)(2,1)}, bf16[2,128,2048]{2,1,0:T(8,128)(2,1)}, u32[]{:S(2)}, u32[]{:S(2)}) collective-permute-start(bf16[2,128,2048]{2,1,0:T(8,128)(2,1)} %bitcast.194), channel_id=1, source_target_pairs={{0,1},{1,0},{2,3},{3,2},{4,5},{5,4},{6,7},{7,6},{8,9},{9,8},{10,11... | collective-permute-start | bytes 3145736 | tf_op jit(solution)/shard_map/ppermute | solution.py:28
  37.8 79.4 %collective-permute-start.1 = (bf16[2,128,2048]{2,1,0:T(8,128)(2,1)}, bf16[2,128,2048]{2,1,0:T(8,128)(2,1)}, u32[]{:S(2)}, u32[]{:S(2)}) collective-permute-start(bf16[2,128,2048]{2,1,0:T(8,128)(2,1)} %bitcast.194), channel_id=1, source_target_pairs={{0,2},{1,3},{2,4},{3,5},{4,6},{5,7},{6,0},{7,1},{8,10},{9,11},{10,... | collective-permute-start | bytes 3145736 | tf_op jit(solution)/shard_map/ppermute | solution.py:28
  40.0 58.2 %collective-permute-start.14 = (f32[2,128,16]{1,2,0:T(8,128)}, f32[2,128,16]{1,2,0:T(8,128)}, u32[]{:S(2)}, u32[]{:S(2)}) collective-permute-start(f32[2,128,16]{1,2,0:T(8,128)} %get-tuple-element.134), channel_id=1, source_target_pairs={{0,2},{1,3},{2,4},{3,5},{4,6},{5,7},{6,0},{7,1},{8,10},{9,11},{10,... | collective-permute-start | bytes 49160 | tf_op jit(solution)/shard_map/ppermute | solution.py:28
  41.6 57.1 %collective-permute-start.13 = (f32[2,128,16]{1,2,0:T(8,128)}, f32[2,128,16]{1,2,0:T(8,128)}, u32[]{:S(2)}, u32[]{:S(2)}) collective-permute-start(f32[2,128,16]{1,2,0:T(8,128)} %get-tuple-element.134), channel_id=1, source_target_pairs={{0,1},{1,0},{2,3},{3,2},{4,5},{5,4},{6,7},{7,6},{8,9},{9,8},{10,11... | collective-permute-start | bytes 49160 | tf_op jit(solution)/shard_map/ppermute | solution.py:28
  44.4 114.9 %collective-permute-start.43 = (bf16[2,128,2048]{1,2,0:T(8,128)(2,1)}, bf16[2,128,2048]{1,2,0:T(8,128)(2,1)}, u32[]{:S(2)}, u32[]{:S(2)}) collective-permute-start(bf16[2,128,2048]{1,2,0:T(8,128)(2,1)} %bitcast.479), channel_id=1, source_target_pairs={{0,1},{1,0},{2,3},{3,2},{4,5},{5,4},{6,7},{7,6},{8,9},{9,8},{10,11... | collective-permute-start | bytes 3145736 | tf_op jit(solution)/shard_map/ppermute | solution.py:28
  108.2 57.2 %collective-permute-start.44 = (bf16[2,128,2048]{1,2,0:T(8,128)(2,1)S(1)}, bf16[2,128,2048]{1,2,0:T(8,128)(2,1)}, u32[]{:S(2)}, u32[]{:S(2)}) collective-permute-start(bf16[2,128,2048]{1,2,0:T(8,128)(2,1)S(1)} %bitcast.481), channel_id=1, source_target_pairs={{0,2},{1,3},{2,4},{3,5},{4,6},{5,7},{6,0},{7,1},{8,10},{9,11},{10,... | collective-permute-start | bytes 3145736 | tf_op jit(solution)/shard_map/ppermute | solution.py:28
  115.5 49.9 %collective-permute-start.8 = (bf16[512,768]{0,1:T(8,128)(2,1)}, bf16[512,768]{0,1:T(8,128)(2,1)}, u32[]{:S(2)}, u32[]{:S(2)}) collective-permute-start(bf16[512,768]{0,1:T(8,128)(2,1)} %pad_maximum_fusion.8), channel_id=1, source_target_pairs={{0,16},{8,24},{16,0},{24,8},{1,17},{9,25},{17,1},{25,9},{2,18},{10... | collective-permute-start | bytes 2359304 | tf_op jit(solution)/shard_map/ppermute | solution.py:28
  117.2 36.9 %collective-permute-start.3 = (bf16[2,128,2048]{2,1,0:T(8,128)(2,1)}, bf16[2,128,2048]{2,1,0:T(8,128)(2,1)S(1)}, u32[]{:S(2)}, u32[]{:S(2)}) collective-permute-start(bf16[2,128,2048]{2,1,0:T(8,128)(2,1)} %collective-permute-done.1), channel_id=1, source_target_pairs={{0,2},{1,3},{2,4},{3,5},{4,6},{5,7},{6,0},{7,1},{8,10},{9,11},{10,... | collective-permute-start | bytes 3145736 | tf_op jit(solution)/shard_map/ppermute | solution.py:28
  119.0 61.4 %collective-permute-start.2 = (bf16[2,128,2048]{2,1,0:T(8,128)(2,1)}, bf16[2,128,2048]{2,1,0:T(8,128)(2,1)S(1)}, u32[]{:S(2)}, u32[]{:S(2)}) collective-permute-start(bf16[2,128,2048]{2,1,0:T(8,128)(2,1)} %collective-permute-done.1), channel_id=1, source_target_pairs={{0,1},{1,0},{2,3},{3,2},{4,5},{5,4},{6,7},{7,6},{8,9},{9,8},{10,11... | collective-permute-start | bytes 3145736 | tf_op jit(solution)/shard_map/ppermute | solution.py:28
  165.4 38.1 %collective-permute-start.7 = (bf16[512,768]{0,1:T(8,128)(2,1)S(1)}, bf16[512,768]{0,1:T(8,128)(2,1)S(1)}, u32[]{:S(2)}, u32[]{:S(2)}) collective-permute-start(bf16[512,768]{0,1:T(8,128)(2,1)S(1)} %copy-done.61), channel_id=1, source_target_pairs={{0,8},{8,0},{16,24},{24,16},{1,9},{9,1},{17,25},{25,17},{2,10},{10... | collective-permute-start | bytes 2359304 | tf_op jit(solution)/shard_map/ppermute | solution.py:28
  165.4 39.6 %collective-permute-start.9 = (bf16[512,768]{0,1:T(8,128)(2,1)}, bf16[512,768]{0,1:T(8,128)(2,1)S(1)}, u32[]{:S(2)}, u32[]{:S(2)}) collective-permute-start(bf16[512,768]{0,1:T(8,128)(2,1)} %collective-permute-done.8), channel_id=1, source_target_pairs={{0,8},{8,0},{16,24},{24,16},{1,9},{9,1},{17,25},{25,17},{2,10},{10... | collective-permute-start | bytes 2359304 | tf_op jit(solution)/shard_map/ppermute | solution.py:28
  185.4 75.2 %collective-permute-start.11 = (bf16[512,2048]{1,0:T(8,128)(2,1)}, bf16[512,2048]{1,0:T(8,128)(2,1)}, u32[]{:S(2)}, u32[]{:S(2)}) collective-permute-start(bf16[512,2048]{1,0:T(8,128)(2,1)} %param.33), channel_id=1, source_target_pairs={{0,16},{8,24},{16,0},{24,8},{1,17},{9,25},{17,1},{25,9},{2,18},{10... | collective-permute-start | bytes 6291464 | tf_op jit(solution)/shard_map/ppermute | solution.py:28
  202.5 58.7 %collective-permute-start.10 = (bf16[512,2048]{1,0:T(8,128)(2,1)}, bf16[512,2048]{1,0:T(8,128)(2,1)}, u32[]{:S(2)}, u32[]{:S(2)}) collective-permute-start(bf16[512,2048]{1,0:T(8,128)(2,1)} %param.33), channel_id=1, source_target_pairs={{0,8},{8,0},{16,24},{24,16},{1,9},{9,1},{17,25},{25,17},{2,10},{10... | collective-permute-start | bytes 6291464 | tf_op jit(solution)/shard_map/ppermute | solution.py:28
  203.5 139.1 %collective-permute-start.31 = (bf16[4,512,1024]{2,1,0:T(8,128)(2,1)}, bf16[4,512,1024]{2,1,0:T(8,128)(2,1)}, u32[]{:S(2)}, u32[]{:S(2)}) collective-permute-start(bf16[4,512,1024]{2,1,0:T(8,128)(2,1)} %param.36), channel_id=1, source_target_pairs={{0,16},{8,24},{16,0},{24,8},{1,17},{9,25},{17,1},{25,9},{2,18},{10... | collective-permute-start | bytes 12582920 | tf_op jit(solution)/shard_map/ppermute | solution.py:28
  205.0 73.6 %collective-permute-start.45 = (bf16[2,128,2048]{1,2,0:T(8,128)(2,1)}, bf16[2,128,2048]{1,2,0:T(8,128)(2,1)}, u32[]{:S(2)}, u32[]{:S(2)}) collective-permute-start(bf16[2,128,2048]{1,2,0:T(8,128)(2,1)} %collective-permute-done.44), channel_id=1, source_target_pairs={{0,1},{1,0},{2,3},{3,2},{4,5},{5,4},{6,7},{7,6},{8,9},{9,8},{10,11... | collective-permute-start | bytes 3145736 | tf_op jit(solution)/shard_map/ppermute | solution.py:28
  206.6 54.6 %collective-permute-start.48 = (bf16[2,128,2048]{1,2,0:T(8,128)(2,1)}, bf16[2,128,2048]{1,2,0:T(8,128)(2,1)}, u32[]{:S(2)}, u32[]{:S(2)}) collective-permute-start(bf16[2,128,2048]{1,2,0:T(8,128)(2,1)} %collective-permute-done.46), channel_id=1, source_target_pairs={{0,2},{1,3},{2,4},{3,5},{4,6},{5,7},{6,0},{7,1},{8,10},{9,11},{10,... | collective-permute-start | bytes 3145736 | tf_op jit(solution)/shard_map/ppermute | solution.py:28
  260.6 31.3 %collective-permute-start.47 = (bf16[2,128,2048]{1,2,0:T(8,128)(2,1)}, bf16[2,128,2048]{1,2,0:T(8,128)(2,1)}, u32[]{:S(2)}, u32[]{:S(2)}) collective-permute-start(bf16[2,128,2048]{1,2,0:T(8,128)(2,1)} %collective-permute-done.46), channel_id=1, source_target_pairs={{0,1},{1,0},{2,3},{3,2},{4,5},{5,4},{6,7},{7,6},{8,9},{9,8},{10,11... | collective-permute-start | bytes 3145736 | tf_op jit(solution)/shard_map/ppermute | solution.py:28
  261.2 31.2 %collective-permute-start.12 = (bf16[512,2048]{1,0:T(8,128)(2,1)}, bf16[512,2048]{1,0:T(8,128)(2,1)}, u32[]{:S(2)}, u32[]{:S(2)}) collective-permute-start(bf16[512,2048]{1,0:T(8,128)(2,1)} %collective-permute-done.11), channel_id=1, source_target_pairs={{0,8},{8,0},{16,24},{24,16},{1,9},{9,1},{17,25},{25,17},{2,10},{10... | collective-permute-start | bytes 6291464 | tf_op jit(solution)/shard_map/ppermute | solution.py:28
  261.2 56.7 %collective-permute-start.49 = (bf16[2,128,2048]{1,2,0:T(8,128)(2,1)}, bf16[2,128,2048]{1,2,0:T(8,128)(2,1)}, u32[]{:S(2)}, u32[]{:S(2)}) collective-permute-start(bf16[2,128,2048]{1,2,0:T(8,128)(2,1)} %collective-permute-done.48), channel_id=1, source_target_pairs={{0,1},{1,0},{2,3},{3,2},{4,5},{5,4},{6,7},{7,6},{8,9},{9,8},{10,11... | collective-permute-start | bytes 3145736 | tf_op jit(solution)/shard_map/ppermute | solution.py:28
  273.3 66.0 %all-to-all-start = ((bf16[8,2,128,256]{3,2,1,0:T(8,128)(2,1)}), bf16[8,2,128,256]{3,2,1,0:T(8,128)(2,1)S(1)}, u32[]{:S(2)}, u32[]{:S(2)}) async-start(bf16[8,2,128,256]{3,2,1,0:T(8,128)(2,1)} %broadcast_select_fusion), calls=%async_computation | async-start | bytes 2097152 | tf_op jit(solution)/shard_map/all_to_all | solution.py:245
  278.6 922.2 %all-gather.2.cloned.1.call-start = ((), (), s32[]{:S(2)}) async-start(), calls=%async_computation.4 | async-start | bytes 9437184 | tf_op jit(solution)/shard_map/all_gather | solution.py:247
  278.7 78.7 %collective-permute-start.30 = (bf16[4,512,1024]{2,1,0:T(8,128)(2,1)}, bf16[4,512,1024]{2,1,0:T(8,128)(2,1)}, u32[]{:S(2)}, u32[]{:S(2)}) collective-permute-start(bf16[4,512,1024]{2,1,0:T(8,128)(2,1)} %param.36), channel_id=1, source_target_pairs={{0,8},{8,0},{16,24},{24,16},{1,9},{9,1},{17,25},{25,17},{2,10},{10... | collective-permute-start | bytes 12582920 | tf_op jit(solution)/shard_map/ppermute | solution.py:28
  291.9 122.2 %collective-permute-start.28 = (bf16[4,512,1024]{2,1,0:T(8,128)(2,1)}, bf16[4,512,1024]{2,1,0:T(8,128)(2,1)}, u32[]{:S(2)}, u32[]{:S(2)}) collective-permute-start(bf16[4,512,1024]{2,1,0:T(8,128)(2,1)} %param.35), channel_id=1, source_target_pairs={{0,16},{8,24},{16,0},{24,8},{1,17},{9,25},{17,1},{25,9},{2,18},{10... | collective-permute-start | bytes 12582920 | tf_op jit(solution)/shard_map/ppermute | solution.py:28
  292.4 202.1 %collective-permute-start.27 = (bf16[4,512,1024]{2,1,0:T(8,128)(2,1)}, bf16[4,512,1024]{2,1,0:T(8,128)(2,1)}, u32[]{:S(2)}, u32[]{:S(2)}) collective-permute-start(bf16[4,512,1024]{2,1,0:T(8,128)(2,1)} %param.35), channel_id=1, source_target_pairs={{0,8},{8,0},{16,24},{24,16},{1,9},{9,1},{17,25},{25,17},{2,10},{10... | collective-permute-start | bytes 12582920 | tf_op jit(solution)/shard_map/ppermute | solution.py:28
  317.9 176.5 %collective-permute-start.34 = (bf16[4,512,1024]{2,1,0:T(8,128)(2,1)}, bf16[4,512,1024]{2,1,0:T(8,128)(2,1)}, u32[]{:S(2)}, u32[]{:S(2)}) collective-permute-start(bf16[4,512,1024]{2,1,0:T(8,128)(2,1)} %param.37), channel_id=1, source_target_pairs={{0,16},{8,24},{16,0},{24,8},{1,17},{9,25},{17,1},{25,9},{2,18},{10... | collective-permute-start | bytes 12582920 | tf_op jit(solution)/shard_map/ppermute | solution.py:28
  342.7 170.0 %collective-permute-start.33 = (bf16[4,512,1024]{2,1,0:T(8,128)(2,1)}, bf16[4,512,1024]{2,1,0:T(8,128)(2,1)}, u32[]{:S(2)}, u32[]{:S(2)}) collective-permute-start(bf16[4,512,1024]{2,1,0:T(8,128)(2,1)} %param.37), channel_id=1, source_target_pairs={{0,8},{8,0},{16,24},{24,16},{1,9},{9,1},{17,25},{25,17},{2,10},{10... | collective-permute-start | bytes 12582920 | tf_op jit(solution)/shard_map/ppermute | solution.py:28
  357.4 220.8 %collective-permute-start.32 = (bf16[4,512,1024]{2,1,0:T(8,128)(2,1)}, bf16[4,512,1024]{2,1,0:T(8,128)(2,1)}, u32[]{:S(2)}, u32[]{:S(2)}) collective-permute-start(bf16[4,512,1024]{2,1,0:T(8,128)(2,1)} %collective-permute-done.31), channel_id=1, source_target_pairs={{0,8},{8,0},{16,24},{24,16},{1,9},{9,1},{17,25},{25,17},{2,10},{10... | collective-permute-start | bytes 12582920 | tf_op jit(solution)/shard_map/ppermute | solution.py:28
  414.1 168.7 %collective-permute-start.29 = (bf16[4,512,1024]{2,1,0:T(8,128)(2,1)}, bf16[4,512,1024]{2,1,0:T(8,128)(2,1)}, u32[]{:S(2)}, u32[]{:S(2)}) collective-permute-start(bf16[4,512,1024]{2,1,0:T(8,128)(2,1)} %collective-permute-done.28), channel_id=1, source_target_pairs={{0,8},{8,0},{16,24},{24,16},{1,9},{9,1},{17,25},{25,17},{2,10},{10... | collective-permute-start | bytes 12582920 | tf_op jit(solution)/shard_map/ppermute | solution.py:28
  494.5 93.2 %collective-permute-start.35 = (bf16[4,512,1024]{2,1,0:T(8,128)(2,1)}, bf16[4,512,1024]{2,1,0:T(8,128)(2,1)}, u32[]{:S(2)}, u32[]{:S(2)}) collective-permute-start(bf16[4,512,1024]{2,1,0:T(8,128)(2,1)} %collective-permute-done.34), channel_id=1, source_target_pairs={{0,8},{8,0},{16,24},{24,16},{1,9},{9,1},{17,25},{25,17},{2,10},{10... | collective-permute-start | bytes 12582920 | tf_op jit(solution)/shard_map/ppermute | solution.py:28
  494.5 28.0 %collective-permute-start.21 = (bf16[2,128,2048]{1,2,0:T(8,128)(2,1)S(1)}, bf16[2,128,2048]{1,2,0:T(8,128)(2,1)}, u32[]{:S(2)}, u32[]{:S(2)}) collective-permute-start(bf16[2,128,2048]{1,2,0:T(8,128)(2,1)S(1)} %copy.422), channel_id=1, source_target_pairs={{0,2},{1,3},{2,4},{3,5},{4,6},{5,7},{6,0},{7,1},{8,10},{9,11},{10,... | collective-permute-start | bytes 3145736 | tf_op jit(solution)/shard_map/ppermute | solution.py:28
  522.5 27.4 %collective-permute-start.23 = (bf16[2,128,2048]{1,2,0:T(8,128)(2,1)}, bf16[2,128,2048]{1,2,0:T(8,128)(2,1)}, u32[]{:S(2)}, u32[]{:S(2)}) collective-permute-start(bf16[2,128,2048]{1,2,0:T(8,128)(2,1)} %collective-permute-done.21), channel_id=1, source_target_pairs={{0,2},{1,3},{2,4},{3,5},{4,6},{5,7},{6,0},{7,1},{8,10},{9,11},{10,... | collective-permute-start | bytes 3145736 | tf_op jit(solution)/shard_map/ppermute | solution.py:28
  563.5 28.9 %collective-permute-start.24 = (bf16[2,128,2048]{1,2,0:T(8,128)(2,1)}, bf16[2,128,2048]{1,2,0:T(8,128)(2,1)S(1)}, u32[]{:S(2)}, u32[]{:S(2)}) collective-permute-start(bf16[2,128,2048]{1,2,0:T(8,128)(2,1)} %collective-permute-done.23), channel_id=1, source_target_pairs={{0,1},{1,0},{2,3},{3,2},{4,5},{5,4},{6,7},{7,6},{8,9},{9,8},{10,11... | collective-permute-start | bytes 3145736 | tf_op jit(solution)/shard_map/ppermute | solution.py:28
  576.7 33.4 %collective-permute-start.26 = (bf16[2,128,2048]{1,2,0:T(8,128)(2,1)}, bf16[2,128,2048]{1,2,0:T(8,128)(2,1)S(1)}, u32[]{:S(2)}, u32[]{:S(2)}) collective-permute-start(bf16[2,128,2048]{1,2,0:T(8,128)(2,1)} %collective-permute-done.25), channel_id=1, source_target_pairs={{0,1},{1,0},{2,3},{3,2},{4,5},{5,4},{6,7},{7,6},{8,9},{9,8},{10,11... | collective-permute-start | bytes 3145736 | tf_op jit(solution)/shard_map/ppermute | solution.py:28
  743.0 100.1 %collective-permute-start.36 = (bf16[2,128,2048]{1,2,0:T(8,128)(2,1)}, bf16[2,128,2048]{1,2,0:T(8,128)(2,1)}, u32[]{:S(2)}, u32[]{:S(2)}) collective-permute-start(bf16[2,128,2048]{1,2,0:T(8,128)(2,1)} %bitcast.40), channel_id=1, source_target_pairs={{0,1},{1,0},{2,3},{3,2},{4,5},{5,4},{6,7},{7,6},{8,9},{9,8},{10,11... | collective-permute-start | bytes 3145736 | tf_op jit(solution)/shard_map/ppermute | solution.py:28
  812.6 36.1 %collective-permute-start.50 = (bf16[2,128,2048]{1,2,0:T(8,128)(2,1)}, bf16[2,128,2048]{1,2,0:T(8,128)(2,1)}, u32[]{:S(2)}, u32[]{:S(2)}) collective-permute-start(bf16[2,128,2048]{1,2,0:T(8,128)(2,1)} %bitcast.505), channel_id=1, source_target_pairs={{0,1},{1,0},{2,3},{3,2},{4,5},{5,4},{6,7},{7,6},{8,9},{9,8},{10,11... | collective-permute-start | bytes 3145736 | tf_op jit(solution)/shard_map/ppermute | solution.py:28
  837.2 41.7 %collective-permute-start.38 = (bf16[2,128,2048]{1,2,0:T(8,128)(2,1)}, bf16[2,128,2048]{1,2,0:T(8,128)(2,1)}, u32[]{:S(2)}, u32[]{:S(2)}) collective-permute-start(bf16[2,128,2048]{1,2,0:T(8,128)(2,1)} %bitcast.503), channel_id=1, source_target_pairs={{0,1},{1,0},{2,3},{3,2},{4,5},{5,4},{6,7},{7,6},{8,9},{9,8},{10,11... | collective-permute-start | bytes 3145736 | tf_op jit(solution)/shard_map/ppermute | solution.py:28
  841.6 44.5 %collective-permute-start.52 = (bf16[2,128,2048]{1,2,0:T(8,128)(2,1)}, bf16[2,128,2048]{1,2,0:T(8,128)(2,1)}, u32[]{:S(2)}, u32[]{:S(2)}) collective-permute-start(bf16[2,128,2048]{1,2,0:T(8,128)(2,1)} %bitcast.499), channel_id=1, source_target_pairs={{0,1},{1,0},{2,3},{3,2},{4,5},{5,4},{6,7},{7,6},{8,9},{9,8},{10,11... | collective-permute-start | bytes 3145736 | tf_op jit(solution)/shard_map/ppermute | solution.py:28
  845.9 34.5 %collective-permute-start.37 = (bf16[2,128,2048]{1,2,0:T(8,128)(2,1)}, bf16[2,128,2048]{1,2,0:T(8,128)(2,1)}, u32[]{:S(2)}, u32[]{:S(2)}) collective-permute-start(bf16[2,128,2048]{1,2,0:T(8,128)(2,1)} %fusion.63), channel_id=1, source_target_pairs={{0,2},{1,3},{2,4},{3,5},{4,6},{5,7},{6,0},{7,1},{8,10},{9,11},{10,... | collective-permute-start | bytes 3145736 | tf_op jit(solution)/shard_map/ppermute | solution.py:28
  851.1 45.5 %collective-permute-start.51 = (bf16[2,128,2048]{1,2,0:T(8,128)(2,1)}, bf16[2,128,2048]{1,2,0:T(8,128)(2,1)}, u32[]{:S(2)}, u32[]{:S(2)}) collective-permute-start(bf16[2,128,2048]{1,2,0:T(8,128)(2,1)} %fusion.59), channel_id=1, source_target_pairs={{0,2},{1,3},{2,4},{3,5},{4,6},{5,7},{6,0},{7,1},{8,10},{9,11},{10,... | collective-permute-start | bytes 3145736 | tf_op jit(solution)/shard_map/ppermute | solution.py:28
  875.4 52.3 %collective-permute-start.40 = (bf16[2,128,2048]{1,2,0:T(8,128)(2,1)}, bf16[2,128,2048]{1,2,0:T(8,128)(2,1)}, u32[]{:S(2)}, u32[]{:S(2)}) collective-permute-start(bf16[2,128,2048]{1,2,0:T(8,128)(2,1)} %bitcast.500), channel_id=1, source_target_pairs={{0,1},{1,0},{2,3},{3,2},{4,5},{5,4},{6,7},{7,6},{8,9},{9,8},{10,11... | collective-permute-start | bytes 3145736 | tf_op jit(solution)/shard_map/ppermute | solution.py:28
  878.9 53.6 %collective-permute-start.54 = (bf16[2,128,2048]{1,2,0:T(8,128)(2,1)}, bf16[2,128,2048]{1,2,0:T(8,128)(2,1)}, u32[]{:S(2)}, u32[]{:S(2)}) collective-permute-start(bf16[2,128,2048]{1,2,0:T(8,128)(2,1)} %bitcast.497), channel_id=1, source_target_pairs={{0,1},{1,0},{2,3},{3,2},{4,5},{5,4},{6,7},{7,6},{8,9},{9,8},{10,11... | collective-permute-start | bytes 3145736 | tf_op jit(solution)/shard_map/ppermute | solution.py:28
  883.6 44.5 %collective-permute-start.39 = (bf16[2,128,2048]{1,2,0:T(8,128)(2,1)}, bf16[2,128,2048]{1,2,0:T(8,128)(2,1)}, u32[]{:S(2)}, u32[]{:S(2)}) collective-permute-start(bf16[2,128,2048]{1,2,0:T(8,128)(2,1)} %add_convert_fusion.12), channel_id=1, source_target_pairs={{0,2},{1,3},{2,4},{3,5},{4,6},{5,7},{6,0},{7,1},{8,10},{9,11},{10,... | collective-permute-start | bytes 3145736 | tf_op jit(solution)/shard_map/ppermute | solution.py:28
  899.5 42.0 %collective-permute-start.53 = (bf16[2,128,2048]{1,2,0:T(8,128)(2,1)}, bf16[2,128,2048]{1,2,0:T(8,128)(2,1)}, u32[]{:S(2)}, u32[]{:S(2)}) collective-permute-start(bf16[2,128,2048]{1,2,0:T(8,128)(2,1)} %add_convert_fusion.10), channel_id=1, source_target_pairs={{0,2},{1,3},{2,4},{3,5},{4,6},{5,7},{6,0},{7,1},{8,10},{9,11},{10,... | collective-permute-start | bytes 3145736 | tf_op jit(solution)/shard_map/ppermute | solution.py:28
  923.2 30.3 %collective-permute-start.42 = (bf16[2,128,2048]{1,2,0:T(8,128)(2,1)}, bf16[2,128,2048]{1,2,0:T(8,128)(2,1)}, u32[]{:S(2)}, u32[]{:S(2)}) collective-permute-start(bf16[2,128,2048]{1,2,0:T(8,128)(2,1)} %bitcast.501), channel_id=1, source_target_pairs={{0,1},{1,0},{2,3},{3,2},{4,5},{5,4},{6,7},{7,6},{8,9},{9,8},{10,11... | collective-permute-start | bytes 3145736 | tf_op jit(solution)/shard_map/ppermute | solution.py:28
  927.6 44.6 %collective-permute-start.56 = (bf16[2,128,2048]{1,2,0:T(8,128)(2,1)}, bf16[2,128,2048]{1,2,0:T(8,128)(2,1)}, u32[]{:S(2)}, u32[]{:S(2)}) collective-permute-start(bf16[2,128,2048]{1,2,0:T(8,128)(2,1)} %bitcast.498), channel_id=1, source_target_pairs={{0,1},{1,0},{2,3},{3,2},{4,5},{5,4},{6,7},{7,6},{8,9},{9,8},{10,11... | collective-permute-start | bytes 3145736 | tf_op jit(solution)/shard_map/ppermute | solution.py:28
  931.4 32.6 %collective-permute-start.41 = (bf16[2,128,2048]{1,2,0:T(8,128)(2,1)}, bf16[2,128,2048]{1,2,0:T(8,128)(2,1)}, u32[]{:S(2)}, u32[]{:S(2)}) collective-permute-start(bf16[2,128,2048]{1,2,0:T(8,128)(2,1)} %add_convert_fusion.11), channel_id=1, source_target_pairs={{0,2},{1,3},{2,4},{3,5},{4,6},{5,7},{6,0},{7,1},{8,10},{9,11},{10,... | collective-permute-start | bytes 3145736 | tf_op jit(solution)/shard_map/ppermute | solution.py:28
  944.4 37.8 %collective-permute-start.55 = (bf16[2,128,2048]{1,2,0:T(8,128)(2,1)}, bf16[2,128,2048]{1,2,0:T(8,128)(2,1)}, u32[]{:S(2)}, u32[]{:S(2)}) collective-permute-start(bf16[2,128,2048]{1,2,0:T(8,128)(2,1)} %add_convert_fusion.9), channel_id=1, source_target_pairs={{0,2},{1,3},{2,4},{3,5},{4,6},{5,7},{6,0},{7,1},{8,10},{9,11},{10,... | collective-permute-start | bytes 3145736 | tf_op jit(solution)/shard_map/ppermute | solution.py:28
  951.5 74.2 %collective-permute-start.73 = (bf16[4,512,1024]{2,1,0:T(8,128)(2,1)}, bf16[4,512,1024]{2,1,0:T(8,128)(2,1)}, u32[]{:S(2)}, u32[]{:S(2)}) collective-permute-start(bf16[4,512,1024]{2,1,0:T(8,128)(2,1)} %get-tuple-element.76), channel_id=1, source_target_pairs={{0,8},{8,0},{16,24},{24,16},{1,9},{9,1},{17,25},{25,17},{2,10},{10... | collective-permute-start | bytes 12582920 | tf_op jit(solution)/shard_map/ppermute | solution.py:28
  953.5 206.6 %collective-permute-start.75 = (bf16[4,512,1024]{2,1,0:T(8,128)(2,1)}, bf16[4,512,1024]{2,1,0:T(8,128)(2,1)}, u32[]{:S(2)}, u32[]{:S(2)}) collective-permute-start(bf16[4,512,1024]{2,1,0:T(8,128)(2,1)} %get-tuple-element.75), channel_id=1, source_target_pairs={{0,8},{8,0},{16,24},{24,16},{1,9},{9,1},{17,25},{25,17},{2,10},{10... | collective-permute-start | bytes 12582920 | tf_op jit(solution)/shard_map/ppermute | solution.py:28
  1008.7 33.6 %all-to-all-start.1 = ((bf16[8,2,128,256]{3,2,1,0:T(8,128)(2,1)}), bf16[8,2,128,256]{3,2,1,0:T(8,128)(2,1)}, u32[]{:S(2)}, u32[]{:S(2)}) async-start(bf16[8,2,128,256]{3,2,1,0:T(8,128)(2,1)} %bitcast.441), calls=%async_computation.1 | async-start | bytes 2097152 | tf_op jit(solution)/shard_map/all_to_all | solution.py:331
  1019.2 111.0 %collective-permute-start.70 = (bf16[4,512,1024]{2,1,0:T(8,128)(2,1)}, bf16[4,512,1024]{2,1,0:T(8,128)(2,1)}, u32[]{:S(2)}, u32[]{:S(2)}) collective-permute-start(bf16[4,512,1024]{2,1,0:T(8,128)(2,1)} %get-tuple-element.78), channel_id=1, source_target_pairs={{0,8},{8,0},{16,24},{24,16},{1,9},{9,1},{17,25},{25,17},{2,10},{10... | collective-permute-start | bytes 12582920 | tf_op jit(solution)/shard_map/ppermute | solution.py:28
  1019.2 220.1 %collective-permute-start.72 = (bf16[4,512,1024]{2,1,0:T(8,128)(2,1)}, bf16[4,512,1024]{2,1,0:T(8,128)(2,1)}, u32[]{:S(2)}, u32[]{:S(2)}) collective-permute-start(bf16[4,512,1024]{2,1,0:T(8,128)(2,1)} %get-tuple-element.77), channel_id=1, source_target_pairs={{0,8},{8,0},{16,24},{24,16},{1,9},{9,1},{17,25},{25,17},{2,10},{10... | collective-permute-start | bytes 12582920 | tf_op jit(solution)/shard_map/ppermute | solution.py:28
  1025.7 114.1 %collective-permute-start.67 = (bf16[4,512,1024]{2,1,0:T(8,128)(2,1)}, bf16[4,512,1024]{2,1,0:T(8,128)(2,1)}, u32[]{:S(2)}, u32[]{:S(2)}) collective-permute-start(bf16[4,512,1024]{2,1,0:T(8,128)(2,1)} %get-tuple-element.80), channel_id=1, source_target_pairs={{0,8},{8,0},{16,24},{24,16},{1,9},{9,1},{17,25},{25,17},{2,10},{10... | collective-permute-start | bytes 12582920 | tf_op jit(solution)/shard_map/ppermute | solution.py:28
  1033.3 152.9 %collective-permute-start.74 = (bf16[4,512,1024]{2,1,0:T(8,128)(2,1)}, bf16[4,512,1024]{2,1,0:T(8,128)(2,1)}, u32[]{:S(2)}, u32[]{:S(2)}) collective-permute-start(bf16[4,512,1024]{2,1,0:T(8,128)(2,1)} %fusion.27), channel_id=1, source_target_pairs={{0,16},{8,24},{16,0},{24,8},{1,17},{9,25},{17,1},{25,9},{2,18},{10... | collective-permute-start | bytes 12582920 | tf_op jit(solution)/shard_map/ppermute | solution.py:28
  1042.4 170.7 %all-to-all-start.2 = ((bf16[8,2,128,256]{3,2,1,0:T(8,128)(2,1)}), bf16[8,2,128,256]{3,2,1,0:T(8,128)(2,1)}, u32[]{:S(2)}, u32[]{:S(2)}) async-start(bf16[8,2,128,256]{3,2,1,0:T(8,128)(2,1)} %bitcast.482), calls=%async_computation.2 | async-start | bytes 2097152 | tf_op jit(solution)/shard_map/all_to_all | solution.py:331
  1139.8 100.6 %collective-permute-start.71 = (bf16[4,512,1024]{2,1,0:T(8,128)(2,1)}, bf16[4,512,1024]{2,1,0:T(8,128)(2,1)}, u32[]{:S(2)}, u32[]{:S(2)}) collective-permute-start(bf16[4,512,1024]{2,1,0:T(8,128)(2,1)} %fusion.29), channel_id=1, source_target_pairs={{0,16},{8,24},{16,0},{24,8},{1,17},{9,25},{17,1},{25,9},{2,18},{10... | collective-permute-start | bytes 12582920 | tf_op jit(solution)/shard_map/ppermute | solution.py:28
  1180.8 72.8 %collective-permute-start.69 = (bf16[4,512,1024]{2,1,0:T(8,128)(2,1)}, bf16[4,512,1024]{2,1,0:T(8,128)(2,1)}, u32[]{:S(2)}, u32[]{:S(2)}) collective-permute-start(bf16[4,512,1024]{2,1,0:T(8,128)(2,1)} %get-tuple-element.79), channel_id=1, source_target_pairs={{0,8},{8,0},{16,24},{24,16},{1,9},{9,1},{17,25},{25,17},{2,10},{10... | collective-permute-start | bytes 12582920 | tf_op jit(solution)/shard_map/ppermute | solution.py:28
  1185.7 137.8 %collective-permute-start.68 = (bf16[4,512,1024]{2,1,0:T(8,128)(2,1)}, bf16[4,512,1024]{2,1,0:T(8,128)(2,1)}, u32[]{:S(2)}, u32[]{:S(2)}) collective-permute-start(bf16[4,512,1024]{2,1,0:T(8,128)(2,1)} %fusion.31), channel_id=1, source_target_pairs={{0,16},{8,24},{16,0},{24,8},{1,17},{9,25},{17,1},{25,9},{2,18},{10... | collective-permute-start | bytes 12582920 | tf_op jit(solution)/shard_map/ppermute | solution.py:28
  1186.2 26.9 %collective-permute-start.61 = (bf16[2,128,2048]{1,2,0:T(8,128)(2,1)}, bf16[2,128,2048]{1,2,0:T(8,128)(2,1)S(1)}, u32[]{:S(2)}, u32[]{:S(2)}) collective-permute-start(bf16[2,128,2048]{1,2,0:T(8,128)(2,1)} %bitcast.502), channel_id=1, source_target_pairs={{0,1},{1,0},{2,3},{3,2},{4,5},{5,4},{6,7},{7,6},{8,9},{9,8},{10,11... | collective-permute-start | bytes 3145736 | tf_op jit(solution)/shard_map/ppermute | solution.py:28
  1239.3 95.3 %collective-permute-start.63 = (bf16[2,128,2048]{1,2,0:T(8,128)(2,1)S(1)}, bf16[2,128,2048]{1,2,0:T(8,128)(2,1)S(1)}, u32[]{:S(2)}, u32[]{:S(2)}) collective-permute-start(bf16[2,128,2048]{1,2,0:T(8,128)(2,1)S(1)} %bitcast.496), channel_id=1, source_target_pairs={{0,1},{1,0},{2,3},{3,2},{4,5},{5,4},{6,7},{7,6},{8,9},{9,8},{10,11... | collective-permute-start | bytes 3145736 | tf_op jit(solution)/shard_map/ppermute | solution.py:28
  1240.4 94.2 %collective-permute-start.62 = (bf16[2,128,2048]{1,2,0:T(8,128)(2,1)S(1)}, bf16[2,128,2048]{1,2,0:T(8,128)(2,1)S(1)}, u32[]{:S(2)}, u32[]{:S(2)}) collective-permute-start(bf16[2,128,2048]{1,2,0:T(8,128)(2,1)S(1)} %add_convert_fusion.7), channel_id=1, source_target_pairs={{0,2},{1,3},{2,4},{3,5},{4,6},{5,7},{6,0},{7,1},{8,10},{9,11},{10,... | collective-permute-start | bytes 3145736 | tf_op jit(solution)/shard_map/ppermute | solution.py:28
  1251.9 90.9 %collective-permute-start.66 = (bf16[512,1024]{0,1:T(8,128)(2,1)}, bf16[512,1024]{0,1:T(8,128)(2,1)S(1)}, u32[]{:S(2)}, u32[]{:S(2)}) collective-permute-start(bf16[512,1024]{0,1:T(8,128)(2,1)} %get-tuple-element.107), channel_id=1, source_target_pairs={{0,8},{8,0},{16,24},{24,16},{1,9},{9,1},{17,25},{25,17},{2,10},{10... | collective-permute-start | bytes 3145736 | tf_op jit(solution)/shard_map/ppermute | solution.py:28
  1253.5 90.8 %collective-permute-start.65 = (bf16[512,1024]{0,1:T(8,128)(2,1)}, bf16[512,1024]{0,1:T(8,128)(2,1)}, u32[]{:S(2)}, u32[]{:S(2)}) collective-permute-start(bf16[512,1024]{0,1:T(8,128)(2,1)} %add_convert_fusion.6), channel_id=1, source_target_pairs={{0,16},{8,24},{16,0},{24,8},{1,17},{9,25},{17,1},{25,9},{2,18},{10... | collective-permute-start | bytes 3145736 | tf_op jit(solution)/shard_map/ppermute | solution.py:28
  1347.6 61.8 %all-to-all-start.3 = ((bf16[8,64,1024]{2,1,0:T(8,128)(2,1)}), bf16[8,64,1024]{2,1,0:T(8,128)(2,1)}, u32[]{:S(2)}, u32[]{:S(2)}) async-start(bf16[8,64,1024]{2,1,0:T(8,128)(2,1)} %bitcast.116), calls=%async_computation.3 | async-start | bytes 2097152 | tf_op jit(solution)/shard_map/all_to_all | solution.py:367
  (127 other events, 2187.0 us)
Sparse Core Ops, SparseCore 0:
  334.0 126.1 all-gather.1

commit v2 on v1

v2 whole, which is shorter than its diff:
```python
import math

import jax
import jax.numpy as jnp
from jax import lax
from jax.experimental import pallas as pl
from jax.experimental.pallas import tpu as pltpu
from jax.sharding import PartitionSpec as P

D = 2048
H = 16
HD = 128
FFE = 1024
TOP = 8
SEQ_LEN = 1024

eps = 1e-06
rope_base = 10000.0
masked_score = -1e30
f32 = jnp.float32
little = pl.CostEstimate(flops=1, bytes_accessed=1, transcendentals=0)
bf16 = jnp.bfloat16


def shift(value, axis, outer, inner, by_outer, by_inner):
    pairs = []
    for a in range(outer):
        for b in range(inner):
            there = ((a + by_outer) % outer) * inner + (b + by_inner) % inner
            pairs.append((a * inner + b, there))
    return lax.ppermute(value, axis, pairs)


def sizes(axis):
    count = lax.axis_size(axis)
    return (count // 2, 2) if axis == "fsdp" else (4, count // 4)


def after(value, *others):
    others = [v for v in others if v is not None]
    if not others:
        return value
    anywhere = pl.BlockSpec(memory_space=pl.ANY)
    return pl.pallas_call(
        lambda *refs: None,
        in_specs=[anywhere] * (1 + len(others)),
        out_specs=anywhere,
        out_shape=jax.ShapeDtypeStruct(value.shape, value.dtype),
        input_output_aliases={0: 0},
        cost_estimate=little,
        name="after",
    )(value, *others)


def beside_step(moved, work):
    if work is None:
        return moved
    return [after(v, work) for v in moved]


def ring_gather(value, axis, work=(), then={}):
    outer, inner = sizes(axis)
    work = list(work) + [None] * (outer - len(work))
    blocks, arrived = [], []
    for a in range(outer):
        row = [value]
        for b in range(1, inner):
            row.append(shift(row[-1], axis, outer, inner, 0, 1))
        moved = row[1:]
        if a + 1 < outer:
            moved.append(shift(value, axis, outer, inner, 1, 0))
        moved = beside_step(moved, work[a] and work[a](arrived))
        if a in then:
            then[a](moved)
        blocks += [value] + moved[: inner - 1]
        value, arrived = moved[-1], moved
    return blocks


def ring_scatter(parts, axis, work=(), then={}):
    outer, inner = sizes(axis)
    work = list(work) + [None] * (outer - len(work))
    total, arrived = None, []
    for step in range(outer):
        a = (step + 1) % outer
        row = parts[a * inner + 1 % inner]
        for b in range(2, inner):
            row = shift(row, axis, outer, inner, 0, 1)
            row = (row.astype(f32) + parts[a * inner + b].astype(f32)).astype(bf16)
        moved = [shift(row, axis, outer, inner, 0, 1)] if inner > 1 else [row]
        if total is not None:
            moved.append(shift(total, axis, outer, inner, 1, 0))
        moved = beside_step(moved, work[step] and work[step](arrived))
        if step in then:
            then[step](moved)
        arrived = moved
        total = moved[0].astype(f32) + parts[a * inner].astype(f32)
        if step:
            total = total.astype(bf16).astype(f32) + moved[1].astype(f32)
        if step + 1 < outer:
            total = total.astype(bf16)
    return total


def relative_order(axis):
    outer, inner = sizes(axis)
    me = lax.axis_index(axis)
    a, b = me // inner, me % inner
    k = jnp.arange(outer * inner)
    return ((a - k // inner) % outer) * inner + (b - k % inner) % inner


def rms_scale(values):
    return lax.rsqrt(jnp.mean(values * values, axis=-1, keepdims=True) + eps)


def exchanges():
    steps = []
    for axis in ("fsdp", "seq"):
        count = lax.axis_size(axis)
        for k in range(count.bit_length() - 1):
            steps.append((axis, [(i, i ^ (1 << k)) for i in range(count)]))
    return steps


def turn(values, cosine, sine):
    return values * cosine + pltpu.roll(values, HD // 2, 1) * sine


def turn_back(values, cosine, sine):
    return values * cosine - pltpu.roll(values, HD // 2, 1) * sine


def dot(left, right, left_dim, right_dim):
    return lax.dot_general(
        left, right, (((left_dim,), (right_dim,)), ((), ())), preferred_element_type=f32
    )


def attend_kernel(tile, qkv_ref, cos_ref, sin_ref, seg_row_ref, seg_col_ref, gain_ref, o_ref):
    blocks, _, rows, _ = qkv_ref.shape
    group = blocks * rows
    cosine, sine = cos_ref[...], sin_ref[...]

    def turned(part, row):
        raw = qkv_ref[:, 0, :, part * HD : (part + 1) * HD].reshape(group, HD).astype(f32)
        return turn(raw * rms_scale(raw) * gain_ref[row : row + 1, :], cosine, sine).astype(bf16)

    queries, keys = turned(0, 0), turned(1, 1)
    values = qkv_ref[:, 0, :, 2 * HD : 3 * HD].reshape(group, HD)
    seg_row = seg_row_ref[0]
    for start in range(0, group, tile):
        scores = dot(queries[start : start + tile], keys, 1, 1) * (1.0 / math.sqrt(HD))
        allowed = seg_col_ref[0, start : start + tile, :] == seg_row
        scores = jnp.where(allowed, scores, masked_score)
        powered = jnp.exp(scores - jnp.max(scores, axis=-1, keepdims=True))
        scale = 1.0 / jnp.sum(powered, axis=-1, keepdims=True)
        attended = dot((powered * scale).astype(bf16), values, 1, 0).astype(bf16)
        o_ref[start // rows : (start + tile) // rows, 0, :, :] = attended.reshape(
            tile // rows, rows, HD
        )


def attend_back_kernel(
    tile,
    qkv_ref,
    do_ref,
    cos_ref,
    sin_ref,
    seg_row_ref,
    seg_col_ref,
    gain_ref,
    grad_ref,
    grad_gain_ref,
):
    blocks, _, rows, _ = qkv_ref.shape
    group = blocks * rows
    cosine, sine = cos_ref[...], sin_ref[...]
    scaling = 1.0 / math.sqrt(HD)

    def normed(part):
        raw = qkv_ref[:, 0, :, part * HD : (part + 1) * HD].reshape(group, HD).astype(f32)
        inverse = rms_scale(raw)
        return raw * inverse, inverse

    def turned(part):
        return turn(normed(part)[0] * gain_ref[part : part + 1, :], cosine, sine).astype(bf16)

    def finish(part, grad_turned):
        unit, inverse = normed(part)
        grad_scaled = turn_back(grad_turned, cosine, sine)
        grad_gain_ref[0, part : part + 1, :] = jnp.sum(grad_scaled * unit, axis=0, keepdims=True)
        grad_unit = grad_scaled * gain_ref[part : part + 1, :]
        grad_raw = inverse * (
            grad_unit - unit * jnp.mean(grad_unit * unit, axis=-1, keepdims=True)
        )
        return grad_raw

    def put(part, value):
        grad_ref[:, 0, :, part * HD : (part + 1) * HD] = value.astype(bf16).reshape(
            blocks, rows, HD
        )

    queries, keys = turned(0), turned(1)
    values = qkv_ref[:, 0, :, 2 * HD : 3 * HD].reshape(group, HD)
    grad_out = do_ref[:, 0, :, :].reshape(group, HD)
    seg_row = seg_row_ref[0]
    grad_query = []
    grad_key = jnp.zeros((group, HD), f32)
    grad_value = jnp.zeros((group, HD), f32)
    for start in range(0, group, tile):
        part = queries[start : start + tile]
        grad_part = grad_out[start : start + tile]
        scores = dot(part, keys, 1, 1) * scaling
        allowed = seg_col_ref[0, start : start + tile, :] == seg_row
        scores = jnp.where(allowed, scores, masked_score)
        powered = jnp.exp(scores - jnp.max(scores, axis=-1, keepdims=True))
        probabilities = powered * (1.0 / jnp.sum(powered, axis=-1, keepdims=True))
        grad_probs = dot(grad_part, values, 1, 1)
        centre = jnp.sum(probabilities * grad_probs, axis=-1, keepdims=True)
        grad_scores = (probabilities * (grad_probs - centre)).astype(bf16)
        grad_query.append(dot(grad_scores, keys, 1, 0) * scaling)
        grad_key = grad_key + dot(grad_scores, part, 0, 0)
        grad_value = grad_value + dot(probabilities.astype(bf16), grad_part, 0, 0)
    put(0, finish(0, jnp.concatenate(grad_query, axis=0)))
    put(1, finish(1, grad_key * scaling))
    put(2, grad_value)


def attention_specs(ns, micro, rows, heads):
    group = ns * rows
    tile = max(rows, 256)
    return (
        tile,
        pl.BlockSpec((ns, 1, rows, 3 * HD), lambda m, h: (0, m, 0, h)),
        pl.BlockSpec((ns, 1, rows, HD), lambda m, h: (0, m, 0, h)),
        [
            pl.BlockSpec((group, HD), lambda m, h: (0, 0)),
            pl.BlockSpec((group, HD), lambda m, h: (0, 0)),
            pl.BlockSpec((1, 1, group), lambda m, h: (m, 0, 0)),
            pl.BlockSpec((1, group, 1), lambda m, h: (m, 0, 0)),
            pl.BlockSpec((2, HD), lambda m, h: (0, 0)),
        ],
    )


def attend(qkv, tables):
    ns, micro, rows, width = qkv.shape
    heads = width // (3 * HD)
    tile, wide, narrow, shared = attention_specs(ns, micro, rows, heads)
    group = ns * rows
    return pl.pallas_call(
        lambda *refs: attend_kernel(tile, *refs),
        grid=(micro, heads),
        in_specs=[wide] + shared,
        out_specs=narrow,
        out_shape=jax.ShapeDtypeStruct((ns, micro, rows, heads * HD), bf16),
        compiler_params=pltpu.CompilerParams(vmem_limit_bytes=40 * 2**20),
        cost_estimate=little,
        name="attend",
    )(qkv, *tables)


def attend_back(qkv, grad_out, tables, ties=()):
    ns, micro, rows, width = qkv.shape
    heads = width // (3 * HD)
    tile, wide, narrow, shared = attention_specs(ns, micro, rows, heads)
    group = ns * rows
    return pl.pallas_call(
        lambda *refs: attend_back_kernel(tile, *refs[:7], *refs[-2:]),
        grid=(micro, heads),
        in_specs=[wide, narrow] + shared + [pl.BlockSpec(memory_space=pl.ANY)] * len(ties),
        out_specs=[wide, pl.BlockSpec((1, 2, HD), lambda m, h: (m * heads + h, 0, 0))],
        out_shape=[
            jax.ShapeDtypeStruct((ns, micro, rows, width), bf16),
            jax.ShapeDtypeStruct((micro * heads, 2, HD), f32),
        ],
        compiler_params=pltpu.CompilerParams(vmem_limit_bytes=40 * 2**20),
        cost_estimate=little,
        name="attend_back",
    )(qkv, grad_out, *tables, *ties)


part = 512


def spans(shape, *block):
    block = block or (1,)
    return pl.BlockSpec(
        tuple(block) + tuple(shape[len(block) :]), lambda e, *_: (e,) + (0,) * (len(shape) - 1)
    )


def whole_of(shape):
    return pl.BlockSpec(
        tuple(shape), lambda *_: (0,) * len(shape), pipeline_mode=pl.Buffered(buffer_count=1)
    )


def call(kernel, name, grid, ins, outs, flops, scratch=(), ties=()):
    ties = [t for t in ties if t is not None]
    count = len(ins)

    def run(*refs):
        kernel(*refs[:count], *refs[count + len(ties) :])

    return pl.pallas_call(
        run,
        grid=grid,
        in_specs=[spec for _, spec in ins] + [pl.BlockSpec(memory_space=pl.ANY)] * len(ties),
        out_specs=[spec for _, spec in outs],
        out_shape=[shape for shape, _ in outs],
        scratch_shapes=list(scratch),
        compiler_params=pltpu.CompilerParams(vmem_limit_bytes=56 * 2**20),
        cost_estimate=little,
        name=name,
    )(*[value for value, _ in ins], *ties)


def picked(slot_row, capacity):
    place = lax.broadcasted_iota(jnp.int32, (capacity, slot_row.shape[1]), 0)
    return place == slot_row


def slot_weights(slot_row, weight_row, capacity):
    chosen = jnp.where(picked(slot_row, capacity), weight_row, 0.0)
    return jnp.sum(chosen, axis=1, keepdims=True)


def dispatch_kernel(scaled, blocks, *refs):
    value_refs, (slot_ref, weight_ref, w_ref, rows_ref, act_ref) = refs[:blocks], refs[blocks:]
    capacity, each = rows_ref.shape[2], blocks // 2
    for h in range(2):
        slot_row = slot_ref[0, h : h + 1, :]
        pick = picked(slot_row, capacity).astype(f32).astype(bf16)
        if scaled:
            scale = slot_weights(slot_row, weight_ref[0, h : h + 1, :], capacity)
        for d in range(0, D, part):
            values = jnp.concatenate(
                [ref[:, d : d + part] for ref in value_refs[h * each : (h + 1) * each]], axis=0
            )
            taken = dot(pick, values, 1, 0)
            if scaled:
                taken = taken * scale
            rows_ref[0, h, :, d : d + part] = taken.astype(bf16)
        act_ref[0, h] = dot(rows_ref[0, h], w_ref[0], 1, 0)


def dispatch(values, slots, weights, bank, capacity, scaled, ties=()):
    count = bank.shape[0]
    values = [v.reshape(-1, v.shape[-1]) for v in values]
    rows_shape = (count, 2, capacity, D)
    act_shape = (count, 2, capacity, FFE)
    return call(
        lambda *refs: dispatch_kernel(scaled, len(values), *refs),
        "dispatch",
        (count,),
        [(v, whole_of(v.shape)) for v in values]
        + [(v, spans(v.shape)) for v in (slots, weights, bank)],
        [
            (jax.ShapeDtypeStruct(rows_shape, bf16), spans(rows_shape)),
            (jax.ShapeDtypeStruct(act_shape, f32), spans(act_shape)),
        ],
        4 * count * capacity * D * (FFE + len(values) * values[0].shape[0] // 2),
        ties=ties,
    )


def act_kernel(taken_ref, gate_ref, grad_ref, w_ref, hidden_ref, grad_gate_ref, grad_up_ref):
    up_act = dot(taken_ref[0, 0], w_ref[0], 1, 0)
    gate_act, grad_hidden = gate_ref[0, 0], grad_ref[0, 0]
    gate_sig = jax.nn.sigmoid(gate_act)
    gate_silu = gate_act * gate_sig
    hidden_ref[0, 0] = (gate_silu * up_act).astype(bf16)
    grad_gate = grad_hidden * up_act * gate_sig * (1.0 + gate_act * (1.0 - gate_sig))
    grad_gate_ref[0, 0] = grad_gate.astype(bf16)
    grad_up_ref[0, 0] = (grad_hidden * gate_silu).astype(bf16)


def activate(taken, gate_act, grad_hidden, w_up, ties=()):
    count, _, capacity, _ = taken.shape

    def of(width):
        return pl.BlockSpec((1, 1, capacity, width), lambda e, h: (e, h, 0, 0))

    result = jax.ShapeDtypeStruct((count, 2, capacity, FFE), bf16)
    return call(
        act_kernel,
        "activate",
        (count, 2),
        [
            (taken, of(D)),
            (gate_act, of(FFE)),
            (grad_hidden, of(FFE)),
            (w_up, spans(w_up.shape)),
        ],
        [(result, of(FFE))] * 3,
        4 * count * capacity * D * FFE,
        ties=ties,
    )


def bank_kernel(left_ref, right_ref, out_ref):
    rows = left_ref.shape[1] * left_ref.shape[2]
    left, right = left_ref[0].reshape(rows, -1), right_ref[0].reshape(rows, -1)
    out_ref[0] = dot(left, right, 0, 0).astype(bf16)


def bank_grad(left, right, ties=()):
    count, _, capacity, _ = left.shape
    result = jax.ShapeDtypeStruct((count, D, FFE), bf16)
    return call(
        bank_kernel,
        "bank_grad",
        (count, D // part),
        [
            (left, pl.BlockSpec((1, 2, capacity, part), lambda e, d: (e, 0, 0, d))),
            (right, pl.BlockSpec((1, 2, capacity, FFE), lambda e, d: (e, 0, 0, 0))),
        ],
        [(result, pl.BlockSpec((1, part, FFE), lambda e, d: (e, d, 0)))],
        4 * count * capacity * D * FFE,
        ties=ties,
    )[0]


def combine_kernel(scaled, acts, blocks, h, *refs):
    act_refs, w_refs = refs[:acts], refs[acts : 2 * acts]
    column_ref, slot_ref, weight_ref = refs[2 * acts : 2 * acts + 3]
    out_refs, total_ref = refs[2 * acts + 3 : -1], refs[-1]
    expert = pl.program_id(0)
    capacity = act_refs[0].shape[2]
    half = total_ref.shape[0]
    place = lax.broadcasted_iota(jnp.int32, (half, capacity), 1)
    pick = (place == column_ref[0, 0]).astype(f32).astype(bf16)
    if scaled:
        scale = slot_weights(slot_ref[0, h : h + 1, :], weight_ref[0, h : h + 1, :], capacity)

    @pl.when(expert == 0)
    def _():
        total_ref[...] = jnp.zeros_like(total_ref)

    for d in range(0, D, part):
        grads = [
            dot(a_ref[0, 0], w_ref[0, d : d + part, :], 1, 1)
            for a_ref, w_ref in zip(act_refs, w_refs)
        ]
        rows = sum(grads[1:], grads[0])
        if scaled:
            rows = rows * scale
        total_ref[:, d : d + part] += dot(pick, rows.astype(bf16), 1, 0)

    @pl.when(expert == pl.num_programs(0) - 1)
    def _():
        n = half // blocks
        for b, ref in enumerate(out_refs):
            ref[...] = total_ref[b * n : (b + 1) * n, :].astype(bf16)


def combine(acts, banks, columns, slots, weights, h, blocks, scaled, ties=()):
    count, _, capacity, _ = acts[0].shape
    half = columns.shape[2]
    result = jax.ShapeDtypeStruct((half // blocks, D), bf16)
    return call(
        lambda *refs: combine_kernel(scaled, len(acts), blocks, h, *refs),
        "combine",
        (count,),
        [(a, pl.BlockSpec((1, 1, capacity, FFE), lambda e: (e, h, 0, 0))) for a in acts]
        + [(w, spans(w.shape)) for w in banks]
        + [(columns, pl.BlockSpec((1, 1, half, 1), lambda e: (e, h, 0, 0)))]
        + [(v, spans(v.shape)) for v in (slots, weights)],
        [(result, whole_of(result.shape))] * blocks,
        2 * count * capacity * D * (FFE * len(acts) + half),
        scratch=[pltpu.VMEM((half, D), f32)],
        ties=ties,
    )


def body(
    layer_input,
    cotangent,
    segments,
    routes,
    route_weights,
    gain_attention,
    gain_experts,
    query_proj,
    key_proj,
    value_proj,
    output_proj,
    head_gains,
    expert_gate,
    expert_up,
    expert_down,
):
    micro, rows, _ = layer_input.shape
    nf, ns = lax.axis_size("fsdp"), lax.axis_size("seq")
    seq_index = lax.axis_index("seq")
    seq_order = relative_order("seq")
    tokens = micro * rows
    group = rows * ns
    half = group * micro // 2
    heads_local = H // ns
    width = heads_local * HD
    local_experts = expert_gate.shape[0]
    experts = local_experts * ns
    capacity = micro * ns // 2 * min(rows, 3 * rows * TOP // (2 * experts))
    share = D // (nf * ns)

    def spread(value, axis):
        return lax.all_gather(value, "fsdp", axis=axis, tiled=True)

    def gather_tokens(value):
        return jnp.stack(ring_gather(value, "seq"))

    def scatter_tokens(parts, work=(), then={}):
        parts = [v.reshape(micro, rows, D) for v in parts]
        return ring_scatter(parts, "seq", work, then).reshape(tokens, D)

    columns = [
        lax.dynamic_slice_in_dim(w, seq_index * width, width, axis=1).reshape(-1, heads_local, HD)
        for w in (query_proj, key_proj, value_proj)
    ]
    columns = jnp.stack(columns, axis=2).reshape(-1, 3 * width)
    extra = jnp.pad(jnp.stack([gain_attention, gain_experts], axis=1), ((0, 0), (0, HD - 2)))
    w_first = spread(jnp.concatenate([columns, extra], axis=1), 0)
    w_qkv = w_first[:, : 3 * width]
    gain_one = w_first[:, 3 * width].astype(f32)
    gain_two = w_first[:, 3 * width + 1].astype(f32)
    w_down = spread(expert_down, 1)
    w_output = spread(output_proj, 0)
    w_gate = spread(expert_gate, 1)
    w_up = spread(expert_up, 1)

    x_all = gather_tokens(layer_input)
    x_wide = x_all.astype(f32)
    inv_all = rms_scale(x_wide)
    h_one = (x_wide * inv_all * gain_one).astype(bf16)
    qkv = jnp.einsum("smtd,de->smte", h_one, w_qkv, preferred_element_type=f32).astype(bf16)

    places = (seq_order[:, None] * rows + jnp.arange(rows)[None, :]).reshape(-1)
    lane = jnp.arange(HD) % (HD // 2)
    frequency = jnp.exp(-jnp.log(rope_base) * (2.0 * lane.astype(f32) / HD))
    angles = places.astype(f32)[:, None] * frequency[None, :]
    sign = jnp.where(jnp.arange(HD) < HD // 2, -1.0, 1.0)
    segment = jnp.take(segments.reshape(micro, ns, rows), seq_order, axis=1).reshape(micro, group)
    tables = (
        jnp.cos(angles),
        jnp.sin(angles) * sign,
        segment[:, None, :],
        segment[:, :, None],
        head_gains.astype(f32),
    )
    o_heads = attend(qkv, tables)

    inverse_seq = jnp.argsort(seq_order)
    o_heads = jnp.take(o_heads, inverse_seq, axis=0)
    o_back = lax.all_to_all(o_heads, "seq", split_axis=0, concat_axis=0, tiled=True)
    o_rows = jnp.moveaxis(o_back, 0, 2).reshape(tokens, D)

    x_rows = layer_input.astype(f32).reshape(tokens, D)
    middle = x_rows + jnp.dot(o_rows, w_output, preferred_element_type=f32)
    inv_two = rms_scale(middle)
    normed_two = middle * inv_two
    h_two_own = (normed_two * gain_two).astype(bf16).reshape(micro, rows, D)
    weight_high = route_weights.astype(bf16)
    weight_low = (route_weights - weight_high.astype(f32)).astype(bf16)
    packed = jnp.concatenate([cotangent, routes.astype(bf16), weight_high, weight_low], axis=-1)
    packed = jnp.pad(packed, ((0, 0), (0, 0), (0, HD - 3 * TOP)))
    g_blocks = ring_gather(
        after(packed, x_all),
        "seq",
        (lambda _: qkv, lambda _: h_two_own),
    )

    packed = jnp.stack([v[..., D : D + 3 * TOP] for v in g_blocks]).astype(f32)
    packed = packed.reshape(2, half, 3 * TOP)
    route_all = packed[..., :TOP].astype(jnp.int32)
    weight_all = packed[..., TOP : 2 * TOP] + packed[..., 2 * TOP :]
    mine = seq_index * local_experts + jnp.arange(local_experts)
    hit = route_all[:, :, None, :] == mine[None, None, :, None]
    chosen = jnp.any(hit, axis=-1)
    weight_of = jnp.sum(jnp.where(hit, weight_all[:, :, None, :], 0.0), axis=-1)
    block = 128
    counted = chosen.reshape(2, half // block, block, local_experts).astype(f32)
    below = jnp.tril(jnp.ones((block, block), f32), -1)
    inside = jnp.einsum("ab,mkbe->mkae", below, counted)
    sums = jnp.sum(counted, axis=2)
    before = jnp.cumsum(sums, axis=1) - sums
    slot = (inside + before[:, :, None, :]).reshape(2, half, local_experts).astype(jnp.int32)
    slots = jnp.transpose(jnp.where(chosen, slot, -1), (2, 0, 1))
    weights = jnp.transpose(weight_of, (2, 0, 1))
    slot_columns = slots[..., None]

    grad_top = cotangent.astype(f32).reshape(tokens, D)
    done = {}

    def keep(**found):
        done.update(found)
        return next(iter(found.values()))

    def grad_work(ties):
        grad_rows, grad_hidden = dispatch(g_blocks, slots, weights, w_down, capacity, True, ties)
        return keep(grad_rows=grad_rows, grad_hidden=grad_hidden)

    h_blocks = ring_gather(h_two_own, "seq", (None, grad_work))
    grad_rows, grad_hidden = done["grad_rows"], done["grad_hidden"]

    def combined(acts, banks, h, scaled, ties=()):
        return combine(acts, banks, slot_columns, slots, weights, h, ns // 2, scaled, ties)

    def take_work(_):
        taken, gate_act = dispatch(h_blocks, slots, weights, w_gate, capacity, False)
        return keep(taken=taken, gate_act=gate_act)

    def act_work(ties):
        hidden, grad_gate_act, grad_up_act = activate(
            done["taken"], done["gate_act"], grad_hidden, w_up, ties
        )
        return keep(hidden=hidden, grad_gate_act=grad_gate_act, grad_up_act=grad_up_act)

    def down_work(ties):
        return keep(whole_down=bank_grad(grad_rows, done["hidden"], ties))

    def first_work(ties):
        acts = (done["grad_gate_act"], done["grad_up_act"])
        first = combined(acts, (w_gate, w_up), 0, False, tuple(ties) + (done["whole_down"],))
        return keep(tail=first[0], first=first)

    o_all = ring_gather(
        after(o_heads.reshape(group * micro, width), h_blocks[-1]),
        "seq",
        (take_work, act_work, down_work, first_work),
        {2: lambda moved: keep(sum_down=after(done["whole_down"], *moved))},
    )
    o_all = jnp.concatenate(o_all, axis=1)
    taken, hidden, first = done["taken"], done["hidden"], done["first"]
    grad_gate_act, grad_up_act = done["grad_gate_act"], done["grad_up_act"]
    second = combined((grad_gate_act, grad_up_act), (w_gate, w_up), 1, False, (first[0],))

    def gate_work(ties):
        return keep(whole_gate=bank_grad(taken, grad_gate_act, ties))

    def up_work(ties):
        return keep(whole_up=bank_grad(taken, grad_up_act, ties))

    def mixed_work(ties):
        mixed = combined((hidden,), (w_down,), 0, True, ties)
        return keep(tail=mixed[0], mixed_first=mixed)

    grad_h_two = scatter_tokens(
        list(first) + list(second),
        (lambda _: second[0], gate_work, up_work, mixed_work),
        {
            1: lambda moved: keep(sum_gate=after(done["whole_gate"], *moved)),
            2: lambda moved: keep(sum_up=after(done["whole_up"], *moved)),
        },
    )

    def bank_sum(whole):
        return lax.psum_scatter(whole, "fsdp", scatter_dimension=1, tiled=True).astype(f32)

    grad_down = bank_sum(done["sum_down"])
    grad_gate = bank_sum(done["sum_gate"])
    grad_up = bank_sum(done["sum_up"])

    grad_gain_two = jnp.sum(grad_h_two * normed_two, axis=0)
    grad_unit = grad_h_two * gain_two
    grad_middle = grad_top + inv_two * (
        grad_unit - normed_two * jnp.mean(grad_unit * normed_two, axis=-1, keepdims=True)
    )
    grad_attn = grad_middle.astype(bf16)
    grad_o = jnp.einsum("te,de->td", grad_attn, w_output, preferred_element_type=f32).astype(bf16)

    def to_heads(value):
        cut = value.reshape(micro, rows, ns, width)
        return lax.all_to_all(
            jnp.moveaxis(cut, 2, 0), "seq", split_axis=0, concat_axis=0, tiled=True
        )

    mixed_second = combined((hidden,), (w_down,), 1, True, (grad_o,))
    do_blocks = after(to_heads(grad_o), mixed_second[0])
    do_heads = jnp.take(do_blocks, seq_order, axis=0)

    def attend_work(ties):
        grad_qkv, grad_head = attend_back(qkv, do_heads, tables, ties)
        return keep(grad_qkv=grad_qkv, grad_head=grad_head)

    def attended_then(moved):
        columns = to_heads(after(grad_attn, *moved)).reshape(micro * group, width)
        keep(columns=columns, head=after(jnp.sum(done["grad_head"], axis=0), *moved), left=exchanges())

    def exchange(moved):
        if done["left"]:
            axis, pairs = done["left"].pop(0)
            keep(head=done["head"] + after(lax.ppermute(done["head"], axis, pairs), *moved))

    def qkv_work(_):
        grads = jnp.einsum(
            "smtd,smte->de", h_one, done["grad_qkv"], preferred_element_type=f32
        )
        return keep(from_qkv=grads)

    def part_work(_):
        wide = jnp.einsum("smte,de->smtd", done["grad_qkv"], w_qkv, preferred_element_type=f32)
        return keep(part=wide.astype(bf16), wide=wide)

    mixed = list(done["mixed_first"]) + list(mixed_second)
    mixed[ns // 4 + 1] = after(mixed[ns // 4 + 1], grad_h_two)
    mixed = scatter_tokens(
        mixed,
        (lambda _: do_heads, attend_work, part_work, qkv_work),
        {1: attended_then, 2: exchange, 3: exchange},
    )
    layer_output = (middle + mixed).astype(bf16).reshape(micro, rows, D)
    def out_work(ties):
        grads = jnp.einsum(
            "td,te->de", after(o_all, *ties), done["columns"], preferred_element_type=f32
        )
        return keep(from_out=grads)

    part_h_one = done["part"]
    grad_h_one = scatter_tokens(
        [part_h_one[k] for k in range(ns)],
        (lambda _: done["from_qkv"], out_work, lambda _: grad_down, lambda _: grad_gate),
        {step: exchange for step in range(4)},
    )
    while done["left"]:
        exchange(())
    grad_head_gains = done["head"]
    grad_gain_one = jnp.sum(done["wide"] * (x_wide * inv_all), axis=(0, 1, 2))
    inv_one = rms_scale(x_rows)
    normed_one = x_rows * inv_one
    grad_unit = grad_h_one * gain_one
    input_grad = grad_middle + inv_one * (
        grad_unit - normed_one * jnp.mean(grad_unit * normed_one, axis=-1, keepdims=True)
    )
    input_grad = input_grad.reshape(micro, rows, D)

    from_qkv, from_out = done["from_qkv"], done["from_out"]
    from_out = jnp.take(from_out.reshape(ns, width, width), inverse_seq, axis=0).reshape(D, width)
    from_gains = jnp.pad(jnp.stack([grad_gain_one, grad_gain_two], axis=1), ((0, 0), (0, HD - 2)))
    whole = jnp.concatenate([from_qkv, from_out, from_gains], axis=1).astype(bf16)
    order = relative_order("fsdp")
    whole = jnp.take(whole.reshape(nf, D // nf, -1), order, axis=0)
    owned = ring_scatter([whole[k] for k in range(nf)], "fsdp").astype(bf16)
    owned = lax.all_to_all(
        owned.reshape(ns, share, -1), "seq", split_axis=0, concat_axis=0, tiled=True
    ).astype(f32)
    of_qkv = owned[..., : 3 * width].reshape(ns, share, heads_local, 3, HD)
    grad_query, grad_key, grad_value = (
        jnp.moveaxis(of_qkv[..., k, :], 0, 1).reshape(share, D) for k in range(3)
    )
    grad_output = jnp.moveaxis(owned[..., 3 * width : 4 * width], 0, 1).reshape(share, D)
    of_gains = jnp.sum(owned[..., 4 * width : 4 * width + 2], axis=0)
    return (
        layer_output,
        input_grad,
        of_gains[:, 0],
        of_gains[:, 1],
        grad_query,
        grad_key,
        grad_value,
        grad_output,
        grad_head_gains,
        grad_gate,
        grad_up,
        grad_down,
    )


def solution(mesh):
    placed = (
        P(None, ("fsdp", "seq"), None),
        P(None, ("fsdp", "seq"), None),
        P(None, "fsdp"),
        P(None, ("fsdp", "seq"), None),
        P(None, ("fsdp", "seq"), None),
        P("fsdp"),
        P("fsdp"),
        P("fsdp", None),
        P("fsdp", None),
        P("fsdp", None),
        P("fsdp", None),
        P(),
        P("seq", "fsdp", None),
        P("seq", "fsdp", None),
        P("seq", "fsdp", None),
    )
    return jax.shard_map(
        body,
        mesh=mesh,
        in_specs=placed,
        out_specs=(
            P(None, ("fsdp", "seq"), None),
            P(None, ("fsdp", "seq"), None),
            P(("fsdp", "seq")),
            P(("fsdp", "seq")),
            P(("fsdp", "seq"), None),
            P(("fsdp", "seq"), None),
            P(("fsdp", "seq"), None),
            P(("fsdp", "seq"), None),
            P(),
            P("seq", "fsdp", None),
            P("seq", "fsdp", None),
            P("seq", "fsdp", None),
        ),
        check_vma=False,
    )
```

time: 1440 us -> 1120 us (0.78)
  Pallas kernels: 0 us -> 340 us
  matrix products: 365 us -> 54 us
  local copies, waits for them, and re-layouts: 301 us -> 131 us
  other arithmetic: 185 us -> 92.8 us
  blocking collectives: 46.5 us -> 0 us
  waiting for transfers between devices: 421 us -> 398 us
    pallas_call x0 -> x61, Pallas kernels: none -> 340 us  [the longest x10 290 us: call(): pl.pallas_call(run, grid=grid, in_specs=[spec for _, spec in ins] + [pl.B...]
    dot_general x24 -> x5, matrix products: 362 us -> 47.4 us  [the longest x1 12.3 us: part_work(): jnp.einsum('smte,de->smtd', done['grad_qkv'], w_qkv, preferred_element_ty...]
    ppermute x76 -> x52, waiting for transfers between devices: 421 us -> 327 us  [shift(): return lax.ppermute(value, axis, pairs)]
    unnamed x300 -> x240, local copies, waits for them, and re-layouts: 147 us -> 74.7 us
    psum x1 -> x0, blocking collectives: 40.3 us -> none  [body(): lax.psum(jnp.concatenate([grad_gain_one, grad_gain_two, grad_q_gain, grad...]
    add x8 -> x9, other arithmetic: 47.1 us -> 12.6 us  [the longest x2 5.7 us: ring_scatter(): total = total.astype(bf16).astype(f32) + moved[1].astype(f32)]
    convert_element_type x15 -> x11, other arithmetic: 51.8 us -> 26.8 us  [the longest x3 20.1 us: bank_sum(): lax.psum_scatter(whole, 'fsdp', scatter_dimension=1, tiled=True).astype(f32)]
    all_to_all x1, waiting for transfers between devices: 0.01 us -> 24.1 us  [body(): lax.all_to_all(owned.reshape(ns, share, -1), 'seq', split_axis=0, concat_...]
  transfers between devices with their start and end apart: 81 -> 69, of which waited for: 27 -> 25; matrix products, arithmetic and copies ran while one was open for 57% -> 20% of each run, Pallas kernels for 0% -> 31%
where the time goes in v2:
time: 1120 us; the launch traced here: 1110 us
  waiting for transfers between devices  398 us (36%)
  Pallas kernels  340 us (30%)
  local copies, waits for them, and re-layouts  131 us (12%)
  other arithmetic  92.8 us (8%)
  starting transfers between devices  81.3 us (7%)
  matrix products  54 us (5%)
  between operations  16 us (1%)
    ppermute x52, waiting for transfers between devices, shift(): return lax.ppermute(value, axis, pairs)  327 us
    pallas_call x10, Pallas kernels, call(): pl.pallas_call(run, grid=grid, in_specs=[spec for _, spec in ins] + [pl.B...  290 us
    unnamed x240, local copies, waits for them, and re-layouts  74.7 us
    ppermute x52, starting transfers between devices, shift(): return lax.ppermute(value, axis, pairs)  53.5 us
    pallas_call x1, Pallas kernels, attend_back(): pl.pallas_call(lambda *refs: attend_back_kernel(tile, *refs[:7], *refs[-2...  33.2 us
    convert_element_type x10, other arithmetic, ring_scatter(): total = total.astype(bf16)  26.4 us
    all_to_all x1, waiting for transfers between devices, body(): lax.all_to_all(owned.reshape(ns, share, -1), 'seq', split_axis=0, concat_...  24.1 us
    all_to_all x1, waiting for transfers between devices, body(): lax.all_to_all(o_heads, 'seq', split_axis=0, concat_axis=0, tiled=True)  22.7 us
  transfers between devices with their start and end apart: 69, of which 25 were waited for; matrix products, arithmetic and copies ran while one was open for 20% of the time, Pallas kernels for 31%

profile of v2, /device:TPU:0, one launch (start us, length us, event | category | flops | bytes accessed | tf_op | source)
XLA Modules:
  0.0 1112.9 jit_solution(13067989971904368598)
XLA Ops:
  14.3 3.0 collective-permute-start.1
  21.6 3.1 fusion.38
  24.7 17.9 %collective-permute-done.1 = bf16[2,128,2048]{2,1,0:T(8,128)(2,1)S(1)} collective-permute-done((bf16[2,128,2048]{2,1,0:T(8,128)(2,1)S(1)}, bf16[2,128,2048]{2,1,0:T(8,128)(2,1)S(1)}, u32[]{:S(2)}, u32[]{:S(2)}) %collective-permute-start.1) | collective-permute-done | bytes 1048608 | tf_op jit(solution)/shard_map/ppermute | solution.py:31
  45.5 23.2 %collective-permute-done.3 = bf16[2,128,2048]{2,1,0:T(8,128)(2,1)S(1)} collective-permute-done((bf16[2,128,2048]{2,1,0:T(8,128)(2,1)S(1)}, bf16[2,128,2048]{2,1,0:T(8,128)(2,1)S(1)}, u32[]{:S(2)}, u32[]{:S(2)}) %collective-permute-start.3) | collective-permute-done | bytes 1048608 | tf_op jit(solution)/shard_map/ppermute | solution.py:31
  71.8 22.3 %collective-permute-done.5 = bf16[2,128,2048]{2,1,0:T(8,128)(2,1)S(1)} collective-permute-done((bf16[2,128,2048]{2,1,0:T(8,128)(2,1)S(1)}, bf16[2,128,2048]{2,1,0:T(8,128)(2,1)S(1)}, u32[]{:S(2)}, u32[]{:S(2)}) %collective-permute-start.5) | collective-permute-done | bytes 1048608 | tf_op jit(solution)/shard_map/ppermute | solution.py:31
  95.5 21.2 %collective-permute-done.6 = bf16[2,128,2048]{2,1,0:T(8,128)(2,1)S(1)} collective-permute-done((bf16[2,128,2048]{2,1,0:T(8,128)(2,1)S(1)}, bf16[2,128,2048]{2,1,0:T(8,128)(2,1)S(1)}, u32[]{:S(2)}, u32[]{:S(2)}) %collective-permute-start.6) | collective-permute-done | bytes 1048608 | tf_op jit(solution)/shard_map/ppermute | solution.py:31
  116.7 4.4 copy-done.18
  124.8 10.5 fusion.15.refs_0_.refs_1_
  135.4 16.5 %attend.1 = bf16[8,2,128,256]{3,2,1,0:T(8,128)(2,1)S(1)} custom-call(bf16[8,2,128,768]{3,2,1,0:T(8,128)(2,1)S(1)} %fusion.15.refs_0_.refs_1_, f32[1024,128]{1,0:T(8,128)S(1)} %copy-done.11, f32[1024,128]{1,0:T(8,128)S(1)} %copy-done.9, s32[2,1,1024]{2,1,0:T(1,128)S(1)} %broadcast_select_fusion.4.refs_3_.refs_4_, s32[2,1024,1]{2,1,0:T(8,128)S(1)} %copy-done.7, ...), custom_call_target="tpu_custom_call" | custom-call | flops 1 | bytes 1 | tf_op jit(solution)/shard_map/attend/pallas_call | solution.py:252
  158.2 5.3 all-to-all-start
  169.5 37.7 %collective-permute-done.11.refs_0_ = bf16[2,128,2176]{2,1,0:T(8,128)(2,1)S(1)} collective-permute-done((bf16[2,128,2176]{2,1,0:T(8,128)(2,1)}, bf16[2,128,2176]{2,1,0:T(8,128)(2,1)S(1)}, u32[]{:S(2)}, u32[]{:S(2)}) %collective-permute-start.11) | collective-permute-done | bytes 1114144 | tf_op jit(solution)/shard_map/ppermute | solution.py:31
  209.5 3.7 collective-permute-start.13
  213.2 22.7 %all-to-all-done = bf16[8,2,128,256]{3,2,1,0:T(8,128)(2,1)} async-done(((bf16[8,2,128,256]{3,2,1,0:T(8,128)(2,1)}), bf16[8,2,128,256]{3,2,1,0:T(8,128)(2,1)}, u32[]{:S(2)}, u32[]{:S(2)}) %all-to-all-start) | async-done | bytes 1048608 | tf_op jit(solution)/shard_map/all_to_all | solution.py:557
  239.1 6.4 multiply_reduce_fusion.4
  255.0 21.9 %collective-permute-done.15 = bf16[2,128,2176]{2,1,0:T(8,128)(2,1)} collective-permute-done((bf16[2,128,2176]{2,1,0:T(8,128)(2,1)}, bf16[2,128,2176]{2,1,0:T(8,128)(2,1)}, u32[]{:S(2)}, u32[]{:S(2)}) %collective-permute-start.15) | collective-permute-done | bytes 1114144 | tf_op jit(solution)/shard_map/ppermute | solution.py:31
  278.1 14.3 %collective-permute-done.8.refs_12_ = bf16[2,128,2048]{2,1,0:T(8,128)(2,1)} collective-permute-done((bf16[2,128,2048]{2,1,0:T(8,128)(2,1)S(1)}, bf16[2,128,2048]{2,1,0:T(8,128)(2,1)}, u32[]{:S(2)}, u32[]{:S(2)}) %collective-permute-start.8) | collective-permute-done | bytes 1048608 | tf_op jit(solution)/shard_map/ppermute | solution.py:31
  294.7 18.8 %collective-permute-done.16 = bf16[2,128,2176]{2,1,0:T(8,128)(2,1)} collective-permute-done((bf16[2,128,2176]{2,1,0:T(8,128)(2,1)}, bf16[2,128,2176]{2,1,0:T(8,128)(2,1)}, u32[]{:S(2)}, u32[]{:S(2)}) %collective-permute-start.16) | collective-permute-done | bytes 1114144 | tf_op jit(solution)/shard_map/ppermute | solution.py:31
  317.3 34.3 %dispatch.2 = (bf16[4,2,384,2048]{3,2,1,0:T(8,128)(2,1)}, f32[4,2,384,1024]{3,2,1,0:T(8,128)}) custom-call(bf16[256,2176]{1,0:T(8,128)(2,1)} %bitcast.266, bf16[256,2176]{1,0:T(8,128)(2,1)} %bitcast.27.refs_1_, bf16[256,2176]{1,0:T(8,128)(2,1)} %bitcast.271, bf16[256,2176]{1,0:T(8,128)(2,1)} %bitcast.270, bf16[256,2176]{1,0:T(8,128)(2,1)} %bitcast.30.refs_4_, ...), custom_call_target="tpu_custom_call" | custom-call | flops 1 | bytes 1 | tf_op jit(solution)/shard_map/dispatch/pallas_call | solution.py:307
  355.0 14.7 %collective-permute-done.19 = bf16[2,128,2048]{2,1,0:T(8,128)(2,1)S(1)} collective-permute-done((bf16[2,128,2048]{2,1,0:T(8,128)(2,1)}, bf16[2,128,2048]{2,1,0:T(8,128)(2,1)S(1)}, u32[]{:S(2)}, u32[]{:S(2)}) %collective-permute-start.19) | collective-permute-done | bytes 1048608 | tf_op jit(solution)/shard_map/ppermute | solution.py:31
  371.8 24.0 %collective-permute-done.20.refs_1_ = bf16[2,128,2048]{2,1,0:T(8,128)(2,1)S(1)} collective-permute-done((bf16[2,128,2048]{2,1,0:T(8,128)(2,1)S(1)}, bf16[2,128,2048]{2,1,0:T(8,128)(2,1)S(1)}, u32[]{:S(2)}, u32[]{:S(2)}) %collective-permute-start.20) | collective-permute-done | bytes 1048608 | tf_op jit(solution)/shard_map/ppermute | solution.py:31
  399.6 18.7 %collective-permute-done.9.refs_0_ = bf16[2,128,2048]{2,1,0:T(8,128)(2,1)S(1)} collective-permute-done((bf16[2,128,2048]{2,1,0:T(8,128)(2,1)}, bf16[2,128,2048]{2,1,0:T(8,128)(2,1)S(1)}, u32[]{:S(2)}, u32[]{:S(2)}) %collective-permute-start.9) | collective-permute-done | bytes 1048608 | tf_op jit(solution)/shard_map/ppermute | solution.py:31
  419.3 21.6 %collective-permute-done.18 = bf16[2,128,2048]{2,1,0:T(8,128)(2,1)} collective-permute-done((bf16[2,128,2048]{2,1,0:T(8,128)(2,1)}, bf16[2,128,2048]{2,1,0:T(8,128)(2,1)}, u32[]{:S(2)}, u32[]{:S(2)}) %collective-permute-start.18) | collective-permute-done | bytes 1048608 | tf_op jit(solution)/shard_map/ppermute | solution.py:31
  440.9 33.1 %dispatch.3 = (bf16[4,2,384,2048]{3,2,1,0:T(8,128)(2,1)}, f32[4,2,384,1024]{3,2,1,0:T(8,128)}) custom-call(bf16[256,2048]{1,0:T(8,128)(2,1)} %multiply_convert_fusion.refs_0_, bf16[256,2048]{1,0:T(8,128)(2,1)} %bitcast.24.refs_1_, bf16[256,2048]{1,0:T(8,128)(2,1)} %bitcast.25.refs_2_, bf16[256,2048]{1,0:T(8,128)(2,1)} %bitcast.275, ...), custom_call_target="tpu_custom_call" | custom-call | flops 1 | bytes 1 | tf_op jit(solution)/shard_map/dispatch/pallas_call | solution.py:307
  478.3 31.7 %activate.1 = (bf16[4,2,384,1024]{3,2,1,0:T(8,128)(2,1)}, bf16[4,2,384,1024]{3,2,1,0:T(8,128)(2,1)}, bf16[4,2,384,1024]{3,2,1,0:T(8,128)(2,1)}) custom-call(bf16[4,2,384,2048]{3,2,1,0:T(8,128)(2,1)} %get-tuple-element.41.refs_1_.refs_0_, f32[4,2,384,1024]{3,2,1,0:T(8,128)} %get-tuple-element.42.refs_1_, f32[4,2,384,1024]{3,2,1,0:T(8,128)} %get-tuple-element.43.refs_2_, ...), custom_call_target="tpu_custom_call" | custom-call | flops 1 | bytes 1 | tf_op jit(solution)/shard_map/activate/pallas_call | solution.py:307
  515.3 24.1 %bank_grad.3.refs_1_.refs_9_ = bf16[4,2048,1024]{2,1,0:T(8,128)(2,1)} custom-call(bf16[4,2,384,2048]{3,2,1,0:T(8,128)(2,1)} %get-tuple-element.40.refs_1_.refs_0_, bf16[4,2,384,1024]{3,2,1,0:T(8,128)(2,1)} %get-tuple-element.44.refs_1_.refs_0_, bf16[2048,256]{1,0:T(8,128)(2,1)} %after.60.refs_2_, bf16[2048,256]{1,0:T(8,128)(2,1)} %after.59.refs_3_), custom_call_target="tpu_custom_call" | custom-call | flops 1 | bytes 1 | tf_op jit(solution)/shard_map/bank_grad/pallas_call | solution.py:307
  539.4 13.9 %copy.414.refs_0_ = bf16[4,2048,1024]{2,1,0:T(8,128)(2,1)} copy(bf16[4,2048,1024]{2,1,0:T(8,128)(2,1)} %bank_grad.3.refs_1_.refs_9_) | data formatting | bytes 33554432
  558.1 33.5 %combine.4 = (bf16[256,2048]{1,0:T(8,128)(2,1)}, bf16[256,2048]{1,0:T(8,128)(2,1)}, bf16[256,2048]{1,0:T(8,128)(2,1)}, bf16[256,2048]{1,0:T(8,128)(2,1)}) custom-call(bf16[4,2,384,1024]{3,2,1,0:T(8,128)(2,1)} %get-tuple-element.45.refs_0_.refs_1_, bf16[4,2,384,1024]{3,2,1,0:T(8,128)(2,1)} %get-tuple-element.46.refs_1_, ...), custom_call_target="tpu_custom_call" | custom-call | flops 1 | bytes 1 | tf_op jit(solution)/shard_map/combine/pallas_call | solution.py:307
  591.6 32.5 %combine.5 = (bf16[256,2048]{1,0:T(8,128)(2,1)}, bf16[256,2048]{1,0:T(8,128)(2,1)}, bf16[256,2048]{1,0:T(8,128)(2,1)}, bf16[256,2048]{1,0:T(8,128)(2,1)}) custom-call(bf16[4,2,384,1024]{3,2,1,0:T(8,128)(2,1)} %get-tuple-element.45.refs_0_.refs_1_, bf16[4,2,384,1024]{3,2,1,0:T(8,128)(2,1)} %get-tuple-element.46.refs_1_, ...), custom_call_target="tpu_custom_call" | custom-call | flops 1 | bytes 1 | tf_op jit(solution)/shard_map/combine/pallas_call | solution.py:307
  628.8 25.5 %bank_grad.4.refs_1_.refs_0_ = bf16[4,2048,1024]{2,1,0:T(8,128)(2,1)} custom-call(bf16[4,2,384,2048]{3,2,1,0:T(8,128)(2,1)} %get-tuple-element.41.refs_1_.refs_0_, bf16[4,2,384,1024]{3,2,1,0:T(8,128)(2,1)} %get-tuple-element.45.refs_0_.refs_1_, bf16[2,128,2048]{2,1,0:T(8,128)(2,1)} %after.63.refs_2_), custom_call_target="tpu_custom_call" | custom-call | flops 1 | bytes 1 | tf_op jit(solution)/shard_map/bank_grad/pallas_call | solution.py:307
  660.6 24.1 %bank_grad.5.refs_1_.refs_0_ = bf16[4,2048,1024]{2,1,0:T(8,128)(2,1)} custom-call(bf16[4,2,384,2048]{3,2,1,0:T(8,128)(2,1)} %get-tuple-element.41.refs_1_.refs_0_, bf16[4,2,384,1024]{3,2,1,0:T(8,128)(2,1)} %get-tuple-element.46.refs_1_, bf16[2,128,2048]{2,1,0:T(8,128)(2,1)} %after.64.refs_2_.refs_1_, bf16[2,128,2048]{2,1,0:T(8,128)(2,1)} %after.65.refs_3_.refs_2_), custom_call_target="tpu_custom_call" | custom-call | flops 1 | bytes 1 | tf_op jit(solution)/shard_map/bank_grad/pallas_call | solution.py:307
  691.1 3.7 collective-permute-start.34
  695.0 26.3 %combine.6 = (bf16[256,2048]{1,0:T(8,128)(2,1)}, bf16[256,2048]{1,0:T(8,128)(2,1)}, bf16[256,2048]{1,0:T(8,128)(2,1)}, bf16[256,2048]{1,0:T(8,128)(2,1)}) custom-call(bf16[4,2,384,1024]{3,2,1,0:T(8,128)(2,1)} %get-tuple-element.44.refs_1_.refs_0_, bf16[4,2048,1024]{2,1,0:T(8,128)(2,1)} %all-gather.10.cloned.1.call-done.refs_10_.refs_1_, ...), custom_call_target="tpu_custom_call" | custom-call | flops 1 | bytes 1 | tf_op jit(solution)/shard_map/combine/pallas_call | solution.py:307
  729.0 6.4 convolution_convert_fusion.refs_5_
  737.0 4.4 all-to-all-start.1
  753.2 15.5 %collective-permute-done.44.refs_0_ = bf16[2048,256]{1,0:T(8,128)(2,1)} collective-permute-done((bf16[2048,256]{1,0:T(8,128)(2,1)S(1)}, bf16[2048,256]{1,0:T(8,128)(2,1)}, u32[]{:S(2)}, u32[]{:S(2)}) %collective-permute-start.44) | collective-permute-done | bytes 1048608 | tf_op jit(solution)/shard_map/ppermute | solution.py:31
  770.9 25.0 %combine.7 = (bf16[256,2048]{1,0:T(8,128)(2,1)}, bf16[256,2048]{1,0:T(8,128)(2,1)}, bf16[256,2048]{1,0:T(8,128)(2,1)}, bf16[256,2048]{1,0:T(8,128)(2,1)}) custom-call(bf16[4,2,384,1024]{3,2,1,0:T(8,128)(2,1)} %get-tuple-element.44.refs_1_.refs_0_, bf16[4,2048,1024]{2,1,0:T(8,128)(2,1)} %all-gather.10.cloned.1.call-done.refs_10_.refs_1_, ...), custom_call_target="tpu_custom_call" | custom-call | flops 1 | bytes 1 | tf_op jit(solution)/shard_map/combine/pallas_call | solution.py:307
  806.7 33.2 %attend_back.1 = (bf16[8,2,128,768]{3,2,1,0:T(8,128)(2,1)S(1)}, f32[4,2,128]{2,1,0:T(2,128)S(1)}) custom-call(bf16[8,2,128,768]{3,2,1,0:T(8,128)(2,1)S(1)} %copy-done.3, bf16[8,2,128,256]{3,2,1,0:T(8,128)(2,1)S(1)} %copy-done.6, f32[1024,128]{1,0:T(8,128)S(1)} %copy-done.12, f32[1024,128]{1,0:T(8,128)S(1)} %copy-done.10, ...), custom_call_target="tpu_custom_call" | custom-call | flops 1 | bytes 1 | tf_op jit(solution)/shard_map/attend_back/pallas_call | solution.py:269
  842.8 12.3 %fusion.3 = (bf16[2048]{0:T(1024)(128)(2,1)S(1)}, bf16[8,2,128,2048]{3,2,1,0:T(8,128)(2,1)}) fusion(bf16[8,2,128,2048]{3,2,1,0:T(8,128)(2,1)} %copy-done.18, f32[8,2,128]{2,1,0:T(2,128)S(1)} %copy-done.89, bf16[8,2,128,768]{3,2,1,0:T(8,128)(2,1)S(1)} %get-tuple-element.59.refs_1_, bf16[2048,896]{1,0:T(8,128)(2,1)S(1)} %copy-done.77), kind=kOutput, calls=%fused_computation.10 | convolution fusion | flops 6463420416 | bytes 23080960 | tf_op jit(solution)/shard_map/smte,de->smtd/dot_general | solution.py:704
  855.1 4.4 slice_bitcast_fusion.16
  859.4 7.6 collective-permute-done.38.refs_0_
  872.1 4.6 all-to-all-start.2
  876.7 12.1 %fusion.82 = (bf16[2048,768]{1,0:T(8,128)(2,1)}, f32[2048,768]{1,0:T(8,128)}) fusion(bf16[8,2,128,768]{3,2,1,0:T(8,128)(2,1)S(1)} %copy-done.5, bf16[8,2,128,2048]{3,2,1,0:T(8,128)(2,1)} %copy-done.18, f32[2048]{0:T(1024)S(1)} %copy-done.81, f32[8,2,128]{2,1,0:T(2,128)S(1)} %copy-done.89), kind=kOutput, calls=%fused_computation.269 | convolution fusion | flops 6460801024 | bytes 20987904 | tf_op jit(solution)/shard_map/smtd,smte->de/dot_general | solution.py:698
  890.1 3.0 all-to-all-done.2
  893.1 6.2 fusion.83.refs_1_
  902.7 3.8 pad_maximum_fusion
  906.4 5.6 gather_fusion.2
  926.9 16.2 %collective-permute-done.36.refs_0_ = bf16[2,128,2048]{2,1,0:T(8,128)(2,1)S(1)} collective-permute-done((bf16[2,128,2048]{2,1,0:T(8,128)(2,1)S(1)}, bf16[2,128,2048]{2,1,0:T(8,128)(2,1)S(1)}, u32[]{:S(2)}, u32[]{:S(2)}) %collective-permute-start.36) | collective-permute-done | bytes 1048608 | tf_op jit(solution)/shard_map/ppermute | solution.py:31
  944.1 5.8 collective-permute-done.39.refs_0_
  954.5 11.2 %collective-permute-done.43.refs_0_ = bf16[2,128,2048]{2,1,0:T(8,128)(2,1)} collective-permute-done((bf16[2,128,2048]{2,1,0:T(8,128)(2,1)}, bf16[2,128,2048]{2,1,0:T(8,128)(2,1)}, u32[]{:S(2)}, u32[]{:S(2)}) %collective-permute-start.43) | collective-permute-done | bytes 1048608 | tf_op jit(solution)/shard_map/ppermute | solution.py:31
  966.8 3.7 collective-permute-done.46.refs_0_
  970.5 3.4 add_convert_fusion.2
  974.2 3.4 add_convert_fusion
  977.6 6.2 all-to-all-start.3
  988.3 10.5 collective-permute-done.40.refs_0_
  1002.1 11.7 %collective-permute-done.54.refs_0_ = f32[2,128]{1,0:T(2,128)S(1)} collective-permute-done((f32[2,128]{1,0:T(2,128)S(1)}, f32[2,128]{1,0:T(2,128)S(1)}, u32[]{:S(2)}, u32[]{:S(2)}) %collective-permute-start.54) | collective-permute-done | bytes 1056 | tf_op jit(solution)/shard_map/ppermute | solution.py:695
  1015.1 6.6 convert_element_type.457.refs_1_
  1021.8 3.5 add_convert_fusion.1
  1027.3 3.4 convert_add_fusion.16
  1030.7 5.3 collective-permute-done.55.refs_0_
  1037.2 4.7 collective-permute-start.56
  1042.0 24.1 %all-to-all-done.3 = bf16[8,64,1152]{2,1,0:T(8,128)(2,1)S(1)} async-done(((bf16[8,64,1152]{2,1,0:T(8,128)(2,1)}), bf16[8,64,1152]{2,1,0:T(8,128)(2,1)S(1)}, u32[]{:S(2)}, u32[]{:S(2)}) %all-to-all-start.3) | async-done | bytes 1179680 | tf_op jit(solution)/shard_map/all_to_all | solution.py:746
  1067.3 3.7 reshape.749
  1084.2 6.6 convert_element_type.451.refs_1_
  1098.8 6.8 convert_element_type.489
  (536 shorter events, 201.7 us)
Async XLA Ops:
  7.2 115.7 %all-gather.6.cloned.1.call-start = ((), (), s32[]{:S(2)}) async-start(), calls=%async_computation.7 | async-start | bytes 4587520 | tf_op jit(solution)/shard_map/all_gather | solution.py:510
  11.1 228.0 %all-gather.8.cloned.1.call-start = ((), (), s32[]{:S(2)}) async-start(), calls=%async_computation.8 | async-start | bytes 10485760 | tf_op jit(solution)/shard_map/all_gather | solution.py:510
  11.8 305.5 %all-gather.10.cloned.1.call-start = ((), (), s32[]{:S(2)}) async-start(), calls=%async_computation.9 | async-start | bytes 20971520 | tf_op jit(solution)/shard_map/all_gather | solution.py:510
  12.5 406.7 %all-gather.12.cloned.1.call-start = ((), (), s32[]{:S(2)}) async-start(), calls=%async_computation.10 | async-start | bytes 20971520 | tf_op jit(solution)/shard_map/all_gather | solution.py:510
  13.1 465.2 %all-gather.14.cloned.1.call-start = ((), (), s32[]{:S(2)}) async-start(), calls=%async_computation.11 | async-start | bytes 20971520 | tf_op jit(solution)/shard_map/all_gather | solution.py:510
  14.3 28.2 %collective-permute-start.1 = (bf16[2,128,2048]{2,1,0:T(8,128)(2,1)S(1)}, bf16[2,128,2048]{2,1,0:T(8,128)(2,1)S(1)}, u32[]{:S(2)}, u32[]{:S(2)}) collective-permute-start(bf16[2,128,2048]{2,1,0:T(8,128)(2,1)S(1)} %copy-done.36), channel_id=1, source_target_pairs={{0,2},{1,3},{2,4},{3,5},{4,6},{5,7},{6,0},{7,1},{8,10},{9,11},{10,... | collective-permute-start | bytes 3145736 | tf_op jit(solution)/shard_map/ppermute | solution.py:31
  17.4 51.5 %collective-permute-start = (bf16[2,128,2048]{2,1,0:T(8,128)(2,1)S(1)}, bf16[2,128,2048]{2,1,0:T(8,128)(2,1)}, u32[]{:S(2)}, u32[]{:S(2)}) collective-permute-start(bf16[2,128,2048]{2,1,0:T(8,128)(2,1)S(1)} %copy-done.36), channel_id=1, source_target_pairs={{0,1},{1,0},{2,3},{3,2},{4,5},{5,4},{6,7},{7,6},{8,9},{9,8},{10,11... | collective-permute-start | bytes 3145736 | tf_op jit(solution)/shard_map/ppermute | solution.py:31
  42.6 26.1 %collective-permute-start.3 = (bf16[2,128,2048]{2,1,0:T(8,128)(2,1)S(1)}, bf16[2,128,2048]{2,1,0:T(8,128)(2,1)S(1)}, u32[]{:S(2)}, u32[]{:S(2)}) collective-permute-start(bf16[2,128,2048]{2,1,0:T(8,128)(2,1)S(1)} %collective-permute-done.1), channel_id=1, source_target_pairs={{0,2},{1,3},{2,4},{3,5},{4,6},{5,7},{6,0},{7,1},{8,10},{9,11},{10,... | collective-permute-start | bytes 3145736 | tf_op jit(solution)/shard_map/ppermute | solution.py:31
  43.9 27.8 %collective-permute-start.2 = (bf16[2,128,2048]{2,1,0:T(8,128)(2,1)S(1)}, bf16[2,128,2048]{2,1,0:T(8,128)(2,1)S(1)}, u32[]{:S(2)}, u32[]{:S(2)}) collective-permute-start(bf16[2,128,2048]{2,1,0:T(8,128)(2,1)S(1)} %collective-permute-done.1), channel_id=1, source_target_pairs={{0,1},{1,0},{2,3},{3,2},{4,5},{5,4},{6,7},{7,6},{8,9},{9,8},{10,11... | collective-permute-start | bytes 3145736 | tf_op jit(solution)/shard_map/ppermute | solution.py:31
  68.7 25.4 %collective-permute-start.5 = (bf16[2,128,2048]{2,1,0:T(8,128)(2,1)S(1)}, bf16[2,128,2048]{2,1,0:T(8,128)(2,1)S(1)}, u32[]{:S(2)}, u32[]{:S(2)}) collective-permute-start(bf16[2,128,2048]{2,1,0:T(8,128)(2,1)S(1)} %collective-permute-done.3), channel_id=1, source_target_pairs={{0,2},{1,3},{2,4},{3,5},{4,6},{5,7},{6,0},{7,1},{8,10},{9,11},{10,... | collective-permute-start | bytes 3145736 | tf_op jit(solution)/shard_map/ppermute | solution.py:31
  70.2 25.0 %collective-permute-start.4 = (bf16[2,128,2048]{2,1,0:T(8,128)(2,1)S(1)}, bf16[2,128,2048]{2,1,0:T(8,128)(2,1)S(1)}, u32[]{:S(2)}, u32[]{:S(2)}) collective-permute-start(bf16[2,128,2048]{2,1,0:T(8,128)(2,1)S(1)} %collective-permute-done.3), channel_id=1, source_target_pairs={{0,1},{1,0},{2,3},{3,2},{4,5},{5,4},{6,7},{7,6},{8,9},{9,8},{10,11... | collective-permute-start | bytes 3145736 | tf_op jit(solution)/shard_map/ppermute | solution.py:31
  94.1 22.5 %collective-permute-start.6 = (bf16[2,128,2048]{2,1,0:T(8,128)(2,1)S(1)}, bf16[2,128,2048]{2,1,0:T(8,128)(2,1)S(1)}, u32[]{:S(2)}, u32[]{:S(2)}) collective-permute-start(bf16[2,128,2048]{2,1,0:T(8,128)(2,1)S(1)} %collective-permute-done.5), channel_id=1, source_target_pairs={{0,1},{1,0},{2,3},{3,2},{4,5},{5,4},{6,7},{7,6},{8,9},{9,8},{10,11... | collective-permute-start | bytes 3145736 | tf_op jit(solution)/shard_map/ppermute | solution.py:31
  158.2 77.7 %all-to-all-start = ((bf16[8,2,128,256]{3,2,1,0:T(8,128)(2,1)}), bf16[8,2,128,256]{3,2,1,0:T(8,128)(2,1)}, u32[]{:S(2)}, u32[]{:S(2)}) async-start(bf16[8,2,128,256]{3,2,1,0:T(8,128)(2,1)} %broadcast_select_fusion.2), calls=%async_computation | async-start | bytes 2097152 | tf_op jit(solution)/shard_map/all_to_all | solution.py:557
  163.5 851.6 %reduce-scatter.6.cloned.1.call-start = ((), (), s32[]{:S(2)}) async-start(), calls=%async_computation.13 | async-start | bytes 20971520 | tf_op jit(solution)/shard_map/reduce_scatter | solution.py:660
  166.1 41.1 %collective-permute-start.11 = (bf16[2,128,2176]{2,1,0:T(8,128)(2,1)}, bf16[2,128,2176]{2,1,0:T(8,128)(2,1)S(1)}, u32[]{:S(2)}, u32[]{:S(2)}) collective-permute-start(bf16[2,128,2176]{2,1,0:T(8,128)(2,1)} %after.49), channel_id=1, source_target_pairs={{0,2},{1,3},{2,4},{3,5},{4,6},{5,7},{6,0},{7,1},{8,10},{9,11},{10,... | collective-permute-start | bytes 3342344 | tf_op jit(solution)/shard_map/ppermute | solution.py:31
  168.1 80.9 %collective-permute-start.10 = (bf16[2,128,2176]{2,1,0:T(8,128)(2,1)}, bf16[2,128,2176]{2,1,0:T(8,128)(2,1)}, u32[]{:S(2)}, u32[]{:S(2)}) collective-permute-start(bf16[2,128,2176]{2,1,0:T(8,128)(2,1)} %after.49), channel_id=1, source_target_pairs={{0,1},{1,0},{2,3},{3,2},{4,5},{5,4},{6,7},{7,6},{8,9},{9,8},{10,11... | collective-permute-start | bytes 3342344 | tf_op jit(solution)/shard_map/ppermute | solution.py:31
  208.2 44.9 %collective-permute-start.12 = (bf16[2,128,2176]{2,1,0:T(8,128)(2,1)}, bf16[2,128,2176]{2,1,0:T(8,128)(2,1)S(1)}, u32[]{:S(2)}, u32[]{:S(2)}) collective-permute-start(bf16[2,128,2176]{2,1,0:T(8,128)(2,1)} %after.51), channel_id=1, source_target_pairs={{0,1},{1,0},{2,3},{3,2},{4,5},{5,4},{6,7},{7,6},{8,9},{9,8},{10,11... | collective-permute-start | bytes 3342344 | tf_op jit(solution)/shard_map/ppermute | solution.py:31
  209.5 38.5 %collective-permute-start.13 = (bf16[2,128,2176]{2,1,0:T(8,128)(2,1)}, bf16[2,128,2176]{2,1,0:T(8,128)(2,1)}, u32[]{:S(2)}, u32[]{:S(2)}) collective-permute-start(bf16[2,128,2176]{2,1,0:T(8,128)(2,1)} %after.51), channel_id=1, source_target_pairs={{0,2},{1,3},{2,4},{3,5},{4,6},{5,7},{6,0},{7,1},{8,10},{9,11},{10,... | collective-permute-start | bytes 3342344 | tf_op jit(solution)/shard_map/ppermute | solution.py:31
  248.0 28.9 %collective-permute-start.15 = (bf16[2,128,2176]{2,1,0:T(8,128)(2,1)}, bf16[2,128,2176]{2,1,0:T(8,128)(2,1)}, u32[]{:S(2)}, u32[]{:S(2)}) collective-permute-start(bf16[2,128,2176]{2,1,0:T(8,128)(2,1)} %after.53), channel_id=1, source_target_pairs={{0,2},{1,3},{2,4},{3,5},{4,6},{5,7},{6,0},{7,1},{8,10},{9,11},{10,... | collective-permute-start | bytes 3342344 | tf_op jit(solution)/shard_map/ppermute | solution.py:31
  250.0 42.9 %collective-permute-start.14 = (bf16[2,128,2176]{2,1,0:T(8,128)(2,1)}, bf16[2,128,2176]{2,1,0:T(8,128)(2,1)}, u32[]{:S(2)}, u32[]{:S(2)}) collective-permute-start(bf16[2,128,2176]{2,1,0:T(8,128)(2,1)} %after.53), channel_id=1, source_target_pairs={{0,1},{1,0},{2,3},{3,2},{4,5},{5,4},{6,7},{7,6},{8,9},{9,8},{10,11... | collective-permute-start | bytes 3342344 | tf_op jit(solution)/shard_map/ppermute | solution.py:31
  251.2 41.2 %collective-permute-start.8 = (bf16[2,128,2048]{2,1,0:T(8,128)(2,1)S(1)}, bf16[2,128,2048]{2,1,0:T(8,128)(2,1)}, u32[]{:S(2)}, u32[]{:S(2)}) collective-permute-start(bf16[2,128,2048]{2,1,0:T(8,128)(2,1)S(1)} %bitcast.262), channel_id=1, source_target_pairs={{0,2},{1,3},{2,4},{3,5},{4,6},{5,7},{6,0},{7,1},{8,10},{9,11},{10,... | collective-permute-start | bytes 3145736 | tf_op jit(solution)/shard_map/ppermute | solution.py:31
  252.2 65.1 %collective-permute-start.7 = (bf16[2,128,2048]{2,1,0:T(8,128)(2,1)S(1)}, bf16[2,128,2048]{2,1,0:T(8,128)(2,1)}, u32[]{:S(2)}, u32[]{:S(2)}) collective-permute-start(bf16[2,128,2048]{2,1,0:T(8,128)(2,1)S(1)} %bitcast.263), channel_id=1, source_target_pairs={{0,1},{1,0},{2,3},{3,2},{4,5},{5,4},{6,7},{7,6},{8,9},{9,8},{10,11... | collective-permute-start | bytes 3145736 | tf_op jit(solution)/shard_map/ppermute | solution.py:31
  276.9 36.6 %collective-permute-start.16 = (bf16[2,128,2176]{2,1,0:T(8,128)(2,1)}, bf16[2,128,2176]{2,1,0:T(8,128)(2,1)}, u32[]{:S(2)}, u32[]{:S(2)}) collective-permute-start(bf16[2,128,2176]{2,1,0:T(8,128)(2,1)} %collective-permute-done.15), channel_id=1, source_target_pairs={{0,1},{1,0},{2,3},{3,2},{4,5},{5,4},{6,7},{7,6},{8,9},{9,8},{10,11... | collective-permute-start | bytes 3342344 | tf_op jit(solution)/shard_map/ppermute | solution.py:31
  292.4 59.2 %collective-permute-start.17 = (bf16[2,128,2048]{2,1,0:T(8,128)(2,1)}, bf16[2,128,2048]{2,1,0:T(8,128)(2,1)S(1)}, u32[]{:S(2)}, u32[]{:S(2)}) collective-permute-start(bf16[2,128,2048]{2,1,0:T(8,128)(2,1)} %collective-permute-done.8.refs_12_), channel_id=1, source_target_pairs={{0,2},{1,3},{2,4},{3,5},{4,6},{5,7},{6,0},{7,1},{8,10},{9,11},{10,... | collective-permute-start | bytes 3145736 | tf_op jit(solution)/shard_map/ppermute | solution.py:31
  369.7 26.1 %collective-permute-start.20 = (bf16[2,128,2048]{2,1,0:T(8,128)(2,1)S(1)}, bf16[2,128,2048]{2,1,0:T(8,128)(2,1)S(1)}, u32[]{:S(2)}, u32[]{:S(2)}) collective-permute-start(bf16[2,128,2048]{2,1,0:T(8,128)(2,1)S(1)} %collective-permute-done.19), channel_id=1, source_target_pairs={{0,1},{1,0},{2,3},{3,2},{4,5},{5,4},{6,7},{7,6},{8,9},{9,8},{10,11... | collective-permute-start | bytes 3145736 | tf_op jit(solution)/shard_map/ppermute | solution.py:31
  369.7 48.6 %collective-permute-start.9 = (bf16[2,128,2048]{2,1,0:T(8,128)(2,1)}, bf16[2,128,2048]{2,1,0:T(8,128)(2,1)S(1)}, u32[]{:S(2)}, u32[]{:S(2)}) collective-permute-start(bf16[2,128,2048]{2,1,0:T(8,128)(2,1)} %collective-permute-done.8.refs_12_), channel_id=1, source_target_pairs={{0,1},{1,0},{2,3},{3,2},{4,5},{5,4},{6,7},{7,6},{8,9},{9,8},{10,11... | collective-permute-start | bytes 3145736 | tf_op jit(solution)/shard_map/ppermute | solution.py:31
  371.7 69.1 %collective-permute-start.18 = (bf16[2,128,2048]{2,1,0:T(8,128)(2,1)}, bf16[2,128,2048]{2,1,0:T(8,128)(2,1)}, u32[]{:S(2)}, u32[]{:S(2)}) collective-permute-start(bf16[2,128,2048]{2,1,0:T(8,128)(2,1)} %after.55), channel_id=1, source_target_pairs={{0,1},{1,0},{2,3},{3,2},{4,5},{5,4},{6,7},{7,6},{8,9},{9,8},{10,11... | collective-permute-start | bytes 3145736 | tf_op jit(solution)/shard_map/ppermute | solution.py:31
  396.8 77.2 %collective-permute-start.22 = (bf16[2048,256]{1,0:T(8,128)(2,1)}, bf16[2048,256]{1,0:T(8,128)(2,1)S(1)}, u32[]{:S(2)}, u32[]{:S(2)}) collective-permute-start(bf16[2048,256]{1,0:T(8,128)(2,1)} %after.56), channel_id=1, source_target_pairs={{0,2},{1,3},{2,4},{3,5},{4,6},{5,7},{6,0},{7,1},{8,10},{9,11},{10,... | collective-permute-start | bytes 3145736 | tf_op jit(solution)/shard_map/ppermute | solution.py:31
  419.3 58.1 %collective-permute-start.21 = (bf16[2048,256]{1,0:T(8,128)(2,1)}, bf16[2048,256]{1,0:T(8,128)(2,1)S(1)}, u32[]{:S(2)}, u32[]{:S(2)}) collective-permute-start(bf16[2048,256]{1,0:T(8,128)(2,1)} %after.56), channel_id=1, source_target_pairs={{0,1},{1,0},{2,3},{3,2},{4,5},{5,4},{6,7},{7,6},{8,9},{9,8},{10,11... | collective-permute-start | bytes 3145736 | tf_op jit(solution)/shard_map/ppermute | solution.py:31
  474.9 35.1 %collective-permute-start.23 = (bf16[2048,256]{1,0:T(8,128)(2,1)}, bf16[2048,256]{1,0:T(8,128)(2,1)S(1)}, u32[]{:S(2)}, u32[]{:S(2)}) collective-permute-start(bf16[2048,256]{1,0:T(8,128)(2,1)} %after.58.refs_5_), channel_id=1, source_target_pairs={{0,2},{1,3},{2,4},{3,5},{4,6},{5,7},{6,0},{7,1},{8,10},{9,11},{10,... | collective-permute-start | bytes 3145736 | tf_op jit(solution)/shard_map/ppermute | solution.py:31
  477.3 37.0 %collective-permute-start.25 = (bf16[2048,256]{1,0:T(8,128)(2,1)}, bf16[2048,256]{1,0:T(8,128)(2,1)S(1)}, u32[]{:S(2)}, u32[]{:S(2)}) collective-permute-start(bf16[2048,256]{1,0:T(8,128)(2,1)} %after.58.refs_5_), channel_id=1, source_target_pairs={{0,1},{1,0},{2,3},{3,2},{4,5},{5,4},{6,7},{7,6},{8,9},{9,8},{10,11... | collective-permute-start | bytes 3145736 | tf_op jit(solution)/shard_map/ppermute | solution.py:31
  511.1 42.2 %collective-permute-start.26 = (bf16[2048,256]{1,0:T(8,128)(2,1)}, bf16[2048,256]{1,0:T(8,128)(2,1)S(1)}, u32[]{:S(2)}, u32[]{:S(2)}) collective-permute-start(bf16[2048,256]{1,0:T(8,128)(2,1)} %after.59.refs_3_), channel_id=1, source_target_pairs={{0,2},{1,3},{2,4},{3,5},{4,6},{5,7},{6,0},{7,1},{8,10},{9,11},{10,... | collective-permute-start | bytes 3145736 | tf_op jit(solution)/shard_map/ppermute | solution.py:31
  512.3 41.9 %collective-permute-start.24 = (bf16[2048,256]{1,0:T(8,128)(2,1)}, bf16[2048,256]{1,0:T(8,128)(2,1)S(1)}, u32[]{:S(2)}, u32[]{:S(2)}) collective-permute-start(bf16[2048,256]{1,0:T(8,128)(2,1)} %after.59.refs_3_), channel_id=1, source_target_pairs={{0,1},{1,0},{2,3},{3,2},{4,5},{5,4},{6,7},{7,6},{8,9},{9,8},{10,11... | collective-permute-start | bytes 3145736 | tf_op jit(solution)/shard_map/ppermute | solution.py:31
  555.2 529.0 %reduce-scatter.4.cloned.1.call-start = ((), (), s32[]{:S(2)}) async-start(), calls=%async_computation.12 | async-start | bytes 20971520 | tf_op jit(solution)/shard_map/reduce_scatter | solution.py:660
  591.6 34.5 %collective-permute-start.29 = (bf16[2,128,2048]{2,1,0:T(8,128)(2,1)}, bf16[2,128,2048]{2,1,0:T(8,128)(2,1)S(1)}, u32[]{:S(2)}, u32[]{:S(2)}) collective-permute-start(bf16[2,128,2048]{2,1,0:T(8,128)(2,1)} %bitcast.320), channel_id=1, source_target_pairs={{0,1},{1,0},{2,3},{3,2},{4,5},{5,4},{6,7},{7,6},{8,9},{9,8},{10,11... | collective-permute-start | bytes 3145736 | tf_op jit(solution)/shard_map/ppermute | solution.py:31
  624.0 30.3 %collective-permute-start.28 = (bf16[2,128,2048]{2,1,0:T(8,128)(2,1)}, bf16[2,128,2048]{2,1,0:T(8,128)(2,1)S(1)}, u32[]{:S(2)}, u32[]{:S(2)}) collective-permute-start(bf16[2,128,2048]{2,1,0:T(8,128)(2,1)} %bitcast.319), channel_id=1, source_target_pairs={{0,1},{1,0},{2,3},{3,2},{4,5},{5,4},{6,7},{7,6},{8,9},{9,8},{10,11... | collective-permute-start | bytes 3145736 | tf_op jit(solution)/shard_map/ppermute | solution.py:31
  628.7 26.6 %collective-permute-start.30 = (bf16[2,128,2048]{2,1,0:T(8,128)(2,1)S(1)}, bf16[2,128,2048]{2,1,0:T(8,128)(2,1)S(1)}, u32[]{:S(2)}, u32[]{:S(2)}) collective-permute-start(bf16[2,128,2048]{2,1,0:T(8,128)(2,1)S(1)} %fusion.27), channel_id=1, source_target_pairs={{0,2},{1,3},{2,4},{3,5},{4,6},{5,7},{6,0},{7,1},{8,10},{9,11},{10,... | collective-permute-start | bytes 3145736 | tf_op jit(solution)/shard_map/ppermute | solution.py:31
  656.3 442.5 %reduce-scatter.8.cloned.1.call-start = ((), (), s32[]{:S(2)}) async-start(), calls=%async_computation.14 | async-start | bytes 20971520 | tf_op jit(solution)/shard_map/reduce_scatter | solution.py:660
  656.3 28.4 %collective-permute-start.27 = (bf16[2,128,2048]{2,1,0:T(8,128)(2,1)}, bf16[2,128,2048]{2,1,0:T(8,128)(2,1)S(1)}, u32[]{:S(2)}, u32[]{:S(2)}) collective-permute-start(bf16[2,128,2048]{2,1,0:T(8,128)(2,1)} %bitcast.317), channel_id=1, source_target_pairs={{0,1},{1,0},{2,3},{3,2},{4,5},{5,4},{6,7},{7,6},{8,9},{9,8},{10,11... | collective-permute-start | bytes 3145736 | tf_op jit(solution)/shard_map/ppermute | solution.py:31
  660.6 25.1 %collective-permute-start.31 = (bf16[2,128,2048]{2,1,0:T(8,128)(2,1)}, bf16[2,128,2048]{2,1,0:T(8,128)(2,1)S(1)}, u32[]{:S(2)}, u32[]{:S(2)}) collective-permute-start(bf16[2,128,2048]{2,1,0:T(8,128)(2,1)} %add_convert_fusion.6), channel_id=1, source_target_pairs={{0,2},{1,3},{2,4},{3,5},{4,6},{5,7},{6,0},{7,1},{8,10},{9,11},{10,... | collective-permute-start | bytes 3145736 | tf_op jit(solution)/shard_map/ppermute | solution.py:31
  686.7 34.6 %collective-permute-start.33 = (bf16[2,128,2048]{2,1,0:T(8,128)(2,1)}, bf16[2,128,2048]{2,1,0:T(8,128)(2,1)S(1)}, u32[]{:S(2)}, u32[]{:S(2)}) collective-permute-start(bf16[2,128,2048]{2,1,0:T(8,128)(2,1)} %bitcast.316), channel_id=1, source_target_pairs={{0,1},{1,0},{2,3},{3,2},{4,5},{5,4},{6,7},{7,6},{8,9},{9,8},{10,11... | collective-permute-start | bytes 3145736 | tf_op jit(solution)/shard_map/ppermute | solution.py:31
  691.1 31.2 %collective-permute-start.34 = (bf16[2,128,2048]{2,1,0:T(8,128)(2,1)}, bf16[2,128,2048]{2,1,0:T(8,128)(2,1)S(1)}, u32[]{:S(2)}, u32[]{:S(2)}) collective-permute-start(bf16[2,128,2048]{2,1,0:T(8,128)(2,1)} %add_convert_fusion.5), channel_id=1, source_target_pairs={{0,2},{1,3},{2,4},{3,5},{4,6},{5,7},{6,0},{7,1},{8,10},{9,11},{10,... | collective-permute-start | bytes 3145736 | tf_op jit(solution)/shard_map/ppermute | solution.py:31
  737.0 60.2 %all-to-all-start.1 = ((bf16[8,2,128,256]{3,2,1,0:T(8,128)(2,1)}), bf16[8,2,128,256]{3,2,1,0:T(8,128)(2,1)}, u32[]{:S(2)}, u32[]{:S(2)}) async-start(bf16[8,2,128,256]{3,2,1,0:T(8,128)(2,1)} %bitcast.256), calls=%async_computation.1 | async-start | bytes 2097152 | tf_op jit(solution)/shard_map/all_to_all | solution.py:676
  744.9 23.7 %collective-permute-start.44 = (bf16[2048,256]{1,0:T(8,128)(2,1)S(1)}, bf16[2048,256]{1,0:T(8,128)(2,1)}, u32[]{:S(2)}, u32[]{:S(2)}) collective-permute-start(bf16[2048,256]{1,0:T(8,128)(2,1)S(1)} %copy-done.26), channel_id=1, source_target_pairs={{0,1},{1,0},{2,3},{3,2},{4,5},{5,4},{6,7},{7,6},{8,9},{9,8},{10,11... | collective-permute-start | bytes 3145736 | tf_op jit(solution)/shard_map/ppermute | solution.py:31
  748.8 51.4 %collective-permute-start.35 = (bf16[2,128,2048]{2,1,0:T(8,128)(2,1)}, bf16[2,128,2048]{2,1,0:T(8,128)(2,1)}, u32[]{:S(2)}, u32[]{:S(2)}) collective-permute-start(bf16[2,128,2048]{2,1,0:T(8,128)(2,1)} %bitcast.307), channel_id=1, source_target_pairs={{0,1},{1,0},{2,3},{3,2},{4,5},{5,4},{6,7},{7,6},{8,9},{9,8},{10,11... | collective-permute-start | bytes 3145736 | tf_op jit(solution)/shard_map/ppermute | solution.py:31
  795.9 59.1 %collective-permute-start.37 = (bf16[2,128,2048]{2,1,0:T(8,128)(2,1)}, bf16[2,128,2048]{2,1,0:T(8,128)(2,1)}, u32[]{:S(2)}, u32[]{:S(2)}) collective-permute-start(bf16[2,128,2048]{2,1,0:T(8,128)(2,1)} %bitcast.318), channel_id=1, source_target_pairs={{0,1},{1,0},{2,3},{3,2},{4,5},{5,4},{6,7},{7,6},{8,9},{9,8},{10,11... | collective-permute-start | bytes 3145736 | tf_op jit(solution)/shard_map/ppermute | solution.py:31
  842.4 24.6 %collective-permute-start.38 = (bf16[2,128,2048]{2,1,0:T(8,128)(2,1)S(1)}, bf16[2,128,2048]{2,1,0:T(8,128)(2,1)S(1)}, u32[]{:S(2)}, u32[]{:S(2)}) collective-permute-start(bf16[2,128,2048]{2,1,0:T(8,128)(2,1)S(1)} %fusion.20), channel_id=1, source_target_pairs={{0,2},{1,3},{2,4},{3,5},{4,6},{5,7},{6,0},{7,1},{8,10},{9,11},{10,... | collective-permute-start | bytes 3145736 | tf_op jit(solution)/shard_map/ppermute | solution.py:31
  868.0 21.1 %collective-permute-start.45 = (bf16[2,128,2048]{2,1,0:T(8,128)(2,1)}, bf16[2,128,2048]{2,1,0:T(8,128)(2,1)}, u32[]{:S(2)}, u32[]{:S(2)}) collective-permute-start(bf16[2,128,2048]{2,1,0:T(8,128)(2,1)} %get-tuple-element.80), channel_id=1, source_target_pairs={{0,1},{1,0},{2,3},{3,2},{4,5},{5,4},{6,7},{7,6},{8,9},{9,8},{10,11... | collective-permute-start | bytes 3145736 | tf_op jit(solution)/shard_map/ppermute | solution.py:31
  872.1 21.0 %all-to-all-start.2 = ((bf16[8,2,128,256]{3,2,1,0:T(8,128)(2,1)}), bf16[8,2,128,256]{3,2,1,0:T(8,128)(2,1)}, u32[]{:S(2)}, u32[]{:S(2)}) async-start(bf16[8,2,128,256]{3,2,1,0:T(8,128)(2,1)} %bitcast.280), calls=%async_computation.4 | async-start | bytes 2097152 | tf_op jit(solution)/shard_map/all_to_all | solution.py:676
  917.0 26.1 %collective-permute-start.36 = (bf16[2,128,2048]{2,1,0:T(8,128)(2,1)S(1)}, bf16[2,128,2048]{2,1,0:T(8,128)(2,1)S(1)}, u32[]{:S(2)}, u32[]{:S(2)}) collective-permute-start(bf16[2,128,2048]{2,1,0:T(8,128)(2,1)S(1)} %bitcast.315), channel_id=1, source_target_pairs={{0,1},{1,0},{2,3},{3,2},{4,5},{5,4},{6,7},{7,6},{8,9},{9,8},{10,11... | collective-permute-start | bytes 3145736 | tf_op jit(solution)/shard_map/ppermute | solution.py:31
  918.1 47.6 %collective-permute-start.43 = (bf16[2,128,2048]{2,1,0:T(8,128)(2,1)}, bf16[2,128,2048]{2,1,0:T(8,128)(2,1)}, u32[]{:S(2)}, u32[]{:S(2)}) collective-permute-start(bf16[2,128,2048]{2,1,0:T(8,128)(2,1)} %get-tuple-element.81), channel_id=1, source_target_pairs={{0,1},{1,0},{2,3},{3,2},{4,5},{5,4},{6,7},{7,6},{8,9},{9,8},{10,11... | collective-permute-start | bytes 3145736 | tf_op jit(solution)/shard_map/ppermute | solution.py:31
  921.8 28.1 %collective-permute-start.39 = (bf16[2,128,2048]{2,1,0:T(8,128)(2,1)}, bf16[2,128,2048]{2,1,0:T(8,128)(2,1)S(1)}, u32[]{:S(2)}, u32[]{:S(2)}) collective-permute-start(bf16[2,128,2048]{2,1,0:T(8,128)(2,1)} %add_convert_fusion.4), channel_id=1, source_target_pairs={{0,2},{1,3},{2,4},{3,5},{4,6},{5,7},{6,0},{7,1},{8,10},{9,11},{10,... | collective-permute-start | bytes 3145736 | tf_op jit(solution)/shard_map/ppermute | solution.py:31
  924.7 45.8 %collective-permute-start.46 = (bf16[2,128,2048]{2,1,0:T(8,128)(2,1)}, bf16[2,128,2048]{2,1,0:T(8,128)(2,1)}, u32[]{:S(2)}, u32[]{:S(2)}) collective-permute-start(bf16[2,128,2048]{2,1,0:T(8,128)(2,1)} %fusion.16), channel_id=1, source_target_pairs={{0,2},{1,3},{2,4},{3,5},{4,6},{5,7},{6,0},{7,1},{8,10},{9,11},{10,... | collective-permute-start | bytes 3145736 | tf_op jit(solution)/shard_map/ppermute | solution.py:31
  925.5 48.4 %collective-permute-start.49 = (bf16[512,1152]{1,0:T(8,128)(2,1)}, bf16[512,1152]{1,0:T(8,128)(2,1)}, u32[]{:S(2)}, u32[]{:S(2)}) collective-permute-start(bf16[512,1152]{1,0:T(8,128)(2,1)} %get-tuple-element.83), channel_id=1, source_target_pairs={{0,8},{8,0},{16,24},{24,16},{1,9},{9,1},{17,25},{25,17},{2,10},{10... | collective-permute-start | bytes 3538952 | tf_op jit(solution)/shard_map/ppermute | solution.py:31
  943.1 31.1 %collective-permute-start.51 = (bf16[512,1152]{1,0:T(8,128)(2,1)}, bf16[512,1152]{1,0:T(8,128)(2,1)}, u32[]{:S(2)}, u32[]{:S(2)}) collective-permute-start(bf16[512,1152]{1,0:T(8,128)(2,1)} %fusion.13), channel_id=1, source_target_pairs={{0,16},{8,24},{16,0},{24,8},{1,17},{9,25},{17,1},{25,9},{2,18},{10... | collective-permute-start | bytes 3538952 | tf_op jit(solution)/shard_map/ppermute | solution.py:31
  949.9 38.4 %collective-permute-start.32 = (bf16[2,128,2048]{2,1,0:T(8,128)(2,1)}, bf16[2,128,2048]{2,1,0:T(8,128)(2,1)}, u32[]{:S(2)}, u32[]{:S(2)}) collective-permute-start(bf16[2,128,2048]{2,1,0:T(8,128)(2,1)} %bitcast.314), channel_id=1, source_target_pairs={{0,1},{1,0},{2,3},{3,2},{4,5},{5,4},{6,7},{7,6},{8,9},{9,8},{10,11... | collective-permute-start | bytes 3145736 | tf_op jit(solution)/shard_map/ppermute | solution.py:31
  965.7 56.0 %collective-permute-start.42 = (bf16[2,128,2048]{2,1,0:T(8,128)(2,1)}, bf16[2,128,2048]{2,1,0:T(8,128)(2,1)}, u32[]{:S(2)}, u32[]{:S(2)}) collective-permute-start(bf16[2,128,2048]{2,1,0:T(8,128)(2,1)} %get-tuple-element.82), channel_id=1, source_target_pairs={{0,1},{1,0},{2,3},{3,2},{4,5},{5,4},{6,7},{7,6},{8,9},{9,8},{10,11... | collective-permute-start | bytes 3145736 | tf_op jit(solution)/shard_map/ppermute | solution.py:31
  970.5 28.3 %collective-permute-start.40 = (bf16[2,128,2048]{2,1,0:T(8,128)(2,1)}, bf16[2,128,2048]{2,1,0:T(8,128)(2,1)}, u32[]{:S(2)}, u32[]{:S(2)}) collective-permute-start(bf16[2,128,2048]{2,1,0:T(8,128)(2,1)} %add_convert_fusion.3), channel_id=1, source_target_pairs={{0,2},{1,3},{2,4},{3,5},{4,6},{5,7},{6,0},{7,1},{8,10},{9,11},{10,... | collective-permute-start | bytes 3145736 | tf_op jit(solution)/shard_map/ppermute | solution.py:31
  973.9 47.8 %collective-permute-start.47 = (bf16[2,128,2048]{2,1,0:T(8,128)(2,1)}, bf16[2,128,2048]{2,1,0:T(8,128)(2,1)}, u32[]{:S(2)}, u32[]{:S(2)}) collective-permute-start(bf16[2,128,2048]{2,1,0:T(8,128)(2,1)} %add_convert_fusion.2), channel_id=1, source_target_pairs={{0,2},{1,3},{2,4},{3,5},{4,6},{5,7},{6,0},{7,1},{8,10},{9,11},{10,... | collective-permute-start | bytes 3145736 | tf_op jit(solution)/shard_map/ppermute | solution.py:31
  977.6 88.4 %all-to-all-start.3 = ((bf16[8,64,1152]{2,1,0:T(8,128)(2,1)}), bf16[8,64,1152]{2,1,0:T(8,128)(2,1)S(1)}, u32[]{:S(2)}, u32[]{:S(2)}) async-start(bf16[8,64,1152]{2,1,0:T(8,128)(2,1)} %bitcast.272), calls=%async_computation.5 | async-start | bytes 2359296 | tf_op jit(solution)/shard_map/all_to_all | solution.py:746
  1001.3 89.6 %collective-permute-start.41 = (bf16[2,128,2048]{2,1,0:T(8,128)(2,1)}, bf16[2,128,2048]{2,1,0:T(8,128)(2,1)S(1)}, u32[]{:S(2)}, u32[]{:S(2)}) collective-permute-start(bf16[2,128,2048]{2,1,0:T(8,128)(2,1)} %get-tuple-element.79), channel_id=1, source_target_pairs={{0,1},{1,0},{2,3},{3,2},{4,5},{5,4},{6,7},{7,6},{8,9},{9,8},{10,11... | collective-permute-start | bytes 3145736 | tf_op jit(solution)/shard_map/ppermute | solution.py:31
  1015.1 20.9 %collective-permute-start.55 = (f32[2,128]{1,0:T(2,128)S(1)}, f32[2,128]{1,0:T(2,128)S(1)}, u32[]{:S(2)}, u32[]{:S(2)}) collective-permute-start(f32[2,128]{1,0:T(2,128)S(1)} %add.477), channel_id=1, source_target_pairs={{0,2},{1,3},{2,0},{3,1},{4,6},{5,7},{6,4},{7,5},{8,10},{9,11},{10,... | collective-permute-start | bytes 3080 | tf_op jit(solution)/shard_map/ppermute | solution.py:695
  1025.3 66.6 %collective-permute-start.48 = (bf16[2,128,2048]{2,1,0:T(8,128)(2,1)}, bf16[2,128,2048]{2,1,0:T(8,128)(2,1)}, u32[]{:S(2)}, u32[]{:S(2)}) collective-permute-start(bf16[2,128,2048]{2,1,0:T(8,128)(2,1)} %add_convert_fusion.1), channel_id=1, source_target_pairs={{0,2},{1,3},{2,4},{3,5},{4,6},{5,7},{6,0},{7,1},{8,10},{9,11},{10,... | collective-permute-start | bytes 3145736 | tf_op jit(solution)/shard_map/ppermute | solution.py:31
  1037.2 45.2 %collective-permute-start.56 = (f32[2,128]{1,0:T(2,128)S(1)}, f32[2,128]{1,0:T(2,128)S(1)}, u32[]{:S(2)}, u32[]{:S(2)}) collective-permute-start(f32[2,128]{1,0:T(2,128)S(1)} %add.478), channel_id=1, source_target_pairs={{0,4},{1,5},{2,6},{3,7},{4,0},{5,1},{6,2},{7,3},{8,12},{9,13},{10,... | collective-permute-start | bytes 3080 | tf_op jit(solution)/shard_map/ppermute | solution.py:695
  (110 other events, 919.8 us)
Sparse Core Ops, SparseCore 0:
  11.2 34.2 all-gather.5
  47.0 58.2 all-gather.7
  106.9 105.9 all-gather.9
  214.2 105.9 all-gather.11
  321.6 105.9 all-gather.13
  555.4 125.0 reduce-scatter.5
  683.2 126.0 reduce-scatter.3
  811.9 126.1 reduce-scatter.7

commit v3 on v2

--- a/solution.py
+++ b/solution.py
@@ -52,15 +52,15 @@
     )(value, *others)
 
 
-def beside_step(moved, work):
-    if work is None:
-        return moved
-    return [after(v, work) for v in moved]
-
-
-def ring_gather(value, axis, work=(), then={}):
+def together(work, *moved):
+    moved = list(moved)
+    for k in range(len(moved)):
+        moved[k] = after(moved[k], *work, *moved[:k], *moved[k + 1 :])
+    return moved
+
+
+def ring_gather(value, axis, work=None, then={}):
     outer, inner = sizes(axis)
-    work = list(work) + [None] * (outer - len(work))
     blocks, arrived = [], []
     for a in range(outer):
         row = [value]
@@ -69,7 +69,8 @@
         moved = row[1:]
         if a + 1 < outer:
             moved.append(shift(value, axis, outer, inner, 1, 0))
-        moved = beside_step(moved, work[a] and work[a](arrived))
+        if work is not None:
+            moved = together([f(arrived) for f in work[a : a + 1] if f], *moved)
         if a in then:
             then[a](moved)
         blocks += [value] + moved[: inner - 1]
@@ -77,27 +78,44 @@
     return blocks
 
 
+def row_move(parts, a, axis):
+    outer, inner = sizes(axis)
+    row = parts[a * inner + 1 % inner]
+    for b in range(2, inner):
+        row = shift(row, axis, outer, inner, 0, 1)
+        row = (row.astype(f32) + parts[a * inner + b].astype(f32)).astype(bf16)
+    return shift(row, axis, outer, inner, 0, 1) if inner > 1 else row
+
+
+def row_sum(moved, parts, a, axis):
+    total = moved.astype(f32) + parts[a * sizes(axis)[1]].astype(f32)
+    return total.astype(bf16)
+
+
+def ahead(value, axis):
+    return shift(value, axis, *sizes(axis), 1, 0)
+
+
+def add(one, other):
+    return one.astype(f32) + other.astype(f32)
+
+
 def ring_scatter(parts, axis, work=(), then={}):
-    outer, inner = sizes(axis)
-    work = list(work) + [None] * (outer - len(work))
+    outer, _ = sizes(axis)
     total, arrived = None, []
     for step in range(outer):
         a = (step + 1) % outer
-        row = parts[a * inner + 1 % inner]
-        for b in range(2, inner):
-            row = shift(row, axis, outer, inner, 0, 1)
-            row = (row.astype(f32) + parts[a * inner + b].astype(f32)).astype(bf16)
-        moved = [shift(row, axis, outer, inner, 0, 1)] if inner > 1 else [row]
-        if total is not None:
-            moved.append(shift(total, axis, outer, inner, 1, 0))
-        moved = beside_step(moved, work[step] and work[step](arrived))
+        moved = [row_move(parts, a, axis)]
+        if step:
+            moved.append(ahead(total, axis))
+        moved = together([f(arrived) for f in work[step : step + 1]], *moved)
         if step in then:
             then[step](moved)
         arrived = moved
-        total = moved[0].astype(f32) + parts[a * inner].astype(f32)
+        total = row_sum(moved[0], parts, a, axis)
         if step:
-            total = total.astype(bf16).astype(f32) + moved[1].astype(f32)
-        if step + 1 < outer:
+            total = add(total, moved[1])
+        if step and step + 1 < outer:
             total = total.astype(bf16)
     return total
 
@@ -297,7 +315,7 @@
     )
 
 
-def call(kernel, name, grid, ins, outs, flops, scratch=(), ties=()):
+def call(kernel, name, grid, ins, outs, flops, scratch=(), ties=(), aliases={}):
     ties = [t for t in ties if t is not None]
     count = len(ins)
 
@@ -311,6 +329,7 @@
         out_specs=[spec for _, spec in outs],
         out_shape=[shape for shape, _ in outs],
         scratch_shapes=list(scratch),
+        input_output_aliases=aliases,
         compiler_params=pltpu.CompilerParams(vmem_limit_bytes=56 * 2**20),
         cost_estimate=little,
         name=name,
@@ -377,26 +396,23 @@
     grad_up_ref[0, 0] = (grad_hidden * gate_silu).astype(bf16)
 
 
-def activate(taken, gate_act, grad_hidden, w_up, ties=()):
-    count, _, capacity, _ = taken.shape
+def activate(taken, gate_act, grad_hidden, w_up, first, count, before, ties=()):
+    capacity = taken.shape[2]
 
     def of(width):
-        return pl.BlockSpec((1, 1, capacity, width), lambda e, h: (e, h, 0, 0))
-
-    result = jax.ShapeDtypeStruct((count, 2, capacity, FFE), bf16)
+        return pl.BlockSpec((1, 1, capacity, width), lambda e, h: (first + e, h, 0, 0))
+
+    result = jax.ShapeDtypeStruct(gate_act.shape, bf16)
+    bank = pl.BlockSpec((1,) + w_up.shape[1:], lambda e, h: (first + e, 0, 0))
     return call(
         act_kernel,
         "activate",
         (count, 2),
-        [
-            (taken, of(D)),
-            (gate_act, of(FFE)),
-            (grad_hidden, of(FFE)),
-            (w_up, spans(w_up.shape)),
-        ],
+        [(taken, of(D)), (gate_act, of(FFE)), (grad_hidden, of(FFE)), (w_up, bank)],
         [(result, of(FFE))] * 3,
         4 * count * capacity * D * FFE,
-        ties=ties,
+        ties=tuple(before) + tuple(ties),
+        aliases={4 + k: k for k in range(len(before))},
     )
 
 
@@ -406,16 +422,17 @@
     out_ref[0] = dot(left, right, 0, 0).astype(bf16)
 
 
-def bank_grad(left, right, ties=()):
-    count, _, capacity, _ = left.shape
+def bank_grad(left, right, ties=(), first=0, count=None):
+    capacity = left.shape[2]
+    count = count or left.shape[0]
     result = jax.ShapeDtypeStruct((count, D, FFE), bf16)
     return call(
         bank_kernel,
         "bank_grad",
         (count, D // part),
         [
-            (left, pl.BlockSpec((1, 2, capacity, part), lambda e, d: (e, 0, 0, d))),
-            (right, pl.BlockSpec((1, 2, capacity, FFE), lambda e, d: (e, 0, 0, 0))),
+            (left, pl.BlockSpec((1, 2, capacity, part), lambda e, d: (first + e, 0, 0, d))),
+            (right, pl.BlockSpec((1, 2, capacity, FFE), lambda e, d: (first + e, 0, 0, 0))),
         ],
         [(result, pl.BlockSpec((1, part, FFE), lambda e, d: (e, d, 0)))],
         4 * count * capacity * D * FFE,
@@ -512,10 +529,6 @@
     def gather_tokens(value):
         return jnp.stack(ring_gather(value, "seq"))
 
-    def scatter_tokens(parts, work=(), then={}):
-        parts = [v.reshape(micro, rows, D) for v in parts]
-        return ring_scatter(parts, "seq", work, then).reshape(tokens, D)
-
     columns = [
         lax.dynamic_slice_in_dim(w, seq_index * width, width, axis=1).reshape(-1, heads_local, HD)
         for w in (query_proj, key_proj, value_proj)
@@ -531,8 +544,14 @@
     w_gate = spread(expert_gate, 1)
     w_up = spread(expert_up, 1)
 
-    x_all = gather_tokens(layer_input)
-    x_wide = x_all.astype(f32)
+    weight_high = route_weights.astype(bf16)
+    weight_low = (route_weights - weight_high.astype(f32)).astype(bf16)
+    packed = jnp.concatenate(
+        [layer_input, routes.astype(bf16), weight_high, weight_low], axis=-1
+    )
+    packed = jnp.pad(packed, ((0, 0), (0, 0), (0, HD - 3 * TOP)))
+    packed = gather_tokens(packed)
+    x_wide = packed[..., :D].astype(f32)
     inv_all = rms_scale(x_wide)
     h_one = (x_wide * inv_all * gain_one).astype(bf16)
     qkv = jnp.einsum("smtd,de->smte", h_one, w_qkv, preferred_element_type=f32).astype(bf16)
@@ -562,17 +581,9 @@
     inv_two = rms_scale(middle)
     normed_two = middle * inv_two
     h_two_own = (normed_two * gain_two).astype(bf16).reshape(micro, rows, D)
-    weight_high = route_weights.astype(bf16)
-    weight_low = (route_weights - weight_high.astype(f32)).astype(bf16)
-    packed = jnp.concatenate([cotangent, routes.astype(bf16), weight_high, weight_low], axis=-1)
-    packed = jnp.pad(packed, ((0, 0), (0, 0), (0, HD - 3 * TOP)))
-    g_blocks = ring_gather(
-        after(packed, x_all),
-        "seq",
-        (lambda _: qkv, lambda _: h_two_own),
-    )
-
-    packed = jnp.stack([v[..., D : D + 3 * TOP] for v in g_blocks]).astype(f32)
+    h_blocks = ring_gather(h_two_own, "seq", ())
+
+    packed = packed[..., D : D + 3 * TOP].astype(f32)
     packed = packed.reshape(2, half, 3 * TOP)
     route_all = packed[..., :TOP].astype(jnp.int32)
     weight_all = packed[..., TOP : 2 * TOP] + packed[..., 2 * TOP :]
@@ -598,44 +609,54 @@
         done.update(found)
         return next(iter(found.values()))
 
-    def grad_work(ties):
-        grad_rows, grad_hidden = dispatch(g_blocks, slots, weights, w_down, capacity, True, ties)
-        return keep(grad_rows=grad_rows, grad_hidden=grad_hidden)
-
-    h_blocks = ring_gather(h_two_own, "seq", (None, grad_work))
-    grad_rows, grad_hidden = done["grad_rows"], done["grad_hidden"]
-
     def combined(acts, banks, h, scaled, ties=()):
         return combine(acts, banks, slot_columns, slots, weights, h, ns // 2, scaled, ties)
 
-    def take_work(_):
-        taken, gate_act = dispatch(h_blocks, slots, weights, w_gate, capacity, False)
+    def take_work(ties):
+        taken, gate_act = dispatch(h_blocks, slots, weights, w_gate, capacity, False, ties)
         return keep(taken=taken, gate_act=gate_act)
 
-    def act_work(ties):
-        hidden, grad_gate_act, grad_up_act = activate(
-            done["taken"], done["gate_act"], grad_hidden, w_up, ties
-        )
-        return keep(hidden=hidden, grad_gate_act=grad_gate_act, grad_up_act=grad_up_act)
-
-    def down_work(ties):
-        return keep(whole_down=bank_grad(grad_rows, done["hidden"], ties))
+    g_blocks = ring_gather(after(cotangent, h_blocks[-1]), "seq", (None, take_work))
+
+    def grad_work(_):
+        grad_rows, grad_hidden = dispatch(g_blocks, slots, weights, w_down, capacity, True)
+        return keep(grad_rows=grad_rows, grad_hidden=grad_hidden)
+
+    pair = local_experts // 2
+
+    def act_work(first):
+        def work(ties):
+            before = done.get("acts", ())
+            acts = activate(
+                done["taken"], done["gate_act"], done["grad_hidden"], w_up, first, pair, before, ties
+            )
+            whole = bank_grad(done["grad_rows"], acts[0], (), first, pair)
+            done.setdefault("whole_down", []).append(whole)
+            done["acts"] = acts
+            return whole
+
+        return work
+
+    def down_then(moved):
+        done.setdefault("sum_down", []).append(after(done["whole_down"][-1], *moved))
 
     def first_work(ties):
-        acts = (done["grad_gate_act"], done["grad_up_act"])
-        first = combined(acts, (w_gate, w_up), 0, False, tuple(ties) + (done["whole_down"],))
+        first = combined(done["acts"][1:], (w_gate, w_up), 0, False, ties)
         return keep(tail=first[0], first=first)
 
     o_all = ring_gather(
-        after(o_heads.reshape(group * micro, width), h_blocks[-1]),
+        after(o_heads.reshape(group * micro, width), g_blocks[-1]),
         "seq",
-        (take_work, act_work, down_work, first_work),
-        {2: lambda moved: keep(sum_down=after(done["whole_down"], *moved))},
-    )
+        (grad_work, act_work(0), act_work(pair), first_work),
+        {1: down_then, 2: down_then},
+    )
+    o_last = o_all[-1]
     o_all = jnp.concatenate(o_all, axis=1)
-    taken, hidden, first = done["taken"], done["hidden"], done["first"]
-    grad_gate_act, grad_up_act = done["grad_gate_act"], done["grad_up_act"]
-    second = combined((grad_gate_act, grad_up_act), (w_gate, w_up), 1, False, (first[0],))
+    taken, first = done["taken"], done["first"]
+    hidden, grad_gate_act, grad_up_act = done["acts"]
+    second = combined(
+        (grad_gate_act, grad_up_act), (w_gate, w_up), 1, False, (first[0], o_last)
+    )
 
     def gate_work(ties):
         return keep(whole_gate=bank_grad(taken, grad_gate_act, ties))
@@ -647,19 +668,22 @@
         mixed = combined((hidden,), (w_down,), 0, True, ties)
         return keep(tail=mixed[0], mixed_first=mixed)
 
-    grad_h_two = scatter_tokens(
-        list(first) + list(second),
+    parts = [v.reshape(micro, rows, D) for v in list(first) + list(second)]
+    grad_h_two = ring_scatter(
+        parts,
+        "seq",
         (lambda _: second[0], gate_work, up_work, mixed_work),
         {
             1: lambda moved: keep(sum_gate=after(done["whole_gate"], *moved)),
             2: lambda moved: keep(sum_up=after(done["whole_up"], *moved)),
+            3: lambda moved: keep(last=moved),
         },
-    )
+    ).reshape(tokens, D)
 
     def bank_sum(whole):
         return lax.psum_scatter(whole, "fsdp", scatter_dimension=1, tiled=True).astype(f32)
 
-    grad_down = bank_sum(done["sum_down"])
+    grad_down = jnp.concatenate([bank_sum(v) for v in done["sum_down"]], axis=0)
     grad_gate = bank_sum(done["sum_gate"])
     grad_up = bank_sum(done["sum_up"])
 
@@ -678,56 +702,96 @@
         )
 
     mixed_second = combined((hidden,), (w_down,), 1, True, (grad_o,))
-    do_blocks = after(to_heads(grad_o), mixed_second[0])
+    mixed = [v.reshape(micro, rows, D) for v in list(done["mixed_first"]) + list(mixed_second)]
+    inner = sizes("seq")[1]
+    for a in (0, 1):
+        k = a * inner + 1 % inner
+        mixed[k] = after(mixed[k], *done["last"])
+    one, zero, do_blocks = together(
+        (mixed_second[0],), row_move(mixed, 1, "seq"), row_move(mixed, 0, "seq"), to_heads(grad_o)
+    )
     do_heads = jnp.take(do_blocks, seq_order, axis=0)
 
-    def attend_work(ties):
-        grad_qkv, grad_head = attend_back(qkv, do_heads, tables, ties)
-        return keep(grad_qkv=grad_qkv, grad_head=grad_head)
-
-    def attended_then(moved):
-        columns = to_heads(after(grad_attn, *moved)).reshape(micro * group, width)
-        keep(columns=columns, head=after(jnp.sum(done["grad_head"], axis=0), *moved), left=exchanges())
-
-    def exchange(moved):
-        if done["left"]:
-            axis, pairs = done["left"].pop(0)
-            keep(head=done["head"] + after(lax.ppermute(done["head"], axis, pairs), *moved))
-
-    def qkv_work(_):
-        grads = jnp.einsum(
-            "smtd,smte->de", h_one, done["grad_qkv"], preferred_element_type=f32
-        )
-        return keep(from_qkv=grads)
-
-    def part_work(_):
-        wide = jnp.einsum("smte,de->smtd", done["grad_qkv"], w_qkv, preferred_element_type=f32)
-        return keep(part=wide.astype(bf16), wide=wide)
-
-    mixed = list(done["mixed_first"]) + list(mixed_second)
-    mixed[ns // 4 + 1] = after(mixed[ns // 4 + 1], grad_h_two)
-    mixed = scatter_tokens(
-        mixed,
-        (lambda _: do_heads, attend_work, part_work, qkv_work),
-        {1: attended_then, 2: exchange, 3: exchange},
-    )
+    total = ahead(row_sum(one, mixed, 1, "seq"), "seq")
+    grad_qkv, grad_head = attend_back(qkv, do_heads, tables)
+    wide = jnp.einsum("smte,de->smtd", grad_qkv, w_qkv, preferred_element_type=f32)
+    part_h_one = wide.astype(bf16)
+    total, two, columns = together(
+        (part_h_one,), total, row_move(mixed, 2, "seq"), to_heads(after(grad_attn, do_blocks))
+    )
+
+    part_h_one = after(part_h_one, total)
+    part_h_one = [part_h_one[k] for k in range(ns)]
+    from_qkv = jnp.einsum(
+        "smtd,smte->de", after(h_one, total), grad_qkv, preferred_element_type=f32
+    )
+    from_out = jnp.einsum(
+        "td,te->de",
+        after(o_all, total),
+        columns.reshape(micro * group, width),
+        preferred_element_type=f32,
+    )
+    left = exchanges()
+    head = jnp.sum(after(grad_head, total), axis=0)
+
+    def exchange(head):
+        axis, pairs = left.pop(0)
+        return lax.ppermute(head, axis, pairs)
+
+    total = ahead(add(row_sum(two, mixed, 2, "seq"), total).astype(bf16), "seq")
+    head = head + exchange(head)
+    total, three, one, moved = together(
+        (from_qkv, from_out),
+        total,
+        row_move(mixed, 3, "seq"),
+        row_move(part_h_one, 1, "seq"),
+        exchange(head),
+    )
+    head = head + moved
+
+    from_out = jnp.take(from_out.reshape(ns, width, width), inverse_seq, axis=0).reshape(D, width)
+    grad_gain_one = jnp.sum(wide * (x_wide * inv_all), axis=(0, 1, 2))
+    from_gains = jnp.pad(jnp.stack([grad_gain_one, grad_gain_two], axis=1), ((0, 0), (0, HD - 2)))
+    whole = jnp.concatenate([from_qkv, from_out, from_gains], axis=1).astype(bf16)
+    whole = after(whole, total)
+    whole = jnp.take(whole.reshape(nf, D // nf, -1), relative_order("fsdp"), axis=0)
+    owned = ring_scatter([whole[k] for k in range(nf)], "fsdp").astype(bf16)
+
+    total = ahead(add(row_sum(three, mixed, 3, "seq"), total).astype(bf16), "seq")
+    grad_total = ahead(row_sum(one, part_h_one, 1, "seq"), "seq")
+    total, grad_total, two, moved = together(
+        (), total, grad_total, row_move(part_h_one, 2, "seq"), exchange(head)
+    )
+    head = head + moved
+    mixed = add(row_sum(zero, mixed, 0, "seq"), total).reshape(tokens, D)
     layer_output = (middle + mixed).astype(bf16).reshape(micro, rows, D)
-    def out_work(ties):
-        grads = jnp.einsum(
-            "td,te->de", after(o_all, *ties), done["columns"], preferred_element_type=f32
-        )
-        return keep(from_out=grads)
-
-    part_h_one = done["part"]
-    grad_h_one = scatter_tokens(
-        [part_h_one[k] for k in range(ns)],
-        (lambda _: done["from_qkv"], out_work, lambda _: grad_down, lambda _: grad_gate),
-        {step: exchange for step in range(4)},
-    )
-    while done["left"]:
-        exchange(())
-    grad_head_gains = done["head"]
-    grad_gain_one = jnp.sum(done["wide"] * (x_wide * inv_all), axis=(0, 1, 2))
+
+    grad_total = add(row_sum(two, part_h_one, 2, "seq"), grad_total).astype(bf16)
+    grad_total, three, moved, owned = together(
+        (grad_down,),
+        ahead(grad_total, "seq"),
+        row_move(part_h_one, 3, "seq"),
+        exchange(head),
+        owned,
+    )
+    head = head + moved
+    owned = lax.all_to_all(
+        owned.reshape(ns, share, -1), "seq", split_axis=0, concat_axis=0, tiled=True
+    )
+
+    grad_total = add(row_sum(three, part_h_one, 3, "seq"), grad_total).astype(bf16)
+    grad_total, zero, moved, owned = together(
+        (grad_gate,),
+        ahead(grad_total, "seq"),
+        row_move(part_h_one, 0, "seq"),
+        exchange(head),
+        owned,
+    )
+    head = head + moved
+    while left:
+        head = head + exchange(head)
+    grad_head_gains = head
+    grad_h_one = add(row_sum(zero, part_h_one, 0, "seq"), grad_total).reshape(tokens, D)
     inv_one = rms_scale(x_rows)
     normed_one = x_rows * inv_one
     grad_unit = grad_h_one * gain_one
@@ -735,17 +799,7 @@
         grad_unit - normed_one * jnp.mean(grad_unit * normed_one, axis=-1, keepdims=True)
     )
     input_grad = input_grad.reshape(micro, rows, D)
-
-    from_qkv, from_out = done["from_qkv"], done["from_out"]
-    from_out = jnp.take(from_out.reshape(ns, width, width), inverse_seq, axis=0).reshape(D, width)
-    from_gains = jnp.pad(jnp.stack([grad_gain_one, grad_gain_two], axis=1), ((0, 0), (0, HD - 2)))
-    whole = jnp.concatenate([from_qkv, from_out, from_gains], axis=1).astype(bf16)
-    order = relative_order("fsdp")
-    whole = jnp.take(whole.reshape(nf, D // nf, -1), order, axis=0)
-    owned = ring_scatter([whole[k] for k in range(nf)], "fsdp").astype(bf16)
-    owned = lax.all_to_all(
-        owned.reshape(ns, share, -1), "seq", split_axis=0, concat_axis=0, tiled=True
-    ).astype(f32)
+    owned = owned.astype(f32)
     of_qkv = owned[..., : 3 * width].reshape(ns, share, heads_local, 3, HD)
     grad_query, grad_key, grad_value = (
         jnp.moveaxis(of_qkv[..., k, :], 0, 1).reshape(share, D) for k in range(3)

time: 1120 us -> 1080 us (0.964)
  waiting for transfers between devices: 398 us -> 340 us
  blocking collectives: 0 us -> 26.4 us
  local copies, waits for them, and re-layouts: 131 us -> 112 us
    convert_element_type x1 -> x10, other arithmetic: 0.18 us -> 27.2 us  [the longest x4 9.93 us: row_sum(): return total.astype(bf16)]
    all_to_all x0 -> x1, blocking collectives: none -> 26.4 us  [body(): lax.all_to_all(o_heads, 'seq', split_axis=0, concat_axis=0, tiled=True)]
    all_to_all x1, waiting for transfers between devices: 24.1 us -> 0.01 us  [body(): lax.all_to_all(owned.reshape(ns, share, -1), 'seq', split_axis=0, concat_...]
    all_to_all x1 -> x0, waiting for transfers between devices: 22.7 us -> none  [body(): lax.all_to_all(o_heads, 'seq', split_axis=0, concat_axis=0, tiled=True)]
    convert_element_type x10 -> x2, other arithmetic: 26.4 us -> 5.97 us  [ring_scatter(): total = total.astype(bf16)]
    unnamed x240 -> x229, local copies, waits for them, and re-layouts: 74.7 us -> 62.3 us
    pallas_call x10 -> x12, Pallas kernels: 290 us -> 296 us  [call(): pl.pallas_call(run, grid=grid, in_specs=[spec for _, spec in ins] + [pl.B...]
  transfers between devices with their start and end apart: 69 -> 69, of which waited for: 25 -> 28; matrix products, arithmetic and copies ran while one was open for 20% -> 20% of each run, Pallas kernels for 31% -> 32%
where the time goes in v3:
time: 1080 us; the launch traced here: 1070 us
  Pallas kernels  346 us (32%)
  waiting for transfers between devices  340 us (31%)
  local copies, waits for them, and re-layouts  112 us (10%)
  other arithmetic  95.6 us (9%)
  starting transfers between devices  86.3 us (8%)
  matrix products  50.2 us (5%)
  blocking collectives  26.4 us (2%)
  between operations  15.4 us (1%)
    ppermute x52, waiting for transfers between devices, shift(): return lax.ppermute(value, axis, pairs)  320 us
    pallas_call x12, Pallas kernels, call(): pl.pallas_call(run, grid=grid, in_specs=[spec for _, spec in ins] + [pl.B...  296 us
    unnamed x229, local copies, waits for them, and re-layouts  62.3 us
    ppermute x52, starting transfers between devices, shift(): return lax.ppermute(value, axis, pairs)  59.8 us
    pallas_call x1, Pallas kernels, attend_back(): pl.pallas_call(lambda *refs: attend_back_kernel(tile, *refs[:7], *refs[-2...  33.3 us
    all_to_all x1, blocking collectives, body(): lax.all_to_all(o_heads, 'seq', split_axis=0, concat_axis=0, tiled=True)  26.4 us
  transfers between devices with their start and end apart: 69, of which 28 were waited for; matrix products, arithmetic and copies ran while one was open for 20% of the time, Pallas kernels for 32%

profile of v3, /device:TPU:0, one launch (start us, length us, event | category | flops | bytes accessed | tf_op | source)
XLA Modules:
  0.0 1071.8 jit_solution(1902424921853093118)
XLA Ops:
  15.9 3.0 collective-permute-start
  28.1 19.1 %collective-permute-done.1 = bf16[2,128,2176]{2,1,0:T(8,128)(2,1)} collective-permute-done((bf16[2,128,2176]{2,1,0:T(8,128)(2,1)}, bf16[2,128,2176]{2,1,0:T(8,128)(2,1)}, u32[]{:S(2)}, u32[]{:S(2)}) %collective-permute-start.1) | collective-permute-done | bytes 1114144 | tf_op jit(solution)/shard_map/ppermute | solution.py:31
  50.4 24.4 %collective-permute-done.3 = bf16[2,128,2176]{2,1,0:T(8,128)(2,1)S(1)} collective-permute-done((bf16[2,128,2176]{2,1,0:T(8,128)(2,1)}, bf16[2,128,2176]{2,1,0:T(8,128)(2,1)S(1)}, u32[]{:S(2)}, u32[]{:S(2)}) %collective-permute-start.3) | collective-permute-done | bytes 1114144 | tf_op jit(solution)/shard_map/ppermute | solution.py:31
  76.7 25.2 %collective-permute-done.5 = bf16[2,128,2176]{2,1,0:T(8,128)(2,1)S(1)} collective-permute-done((bf16[2,128,2176]{2,1,0:T(8,128)(2,1)S(1)}, bf16[2,128,2176]{2,1,0:T(8,128)(2,1)S(1)}, u32[]{:S(2)}, u32[]{:S(2)}) %collective-permute-start.5) | collective-permute-done | bytes 1114144 | tf_op jit(solution)/shard_map/ppermute | solution.py:31
  103.1 21.6 %collective-permute-done.6 = bf16[2,128,2176]{2,1,0:T(8,128)(2,1)S(1)} collective-permute-done((bf16[2,128,2176]{2,1,0:T(8,128)(2,1)S(1)}, bf16[2,128,2176]{2,1,0:T(8,128)(2,1)S(1)}, u32[]{:S(2)}, u32[]{:S(2)}) %collective-permute-start.6) | collective-permute-done | bytes 1114144 | tf_op jit(solution)/shard_map/ppermute | solution.py:31
  124.9 3.5 copy-done.12
  132.0 5.5 fusion.2.refs_0_
  137.5 6.9 fusion.17.refs_0_
  144.4 16.5 %attend.1 = bf16[8,2,128,256]{3,2,1,0:T(8,128)(2,1)S(1)} custom-call(bf16[8,2,128,768]{3,2,1,0:T(8,128)(2,1)S(1)} %fusion.17.refs_0_, f32[1024,128]{1,0:T(8,128)S(1)} %get-tuple-element.99.refs_1_.refs_2_, f32[1024,128]{1,0:T(8,128)S(1)} %get-tuple-element.98.refs_2_.refs_3_, s32[2,1,1024]{2,1,0:T(1,128)S(1)} %broadcast_select_fusion.4.refs_3_.refs_4_, ...), custom_call_target="tpu_custom_call" | custom-call | flops 1 | bytes 1 | tf_op jit(solution)/shard_map/attend/pallas_call | solution.py:270
  165.7 26.4 %all_to_all.20 = bf16[8,2,128,256]{3,2,1,0:T(8,128)(2,1)S(1)} all-to-all(bf16[8,2,128,256]{3,2,1,0:T(8,128)(2,1)S(1)} %broadcast_select_fusion.2), channel_id=1, replica_groups=mesh['fsdp'=4,'seq'=8] {'seq'}, dimensions={0} | all-to-all | bytes 2097152 | tf_op jit(solution)/shard_map/all_to_all | solution.py:576
  193.9 6.5 multiply_reduce_fusion.3
  203.6 21.4 %collective-permute-done.7.refs_0_ = bf16[2,128,2048]{2,1,0:T(8,128)(2,1)S(1)} collective-permute-done((bf16[2,128,2048]{2,1,0:T(8,128)(2,1)S(1)}, bf16[2,128,2048]{2,1,0:T(8,128)(2,1)S(1)}, u32[]{:S(2)}, u32[]{:S(2)}) %collective-permute-start.7) | collective-permute-done | bytes 1048608 | tf_op jit(solution)/shard_map/ppermute | solution.py:31
  228.7 22.5 %collective-permute-done.10.refs_1_.refs_0_ = bf16[2,128,2048]{2,1,0:T(8,128)(2,1)S(1)} collective-permute-done((bf16[2,128,2048]{2,1,0:T(8,128)(2,1)}, bf16[2,128,2048]{2,1,0:T(8,128)(2,1)S(1)}, u32[]{:S(2)}, u32[]{:S(2)}) %collective-permute-start.10) | collective-permute-done | bytes 1048608 | tf_op jit(solution)/shard_map/ppermute | solution.py:31
  253.2 19.6 %collective-permute-done.11.refs_0_ = bf16[2,128,2048]{2,1,0:T(8,128)(2,1)S(1)} collective-permute-done((bf16[2,128,2048]{2,1,0:T(8,128)(2,1)}, bf16[2,128,2048]{2,1,0:T(8,128)(2,1)S(1)}, u32[]{:S(2)}, u32[]{:S(2)}) %collective-permute-start.11) | collective-permute-done | bytes 1048608 | tf_op jit(solution)/shard_map/ppermute | solution.py:31
  272.9 2.9 collective-permute-done.12.refs_1_.refs_0_
  278.0 21.1 %collective-permute-done.13.refs_1_ = bf16[2,128,2048]{2,1,0:T(8,128)(2,1)} collective-permute-done((bf16[2,128,2048]{2,1,0:T(8,128)(2,1)}, bf16[2,128,2048]{2,1,0:T(8,128)(2,1)}, u32[]{:S(2)}, u32[]{:S(2)}) %collective-permute-start.13) | collective-permute-done | bytes 1048608 | tf_op jit(solution)/shard_map/ppermute | solution.py:31
  304.5 16.7 %collective-permute-done.14.refs_0_ = bf16[2,128,2048]{2,1,0:T(8,128)(2,1)S(1)} collective-permute-done((bf16[2,128,2048]{2,1,0:T(8,128)(2,1)}, bf16[2,128,2048]{2,1,0:T(8,128)(2,1)S(1)}, u32[]{:S(2)}, u32[]{:S(2)}) %collective-permute-start.14) | collective-permute-done | bytes 1048608 | tf_op jit(solution)/shard_map/ppermute | solution.py:31
  328.5 35.3 %dispatch.2 = (bf16[4,2,384,2048]{3,2,1,0:T(8,128)(2,1)}, f32[4,2,384,1024]{3,2,1,0:T(8,128)}) custom-call(bf16[256,2048]{1,0:T(8,128)(2,1)} %copy-done.66, bf16[256,2048]{1,0:T(8,128)(2,1)} %bitcast.262, bf16[256,2048]{1,0:T(8,128)(2,1)} %bitcast.25.refs_2_, bf16[256,2048]{1,0:T(8,128)(2,1)} %bitcast.26.refs_3_, bf16[256,2048]{1,0:T(8,128)(2,1)} %bitcast.261, ...), custom_call_target="tpu_custom_call" | custom-call | flops 1 | bytes 1 | tf_op jit(solution)/shard_map/dispatch/pallas_call | solution.py:325
  365.4 20.9 %collective-permute-done.18.refs_0_ = bf16[2,128,2048]{2,1,0:T(8,128)(2,1)S(1)} collective-permute-done((bf16[2,128,2048]{2,1,0:T(8,128)(2,1)}, bf16[2,128,2048]{2,1,0:T(8,128)(2,1)S(1)}, u32[]{:S(2)}, u32[]{:S(2)}) %collective-permute-start.18) | collective-permute-done | bytes 1048608 | tf_op jit(solution)/shard_map/ppermute | solution.py:31
  389.3 21.4 %collective-permute-done.20.refs_1_ = bf16[2,128,2048]{2,1,0:T(8,128)(2,1)S(1)} collective-permute-done((bf16[2,128,2048]{2,1,0:T(8,128)(2,1)}, bf16[2,128,2048]{2,1,0:T(8,128)(2,1)S(1)}, u32[]{:S(2)}, u32[]{:S(2)}) %collective-permute-start.20) | collective-permute-done | bytes 1048608 | tf_op jit(solution)/shard_map/ppermute | solution.py:31
  414.2 34.2 %dispatch.3 = (bf16[4,2,384,2048]{3,2,1,0:T(8,128)(2,1)}, f32[4,2,384,1024]{3,2,1,0:T(8,128)}) custom-call(bf16[256,2048]{1,0:T(8,128)(2,1)} %bitcast.258, bf16[256,2048]{1,0:T(8,128)(2,1)} %bitcast.255, bf16[256,2048]{1,0:T(8,128)(2,1)} %bitcast.40.refs_2_, bf16[256,2048]{1,0:T(8,128)(2,1)} %bitcast.41.refs_3_, bf16[256,2048]{1,0:T(8,128)(2,1)} %bitcast.42.refs_4_, ...), custom_call_target="tpu_custom_call" | custom-call | flops 1 | bytes 1 | tf_op jit(solution)/shard_map/dispatch/pallas_call | solution.py:325
  452.0 16.9 %activate.2 = (bf16[4,2,384,1024]{3,2,1,0:T(8,128)(2,1)}, bf16[4,2,384,1024]{3,2,1,0:T(8,128)(2,1)}, bf16[4,2,384,1024]{3,2,1,0:T(8,128)(2,1)}) custom-call(bf16[4,2,384,2048]{3,2,1,0:T(8,128)(2,1)} %get-tuple-element.43.refs_1_.refs_0_, f32[4,2,384,1024]{3,2,1,0:T(8,128)} %get-tuple-element.44.refs_1_, f32[4,2,384,1024]{3,2,1,0:T(8,128)} %get-tuple-element.45.refs_2_, ...), custom_call_target="tpu_custom_call" | custom-call | flops 1 | bytes 1 | tf_op jit(solution)/shard_map/activate/pallas_call | solution.py:325
  468.9 12.9 %bank_grad.4.refs_1_.refs_0_ = bf16[2,2048,1024]{2,1,0:T(8,128)(2,1)} custom-call(bf16[4,2,384,2048]{3,2,1,0:T(8,128)(2,1)} %get-tuple-element.46.refs_1_.refs_0_, bf16[4,2,384,1024]{3,2,1,0:T(8,128)(2,1)} %get-tuple-element.47.refs_1_.refs_4_), custom_call_target="tpu_custom_call" | custom-call | flops 1 | bytes 1 | tf_op jit(solution)/shard_map/bank_grad/pallas_call | solution.py:325
  484.8 6.0 collective-permute-start.26
  490.8 19.0 %activate.3 = (bf16[4,2,384,1024]{3,2,1,0:T(8,128)(2,1)}, bf16[4,2,384,1024]{3,2,1,0:T(8,128)(2,1)}, bf16[4,2,384,1024]{3,2,1,0:T(8,128)(2,1)}) custom-call(bf16[4,2,384,2048]{3,2,1,0:T(8,128)(2,1)} %get-tuple-element.43.refs_1_.refs_0_, f32[4,2,384,1024]{3,2,1,0:T(8,128)} %get-tuple-element.44.refs_1_, ...), custom_call_target="tpu_custom_call", output_to_operand_aliasing={{0}: (4, {}), {1}: (5, {}), {2}: (6, {})} | custom-call | flops 1 | bytes 1 | tf_op jit(solution)/shard_map/activate/pallas_call | solution.py:325
  509.8 12.9 %bank_grad.5.refs_1_.refs_0_ = bf16[2,2048,1024]{2,1,0:T(8,128)(2,1)} custom-call(bf16[4,2,384,2048]{3,2,1,0:T(8,128)(2,1)} %get-tuple-element.46.refs_1_.refs_0_, bf16[4,2,384,1024]{3,2,1,0:T(8,128)(2,1)} %get-tuple-element.50.refs_1_.refs_0_), custom_call_target="tpu_custom_call" | custom-call | flops 1 | bytes 1 | tf_op jit(solution)/shard_map/bank_grad/pallas_call | solution.py:325
  526.7 32.1 %combine.4 = (bf16[256,2048]{1,0:T(8,128)(2,1)}, bf16[256,2048]{1,0:T(8,128)(2,1)}, bf16[256,2048]{1,0:T(8,128)(2,1)}, bf16[256,2048]{1,0:T(8,128)(2,1)}) custom-call(bf16[4,2,384,1024]{3,2,1,0:T(8,128)(2,1)} %get-tuple-element.51.refs_0_.refs_1_, bf16[4,2,384,1024]{3,2,1,0:T(8,128)(2,1)} %get-tuple-element.52.refs_1_, ...), custom_call_target="tpu_custom_call" | custom-call | flops 1 | bytes 1 | tf_op jit(solution)/shard_map/combine/pallas_call | solution.py:325
  560.8 32.3 %combine.5 = (bf16[256,2048]{1,0:T(8,128)(2,1)}, bf16[256,2048]{1,0:T(8,128)(2,1)}, bf16[256,2048]{1,0:T(8,128)(2,1)}, bf16[256,2048]{1,0:T(8,128)(2,1)}) custom-call(bf16[4,2,384,1024]{3,2,1,0:T(8,128)(2,1)} %get-tuple-element.51.refs_0_.refs_1_, bf16[4,2,384,1024]{3,2,1,0:T(8,128)(2,1)} %get-tuple-element.52.refs_1_, ...), custom_call_target="tpu_custom_call" | custom-call | flops 1 | bytes 1 | tf_op jit(solution)/shard_map/combine/pallas_call | solution.py:325
  596.4 24.3 %bank_grad.6.refs_1_.refs_0_ = bf16[4,2048,1024]{2,1,0:T(8,128)(2,1)} custom-call(bf16[4,2,384,2048]{3,2,1,0:T(8,128)(2,1)} %get-tuple-element.43.refs_1_.refs_0_, bf16[4,2,384,1024]{3,2,1,0:T(8,128)(2,1)} %get-tuple-element.51.refs_0_.refs_1_, bf16[2,128,2048]{2,1,0:T(8,128)(2,1)} %after.85.refs_2_), custom_call_target="tpu_custom_call" | custom-call | flops 1 | bytes 1 | tf_op jit(solution)/shard_map/bank_grad/pallas_call | solution.py:325
  627.2 24.4 %bank_grad.7.refs_1_.refs_0_ = bf16[4,2048,1024]{2,1,0:T(8,128)(2,1)} custom-call(bf16[4,2,384,2048]{3,2,1,0:T(8,128)(2,1)} %get-tuple-element.43.refs_1_.refs_0_, bf16[4,2,384,1024]{3,2,1,0:T(8,128)(2,1)} %get-tuple-element.52.refs_1_, bf16[2,128,2048]{2,1,0:T(8,128)(2,1)} %after.86.refs_2_.refs_1_, bf16[2,128,2048]{2,1,0:T(8,128)(2,1)} %after.87.refs_3_.refs_2_), custom_call_target="tpu_custom_call" | custom-call | flops 1 | bytes 1 | tf_op jit(solution)/shard_map/bank_grad/pallas_call | solution.py:325
  654.1 3.5 add_convert_fusion.5
  658.3 26.6 %combine.6 = (bf16[256,2048]{1,0:T(8,128)(2,1)}, bf16[256,2048]{1,0:T(8,128)(2,1)}, bf16[256,2048]{1,0:T(8,128)(2,1)}, bf16[256,2048]{1,0:T(8,128)(2,1)}) custom-call(bf16[4,2,384,1024]{3,2,1,0:T(8,128)(2,1)} %get-tuple-element.50.refs_1_.refs_0_, bf16[4,2048,1024]{2,1,0:T(8,128)(2,1)} %all-gather.12.cloned.1.call-done.refs_10_.refs_1_, ...), custom_call_target="tpu_custom_call" | custom-call | flops 1 | bytes 1 | tf_op jit(solution)/shard_map/combine/pallas_call | solution.py:325
  692.0 6.1 convolution_convert_fusion.refs_5_
  700.6 5.4 all-to-all-start.1
  724.5 25.0 %combine.7 = (bf16[256,2048]{1,0:T(8,128)(2,1)}, bf16[256,2048]{1,0:T(8,128)(2,1)}, bf16[256,2048]{1,0:T(8,128)(2,1)}, bf16[256,2048]{1,0:T(8,128)(2,1)}) custom-call(bf16[4,2,384,1024]{3,2,1,0:T(8,128)(2,1)} %get-tuple-element.50.refs_1_.refs_0_, bf16[4,2048,1024]{2,1,0:T(8,128)(2,1)} %all-gather.12.cloned.1.call-done.refs_10_.refs_1_, ...), custom_call_target="tpu_custom_call" | custom-call | flops 1 | bytes 1 | tf_op jit(solution)/shard_map/combine/pallas_call | solution.py:325
  749.6 8.5 collective-permute-done.36.refs_0_
  765.6 5.6 all-to-all-start.2
  775.2 33.3 %attend_back.1 = (bf16[8,2,128,768]{3,2,1,0:T(8,128)(2,1)S(1)}, f32[4,2,128]{2,1,0:T(2,128)S(1)}) custom-call(bf16[8,2,128,768]{3,2,1,0:T(8,128)(2,1)S(1)} %copy-done.3, bf16[8,2,128,256]{3,2,1,0:T(8,128)(2,1)S(1)} %broadcast_select_fusion.1.refs_1_, f32[1024,128]{1,0:T(8,128)S(1)} %get-tuple-element.99.refs_1_.refs_2_, ...), custom_call_target="tpu_custom_call" | custom-call | flops 1 | bytes 1 | tf_op jit(solution)/shard_map/attend_back/pallas_call | solution.py:287
  811.4 11.6 %fusion.3 = (bf16[2048]{0:T(1024)(128)(2,1)S(1)}, bf16[8,2,128,2048]{3,2,1,0:T(8,128)(2,1)}) fusion(f32[8,2,128]{2,1,0:T(2,128)S(1)} %copy-done.78, bf16[8,2,128,2176]{3,2,1,0:T(8,128)(2,1)} %copy-done.12, bf16[8,2,128,768]{3,2,1,0:T(8,128)(2,1)S(1)} %get-tuple-element.67, bf16[2048,896]{1,0:T(8,128)(2,1)S(1)} %copy-done.71), kind=kOutput, calls=%fused_computation.10 | convolution fusion | flops 6463420416 | bytes 23080960 | tf_op jit(solution)/shard_map/smte,de->smtd/dot_general | solution.py:717
  822.9 2.9 collective-permute-done.38.refs_0_
  829.5 7.5 fusion.86.refs_2_
  841.5 4.4 slice_bitcast_fusion.13
  847.7 11.4 %fusion.85 = (bf16[2048,768]{1,0:T(8,128)(2,1)S(1)}, f32[2048,768]{1,0:T(8,128)}) fusion(bf16[8,2,128,768]{3,2,1,0:T(8,128)(2,1)S(1)} %copy-done.7, bf16[8,2,128,2048]{3,2,1,0:T(8,128)(2,1)} %after.99), kind=kOutput, calls=%fused_computation.257 | convolution fusion | flops 6444023808 | bytes 20971520 | tf_op jit(solution)/shard_map/smtd,smte->de/dot_general | solution.py:725
  859.6 6.6 collective-permute-start.43
  872.3 5.6 gather_fusion.2
  877.9 2.9 broadcast_select_fusion
  890.2 2.9 fusion.21
  894.6 2.9 fusion.16
  897.5 7.0 collective-permute-start.54
  905.2 4.2 collective-permute-done.46.refs_2_.refs_0_
  913.0 4.6 collective-permute-done.44.refs_0_
  917.6 21.7 %collective-permute-done.45.refs_1_.refs_0_ = bf16[2,128,2048]{2,1,0:T(8,128)(2,1)S(1)} collective-permute-done((bf16[2,128,2048]{2,1,0:T(8,128)(2,1)}, bf16[2,128,2048]{2,1,0:T(8,128)(2,1)S(1)}, u32[]{:S(2)}, u32[]{:S(2)}) %collective-permute-start.45) | collective-permute-done | bytes 1048608 | tf_op jit(solution)/shard_map/ppermute | solution.py:31
  941.6 3.0 add_convert_fusion.2
  945.7 3.4 add_convert_fusion.refs_4_.refs_0_
  949.1 6.2 maximum_convert_fusion.refs_1_
  955.2 9.8 collective-permute-done.49.refs_2_.refs_0_
  967.1 3.9 collective-permute-done.50.refs_0_
  972.0 3.7 all-to-all-start.3
  977.6 3.0 add_convert_fusion.1
  984.5 6.6 convert_element_type.445.refs_1_
  991.2 20.9 %collective-permute-done.48.refs_2_.refs_0_ = bf16[2,128,2048]{2,1,0:T(8,128)(2,1)} collective-permute-done((bf16[2,128,2048]{2,1,0:T(8,128)(2,1)}, bf16[2,128,2048]{2,1,0:T(8,128)(2,1)}, u32[]{:S(2)}, u32[]{:S(2)}) %collective-permute-start.48) | collective-permute-done | bytes 1048608 | tf_op jit(solution)/shard_map/ppermute | solution.py:31
  1012.0 13.8 %collective-permute-done.56.refs_3_.refs_0_ = f32[2,128]{1,0:T(2,128)S(1)} collective-permute-done((f32[2,128]{1,0:T(2,128)S(1)}, f32[2,128]{1,0:T(2,128)S(1)}, u32[]{:S(2)}, u32[]{:S(2)}) %collective-permute-start.56) | collective-permute-done | bytes 1056 | tf_op jit(solution)/shard_map/ppermute | solution.py:739
  1030.9 3.0 convert_add_fusion.16
  1058.2 6.8 convert_element_type.478
  (528 shorter events, 206.9 us)
Async XLA Ops:
  7.2 123.0 %all-gather.6.cloned.1.call-start = ((), (), s32[]{:S(2)}) async-start(), calls=%async_computation.8 | async-start | bytes 4587520 | tf_op jit(solution)/shard_map/all_gather | solution.py:527
  11.1 182.9 %all-gather.8.cloned.1.call-start = ((), (), s32[]{:S(2)}) async-start(), calls=%async_computation.9 | async-start | bytes 10485760 | tf_op jit(solution)/shard_map/all_gather | solution.py:527
  11.8 316.7 %all-gather.10.cloned.1.call-start = ((), (), s32[]{:S(2)}) async-start(), calls=%async_computation.10 | async-start | bytes 20971520 | tf_op jit(solution)/shard_map/all_gather | solution.py:527
  12.6 401.6 %all-gather.12.cloned.1.call-start = ((), (), s32[]{:S(2)}) async-start(), calls=%async_computation.11 | async-start | bytes 20971520 | tf_op jit(solution)/shard_map/all_gather | solution.py:527
  13.2 438.9 %all-gather.14.cloned.1.call-start = ((), (), s32[]{:S(2)}) async-start(), calls=%async_computation.12 | async-start | bytes 20971520 | tf_op jit(solution)/shard_map/all_gather | solution.py:527
  15.9 31.7 %collective-permute-start = (bf16[2,128,2176]{2,1,0:T(8,128)(2,1)}, bf16[2,128,2176]{2,1,0:T(8,128)(2,1)}, u32[]{:S(2)}, u32[]{:S(2)}) collective-permute-start(bf16[2,128,2176]{2,1,0:T(8,128)(2,1)} %pad.13), channel_id=1, source_target_pairs={{0,1},{1,0},{2,3},{3,2},{4,5},{5,4},{6,7},{7,6},{8,9},{9,8},{10,11... | collective-permute-start | bytes 3342344 | tf_op jit(solution)/shard_map/ppermute | solution.py:31
  18.9 28.2 %collective-permute-start.1 = (bf16[2,128,2176]{2,1,0:T(8,128)(2,1)}, bf16[2,128,2176]{2,1,0:T(8,128)(2,1)}, u32[]{:S(2)}, u32[]{:S(2)}) collective-permute-start(bf16[2,128,2176]{2,1,0:T(8,128)(2,1)} %pad.13), channel_id=1, source_target_pairs={{0,2},{1,3},{2,4},{3,5},{4,6},{5,7},{6,0},{7,1},{8,10},{9,11},{10,... | collective-permute-start | bytes 3342344 | tf_op jit(solution)/shard_map/ppermute | solution.py:31
  20.5 928.6 %reduce-scatter.7.cloned.1.call-start = ((), (), s32[]{:S(2)}) async-start(), calls=%async_computation.14 | async-start | bytes 10485760 | tf_op jit(solution)/shard_map/reduce_scatter | solution.py:684
  47.1 29.3 %collective-permute-start.2 = (bf16[2,128,2176]{2,1,0:T(8,128)(2,1)}, bf16[2,128,2176]{2,1,0:T(8,128)(2,1)S(1)}, u32[]{:S(2)}, u32[]{:S(2)}) collective-permute-start(bf16[2,128,2176]{2,1,0:T(8,128)(2,1)} %collective-permute-done.1), channel_id=1, source_target_pairs={{0,1},{1,0},{2,3},{3,2},{4,5},{5,4},{6,7},{7,6},{8,9},{9,8},{10,11... | collective-permute-start | bytes 3342344 | tf_op jit(solution)/shard_map/ppermute | solution.py:31
  47.6 27.2 %collective-permute-start.3 = (bf16[2,128,2176]{2,1,0:T(8,128)(2,1)}, bf16[2,128,2176]{2,1,0:T(8,128)(2,1)S(1)}, u32[]{:S(2)}, u32[]{:S(2)}) collective-permute-start(bf16[2,128,2176]{2,1,0:T(8,128)(2,1)} %collective-permute-done.1), channel_id=1, source_target_pairs={{0,2},{1,3},{2,4},{3,5},{4,6},{5,7},{6,0},{7,1},{8,10},{9,11},{10,... | collective-permute-start | bytes 3342344 | tf_op jit(solution)/shard_map/ppermute | solution.py:31
  74.8 28.0 %collective-permute-start.4 = (bf16[2,128,2176]{2,1,0:T(8,128)(2,1)S(1)}, bf16[2,128,2176]{2,1,0:T(8,128)(2,1)S(1)}, u32[]{:S(2)}, u32[]{:S(2)}) collective-permute-start(bf16[2,128,2176]{2,1,0:T(8,128)(2,1)S(1)} %collective-permute-done.3), channel_id=1, source_target_pairs={{0,1},{1,0},{2,3},{3,2},{4,5},{5,4},{6,7},{7,6},{8,9},{9,8},{10,11... | collective-permute-start | bytes 3342344 | tf_op jit(solution)/shard_map/ppermute | solution.py:31
  76.1 25.8 %collective-permute-start.5 = (bf16[2,128,2176]{2,1,0:T(8,128)(2,1)S(1)}, bf16[2,128,2176]{2,1,0:T(8,128)(2,1)S(1)}, u32[]{:S(2)}, u32[]{:S(2)}) collective-permute-start(bf16[2,128,2176]{2,1,0:T(8,128)(2,1)S(1)} %collective-permute-done.3), channel_id=1, source_target_pairs={{0,2},{1,3},{2,4},{3,5},{4,6},{5,7},{6,0},{7,1},{8,10},{9,11},{10,... | collective-permute-start | bytes 3342344 | tf_op jit(solution)/shard_map/ppermute | solution.py:31
  101.9 22.8 %collective-permute-start.6 = (bf16[2,128,2176]{2,1,0:T(8,128)(2,1)S(1)}, bf16[2,128,2176]{2,1,0:T(8,128)(2,1)S(1)}, u32[]{:S(2)}, u32[]{:S(2)}) collective-permute-start(bf16[2,128,2176]{2,1,0:T(8,128)(2,1)S(1)} %collective-permute-done.5), channel_id=1, source_target_pairs={{0,1},{1,0},{2,3},{3,2},{4,5},{5,4},{6,7},{7,6},{8,9},{9,8},{10,11... | collective-permute-start | bytes 3342344 | tf_op jit(solution)/shard_map/ppermute | solution.py:31
  202.0 22.9 %collective-permute-start.7 = (bf16[2,128,2048]{2,1,0:T(8,128)(2,1)S(1)}, bf16[2,128,2048]{2,1,0:T(8,128)(2,1)S(1)}, u32[]{:S(2)}, u32[]{:S(2)}) collective-permute-start(bf16[2,128,2048]{2,1,0:T(8,128)(2,1)S(1)} %bitcast.275), channel_id=1, source_target_pairs={{0,1},{1,0},{2,3},{3,2},{4,5},{5,4},{6,7},{7,6},{8,9},{9,8},{10,11... | collective-permute-start | bytes 3145736 | tf_op jit(solution)/shard_map/ppermute | solution.py:31
  203.6 24.2 %collective-permute-start.8 = (bf16[2,128,2048]{2,1,0:T(8,128)(2,1)S(1)}, bf16[2,128,2048]{2,1,0:T(8,128)(2,1)}, u32[]{:S(2)}, u32[]{:S(2)}) collective-permute-start(bf16[2,128,2048]{2,1,0:T(8,128)(2,1)S(1)} %bitcast.276), channel_id=1, source_target_pairs={{0,2},{1,3},{2,4},{3,5},{4,6},{5,7},{6,0},{7,1},{8,10},{9,11},{10,... | collective-permute-start | bytes 3145736 | tf_op jit(solution)/shard_map/ppermute | solution.py:31
  227.8 23.4 %collective-permute-start.10 = (bf16[2,128,2048]{2,1,0:T(8,128)(2,1)}, bf16[2,128,2048]{2,1,0:T(8,128)(2,1)S(1)}, u32[]{:S(2)}, u32[]{:S(2)}) collective-permute-start(bf16[2,128,2048]{2,1,0:T(8,128)(2,1)} %after.65), channel_id=1, source_target_pairs={{0,2},{1,3},{2,4},{3,5},{4,6},{5,7},{6,0},{7,1},{8,10},{9,11},{10,... | collective-permute-start | bytes 3145736 | tf_op jit(solution)/shard_map/ppermute | solution.py:31
  227.8 23.4 %collective-permute-start.9 = (bf16[2,128,2048]{2,1,0:T(8,128)(2,1)}, bf16[2,128,2048]{2,1,0:T(8,128)(2,1)}, u32[]{:S(2)}, u32[]{:S(2)}) collective-permute-start(bf16[2,128,2048]{2,1,0:T(8,128)(2,1)} %after.65), channel_id=1, source_target_pairs={{0,1},{1,0},{2,3},{3,2},{4,5},{5,4},{6,7},{7,6},{8,9},{9,8},{10,11... | collective-permute-start | bytes 3145736 | tf_op jit(solution)/shard_map/ppermute | solution.py:31
  252.2 20.7 %collective-permute-start.11 = (bf16[2,128,2048]{2,1,0:T(8,128)(2,1)}, bf16[2,128,2048]{2,1,0:T(8,128)(2,1)S(1)}, u32[]{:S(2)}, u32[]{:S(2)}) collective-permute-start(bf16[2,128,2048]{2,1,0:T(8,128)(2,1)} %after.67), channel_id=1, source_target_pairs={{0,1},{1,0},{2,3},{3,2},{4,5},{5,4},{6,7},{7,6},{8,9},{9,8},{10,11... | collective-permute-start | bytes 3145736 | tf_op jit(solution)/shard_map/ppermute | solution.py:31
  253.2 22.6 %collective-permute-start.12 = (bf16[2,128,2048]{2,1,0:T(8,128)(2,1)}, bf16[2,128,2048]{2,1,0:T(8,128)(2,1)}, u32[]{:S(2)}, u32[]{:S(2)}) collective-permute-start(bf16[2,128,2048]{2,1,0:T(8,128)(2,1)} %after.67), channel_id=1, source_target_pairs={{0,2},{1,3},{2,4},{3,5},{4,6},{5,7},{6,0},{7,1},{8,10},{9,11},{10,... | collective-permute-start | bytes 3145736 | tf_op jit(solution)/shard_map/ppermute | solution.py:31
  275.8 23.3 %collective-permute-start.13 = (bf16[2,128,2048]{2,1,0:T(8,128)(2,1)}, bf16[2,128,2048]{2,1,0:T(8,128)(2,1)}, u32[]{:S(2)}, u32[]{:S(2)}) collective-permute-start(bf16[2,128,2048]{2,1,0:T(8,128)(2,1)} %after.69), channel_id=1, source_target_pairs={{0,1},{1,0},{2,3},{3,2},{4,5},{5,4},{6,7},{7,6},{8,9},{9,8},{10,11... | collective-permute-start | bytes 3145736 | tf_op jit(solution)/shard_map/ppermute | solution.py:31
  299.1 22.2 %collective-permute-start.14 = (bf16[2,128,2048]{2,1,0:T(8,128)(2,1)}, bf16[2,128,2048]{2,1,0:T(8,128)(2,1)S(1)}, u32[]{:S(2)}, u32[]{:S(2)}) collective-permute-start(bf16[2,128,2048]{2,1,0:T(8,128)(2,1)} %after.70), channel_id=1, source_target_pairs={{0,1},{1,0},{2,3},{3,2},{4,5},{5,4},{6,7},{7,6},{8,9},{9,8},{10,11... | collective-permute-start | bytes 3145736 | tf_op jit(solution)/shard_map/ppermute | solution.py:31
  299.9 21.4 %collective-permute-start.15 = (bf16[2,128,2048]{2,1,0:T(8,128)(2,1)}, bf16[2,128,2048]{2,1,0:T(8,128)(2,1)}, u32[]{:S(2)}, u32[]{:S(2)}) collective-permute-start(bf16[2,128,2048]{2,1,0:T(8,128)(2,1)} %after.70), channel_id=1, source_target_pairs={{0,2},{1,3},{2,4},{3,5},{4,6},{5,7},{6,0},{7,1},{8,10},{9,11},{10,... | collective-permute-start | bytes 3145736 | tf_op jit(solution)/shard_map/ppermute | solution.py:31
  322.3 41.6 %collective-permute-start.16 = (bf16[2,128,2048]{2,1,0:T(8,128)(2,1)}, bf16[2,128,2048]{2,1,0:T(8,128)(2,1)}, u32[]{:S(2)}, u32[]{:S(2)}) collective-permute-start(bf16[2,128,2048]{2,1,0:T(8,128)(2,1)} %after.72.refs_12_), channel_id=1, source_target_pairs={{0,1},{1,0},{2,3},{3,2},{4,5},{5,4},{6,7},{7,6},{8,9},{9,8},{10,11... | collective-permute-start | bytes 3145736 | tf_op jit(solution)/shard_map/ppermute | solution.py:31
  323.1 40.8 %collective-permute-start.17 = (bf16[2,128,2048]{2,1,0:T(8,128)(2,1)}, bf16[2,128,2048]{2,1,0:T(8,128)(2,1)}, u32[]{:S(2)}, u32[]{:S(2)}) collective-permute-start(bf16[2,128,2048]{2,1,0:T(8,128)(2,1)} %after.72.refs_12_), channel_id=1, source_target_pairs={{0,2},{1,3},{2,4},{3,5},{4,6},{5,7},{6,0},{7,1},{8,10},{9,11},{10,... | collective-permute-start | bytes 3145736 | tf_op jit(solution)/shard_map/ppermute | solution.py:31
  363.9 22.4 %collective-permute-start.18 = (bf16[2,128,2048]{2,1,0:T(8,128)(2,1)}, bf16[2,128,2048]{2,1,0:T(8,128)(2,1)S(1)}, u32[]{:S(2)}, u32[]{:S(2)}) collective-permute-start(bf16[2,128,2048]{2,1,0:T(8,128)(2,1)} %after.74), channel_id=1, source_target_pairs={{0,1},{1,0},{2,3},{3,2},{4,5},{5,4},{6,7},{7,6},{8,9},{9,8},{10,11... | collective-permute-start | bytes 3145736 | tf_op jit(solution)/shard_map/ppermute | solution.py:31
  365.3 21.0 %collective-permute-start.19 = (bf16[2,128,2048]{2,1,0:T(8,128)(2,1)}, bf16[2,128,2048]{2,1,0:T(8,128)(2,1)}, u32[]{:S(2)}, u32[]{:S(2)}) collective-permute-start(bf16[2,128,2048]{2,1,0:T(8,128)(2,1)} %after.74), channel_id=1, source_target_pairs={{0,2},{1,3},{2,4},{3,5},{4,6},{5,7},{6,0},{7,1},{8,10},{9,11},{10,... | collective-permute-start | bytes 3145736 | tf_op jit(solution)/shard_map/ppermute | solution.py:31
  387.3 23.4 %collective-permute-start.20 = (bf16[2,128,2048]{2,1,0:T(8,128)(2,1)}, bf16[2,128,2048]{2,1,0:T(8,128)(2,1)S(1)}, u32[]{:S(2)}, u32[]{:S(2)}) collective-permute-start(bf16[2,128,2048]{2,1,0:T(8,128)(2,1)} %after.76), channel_id=1, source_target_pairs={{0,1},{1,0},{2,3},{3,2},{4,5},{5,4},{6,7},{7,6},{8,9},{9,8},{10,11... | collective-permute-start | bytes 3145736 | tf_op jit(solution)/shard_map/ppermute | solution.py:31
  411.6 36.8 %collective-permute-start.21 = (bf16[2048,256]{1,0:T(8,128)(2,1)}, bf16[2048,256]{1,0:T(8,128)(2,1)S(1)}, u32[]{:S(2)}, u32[]{:S(2)}) collective-permute-start(bf16[2048,256]{1,0:T(8,128)(2,1)} %after.77), channel_id=1, source_target_pairs={{0,1},{1,0},{2,3},{3,2},{4,5},{5,4},{6,7},{7,6},{8,9},{9,8},{10,11... | collective-permute-start | bytes 3145736 | tf_op jit(solution)/shard_map/ppermute | solution.py:31
  414.0 34.4 %collective-permute-start.22 = (bf16[2048,256]{1,0:T(8,128)(2,1)}, bf16[2048,256]{1,0:T(8,128)(2,1)}, u32[]{:S(2)}, u32[]{:S(2)}) collective-permute-start(bf16[2048,256]{1,0:T(8,128)(2,1)} %after.77), channel_id=1, source_target_pairs={{0,2},{1,3},{2,4},{3,5},{4,6},{5,7},{6,0},{7,1},{8,10},{9,11},{10,... | collective-permute-start | bytes 3145736 | tf_op jit(solution)/shard_map/ppermute | solution.py:31
  449.4 32.4 %collective-permute-start.23 = (bf16[2048,256]{1,0:T(8,128)(2,1)}, bf16[2048,256]{1,0:T(8,128)(2,1)S(1)}, u32[]{:S(2)}, u32[]{:S(2)}) collective-permute-start(bf16[2048,256]{1,0:T(8,128)(2,1)} %after.79.refs_5_), channel_id=1, source_target_pairs={{0,1},{1,0},{2,3},{3,2},{4,5},{5,4},{6,7},{7,6},{8,9},{9,8},{10,11... | collective-permute-start | bytes 3145736 | tf_op jit(solution)/shard_map/ppermute | solution.py:31
  449.4 32.4 %collective-permute-start.24 = (bf16[2048,256]{1,0:T(8,128)(2,1)}, bf16[2048,256]{1,0:T(8,128)(2,1)}, u32[]{:S(2)}, u32[]{:S(2)}) collective-permute-start(bf16[2048,256]{1,0:T(8,128)(2,1)} %after.79.refs_5_), channel_id=1, source_target_pairs={{0,2},{1,3},{2,4},{3,5},{4,6},{5,7},{6,0},{7,1},{8,10},{9,11},{10,... | collective-permute-start | bytes 3145736 | tf_op jit(solution)/shard_map/ppermute | solution.py:31
  482.8 466.3 %reduce-scatter.9.cloned.1.call-start = ((), (), s32[]{:S(2)}) async-start(), calls=%async_computation.15 | async-start | bytes 10485760 | tf_op jit(solution)/shard_map/reduce_scatter | solution.py:684
  482.8 39.9 %collective-permute-start.25 = (bf16[2048,256]{1,0:T(8,128)(2,1)}, bf16[2048,256]{1,0:T(8,128)(2,1)S(1)}, u32[]{:S(2)}, u32[]{:S(2)}) collective-permute-start(bf16[2048,256]{1,0:T(8,128)(2,1)} %after.81.refs_8_.refs_2_), channel_id=1, source_target_pairs={{0,1},{1,0},{2,3},{3,2},{4,5},{5,4},{6,7},{7,6},{8,9},{9,8},{10,11... | collective-permute-start | bytes 3145736 | tf_op jit(solution)/shard_map/ppermute | solution.py:31
  484.8 38.0 %collective-permute-start.26 = (bf16[2048,256]{1,0:T(8,128)(2,1)}, bf16[2048,256]{1,0:T(8,128)(2,1)}, u32[]{:S(2)}, u32[]{:S(2)}) collective-permute-start(bf16[2048,256]{1,0:T(8,128)(2,1)} %after.81.refs_8_.refs_2_), channel_id=1, source_target_pairs={{0,2},{1,3},{2,4},{3,5},{4,6},{5,7},{6,0},{7,1},{8,10},{9,11},{10,... | collective-permute-start | bytes 3145736 | tf_op jit(solution)/shard_map/ppermute | solution.py:31
  523.7 460.8 %reduce-scatter.5.cloned.1.call-start = ((), (), s32[]{:S(2)}) async-start(), calls=%async_computation.13 | async-start | bytes 20971520 | tf_op jit(solution)/shard_map/reduce_scatter | solution.py:684
  526.7 34.1 %collective-permute-start.27 = (bf16[2048,256]{1,0:T(8,128)(2,1)}, bf16[2048,256]{1,0:T(8,128)(2,1)}, u32[]{:S(2)}, u32[]{:S(2)}) collective-permute-start(bf16[2048,256]{1,0:T(8,128)(2,1)} %after.83.refs_8_.refs_2_), channel_id=1, source_target_pairs={{0,1},{1,0},{2,3},{3,2},{4,5},{5,4},{6,7},{7,6},{8,9},{9,8},{10,11... | collective-permute-start | bytes 3145736 | tf_op jit(solution)/shard_map/ppermute | solution.py:31
  558.8 34.3 %collective-permute-start.30 = (bf16[2,128,2048]{2,1,0:T(8,128)(2,1)}, bf16[2,128,2048]{2,1,0:T(8,128)(2,1)S(1)}, u32[]{:S(2)}, u32[]{:S(2)}) collective-permute-start(bf16[2,128,2048]{2,1,0:T(8,128)(2,1)} %bitcast.308), channel_id=1, source_target_pairs={{0,1},{1,0},{2,3},{3,2},{4,5},{5,4},{6,7},{7,6},{8,9},{9,8},{10,11... | collective-permute-start | bytes 3145736 | tf_op jit(solution)/shard_map/ppermute | solution.py:31
  596.1 24.9 %collective-permute-start.31 = (bf16[2,128,2048]{2,1,0:T(8,128)(2,1)S(1)}, bf16[2,128,2048]{2,1,0:T(8,128)(2,1)S(1)}, u32[]{:S(2)}, u32[]{:S(2)}) collective-permute-start(bf16[2,128,2048]{2,1,0:T(8,128)(2,1)S(1)} %fusion.29), channel_id=1, source_target_pairs={{0,2},{1,3},{2,4},{3,5},{4,6},{5,7},{6,0},{7,1},{8,10},{9,11},{10,... | collective-permute-start | bytes 3145736 | tf_op jit(solution)/shard_map/ppermute | solution.py:31
  596.3 25.3 %collective-permute-start.29 = (bf16[2,128,2048]{2,1,0:T(8,128)(2,1)S(1)}, bf16[2,128,2048]{2,1,0:T(8,128)(2,1)}, u32[]{:S(2)}, u32[]{:S(2)}) collective-permute-start(bf16[2,128,2048]{2,1,0:T(8,128)(2,1)S(1)} %bitcast.307), channel_id=1, source_target_pairs={{0,1},{1,0},{2,3},{3,2},{4,5},{5,4},{6,7},{7,6},{8,9},{9,8},{10,11... | collective-permute-start | bytes 3145736 | tf_op jit(solution)/shard_map/ppermute | solution.py:31
  622.0 436.2 %reduce-scatter.11.cloned.1.call-start = ((), (), s32[]{:S(2)}) async-start(), calls=%async_computation.16 | async-start | bytes 20971520 | tf_op jit(solution)/shard_map/reduce_scatter | solution.py:684
  622.1 29.5 %collective-permute-start.28 = (bf16[2,128,2048]{2,1,0:T(8,128)(2,1)}, bf16[2,128,2048]{2,1,0:T(8,128)(2,1)S(1)}, u32[]{:S(2)}, u32[]{:S(2)}) collective-permute-start(bf16[2,128,2048]{2,1,0:T(8,128)(2,1)} %bitcast.306), channel_id=1, source_target_pairs={{0,1},{1,0},{2,3},{3,2},{4,5},{5,4},{6,7},{7,6},{8,9},{9,8},{10,11... | collective-permute-start | bytes 3145736 | tf_op jit(solution)/shard_map/ppermute | solution.py:31
  626.1 25.6 %collective-permute-start.32 = (bf16[2,128,2048]{2,1,0:T(8,128)(2,1)S(1)}, bf16[2,128,2048]{2,1,0:T(8,128)(2,1)}, u32[]{:S(2)}, u32[]{:S(2)}) collective-permute-start(bf16[2,128,2048]{2,1,0:T(8,128)(2,1)S(1)} %add_convert_fusion.6), channel_id=1, source_target_pairs={{0,2},{1,3},{2,4},{3,5},{4,6},{5,7},{6,0},{7,1},{8,10},{9,11},{10,... | collective-permute-start | bytes 3145736 | tf_op jit(solution)/shard_map/ppermute | solution.py:31
  652.6 32.2 %collective-permute-start.33 = (bf16[2,128,2048]{2,1,0:T(8,128)(2,1)}, bf16[2,128,2048]{2,1,0:T(8,128)(2,1)}, u32[]{:S(2)}, u32[]{:S(2)}) collective-permute-start(bf16[2,128,2048]{2,1,0:T(8,128)(2,1)} %bitcast.304), channel_id=1, source_target_pairs={{0,1},{1,0},{2,3},{3,2},{4,5},{5,4},{6,7},{7,6},{8,9},{9,8},{10,11... | collective-permute-start | bytes 3145736 | tf_op jit(solution)/shard_map/ppermute | solution.py:31
  657.6 27.3 %collective-permute-start.34 = (bf16[2,128,2048]{2,1,0:T(8,128)(2,1)}, bf16[2,128,2048]{2,1,0:T(8,128)(2,1)S(1)}, u32[]{:S(2)}, u32[]{:S(2)}) collective-permute-start(bf16[2,128,2048]{2,1,0:T(8,128)(2,1)} %add_convert_fusion.5), channel_id=1, source_target_pairs={{0,2},{1,3},{2,4},{3,5},{4,6},{5,7},{6,0},{7,1},{8,10},{9,11},{10,... | collective-permute-start | bytes 3145736 | tf_op jit(solution)/shard_map/ppermute | solution.py:31
  700.6 57.5 %all-to-all-start.1 = ((bf16[8,2,128,256]{3,2,1,0:T(8,128)(2,1)}), bf16[8,2,128,256]{3,2,1,0:T(8,128)(2,1)S(1)}, u32[]{:S(2)}, u32[]{:S(2)}) async-start(bf16[8,2,128,256]{3,2,1,0:T(8,128)(2,1)} %bitcast.268), calls=%async_computation.1 | async-start | bytes 2097152 | tf_op jit(solution)/shard_map/all_to_all | solution.py:700
  711.9 37.7 %collective-permute-start.35 = (bf16[2,128,2048]{2,1,0:T(8,128)(2,1)}, bf16[2,128,2048]{2,1,0:T(8,128)(2,1)}, u32[]{:S(2)}, u32[]{:S(2)}) collective-permute-start(bf16[2,128,2048]{2,1,0:T(8,128)(2,1)} %after.92), channel_id=1, source_target_pairs={{0,1},{1,0},{2,3},{3,2},{4,5},{5,4},{6,7},{7,6},{8,9},{9,8},{10,11... | collective-permute-start | bytes 3145736 | tf_op jit(solution)/shard_map/ppermute | solution.py:31
  713.9 44.2 %collective-permute-start.36 = (bf16[2,128,2048]{2,1,0:T(8,128)(2,1)}, bf16[2,128,2048]{2,1,0:T(8,128)(2,1)}, u32[]{:S(2)}, u32[]{:S(2)}) collective-permute-start(bf16[2,128,2048]{2,1,0:T(8,128)(2,1)} %after.93), channel_id=1, source_target_pairs={{0,1},{1,0},{2,3},{3,2},{4,5},{5,4},{6,7},{7,6},{8,9},{9,8},{10,11... | collective-permute-start | bytes 3145736 | tf_op jit(solution)/shard_map/ppermute | solution.py:31
  759.1 63.8 %collective-permute-start.39 = (bf16[2,128,2048]{2,1,0:T(8,128)(2,1)}, bf16[2,128,2048]{2,1,0:T(8,128)(2,1)}, u32[]{:S(2)}, u32[]{:S(2)}) collective-permute-start(bf16[2,128,2048]{2,1,0:T(8,128)(2,1)} %bitcast.66), channel_id=1, source_target_pairs={{0,1},{1,0},{2,3},{3,2},{4,5},{5,4},{6,7},{7,6},{8,9},{9,8},{10,11... | collective-permute-start | bytes 3145736 | tf_op jit(solution)/shard_map/ppermute | solution.py:31
  759.3 109.3 %collective-permute-start.37 = (bf16[2,128,2048]{2,1,0:T(8,128)(2,1)}, bf16[2,128,2048]{2,1,0:T(8,128)(2,1)}, u32[]{:S(2)}, u32[]{:S(2)}) collective-permute-start(bf16[2,128,2048]{2,1,0:T(8,128)(2,1)} %bitcast.305), channel_id=1, source_target_pairs={{0,1},{1,0},{2,3},{3,2},{4,5},{5,4},{6,7},{7,6},{8,9},{9,8},{10,11... | collective-permute-start | bytes 3145736 | tf_op jit(solution)/shard_map/ppermute | solution.py:31
  765.6 60.3 %all-to-all-start.2 = ((bf16[8,2,128,256]{3,2,1,0:T(8,128)(2,1)}), bf16[8,2,128,256]{3,2,1,0:T(8,128)(2,1)S(1)}, u32[]{:S(2)}, u32[]{:S(2)}) async-start(bf16[8,2,128,256]{3,2,1,0:T(8,128)(2,1)} %bitcast.270), calls=%async_computation.2 | async-start | bytes 2097152 | tf_op jit(solution)/shard_map/all_to_all | solution.py:700
  841.3 27.4 %collective-permute-start.40 = (bf16[2,128,2048]{2,1,0:T(8,128)(2,1)S(1)}, bf16[2,128,2048]{2,1,0:T(8,128)(2,1)S(1)}, u32[]{:S(2)}, u32[]{:S(2)}) collective-permute-start(bf16[2,128,2048]{2,1,0:T(8,128)(2,1)S(1)} %add_convert_fusion.4), channel_id=1, source_target_pairs={{0,2},{1,3},{2,4},{3,5},{4,6},{5,7},{6,0},{7,1},{8,10},{9,11},{10,... | collective-permute-start | bytes 3145736 | tf_op jit(solution)/shard_map/ppermute | solution.py:31
  845.9 25.4 %collective-permute-start.41 = (bf16[2,128,2048]{2,1,0:T(8,128)(2,1)S(1)}, bf16[2,128,2048]{2,1,0:T(8,128)(2,1)S(1)}, u32[]{:S(2)}, u32[]{:S(2)}) collective-permute-start(bf16[2,128,2048]{2,1,0:T(8,128)(2,1)S(1)} %get-tuple-element.88), channel_id=1, source_target_pairs={{0,1},{1,0},{2,3},{3,2},{4,5},{5,4},{6,7},{7,6},{8,9},{9,8},{10,11... | collective-permute-start | bytes 3145736 | tf_op jit(solution)/shard_map/ppermute | solution.py:31
  883.7 25.8 %collective-permute-start.46 = (bf16[2,128,2048]{2,1,0:T(8,128)(2,1)}, bf16[2,128,2048]{2,1,0:T(8,128)(2,1)S(1)}, u32[]{:S(2)}, u32[]{:S(2)}) collective-permute-start(bf16[2,128,2048]{2,1,0:T(8,128)(2,1)} %get-tuple-element.87), channel_id=1, source_target_pairs={{0,1},{1,0},{2,3},{3,2},{4,5},{5,4},{6,7},{7,6},{8,9},{9,8},{10,11... | collective-permute-start | bytes 3145736 | tf_op jit(solution)/shard_map/ppermute | solution.py:31
  885.4 59.8 %collective-permute-start.52 = (bf16[512,1152]{1,0:T(8,128)(2,1)}, bf16[512,1152]{1,0:T(8,128)(2,1)}, u32[]{:S(2)}, u32[]{:S(2)}) collective-permute-start(bf16[512,1152]{1,0:T(8,128)(2,1)} %get-tuple-element.89), channel_id=1, source_target_pairs={{0,8},{8,0},{16,24},{24,16},{1,9},{9,1},{17,25},{25,17},{2,10},{10... | collective-permute-start | bytes 3538952 | tf_op jit(solution)/shard_map/ppermute | solution.py:31
  889.6 28.0 %collective-permute-start.44 = (bf16[2,128,2048]{2,1,0:T(8,128)(2,1)}, bf16[2,128,2048]{2,1,0:T(8,128)(2,1)S(1)}, u32[]{:S(2)}, u32[]{:S(2)}) collective-permute-start(bf16[2,128,2048]{2,1,0:T(8,128)(2,1)} %add_convert_fusion.3), channel_id=1, source_target_pairs={{0,2},{1,3},{2,4},{3,5},{4,6},{5,7},{6,0},{7,1},{8,10},{9,11},{10,... | collective-permute-start | bytes 3145736 | tf_op jit(solution)/shard_map/ppermute | solution.py:31
  893.2 46.2 %collective-permute-start.45 = (bf16[2,128,2048]{2,1,0:T(8,128)(2,1)}, bf16[2,128,2048]{2,1,0:T(8,128)(2,1)S(1)}, u32[]{:S(2)}, u32[]{:S(2)}) collective-permute-start(bf16[2,128,2048]{2,1,0:T(8,128)(2,1)} %fusion.21), channel_id=1, source_target_pairs={{0,2},{1,3},{2,4},{3,5},{4,6},{5,7},{6,0},{7,1},{8,10},{9,11},{10,... | collective-permute-start | bytes 3145736 | tf_op jit(solution)/shard_map/ppermute | solution.py:31
  897.5 47.7 %collective-permute-start.54 = (bf16[512,1152]{1,0:T(8,128)(2,1)}, bf16[512,1152]{1,0:T(8,128)(2,1)}, u32[]{:S(2)}, u32[]{:S(2)}) collective-permute-start(bf16[512,1152]{1,0:T(8,128)(2,1)} %fusion.16), channel_id=1, source_target_pairs={{0,16},{8,24},{16,0},{24,8},{1,17},{9,25},{17,1},{25,9},{2,18},{10... | collective-permute-start | bytes 3538952 | tf_op jit(solution)/shard_map/ppermute | solution.py:31
  940.4 24.6 %collective-permute-start.49 = (bf16[2,128,2048]{2,1,0:T(8,128)(2,1)}, bf16[2,128,2048]{2,1,0:T(8,128)(2,1)S(1)}, u32[]{:S(2)}, u32[]{:S(2)}) collective-permute-start(bf16[2,128,2048]{2,1,0:T(8,128)(2,1)} %get-tuple-element.86), channel_id=1, source_target_pairs={{0,1},{1,0},{2,3},{3,2},{4,5},{5,4},{6,7},{7,6},{8,9},{9,8},{10,11... | collective-permute-start | bytes 3145736 | tf_op jit(solution)/shard_map/ppermute | solution.py:31
  944.5 26.5 %collective-permute-start.50 = (bf16[2,128,2048]{2,1,0:T(8,128)(2,1)}, bf16[2,128,2048]{2,1,0:T(8,128)(2,1)S(1)}, u32[]{:S(2)}, u32[]{:S(2)}) collective-permute-start(bf16[2,128,2048]{2,1,0:T(8,128)(2,1)} %add_convert_fusion.2), channel_id=1, source_target_pairs={{0,2},{1,3},{2,4},{3,5},{4,6},{5,7},{6,0},{7,1},{8,10},{9,11},{10,... | collective-permute-start | bytes 3145736 | tf_op jit(solution)/shard_map/ppermute | solution.py:31
  945.2 21.9 %collective-permute-start.51 = (f32[2,128]{1,0:T(2,128)S(1)}, f32[2,128]{1,0:T(2,128)S(1)}, u32[]{:S(2)}, u32[]{:S(2)}) collective-permute-start(f32[2,128]{1,0:T(2,128)S(1)} %add.459), channel_id=1, source_target_pairs={{0,2},{1,3},{2,0},{3,1},{4,6},{5,7},{6,4},{7,5},{8,10},{9,11},{10,... | collective-permute-start | bytes 3080 | tf_op jit(solution)/shard_map/ppermute | solution.py:739
  972.0 53.8 %all-to-all-start.3 = ((bf16[8,64,1152]{2,1,0:T(8,128)(2,1)}), bf16[8,64,1152]{2,1,0:T(8,128)(2,1)S(1)}, u32[]{:S(2)}, u32[]{:S(2)}) async-start(bf16[8,64,1152]{2,1,0:T(8,128)(2,1)} %bitcast.248), calls=%async_computation.6 | async-start | bytes 2359296 | tf_op jit(solution)/shard_map/all_to_all | solution.py:778
  975.7 36.3 %collective-permute-start.48 = (bf16[2,128,2048]{2,1,0:T(8,128)(2,1)}, bf16[2,128,2048]{2,1,0:T(8,128)(2,1)}, u32[]{:S(2)}, u32[]{:S(2)}) collective-permute-start(bf16[2,128,2048]{2,1,0:T(8,128)(2,1)} %get-tuple-element.85), channel_id=1, source_target_pairs={{0,1},{1,0},{2,3},{3,2},{4,5},{5,4},{6,7},{7,6},{8,9},{9,8},{10,11... | collective-permute-start | bytes 3145736 | tf_op jit(solution)/shard_map/ppermute | solution.py:31
  980.6 45.2 %collective-permute-start.55 = (bf16[2,128,2048]{2,1,0:T(8,128)(2,1)}, bf16[2,128,2048]{2,1,0:T(8,128)(2,1)S(1)}, u32[]{:S(2)}, u32[]{:S(2)}) collective-permute-start(bf16[2,128,2048]{2,1,0:T(8,128)(2,1)} %add_convert_fusion.1), channel_id=1, source_target_pairs={{0,2},{1,3},{2,4},{3,5},{4,6},{5,7},{6,0},{7,1},{8,10},{9,11},{10,... | collective-permute-start | bytes 3145736 | tf_op jit(solution)/shard_map/ppermute | solution.py:31
  982.1 43.7 %collective-permute-start.56 = (f32[2,128]{1,0:T(2,128)S(1)}, f32[2,128]{1,0:T(2,128)S(1)}, u32[]{:S(2)}, u32[]{:S(2)}) collective-permute-start(f32[2,128]{1,0:T(2,128)S(1)} %add.477), channel_id=1, source_target_pairs={{0,4},{1,5},{2,6},{3,7},{4,0},{5,1},{6,2},{7,3},{8,12},{9,13},{10,... | collective-permute-start | bytes 3080 | tf_op jit(solution)/shard_map/ppermute | solution.py:739
  (108 other events, 895.5 us)
Sparse Core Ops, SparseCore 0:
  11.2 34.1 all-gather.5
  47.0 58.2 all-gather.7
  106.9 105.9 all-gather.9
  214.2 105.9 all-gather.11
  321.6 105.9 all-gather.13
  482.9 77.2 reduce-scatter.6
  563.5 71.7 reduce-scatter.8
  637.8 126.1 reduce-scatter.4
  766.8 126.1 reduce-scatter.10

commit v4 on v3

--- a/solution.py
+++ b/solution.py
@@ -126,6 +126,12 @@
     a, b = me // inner, me % inner
     k = jnp.arange(outer * inner)
     return ((a - k // inner) % outer) * inner + (b - k % inner) % inner
+
+
+def reorder(value, order, axis=0):
+    value = jnp.moveaxis(value, axis, 0)
+    value = value.at[order].get(mode="promise_in_bounds", unique_indices=True)
+    return jnp.moveaxis(value, 0, axis)
 
 
 def rms_scale(values):
@@ -299,6 +305,42 @@
     )(qkv, grad_out, *tables, *ties)
 
 
+def part_kernel(grad_ref, w_ref, x_ref, inv_ref, *out_refs):
+    out_refs, gain_ref = out_refs[:-1], out_refs[-1]
+    rows = out_refs[0].shape[0]
+    gain = jnp.zeros(gain_ref.shape, f32)
+    for b, ref in enumerate(out_refs):
+        span = slice(b * rows, (b + 1) * rows)
+        wide = dot(grad_ref[span, :], w_ref[...], 1, 1)
+        ref[...] = wide.astype(bf16)
+        normed = x_ref[span, :].astype(f32) * inv_ref[span, :]
+        gain = gain + jnp.sum(wide * normed, axis=0, keepdims=True)
+    gain_ref[...] = gain
+
+
+def part_grads(grad_qkv, w_qkv, x_all, inv_all, ties=()):
+    blocks = grad_qkv.shape[0]
+    width = grad_qkv.shape[-1]
+    count = grad_qkv.size // width
+    block = jax.ShapeDtypeStruct((count // blocks, D), bf16)
+    found = call(
+        part_kernel,
+        "part_grads",
+        (D // part,),
+        [
+            (grad_qkv.reshape(count, width), whole_of((count, width))),
+            (w_qkv, pl.BlockSpec((part, width), lambda d: (d, 0))),
+            (x_all.reshape(count, x_all.shape[-1]), pl.BlockSpec((count, part), lambda d: (0, d))),
+            (inv_all.reshape(count, 1), whole_of((count, 1))),
+        ],
+        [(block, pl.BlockSpec((block.shape[0], part), lambda d: (0, d)))] * blocks
+        + [(jax.ShapeDtypeStruct((1, D), f32), pl.BlockSpec((1, part), lambda d: (0, d)))],
+        2 * count * width * D,
+        ties=ties,
+    )
+    return found[:-1], found[-1][0]
+
+
 part = 512
 
 
@@ -365,23 +407,31 @@
         act_ref[0, h] = dot(rows_ref[0, h], w_ref[0], 1, 0)
 
 
-def dispatch(values, slots, weights, bank, capacity, scaled, ties=()):
-    count = bank.shape[0]
+def dispatch(
+    values, slots, weights, bank, capacity, scaled, ties=(), first=0, count=None, before=()
+):
+    experts = bank.shape[0]
+    count = count or experts
     values = [v.reshape(-1, v.shape[-1]) for v in values]
-    rows_shape = (count, 2, capacity, D)
-    act_shape = (count, 2, capacity, FFE)
+    rows_shape = (experts, 2, capacity, D)
+    act_shape = (experts, 2, capacity, FFE)
+
+    def of(shape):
+        return pl.BlockSpec((1,) + shape[1:], lambda e: (first + e,) + (0,) * (len(shape) - 1))
+
     return call(
         lambda *refs: dispatch_kernel(scaled, len(values), *refs),
         "dispatch",
         (count,),
         [(v, whole_of(v.shape)) for v in values]
-        + [(v, spans(v.shape)) for v in (slots, weights, bank)],
+        + [(v, of(v.shape)) for v in (slots, weights, bank)],
         [
-            (jax.ShapeDtypeStruct(rows_shape, bf16), spans(rows_shape)),
-            (jax.ShapeDtypeStruct(act_shape, f32), spans(act_shape)),
+            (jax.ShapeDtypeStruct(rows_shape, bf16), of(rows_shape)),
+            (jax.ShapeDtypeStruct(act_shape, f32), of(act_shape)),
         ],
         4 * count * capacity * D * (FFE + len(values) * values[0].shape[0] // 2),
-        ties=ties,
+        ties=tuple(before) + tuple(ties),
+        aliases={len(values) + 3 + k: k for k in range(len(before))},
     )
 
 
@@ -396,23 +446,26 @@
     grad_up_ref[0, 0] = (grad_hidden * gate_silu).astype(bf16)
 
 
-def activate(taken, gate_act, grad_hidden, w_up, first, count, before, ties=()):
-    capacity = taken.shape[2]
+def activate(taken, gate_act, grad_hidden, w_up, ties=()):
+    count, _, capacity, _ = taken.shape
 
     def of(width):
-        return pl.BlockSpec((1, 1, capacity, width), lambda e, h: (first + e, h, 0, 0))
+        return pl.BlockSpec((1, 1, capacity, width), lambda e, h: (e, h, 0, 0))
 
     result = jax.ShapeDtypeStruct(gate_act.shape, bf16)
-    bank = pl.BlockSpec((1,) + w_up.shape[1:], lambda e, h: (first + e, 0, 0))
     return call(
         act_kernel,
         "activate",
         (count, 2),
-        [(taken, of(D)), (gate_act, of(FFE)), (grad_hidden, of(FFE)), (w_up, bank)],
+        [
+            (taken, of(D)),
+            (gate_act, of(FFE)),
+            (grad_hidden, of(FFE)),
+            (w_up, spans(w_up.shape)),
+        ],
         [(result, of(FFE))] * 3,
         4 * count * capacity * D * FFE,
-        ties=tuple(before) + tuple(ties),
-        aliases={4 + k: k for k in range(len(before))},
+        ties=ties,
     )
 
 
@@ -422,17 +475,16 @@
     out_ref[0] = dot(left, right, 0, 0).astype(bf16)
 
 
-def bank_grad(left, right, ties=(), first=0, count=None):
-    capacity = left.shape[2]
-    count = count or left.shape[0]
+def bank_grad(left, right, ties=()):
+    count, _, capacity, _ = left.shape
     result = jax.ShapeDtypeStruct((count, D, FFE), bf16)
     return call(
         bank_kernel,
         "bank_grad",
         (count, D // part),
         [
-            (left, pl.BlockSpec((1, 2, capacity, part), lambda e, d: (first + e, 0, 0, d))),
-            (right, pl.BlockSpec((1, 2, capacity, FFE), lambda e, d: (first + e, 0, 0, 0))),
+            (left, pl.BlockSpec((1, 2, capacity, part), lambda e, d: (e, 0, 0, d))),
+            (right, pl.BlockSpec((1, 2, capacity, FFE), lambda e, d: (e, 0, 0, 0))),
         ],
         [(result, pl.BlockSpec((1, part, FFE), lambda e, d: (e, d, 0)))],
         4 * count * capacity * D * FFE,
@@ -550,7 +602,7 @@
         [layer_input, routes.astype(bf16), weight_high, weight_low], axis=-1
     )
     packed = jnp.pad(packed, ((0, 0), (0, 0), (0, HD - 3 * TOP)))
-    packed = gather_tokens(packed)
+    packed = x_all = gather_tokens(packed)
     x_wide = packed[..., :D].astype(f32)
     inv_all = rms_scale(x_wide)
     h_one = (x_wide * inv_all * gain_one).astype(bf16)
@@ -561,7 +613,7 @@
     frequency = jnp.exp(-jnp.log(rope_base) * (2.0 * lane.astype(f32) / HD))
     angles = places.astype(f32)[:, None] * frequency[None, :]
     sign = jnp.where(jnp.arange(HD) < HD // 2, -1.0, 1.0)
-    segment = jnp.take(segments.reshape(micro, ns, rows), seq_order, axis=1).reshape(micro, group)
+    segment = reorder(segments.reshape(micro, ns, rows), seq_order, axis=1).reshape(micro, group)
     tables = (
         jnp.cos(angles),
         jnp.sin(angles) * sign,
@@ -572,7 +624,7 @@
     o_heads = attend(qkv, tables)
 
     inverse_seq = jnp.argsort(seq_order)
-    o_heads = jnp.take(o_heads, inverse_seq, axis=0)
+    o_heads = reorder(o_heads, inverse_seq, axis=0)
     o_back = lax.all_to_all(o_heads, "seq", split_axis=0, concat_axis=0, tiled=True)
     o_rows = jnp.moveaxis(o_back, 0, 2).reshape(tokens, D)
 
@@ -612,33 +664,30 @@
     def combined(acts, banks, h, scaled, ties=()):
         return combine(acts, banks, slot_columns, slots, weights, h, ns // 2, scaled, ties)
 
-    def take_work(ties):
-        taken, gate_act = dispatch(h_blocks, slots, weights, w_gate, capacity, False, ties)
-        return keep(taken=taken, gate_act=gate_act)
-
-    g_blocks = ring_gather(after(cotangent, h_blocks[-1]), "seq", (None, take_work))
+    pair = local_experts // 2
+
+    def take_work(first):
+        def work(ties):
+            before = done.get("takes", ())
+            done["takes"] = dispatch(
+                h_blocks, slots, weights, w_gate, capacity, False, ties, first, pair, before
+            )
+            return done["takes"][0]
+
+        return work
+
+    g_blocks = ring_gather(
+        after(cotangent, h_blocks[-1]), "seq", (None, take_work(0), take_work(pair))
+    )
+    taken, gate_act = done["takes"]
 
     def grad_work(_):
         grad_rows, grad_hidden = dispatch(g_blocks, slots, weights, w_down, capacity, True)
         return keep(grad_rows=grad_rows, grad_hidden=grad_hidden)
 
-    pair = local_experts // 2
-
-    def act_work(first):
-        def work(ties):
-            before = done.get("acts", ())
-            acts = activate(
-                done["taken"], done["gate_act"], done["grad_hidden"], w_up, first, pair, before, ties
-            )
-            whole = bank_grad(done["grad_rows"], acts[0], (), first, pair)
-            done.setdefault("whole_down", []).append(whole)
-            done["acts"] = acts
-            return whole
-
-        return work
-
-    def down_then(moved):
-        done.setdefault("sum_down", []).append(after(done["whole_down"][-1], *moved))
+    def act_work(ties):
+        acts = activate(taken, gate_act, done["grad_hidden"], w_up, ties)
+        return keep(tail=acts[0], acts=acts)
 
     def first_work(ties):
         first = combined(done["acts"][1:], (w_gate, w_up), 0, False, ties)
@@ -647,35 +696,33 @@
     o_all = ring_gather(
         after(o_heads.reshape(group * micro, width), g_blocks[-1]),
         "seq",
-        (grad_work, act_work(0), act_work(pair), first_work),
-        {1: down_then, 2: down_then},
+        (grad_work, act_work, first_work),
     )
     o_last = o_all[-1]
     o_all = jnp.concatenate(o_all, axis=1)
-    taken, first = done["taken"], done["first"]
+    first = done["first"]
+    grad_rows = done["grad_rows"]
     hidden, grad_gate_act, grad_up_act = done["acts"]
-    second = combined(
-        (grad_gate_act, grad_up_act), (w_gate, w_up), 1, False, (first[0], o_last)
-    )
-
-    def gate_work(ties):
-        return keep(whole_gate=bank_grad(taken, grad_gate_act, ties))
-
-    def up_work(ties):
-        return keep(whole_up=bank_grad(taken, grad_up_act, ties))
-
-    def mixed_work(ties):
-        mixed = combined((hidden,), (w_down,), 0, True, ties)
-        return keep(tail=mixed[0], mixed_first=mixed)
+    second = combined((grad_gate_act, grad_up_act), (w_gate, w_up), 1, False, (first[0],))
+
+    def down_work(ties):
+        return keep(whole_down=bank_grad(grad_rows, hidden, tuple(ties) + (o_last,)))
+
+    def mixed_work(h):
+        def work(ties):
+            mixed = combined((hidden,), (w_down,), h, True, ties)
+            done.setdefault("mixed", []).extend(mixed)
+            return mixed[0]
+
+        return work
 
     parts = [v.reshape(micro, rows, D) for v in list(first) + list(second)]
     grad_h_two = ring_scatter(
         parts,
         "seq",
-        (lambda _: second[0], gate_work, up_work, mixed_work),
+        (lambda _: second[0], down_work, mixed_work(0), mixed_work(1)),
         {
-            1: lambda moved: keep(sum_gate=after(done["whole_gate"], *moved)),
-            2: lambda moved: keep(sum_up=after(done["whole_up"], *moved)),
+            1: lambda moved: keep(sum_down=after(done["whole_down"], *moved)),
             3: lambda moved: keep(last=moved),
         },
     ).reshape(tokens, D)
@@ -683,9 +730,7 @@
     def bank_sum(whole):
         return lax.psum_scatter(whole, "fsdp", scatter_dimension=1, tiled=True).astype(f32)
 
-    grad_down = jnp.concatenate([bank_sum(v) for v in done["sum_down"]], axis=0)
-    grad_gate = bank_sum(done["sum_gate"])
-    grad_up = bank_sum(done["sum_up"])
+    grad_down = bank_sum(done["sum_down"])
 
     grad_gain_two = jnp.sum(grad_h_two * normed_two, axis=0)
     grad_unit = grad_h_two * gain_two
@@ -701,27 +746,23 @@
             jnp.moveaxis(cut, 2, 0), "seq", split_axis=0, concat_axis=0, tiled=True
         )
 
-    mixed_second = combined((hidden,), (w_down,), 1, True, (grad_o,))
-    mixed = [v.reshape(micro, rows, D) for v in list(done["mixed_first"]) + list(mixed_second)]
-    inner = sizes("seq")[1]
-    for a in (0, 1):
-        k = a * inner + 1 % inner
-        mixed[k] = after(mixed[k], *done["last"])
-    one, zero, do_blocks = together(
-        (mixed_second[0],), row_move(mixed, 1, "seq"), row_move(mixed, 0, "seq"), to_heads(grad_o)
-    )
-    do_heads = jnp.take(do_blocks, seq_order, axis=0)
-
-    total = ahead(row_sum(one, mixed, 1, "seq"), "seq")
+    whole_gate = bank_grad(taken, grad_gate_act, (grad_o,))
+    (do_blocks,) = together((whole_gate,), to_heads(grad_o))
+    grad_gate = bank_sum(after(whole_gate, do_blocks))
+    do_heads = reorder(do_blocks, seq_order)
+
+    mixed = [v.reshape(micro, rows, D) for v in done["mixed"]]
+    k = sizes("seq")[1] + 1 % sizes("seq")[1]
+    mixed[k] = after(mixed[k], do_blocks)
     grad_qkv, grad_head = attend_back(qkv, do_heads, tables)
-    wide = jnp.einsum("smte,de->smtd", grad_qkv, w_qkv, preferred_element_type=f32)
-    part_h_one = wide.astype(bf16)
-    total, two, columns = together(
-        (part_h_one,), total, row_move(mixed, 2, "seq"), to_heads(after(grad_attn, do_blocks))
-    )
-
-    part_h_one = after(part_h_one, total)
-    part_h_one = [part_h_one[k] for k in range(ns)]
+    part_h_one, grad_gain_one = part_grads(grad_qkv, w_qkv, x_all, inv_all)
+    one, columns = together(
+        (grad_gain_one,), row_move(mixed, 1, "seq"), to_heads(after(grad_attn, do_blocks))
+    )
+
+    total = one
+    part_h_one = [v.reshape(micro, rows, D) for v in part_h_one]
+    part_h_one[k] = after(part_h_one[k], total)
     from_qkv = jnp.einsum(
         "smtd,smte->de", after(h_one, total), grad_qkv, preferred_element_type=f32
     )
@@ -738,56 +779,63 @@
         axis, pairs = left.pop(0)
         return lax.ppermute(head, axis, pairs)
 
-    total = ahead(add(row_sum(two, mixed, 2, "seq"), total).astype(bf16), "seq")
+    total = ahead(row_sum(total, mixed, 1, "seq"), "seq")
     head = head + exchange(head)
-    total, three, one, moved = together(
+    total, two, one, moved = together(
         (from_qkv, from_out),
         total,
-        row_move(mixed, 3, "seq"),
+        row_move(mixed, 2, "seq"),
         row_move(part_h_one, 1, "seq"),
         exchange(head),
     )
     head = head + moved
 
-    from_out = jnp.take(from_out.reshape(ns, width, width), inverse_seq, axis=0).reshape(D, width)
-    grad_gain_one = jnp.sum(wide * (x_wide * inv_all), axis=(0, 1, 2))
+    from_out = reorder(from_out.reshape(ns, width, width), inverse_seq, axis=0).reshape(D, width)
     from_gains = jnp.pad(jnp.stack([grad_gain_one, grad_gain_two], axis=1), ((0, 0), (0, HD - 2)))
     whole = jnp.concatenate([from_qkv, from_out, from_gains], axis=1).astype(bf16)
     whole = after(whole, total)
-    whole = jnp.take(whole.reshape(nf, D // nf, -1), relative_order("fsdp"), axis=0)
+    whole = reorder(whole.reshape(nf, D // nf, -1), relative_order("fsdp"), axis=0)
     owned = ring_scatter([whole[k] for k in range(nf)], "fsdp").astype(bf16)
 
+    whole_up = bank_grad(taken, grad_up_act, (one,))
+    total = ahead(add(row_sum(two, mixed, 2, "seq"), total).astype(bf16), "seq")
+    grad_total = ahead(row_sum(one, part_h_one, 1, "seq"), "seq")
+    total, grad_total, three, two, owned = together(
+        (whole_up,),
+        total,
+        grad_total,
+        row_move(mixed, 3, "seq"),
+        row_move(part_h_one, 2, "seq"),
+        owned,
+    )
+    grad_up = bank_sum(after(whole_up, owned))
+    owned = lax.all_to_all(
+        owned.reshape(ns, share, -1), "seq", split_axis=0, concat_axis=0, tiled=True
+    )
+
     total = ahead(add(row_sum(three, mixed, 3, "seq"), total).astype(bf16), "seq")
-    grad_total = ahead(row_sum(one, part_h_one, 1, "seq"), "seq")
-    total, grad_total, two, moved = together(
-        (), total, grad_total, row_move(part_h_one, 2, "seq"), exchange(head)
-    )
-    head = head + moved
-    mixed = add(row_sum(zero, mixed, 0, "seq"), total).reshape(tokens, D)
-    layer_output = (middle + mixed).astype(bf16).reshape(micro, rows, D)
-
     grad_total = add(row_sum(two, part_h_one, 2, "seq"), grad_total).astype(bf16)
-    grad_total, three, moved, owned = together(
+    total, grad_total, three, moved, owned = together(
         (grad_down,),
+        total,
         ahead(grad_total, "seq"),
         row_move(part_h_one, 3, "seq"),
         exchange(head),
         owned,
     )
     head = head + moved
-    owned = lax.all_to_all(
-        owned.reshape(ns, share, -1), "seq", split_axis=0, concat_axis=0, tiled=True
-    )
 
     grad_total = add(row_sum(three, part_h_one, 3, "seq"), grad_total).astype(bf16)
-    grad_total, zero, moved, owned = together(
+    grad_total, zero, moved, last = together(
         (grad_gate,),
         ahead(grad_total, "seq"),
         row_move(part_h_one, 0, "seq"),
         exchange(head),
-        owned,
+        row_move(mixed, 0, "seq"),
     )
     head = head + moved
+    mixed = add(row_sum(last, mixed, 0, "seq"), total).reshape(tokens, D)
+    layer_output = (middle + mixed).astype(bf16).reshape(micro, rows, D)
     while left:
         head = head + exchange(head)
     grad_head_gains = head

time: 1080 us -> 1080 us (level)
  local copies, waits for them, and re-layouts: 112 us -> 138 us
  matrix products: 50.2 us -> 36.8 us
  Pallas kernels: 346 us -> 358 us
    ppermute x5, waiting for transfers between devices: 17.7 us -> 1.97 us  [exchange(): return lax.ppermute(head, axis, pairs)]
    pallas_call x12, Pallas kernels: 296 us -> 308 us  [call(): pl.pallas_call(run, grid=grid, in_specs=[spec for _, spec in ins] + [pl.B...]
    dot_general x1 -> x0, matrix products: 11.6 us -> none  [body(): jnp.einsum('smte,de->smtd', grad_qkv, w_qkv, preferred_element_type=f32)]
    unnamed x229 -> x267, local copies, waits for them, and re-layouts: 62.3 us -> 73.8 us
  transfers between devices with their start and end apart: 69 -> 68, of which waited for: 28 -> 22; matrix products, arithmetic and copies ran while one was open for 20% -> 19% of each run, Pallas kernels for 32% -> 33%
where the time goes in v4:
time: 1080 us; the launch traced here: 1070 us
  Pallas kernels  358 us (33%)
  waiting for transfers between devices  332 us (31%)
  local copies, waits for them, and re-layouts  138 us (13%)
  other arithmetic  88.8 us (8%)
  starting transfers between devices  77.7 us (7%)
  matrix products  36.8 us (3%)
  blocking collectives  26.1 us (2%)
  between operations  16.1 us (1%)
    ppermute x52, waiting for transfers between devices, shift(): return lax.ppermute(value, axis, pairs)  322 us
    pallas_call x12, Pallas kernels, call(): pl.pallas_call(run, grid=grid, in_specs=[spec for _, spec in ins] + [pl.B...  308 us
    unnamed x267, local copies, waits for them, and re-layouts  73.8 us
    ppermute x52, starting transfers between devices, shift(): return lax.ppermute(value, axis, pairs)  55 us
    pallas_call x1, Pallas kernels, attend_back(): pl.pallas_call(lambda *refs: attend_back_kernel(tile, *refs[:7], *refs[-2...  33.1 us
    all_to_all x1, blocking collectives, body(): lax.all_to_all(o_heads, 'seq', split_axis=0, concat_axis=0, tiled=True)  26.1 us
  transfers between devices with their start and end apart: 68, of which 22 were waited for; matrix products, arithmetic and copies ran while one was open for 19% of the time, Pallas kernels for 33%

profile of v4, /device:TPU:0, one launch (start us, length us, event | category | flops | bytes accessed | tf_op | source)
XLA Modules:
  0.0 1073.2 jit_solution(9267510178256571900)
XLA Ops:
  16.7 3.0 collective-permute-start
  28.0 19.9 %collective-permute-done.1 = bf16[2,128,2176]{2,1,0:T(8,128)(2,1)} collective-permute-done((bf16[2,128,2176]{2,1,0:T(8,128)(2,1)}, bf16[2,128,2176]{2,1,0:T(8,128)(2,1)}, u32[]{:S(2)}, u32[]{:S(2)}) %collective-permute-start.1) | collective-permute-done | bytes 1114144 | tf_op jit(solution)/shard_map/ppermute | solution.py:31
  53.0 22.5 %collective-permute-done.3 = bf16[2,128,2176]{2,1,0:T(8,128)(2,1)S(1)} collective-permute-done((bf16[2,128,2176]{2,1,0:T(8,128)(2,1)}, bf16[2,128,2176]{2,1,0:T(8,128)(2,1)S(1)}, u32[]{:S(2)}, u32[]{:S(2)}) %collective-permute-start.3) | collective-permute-done | bytes 1114144 | tf_op jit(solution)/shard_map/ppermute | solution.py:31
  79.2 23.3 %collective-permute-done.5 = bf16[2,128,2176]{2,1,0:T(8,128)(2,1)S(1)} collective-permute-done((bf16[2,128,2176]{2,1,0:T(8,128)(2,1)S(1)}, bf16[2,128,2176]{2,1,0:T(8,128)(2,1)S(1)}, u32[]{:S(2)}, u32[]{:S(2)}) %collective-permute-start.5) | collective-permute-done | bytes 1114144 | tf_op jit(solution)/shard_map/ppermute | solution.py:31
  105.7 19.7 %collective-permute-done.6 = bf16[2,128,2176]{2,1,0:T(8,128)(2,1)S(1)} collective-permute-done((bf16[2,128,2176]{2,1,0:T(8,128)(2,1)S(1)}, bf16[2,128,2176]{2,1,0:T(8,128)(2,1)S(1)}, u32[]{:S(2)}, u32[]{:S(2)}) %collective-permute-start.6) | collective-permute-done | bytes 1114144 | tf_op jit(solution)/shard_map/ppermute | solution.py:31
  126.4 5.1 fusion
  133.4 5.3 fusion.2.refs_0_
  138.7 6.9 fusion.15.refs_0_
  145.7 16.5 %attend.1 = bf16[8,2,128,256]{3,2,1,0:T(8,128)(2,1)S(1)} custom-call(bf16[8,2,128,768]{3,2,1,0:T(8,128)(2,1)S(1)} %fusion.15.refs_0_, f32[1024,128]{1,0:T(8,128)S(1)} %get-tuple-element.108.refs_1_.refs_2_, f32[1024,128]{1,0:T(8,128)S(1)} %get-tuple-element.107.refs_2_.refs_3_, s32[2,1,1024]{2,1,0:T(1,128)S(1)} %bitcast.231, ...), custom_call_target="tpu_custom_call" | custom-call | flops 1 | bytes 1 | tf_op jit(solution)/shard_map/attend/pallas_call | solution.py:276
  164.4 26.1 %all_to_all.20 = bf16[8,2,128,256]{3,2,1,0:T(8,128)(2,1)S(1)} all-to-all(bf16[8,2,128,256]{3,2,1,0:T(8,128)(2,1)S(1)} %gather_fusion.1), channel_id=1, replica_groups=mesh['fsdp'=4,'seq'=8] {'seq'}, dimensions={0} | all-to-all | bytes 2097152 | tf_op jit(solution)/shard_map/all_to_all | solution.py:628
  191.7 5.8 multiply_reduce_fusion.3
  200.7 21.6 %collective-permute-done.7.refs_0_ = bf16[2,128,2048]{2,1,0:T(8,128)(2,1)S(1)} collective-permute-done((bf16[2,128,2048]{2,1,0:T(8,128)(2,1)S(1)}, bf16[2,128,2048]{2,1,0:T(8,128)(2,1)S(1)}, u32[]{:S(2)}, u32[]{:S(2)}) %collective-permute-start.7) | collective-permute-done | bytes 1048608 | tf_op jit(solution)/shard_map/ppermute | solution.py:31
  222.3 3.2 collective-permute-done.8.refs_1_.refs_0_
  226.9 23.6 %collective-permute-done.10.refs_1_.refs_0_ = bf16[2,128,2048]{2,1,0:T(8,128)(2,1)S(1)} collective-permute-done((bf16[2,128,2048]{2,1,0:T(8,128)(2,1)}, bf16[2,128,2048]{2,1,0:T(8,128)(2,1)S(1)}, u32[]{:S(2)}, u32[]{:S(2)}) %collective-permute-start.10) | collective-permute-done | bytes 1048608 | tf_op jit(solution)/shard_map/ppermute | solution.py:31
  252.7 21.2 %collective-permute-done.11.refs_0_ = bf16[2,128,2048]{2,1,0:T(8,128)(2,1)S(1)} collective-permute-done((bf16[2,128,2048]{2,1,0:T(8,128)(2,1)}, bf16[2,128,2048]{2,1,0:T(8,128)(2,1)S(1)}, u32[]{:S(2)}, u32[]{:S(2)}) %collective-permute-start.11) | collective-permute-done | bytes 1048608 | tf_op jit(solution)/shard_map/ppermute | solution.py:31
  279.4 19.5 %collective-permute-done.13.refs_1_ = bf16[2,128,2048]{2,1,0:T(8,128)(2,1)S(1)} collective-permute-done((bf16[2,128,2048]{2,1,0:T(8,128)(2,1)}, bf16[2,128,2048]{2,1,0:T(8,128)(2,1)S(1)}, u32[]{:S(2)}, u32[]{:S(2)}) %collective-permute-start.13) | collective-permute-done | bytes 1048608 | tf_op jit(solution)/shard_map/ppermute | solution.py:31
  305.4 15.7 %collective-permute-done.14.refs_0_ = bf16[2,128,2048]{2,1,0:T(8,128)(2,1)S(1)} collective-permute-done((bf16[2,128,2048]{2,1,0:T(8,128)(2,1)}, bf16[2,128,2048]{2,1,0:T(8,128)(2,1)S(1)}, u32[]{:S(2)}, u32[]{:S(2)}) %collective-permute-start.14) | collective-permute-done | bytes 1048608 | tf_op jit(solution)/shard_map/ppermute | solution.py:31
  330.5 22.0 %dispatch.3 = (bf16[4,2,384,2048]{3,2,1,0:T(8,128)(2,1)}, f32[4,2,384,1024]{3,2,1,0:T(8,128)}) custom-call(bf16[256,2048]{1,0:T(8,128)(2,1)} %copy-done.87, bf16[256,2048]{1,0:T(8,128)(2,1)} %bitcast.242, bf16[256,2048]{1,0:T(8,128)(2,1)} %bitcast.246, bf16[256,2048]{1,0:T(8,128)(2,1)} %bitcast.250, bf16[256,2048]{1,0:T(8,128)(2,1)} %bitcast.240, ...), custom_call_target="tpu_custom_call" | custom-call | flops 1 | bytes 1 | tf_op jit(solution)/shard_map/dispatch/pallas_call | solution.py:367
  354.3 19.7 %dispatch.4 = (bf16[4,2,384,2048]{3,2,1,0:T(8,128)(2,1)}, f32[4,2,384,1024]{3,2,1,0:T(8,128)}) custom-call(bf16[256,2048]{1,0:T(8,128)(2,1)} %copy-done.87, bf16[256,2048]{1,0:T(8,128)(2,1)} %bitcast.243, bf16[256,2048]{1,0:T(8,128)(2,1)} %bitcast.247, bf16[256,2048]{1,0:T(8,128)(2,1)} %bitcast.251, ...), custom_call_target="tpu_custom_call", output_to_operand_aliasing={{0}: (11, {}), {1}: (12, {})} | custom-call | flops 1 | bytes 1 | tf_op jit(solution)/shard_map/dispatch/pallas_call | solution.py:367
  377.3 20.2 %collective-permute-done.20.refs_1_ = bf16[2,128,2048]{2,1,0:T(8,128)(2,1)S(1)} collective-permute-done((bf16[2,128,2048]{2,1,0:T(8,128)(2,1)}, bf16[2,128,2048]{2,1,0:T(8,128)(2,1)S(1)}, u32[]{:S(2)}, u32[]{:S(2)}) %collective-permute-start.20) | collective-permute-done | bytes 1048608 | tf_op jit(solution)/shard_map/ppermute | solution.py:31
  401.5 34.2 %dispatch.5 = (bf16[4,2,384,2048]{3,2,1,0:T(8,128)(2,1)}, f32[4,2,384,1024]{3,2,1,0:T(8,128)}) custom-call(bf16[256,2048]{1,0:T(8,128)(2,1)} %bitcast.254, bf16[256,2048]{1,0:T(8,128)(2,1)} %bitcast.238, bf16[256,2048]{1,0:T(8,128)(2,1)} %bitcast.239, bf16[256,2048]{1,0:T(8,128)(2,1)} %bitcast.252, bf16[256,2048]{1,0:T(8,128)(2,1)} %bitcast.253, ...), custom_call_target="tpu_custom_call" | custom-call | flops 1 | bytes 1 | tf_op jit(solution)/shard_map/dispatch/pallas_call | solution.py:367
  437.1 5.8 collective-permute-start.24
  442.8 31.7 %activate.1 = (bf16[4,2,384,1024]{3,2,1,0:T(8,128)(2,1)}, bf16[4,2,384,1024]{3,2,1,0:T(8,128)(2,1)}, bf16[4,2,384,1024]{3,2,1,0:T(8,128)(2,1)}) custom-call(bf16[4,2,384,2048]{3,2,1,0:T(8,128)(2,1)} %get-tuple-element.52.refs_1_.refs_0_, f32[4,2,384,1024]{3,2,1,0:T(8,128)} %get-tuple-element.53.refs_1_, f32[4,2,384,1024]{3,2,1,0:T(8,128)} %get-tuple-element.54.refs_2_, ...), custom_call_target="tpu_custom_call" | custom-call | flops 1 | bytes 1 | tf_op jit(solution)/shard_map/activate/pallas_call | solution.py:367
  477.9 3.0 copy.301.refs_4_.refs_2_
  480.9 31.9 %combine.4 = (bf16[256,2048]{1,0:T(8,128)(2,1)}, bf16[256,2048]{1,0:T(8,128)(2,1)}, bf16[256,2048]{1,0:T(8,128)(2,1)}, bf16[256,2048]{1,0:T(8,128)(2,1)}) custom-call(bf16[4,2,384,1024]{3,2,1,0:T(8,128)(2,1)} %get-tuple-element.57.refs_0_.refs_1_, bf16[4,2,384,1024]{3,2,1,0:T(8,128)(2,1)} %get-tuple-element.58.refs_1_, ...), custom_call_target="tpu_custom_call" | custom-call | flops 1 | bytes 1 | tf_op jit(solution)/shard_map/combine/pallas_call | solution.py:367
  512.9 32.3 %combine.5 = (bf16[256,2048]{1,0:T(8,128)(2,1)}, bf16[256,2048]{1,0:T(8,128)(2,1)}, bf16[256,2048]{1,0:T(8,128)(2,1)}, bf16[256,2048]{1,0:T(8,128)(2,1)}) custom-call(bf16[4,2,384,1024]{3,2,1,0:T(8,128)(2,1)} %get-tuple-element.57.refs_0_.refs_1_, bf16[4,2,384,1024]{3,2,1,0:T(8,128)(2,1)} %get-tuple-element.58.refs_1_, ...), custom_call_target="tpu_custom_call" | custom-call | flops 1 | bytes 1 | tf_op jit(solution)/shard_map/combine/pallas_call | solution.py:367
  552.4 28.2 %collective-permute-done.29.refs_3_ = bf16[2048,256]{1,0:T(8,128)(2,1)} collective-permute-done((bf16[2048,256]{1,0:T(8,128)(2,1)}, bf16[2048,256]{1,0:T(8,128)(2,1)}, u32[]{:S(2)}, u32[]{:S(2)}) %collective-permute-start.29) | collective-permute-done | bytes 1048608 | tf_op jit(solution)/shard_map/ppermute | solution.py:31
  580.6 24.1 %bank_grad.3.refs_1_.refs_0_ = bf16[4,2048,1024]{2,1,0:T(8,128)(2,1)} custom-call(bf16[4,2,384,2048]{3,2,1,0:T(8,128)(2,1)} %get-tuple-element.55.refs_1_.refs_0_, bf16[4,2,384,1024]{3,2,1,0:T(8,128)(2,1)} %get-tuple-element.56.refs_1_.refs_0_, bf16[2,128,2048]{2,1,0:T(8,128)(2,1)} %after.78.refs_2_, bf16[2048,256]{1,0:T(8,128)(2,1)} %collective-permute-done.29.refs_3_), custom_call_target="tpu_custom_call" | custom-call | flops 1 | bytes 1 | tf_op jit(solution)/shard_map/bank_grad/pallas_call | solution.py:367
  611.5 25.5 %combine.6 = (bf16[256,2048]{1,0:T(8,128)(2,1)}, bf16[256,2048]{1,0:T(8,128)(2,1)}, bf16[256,2048]{1,0:T(8,128)(2,1)}, bf16[256,2048]{1,0:T(8,128)(2,1)}) custom-call(bf16[4,2,384,1024]{3,2,1,0:T(8,128)(2,1)} %get-tuple-element.56.refs_1_.refs_0_, bf16[4,2048,1024]{2,1,0:T(8,128)(2,1)} %all-gather.12.cloned.1.call-done.refs_10_.refs_1_, ...), custom_call_target="tpu_custom_call" | custom-call | flops 1 | bytes 1 | tf_op jit(solution)/shard_map/combine/pallas_call | solution.py:367
  643.7 25.4 %combine.7 = (bf16[256,2048]{1,0:T(8,128)(2,1)}, bf16[256,2048]{1,0:T(8,128)(2,1)}, bf16[256,2048]{1,0:T(8,128)(2,1)}, bf16[256,2048]{1,0:T(8,128)(2,1)}) custom-call(bf16[4,2,384,1024]{3,2,1,0:T(8,128)(2,1)} %get-tuple-element.56.refs_1_.refs_0_, bf16[4,2048,1024]{2,1,0:T(8,128)(2,1)} %all-gather.12.cloned.1.call-done.refs_10_.refs_1_, ...), custom_call_target="tpu_custom_call" | custom-call | flops 1 | bytes 1 | tf_op jit(solution)/shard_map/combine/pallas_call | solution.py:367
  676.6 6.1 convolution_convert_fusion.refs_2_
  684.3 4.6 all-to-all-start.1
  688.9 24.6 %bank_grad.4.refs_1_.refs_0_ = bf16[4,2048,1024]{2,1,0:T(8,128)(2,1)} custom-call(bf16[4,2,384,2048]{3,2,1,0:T(8,128)(2,1)} %get-tuple-element.52.refs_1_.refs_0_, bf16[4,2,384,1024]{3,2,1,0:T(8,128)(2,1)} %get-tuple-element.57.refs_0_.refs_1_, bf16[256,2048]{1,0:T(8,128)(2,1)} %copy-done.92), custom_call_target="tpu_custom_call" | custom-call | flops 1 | bytes 1 | tf_op jit(solution)/shard_map/bank_grad/pallas_call | solution.py:367
  715.6 3.9 slice.92.refs_1_
  726.0 6.2 all-to-all-start.2
  742.2 3.2 gather_fusion.2
  750.6 33.1 %attend_back.1 = (bf16[8,2,128,768]{3,2,1,0:T(8,128)(2,1)S(1)}, f32[4,2,128]{2,1,0:T(2,128)S(1)}) custom-call(bf16[8,2,128,768]{3,2,1,0:T(8,128)(2,1)S(1)} %copy-done.3, bf16[8,2,128,256]{3,2,1,0:T(8,128)(2,1)S(1)} %copy-done.10, f32[1024,128]{1,0:T(8,128)S(1)} %copy-done.9, f32[1024,128]{1,0:T(8,128)S(1)} %copy-done.7, s32[2,1,1024]{2,1,0:T(1,128)S(1)} %bitcast.232, ...), custom_call_target="tpu_custom_call" | custom-call | flops 1 | bytes 1 | tf_op jit(solution)/shard_map/attend_back/pallas_call | solution.py:293
  786.0 12.6 %part_grads.1 = (bf16[256,2048]{1,0:T(8,128)(2,1)}, bf16[256,2048]{1,0:T(8,128)(2,1)}, bf16[256,2048]{1,0:T(8,128)(2,1)}, bf16[256,2048]{1,0:T(8,128)(2,1)}, bf1...) custom-call(bf16[2048,768]{1,0:T(8,128)(2,1)} %bitcast.230, ...), custom_call_target="tpu_custom_call" | custom-call | flops 1 | bytes 1 | tf_op jit(solution)/shard_map/part_grads/pallas_call | solution.py:367
  807.7 11.4 %fusion.79 = (bf16[2048,768]{1,0:T(8,128)(2,1)}, f32[2048,768]{1,0:T(8,128)}) fusion(bf16[8,2,128,768]{3,2,1,0:T(8,128)(2,1)S(1)} %copy-done.12, bf16[8,2,128,2048]{3,2,1,0:T(8,128)(2,1)} %after.94), kind=kOutput, calls=%fused_computation.216 | convolution fusion | flops 6444023808 | bytes 20971520 | tf_op jit(solution)/shard_map/smtd,smte->de/dot_general | solution.py:766
  819.1 6.3 fusion.80.refs_2_
  826.4 4.0 fusion.6.refs_0_
  831.7 5.8 gather_fusion.4
  837.6 3.4 slice_bitcast_fusion.3
  847.6 3.1 add_convert_fusion.4
  852.3 2.9 fusion.23
  856.6 28.4 %collective-permute-done.49.refs_1_.refs_0_ = bf16[512,1152]{1,0:T(8,128)(2,1)} collective-permute-done((bf16[512,1152]{1,0:T(8,128)(2,1)}, bf16[512,1152]{1,0:T(8,128)(2,1)}, u32[]{:S(2)}, u32[]{:S(2)}) %collective-permute-start.49) | collective-permute-done | bytes 1179680 | tf_op jit(solution)/shard_map/ppermute | solution.py:31
  885.0 24.1 %bank_grad.5.refs_1_.refs_0_ = bf16[4,2048,1024]{2,1,0:T(8,128)(2,1)} custom-call(bf16[4,2,384,2048]{3,2,1,0:T(8,128)(2,1)} %get-tuple-element.52.refs_1_.refs_0_, bf16[4,2,384,1024]{3,2,1,0:T(8,128)(2,1)} %get-tuple-element.58.refs_1_, bf16[2,128,2048]{2,1,0:T(8,128)(2,1)} %after.100.refs_2_.refs_5_), custom_call_target="tpu_custom_call" | custom-call | flops 1 | bytes 1 | tf_op jit(solution)/shard_map/bank_grad/pallas_call | solution.py:367
  909.1 3.4 add_convert_fusion.refs_5_.refs_0_
  915.8 4.6 all-to-all-start.3
  920.4 2.9 add_convert_fusion.3
  925.4 3.0 add_convert_fusion.2
  932.2 7.9 convert_element_type.414.refs_1_
  940.1 10.0 collective-permute-done.36.refs_3_.refs_0_
  952.1 15.3 %collective-permute-done.50.refs_0_ = bf16[2,128,2048]{2,1,0:T(8,128)(2,1)S(1)} collective-permute-done((bf16[2,128,2048]{2,1,0:T(8,128)(2,1)}, bf16[2,128,2048]{2,1,0:T(8,128)(2,1)S(1)}, u32[]{:S(2)}, u32[]{:S(2)}) %collective-permute-start.50) | collective-permute-done | bytes 1048608 | tf_op jit(solution)/shard_map/ppermute | solution.py:31
  967.5 21.0 %collective-permute-done.51.refs_2_.refs_0_ = bf16[2,128,2048]{2,1,0:T(8,128)(2,1)S(1)} collective-permute-done((bf16[2,128,2048]{2,1,0:T(8,128)(2,1)}, bf16[2,128,2048]{2,1,0:T(8,128)(2,1)S(1)}, u32[]{:S(2)}, u32[]{:S(2)}) %collective-permute-start.51) | collective-permute-done | bytes 1048608 | tf_op jit(solution)/shard_map/ppermute | solution.py:31
  988.4 5.4 all-to-all-done.3.refs_5_.refs_0_
  997.5 3.1 add_convert_fusion.1
  1008.1 3.7 reshape.718
  1014.7 5.4 fusion.78
  1030.3 6.6 convert_element_type.413.refs_1_
  1036.9 4.4 collective-permute-done.54.refs_2_.refs_0_
  1048.1 2.9 collective-permute-start.56
  1055.7 2.9 fusion.32
  1059.1 6.8 convert_element_type.476
  (545 shorter events, 201.4 us)
Async XLA Ops:
  7.2 124.4 %all-gather.6.cloned.1.call-start = ((), (), s32[]{:S(2)}) async-start(), calls=%async_computation.7 | async-start | bytes 4587520 | tf_op jit(solution)/shard_map/all_gather | solution.py:579
  11.1 180.3 %all-gather.8.cloned.1.call-start = ((), (), s32[]{:S(2)}) async-start(), calls=%async_computation.8 | async-start | bytes 10485760 | tf_op jit(solution)/shard_map/all_gather | solution.py:579
  11.8 318.7 %all-gather.10.cloned.1.call-start = ((), (), s32[]{:S(2)}) async-start(), calls=%async_computation.9 | async-start | bytes 20971520 | tf_op jit(solution)/shard_map/all_gather | solution.py:579
  12.5 388.9 %all-gather.12.cloned.1.call-start = ((), (), s32[]{:S(2)}) async-start(), calls=%async_computation.10 | async-start | bytes 20971520 | tf_op jit(solution)/shard_map/all_gather | solution.py:579
  13.2 429.7 %all-gather.14.cloned.1.call-start = ((), (), s32[]{:S(2)}) async-start(), calls=%async_computation.11 | async-start | bytes 20971520 | tf_op jit(solution)/shard_map/all_gather | solution.py:579
  13.7 918.5 %reduce-scatter.6.cloned.1.call-start = ((), (), s32[]{:S(2)}) async-start(), calls=%async_computation.13 | async-start | bytes 20971520 | tf_op jit(solution)/shard_map/reduce_scatter | solution.py:731
  16.7 31.7 %collective-permute-start = (bf16[2,128,2176]{2,1,0:T(8,128)(2,1)}, bf16[2,128,2176]{2,1,0:T(8,128)(2,1)}, u32[]{:S(2)}, u32[]{:S(2)}) collective-permute-start(bf16[2,128,2176]{2,1,0:T(8,128)(2,1)} %pad.13), channel_id=1, source_target_pairs={{0,1},{1,0},{2,3},{3,2},{4,5},{5,4},{6,7},{7,6},{8,9},{9,8},{10,11... | collective-permute-start | bytes 3342344 | tf_op jit(solution)/shard_map/ppermute | solution.py:31
  19.6 28.2 %collective-permute-start.1 = (bf16[2,128,2176]{2,1,0:T(8,128)(2,1)}, bf16[2,128,2176]{2,1,0:T(8,128)(2,1)}, u32[]{:S(2)}, u32[]{:S(2)}) collective-permute-start(bf16[2,128,2176]{2,1,0:T(8,128)(2,1)} %pad.13), channel_id=1, source_target_pairs={{0,2},{1,3},{2,4},{3,5},{4,6},{5,7},{6,0},{7,1},{8,10},{9,11},{10,... | collective-permute-start | bytes 3342344 | tf_op jit(solution)/shard_map/ppermute | solution.py:31
  47.9 29.1 %collective-permute-start.2 = (bf16[2,128,2176]{2,1,0:T(8,128)(2,1)}, bf16[2,128,2176]{2,1,0:T(8,128)(2,1)S(1)}, u32[]{:S(2)}, u32[]{:S(2)}) collective-permute-start(bf16[2,128,2176]{2,1,0:T(8,128)(2,1)} %collective-permute-done.1), channel_id=1, source_target_pairs={{0,1},{1,0},{2,3},{3,2},{4,5},{5,4},{6,7},{7,6},{8,9},{9,8},{10,11... | collective-permute-start | bytes 3342344 | tf_op jit(solution)/shard_map/ppermute | solution.py:31
  48.4 27.2 %collective-permute-start.3 = (bf16[2,128,2176]{2,1,0:T(8,128)(2,1)}, bf16[2,128,2176]{2,1,0:T(8,128)(2,1)S(1)}, u32[]{:S(2)}, u32[]{:S(2)}) collective-permute-start(bf16[2,128,2176]{2,1,0:T(8,128)(2,1)} %collective-permute-done.1), channel_id=1, source_target_pairs={{0,2},{1,3},{2,4},{3,5},{4,6},{5,7},{6,0},{7,1},{8,10},{9,11},{10,... | collective-permute-start | bytes 3342344 | tf_op jit(solution)/shard_map/ppermute | solution.py:31
  75.5 27.9 %collective-permute-start.4 = (bf16[2,128,2176]{2,1,0:T(8,128)(2,1)S(1)}, bf16[2,128,2176]{2,1,0:T(8,128)(2,1)S(1)}, u32[]{:S(2)}, u32[]{:S(2)}) collective-permute-start(bf16[2,128,2176]{2,1,0:T(8,128)(2,1)S(1)} %collective-permute-done.3), channel_id=1, source_target_pairs={{0,1},{1,0},{2,3},{3,2},{4,5},{5,4},{6,7},{7,6},{8,9},{9,8},{10,11... | collective-permute-start | bytes 3342344 | tf_op jit(solution)/shard_map/ppermute | solution.py:31
  76.8 25.7 %collective-permute-start.5 = (bf16[2,128,2176]{2,1,0:T(8,128)(2,1)S(1)}, bf16[2,128,2176]{2,1,0:T(8,128)(2,1)S(1)}, u32[]{:S(2)}, u32[]{:S(2)}) collective-permute-start(bf16[2,128,2176]{2,1,0:T(8,128)(2,1)S(1)} %collective-permute-done.3), channel_id=1, source_target_pairs={{0,2},{1,3},{2,4},{3,5},{4,6},{5,7},{6,0},{7,1},{8,10},{9,11},{10,... | collective-permute-start | bytes 3342344 | tf_op jit(solution)/shard_map/ppermute | solution.py:31
  102.5 22.8 %collective-permute-start.6 = (bf16[2,128,2176]{2,1,0:T(8,128)(2,1)S(1)}, bf16[2,128,2176]{2,1,0:T(8,128)(2,1)S(1)}, u32[]{:S(2)}, u32[]{:S(2)}) collective-permute-start(bf16[2,128,2176]{2,1,0:T(8,128)(2,1)S(1)} %collective-permute-done.5), channel_id=1, source_target_pairs={{0,1},{1,0},{2,3},{3,2},{4,5},{5,4},{6,7},{7,6},{8,9},{9,8},{10,11... | collective-permute-start | bytes 3342344 | tf_op jit(solution)/shard_map/ppermute | solution.py:31
  199.1 23.2 %collective-permute-start.7 = (bf16[2,128,2048]{2,1,0:T(8,128)(2,1)S(1)}, bf16[2,128,2048]{2,1,0:T(8,128)(2,1)S(1)}, u32[]{:S(2)}, u32[]{:S(2)}) collective-permute-start(bf16[2,128,2048]{2,1,0:T(8,128)(2,1)S(1)} %bitcast.260), channel_id=1, source_target_pairs={{0,1},{1,0},{2,3},{3,2},{4,5},{5,4},{6,7},{7,6},{8,9},{9,8},{10,11... | collective-permute-start | bytes 3145736 | tf_op jit(solution)/shard_map/ppermute | solution.py:31
  200.7 24.8 %collective-permute-start.8 = (bf16[2,128,2048]{2,1,0:T(8,128)(2,1)S(1)}, bf16[2,128,2048]{2,1,0:T(8,128)(2,1)S(1)}, u32[]{:S(2)}, u32[]{:S(2)}) collective-permute-start(bf16[2,128,2048]{2,1,0:T(8,128)(2,1)S(1)} %bitcast.261), channel_id=1, source_target_pairs={{0,2},{1,3},{2,4},{3,5},{4,6},{5,7},{6,0},{7,1},{8,10},{9,11},{10,... | collective-permute-start | bytes 3145736 | tf_op jit(solution)/shard_map/ppermute | solution.py:31
  226.4 24.1 %collective-permute-start.10 = (bf16[2,128,2048]{2,1,0:T(8,128)(2,1)}, bf16[2,128,2048]{2,1,0:T(8,128)(2,1)S(1)}, u32[]{:S(2)}, u32[]{:S(2)}) collective-permute-start(bf16[2,128,2048]{2,1,0:T(8,128)(2,1)} %after.61), channel_id=1, source_target_pairs={{0,2},{1,3},{2,4},{3,5},{4,6},{5,7},{6,0},{7,1},{8,10},{9,11},{10,... | collective-permute-start | bytes 3145736 | tf_op jit(solution)/shard_map/ppermute | solution.py:31
  226.4 24.1 %collective-permute-start.9 = (bf16[2,128,2048]{2,1,0:T(8,128)(2,1)}, bf16[2,128,2048]{2,1,0:T(8,128)(2,1)S(1)}, u32[]{:S(2)}, u32[]{:S(2)}) collective-permute-start(bf16[2,128,2048]{2,1,0:T(8,128)(2,1)} %after.61), channel_id=1, source_target_pairs={{0,1},{1,0},{2,3},{3,2},{4,5},{5,4},{6,7},{7,6},{8,9},{9,8},{10,11... | collective-permute-start | bytes 3145736 | tf_op jit(solution)/shard_map/ppermute | solution.py:31
  252.5 21.4 %collective-permute-start.11 = (bf16[2,128,2048]{2,1,0:T(8,128)(2,1)}, bf16[2,128,2048]{2,1,0:T(8,128)(2,1)S(1)}, u32[]{:S(2)}, u32[]{:S(2)}) collective-permute-start(bf16[2,128,2048]{2,1,0:T(8,128)(2,1)} %after.63), channel_id=1, source_target_pairs={{0,1},{1,0},{2,3},{3,2},{4,5},{5,4},{6,7},{7,6},{8,9},{9,8},{10,11... | collective-permute-start | bytes 3145736 | tf_op jit(solution)/shard_map/ppermute | solution.py:31
  252.7 23.0 %collective-permute-start.12 = (bf16[2,128,2048]{2,1,0:T(8,128)(2,1)}, bf16[2,128,2048]{2,1,0:T(8,128)(2,1)S(1)}, u32[]{:S(2)}, u32[]{:S(2)}) collective-permute-start(bf16[2,128,2048]{2,1,0:T(8,128)(2,1)} %after.63), channel_id=1, source_target_pairs={{0,2},{1,3},{2,4},{3,5},{4,6},{5,7},{6,0},{7,1},{8,10},{9,11},{10,... | collective-permute-start | bytes 3145736 | tf_op jit(solution)/shard_map/ppermute | solution.py:31
  276.7 22.2 %collective-permute-start.13 = (bf16[2,128,2048]{2,1,0:T(8,128)(2,1)}, bf16[2,128,2048]{2,1,0:T(8,128)(2,1)S(1)}, u32[]{:S(2)}, u32[]{:S(2)}) collective-permute-start(bf16[2,128,2048]{2,1,0:T(8,128)(2,1)} %after.65), channel_id=1, source_target_pairs={{0,1},{1,0},{2,3},{3,2},{4,5},{5,4},{6,7},{7,6},{8,9},{9,8},{10,11... | collective-permute-start | bytes 3145736 | tf_op jit(solution)/shard_map/ppermute | solution.py:31
  299.9 21.2 %collective-permute-start.14 = (bf16[2,128,2048]{2,1,0:T(8,128)(2,1)}, bf16[2,128,2048]{2,1,0:T(8,128)(2,1)S(1)}, u32[]{:S(2)}, u32[]{:S(2)}) collective-permute-start(bf16[2,128,2048]{2,1,0:T(8,128)(2,1)} %after.66), channel_id=1, source_target_pairs={{0,1},{1,0},{2,3},{3,2},{4,5},{5,4},{6,7},{7,6},{8,9},{9,8},{10,11... | collective-permute-start | bytes 3145736 | tf_op jit(solution)/shard_map/ppermute | solution.py:31
  301.6 19.4 %collective-permute-start.15 = (bf16[2,128,2048]{2,1,0:T(8,128)(2,1)}, bf16[2,128,2048]{2,1,0:T(8,128)(2,1)S(1)}, u32[]{:S(2)}, u32[]{:S(2)}) collective-permute-start(bf16[2,128,2048]{2,1,0:T(8,128)(2,1)} %after.66), channel_id=1, source_target_pairs={{0,2},{1,3},{2,4},{3,5},{4,6},{5,7},{6,0},{7,1},{8,10},{9,11},{10,... | collective-permute-start | bytes 3145736 | tf_op jit(solution)/shard_map/ppermute | solution.py:31
  323.1 29.5 %collective-permute-start.16 = (bf16[2,128,2048]{2,1,0:T(8,128)(2,1)}, bf16[2,128,2048]{2,1,0:T(8,128)(2,1)S(1)}, u32[]{:S(2)}, u32[]{:S(2)}) collective-permute-start(bf16[2,128,2048]{2,1,0:T(8,128)(2,1)} %after.68.refs_12_), channel_id=1, source_target_pairs={{0,1},{1,0},{2,3},{3,2},{4,5},{5,4},{6,7},{7,6},{8,9},{9,8},{10,11... | collective-permute-start | bytes 3145736 | tf_op jit(solution)/shard_map/ppermute | solution.py:31
  324.9 27.7 %collective-permute-start.17 = (bf16[2,128,2048]{2,1,0:T(8,128)(2,1)}, bf16[2,128,2048]{2,1,0:T(8,128)(2,1)S(1)}, u32[]{:S(2)}, u32[]{:S(2)}) collective-permute-start(bf16[2,128,2048]{2,1,0:T(8,128)(2,1)} %after.68.refs_12_), channel_id=1, source_target_pairs={{0,2},{1,3},{2,4},{3,5},{4,6},{5,7},{6,0},{7,1},{8,10},{9,11},{10,... | collective-permute-start | bytes 3145736 | tf_op jit(solution)/shard_map/ppermute | solution.py:31
  353.9 20.1 %collective-permute-start.18 = (bf16[2,128,2048]{2,1,0:T(8,128)(2,1)}, bf16[2,128,2048]{2,1,0:T(8,128)(2,1)S(1)}, u32[]{:S(2)}, u32[]{:S(2)}) collective-permute-start(bf16[2,128,2048]{2,1,0:T(8,128)(2,1)} %after.70.refs_14_), channel_id=1, source_target_pairs={{0,1},{1,0},{2,3},{3,2},{4,5},{5,4},{6,7},{7,6},{8,9},{9,8},{10,11... | collective-permute-start | bytes 3145736 | tf_op jit(solution)/shard_map/ppermute | solution.py:31
  353.9 20.1 %collective-permute-start.19 = (bf16[2,128,2048]{2,1,0:T(8,128)(2,1)}, bf16[2,128,2048]{2,1,0:T(8,128)(2,1)S(1)}, u32[]{:S(2)}, u32[]{:S(2)}) collective-permute-start(bf16[2,128,2048]{2,1,0:T(8,128)(2,1)} %after.70.refs_14_), channel_id=1, source_target_pairs={{0,2},{1,3},{2,4},{3,5},{4,6},{5,7},{6,0},{7,1},{8,10},{9,11},{10,... | collective-permute-start | bytes 3145736 | tf_op jit(solution)/shard_map/ppermute | solution.py:31
  375.3 22.3 %collective-permute-start.20 = (bf16[2,128,2048]{2,1,0:T(8,128)(2,1)}, bf16[2,128,2048]{2,1,0:T(8,128)(2,1)S(1)}, u32[]{:S(2)}, u32[]{:S(2)}) collective-permute-start(bf16[2,128,2048]{2,1,0:T(8,128)(2,1)} %after.72), channel_id=1, source_target_pairs={{0,1},{1,0},{2,3},{3,2},{4,5},{5,4},{6,7},{7,6},{8,9},{9,8},{10,11... | collective-permute-start | bytes 3145736 | tf_op jit(solution)/shard_map/ppermute | solution.py:31
  398.5 37.1 %collective-permute-start.21 = (bf16[2048,256]{1,0:T(8,128)(2,1)}, bf16[2048,256]{1,0:T(8,128)(2,1)S(1)}, u32[]{:S(2)}, u32[]{:S(2)}) collective-permute-start(bf16[2048,256]{1,0:T(8,128)(2,1)} %after.73), channel_id=1, source_target_pairs={{0,1},{1,0},{2,3},{3,2},{4,5},{5,4},{6,7},{7,6},{8,9},{9,8},{10,11... | collective-permute-start | bytes 3145736 | tf_op jit(solution)/shard_map/ppermute | solution.py:31
  400.2 35.5 %collective-permute-start.22 = (bf16[2048,256]{1,0:T(8,128)(2,1)}, bf16[2048,256]{1,0:T(8,128)(2,1)S(1)}, u32[]{:S(2)}, u32[]{:S(2)}) collective-permute-start(bf16[2048,256]{1,0:T(8,128)(2,1)} %after.73), channel_id=1, source_target_pairs={{0,2},{1,3},{2,4},{3,5},{4,6},{5,7},{6,0},{7,1},{8,10},{9,11},{10,... | collective-permute-start | bytes 3145736 | tf_op jit(solution)/shard_map/ppermute | solution.py:31
  437.0 37.5 %collective-permute-start.23 = (bf16[2048,256]{1,0:T(8,128)(2,1)}, bf16[2048,256]{1,0:T(8,128)(2,1)S(1)}, u32[]{:S(2)}, u32[]{:S(2)}) collective-permute-start(bf16[2048,256]{1,0:T(8,128)(2,1)} %after.75.refs_5_), channel_id=1, source_target_pairs={{0,1},{1,0},{2,3},{3,2},{4,5},{5,4},{6,7},{7,6},{8,9},{9,8},{10,11... | collective-permute-start | bytes 3145736 | tf_op jit(solution)/shard_map/ppermute | solution.py:31
  437.1 37.5 %collective-permute-start.24 = (bf16[2048,256]{1,0:T(8,128)(2,1)}, bf16[2048,256]{1,0:T(8,128)(2,1)S(1)}, u32[]{:S(2)}, u32[]{:S(2)}) collective-permute-start(bf16[2048,256]{1,0:T(8,128)(2,1)} %after.75.refs_5_), channel_id=1, source_target_pairs={{0,2},{1,3},{2,4},{3,5},{4,6},{5,7},{6,0},{7,1},{8,10},{9,11},{10,... | collective-permute-start | bytes 3145736 | tf_op jit(solution)/shard_map/ppermute | solution.py:31
  475.9 69.3 %collective-permute-start.27 = (bf16[2048,256]{1,0:T(8,128)(2,1)}, bf16[2048,256]{1,0:T(8,128)(2,1)S(1)}, u32[]{:S(2)}, u32[]{:S(2)}) collective-permute-start(bf16[2048,256]{1,0:T(8,128)(2,1)} %after.77.refs_8_), channel_id=1, source_target_pairs={{0,2},{1,3},{2,4},{3,5},{4,6},{5,7},{6,0},{7,1},{8,10},{9,11},{10,... | collective-permute-start | bytes 3145736 | tf_op jit(solution)/shard_map/ppermute | solution.py:31
  475.9 69.2 %collective-permute-start.28 = (bf16[2048,256]{1,0:T(8,128)(2,1)}, bf16[2048,256]{1,0:T(8,128)(2,1)S(1)}, u32[]{:S(2)}, u32[]{:S(2)}) collective-permute-start(bf16[2048,256]{1,0:T(8,128)(2,1)} %after.77.refs_8_), channel_id=1, source_target_pairs={{0,1},{1,0},{2,3},{3,2},{4,5},{5,4},{6,7},{7,6},{8,9},{9,8},{10,11... | collective-permute-start | bytes 3145736 | tf_op jit(solution)/shard_map/ppermute | solution.py:31
  512.8 36.4 %collective-permute-start.26 = (bf16[2,128,2048]{2,1,0:T(8,128)(2,1)}, bf16[2,128,2048]{2,1,0:T(8,128)(2,1)S(1)}, u32[]{:S(2)}, u32[]{:S(2)}) collective-permute-start(bf16[2,128,2048]{2,1,0:T(8,128)(2,1)} %bitcast.313), channel_id=1, source_target_pairs={{0,1},{1,0},{2,3},{3,2},{4,5},{5,4},{6,7},{7,6},{8,9},{9,8},{10,11... | collective-permute-start | bytes 3145736 | tf_op jit(solution)/shard_map/ppermute | solution.py:31
  547.2 57.5 %collective-permute-start.25 = (bf16[2,128,2048]{2,1,0:T(8,128)(2,1)}, bf16[2,128,2048]{2,1,0:T(8,128)(2,1)S(1)}, u32[]{:S(2)}, u32[]{:S(2)}) collective-permute-start(bf16[2,128,2048]{2,1,0:T(8,128)(2,1)} %bitcast.312), channel_id=1, source_target_pairs={{0,1},{1,0},{2,3},{3,2},{4,5},{5,4},{6,7},{7,6},{8,9},{9,8},{10,11... | collective-permute-start | bytes 3145736 | tf_op jit(solution)/shard_map/ppermute | solution.py:31
  549.1 31.5 %collective-permute-start.29 = (bf16[2048,256]{1,0:T(8,128)(2,1)}, bf16[2048,256]{1,0:T(8,128)(2,1)}, u32[]{:S(2)}, u32[]{:S(2)}) collective-permute-start(bf16[2048,256]{1,0:T(8,128)(2,1)} %after.80), channel_id=1, source_target_pairs={{0,1},{1,0},{2,3},{3,2},{4,5},{5,4},{6,7},{7,6},{8,9},{9,8},{10,11... | collective-permute-start | bytes 3145736 | tf_op jit(solution)/shard_map/ppermute | solution.py:31
  552.3 52.3 %collective-permute-start.30 = (bf16[2,128,2048]{2,1,0:T(8,128)(2,1)S(1)}, bf16[2,128,2048]{2,1,0:T(8,128)(2,1)S(1)}, u32[]{:S(2)}, u32[]{:S(2)}) collective-permute-start(bf16[2,128,2048]{2,1,0:T(8,128)(2,1)S(1)} %fusion.29), channel_id=1, source_target_pairs={{0,2},{1,3},{2,4},{3,5},{4,6},{5,7},{6,0},{7,1},{8,10},{9,11},{10,... | collective-permute-start | bytes 3145736 | tf_op jit(solution)/shard_map/ppermute | solution.py:31
  606.7 30.3 %collective-permute-start.33 = (bf16[2,128,2048]{2,1,0:T(8,128)(2,1)}, bf16[2,128,2048]{2,1,0:T(8,128)(2,1)S(1)}, u32[]{:S(2)}, u32[]{:S(2)}) collective-permute-start(bf16[2,128,2048]{2,1,0:T(8,128)(2,1)} %bitcast.311), channel_id=1, source_target_pairs={{0,1},{1,0},{2,3},{3,2},{4,5},{5,4},{6,7},{7,6},{8,9},{9,8},{10,11... | collective-permute-start | bytes 3145736 | tf_op jit(solution)/shard_map/ppermute | solution.py:31
  610.0 27.1 %collective-permute-start.34 = (bf16[2,128,2048]{2,1,0:T(8,128)(2,1)S(1)}, bf16[2,128,2048]{2,1,0:T(8,128)(2,1)S(1)}, u32[]{:S(2)}, u32[]{:S(2)}) collective-permute-start(bf16[2,128,2048]{2,1,0:T(8,128)(2,1)S(1)} %add_convert_fusion.6), channel_id=1, source_target_pairs={{0,2},{1,3},{2,4},{3,5},{4,6},{5,7},{6,0},{7,1},{8,10},{9,11},{10,... | collective-permute-start | bytes 3145736 | tf_op jit(solution)/shard_map/ppermute | solution.py:31
  638.3 30.7 %collective-permute-start.32 = (bf16[2,128,2048]{2,1,0:T(8,128)(2,1)}, bf16[2,128,2048]{2,1,0:T(8,128)(2,1)S(1)}, u32[]{:S(2)}, u32[]{:S(2)}) collective-permute-start(bf16[2,128,2048]{2,1,0:T(8,128)(2,1)} %bitcast.310), channel_id=1, source_target_pairs={{0,1},{1,0},{2,3},{3,2},{4,5},{5,4},{6,7},{7,6},{8,9},{9,8},{10,11... | collective-permute-start | bytes 3145736 | tf_op jit(solution)/shard_map/ppermute | solution.py:31
  642.0 27.0 %collective-permute-start.35 = (bf16[2,128,2048]{2,1,0:T(8,128)(2,1)S(1)}, bf16[2,128,2048]{2,1,0:T(8,128)(2,1)S(1)}, u32[]{:S(2)}, u32[]{:S(2)}) collective-permute-start(bf16[2,128,2048]{2,1,0:T(8,128)(2,1)S(1)} %add_convert_fusion.5), channel_id=1, source_target_pairs={{0,2},{1,3},{2,4},{3,5},{4,6},{5,7},{6,0},{7,1},{8,10},{9,11},{10,... | collective-permute-start | bytes 3145736 | tf_op jit(solution)/shard_map/ppermute | solution.py:31
  684.3 29.3 %all-to-all-start.1 = ((bf16[8,2,128,256]{3,2,1,0:T(8,128)(2,1)}), bf16[8,2,128,256]{3,2,1,0:T(8,128)(2,1)}, u32[]{:S(2)}, u32[]{:S(2)}) async-start(bf16[8,2,128,256]{3,2,1,0:T(8,128)(2,1)} %bitcast.228), calls=%async_computation.1 | async-start | bytes 2097152 | tf_op jit(solution)/shard_map/all_to_all | solution.py:745
  688.9 341.4 %reduce-scatter.4.cloned.1.call-start = ((), (), s32[]{:S(2)}) async-start(), calls=%async_computation.12 | async-start | bytes 20971520 | tf_op jit(solution)/shard_map/reduce_scatter | solution.py:731
  726.0 73.4 %all-to-all-start.2 = ((bf16[8,2,128,256]{3,2,1,0:T(8,128)(2,1)}), bf16[8,2,128,256]{3,2,1,0:T(8,128)(2,1)}, u32[]{:S(2)}, u32[]{:S(2)}) async-start(bf16[8,2,128,256]{3,2,1,0:T(8,128)(2,1)} %bitcast.227), calls=%async_computation.4 | async-start | bytes 2097152 | tf_op jit(solution)/shard_map/all_to_all | solution.py:745
  732.2 327.0 %reduce-scatter.8.cloned.1.call-start = ((), (), s32[]{:S(2)}) async-start(), calls=%async_computation.14 | async-start | bytes 20971520 | tf_op jit(solution)/shard_map/reduce_scatter | solution.py:731
  735.5 63.8 %collective-permute-start.38 = (bf16[2,128,2048]{2,1,0:T(8,128)(2,1)}, bf16[2,128,2048]{2,1,0:T(8,128)(2,1)}, u32[]{:S(2)}, u32[]{:S(2)}) collective-permute-start(bf16[2,128,2048]{2,1,0:T(8,128)(2,1)} %after.90), channel_id=1, source_target_pairs={{0,1},{1,0},{2,3},{3,2},{4,5},{5,4},{6,7},{7,6},{8,9},{9,8},{10,11... | collective-permute-start | bytes 3145736 | tf_op jit(solution)/shard_map/ppermute | solution.py:31
  740.9 89.5 %collective-permute-start.41 = (bf16[2,128,2048]{2,1,0:T(8,128)(2,1)}, bf16[2,128,2048]{2,1,0:T(8,128)(2,1)}, u32[]{:S(2)}, u32[]{:S(2)}) collective-permute-start(bf16[2,128,2048]{2,1,0:T(8,128)(2,1)} %bitcast.76), channel_id=1, source_target_pairs={{0,1},{1,0},{2,3},{3,2},{4,5},{5,4},{6,7},{7,6},{8,9},{9,8},{10,11... | collective-permute-start | bytes 3145736 | tf_op jit(solution)/shard_map/ppermute | solution.py:31
  801.2 25.0 %collective-permute-start.42 = (f32[2,128]{1,0:T(2,128)S(1)}, f32[2,128]{1,0:T(2,128)S(1)}, u32[]{:S(2)}, u32[]{:S(2)}) collective-permute-start(f32[2,128]{1,0:T(2,128)S(1)} %reduce_sum.95), channel_id=1, source_target_pairs={{0,8},{8,0},{16,24},{24,16},{1,9},{9,1},{17,25},{25,17},{2,10},{10... | collective-permute-start | bytes 3080 | tf_op jit(solution)/shard_map/ppermute | solution.py:780
  804.3 27.4 %collective-permute-start.40 = (bf16[2,128,2048]{2,1,0:T(8,128)(2,1)}, bf16[2,128,2048]{2,1,0:T(8,128)(2,1)}, u32[]{:S(2)}, u32[]{:S(2)}) collective-permute-start(bf16[2,128,2048]{2,1,0:T(8,128)(2,1)} %fusion.25), channel_id=1, source_target_pairs={{0,2},{1,3},{2,4},{3,5},{4,6},{5,7},{6,0},{7,1},{8,10},{9,11},{10,... | collective-permute-start | bytes 3145736 | tf_op jit(solution)/shard_map/ppermute | solution.py:31
  805.8 25.9 %collective-permute-start.39 = (bf16[2,128,2048]{2,1,0:T(8,128)(2,1)}, bf16[2,128,2048]{2,1,0:T(8,128)(2,1)}, u32[]{:S(2)}, u32[]{:S(2)}) collective-permute-start(bf16[2,128,2048]{2,1,0:T(8,128)(2,1)} %after.93), channel_id=1, source_target_pairs={{0,1},{1,0},{2,3},{3,2},{4,5},{5,4},{6,7},{7,6},{8,9},{9,8},{10,11... | collective-permute-start | bytes 3145736 | tf_op jit(solution)/shard_map/ppermute | solution.py:31
  841.0 71.6 %collective-permute-start.37 = (bf16[2,128,2048]{2,1,0:T(8,128)(2,1)}, bf16[2,128,2048]{2,1,0:T(8,128)(2,1)S(1)}, u32[]{:S(2)}, u32[]{:S(2)}) collective-permute-start(bf16[2,128,2048]{2,1,0:T(8,128)(2,1)} %bitcast.66), channel_id=1, source_target_pairs={{0,1},{1,0},{2,3},{3,2},{4,5},{5,4},{6,7},{7,6},{8,9},{9,8},{10,11... | collective-permute-start | bytes 3145736 | tf_op jit(solution)/shard_map/ppermute | solution.py:31
  841.0 71.6 %collective-permute-start.46 = (bf16[2,128,2048]{2,1,0:T(8,128)(2,1)}, bf16[2,128,2048]{2,1,0:T(8,128)(2,1)S(1)}, u32[]{:S(2)}, u32[]{:S(2)}) collective-permute-start(bf16[2,128,2048]{2,1,0:T(8,128)(2,1)} %bitcast.80), channel_id=1, source_target_pairs={{0,1},{1,0},{2,3},{3,2},{4,5},{5,4},{6,7},{7,6},{8,9},{9,8},{10,11... | collective-permute-start | bytes 3145736 | tf_op jit(solution)/shard_map/ppermute | solution.py:31
  846.6 38.4 %collective-permute-start.49 = (bf16[512,1152]{1,0:T(8,128)(2,1)}, bf16[512,1152]{1,0:T(8,128)(2,1)}, u32[]{:S(2)}, u32[]{:S(2)}) collective-permute-start(bf16[512,1152]{1,0:T(8,128)(2,1)} %fusion.14), channel_id=1, source_target_pairs={{0,16},{8,24},{16,0},{24,8},{1,17},{9,25},{17,1},{25,9},{2,18},{10... | collective-permute-start | bytes 3538952 | tf_op jit(solution)/shard_map/ppermute | solution.py:31
  850.6 61.9 %collective-permute-start.44 = (bf16[2,128,2048]{2,1,0:T(8,128)(2,1)}, bf16[2,128,2048]{2,1,0:T(8,128)(2,1)S(1)}, u32[]{:S(2)}, u32[]{:S(2)}) collective-permute-start(bf16[2,128,2048]{2,1,0:T(8,128)(2,1)} %add_convert_fusion.4), channel_id=1, source_target_pairs={{0,2},{1,3},{2,4},{3,5},{4,6},{5,7},{6,0},{7,1},{8,10},{9,11},{10,... | collective-permute-start | bytes 3145736 | tf_op jit(solution)/shard_map/ppermute | solution.py:31
  855.2 57.4 %collective-permute-start.45 = (bf16[2,128,2048]{2,1,0:T(8,128)(2,1)}, bf16[2,128,2048]{2,1,0:T(8,128)(2,1)}, u32[]{:S(2)}, u32[]{:S(2)}) collective-permute-start(bf16[2,128,2048]{2,1,0:T(8,128)(2,1)} %fusion.23), channel_id=1, source_target_pairs={{0,2},{1,3},{2,4},{3,5},{4,6},{5,7},{6,0},{7,1},{8,10},{9,11},{10,... | collective-permute-start | bytes 3145736 | tf_op jit(solution)/shard_map/ppermute | solution.py:31
  914.2 35.9 %collective-permute-start.36 = (bf16[2,128,2048]{2,1,0:T(8,128)(2,1)}, bf16[2,128,2048]{2,1,0:T(8,128)(2,1)}, u32[]{:S(2)}, u32[]{:S(2)}) collective-permute-start(bf16[2,128,2048]{2,1,0:T(8,128)(2,1)} %bitcast.65), channel_id=1, source_target_pairs={{0,1},{1,0},{2,3},{3,2},{4,5},{5,4},{6,7},{7,6},{8,9},{9,8},{10,11... | collective-permute-start | bytes 3145736 | tf_op jit(solution)/shard_map/ppermute | solution.py:31
  915.8 78.1 %all-to-all-start.3 = ((bf16[8,64,1152]{2,1,0:T(8,128)(2,1)}), bf16[8,64,1152]{2,1,0:T(8,128)(2,1)S(1)}, u32[]{:S(2)}, u32[]{:S(2)}) async-start(bf16[8,64,1152]{2,1,0:T(8,128)(2,1)} %bitcast.94), calls=%async_computation.5 | async-start | bytes 2359296 | tf_op jit(solution)/shard_map/all_to_all | solution.py:812
  923.3 44.1 %collective-permute-start.50 = (bf16[2,128,2048]{2,1,0:T(8,128)(2,1)}, bf16[2,128,2048]{2,1,0:T(8,128)(2,1)S(1)}, u32[]{:S(2)}, u32[]{:S(2)}) collective-permute-start(bf16[2,128,2048]{2,1,0:T(8,128)(2,1)} %add_convert_fusion.3), channel_id=1, source_target_pairs={{0,2},{1,3},{2,4},{3,5},{4,6},{5,7},{6,0},{7,1},{8,10},{9,11},{10,... | collective-permute-start | bytes 3145736 | tf_op jit(solution)/shard_map/ppermute | solution.py:31
  928.3 60.1 %collective-permute-start.51 = (bf16[2,128,2048]{2,1,0:T(8,128)(2,1)}, bf16[2,128,2048]{2,1,0:T(8,128)(2,1)S(1)}, u32[]{:S(2)}, u32[]{:S(2)}) collective-permute-start(bf16[2,128,2048]{2,1,0:T(8,128)(2,1)} %add_convert_fusion.2), channel_id=1, source_target_pairs={{0,2},{1,3},{2,4},{3,5},{4,6},{5,7},{6,0},{7,1},{8,10},{9,11},{10,... | collective-permute-start | bytes 3145736 | tf_op jit(solution)/shard_map/ppermute | solution.py:31
  930.8 21.4 %collective-permute-start.52 = (f32[2,128]{1,0:T(2,128)S(1)}, f32[2,128]{1,0:T(2,128)S(1)}, u32[]{:S(2)}, u32[]{:S(2)}) collective-permute-start(f32[2,128]{1,0:T(2,128)S(1)} %add.429), channel_id=1, source_target_pairs={{0,1},{1,0},{2,3},{3,2},{4,5},{5,4},{6,7},{7,6},{8,9},{9,8},{10,11... | collective-permute-start | bytes 3080 | tf_op jit(solution)/shard_map/ppermute | solution.py:780
  994.9 42.1 %collective-permute-start.31 = (bf16[2,128,2048]{2,1,0:T(8,128)(2,1)}, bf16[2,128,2048]{2,1,0:T(8,128)(2,1)S(1)}, u32[]{:S(2)}, u32[]{:S(2)}) collective-permute-start(bf16[2,128,2048]{2,1,0:T(8,128)(2,1)} %bitcast.308), channel_id=1, source_target_pairs={{0,1},{1,0},{2,3},{3,2},{4,5},{5,4},{6,7},{7,6},{8,9},{9,8},{10,11... | collective-permute-start | bytes 3145736 | tf_op jit(solution)/shard_map/ppermute | solution.py:31
  996.3 45.0 %collective-permute-start.54 = (bf16[2,128,2048]{2,1,0:T(8,128)(2,1)}, bf16[2,128,2048]{2,1,0:T(8,128)(2,1)S(1)}, u32[]{:S(2)}, u32[]{:S(2)}) collective-permute-start(bf16[2,128,2048]{2,1,0:T(8,128)(2,1)} %bitcast.309), channel_id=1, source_target_pairs={{0,1},{1,0},{2,3},{3,2},{4,5},{5,4},{6,7},{7,6},{8,9},{9,8},{10,11... | collective-permute-start | bytes 3145736 | tf_op jit(solution)/shard_map/ppermute | solution.py:31
  1000.7 40.7 %collective-permute-start.53 = (bf16[2,128,2048]{2,1,0:T(8,128)(2,1)}, bf16[2,128,2048]{2,1,0:T(8,128)(2,1)S(1)}, u32[]{:S(2)}, u32[]{:S(2)}) collective-permute-start(bf16[2,128,2048]{2,1,0:T(8,128)(2,1)} %add_convert_fusion.1), channel_id=1, source_target_pairs={{0,2},{1,3},{2,4},{3,5},{4,6},{5,7},{6,0},{7,1},{8,10},{9,11},{10,... | collective-permute-start | bytes 3145736 | tf_op jit(solution)/shard_map/ppermute | solution.py:31
  1005.8 35.5 %collective-permute-start.55 = (f32[2,128]{1,0:T(2,128)S(1)}, f32[2,128]{1,0:T(2,128)S(1)}, u32[]{:S(2)}, u32[]{:S(2)}) collective-permute-start(f32[2,128]{1,0:T(2,128)S(1)} %add.432), channel_id=1, source_target_pairs={{0,2},{1,3},{2,0},{3,1},{4,6},{5,7},{6,4},{7,5},{8,10},{9,11},{10,... | collective-permute-start | bytes 3080 | tf_op jit(solution)/shard_map/ppermute | solution.py:780
  (126 other events, 1013.5 us)
Sparse Core Ops, SparseCore 0:
  11.2 34.1 all-gather.5
  47.0 58.2 all-gather.7
  106.9 105.9 all-gather.9
  214.2 105.9 all-gather.11
  321.6 105.9 all-gather.13
  606.8 125.2 reduce-scatter.5
  734.8 136.2 reduce-scatter.3
  914.3 126.1 reduce-scatter.7

commit v5 on v4

--- a/solution.py
+++ b/solution.py
@@ -59,7 +59,7 @@
     return moved
 
 
-def ring_gather(value, axis, work=None, then={}):
+def ring_gather(value, axis, work=None, then={}, tie_last=True):
     outer, inner = sizes(axis)
     blocks, arrived = [], []
     for a in range(outer):
@@ -69,7 +69,7 @@
         moved = row[1:]
         if a + 1 < outer:
             moved.append(shift(value, axis, outer, inner, 1, 0))
-        if work is not None:
+        if work is not None and (tie_last or a + 1 < outer):
             moved = together([f(arrived) for f in work[a : a + 1] if f], *moved)
         if a in then:
             then[a](moved)
@@ -108,7 +108,7 @@
         moved = [row_move(parts, a, axis)]
         if step:
             moved.append(ahead(total, axis))
-        moved = together([f(arrived) for f in work[step : step + 1]], *moved)
+        moved = together([f(arrived) for f in work[step : step + 1] if f], *moved)
         if step in then:
             then[step](moved)
         arrived = moved
@@ -318,7 +318,7 @@
     gain_ref[...] = gain
 
 
-def part_grads(grad_qkv, w_qkv, x_all, inv_all, ties=()):
+def part_grads(grad_qkv, w_first, x_all, inv_all, ties=()):
     blocks = grad_qkv.shape[0]
     width = grad_qkv.shape[-1]
     count = grad_qkv.size // width
@@ -329,7 +329,7 @@
         (D // part,),
         [
             (grad_qkv.reshape(count, width), whole_of((count, width))),
-            (w_qkv, pl.BlockSpec((part, width), lambda d: (d, 0))),
+            (w_first, pl.BlockSpec((part, width), lambda d: (d, 0))),
             (x_all.reshape(count, x_all.shape[-1]), pl.BlockSpec((count, part), lambda d: (0, d))),
             (inv_all.reshape(count, 1), whole_of((count, 1))),
         ],
@@ -339,6 +339,62 @@
         ties=ties,
     )
     return found[:-1], found[-1][0]
+
+
+def proj_kernel(blocks, order_ref, place_ref, h_ref, grad_ref, column_ref, gain_ref, *refs):
+    o_refs, out_refs, found_ref = refs[:blocks], refs[blocks:-1], refs[-1]
+    k = pl.program_id(0)
+    inputs, width = grad_ref.shape[1], column_ref.shape[1]
+    owners = found_ref.shape[0] // width
+    found_ref[:, :inputs] = dot(h_ref[...], grad_ref[...], 0, 0)
+    for j in range(owners):
+        place = place_ref[order_ref[k] * owners + j]
+        for b in range(blocks):
+
+            @pl.when(place == b)
+            def _(b=b, j=j):
+                found_ref[j * width : (j + 1) * width, inputs : inputs + width] = dot(
+                    o_refs[b][...], column_ref[...], 0, 0
+                )
+
+    found_ref[:, inputs + width :] = gain_ref[...]
+    for b, ref in enumerate(out_refs):
+
+        @pl.when(k == b)
+        def _(ref=ref):
+            ref[...] = found_ref[...].astype(bf16)
+
+
+def proj_grads(h_one, grad_qkv, o_blocks, columns, gains, order, places, ties=()):
+    count, inputs = h_one.size // D, grad_qkv.shape[-1]
+    width, nf = columns.shape[1], order.shape[0]
+    rows, across = D // nf, inputs + width + gains.shape[1]
+    result = jax.ShapeDtypeStruct((rows, across), bf16)
+    ins = [
+        (h_one.reshape(count, D), pl.BlockSpec((count, rows), lambda k, order, _: (0, order[k]))),
+        (grad_qkv.reshape(count, inputs), whole_of((count, inputs))),
+        (columns, whole_of(columns.shape)),
+        (gains, pl.BlockSpec((rows, gains.shape[1]), lambda k, order, _: (order[k], 0))),
+    ] + [(v, whole_of(v.shape)) for v in o_blocks]
+
+    def run(*refs):
+        lead = 2 + len(ins)
+        proj_kernel(len(o_blocks), *refs[:lead], *refs[lead + len(ties) :])
+
+    return pl.pallas_call(
+        run,
+        grid_spec=pltpu.PrefetchScalarGridSpec(
+            num_scalar_prefetch=2,
+            grid=(nf,),
+            in_specs=[spec for _, spec in ins] + [pl.BlockSpec(memory_space=pl.ANY)] * len(ties),
+            out_specs=[whole_of(result.shape)] * nf,
+            scratch_shapes=[pltpu.VMEM((rows, across), f32)],
+        ),
+        out_shape=[result] * nf,
+        compiler_params=pltpu.CompilerParams(vmem_limit_bytes=56 * 2**20),
+        cost_estimate=little,
+        name="proj_grads",
+    )(order, places, *[value for value, _ in ins], *ties)
 
 
 part = 512
@@ -697,20 +753,28 @@
         after(o_heads.reshape(group * micro, width), g_blocks[-1]),
         "seq",
         (grad_work, act_work, first_work),
-    )
-    o_last = o_all[-1]
-    o_all = jnp.concatenate(o_all, axis=1)
+        {2: lambda moved: keep(o_moved=moved)},
+        tie_last=False,
+    )
+    across = sizes("seq")[1] - 1
+    o_all, o_last = o_all[:-across], o_all[-across:]
     first = done["first"]
     grad_rows = done["grad_rows"]
     hidden, grad_gate_act, grad_up_act = done["acts"]
-    second = combined((grad_gate_act, grad_up_act), (w_gate, w_up), 1, False, (first[0],))
+    second = combined(
+        (grad_gate_act, grad_up_act), (w_gate, w_up), 1, False, (first[0], *done["o_moved"])
+    )
 
     def down_work(ties):
-        return keep(whole_down=bank_grad(grad_rows, hidden, tuple(ties) + (o_last,)))
+        return keep(whole_down=bank_grad(grad_rows, hidden, ties))
+
+    def down_then(moved):
+        o_all.extend(together((done["whole_down"], *moved), *o_last))
+        keep(sum_down=after(done["whole_down"], o_all[-1]))
 
     def mixed_work(h):
         def work(ties):
-            mixed = combined((hidden,), (w_down,), h, True, ties)
+            mixed = combined((hidden,), (w_down,), h, True, tuple(ties) + tuple(o_all[-across:]))
             done.setdefault("mixed", []).extend(mixed)
             return mixed[0]
 
@@ -722,7 +786,7 @@
         "seq",
         (lambda _: second[0], down_work, mixed_work(0), mixed_work(1)),
         {
-            1: lambda moved: keep(sum_down=after(done["whole_down"], *moved)),
+            1: down_then,
             3: lambda moved: keep(last=moved),
         },
     ).reshape(tokens, D)
@@ -755,7 +819,7 @@
     k = sizes("seq")[1] + 1 % sizes("seq")[1]
     mixed[k] = after(mixed[k], do_blocks)
     grad_qkv, grad_head = attend_back(qkv, do_heads, tables)
-    part_h_one, grad_gain_one = part_grads(grad_qkv, w_qkv, x_all, inv_all)
+    part_h_one, grad_gain_one = part_grads(grad_qkv, w_first, x_all, inv_all)
     one, columns = together(
         (grad_gain_one,), row_move(mixed, 1, "seq"), to_heads(after(grad_attn, do_blocks))
     )
@@ -763,14 +827,16 @@
     total = one
     part_h_one = [v.reshape(micro, rows, D) for v in part_h_one]
     part_h_one[k] = after(part_h_one[k], total)
-    from_qkv = jnp.einsum(
-        "smtd,smte->de", after(h_one, total), grad_qkv, preferred_element_type=f32
-    )
-    from_out = jnp.einsum(
-        "td,te->de",
-        after(o_all, total),
+    gains = jnp.pad(jnp.stack([grad_gain_one, grad_gain_two], axis=1), ((0, 0), (0, HD - 2)))
+    whole = proj_grads(
+        h_one,
+        grad_qkv,
+        o_all,
         columns.reshape(micro * group, width),
-        preferred_element_type=f32,
+        gains,
+        relative_order("fsdp"),
+        inverse_seq,
+        (total,),
     )
     left = exchanges()
     head = jnp.sum(after(grad_head, total), axis=0)
@@ -782,7 +848,7 @@
     total = ahead(row_sum(total, mixed, 1, "seq"), "seq")
     head = head + exchange(head)
     total, two, one, moved = together(
-        (from_qkv, from_out),
+        (whole[0],),
         total,
         row_move(mixed, 2, "seq"),
         row_move(part_h_one, 1, "seq"),
@@ -790,14 +856,10 @@
     )
     head = head + moved
 
-    from_out = reorder(from_out.reshape(ns, width, width), inverse_seq, axis=0).reshape(D, width)
-    from_gains = jnp.pad(jnp.stack([grad_gain_one, grad_gain_two], axis=1), ((0, 0), (0, HD - 2)))
-    whole = jnp.concatenate([from_qkv, from_out, from_gains], axis=1).astype(bf16)
-    whole = after(whole, total)
-    whole = reorder(whole.reshape(nf, D // nf, -1), relative_order("fsdp"), axis=0)
-    owned = ring_scatter([whole[k] for k in range(nf)], "fsdp").astype(bf16)
-
     whole_up = bank_grad(taken, grad_up_act, (one,))
+    whole = [after(v, one) for v in whole]
+    owned = ring_scatter(whole, "fsdp", (None, lambda _: whole_up)).astype(bf16)
+
     total = ahead(add(row_sum(two, mixed, 2, "seq"), total).astype(bf16), "seq")
     grad_total = ahead(row_sum(one, part_h_one, 1, "seq"), "seq")
     total, grad_total, three, two, owned = together(
@@ -813,11 +875,9 @@
         owned.reshape(ns, share, -1), "seq", split_axis=0, concat_axis=0, tiled=True
     )
 
-    total = ahead(add(row_sum(three, mixed, 3, "seq"), total).astype(bf16), "seq")
     grad_total = add(row_sum(two, part_h_one, 2, "seq"), grad_total).astype(bf16)
-    total, grad_total, three, moved, owned = together(
+    grad_total, zero, moved, owned = together(
         (grad_down,),
-        total,
         ahead(grad_total, "seq"),
         row_move(part_h_one, 3, "seq"),
         exchange(head),
@@ -825,13 +885,17 @@
     )
     head = head + moved
 
-    grad_total = add(row_sum(three, part_h_one, 3, "seq"), grad_total).astype(bf16)
-    grad_total, zero, moved, last = together(
+    k = 1 % sizes("seq")[1]
+    mixed[k], part_h_one[k] = after(mixed[k], owned), after(part_h_one[k], owned)
+    total = ahead(add(row_sum(three, mixed, 3, "seq"), total).astype(bf16), "seq")
+    grad_total = add(row_sum(zero, part_h_one, 3, "seq"), grad_total).astype(bf16)
+    grad_total, zero, moved, last, total = together(
         (grad_gate,),
         ahead(grad_total, "seq"),
         row_move(part_h_one, 0, "seq"),
         exchange(head),
         row_move(mixed, 0, "seq"),
+        total,
     )
     head = head + moved
     mixed = add(row_sum(last, mixed, 0, "seq"), total).reshape(tokens, D)

time: 1080 us -> 1030 us (0.954)
  local copies, waits for them, and re-layouts: 138 us -> 114 us
  Pallas kernels: 358 us -> 379 us
  matrix products: 36.8 us -> 19.3 us
  waiting for transfers between devices: 332 us -> 315 us
    ppermute x52, waiting for transfers between devices: 322 us -> 287 us  [shift(): return lax.ppermute(value, axis, pairs)]
    pallas_call x0 -> x1, Pallas kernels: none -> 20.8 us  [proj_grads(): pl.pallas_call(run, grid_spec=pltpu.PrefetchScalarGridSpec(num_scalar_pre...]
    dot_general x2 -> x0, matrix products: 17.7 us -> none  [the longest x1 11.4 us: body(): jnp.einsum('smtd,smte->de', after(h_one, total), grad_qkv, preferred_elem...]
    reduce_scatter x3, waiting for transfers between devices: 0.01 us -> 11.4 us  [bank_sum(): lax.psum_scatter(whole, 'fsdp', scatter_dimension=1, tiled=True).astype(f32)]
    unnamed x267 -> x258, local copies, waits for them, and re-layouts: 73.8 us -> 68.9 us
  transfers between devices with their start and end apart: 68 -> 68, of which waited for: 22 -> 25; matrix products, arithmetic and copies ran while one was open for 19% -> 15% of each run, Pallas kernels for 33% -> 37%
where the time goes in v5:
time: 1030 us; the launch traced here: 1020 us
  Pallas kernels  379 us (37%)
  waiting for transfers between devices  315 us (31%)
  local copies, waits for them, and re-layouts  114 us (11%)
  other arithmetic  79.5 us (8%)
  starting transfers between devices  72.1 us (7%)
  blocking collectives  26 us (3%)
  matrix products  19.3 us (2%)
  between operations  16 us (2%)
    pallas_call x12, Pallas kernels, call(): pl.pallas_call(run, grid=grid, in_specs=[spec for _, spec in ins] + [pl.B...  308 us
    ppermute x52, waiting for transfers between devices, shift(): return lax.ppermute(value, axis, pairs)  287 us
    unnamed x258, local copies, waits for them, and re-layouts  68.9 us
    ppermute x52, starting transfers between devices, shift(): return lax.ppermute(value, axis, pairs)  51.4 us
    pallas_call x1, Pallas kernels, attend_back(): pl.pallas_call(lambda *refs: attend_back_kernel(tile, *refs[:7], *refs[-2...  33.3 us
    all_to_all x1, blocking collectives, body(): lax.all_to_all(o_heads, 'seq', split_axis=0, concat_axis=0, tiled=True)  26 us
    convert_element_type x3, other arithmetic, bank_sum(): lax.psum_scatter(whole, 'fsdp', scatter_dimension=1, tiled=True).astype(f32)  20.8 us
    pallas_call x1, Pallas kernels, proj_grads(): pl.pallas_call(run, grid_spec=pltpu.PrefetchScalarGridSpec(num_scalar_pre...  20.8 us
  transfers between devices with their start and end apart: 68, of which 25 were waited for; matrix products, arithmetic and copies ran while one was open for 15% of the time, Pallas kernels for 37%

profile of v5, /device:TPU:0, one launch (start us, length us, event | category | flops | bytes accessed | tf_op | source)
XLA Modules:
  0.0 1020.2 jit_solution(2698265542605837984)
XLA Ops:
  16.7 3.0 collective-permute-start
  25.7 2.7 bitcast_dynamic-update-slice_fusion.7
  28.4 19.4 %collective-permute-done.1 = bf16[2,128,2176]{2,1,0:T(8,128)(2,1)} collective-permute-done((bf16[2,128,2176]{2,1,0:T(8,128)(2,1)}, bf16[2,128,2176]{2,1,0:T(8,128)(2,1)}, u32[]{:S(2)}, u32[]{:S(2)}) %collective-permute-start.1) | collective-permute-done | bytes 1114144 | tf_op jit(solution)/shard_map/ppermute | solution.py:31
  48.4 2.3 bitcast_dynamic-update-slice_fusion.6
  50.7 2.3 bitcast_dynamic-update-slice_fusion.5
  53.0 22.5 %collective-permute-done.3 = bf16[2,128,2176]{2,1,0:T(8,128)(2,1)S(1)} collective-permute-done((bf16[2,128,2176]{2,1,0:T(8,128)(2,1)}, bf16[2,128,2176]{2,1,0:T(8,128)(2,1)S(1)}, u32[]{:S(2)}, u32[]{:S(2)}) %collective-permute-start.3) | collective-permute-done | bytes 1114144 | tf_op jit(solution)/shard_map/ppermute | solution.py:31
  79.2 23.3 %collective-permute-done.5 = bf16[2,128,2176]{2,1,0:T(8,128)(2,1)S(1)} collective-permute-done((bf16[2,128,2176]{2,1,0:T(8,128)(2,1)S(1)}, bf16[2,128,2176]{2,1,0:T(8,128)(2,1)S(1)}, u32[]{:S(2)}, u32[]{:S(2)}) %collective-permute-start.5) | collective-permute-done | bytes 1114144 | tf_op jit(solution)/shard_map/ppermute | solution.py:31
  105.7 19.7 %collective-permute-done.6 = bf16[2,128,2176]{2,1,0:T(8,128)(2,1)S(1)} collective-permute-done((bf16[2,128,2176]{2,1,0:T(8,128)(2,1)S(1)}, bf16[2,128,2176]{2,1,0:T(8,128)(2,1)S(1)}, u32[]{:S(2)}, u32[]{:S(2)}) %collective-permute-start.6) | collective-permute-done | bytes 1114144 | tf_op jit(solution)/shard_map/ppermute | solution.py:31
  126.4 5.1 fusion
  133.5 5.3 fusion.2
  138.8 6.9 fusion.4.refs_0_
  145.8 16.5 %attend.1 = bf16[8,2,128,256]{3,2,1,0:T(8,128)(2,1)S(1)} custom-call(bf16[8,2,128,768]{3,2,1,0:T(8,128)(2,1)S(1)} %fusion.4.refs_0_, f32[1024,128]{1,0:T(8,128)S(1)} %get-tuple-element.117.refs_1_.refs_2_, f32[1024,128]{1,0:T(8,128)S(1)} %get-tuple-element.116.refs_2_.refs_3_, s32[2,1,1024]{2,1,0:T(1,128)S(1)} %bitcast.205, ...), custom_call_target="tpu_custom_call" | custom-call | flops 1 | bytes 1 | tf_op jit(solution)/shard_map/attend/pallas_call | solution.py:276
  164.5 26.0 %all_to_all.20 = bf16[8,2,128,256]{3,2,1,0:T(8,128)(2,1)S(1)} all-to-all(bf16[8,2,128,256]{3,2,1,0:T(8,128)(2,1)S(1)} %gather_fusion.1), channel_id=1, replica_groups=mesh['fsdp'=4,'seq'=8] {'seq'}, dimensions={0} | all-to-all | bytes 2097152 | tf_op jit(solution)/shard_map/all_to_all | solution.py:684
  191.8 5.8 multiply_reduce_fusion.3
  200.7 21.6 %collective-permute-done.7.refs_0_ = bf16[2,128,2048]{2,1,0:T(8,128)(2,1)S(1)} collective-permute-done((bf16[2,128,2048]{2,1,0:T(8,128)(2,1)S(1)}, bf16[2,128,2048]{2,1,0:T(8,128)(2,1)S(1)}, u32[]{:S(2)}, u32[]{:S(2)}) %collective-permute-start.7) | collective-permute-done | bytes 1048608 | tf_op jit(solution)/shard_map/ppermute | solution.py:31
  222.3 3.2 collective-permute-done.8.refs_1_.refs_0_
  226.9 23.7 %collective-permute-done.10.refs_1_.refs_0_ = bf16[2,128,2048]{2,1,0:T(8,128)(2,1)S(1)} collective-permute-done((bf16[2,128,2048]{2,1,0:T(8,128)(2,1)}, bf16[2,128,2048]{2,1,0:T(8,128)(2,1)S(1)}, u32[]{:S(2)}, u32[]{:S(2)}) %collective-permute-start.10) | collective-permute-done | bytes 1048608 | tf_op jit(solution)/shard_map/ppermute | solution.py:31
  252.7 21.2 %collective-permute-done.11.refs_0_ = bf16[2,128,2048]{2,1,0:T(8,128)(2,1)S(1)} collective-permute-done((bf16[2,128,2048]{2,1,0:T(8,128)(2,1)}, bf16[2,128,2048]{2,1,0:T(8,128)(2,1)S(1)}, u32[]{:S(2)}, u32[]{:S(2)}) %collective-permute-start.11) | collective-permute-done | bytes 1048608 | tf_op jit(solution)/shard_map/ppermute | solution.py:31
  279.5 19.6 %collective-permute-done.13.refs_1_ = bf16[2,128,2048]{2,1,0:T(8,128)(2,1)S(1)} collective-permute-done((bf16[2,128,2048]{2,1,0:T(8,128)(2,1)}, bf16[2,128,2048]{2,1,0:T(8,128)(2,1)S(1)}, u32[]{:S(2)}, u32[]{:S(2)}) %collective-permute-start.13) | collective-permute-done | bytes 1048608 | tf_op jit(solution)/shard_map/ppermute | solution.py:31
  301.7 18.4 %collective-permute-done.14.refs_0_ = bf16[2,128,2048]{2,1,0:T(8,128)(2,1)S(1)} collective-permute-done((bf16[2,128,2048]{2,1,0:T(8,128)(2,1)}, bf16[2,128,2048]{2,1,0:T(8,128)(2,1)S(1)}, u32[]{:S(2)}, u32[]{:S(2)}) %collective-permute-start.14) | collective-permute-done | bytes 1048608 | tf_op jit(solution)/shard_map/ppermute | solution.py:31
  334.6 22.3 %dispatch.3 = (bf16[4,2,384,2048]{3,2,1,0:T(8,128)(2,1)}, f32[4,2,384,1024]{3,2,1,0:T(8,128)}) custom-call(bf16[256,2048]{1,0:T(8,128)(2,1)} %copy-done.78, bf16[256,2048]{1,0:T(8,128)(2,1)} %bitcast.216, bf16[256,2048]{1,0:T(8,128)(2,1)} %bitcast.220, bf16[256,2048]{1,0:T(8,128)(2,1)} %bitcast.224, bf16[256,2048]{1,0:T(8,128)(2,1)} %bitcast.214, ...), custom_call_target="tpu_custom_call" | custom-call | flops 1 | bytes 1 | tf_op jit(solution)/shard_map/dispatch/pallas_call | solution.py:423
  359.1 19.8 %dispatch.4 = (bf16[4,2,384,2048]{3,2,1,0:T(8,128)(2,1)}, f32[4,2,384,1024]{3,2,1,0:T(8,128)}) custom-call(bf16[256,2048]{1,0:T(8,128)(2,1)} %copy-done.78, bf16[256,2048]{1,0:T(8,128)(2,1)} %bitcast.217, bf16[256,2048]{1,0:T(8,128)(2,1)} %bitcast.221, bf16[256,2048]{1,0:T(8,128)(2,1)} %bitcast.225, ...), custom_call_target="tpu_custom_call", output_to_operand_aliasing={{0}: (11, {}), {1}: (12, {})} | custom-call | flops 1 | bytes 1 | tf_op jit(solution)/shard_map/dispatch/pallas_call | solution.py:423
  381.7 20.7 %collective-permute-done.20.refs_1_ = bf16[2,128,2048]{2,1,0:T(8,128)(2,1)S(1)} collective-permute-done((bf16[2,128,2048]{2,1,0:T(8,128)(2,1)}, bf16[2,128,2048]{2,1,0:T(8,128)(2,1)S(1)}, u32[]{:S(2)}, u32[]{:S(2)}) %collective-permute-start.20) | collective-permute-done | bytes 1048608 | tf_op jit(solution)/shard_map/ppermute | solution.py:31
  405.8 34.1 %dispatch.5 = (bf16[4,2,384,2048]{3,2,1,0:T(8,128)(2,1)}, f32[4,2,384,1024]{3,2,1,0:T(8,128)}) custom-call(bf16[256,2048]{1,0:T(8,128)(2,1)} %bitcast.228, bf16[256,2048]{1,0:T(8,128)(2,1)} %bitcast.212, bf16[256,2048]{1,0:T(8,128)(2,1)} %bitcast.213, bf16[256,2048]{1,0:T(8,128)(2,1)} %bitcast.226, bf16[256,2048]{1,0:T(8,128)(2,1)} %bitcast.227, ...), custom_call_target="tpu_custom_call" | custom-call | flops 1 | bytes 1 | tf_op jit(solution)/shard_map/dispatch/pallas_call | solution.py:423
  441.4 4.1 collective-permute-start.24
  445.5 31.7 %activate.1 = (bf16[4,2,384,1024]{3,2,1,0:T(8,128)(2,1)}, bf16[4,2,384,1024]{3,2,1,0:T(8,128)(2,1)}, bf16[4,2,384,1024]{3,2,1,0:T(8,128)(2,1)}) custom-call(bf16[4,2,384,2048]{3,2,1,0:T(8,128)(2,1)} %get-tuple-element.56.refs_1_.refs_0_, f32[4,2,384,1024]{3,2,1,0:T(8,128)} %get-tuple-element.57.refs_1_, f32[4,2,384,1024]{3,2,1,0:T(8,128)} %get-tuple-element.58.refs_2_, ...), custom_call_target="tpu_custom_call" | custom-call | flops 1 | bytes 1 | tf_op jit(solution)/shard_map/activate/pallas_call | solution.py:423
  478.6 2.8 copy.234.refs_4_.refs_2_
  483.3 32.1 %combine.4 = (bf16[256,2048]{1,0:T(8,128)(2,1)}, bf16[256,2048]{1,0:T(8,128)(2,1)}, bf16[256,2048]{1,0:T(8,128)(2,1)}, bf16[256,2048]{1,0:T(8,128)(2,1)}) custom-call(bf16[4,2,384,1024]{3,2,1,0:T(8,128)(2,1)} %get-tuple-element.61.refs_0_.refs_1_, bf16[4,2,384,1024]{3,2,1,0:T(8,128)(2,1)} %get-tuple-element.62.refs_1_, ...), custom_call_target="tpu_custom_call" | custom-call | flops 1 | bytes 1 | tf_op jit(solution)/shard_map/combine/pallas_call | solution.py:423
  516.8 32.3 %combine.5 = (bf16[256,2048]{1,0:T(8,128)(2,1)}, bf16[256,2048]{1,0:T(8,128)(2,1)}, bf16[256,2048]{1,0:T(8,128)(2,1)}, bf16[256,2048]{1,0:T(8,128)(2,1)}) custom-call(bf16[4,2,384,1024]{3,2,1,0:T(8,128)(2,1)} %get-tuple-element.61.refs_0_.refs_1_, bf16[4,2,384,1024]{3,2,1,0:T(8,128)(2,1)} %get-tuple-element.62.refs_1_, ...), custom_call_target="tpu_custom_call" | custom-call | flops 1 | bytes 1 | tf_op jit(solution)/shard_map/combine/pallas_call | solution.py:423
  554.5 24.1 %bank_grad.3.refs_1_.refs_0_ = bf16[4,2048,1024]{2,1,0:T(8,128)(2,1)} custom-call(bf16[4,2,384,2048]{3,2,1,0:T(8,128)(2,1)} %get-tuple-element.59.refs_1_.refs_0_, bf16[4,2,384,1024]{3,2,1,0:T(8,128)(2,1)} %get-tuple-element.60.refs_1_.refs_0_, bf16[2,128,2048]{2,1,0:T(8,128)(2,1)} %after.84.refs_2_), custom_call_target="tpu_custom_call" | custom-call | flops 1 | bytes 1 | tf_op jit(solution)/shard_map/bank_grad/pallas_call | solution.py:423
  580.6 14.5 %collective-permute-done.30.refs_0_ = bf16[2048,256]{1,0:T(8,128)(2,1)S(1)} collective-permute-done((bf16[2048,256]{1,0:T(8,128)(2,1)}, bf16[2048,256]{1,0:T(8,128)(2,1)S(1)}, u32[]{:S(2)}, u32[]{:S(2)}) %collective-permute-start.30) | collective-permute-done | bytes 1048608 | tf_op jit(solution)/shard_map/ppermute | solution.py:31
  601.0 25.7 %combine.6 = (bf16[256,2048]{1,0:T(8,128)(2,1)}, bf16[256,2048]{1,0:T(8,128)(2,1)}, bf16[256,2048]{1,0:T(8,128)(2,1)}, bf16[256,2048]{1,0:T(8,128)(2,1)}) custom-call(bf16[4,2,384,1024]{3,2,1,0:T(8,128)(2,1)} %get-tuple-element.60.refs_1_.refs_0_, bf16[4,2048,1024]{2,1,0:T(8,128)(2,1)} %all-gather.12.cloned.1.call-done.refs_10_.refs_1_, ...), custom_call_target="tpu_custom_call" | custom-call | flops 1 | bytes 1 | tf_op jit(solution)/shard_map/combine/pallas_call | solution.py:423
  631.6 25.4 %combine.7 = (bf16[256,2048]{1,0:T(8,128)(2,1)}, bf16[256,2048]{1,0:T(8,128)(2,1)}, bf16[256,2048]{1,0:T(8,128)(2,1)}, bf16[256,2048]{1,0:T(8,128)(2,1)}) custom-call(bf16[4,2,384,1024]{3,2,1,0:T(8,128)(2,1)} %get-tuple-element.60.refs_1_.refs_0_, bf16[4,2048,1024]{2,1,0:T(8,128)(2,1)} %all-gather.12.cloned.1.call-done.refs_10_.refs_1_, ...), custom_call_target="tpu_custom_call" | custom-call | flops 1 | bytes 1 | tf_op jit(solution)/shard_map/combine/pallas_call | solution.py:423
  664.6 6.4 convolution_convert_fusion.refs_2_
  672.5 6.2 all-to-all-start.1
  678.7 24.3 %bank_grad.4.refs_1_.refs_0_ = bf16[4,2048,1024]{2,1,0:T(8,128)(2,1)} custom-call(bf16[4,2,384,2048]{3,2,1,0:T(8,128)(2,1)} %get-tuple-element.56.refs_1_.refs_0_, bf16[4,2,384,1024]{3,2,1,0:T(8,128)(2,1)} %get-tuple-element.61.refs_0_.refs_1_, bf16[256,2048]{1,0:T(8,128)(2,1)} %copy-done.83), custom_call_target="tpu_custom_call" | custom-call | flops 1 | bytes 1 | tf_op jit(solution)/shard_map/bank_grad/pallas_call | solution.py:423
  706.7 5.6 all-to-all-start.2
  715.8 2.9 gather_fusion.2
  723.9 33.3 %attend_back.1 = (bf16[8,2,128,768]{3,2,1,0:T(8,128)(2,1)S(1)}, f32[4,2,128]{2,1,0:T(2,128)S(1)}) custom-call(bf16[8,2,128,768]{3,2,1,0:T(8,128)(2,1)S(1)} %copy-done.3, bf16[8,2,128,256]{3,2,1,0:T(8,128)(2,1)S(1)} %copy-done.11, f32[1024,128]{1,0:T(8,128)S(1)} %copy-done.10, f32[1024,128]{1,0:T(8,128)S(1)} %copy-done.8, s32[2,1,1024]{2,1,0:T(1,128)S(1)} %bitcast.206, ...), custom_call_target="tpu_custom_call" | custom-call | flops 1 | bytes 1 | tf_op jit(solution)/shard_map/attend_back/pallas_call | solution.py:293
  759.4 12.6 %part_grads.1 = (bf16[256,2048]{1,0:T(8,128)(2,1)}, bf16[256,2048]{1,0:T(8,128)(2,1)}, bf16[256,2048]{1,0:T(8,128)(2,1)}, bf16[256,2048]{1,0:T(8,128)(2,1)}, bf1...) custom-call(bf16[2048,768]{1,0:T(8,128)(2,1)} %bitcast.203, ...), custom_call_target="tpu_custom_call" | custom-call | flops 1 | bytes 1 | tf_op jit(solution)/shard_map/part_grads/pallas_call | solution.py:423
  773.2 2.7 fusion.12
  783.5 20.8 %proj_grads.1 = (bf16[512,1152]{1,0:T(8,128)(2,1)}, bf16[512,1152]{1,0:T(8,128)(2,1)}, bf16[512,1152]{1,0:T(8,128)(2,1)}, bf16[512,1152]{1,0:T(8,128)(2,1)}) custom-call(s32[4]{0:T(128)} %fusion.41.refs_0_, s32[8]{0:T(128)} %copy-done.117, bf16[2048,2048]{1,0:T(8,128)(2,1)} %bitcast.207, bf16[2048,768]{1,0:T(8,128)(2,1)} %bitcast.204, ...), custom_call_target="tpu_custom_call" | custom-call | flops 1 | bytes 1 | tf_op jit(solution)/shard_map/proj_grads/pallas_call | solution.py:384
  808.7 2.6 add_convert_fusion.2
  812.0 3.0 add_convert_fusion.6
  819.4 24.1 %bank_grad.5.refs_1_.refs_0_ = bf16[4,2048,1024]{2,1,0:T(8,128)(2,1)} custom-call(bf16[4,2,384,2048]{3,2,1,0:T(8,128)(2,1)} %get-tuple-element.56.refs_1_.refs_0_, bf16[4,2,384,1024]{3,2,1,0:T(8,128)(2,1)} %get-tuple-element.62.refs_1_, bf16[2,128,2048]{2,1,0:T(8,128)(2,1)} %after.101.refs_1_.refs_2_.refs_4_), custom_call_target="tpu_custom_call" | custom-call | flops 1 | bytes 1 | tf_op jit(solution)/shard_map/bank_grad/pallas_call | solution.py:423
  843.4 21.9 %collective-permute-done.43.refs_2_.refs_0_ = bf16[512,1152]{1,0:T(8,128)(2,1)} collective-permute-done((bf16[512,1152]{1,0:T(8,128)(2,1)}, bf16[512,1152]{1,0:T(8,128)(2,1)}, u32[]{:S(2)}, u32[]{:S(2)}) %collective-permute-start.43) | collective-permute-done | bytes 1179680 | tf_op jit(solution)/shard_map/ppermute | solution.py:31
  866.7 3.1 add_convert_fusion.refs_5_.refs_0_
  871.1 4.3 all-to-all-start.3
  877.5 2.7 add_convert_fusion.5
  882.3 7.4 convert_element_type.430.refs_1_
  889.8 22.7 %collective-permute-done.49.refs_2_.refs_0_ = bf16[2,128,2048]{2,1,0:T(8,128)(2,1)} collective-permute-done((bf16[2,128,2048]{2,1,0:T(8,128)(2,1)}, bf16[2,128,2048]{2,1,0:T(8,128)(2,1)}, u32[]{:S(2)}, u32[]{:S(2)}) %collective-permute-start.49) | collective-permute-done | bytes 1048608 | tf_op jit(solution)/shard_map/ppermute | solution.py:31
  912.4 8.1 collective-permute-done.48.refs_0_
  920.6 5.5 all-to-all-done.3.refs_4_.refs_0_
  928.8 2.7 add_convert_fusion.3
  933.6 3.6 add_convert_fusion.4
  942.2 3.7 reshape.570
  948.8 5.7 fusion.63
  960.4 2.3 reshape.572
  962.6 6.6 convert_element_type.438.refs_1_
  969.3 6.4 collective-permute-done.54.refs_3_.refs_0_
  975.7 2.6 collective-permute-done.53.refs_2_.refs_0_
  991.3 2.9 fusion.19
  994.8 11.4 %reduce-scatter.8.cloned.1.call-done = bf16[4,512,1024]{2,1,0:T(8,128)(2,1)} async-done(((bf16[4,2048,1024]{2,1,0:T(8,128)(2,1)}), bf16[4,512,1024]{2,1,0:T(8,128)(2,1)}) %reduce-scatter.8.cloned.1.call-update) | async-done | bytes 4194320 | tf_op jit(solution)/shard_map/reduce_scatter | solution.py:795
  1006.2 6.8 convert_element_type.467
  (529 shorter events, 171.5 us)
Async XLA Ops:
  7.2 124.4 %all-gather.6.cloned.1.call-start = ((), (), s32[]{:S(2)}) async-start(), calls=%async_computation.7 | async-start | bytes 4587520 | tf_op jit(solution)/shard_map/all_gather | solution.py:635
  11.1 180.4 %all-gather.8.cloned.1.call-start = ((), (), s32[]{:S(2)}) async-start(), calls=%async_computation.8 | async-start | bytes 10485760 | tf_op jit(solution)/shard_map/all_gather | solution.py:635
  11.8 322.8 %all-gather.10.cloned.1.call-start = ((), (), s32[]{:S(2)}) async-start(), calls=%async_computation.9 | async-start | bytes 20971520 | tf_op jit(solution)/shard_map/all_gather | solution.py:635
  12.5 393.3 %all-gather.12.cloned.1.call-start = ((), (), s32[]{:S(2)}) async-start(), calls=%async_computation.10 | async-start | bytes 20971520 | tf_op jit(solution)/shard_map/all_gather | solution.py:635
  13.2 432.4 %all-gather.14.cloned.1.call-start = ((), (), s32[]{:S(2)}) async-start(), calls=%async_computation.11 | async-start | bytes 20971520 | tf_op jit(solution)/shard_map/all_gather | solution.py:635
  13.7 868.6 %reduce-scatter.4.cloned.1.call-start = ((), (), s32[]{:S(2)}) async-start(), calls=%async_computation.12 | async-start | bytes 20971520 | tf_op jit(solution)/shard_map/reduce_scatter | solution.py:795
  16.7 31.7 %collective-permute-start = (bf16[2,128,2176]{2,1,0:T(8,128)(2,1)}, bf16[2,128,2176]{2,1,0:T(8,128)(2,1)}, u32[]{:S(2)}, u32[]{:S(2)}) collective-permute-start(bf16[2,128,2176]{2,1,0:T(8,128)(2,1)} %pad.12), channel_id=1, source_target_pairs={{0,1},{1,0},{2,3},{3,2},{4,5},{5,4},{6,7},{7,6},{8,9},{9,8},{10,11... | collective-permute-start | bytes 3342344 | tf_op jit(solution)/shard_map/ppermute | solution.py:31
  19.6 28.2 %collective-permute-start.1 = (bf16[2,128,2176]{2,1,0:T(8,128)(2,1)}, bf16[2,128,2176]{2,1,0:T(8,128)(2,1)}, u32[]{:S(2)}, u32[]{:S(2)}) collective-permute-start(bf16[2,128,2176]{2,1,0:T(8,128)(2,1)} %pad.12), channel_id=1, source_target_pairs={{0,2},{1,3},{2,4},{3,5},{4,6},{5,7},{6,0},{7,1},{8,10},{9,11},{10,... | collective-permute-start | bytes 3342344 | tf_op jit(solution)/shard_map/ppermute | solution.py:31
  47.9 29.1 %collective-permute-start.2 = (bf16[2,128,2176]{2,1,0:T(8,128)(2,1)}, bf16[2,128,2176]{2,1,0:T(8,128)(2,1)S(1)}, u32[]{:S(2)}, u32[]{:S(2)}) collective-permute-start(bf16[2,128,2176]{2,1,0:T(8,128)(2,1)} %collective-permute-done.1), channel_id=1, source_target_pairs={{0,1},{1,0},{2,3},{3,2},{4,5},{5,4},{6,7},{7,6},{8,9},{9,8},{10,11... | collective-permute-start | bytes 3342344 | tf_op jit(solution)/shard_map/ppermute | solution.py:31
  48.4 27.2 %collective-permute-start.3 = (bf16[2,128,2176]{2,1,0:T(8,128)(2,1)}, bf16[2,128,2176]{2,1,0:T(8,128)(2,1)S(1)}, u32[]{:S(2)}, u32[]{:S(2)}) collective-permute-start(bf16[2,128,2176]{2,1,0:T(8,128)(2,1)} %collective-permute-done.1), channel_id=1, source_target_pairs={{0,2},{1,3},{2,4},{3,5},{4,6},{5,7},{6,0},{7,1},{8,10},{9,11},{10,... | collective-permute-start | bytes 3342344 | tf_op jit(solution)/shard_map/ppermute | solution.py:31
  75.5 27.9 %collective-permute-start.4 = (bf16[2,128,2176]{2,1,0:T(8,128)(2,1)S(1)}, bf16[2,128,2176]{2,1,0:T(8,128)(2,1)S(1)}, u32[]{:S(2)}, u32[]{:S(2)}) collective-permute-start(bf16[2,128,2176]{2,1,0:T(8,128)(2,1)S(1)} %collective-permute-done.3), channel_id=1, source_target_pairs={{0,1},{1,0},{2,3},{3,2},{4,5},{5,4},{6,7},{7,6},{8,9},{9,8},{10,11... | collective-permute-start | bytes 3342344 | tf_op jit(solution)/shard_map/ppermute | solution.py:31
  76.8 25.7 %collective-permute-start.5 = (bf16[2,128,2176]{2,1,0:T(8,128)(2,1)S(1)}, bf16[2,128,2176]{2,1,0:T(8,128)(2,1)S(1)}, u32[]{:S(2)}, u32[]{:S(2)}) collective-permute-start(bf16[2,128,2176]{2,1,0:T(8,128)(2,1)S(1)} %collective-permute-done.3), channel_id=1, source_target_pairs={{0,2},{1,3},{2,4},{3,5},{4,6},{5,7},{6,0},{7,1},{8,10},{9,11},{10,... | collective-permute-start | bytes 3342344 | tf_op jit(solution)/shard_map/ppermute | solution.py:31
  102.5 22.8 %collective-permute-start.6 = (bf16[2,128,2176]{2,1,0:T(8,128)(2,1)S(1)}, bf16[2,128,2176]{2,1,0:T(8,128)(2,1)S(1)}, u32[]{:S(2)}, u32[]{:S(2)}) collective-permute-start(bf16[2,128,2176]{2,1,0:T(8,128)(2,1)S(1)} %collective-permute-done.5), channel_id=1, source_target_pairs={{0,1},{1,0},{2,3},{3,2},{4,5},{5,4},{6,7},{7,6},{8,9},{9,8},{10,11... | collective-permute-start | bytes 3342344 | tf_op jit(solution)/shard_map/ppermute | solution.py:31
  199.2 23.1 %collective-permute-start.7 = (bf16[2,128,2048]{2,1,0:T(8,128)(2,1)S(1)}, bf16[2,128,2048]{2,1,0:T(8,128)(2,1)S(1)}, u32[]{:S(2)}, u32[]{:S(2)}) collective-permute-start(bf16[2,128,2048]{2,1,0:T(8,128)(2,1)S(1)} %bitcast.234), channel_id=1, source_target_pairs={{0,1},{1,0},{2,3},{3,2},{4,5},{5,4},{6,7},{7,6},{8,9},{9,8},{10,11... | collective-permute-start | bytes 3145736 | tf_op jit(solution)/shard_map/ppermute | solution.py:31
  200.7 24.8 %collective-permute-start.8 = (bf16[2,128,2048]{2,1,0:T(8,128)(2,1)S(1)}, bf16[2,128,2048]{2,1,0:T(8,128)(2,1)S(1)}, u32[]{:S(2)}, u32[]{:S(2)}) collective-permute-start(bf16[2,128,2048]{2,1,0:T(8,128)(2,1)S(1)} %bitcast.235), channel_id=1, source_target_pairs={{0,2},{1,3},{2,4},{3,5},{4,6},{5,7},{6,0},{7,1},{8,10},{9,11},{10,... | collective-permute-start | bytes 3145736 | tf_op jit(solution)/shard_map/ppermute | solution.py:31
  226.5 24.1 %collective-permute-start.10 = (bf16[2,128,2048]{2,1,0:T(8,128)(2,1)}, bf16[2,128,2048]{2,1,0:T(8,128)(2,1)S(1)}, u32[]{:S(2)}, u32[]{:S(2)}) collective-permute-start(bf16[2,128,2048]{2,1,0:T(8,128)(2,1)} %after.65), channel_id=1, source_target_pairs={{0,2},{1,3},{2,4},{3,5},{4,6},{5,7},{6,0},{7,1},{8,10},{9,11},{10,... | collective-permute-start | bytes 3145736 | tf_op jit(solution)/shard_map/ppermute | solution.py:31
  226.5 24.1 %collective-permute-start.9 = (bf16[2,128,2048]{2,1,0:T(8,128)(2,1)}, bf16[2,128,2048]{2,1,0:T(8,128)(2,1)S(1)}, u32[]{:S(2)}, u32[]{:S(2)}) collective-permute-start(bf16[2,128,2048]{2,1,0:T(8,128)(2,1)} %after.65), channel_id=1, source_target_pairs={{0,1},{1,0},{2,3},{3,2},{4,5},{5,4},{6,7},{7,6},{8,9},{9,8},{10,11... | collective-permute-start | bytes 3145736 | tf_op jit(solution)/shard_map/ppermute | solution.py:31
  252.5 21.4 %collective-permute-start.11 = (bf16[2,128,2048]{2,1,0:T(8,128)(2,1)}, bf16[2,128,2048]{2,1,0:T(8,128)(2,1)S(1)}, u32[]{:S(2)}, u32[]{:S(2)}) collective-permute-start(bf16[2,128,2048]{2,1,0:T(8,128)(2,1)} %after.67), channel_id=1, source_target_pairs={{0,1},{1,0},{2,3},{3,2},{4,5},{5,4},{6,7},{7,6},{8,9},{9,8},{10,11... | collective-permute-start | bytes 3145736 | tf_op jit(solution)/shard_map/ppermute | solution.py:31
  252.7 23.0 %collective-permute-start.12 = (bf16[2,128,2048]{2,1,0:T(8,128)(2,1)}, bf16[2,128,2048]{2,1,0:T(8,128)(2,1)S(1)}, u32[]{:S(2)}, u32[]{:S(2)}) collective-permute-start(bf16[2,128,2048]{2,1,0:T(8,128)(2,1)} %after.67), channel_id=1, source_target_pairs={{0,2},{1,3},{2,4},{3,5},{4,6},{5,7},{6,0},{7,1},{8,10},{9,11},{10,... | collective-permute-start | bytes 3145736 | tf_op jit(solution)/shard_map/ppermute | solution.py:31
  276.8 22.2 %collective-permute-start.13 = (bf16[2,128,2048]{2,1,0:T(8,128)(2,1)}, bf16[2,128,2048]{2,1,0:T(8,128)(2,1)S(1)}, u32[]{:S(2)}, u32[]{:S(2)}) collective-permute-start(bf16[2,128,2048]{2,1,0:T(8,128)(2,1)} %after.69), channel_id=1, source_target_pairs={{0,1},{1,0},{2,3},{3,2},{4,5},{5,4},{6,7},{7,6},{8,9},{9,8},{10,11... | collective-permute-start | bytes 3145736 | tf_op jit(solution)/shard_map/ppermute | solution.py:31
  300.0 20.1 %collective-permute-start.14 = (bf16[2,128,2048]{2,1,0:T(8,128)(2,1)}, bf16[2,128,2048]{2,1,0:T(8,128)(2,1)S(1)}, u32[]{:S(2)}, u32[]{:S(2)}) collective-permute-start(bf16[2,128,2048]{2,1,0:T(8,128)(2,1)} %after.70), channel_id=1, source_target_pairs={{0,1},{1,0},{2,3},{3,2},{4,5},{5,4},{6,7},{7,6},{8,9},{9,8},{10,11... | collective-permute-start | bytes 3145736 | tf_op jit(solution)/shard_map/ppermute | solution.py:31
  301.7 18.8 %collective-permute-start.15 = (bf16[2,128,2048]{2,1,0:T(8,128)(2,1)}, bf16[2,128,2048]{2,1,0:T(8,128)(2,1)S(1)}, u32[]{:S(2)}, u32[]{:S(2)}) collective-permute-start(bf16[2,128,2048]{2,1,0:T(8,128)(2,1)} %after.70), channel_id=1, source_target_pairs={{0,2},{1,3},{2,4},{3,5},{4,6},{5,7},{6,0},{7,1},{8,10},{9,11},{10,... | collective-permute-start | bytes 3145736 | tf_op jit(solution)/shard_map/ppermute | solution.py:31
  323.2 33.7 %collective-permute-start.16 = (bf16[2,128,2048]{2,1,0:T(8,128)(2,1)}, bf16[2,128,2048]{2,1,0:T(8,128)(2,1)S(1)}, u32[]{:S(2)}, u32[]{:S(2)}) collective-permute-start(bf16[2,128,2048]{2,1,0:T(8,128)(2,1)} %after.72.refs_12_), channel_id=1, source_target_pairs={{0,1},{1,0},{2,3},{3,2},{4,5},{5,4},{6,7},{7,6},{8,9},{9,8},{10,11... | collective-permute-start | bytes 3145736 | tf_op jit(solution)/shard_map/ppermute | solution.py:31
  324.9 31.9 %collective-permute-start.17 = (bf16[2,128,2048]{2,1,0:T(8,128)(2,1)}, bf16[2,128,2048]{2,1,0:T(8,128)(2,1)S(1)}, u32[]{:S(2)}, u32[]{:S(2)}) collective-permute-start(bf16[2,128,2048]{2,1,0:T(8,128)(2,1)} %after.72.refs_12_), channel_id=1, source_target_pairs={{0,2},{1,3},{2,4},{3,5},{4,6},{5,7},{6,0},{7,1},{8,10},{9,11},{10,... | collective-permute-start | bytes 3145736 | tf_op jit(solution)/shard_map/ppermute | solution.py:31
  358.2 20.6 %collective-permute-start.18 = (bf16[2,128,2048]{2,1,0:T(8,128)(2,1)}, bf16[2,128,2048]{2,1,0:T(8,128)(2,1)S(1)}, u32[]{:S(2)}, u32[]{:S(2)}) collective-permute-start(bf16[2,128,2048]{2,1,0:T(8,128)(2,1)} %after.74.refs_14_), channel_id=1, source_target_pairs={{0,1},{1,0},{2,3},{3,2},{4,5},{5,4},{6,7},{7,6},{8,9},{9,8},{10,11... | collective-permute-start | bytes 3145736 | tf_op jit(solution)/shard_map/ppermute | solution.py:31
  358.7 20.2 %collective-permute-start.19 = (bf16[2,128,2048]{2,1,0:T(8,128)(2,1)}, bf16[2,128,2048]{2,1,0:T(8,128)(2,1)S(1)}, u32[]{:S(2)}, u32[]{:S(2)}) collective-permute-start(bf16[2,128,2048]{2,1,0:T(8,128)(2,1)} %after.74.refs_14_), channel_id=1, source_target_pairs={{0,2},{1,3},{2,4},{3,5},{4,6},{5,7},{6,0},{7,1},{8,10},{9,11},{10,... | collective-permute-start | bytes 3145736 | tf_op jit(solution)/shard_map/ppermute | solution.py:31
  380.2 22.2 %collective-permute-start.20 = (bf16[2,128,2048]{2,1,0:T(8,128)(2,1)}, bf16[2,128,2048]{2,1,0:T(8,128)(2,1)S(1)}, u32[]{:S(2)}, u32[]{:S(2)}) collective-permute-start(bf16[2,128,2048]{2,1,0:T(8,128)(2,1)} %after.76), channel_id=1, source_target_pairs={{0,1},{1,0},{2,3},{3,2},{4,5},{5,4},{6,7},{7,6},{8,9},{9,8},{10,11... | collective-permute-start | bytes 3145736 | tf_op jit(solution)/shard_map/ppermute | solution.py:31
  403.4 36.6 %collective-permute-start.21 = (bf16[2048,256]{1,0:T(8,128)(2,1)}, bf16[2048,256]{1,0:T(8,128)(2,1)S(1)}, u32[]{:S(2)}, u32[]{:S(2)}) collective-permute-start(bf16[2048,256]{1,0:T(8,128)(2,1)} %after.77.refs_6_), channel_id=1, source_target_pairs={{0,1},{1,0},{2,3},{3,2},{4,5},{5,4},{6,7},{7,6},{8,9},{9,8},{10,11... | collective-permute-start | bytes 3145736 | tf_op jit(solution)/shard_map/ppermute | solution.py:31
  404.5 35.5 %collective-permute-start.22 = (bf16[2048,256]{1,0:T(8,128)(2,1)}, bf16[2048,256]{1,0:T(8,128)(2,1)S(1)}, u32[]{:S(2)}, u32[]{:S(2)}) collective-permute-start(bf16[2048,256]{1,0:T(8,128)(2,1)} %after.77.refs_6_), channel_id=1, source_target_pairs={{0,2},{1,3},{2,4},{3,5},{4,6},{5,7},{6,0},{7,1},{8,10},{9,11},{10,... | collective-permute-start | bytes 3145736 | tf_op jit(solution)/shard_map/ppermute | solution.py:31
  441.3 35.9 %collective-permute-start.23 = (bf16[2048,256]{1,0:T(8,128)(2,1)}, bf16[2048,256]{1,0:T(8,128)(2,1)S(1)}, u32[]{:S(2)}, u32[]{:S(2)}) collective-permute-start(bf16[2048,256]{1,0:T(8,128)(2,1)} %after.79.refs_5_.refs_8_), channel_id=1, source_target_pairs={{0,1},{1,0},{2,3},{3,2},{4,5},{5,4},{6,7},{7,6},{8,9},{9,8},{10,11... | collective-permute-start | bytes 3145736 | tf_op jit(solution)/shard_map/ppermute | solution.py:31
  441.4 35.8 %collective-permute-start.24 = (bf16[2048,256]{1,0:T(8,128)(2,1)}, bf16[2048,256]{1,0:T(8,128)(2,1)S(1)}, u32[]{:S(2)}, u32[]{:S(2)}) collective-permute-start(bf16[2048,256]{1,0:T(8,128)(2,1)} %after.79.refs_5_.refs_8_), channel_id=1, source_target_pairs={{0,2},{1,3},{2,4},{3,5},{4,6},{5,7},{6,0},{7,1},{8,10},{9,11},{10,... | collective-permute-start | bytes 3145736 | tf_op jit(solution)/shard_map/ppermute | solution.py:31
  481.4 34.4 %collective-permute-start.25 = (bf16[2048,256]{1,0:T(8,128)(2,1)}, bf16[2048,256]{1,0:T(8,128)(2,1)S(1)}, u32[]{:S(2)}, u32[]{:S(2)}) collective-permute-start(bf16[2048,256]{1,0:T(8,128)(2,1)} %after.81.refs_8_.refs_10_), channel_id=1, source_target_pairs={{0,1},{1,0},{2,3},{3,2},{4,5},{5,4},{6,7},{7,6},{8,9},{9,8},{10,11... | collective-permute-start | bytes 3145736 | tf_op jit(solution)/shard_map/ppermute | solution.py:31
  483.1 32.7 %collective-permute-start.26 = (bf16[2048,256]{1,0:T(8,128)(2,1)}, bf16[2048,256]{1,0:T(8,128)(2,1)}, u32[]{:S(2)}, u32[]{:S(2)}) collective-permute-start(bf16[2048,256]{1,0:T(8,128)(2,1)} %after.81.refs_8_.refs_10_), channel_id=1, source_target_pairs={{0,2},{1,3},{2,4},{3,5},{4,6},{5,7},{6,0},{7,1},{8,10},{9,11},{10,... | collective-permute-start | bytes 3145736 | tf_op jit(solution)/shard_map/ppermute | solution.py:31
  515.3 33.8 %collective-permute-start.28 = (bf16[2,128,2048]{2,1,0:T(8,128)(2,1)}, bf16[2,128,2048]{2,1,0:T(8,128)(2,1)S(1)}, u32[]{:S(2)}, u32[]{:S(2)}) collective-permute-start(bf16[2,128,2048]{2,1,0:T(8,128)(2,1)} %bitcast.289), channel_id=1, source_target_pairs={{0,1},{1,0},{2,3},{3,2},{4,5},{5,4},{6,7},{7,6},{8,9},{9,8},{10,11... | collective-permute-start | bytes 3145736 | tf_op jit(solution)/shard_map/ppermute | solution.py:31
  552.3 26.3 %collective-permute-start.29 = (bf16[2,128,2048]{2,1,0:T(8,128)(2,1)S(1)}, bf16[2,128,2048]{2,1,0:T(8,128)(2,1)S(1)}, u32[]{:S(2)}, u32[]{:S(2)}) collective-permute-start(bf16[2,128,2048]{2,1,0:T(8,128)(2,1)S(1)} %fusion.16), channel_id=1, source_target_pairs={{0,2},{1,3},{2,4},{3,5},{4,6},{5,7},{6,0},{7,1},{8,10},{9,11},{10,... | collective-permute-start | bytes 3145736 | tf_op jit(solution)/shard_map/ppermute | solution.py:31
  552.5 26.1 %collective-permute-start.27 = (bf16[2,128,2048]{2,1,0:T(8,128)(2,1)S(1)}, bf16[2,128,2048]{2,1,0:T(8,128)(2,1)S(1)}, u32[]{:S(2)}, u32[]{:S(2)}) collective-permute-start(bf16[2,128,2048]{2,1,0:T(8,128)(2,1)S(1)} %bitcast.288), channel_id=1, source_target_pairs={{0,1},{1,0},{2,3},{3,2},{4,5},{5,4},{6,7},{7,6},{8,9},{9,8},{10,11... | collective-permute-start | bytes 3145736 | tf_op jit(solution)/shard_map/ppermute | solution.py:31
  554.0 41.1 %collective-permute-start.30 = (bf16[2048,256]{1,0:T(8,128)(2,1)}, bf16[2048,256]{1,0:T(8,128)(2,1)S(1)}, u32[]{:S(2)}, u32[]{:S(2)}) collective-permute-start(bf16[2048,256]{1,0:T(8,128)(2,1)} %after.83.refs_9_.refs_12_), channel_id=1, source_target_pairs={{0,1},{1,0},{2,3},{3,2},{4,5},{5,4},{6,7},{7,6},{8,9},{9,8},{10,11... | collective-permute-start | bytes 3145736 | tf_op jit(solution)/shard_map/ppermute | solution.py:31
  596.2 30.5 %collective-permute-start.32 = (bf16[2,128,2048]{2,1,0:T(8,128)(2,1)}, bf16[2,128,2048]{2,1,0:T(8,128)(2,1)S(1)}, u32[]{:S(2)}, u32[]{:S(2)}) collective-permute-start(bf16[2,128,2048]{2,1,0:T(8,128)(2,1)} %bitcast.287), channel_id=1, source_target_pairs={{0,1},{1,0},{2,3},{3,2},{4,5},{5,4},{6,7},{7,6},{8,9},{9,8},{10,11... | collective-permute-start | bytes 3145736 | tf_op jit(solution)/shard_map/ppermute | solution.py:31
  599.4 27.2 %collective-permute-start.33 = (bf16[2,128,2048]{2,1,0:T(8,128)(2,1)S(1)}, bf16[2,128,2048]{2,1,0:T(8,128)(2,1)S(1)}, u32[]{:S(2)}, u32[]{:S(2)}) collective-permute-start(bf16[2,128,2048]{2,1,0:T(8,128)(2,1)S(1)} %add_convert_fusion.8), channel_id=1, source_target_pairs={{0,2},{1,3},{2,4},{3,5},{4,6},{5,7},{6,0},{7,1},{8,10},{9,11},{10,... | collective-permute-start | bytes 3145736 | tf_op jit(solution)/shard_map/ppermute | solution.py:31
  628.0 29.0 %collective-permute-start.31 = (bf16[2,128,2048]{2,1,0:T(8,128)(2,1)}, bf16[2,128,2048]{2,1,0:T(8,128)(2,1)S(1)}, u32[]{:S(2)}, u32[]{:S(2)}) collective-permute-start(bf16[2,128,2048]{2,1,0:T(8,128)(2,1)} %bitcast.286), channel_id=1, source_target_pairs={{0,1},{1,0},{2,3},{3,2},{4,5},{5,4},{6,7},{7,6},{8,9},{9,8},{10,11... | collective-permute-start | bytes 3145736 | tf_op jit(solution)/shard_map/ppermute | solution.py:31
  631.6 25.5 %collective-permute-start.34 = (bf16[2,128,2048]{2,1,0:T(8,128)(2,1)S(1)}, bf16[2,128,2048]{2,1,0:T(8,128)(2,1)S(1)}, u32[]{:S(2)}, u32[]{:S(2)}) collective-permute-start(bf16[2,128,2048]{2,1,0:T(8,128)(2,1)S(1)} %add_convert_fusion.7), channel_id=1, source_target_pairs={{0,2},{1,3},{2,4},{3,5},{4,6},{5,7},{6,0},{7,1},{8,10},{9,11},{10,... | collective-permute-start | bytes 3145736 | tf_op jit(solution)/shard_map/ppermute | solution.py:31
  672.5 31.5 %all-to-all-start.1 = ((bf16[8,2,128,256]{3,2,1,0:T(8,128)(2,1)}), bf16[8,2,128,256]{3,2,1,0:T(8,128)(2,1)}, u32[]{:S(2)}, u32[]{:S(2)}) async-start(bf16[8,2,128,256]{3,2,1,0:T(8,128)(2,1)} %bitcast.201), calls=%async_computation.1 | async-start | bytes 2097152 | tf_op jit(solution)/shard_map/all_to_all | solution.py:809
  678.7 284.0 %reduce-scatter.6.cloned.1.call-start = ((), (), s32[]{:S(2)}) async-start(), calls=%async_computation.13 | async-start | bytes 20971520 | tf_op jit(solution)/shard_map/reduce_scatter | solution.py:795
  706.7 65.3 %all-to-all-start.2 = ((bf16[8,2,128,256]{3,2,1,0:T(8,128)(2,1)}), bf16[8,2,128,256]{3,2,1,0:T(8,128)(2,1)}, u32[]{:S(2)}, u32[]{:S(2)}) async-start(bf16[8,2,128,256]{3,2,1,0:T(8,128)(2,1)} %bitcast.200), calls=%async_computation.2 | async-start | bytes 2097152 | tf_op jit(solution)/shard_map/all_to_all | solution.py:809
  712.3 293.8 %reduce-scatter.8.cloned.1.call-start = ((), (), s32[]{:S(2)}) async-start(), calls=%async_computation.14 | async-start | bytes 20971520 | tf_op jit(solution)/shard_map/reduce_scatter | solution.py:795
  712.4 59.6 %collective-permute-start.35 = (bf16[2,128,2048]{2,1,0:T(8,128)(2,1)}, bf16[2,128,2048]{2,1,0:T(8,128)(2,1)}, u32[]{:S(2)}, u32[]{:S(2)}) collective-permute-start(bf16[2,128,2048]{2,1,0:T(8,128)(2,1)} %after.94), channel_id=1, source_target_pairs={{0,1},{1,0},{2,3},{3,2},{4,5},{5,4},{6,7},{7,6},{8,9},{9,8},{10,11... | collective-permute-start | bytes 3145736 | tf_op jit(solution)/shard_map/ppermute | solution.py:31
  718.7 85.6 %collective-permute-start.38 = (bf16[2,128,2048]{2,1,0:T(8,128)(2,1)}, bf16[2,128,2048]{2,1,0:T(8,128)(2,1)}, u32[]{:S(2)}, u32[]{:S(2)}) collective-permute-start(bf16[2,128,2048]{2,1,0:T(8,128)(2,1)} %bitcast.284), channel_id=1, source_target_pairs={{0,1},{1,0},{2,3},{3,2},{4,5},{5,4},{6,7},{7,6},{8,9},{9,8},{10,11... | collective-permute-start | bytes 3145736 | tf_op jit(solution)/shard_map/ppermute | solution.py:31
  775.9 28.4 %collective-permute-start.37 = (bf16[2,128,2048]{2,1,0:T(8,128)(2,1)}, bf16[2,128,2048]{2,1,0:T(8,128)(2,1)S(1)}, u32[]{:S(2)}, u32[]{:S(2)}) collective-permute-start(bf16[2,128,2048]{2,1,0:T(8,128)(2,1)} %fusion.12), channel_id=1, source_target_pairs={{0,2},{1,3},{2,4},{3,5},{4,6},{5,7},{6,0},{7,1},{8,10},{9,11},{10,... | collective-permute-start | bytes 3145736 | tf_op jit(solution)/shard_map/ppermute | solution.py:31
  777.5 26.8 %collective-permute-start.36 = (bf16[2,128,2048]{2,1,0:T(8,128)(2,1)}, bf16[2,128,2048]{2,1,0:T(8,128)(2,1)S(1)}, u32[]{:S(2)}, u32[]{:S(2)}) collective-permute-start(bf16[2,128,2048]{2,1,0:T(8,128)(2,1)} %after.97), channel_id=1, source_target_pairs={{0,1},{1,0},{2,3},{3,2},{4,5},{5,4},{6,7},{7,6},{8,9},{9,8},{10,11... | collective-permute-start | bytes 3145736 | tf_op jit(solution)/shard_map/ppermute | solution.py:31
  780.8 23.5 %collective-permute-start.40 = (f32[2,128]{1,0:T(2,128)S(1)}, f32[2,128]{1,0:T(2,128)S(1)}, u32[]{:S(2)}, u32[]{:S(2)}) collective-permute-start(f32[2,128]{1,0:T(2,128)S(1)} %add.371), channel_id=1, source_target_pairs={{0,16},{8,24},{16,0},{24,8},{1,17},{9,25},{17,1},{25,9},{2,18},{10... | collective-permute-start | bytes 3080 | tf_op jit(solution)/shard_map/ppermute | solution.py:846
  805.6 64.1 %collective-permute-start.46 = (bf16[2,128,2048]{2,1,0:T(8,128)(2,1)}, bf16[2,128,2048]{2,1,0:T(8,128)(2,1)S(1)}, u32[]{:S(2)}, u32[]{:S(2)}) collective-permute-start(bf16[2,128,2048]{2,1,0:T(8,128)(2,1)} %bitcast.77), channel_id=1, source_target_pairs={{0,1},{1,0},{2,3},{3,2},{4,5},{5,4},{6,7},{7,6},{8,9},{9,8},{10,11... | collective-permute-start | bytes 3145736 | tf_op jit(solution)/shard_map/ppermute | solution.py:31
  806.4 63.4 %collective-permute-start.47 = (bf16[2,128,2048]{2,1,0:T(8,128)(2,1)}, bf16[2,128,2048]{2,1,0:T(8,128)(2,1)S(1)}, u32[]{:S(2)}, u32[]{:S(2)}) collective-permute-start(bf16[2,128,2048]{2,1,0:T(8,128)(2,1)} %bitcast.285), channel_id=1, source_target_pairs={{0,1},{1,0},{2,3},{3,2},{4,5},{5,4},{6,7},{7,6},{8,9},{9,8},{10,11... | collective-permute-start | bytes 3145736 | tf_op jit(solution)/shard_map/ppermute | solution.py:31
  811.2 54.1 %collective-permute-start.43 = (bf16[512,1152]{1,0:T(8,128)(2,1)}, bf16[512,1152]{1,0:T(8,128)(2,1)}, u32[]{:S(2)}, u32[]{:S(2)}) collective-permute-start(bf16[512,1152]{1,0:T(8,128)(2,1)} %add_convert_fusion.2), channel_id=1, source_target_pairs={{0,16},{8,24},{16,0},{24,8},{1,17},{9,25},{17,1},{25,9},{2,18},{10... | collective-permute-start | bytes 3538952 | tf_op jit(solution)/shard_map/ppermute | solution.py:31
  815.0 54.8 %collective-permute-start.44 = (bf16[2,128,2048]{2,1,0:T(8,128)(2,1)}, bf16[2,128,2048]{2,1,0:T(8,128)(2,1)}, u32[]{:S(2)}, u32[]{:S(2)}) collective-permute-start(bf16[2,128,2048]{2,1,0:T(8,128)(2,1)} %add_convert_fusion.6), channel_id=1, source_target_pairs={{0,2},{1,3},{2,4},{3,5},{4,6},{5,7},{6,0},{7,1},{8,10},{9,11},{10,... | collective-permute-start | bytes 3145736 | tf_op jit(solution)/shard_map/ppermute | solution.py:31
  817.9 51.9 %collective-permute-start.45 = (bf16[2,128,2048]{2,1,0:T(8,128)(2,1)}, bf16[2,128,2048]{2,1,0:T(8,128)(2,1)}, u32[]{:S(2)}, u32[]{:S(2)}) collective-permute-start(bf16[2,128,2048]{2,1,0:T(8,128)(2,1)} %fusion.10), channel_id=1, source_target_pairs={{0,2},{1,3},{2,4},{3,5},{4,6},{5,7},{6,0},{7,1},{8,10},{9,11},{10,... | collective-permute-start | bytes 3145736 | tf_op jit(solution)/shard_map/ppermute | solution.py:31
  871.1 55.0 %all-to-all-start.3 = ((bf16[8,64,1152]{2,1,0:T(8,128)(2,1)}), bf16[8,64,1152]{2,1,0:T(8,128)(2,1)S(1)}, u32[]{:S(2)}, u32[]{:S(2)}) async-start(bf16[8,64,1152]{2,1,0:T(8,128)(2,1)} %bitcast.79), calls=%async_computation.3 | async-start | bytes 2359296 | tf_op jit(solution)/shard_map/all_to_all | solution.py:874
  875.4 37.0 %collective-permute-start.49 = (bf16[2,128,2048]{2,1,0:T(8,128)(2,1)}, bf16[2,128,2048]{2,1,0:T(8,128)(2,1)}, u32[]{:S(2)}, u32[]{:S(2)}) collective-permute-start(bf16[2,128,2048]{2,1,0:T(8,128)(2,1)} %bitcast.283), channel_id=1, source_target_pairs={{0,1},{1,0},{2,3},{3,2},{4,5},{5,4},{6,7},{7,6},{8,9},{9,8},{10,11... | collective-permute-start | bytes 3145736 | tf_op jit(solution)/shard_map/ppermute | solution.py:31
  880.3 40.3 %collective-permute-start.48 = (bf16[2,128,2048]{2,1,0:T(8,128)(2,1)}, bf16[2,128,2048]{2,1,0:T(8,128)(2,1)S(1)}, u32[]{:S(2)}, u32[]{:S(2)}) collective-permute-start(bf16[2,128,2048]{2,1,0:T(8,128)(2,1)} %add_convert_fusion.5), channel_id=1, source_target_pairs={{0,2},{1,3},{2,4},{3,5},{4,6},{5,7},{6,0},{7,1},{8,10},{9,11},{10,... | collective-permute-start | bytes 3145736 | tf_op jit(solution)/shard_map/ppermute | solution.py:31
  881.7 30.7 %collective-permute-start.50 = (f32[2,128]{1,0:T(2,128)S(1)}, f32[2,128]{1,0:T(2,128)S(1)}, u32[]{:S(2)}, u32[]{:S(2)}) collective-permute-start(f32[2,128]{1,0:T(2,128)S(1)} %add.380), channel_id=1, source_target_pairs={{0,1},{1,0},{2,3},{3,2},{4,5},{5,4},{6,7},{7,6},{8,9},{9,8},{10,11... | collective-permute-start | bytes 3080 | tf_op jit(solution)/shard_map/ppermute | solution.py:846
  931.6 37.7 %collective-permute-start.55 = (bf16[2,128,2048]{2,1,0:T(8,128)(2,1)}, bf16[2,128,2048]{2,1,0:T(8,128)(2,1)S(1)}, u32[]{:S(2)}, u32[]{:S(2)}) collective-permute-start(bf16[2,128,2048]{2,1,0:T(8,128)(2,1)} %add_convert_fusion.3), channel_id=1, source_target_pairs={{0,2},{1,3},{2,4},{3,5},{4,6},{5,7},{6,0},{7,1},{8,10},{9,11},{10,... | collective-permute-start | bytes 3145736 | tf_op jit(solution)/shard_map/ppermute | solution.py:31
  931.6 44.1 %collective-permute-start.51 = (bf16[2,128,2048]{2,1,0:T(8,128)(2,1)}, bf16[2,128,2048]{2,1,0:T(8,128)(2,1)S(1)}, u32[]{:S(2)}, u32[]{:S(2)}) collective-permute-start(bf16[2,128,2048]{2,1,0:T(8,128)(2,1)} %after.119), channel_id=1, source_target_pairs={{0,1},{1,0},{2,3},{3,2},{4,5},{5,4},{6,7},{7,6},{8,9},{9,8},{10,11... | collective-permute-start | bytes 3145736 | tf_op jit(solution)/shard_map/ppermute | solution.py:31
  932.8 45.4 %collective-permute-start.53 = (bf16[2,128,2048]{2,1,0:T(8,128)(2,1)}, bf16[2,128,2048]{2,1,0:T(8,128)(2,1)S(1)}, u32[]{:S(2)}, u32[]{:S(2)}) collective-permute-start(bf16[2,128,2048]{2,1,0:T(8,128)(2,1)} %after.121), channel_id=1, source_target_pairs={{0,1},{1,0},{2,3},{3,2},{4,5},{5,4},{6,7},{7,6},{8,9},{9,8},{10,11... | collective-permute-start | bytes 3145736 | tf_op jit(solution)/shard_map/ppermute | solution.py:31
  937.2 42.0 %collective-permute-start.52 = (bf16[2,128,2048]{2,1,0:T(8,128)(2,1)}, bf16[2,128,2048]{2,1,0:T(8,128)(2,1)}, u32[]{:S(2)}, u32[]{:S(2)}) collective-permute-start(bf16[2,128,2048]{2,1,0:T(8,128)(2,1)} %add_convert_fusion.4), channel_id=1, source_target_pairs={{0,2},{1,3},{2,4},{3,5},{4,6},{5,7},{6,0},{7,1},{8,10},{9,11},{10,... | collective-permute-start | bytes 3145736 | tf_op jit(solution)/shard_map/ppermute | solution.py:31
  942.0 33.7 %collective-permute-start.54 = (f32[2,128]{1,0:T(2,128)S(1)}, f32[2,128]{1,0:T(2,128)S(1)}, u32[]{:S(2)}, u32[]{:S(2)}) collective-permute-start(f32[2,128]{1,0:T(2,128)S(1)} %add.383), channel_id=1, source_target_pairs={{0,2},{1,3},{2,0},{3,1},{4,6},{5,7},{6,4},{7,5},{8,10},{9,11},{10,... | collective-permute-start | bytes 3080 | tf_op jit(solution)/shard_map/ppermute | solution.py:846
  (124 other events, 844.1 us)
Sparse Core Ops, SparseCore 0:
  11.2 34.1 all-gather.5
  47.0 58.2 all-gather.7
  106.9 105.9 all-gather.9
  214.2 105.9 all-gather.11
  321.6 105.9 all-gather.13
  596.3 126.8 reduce-scatter.3
  725.9 151.4 reduce-scatter.5
  880.0 126.1 reduce-scatter.7

commit v6 on v5

--- a/solution.py
+++ b/solution.py
@@ -59,7 +59,7 @@
     return moved
 
 
-def ring_gather(value, axis, work=None, then={}, tie_last=True):
+def ring_gather(value, axis, work=None, split=False):
     outer, inner = sizes(axis)
     blocks, arrived = [], []
     for a in range(outer):
@@ -69,11 +69,16 @@
         moved = row[1:]
         if a + 1 < outer:
             moved.append(shift(value, axis, outer, inner, 1, 0))
-        if work is not None and (tie_last or a + 1 < outer):
+        last = split and inner == 2 and a + 1 == outer
+        if last:
+            cut = value.shape[0] // 2
+            moved = [
+                shift(value[:cut], axis, outer, inner, 0, 1),
+                shift(blocks[-1][cut:], axis, outer, inner, 1, 0),
+            ]
+        if work is not None:
             moved = together([f(arrived) for f in work[a : a + 1] if f], *moved)
-        if a in then:
-            then[a](moved)
-        blocks += [value] + moved[: inner - 1]
+        blocks += [value] + (moved if last else moved[: inner - 1])
         value, arrived = moved[-1], moved
     return blocks
 
@@ -335,7 +340,6 @@
         ],
         [(block, pl.BlockSpec((block.shape[0], part), lambda d: (0, d)))] * blocks
         + [(jax.ShapeDtypeStruct((1, D), f32), pl.BlockSpec((1, part), lambda d: (0, d)))],
-        2 * count * width * D,
         ties=ties,
     )
     return found[:-1], found[-1][0]
@@ -413,7 +417,7 @@
     )
 
 
-def call(kernel, name, grid, ins, outs, flops, scratch=(), ties=(), aliases={}):
+def call(kernel, name, grid, ins, outs, scratch=(), ties=(), aliases={}):
     ties = [t for t in ties if t is not None]
     count = len(ins)
 
@@ -446,7 +450,11 @@
 
 def dispatch_kernel(scaled, blocks, *refs):
     value_refs, (slot_ref, weight_ref, w_ref, rows_ref, act_ref) = refs[:blocks], refs[blocks:]
-    capacity, each = rows_ref.shape[2], blocks // 2
+    capacity, half = rows_ref.shape[2], slot_ref.shape[2]
+    halves, seen = ([], []), 0
+    for ref in value_refs:
+        halves[seen // half].append(ref)
+        seen += ref.shape[0]
     for h in range(2):
         slot_row = slot_ref[0, h : h + 1, :]
         pick = picked(slot_row, capacity).astype(f32).astype(bf16)
@@ -454,7 +462,7 @@
             scale = slot_weights(slot_row, weight_ref[0, h : h + 1, :], capacity)
         for d in range(0, D, part):
             values = jnp.concatenate(
-                [ref[:, d : d + part] for ref in value_refs[h * each : (h + 1) * each]], axis=0
+                [ref[:, d : d + part] for ref in halves[h]], axis=0
             )
             taken = dot(pick, values, 1, 0)
             if scaled:
@@ -485,21 +493,22 @@
             (jax.ShapeDtypeStruct(rows_shape, bf16), of(rows_shape)),
             (jax.ShapeDtypeStruct(act_shape, f32), of(act_shape)),
         ],
-        4 * count * capacity * D * (FFE + len(values) * values[0].shape[0] // 2),
         ties=tuple(before) + tuple(ties),
         aliases={len(values) + 3 + k: k for k in range(len(before))},
     )
 
 
 def act_kernel(taken_ref, gate_ref, grad_ref, w_ref, hidden_ref, grad_gate_ref, grad_up_ref):
-    up_act = dot(taken_ref[0, 0], w_ref[0], 1, 0)
-    gate_act, grad_hidden = gate_ref[0, 0], grad_ref[0, 0]
-    gate_sig = jax.nn.sigmoid(gate_act)
-    gate_silu = gate_act * gate_sig
-    hidden_ref[0, 0] = (gate_silu * up_act).astype(bf16)
-    grad_gate = grad_hidden * up_act * gate_sig * (1.0 + gate_act * (1.0 - gate_sig))
-    grad_gate_ref[0, 0] = grad_gate.astype(bf16)
-    grad_up_ref[0, 0] = (grad_hidden * gate_silu).astype(bf16)
+    for f in range(0, FFE, 256):
+        span = slice(f, f + 256)
+        up_act = dot(taken_ref[0, 0], w_ref[0, :, span], 1, 0)
+        gate_act, grad_hidden = gate_ref[0, 0, :, span], grad_ref[0, 0, :, span]
+        gate_sig = jax.nn.sigmoid(gate_act)
+        gate_silu = gate_act * gate_sig
+        hidden_ref[0, 0, :, span] = (gate_silu * up_act).astype(bf16)
+        grad_gate = grad_hidden * up_act * gate_sig * (1.0 + gate_act * (1.0 - gate_sig))
+        grad_gate_ref[0, 0, :, span] = grad_gate.astype(bf16)
+        grad_up_ref[0, 0, :, span] = (grad_hidden * gate_silu).astype(bf16)
 
 
 def activate(taken, gate_act, grad_hidden, w_up, ties=()):
@@ -520,7 +529,6 @@
             (w_up, spans(w_up.shape)),
         ],
         [(result, of(FFE))] * 3,
-        4 * count * capacity * D * FFE,
         ties=ties,
     )
 
@@ -543,59 +551,62 @@
             (right, pl.BlockSpec((1, 2, capacity, FFE), lambda e, d: (e, 0, 0, 0))),
         ],
         [(result, pl.BlockSpec((1, part, FFE), lambda e, d: (e, d, 0)))],
-        4 * count * capacity * D * FFE,
         ties=ties,
     )[0]
 
 
-def combine_kernel(scaled, acts, blocks, h, *refs):
+def combine_kernel(scaled, acts, h, *refs):
     act_refs, w_refs = refs[:acts], refs[acts : 2 * acts]
     column_ref, slot_ref, weight_ref = refs[2 * acts : 2 * acts + 3]
-    out_refs, total_ref = refs[2 * acts + 3 : -1], refs[-1]
-    expert = pl.program_id(0)
-    capacity = act_refs[0].shape[2]
-    half = total_ref.shape[0]
-    place = lax.broadcasted_iota(jnp.int32, (half, capacity), 1)
-    pick = (place == column_ref[0, 0]).astype(f32).astype(bf16)
-    if scaled:
-        scale = slot_weights(slot_ref[0, h : h + 1, :], weight_ref[0, h : h + 1, :], capacity)
-
-    @pl.when(expert == 0)
+    out_refs, (pick_ref, rows_ref, scale_ref) = refs[2 * acts + 3 : -3], refs[-3:]
+    count, _, capacity, _ = act_refs[0].shape
+    half, stride = pick_ref.shape[0], rows_ref.shape[0] // count
+
+    @pl.when(pl.program_id(0) == 0)
     def _():
-        total_ref[...] = jnp.zeros_like(total_ref)
-
-    for d in range(0, D, part):
-        grads = [
-            dot(a_ref[0, 0], w_ref[0, d : d + part, :], 1, 1)
-            for a_ref, w_ref in zip(act_refs, w_refs)
-        ]
+        rows_ref[...] = jnp.zeros_like(rows_ref)
+        place = lax.broadcasted_iota(jnp.int32, (half, stride), 1)
+        for e in range(count):
+            pick = (place == column_ref[e, 0]).astype(f32).astype(bf16)
+            pick_ref[:, e * stride : (e + 1) * stride] = pick
+            if scaled:
+                scale_ref[e] = slot_weights(
+                    slot_ref[e, h : h + 1, :], weight_ref[e, h : h + 1, :], capacity
+                )
+
+    for e in range(count):
+        grads = [dot(a_ref[e, 0], w_ref[e], 1, 1) for a_ref, w_ref in zip(act_refs, w_refs)]
         rows = sum(grads[1:], grads[0])
         if scaled:
-            rows = rows * scale
-        total_ref[:, d : d + part] += dot(pick, rows.astype(bf16), 1, 0)
-
-    @pl.when(expert == pl.num_programs(0) - 1)
-    def _():
-        n = half // blocks
-        for b, ref in enumerate(out_refs):
-            ref[...] = total_ref[b * n : (b + 1) * n, :].astype(bf16)
+            rows = rows * scale_ref[e]
+        rows_ref[e * stride : e * stride + capacity, :] = rows.astype(bf16)
+    n = out_refs[0].shape[0]
+    for b, ref in enumerate(out_refs):
+        ref[...] = dot(pick_ref[b * n : (b + 1) * n, :], rows_ref[...], 1, 0).astype(bf16)
 
 
 def combine(acts, banks, columns, slots, weights, h, blocks, scaled, ties=()):
     count, _, capacity, _ = acts[0].shape
     half = columns.shape[2]
+    stride = -(-capacity // 128) * 128
     result = jax.ShapeDtypeStruct((half // blocks, D), bf16)
+    once = pl.Buffered(buffer_count=1)
+    act = pl.BlockSpec((count, 1, capacity, FFE), lambda d: (0, h, 0, 0), pipeline_mode=once)
+    column = pl.BlockSpec((count, 1, half, 1), lambda d: (0, h, 0, 0), pipeline_mode=once)
     return call(
-        lambda *refs: combine_kernel(scaled, len(acts), blocks, h, *refs),
+        lambda *refs: combine_kernel(scaled, len(acts), h, *refs),
         "combine",
-        (count,),
-        [(a, pl.BlockSpec((1, 1, capacity, FFE), lambda e: (e, h, 0, 0))) for a in acts]
-        + [(w, spans(w.shape)) for w in banks]
-        + [(columns, pl.BlockSpec((1, 1, half, 1), lambda e: (e, h, 0, 0)))]
-        + [(v, spans(v.shape)) for v in (slots, weights)],
-        [(result, whole_of(result.shape))] * blocks,
-        2 * count * capacity * D * (FFE * len(acts) + half),
-        scratch=[pltpu.VMEM((half, D), f32)],
+        (D // part,),
+        [(a, act) for a in acts]
+        + [(w, pl.BlockSpec((count, part, FFE), lambda d: (0, d, 0))) for w in banks]
+        + [(columns, column)]
+        + [(v, whole_of(v.shape)) for v in (slots, weights)],
+        [(result, pl.BlockSpec((half // blocks, part), lambda d: (0, d)))] * blocks,
+        scratch=[
+            pltpu.VMEM((half, count * stride), bf16),
+            pltpu.VMEM((count * stride, part), bf16),
+            pltpu.VMEM((count, capacity, 1), f32),
+        ],
         ties=ties,
     )
 
@@ -635,7 +646,8 @@
         return lax.all_gather(value, "fsdp", axis=axis, tiled=True)
 
     def gather_tokens(value):
-        return jnp.stack(ring_gather(value, "seq"))
+        blocks = jnp.concatenate(ring_gather(value, "seq", split=True), axis=0)
+        return blocks.reshape((ns,) + value.shape)
 
     columns = [
         lax.dynamic_slice_in_dim(w, seq_index * width, width, axis=1).reshape(-1, heads_local, HD)
@@ -689,7 +701,7 @@
     inv_two = rms_scale(middle)
     normed_two = middle * inv_two
     h_two_own = (normed_two * gain_two).astype(bf16).reshape(micro, rows, D)
-    h_blocks = ring_gather(h_two_own, "seq", ())
+    h_blocks = ring_gather(h_two_own, "seq", (), True)
 
     packed = packed[..., D : D + 3 * TOP].astype(f32)
     packed = packed.reshape(2, half, 3 * TOP)
@@ -733,7 +745,7 @@
         return work
 
     g_blocks = ring_gather(
-        after(cotangent, h_blocks[-1]), "seq", (None, take_work(0), take_work(pair))
+        after(cotangent, h_blocks[-1]), "seq", (None, None, take_work(0), take_work(pair)), True
     )
     taken, gate_act = done["takes"]
 
@@ -752,29 +764,22 @@
     o_all = ring_gather(
         after(o_heads.reshape(group * micro, width), g_blocks[-1]),
         "seq",
-        (grad_work, act_work, first_work),
-        {2: lambda moved: keep(o_moved=moved)},
-        tie_last=False,
-    )
-    across = sizes("seq")[1] - 1
-    o_all, o_last = o_all[:-across], o_all[-across:]
+        (grad_work, None, act_work, first_work),
+    )
     first = done["first"]
     grad_rows = done["grad_rows"]
     hidden, grad_gate_act, grad_up_act = done["acts"]
-    second = combined(
-        (grad_gate_act, grad_up_act), (w_gate, w_up), 1, False, (first[0], *done["o_moved"])
-    )
+    second = combined((grad_gate_act, grad_up_act), (w_gate, w_up), 1, False, (first[0], o_all[-1]))
 
     def down_work(ties):
         return keep(whole_down=bank_grad(grad_rows, hidden, ties))
 
     def down_then(moved):
-        o_all.extend(together((done["whole_down"], *moved), *o_last))
-        keep(sum_down=after(done["whole_down"], o_all[-1]))
+        keep(sum_down=after(done["whole_down"], *moved))
 
     def mixed_work(h):
         def work(ties):
-            mixed = combined((hidden,), (w_down,), h, True, tuple(ties) + tuple(o_all[-across:]))
+            mixed = combined((hidden,), (w_down,), h, True, ties)
             done.setdefault("mixed", []).extend(mixed)
             return mixed[0]
 

time: 1030 us -> 1010 us (0.981)
  Pallas kernels: 379 us -> 360 us
    pallas_call x12, Pallas kernels: 308 us -> 289 us  [call(): pl.pallas_call(run, grid=grid, in_specs=[spec for _, spec in ins] + [pl.B...]
    ppermute x52 -> x55, waiting for transfers between devices: 287 us -> 278 us  [shift(): return lax.ppermute(value, axis, pairs)]
    ppermute x52 -> x55, starting transfers between devices: 51.4 us -> 56.9 us  [shift(): return lax.ppermute(value, axis, pairs)]
    unnamed x258 -> x266, local copies, waits for them, and re-layouts: 68.9 us -> 67.7 us
  transfers between devices with their start and end apart: 68 -> 71, of which waited for: 25 -> 29; matrix products, arithmetic and copies ran while one was open for 15% -> 15% of each run, Pallas kernels for 37% -> 36%
where the time goes in v6:
time: 1010 us
  Pallas kernels  360 us (36%)
  waiting for transfers between devices  313 us (31%)
  local copies, waits for them, and re-layouts  115 us (11%)
  other arithmetic  80.1 us (8%)
  starting transfers between devices  77.1 us (8%)
  blocking collectives  25.7 us (3%)
  matrix products  19.1 us (2%)
  between operations  16.1 us (2%)
    pallas_call x12, Pallas kernels, call(): pl.pallas_call(run, grid=grid, in_specs=[spec for _, spec in ins] + [pl.B...  289 us
    ppermute x55, waiting for transfers between devices, shift(): return lax.ppermute(value, axis, pairs)  278 us
    unnamed x266, local copies, waits for them, and re-layouts  67.7 us
    ppermute x55, starting transfers between devices, shift(): return lax.ppermute(value, axis, pairs)  56.9 us
    pallas_call x1, Pallas kernels, attend_back(): pl.pallas_call(lambda *refs: attend_back_kernel(tile, *refs[:7], *refs[-2...  33.3 us
    all_to_all x1, blocking collectives, body(): lax.all_to_all(o_heads, 'seq', split_axis=0, concat_axis=0, tiled=True)  25.7 us
    pallas_call x1, Pallas kernels, proj_grads(): pl.pallas_call(run, grid_spec=pltpu.PrefetchScalarGridSpec(num_scalar_pre...  20.9 us
    convert_element_type x3, other arithmetic, bank_sum(): lax.psum_scatter(whole, 'fsdp', scatter_dimension=1, tiled=True).astype(f32)  20.3 us
  transfers between devices with their start and end apart: 71, of which 29 were waited for; matrix products, arithmetic and copies ran while one was open for 15% of the time, Pallas kernels for 36%

profile of v6, /device:TPU:0, one launch (start us, length us, event | category | flops | bytes accessed | tf_op | source)
XLA Modules:
  0.0 1005.4 jit_solution(16351244253295117765)
XLA Ops:
  16.9 3.0 collective-permute-start.1
  22.5 24.4 %collective-permute-done.1 = bf16[2,128,2176]{2,1,0:T(8,128)(2,1)} collective-permute-done((bf16[2,128,2176]{2,1,0:T(8,128)(2,1)}, bf16[2,128,2176]{2,1,0:T(8,128)(2,1)}, u32[]{:S(2)}, u32[]{:S(2)}) %collective-permute-start.1) | collective-permute-done | bytes 1114144 | tf_op jit(solution)/shard_map/ppermute | solution.py:31
  51.5 2.8 constant_dynamic-update-slice_fusion.7
  54.2 20.5 %collective-permute-done.3 = bf16[2,128,2176]{2,1,0:T(8,128)(2,1)} collective-permute-done((bf16[2,128,2176]{2,1,0:T(8,128)(2,1)}, bf16[2,128,2176]{2,1,0:T(8,128)(2,1)}, u32[]{:S(2)}, u32[]{:S(2)}) %collective-permute-start.3) | collective-permute-done | bytes 1114144 | tf_op jit(solution)/shard_map/ppermute | solution.py:31
  81.9 20.4 %collective-permute-done.5 = bf16[2,128,2176]{2,1,0:T(8,128)(2,1)S(1)} collective-permute-done((bf16[2,128,2176]{2,1,0:T(8,128)(2,1)}, bf16[2,128,2176]{2,1,0:T(8,128)(2,1)S(1)}, u32[]{:S(2)}, u32[]{:S(2)}) %collective-permute-start.5) | collective-permute-done | bytes 1114144 | tf_op jit(solution)/shard_map/ppermute | solution.py:31
  105.9 7.9 collective-permute-done.6
  117.8 6.5 fusion
  126.3 5.3 fusion.2
  131.6 6.9 fusion.4.refs_0_
  138.6 16.5 %attend.1 = bf16[8,2,128,256]{3,2,1,0:T(8,128)(2,1)S(1)} custom-call(bf16[8,2,128,768]{3,2,1,0:T(8,128)(2,1)S(1)} %fusion.4.refs_0_, f32[1024,128]{1,0:T(8,128)S(1)} %get-tuple-element.119.refs_1_.refs_2_, f32[1024,128]{1,0:T(8,128)S(1)} %get-tuple-element.118.refs_2_.refs_3_, s32[2,1,1024]{2,1,0:T(1,128)S(1)} %bitcast.192, ...), custom_call_target="tpu_custom_call" | custom-call | flops 1 | bytes 1 | tf_op jit(solution)/shard_map/attend/pallas_call | solution.py:281
  155.7 25.7 %all_to_all.20 = bf16[8,2,128,256]{3,2,1,0:T(8,128)(2,1)S(1)} all-to-all(bf16[8,2,128,256]{3,2,1,0:T(8,128)(2,1)S(1)} %gather_fusion.1), channel_id=1, replica_groups=mesh['fsdp'=4,'seq'=8] {'seq'}, dimensions={0} | all-to-all | bytes 2097152 | tf_op jit(solution)/shard_map/all_to_all | solution.py:696
  182.6 5.8 multiply_reduce_fusion.3
  191.6 21.4 %collective-permute-done.8.refs_0_ = bf16[2,128,2048]{2,1,0:T(8,128)(2,1)S(1)} collective-permute-done((bf16[2,128,2048]{2,1,0:T(8,128)(2,1)S(1)}, bf16[2,128,2048]{2,1,0:T(8,128)(2,1)S(1)}, u32[]{:S(2)}, u32[]{:S(2)}) %collective-permute-start.8) | collective-permute-done | bytes 1048608 | tf_op jit(solution)/shard_map/ppermute | solution.py:31
  213.0 3.2 collective-permute-done.9.refs_1_.refs_0_
  217.5 21.8 %collective-permute-done.10.refs_0_ = bf16[2,128,2048]{2,1,0:T(8,128)(2,1)S(1)} collective-permute-done((bf16[2,128,2048]{2,1,0:T(8,128)(2,1)}, bf16[2,128,2048]{2,1,0:T(8,128)(2,1)S(1)}, u32[]{:S(2)}, u32[]{:S(2)}) %collective-permute-start.10) | collective-permute-done | bytes 1048608 | tf_op jit(solution)/shard_map/ppermute | solution.py:31
  243.8 19.2 %collective-permute-done.12.refs_0_ = bf16[2,128,2048]{2,1,0:T(8,128)(2,1)S(1)} collective-permute-done((bf16[2,128,2048]{2,1,0:T(8,128)(2,1)}, bf16[2,128,2048]{2,1,0:T(8,128)(2,1)S(1)}, u32[]{:S(2)}, u32[]{:S(2)}) %collective-permute-start.12) | collective-permute-done | bytes 1048608 | tf_op jit(solution)/shard_map/ppermute | solution.py:31
  263.0 3.2 collective-permute-done.13.refs_1_.refs_0_
  270.0 9.1 collective-permute-done.14.refs_0_
  285.1 18.4 %collective-permute-done.16.refs_1_.refs_0_ = bf16[2,128,2048]{2,1,0:T(8,128)(2,1)S(1)} collective-permute-done((bf16[2,128,2048]{2,1,0:T(8,128)(2,1)}, bf16[2,128,2048]{2,1,0:T(8,128)(2,1)S(1)}, u32[]{:S(2)}, u32[]{:S(2)}) %collective-permute-start.16) | collective-permute-done | bytes 1048608 | tf_op jit(solution)/shard_map/ppermute | solution.py:31
  305.5 2.8 collective-permute-start.18
  308.3 17.0 %collective-permute-done.18.refs_0_ = bf16[2,128,2048]{2,1,0:T(8,128)(2,1)S(1)} collective-permute-done((bf16[2,128,2048]{2,1,0:T(8,128)(2,1)}, bf16[2,128,2048]{2,1,0:T(8,128)(2,1)S(1)}, u32[]{:S(2)}, u32[]{:S(2)}) %collective-permute-start.18) | collective-permute-done | bytes 1048608 | tf_op jit(solution)/shard_map/ppermute | solution.py:31
  328.8 2.8 collective-permute-start.20
  341.2 19.8 %dispatch.3 = (bf16[4,2,384,2048]{3,2,1,0:T(8,128)(2,1)}, f32[4,2,384,1024]{3,2,1,0:T(8,128)}) custom-call(bf16[256,2048]{1,0:T(8,128)(2,1)} %copy-done.80, bf16[256,2048]{1,0:T(8,128)(2,1)} %bitcast.210, bf16[256,2048]{1,0:T(8,128)(2,1)} %bitcast.214, bf16[256,2048]{1,0:T(8,128)(2,1)} %bitcast.212, bf16[256,2048]{1,0:T(8,128)(2,1)} %bitcast.216, ...), custom_call_target="tpu_custom_call" | custom-call | flops 1 | bytes 1 | tf_op jit(solution)/shard_map/dispatch/pallas_call | solution.py:427
  366.6 19.8 %dispatch.4 = (bf16[4,2,384,2048]{3,2,1,0:T(8,128)(2,1)}, f32[4,2,384,1024]{3,2,1,0:T(8,128)}) custom-call(bf16[256,2048]{1,0:T(8,128)(2,1)} %copy-done.80, bf16[256,2048]{1,0:T(8,128)(2,1)} %bitcast.211, bf16[256,2048]{1,0:T(8,128)(2,1)} %bitcast.215, bf16[256,2048]{1,0:T(8,128)(2,1)} %bitcast.213, ...), custom_call_target="tpu_custom_call", output_to_operand_aliasing={{0}: (12, {}), {1}: (13, {})} | custom-call | flops 1 | bytes 1 | tf_op jit(solution)/shard_map/dispatch/pallas_call | solution.py:427
  387.4 3.5 collective-permute-start.24
  392.5 34.2 %dispatch.5 = (bf16[4,2,384,2048]{3,2,1,0:T(8,128)(2,1)}, f32[4,2,384,1024]{3,2,1,0:T(8,128)}) custom-call(bf16[256,2048]{1,0:T(8,128)(2,1)} %bitcast.223, bf16[256,2048]{1,0:T(8,128)(2,1)} %bitcast.222, bf16[256,2048]{1,0:T(8,128)(2,1)} %bitcast.221, bf16[256,2048]{1,0:T(8,128)(2,1)} %bitcast.208, bf16[256,2048]{1,0:T(8,128)(2,1)} %bitcast.209, ...), custom_call_target="tpu_custom_call" | custom-call | flops 1 | bytes 1 | tf_op jit(solution)/shard_map/dispatch/pallas_call | solution.py:427
  428.8 21.5 %collective-permute-done.26.refs_0_ = bf16[2048,256]{1,0:T(8,128)(2,1)S(1)} collective-permute-done((bf16[2048,256]{1,0:T(8,128)(2,1)}, bf16[2048,256]{1,0:T(8,128)(2,1)S(1)}, u32[]{:S(2)}, u32[]{:S(2)}) %collective-permute-start.26) | collective-permute-done | bytes 1048608 | tf_op jit(solution)/shard_map/ppermute | solution.py:31
  455.4 32.2 %activate.1 = (bf16[4,2,384,1024]{3,2,1,0:T(8,128)(2,1)}, bf16[4,2,384,1024]{3,2,1,0:T(8,128)(2,1)}, bf16[4,2,384,1024]{3,2,1,0:T(8,128)(2,1)}) custom-call(bf16[4,2,384,2048]{3,2,1,0:T(8,128)(2,1)} %get-tuple-element.56.refs_1_.refs_0_, f32[4,2,384,1024]{3,2,1,0:T(8,128)} %get-tuple-element.57.refs_1_, f32[4,2,384,1024]{3,2,1,0:T(8,128)} %get-tuple-element.58.refs_2_, ...), custom_call_target="tpu_custom_call" | custom-call | flops 1 | bytes 1 | tf_op jit(solution)/shard_map/activate/pallas_call | solution.py:427
  489.0 2.8 copy.238.refs_4_.refs_2_
  491.8 27.7 %combine.4 = (bf16[256,2048]{1,0:T(8,128)(2,1)}, bf16[256,2048]{1,0:T(8,128)(2,1)}, bf16[256,2048]{1,0:T(8,128)(2,1)}, bf16[256,2048]{1,0:T(8,128)(2,1)}) custom-call(bf16[4,2,384,1024]{3,2,1,0:T(8,128)(2,1)} %get-tuple-element.61.refs_0_.refs_1_, bf16[4,2,384,1024]{3,2,1,0:T(8,128)(2,1)} %get-tuple-element.62.refs_1_, ...), custom_call_target="tpu_custom_call" | custom-call | flops 1 | bytes 1 | tf_op jit(solution)/shard_map/combine/pallas_call | solution.py:427
  522.5 27.9 %combine.5 = (bf16[256,2048]{1,0:T(8,128)(2,1)}, bf16[256,2048]{1,0:T(8,128)(2,1)}, bf16[256,2048]{1,0:T(8,128)(2,1)}, bf16[256,2048]{1,0:T(8,128)(2,1)}) custom-call(bf16[4,2,384,1024]{3,2,1,0:T(8,128)(2,1)} %get-tuple-element.61.refs_0_.refs_1_, bf16[4,2,384,1024]{3,2,1,0:T(8,128)(2,1)} %get-tuple-element.62.refs_1_, ...), custom_call_target="tpu_custom_call" | custom-call | flops 1 | bytes 1 | tf_op jit(solution)/shard_map/combine/pallas_call | solution.py:427
  553.8 24.1 %bank_grad.3.refs_1_.refs_0_ = bf16[4,2048,1024]{2,1,0:T(8,128)(2,1)} custom-call(bf16[4,2,384,2048]{3,2,1,0:T(8,128)(2,1)} %get-tuple-element.59.refs_1_.refs_0_, bf16[4,2,384,1024]{3,2,1,0:T(8,128)(2,1)} %get-tuple-element.60.refs_1_.refs_0_, bf16[2,128,2048]{2,1,0:T(8,128)(2,1)} %after.93.refs_2_), custom_call_target="tpu_custom_call" | custom-call | flops 1 | bytes 1 | tf_op jit(solution)/shard_map/bank_grad/pallas_call | solution.py:427
  584.4 20.5 %combine.6 = (bf16[256,2048]{1,0:T(8,128)(2,1)}, bf16[256,2048]{1,0:T(8,128)(2,1)}, bf16[256,2048]{1,0:T(8,128)(2,1)}, bf16[256,2048]{1,0:T(8,128)(2,1)}) custom-call(bf16[4,2,384,1024]{3,2,1,0:T(8,128)(2,1)} %get-tuple-element.60.refs_1_.refs_0_, bf16[4,2048,1024]{2,1,0:T(8,128)(2,1)} %all-gather.12.cloned.1.call-done.refs_11_.refs_1_, ...), custom_call_target="tpu_custom_call" | custom-call | flops 1 | bytes 1 | tf_op jit(solution)/shard_map/combine/pallas_call | solution.py:427
  604.9 3.5 collective-permute-done.36.refs_2_.refs_0_
  614.9 20.5 %combine.7 = (bf16[256,2048]{1,0:T(8,128)(2,1)}, bf16[256,2048]{1,0:T(8,128)(2,1)}, bf16[256,2048]{1,0:T(8,128)(2,1)}, bf16[256,2048]{1,0:T(8,128)(2,1)}) custom-call(bf16[4,2,384,1024]{3,2,1,0:T(8,128)(2,1)} %get-tuple-element.60.refs_1_.refs_0_, bf16[4,2048,1024]{2,1,0:T(8,128)(2,1)} %all-gather.12.cloned.1.call-done.refs_11_.refs_1_, ...), custom_call_target="tpu_custom_call" | custom-call | flops 1 | bytes 1 | tf_op jit(solution)/shard_map/combine/pallas_call | solution.py:427
  643.0 6.1 convolution_convert_fusion.refs_2_
  650.6 4.8 all-to-all-start.1
  655.4 24.1 %bank_grad.4.refs_1_.refs_0_ = bf16[4,2048,1024]{2,1,0:T(8,128)(2,1)} custom-call(bf16[4,2,384,2048]{3,2,1,0:T(8,128)(2,1)} %get-tuple-element.56.refs_1_.refs_0_, bf16[4,2,384,1024]{3,2,1,0:T(8,128)(2,1)} %get-tuple-element.61.refs_0_.refs_1_, bf16[256,2048]{1,0:T(8,128)(2,1)} %copy-done.87), custom_call_target="tpu_custom_call" | custom-call | flops 1 | bytes 1 | tf_op jit(solution)/shard_map/bank_grad/pallas_call | solution.py:427
  682.4 5.9 all-to-all-start.2
  691.8 2.9 gather_fusion.2
  699.9 33.3 %attend_back.1 = (bf16[8,2,128,768]{3,2,1,0:T(8,128)(2,1)S(1)}, f32[4,2,128]{2,1,0:T(2,128)S(1)}) custom-call(bf16[8,2,128,768]{3,2,1,0:T(8,128)(2,1)S(1)} %copy-done.3, bf16[8,2,128,256]{3,2,1,0:T(8,128)(2,1)S(1)} %copy-done.11, f32[1024,128]{1,0:T(8,128)S(1)} %copy-done.10, f32[1024,128]{1,0:T(8,128)S(1)} %copy-done.8, s32[2,1,1024]{2,1,0:T(1,128)S(1)} %bitcast.193, ...), custom_call_target="tpu_custom_call" | custom-call | flops 1 | bytes 1 | tf_op jit(solution)/shard_map/attend_back/pallas_call | solution.py:298
  735.5 13.1 %part_grads.1 = (bf16[256,2048]{1,0:T(8,128)(2,1)}, bf16[256,2048]{1,0:T(8,128)(2,1)}, bf16[256,2048]{1,0:T(8,128)(2,1)}, bf16[256,2048]{1,0:T(8,128)(2,1)}, bf1...) custom-call(bf16[2048,768]{1,0:T(8,128)(2,1)} %bitcast.190, ...), custom_call_target="tpu_custom_call" | custom-call | flops 1 | bytes 1 | tf_op jit(solution)/shard_map/part_grads/pallas_call | solution.py:427
  749.8 2.6 fusion.12
  761.0 20.9 %proj_grads.1 = (bf16[512,1152]{1,0:T(8,128)(2,1)}, bf16[512,1152]{1,0:T(8,128)(2,1)}, bf16[512,1152]{1,0:T(8,128)(2,1)}, bf16[512,1152]{1,0:T(8,128)(2,1)}) custom-call(s32[4]{0:T(128)} %fusion.41.refs_0_, s32[8]{0:T(128)} %copy-done.121, bf16[2048,2048]{1,0:T(8,128)(2,1)} %bitcast.198, bf16[2048,768]{1,0:T(8,128)(2,1)} %bitcast.191, ...), custom_call_target="tpu_custom_call" | custom-call | flops 1 | bytes 1 | tf_op jit(solution)/shard_map/proj_grads/pallas_call | solution.py:388
  786.3 2.7 add_convert_fusion.2
  789.0 2.9 add_convert_fusion.6
  796.2 25.2 %bank_grad.5.refs_1_.refs_0_ = bf16[4,2048,1024]{2,1,0:T(8,128)(2,1)} custom-call(bf16[4,2,384,2048]{3,2,1,0:T(8,128)(2,1)} %get-tuple-element.56.refs_1_.refs_0_, bf16[4,2,384,1024]{3,2,1,0:T(8,128)(2,1)} %get-tuple-element.62.refs_1_, bf16[2,128,2048]{2,1,0:T(8,128)(2,1)} %after.109.refs_1_.refs_2_.refs_4_), custom_call_target="tpu_custom_call" | custom-call | flops 1 | bytes 1 | tf_op jit(solution)/shard_map/bank_grad/pallas_call | solution.py:427
  821.3 21.8 %collective-permute-done.46.refs_2_.refs_0_ = bf16[512,1152]{1,0:T(8,128)(2,1)} collective-permute-done((bf16[512,1152]{1,0:T(8,128)(2,1)}, bf16[512,1152]{1,0:T(8,128)(2,1)}, u32[]{:S(2)}, u32[]{:S(2)}) %collective-permute-start.46) | collective-permute-done | bytes 1179680 | tf_op jit(solution)/shard_map/ppermute | solution.py:31
  844.4 3.1 add_convert_fusion.refs_5_.refs_0_
  848.8 4.1 all-to-all-start.3
  855.0 2.7 add_convert_fusion.5
  859.8 6.6 convert_element_type.430.refs_1_
  866.4 23.7 %collective-permute-done.52.refs_2_.refs_0_ = bf16[2,128,2048]{2,1,0:T(8,128)(2,1)} collective-permute-done((bf16[2,128,2048]{2,1,0:T(8,128)(2,1)}, bf16[2,128,2048]{2,1,0:T(8,128)(2,1)}, u32[]{:S(2)}, u32[]{:S(2)}) %collective-permute-start.52) | collective-permute-done | bytes 1048608 | tf_op jit(solution)/shard_map/ppermute | solution.py:31
  890.1 8.1 collective-permute-done.51.refs_0_
  898.2 5.4 all-to-all-done.3.refs_4_.refs_0_
  906.2 2.7 add_convert_fusion.3
  911.0 3.6 add_convert_fusion.4
  919.6 3.7 reshape.579
  926.2 5.4 fusion.63
  939.8 6.9 convert_element_type.438.refs_1_
  946.7 7.0 collective-permute-done.57.refs_3_.refs_0_
  968.8 2.9 fusion.19
  972.2 19.2 %reduce-scatter.8.cloned.1.call-done = bf16[4,512,1024]{2,1,0:T(8,128)(2,1)} async-done(((bf16[4,2048,1024]{2,1,0:T(8,128)(2,1)}), bf16[4,512,1024]{2,1,0:T(8,128)(2,1)}) %reduce-scatter.8.cloned.1.call-update) | async-done | bytes 4194320 | tf_op jit(solution)/shard_map/reduce_scatter | solution.py:800
  991.4 6.8 convert_element_type.467
  (552 shorter events, 188.8 us)
Async XLA Ops:
  7.2 117.2 %all-gather.6.cloned.1.call-start = ((), (), s32[]{:S(2)}) async-start(), calls=%async_computation.7 | async-start | bytes 4587520 | tf_op jit(solution)/shard_map/all_gather | solution.py:646
  11.1 171.2 %all-gather.8.cloned.1.call-start = ((), (), s32[]{:S(2)}) async-start(), calls=%async_computation.8 | async-start | bytes 10485760 | tf_op jit(solution)/shard_map/all_gather | solution.py:646
  11.8 329.4 %all-gather.10.cloned.1.call-start = ((), (), s32[]{:S(2)}) async-start(), calls=%async_computation.9 | async-start | bytes 20971520 | tf_op jit(solution)/shard_map/all_gather | solution.py:646
  12.5 380.0 %all-gather.12.cloned.1.call-start = ((), (), s32[]{:S(2)}) async-start(), calls=%async_computation.10 | async-start | bytes 20971520 | tf_op jit(solution)/shard_map/all_gather | solution.py:646
  13.2 442.3 %all-gather.14.cloned.1.call-start = ((), (), s32[]{:S(2)}) async-start(), calls=%async_computation.11 | async-start | bytes 20971520 | tf_op jit(solution)/shard_map/all_gather | solution.py:646
  13.7 846.0 %reduce-scatter.4.cloned.1.call-start = ((), (), s32[]{:S(2)}) async-start(), calls=%async_computation.12 | async-start | bytes 20971520 | tf_op jit(solution)/shard_map/reduce_scatter | solution.py:800
  16.9 29.9 %collective-permute-start.1 = (bf16[2,128,2176]{2,1,0:T(8,128)(2,1)}, bf16[2,128,2176]{2,1,0:T(8,128)(2,1)}, u32[]{:S(2)}, u32[]{:S(2)}) collective-permute-start(bf16[2,128,2176]{2,1,0:T(8,128)(2,1)} %get-tuple-element.111), channel_id=1, source_target_pairs={{0,2},{1,3},{2,4},{3,5},{4,6},{5,7},{6,0},{7,1},{8,10},{9,11},{10,... | collective-permute-start | bytes 3342344 | tf_op jit(solution)/shard_map/ppermute | solution.py:31
  20.0 31.5 %collective-permute-start = (bf16[2,128,2176]{2,1,0:T(8,128)(2,1)}, bf16[2,128,2176]{2,1,0:T(8,128)(2,1)}, u32[]{:S(2)}, u32[]{:S(2)}) collective-permute-start(bf16[2,128,2176]{2,1,0:T(8,128)(2,1)} %get-tuple-element.111), channel_id=1, source_target_pairs={{0,1},{1,0},{2,3},{3,2},{4,5},{5,4},{6,7},{7,6},{8,9},{9,8},{10,11... | collective-permute-start | bytes 3342344 | tf_op jit(solution)/shard_map/ppermute | solution.py:31
  46.9 27.9 %collective-permute-start.3 = (bf16[2,128,2176]{2,1,0:T(8,128)(2,1)}, bf16[2,128,2176]{2,1,0:T(8,128)(2,1)}, u32[]{:S(2)}, u32[]{:S(2)}) collective-permute-start(bf16[2,128,2176]{2,1,0:T(8,128)(2,1)} %collective-permute-done.1), channel_id=1, source_target_pairs={{0,2},{1,3},{2,4},{3,5},{4,6},{5,7},{6,0},{7,1},{8,10},{9,11},{10,... | collective-permute-start | bytes 3342344 | tf_op jit(solution)/shard_map/ppermute | solution.py:31
  48.0 30.4 %collective-permute-start.2 = (bf16[2,128,2176]{2,1,0:T(8,128)(2,1)}, bf16[2,128,2176]{2,1,0:T(8,128)(2,1)S(1)}, u32[]{:S(2)}, u32[]{:S(2)}) collective-permute-start(bf16[2,128,2176]{2,1,0:T(8,128)(2,1)} %collective-permute-done.1), channel_id=1, source_target_pairs={{0,1},{1,0},{2,3},{3,2},{4,5},{5,4},{6,7},{7,6},{8,9},{9,8},{10,11... | collective-permute-start | bytes 3342344 | tf_op jit(solution)/shard_map/ppermute | solution.py:31
  74.7 28.7 %collective-permute-start.4 = (bf16[2,128,2176]{2,1,0:T(8,128)(2,1)}, bf16[2,128,2176]{2,1,0:T(8,128)(2,1)S(1)}, u32[]{:S(2)}, u32[]{:S(2)}) collective-permute-start(bf16[2,128,2176]{2,1,0:T(8,128)(2,1)} %collective-permute-done.3), channel_id=1, source_target_pairs={{0,1},{1,0},{2,3},{3,2},{4,5},{5,4},{6,7},{7,6},{8,9},{9,8},{10,11... | collective-permute-start | bytes 3342344 | tf_op jit(solution)/shard_map/ppermute | solution.py:31
  76.0 26.3 %collective-permute-start.5 = (bf16[2,128,2176]{2,1,0:T(8,128)(2,1)}, bf16[2,128,2176]{2,1,0:T(8,128)(2,1)S(1)}, u32[]{:S(2)}, u32[]{:S(2)}) collective-permute-start(bf16[2,128,2176]{2,1,0:T(8,128)(2,1)} %collective-permute-done.3), channel_id=1, source_target_pairs={{0,2},{1,3},{2,4},{3,5},{4,6},{5,7},{6,0},{7,1},{8,10},{9,11},{10,... | collective-permute-start | bytes 3342344 | tf_op jit(solution)/shard_map/ppermute | solution.py:31
  103.5 13.5 %collective-permute-start.7 = (bf16[1,128,2176]{2,1,0:T(8,128)(2,1)S(1)}, bf16[1,128,2176]{2,1,0:T(8,128)(2,1)S(1)}, u32[]{:S(2)}, u32[]{:S(2)}) collective-permute-start(bf16[1,128,2176]{2,1,0:T(8,128)(2,1)S(1)} %slice.95), channel_id=1, source_target_pairs={{0,2},{1,3},{2,4},{3,5},{4,6},{5,7},{6,0},{7,1},{8,10},{9,11},{10,... | collective-permute-start | bytes 1671176 | tf_op jit(solution)/shard_map/ppermute | solution.py:31
  190.0 22.9 %collective-permute-start.8 = (bf16[2,128,2048]{2,1,0:T(8,128)(2,1)S(1)}, bf16[2,128,2048]{2,1,0:T(8,128)(2,1)S(1)}, u32[]{:S(2)}, u32[]{:S(2)}) collective-permute-start(bf16[2,128,2048]{2,1,0:T(8,128)(2,1)S(1)} %bitcast.227), channel_id=1, source_target_pairs={{0,1},{1,0},{2,3},{3,2},{4,5},{5,4},{6,7},{7,6},{8,9},{9,8},{10,11... | collective-permute-start | bytes 3145736 | tf_op jit(solution)/shard_map/ppermute | solution.py:31
  191.6 24.6 %collective-permute-start.9 = (bf16[2,128,2048]{2,1,0:T(8,128)(2,1)S(1)}, bf16[2,128,2048]{2,1,0:T(8,128)(2,1)S(1)}, u32[]{:S(2)}, u32[]{:S(2)}) collective-permute-start(bf16[2,128,2048]{2,1,0:T(8,128)(2,1)S(1)} %bitcast.228), channel_id=1, source_target_pairs={{0,2},{1,3},{2,4},{3,5},{4,6},{5,7},{6,0},{7,1},{8,10},{9,11},{10,... | collective-permute-start | bytes 3145736 | tf_op jit(solution)/shard_map/ppermute | solution.py:31
  217.2 22.1 %collective-permute-start.10 = (bf16[2,128,2048]{2,1,0:T(8,128)(2,1)}, bf16[2,128,2048]{2,1,0:T(8,128)(2,1)S(1)}, u32[]{:S(2)}, u32[]{:S(2)}) collective-permute-start(bf16[2,128,2048]{2,1,0:T(8,128)(2,1)} %after.69), channel_id=1, source_target_pairs={{0,1},{1,0},{2,3},{3,2},{4,5},{5,4},{6,7},{7,6},{8,9},{9,8},{10,11... | collective-permute-start | bytes 3145736 | tf_op jit(solution)/shard_map/ppermute | solution.py:31
  217.5 23.6 %collective-permute-start.11 = (bf16[2,128,2048]{2,1,0:T(8,128)(2,1)}, bf16[2,128,2048]{2,1,0:T(8,128)(2,1)S(1)}, u32[]{:S(2)}, u32[]{:S(2)}) collective-permute-start(bf16[2,128,2048]{2,1,0:T(8,128)(2,1)} %after.69), channel_id=1, source_target_pairs={{0,2},{1,3},{2,4},{3,5},{4,6},{5,7},{6,0},{7,1},{8,10},{9,11},{10,... | collective-permute-start | bytes 3145736 | tf_op jit(solution)/shard_map/ppermute | solution.py:31
  242.1 20.9 %collective-permute-start.12 = (bf16[2,128,2048]{2,1,0:T(8,128)(2,1)}, bf16[2,128,2048]{2,1,0:T(8,128)(2,1)S(1)}, u32[]{:S(2)}, u32[]{:S(2)}) collective-permute-start(bf16[2,128,2048]{2,1,0:T(8,128)(2,1)} %after.71), channel_id=1, source_target_pairs={{0,1},{1,0},{2,3},{3,2},{4,5},{5,4},{6,7},{7,6},{8,9},{9,8},{10,11... | collective-permute-start | bytes 3145736 | tf_op jit(solution)/shard_map/ppermute | solution.py:31
  243.8 22.4 %collective-permute-start.13 = (bf16[2,128,2048]{2,1,0:T(8,128)(2,1)}, bf16[2,128,2048]{2,1,0:T(8,128)(2,1)S(1)}, u32[]{:S(2)}, u32[]{:S(2)}) collective-permute-start(bf16[2,128,2048]{2,1,0:T(8,128)(2,1)} %after.71), channel_id=1, source_target_pairs={{0,2},{1,3},{2,4},{3,5},{4,6},{5,7},{6,0},{7,1},{8,10},{9,11},{10,... | collective-permute-start | bytes 3145736 | tf_op jit(solution)/shard_map/ppermute | solution.py:31
  283.3 20.2 %collective-permute-start.16 = (bf16[2,128,2048]{2,1,0:T(8,128)(2,1)}, bf16[2,128,2048]{2,1,0:T(8,128)(2,1)S(1)}, u32[]{:S(2)}, u32[]{:S(2)}) collective-permute-start(bf16[2,128,2048]{2,1,0:T(8,128)(2,1)} %after.76), channel_id=1, source_target_pairs={{0,2},{1,3},{2,4},{3,5},{4,6},{5,7},{6,0},{7,1},{8,10},{9,11},{10,... | collective-permute-start | bytes 3145736 | tf_op jit(solution)/shard_map/ppermute | solution.py:31
  283.3 20.2 %collective-permute-start.17 = (bf16[2,128,2048]{2,1,0:T(8,128)(2,1)}, bf16[2,128,2048]{2,1,0:T(8,128)(2,1)S(1)}, u32[]{:S(2)}, u32[]{:S(2)}) collective-permute-start(bf16[2,128,2048]{2,1,0:T(8,128)(2,1)} %after.76), channel_id=1, source_target_pairs={{0,1},{1,0},{2,3},{3,2},{4,5},{5,4},{6,7},{7,6},{8,9},{9,8},{10,11... | collective-permute-start | bytes 3145736 | tf_op jit(solution)/shard_map/ppermute | solution.py:31
  305.5 19.9 %collective-permute-start.18 = (bf16[2,128,2048]{2,1,0:T(8,128)(2,1)}, bf16[2,128,2048]{2,1,0:T(8,128)(2,1)S(1)}, u32[]{:S(2)}, u32[]{:S(2)}) collective-permute-start(bf16[2,128,2048]{2,1,0:T(8,128)(2,1)} %after.78), channel_id=1, source_target_pairs={{0,1},{1,0},{2,3},{3,2},{4,5},{5,4},{6,7},{7,6},{8,9},{9,8},{10,11... | collective-permute-start | bytes 3145736 | tf_op jit(solution)/shard_map/ppermute | solution.py:31
  308.3 18.3 %collective-permute-start.19 = (bf16[2,128,2048]{2,1,0:T(8,128)(2,1)}, bf16[2,128,2048]{2,1,0:T(8,128)(2,1)S(1)}, u32[]{:S(2)}, u32[]{:S(2)}) collective-permute-start(bf16[2,128,2048]{2,1,0:T(8,128)(2,1)} %after.78), channel_id=1, source_target_pairs={{0,2},{1,3},{2,4},{3,5},{4,6},{5,7},{6,0},{7,1},{8,10},{9,11},{10,... | collective-permute-start | bytes 3145736 | tf_op jit(solution)/shard_map/ppermute | solution.py:31
  328.8 32.3 %collective-permute-start.20 = (bf16[2,128,2048]{2,1,0:T(8,128)(2,1)}, bf16[2,128,2048]{2,1,0:T(8,128)(2,1)S(1)}, u32[]{:S(2)}, u32[]{:S(2)}) collective-permute-start(bf16[2,128,2048]{2,1,0:T(8,128)(2,1)} %after.80.refs_13_), channel_id=1, source_target_pairs={{0,1},{1,0},{2,3},{3,2},{4,5},{5,4},{6,7},{7,6},{8,9},{9,8},{10,11... | collective-permute-start | bytes 3145736 | tf_op jit(solution)/shard_map/ppermute | solution.py:31
  331.6 29.5 %collective-permute-start.21 = (bf16[2,128,2048]{2,1,0:T(8,128)(2,1)}, bf16[2,128,2048]{2,1,0:T(8,128)(2,1)S(1)}, u32[]{:S(2)}, u32[]{:S(2)}) collective-permute-start(bf16[2,128,2048]{2,1,0:T(8,128)(2,1)} %after.80.refs_13_), channel_id=1, source_target_pairs={{0,2},{1,3},{2,4},{3,5},{4,6},{5,7},{6,0},{7,1},{8,10},{9,11},{10,... | collective-permute-start | bytes 3145736 | tf_op jit(solution)/shard_map/ppermute | solution.py:31
  364.8 21.6 %collective-permute-start.22 = (bf16[1,128,2048]{2,1,0:T(8,128)(2,1)S(1)}, bf16[1,128,2048]{2,1,0:T(8,128)(2,1)S(1)}, u32[]{:S(2)}, u32[]{:S(2)}) collective-permute-start(bf16[1,128,2048]{2,1,0:T(8,128)(2,1)S(1)} %slice.106), channel_id=1, source_target_pairs={{0,1},{1,0},{2,3},{3,2},{4,5},{5,4},{6,7},{7,6},{8,9},{9,8},{10,11... | collective-permute-start | bytes 1572872 | tf_op jit(solution)/shard_map/ppermute | solution.py:31
  365.2 21.2 %collective-permute-start.23 = (bf16[1,128,2048]{2,1,0:T(8,128)(2,1)S(1)}, bf16[1,128,2048]{2,1,0:T(8,128)(2,1)S(1)}, u32[]{:S(2)}, u32[]{:S(2)}) collective-permute-start(bf16[1,128,2048]{2,1,0:T(8,128)(2,1)S(1)} %slice.107), channel_id=1, source_target_pairs={{0,2},{1,3},{2,4},{3,5},{4,6},{5,7},{6,0},{7,1},{8,10},{9,11},{10,... | collective-permute-start | bytes 1572872 | tf_op jit(solution)/shard_map/ppermute | solution.py:31
  387.4 39.3 %collective-permute-start.24 = (bf16[2048,256]{1,0:T(8,128)(2,1)}, bf16[2048,256]{1,0:T(8,128)(2,1)S(1)}, u32[]{:S(2)}, u32[]{:S(2)}) collective-permute-start(bf16[2048,256]{1,0:T(8,128)(2,1)} %after.85.refs_6_), channel_id=1, source_target_pairs={{0,2},{1,3},{2,4},{3,5},{4,6},{5,7},{6,0},{7,1},{8,10},{9,11},{10,... | collective-permute-start | bytes 3145736 | tf_op jit(solution)/shard_map/ppermute | solution.py:31
  390.8 35.9 %collective-permute-start.25 = (bf16[2048,256]{1,0:T(8,128)(2,1)}, bf16[2048,256]{1,0:T(8,128)(2,1)S(1)}, u32[]{:S(2)}, u32[]{:S(2)}) collective-permute-start(bf16[2048,256]{1,0:T(8,128)(2,1)} %after.85.refs_6_), channel_id=1, source_target_pairs={{0,1},{1,0},{2,3},{3,2},{4,5},{5,4},{6,7},{7,6},{8,9},{9,8},{10,11... | collective-permute-start | bytes 3145736 | tf_op jit(solution)/shard_map/ppermute | solution.py:31
  428.0 22.3 %collective-permute-start.26 = (bf16[2048,256]{1,0:T(8,128)(2,1)}, bf16[2048,256]{1,0:T(8,128)(2,1)S(1)}, u32[]{:S(2)}, u32[]{:S(2)}) collective-permute-start(bf16[2048,256]{1,0:T(8,128)(2,1)} %after.87.refs_8_), channel_id=1, source_target_pairs={{0,1},{1,0},{2,3},{3,2},{4,5},{5,4},{6,7},{7,6},{8,9},{9,8},{10,11... | collective-permute-start | bytes 3145736 | tf_op jit(solution)/shard_map/ppermute | solution.py:31
  428.5 23.4 %collective-permute-start.27 = (bf16[2048,256]{1,0:T(8,128)(2,1)}, bf16[2048,256]{1,0:T(8,128)(2,1)S(1)}, u32[]{:S(2)}, u32[]{:S(2)}) collective-permute-start(bf16[2048,256]{1,0:T(8,128)(2,1)} %after.87.refs_8_), channel_id=1, source_target_pairs={{0,2},{1,3},{2,4},{3,5},{4,6},{5,7},{6,0},{7,1},{8,10},{9,11},{10,... | collective-permute-start | bytes 3145736 | tf_op jit(solution)/shard_map/ppermute | solution.py:31
  452.8 34.8 %collective-permute-start.28 = (bf16[2048,256]{1,0:T(8,128)(2,1)}, bf16[2048,256]{1,0:T(8,128)(2,1)S(1)}, u32[]{:S(2)}, u32[]{:S(2)}) collective-permute-start(bf16[2048,256]{1,0:T(8,128)(2,1)} %after.89.refs_5_.refs_10_), channel_id=1, source_target_pairs={{0,1},{1,0},{2,3},{3,2},{4,5},{5,4},{6,7},{7,6},{8,9},{9,8},{10,11... | collective-permute-start | bytes 3145736 | tf_op jit(solution)/shard_map/ppermute | solution.py:31
  455.3 32.4 %collective-permute-start.29 = (bf16[2048,256]{1,0:T(8,128)(2,1)}, bf16[2048,256]{1,0:T(8,128)(2,1)S(1)}, u32[]{:S(2)}, u32[]{:S(2)}) collective-permute-start(bf16[2048,256]{1,0:T(8,128)(2,1)} %after.89.refs_5_.refs_10_), channel_id=1, source_target_pairs={{0,2},{1,3},{2,4},{3,5},{4,6},{5,7},{6,0},{7,1},{8,10},{9,11},{10,... | collective-permute-start | bytes 3145736 | tf_op jit(solution)/shard_map/ppermute | solution.py:31
  491.8 29.7 %collective-permute-start.30 = (bf16[2048,256]{1,0:T(8,128)(2,1)}, bf16[2048,256]{1,0:T(8,128)(2,1)S(1)}, u32[]{:S(2)}, u32[]{:S(2)}) collective-permute-start(bf16[2048,256]{1,0:T(8,128)(2,1)} %after.91.refs_8_.refs_12_), channel_id=1, source_target_pairs={{0,1},{1,0},{2,3},{3,2},{4,5},{5,4},{6,7},{7,6},{8,9},{9,8},{10,11... | collective-permute-start | bytes 3145736 | tf_op jit(solution)/shard_map/ppermute | solution.py:31
  519.5 30.9 %collective-permute-start.32 = (bf16[2,128,2048]{2,1,0:T(8,128)(2,1)}, bf16[2,128,2048]{2,1,0:T(8,128)(2,1)S(1)}, u32[]{:S(2)}, u32[]{:S(2)}) collective-permute-start(bf16[2,128,2048]{2,1,0:T(8,128)(2,1)} %bitcast.283), channel_id=1, source_target_pairs={{0,1},{1,0},{2,3},{3,2},{4,5},{5,4},{6,7},{7,6},{8,9},{9,8},{10,11... | collective-permute-start | bytes 3145736 | tf_op jit(solution)/shard_map/ppermute | solution.py:31
  553.7 24.2 %collective-permute-start.33 = (bf16[2,128,2048]{2,1,0:T(8,128)(2,1)S(1)}, bf16[2,128,2048]{2,1,0:T(8,128)(2,1)S(1)}, u32[]{:S(2)}, u32[]{:S(2)}) collective-permute-start(bf16[2,128,2048]{2,1,0:T(8,128)(2,1)S(1)} %fusion.16), channel_id=1, source_target_pairs={{0,2},{1,3},{2,4},{3,5},{4,6},{5,7},{6,0},{7,1},{8,10},{9,11},{10,... | collective-permute-start | bytes 3145736 | tf_op jit(solution)/shard_map/ppermute | solution.py:31
  553.8 24.2 %collective-permute-start.31 = (bf16[2,128,2048]{2,1,0:T(8,128)(2,1)S(1)}, bf16[2,128,2048]{2,1,0:T(8,128)(2,1)S(1)}, u32[]{:S(2)}, u32[]{:S(2)}) collective-permute-start(bf16[2,128,2048]{2,1,0:T(8,128)(2,1)S(1)} %bitcast.282), channel_id=1, source_target_pairs={{0,1},{1,0},{2,3},{3,2},{4,5},{5,4},{6,7},{7,6},{8,9},{9,8},{10,11... | collective-permute-start | bytes 3145736 | tf_op jit(solution)/shard_map/ppermute | solution.py:31
  579.9 25.0 %collective-permute-start.35 = (bf16[2,128,2048]{2,1,0:T(8,128)(2,1)}, bf16[2,128,2048]{2,1,0:T(8,128)(2,1)S(1)}, u32[]{:S(2)}, u32[]{:S(2)}) collective-permute-start(bf16[2,128,2048]{2,1,0:T(8,128)(2,1)} %bitcast.281), channel_id=1, source_target_pairs={{0,1},{1,0},{2,3},{3,2},{4,5},{5,4},{6,7},{7,6},{8,9},{9,8},{10,11... | collective-permute-start | bytes 3145736 | tf_op jit(solution)/shard_map/ppermute | solution.py:31
  583.7 24.7 %collective-permute-start.36 = (bf16[2,128,2048]{2,1,0:T(8,128)(2,1)S(1)}, bf16[2,128,2048]{2,1,0:T(8,128)(2,1)S(1)}, u32[]{:S(2)}, u32[]{:S(2)}) collective-permute-start(bf16[2,128,2048]{2,1,0:T(8,128)(2,1)S(1)} %add_convert_fusion.8), channel_id=1, source_target_pairs={{0,2},{1,3},{2,4},{3,5},{4,6},{5,7},{6,0},{7,1},{8,10},{9,11},{10,... | collective-permute-start | bytes 3145736 | tf_op jit(solution)/shard_map/ppermute | solution.py:31
  609.4 25.9 %collective-permute-start.34 = (bf16[2,128,2048]{2,1,0:T(8,128)(2,1)}, bf16[2,128,2048]{2,1,0:T(8,128)(2,1)S(1)}, u32[]{:S(2)}, u32[]{:S(2)}) collective-permute-start(bf16[2,128,2048]{2,1,0:T(8,128)(2,1)} %bitcast.280), channel_id=1, source_target_pairs={{0,1},{1,0},{2,3},{3,2},{4,5},{5,4},{6,7},{7,6},{8,9},{9,8},{10,11... | collective-permute-start | bytes 3145736 | tf_op jit(solution)/shard_map/ppermute | solution.py:31
  612.7 22.7 %collective-permute-start.37 = (bf16[2,128,2048]{2,1,0:T(8,128)(2,1)S(1)}, bf16[2,128,2048]{2,1,0:T(8,128)(2,1)S(1)}, u32[]{:S(2)}, u32[]{:S(2)}) collective-permute-start(bf16[2,128,2048]{2,1,0:T(8,128)(2,1)S(1)} %add_convert_fusion.7), channel_id=1, source_target_pairs={{0,2},{1,3},{2,4},{3,5},{4,6},{5,7},{6,0},{7,1},{8,10},{9,11},{10,... | collective-permute-start | bytes 3145736 | tf_op jit(solution)/shard_map/ppermute | solution.py:31
  650.6 28.9 %all-to-all-start.1 = ((bf16[8,2,128,256]{3,2,1,0:T(8,128)(2,1)}), bf16[8,2,128,256]{3,2,1,0:T(8,128)(2,1)}, u32[]{:S(2)}, u32[]{:S(2)}) async-start(bf16[8,2,128,256]{3,2,1,0:T(8,128)(2,1)} %bitcast.188), calls=%async_computation.1 | async-start | bytes 2097152 | tf_op jit(solution)/shard_map/all_to_all | solution.py:814
  655.4 284.4 %reduce-scatter.6.cloned.1.call-start = ((), (), s32[]{:S(2)}) async-start(), calls=%async_computation.13 | async-start | bytes 20971520 | tf_op jit(solution)/shard_map/reduce_scatter | solution.py:800
  682.4 66.2 %all-to-all-start.2 = ((bf16[8,2,128,256]{3,2,1,0:T(8,128)(2,1)}), bf16[8,2,128,256]{3,2,1,0:T(8,128)(2,1)}, u32[]{:S(2)}, u32[]{:S(2)}) async-start(bf16[8,2,128,256]{3,2,1,0:T(8,128)(2,1)} %bitcast.187), calls=%async_computation.2 | async-start | bytes 2097152 | tf_op jit(solution)/shard_map/all_to_all | solution.py:814
  688.3 303.0 %reduce-scatter.8.cloned.1.call-start = ((), (), s32[]{:S(2)}) async-start(), calls=%async_computation.14 | async-start | bytes 20971520 | tf_op jit(solution)/shard_map/reduce_scatter | solution.py:800
  688.4 60.2 %collective-permute-start.38 = (bf16[2,128,2048]{2,1,0:T(8,128)(2,1)}, bf16[2,128,2048]{2,1,0:T(8,128)(2,1)}, u32[]{:S(2)}, u32[]{:S(2)}) collective-permute-start(bf16[2,128,2048]{2,1,0:T(8,128)(2,1)} %after.102), channel_id=1, source_target_pairs={{0,1},{1,0},{2,3},{3,2},{4,5},{5,4},{6,7},{7,6},{8,9},{9,8},{10,11... | collective-permute-start | bytes 3145736 | tf_op jit(solution)/shard_map/ppermute | solution.py:31
  694.7 87.1 %collective-permute-start.41 = (bf16[2,128,2048]{2,1,0:T(8,128)(2,1)}, bf16[2,128,2048]{2,1,0:T(8,128)(2,1)}, u32[]{:S(2)}, u32[]{:S(2)}) collective-permute-start(bf16[2,128,2048]{2,1,0:T(8,128)(2,1)} %bitcast.278), channel_id=1, source_target_pairs={{0,1},{1,0},{2,3},{3,2},{4,5},{5,4},{6,7},{7,6},{8,9},{9,8},{10,11... | collective-permute-start | bytes 3145736 | tf_op jit(solution)/shard_map/ppermute | solution.py:31
  752.4 29.5 %collective-permute-start.40 = (bf16[2,128,2048]{2,1,0:T(8,128)(2,1)}, bf16[2,128,2048]{2,1,0:T(8,128)(2,1)S(1)}, u32[]{:S(2)}, u32[]{:S(2)}) collective-permute-start(bf16[2,128,2048]{2,1,0:T(8,128)(2,1)} %fusion.12), channel_id=1, source_target_pairs={{0,2},{1,3},{2,4},{3,5},{4,6},{5,7},{6,0},{7,1},{8,10},{9,11},{10,... | collective-permute-start | bytes 3145736 | tf_op jit(solution)/shard_map/ppermute | solution.py:31
  754.0 27.9 %collective-permute-start.39 = (bf16[2,128,2048]{2,1,0:T(8,128)(2,1)}, bf16[2,128,2048]{2,1,0:T(8,128)(2,1)S(1)}, u32[]{:S(2)}, u32[]{:S(2)}) collective-permute-start(bf16[2,128,2048]{2,1,0:T(8,128)(2,1)} %after.105), channel_id=1, source_target_pairs={{0,1},{1,0},{2,3},{3,2},{4,5},{5,4},{6,7},{7,6},{8,9},{9,8},{10,11... | collective-permute-start | bytes 3145736 | tf_op jit(solution)/shard_map/ppermute | solution.py:31
  757.3 24.6 %collective-permute-start.43 = (f32[2,128]{1,0:T(2,128)S(1)}, f32[2,128]{1,0:T(2,128)S(1)}, u32[]{:S(2)}, u32[]{:S(2)}) collective-permute-start(f32[2,128]{1,0:T(2,128)S(1)} %add.371), channel_id=1, source_target_pairs={{0,16},{8,24},{16,0},{24,8},{1,17},{9,25},{17,1},{25,9},{2,18},{10... | collective-permute-start | bytes 3080 | tf_op jit(solution)/shard_map/ppermute | solution.py:851
  783.2 64.2 %collective-permute-start.49 = (bf16[2,128,2048]{2,1,0:T(8,128)(2,1)}, bf16[2,128,2048]{2,1,0:T(8,128)(2,1)S(1)}, u32[]{:S(2)}, u32[]{:S(2)}) collective-permute-start(bf16[2,128,2048]{2,1,0:T(8,128)(2,1)} %bitcast.72), channel_id=1, source_target_pairs={{0,1},{1,0},{2,3},{3,2},{4,5},{5,4},{6,7},{7,6},{8,9},{9,8},{10,11... | collective-permute-start | bytes 3145736 | tf_op jit(solution)/shard_map/ppermute | solution.py:31
  783.8 63.6 %collective-permute-start.50 = (bf16[2,128,2048]{2,1,0:T(8,128)(2,1)}, bf16[2,128,2048]{2,1,0:T(8,128)(2,1)S(1)}, u32[]{:S(2)}, u32[]{:S(2)}) collective-permute-start(bf16[2,128,2048]{2,1,0:T(8,128)(2,1)} %bitcast.279), channel_id=1, source_target_pairs={{0,1},{1,0},{2,3},{3,2},{4,5},{5,4},{6,7},{7,6},{8,9},{9,8},{10,11... | collective-permute-start | bytes 3145736 | tf_op jit(solution)/shard_map/ppermute | solution.py:31
  789.0 54.1 %collective-permute-start.46 = (bf16[512,1152]{1,0:T(8,128)(2,1)}, bf16[512,1152]{1,0:T(8,128)(2,1)}, u32[]{:S(2)}, u32[]{:S(2)}) collective-permute-start(bf16[512,1152]{1,0:T(8,128)(2,1)} %add_convert_fusion.2), channel_id=1, source_target_pairs={{0,16},{8,24},{16,0},{24,8},{1,17},{9,25},{17,1},{25,9},{2,18},{10... | collective-permute-start | bytes 3538952 | tf_op jit(solution)/shard_map/ppermute | solution.py:31
  791.9 55.6 %collective-permute-start.47 = (bf16[2,128,2048]{2,1,0:T(8,128)(2,1)}, bf16[2,128,2048]{2,1,0:T(8,128)(2,1)}, u32[]{:S(2)}, u32[]{:S(2)}) collective-permute-start(bf16[2,128,2048]{2,1,0:T(8,128)(2,1)} %add_convert_fusion.6), channel_id=1, source_target_pairs={{0,2},{1,3},{2,4},{3,5},{4,6},{5,7},{6,0},{7,1},{8,10},{9,11},{10,... | collective-permute-start | bytes 3145736 | tf_op jit(solution)/shard_map/ppermute | solution.py:31
  794.7 52.8 %collective-permute-start.48 = (bf16[2,128,2048]{2,1,0:T(8,128)(2,1)}, bf16[2,128,2048]{2,1,0:T(8,128)(2,1)}, u32[]{:S(2)}, u32[]{:S(2)}) collective-permute-start(bf16[2,128,2048]{2,1,0:T(8,128)(2,1)} %fusion.10), channel_id=1, source_target_pairs={{0,2},{1,3},{2,4},{3,5},{4,6},{5,7},{6,0},{7,1},{8,10},{9,11},{10,... | collective-permute-start | bytes 3145736 | tf_op jit(solution)/shard_map/ppermute | solution.py:31
  848.8 54.8 %all-to-all-start.3 = ((bf16[8,64,1152]{2,1,0:T(8,128)(2,1)}), bf16[8,64,1152]{2,1,0:T(8,128)(2,1)S(1)}, u32[]{:S(2)}, u32[]{:S(2)}) async-start(bf16[8,64,1152]{2,1,0:T(8,128)(2,1)} %bitcast.74), calls=%async_computation.3 | async-start | bytes 2359296 | tf_op jit(solution)/shard_map/all_to_all | solution.py:879
  852.9 37.2 %collective-permute-start.52 = (bf16[2,128,2048]{2,1,0:T(8,128)(2,1)}, bf16[2,128,2048]{2,1,0:T(8,128)(2,1)}, u32[]{:S(2)}, u32[]{:S(2)}) collective-permute-start(bf16[2,128,2048]{2,1,0:T(8,128)(2,1)} %bitcast.277), channel_id=1, source_target_pairs={{0,1},{1,0},{2,3},{3,2},{4,5},{5,4},{6,7},{7,6},{8,9},{9,8},{10,11... | collective-permute-start | bytes 3145736 | tf_op jit(solution)/shard_map/ppermute | solution.py:31
  857.7 40.4 %collective-permute-start.51 = (bf16[2,128,2048]{2,1,0:T(8,128)(2,1)}, bf16[2,128,2048]{2,1,0:T(8,128)(2,1)S(1)}, u32[]{:S(2)}, u32[]{:S(2)}) collective-permute-start(bf16[2,128,2048]{2,1,0:T(8,128)(2,1)} %add_convert_fusion.5), channel_id=1, source_target_pairs={{0,2},{1,3},{2,4},{3,5},{4,6},{5,7},{6,0},{7,1},{8,10},{9,11},{10,... | collective-permute-start | bytes 3145736 | tf_op jit(solution)/shard_map/ppermute | solution.py:31
  859.2 30.9 %collective-permute-start.53 = (f32[2,128]{1,0:T(2,128)S(1)}, f32[2,128]{1,0:T(2,128)S(1)}, u32[]{:S(2)}, u32[]{:S(2)}) collective-permute-start(f32[2,128]{1,0:T(2,128)S(1)} %add.380), channel_id=1, source_target_pairs={{0,1},{1,0},{2,3},{3,2},{4,5},{5,4},{6,7},{7,6},{8,9},{9,8},{10,11... | collective-permute-start | bytes 3080 | tf_op jit(solution)/shard_map/ppermute | solution.py:851
  908.9 37.8 %collective-permute-start.58 = (bf16[2,128,2048]{2,1,0:T(8,128)(2,1)}, bf16[2,128,2048]{2,1,0:T(8,128)(2,1)S(1)}, u32[]{:S(2)}, u32[]{:S(2)}) collective-permute-start(bf16[2,128,2048]{2,1,0:T(8,128)(2,1)} %add_convert_fusion.3), channel_id=1, source_target_pairs={{0,2},{1,3},{2,4},{3,5},{4,6},{5,7},{6,0},{7,1},{8,10},{9,11},{10,... | collective-permute-start | bytes 3145736 | tf_op jit(solution)/shard_map/ppermute | solution.py:31
  908.9 44.7 %collective-permute-start.54 = (bf16[2,128,2048]{2,1,0:T(8,128)(2,1)}, bf16[2,128,2048]{2,1,0:T(8,128)(2,1)S(1)}, u32[]{:S(2)}, u32[]{:S(2)}) collective-permute-start(bf16[2,128,2048]{2,1,0:T(8,128)(2,1)} %after.127), channel_id=1, source_target_pairs={{0,1},{1,0},{2,3},{3,2},{4,5},{5,4},{6,7},{7,6},{8,9},{9,8},{10,11... | collective-permute-start | bytes 3145736 | tf_op jit(solution)/shard_map/ppermute | solution.py:31
  910.3 45.5 %collective-permute-start.56 = (bf16[2,128,2048]{2,1,0:T(8,128)(2,1)}, bf16[2,128,2048]{2,1,0:T(8,128)(2,1)S(1)}, u32[]{:S(2)}, u32[]{:S(2)}) collective-permute-start(bf16[2,128,2048]{2,1,0:T(8,128)(2,1)} %after.129), channel_id=1, source_target_pairs={{0,1},{1,0},{2,3},{3,2},{4,5},{5,4},{6,7},{7,6},{8,9},{9,8},{10,11... | collective-permute-start | bytes 3145736 | tf_op jit(solution)/shard_map/ppermute | solution.py:31
  914.5 42.1 %collective-permute-start.55 = (bf16[2,128,2048]{2,1,0:T(8,128)(2,1)}, bf16[2,128,2048]{2,1,0:T(8,128)(2,1)}, u32[]{:S(2)}, u32[]{:S(2)}) collective-permute-start(bf16[2,128,2048]{2,1,0:T(8,128)(2,1)} %add_convert_fusion.4), channel_id=1, source_target_pairs={{0,2},{1,3},{2,4},{3,5},{4,6},{5,7},{6,0},{7,1},{8,10},{9,11},{10,... | collective-permute-start | bytes 3145736 | tf_op jit(solution)/shard_map/ppermute | solution.py:31
  919.6 34.0 %collective-permute-start.57 = (f32[2,128]{1,0:T(2,128)S(1)}, f32[2,128]{1,0:T(2,128)S(1)}, u32[]{:S(2)}, u32[]{:S(2)}) collective-permute-start(f32[2,128]{1,0:T(2,128)S(1)} %add.383), channel_id=1, source_target_pairs={{0,2},{1,3},{2,0},{3,1},{4,6},{5,7},{6,4},{7,5},{8,10},{9,11},{10,... | collective-permute-start | bytes 3080 | tf_op jit(solution)/shard_map/ppermute | solution.py:851
  (131 other events, 844.8 us)
Sparse Core Ops, SparseCore 0:
  11.2 34.1 all-gather.5
  47.0 58.2 all-gather.7
  106.9 105.9 all-gather.9
  214.2 105.9 all-gather.11
  321.6 105.9 all-gather.13
  580.0 128.2 reduce-scatter.3
  711.1 151.4 reduce-scatter.5
  865.2 126.1 reduce-scatter.7

commit v7 on v6

--- a/solution.py
+++ b/solution.py
@@ -59,10 +59,10 @@
     return moved
 
 
-def ring_gather(value, axis, work=None, split=False):
+def ring_gather(value, axis, work=None, split=False, blocks=(), stop=None):
     outer, inner = sizes(axis)
-    blocks, arrived = [], []
-    for a in range(outer):
+    blocks, arrived = list(blocks), []
+    for a in range(len(blocks) // inner, outer if stop is None else stop):
         row = [value]
         for b in range(1, inner):
             row.append(shift(row[-1], axis, outer, inner, 0, 1))
@@ -80,7 +80,7 @@
             moved = together([f(arrived) for f in work[a : a + 1] if f], *moved)
         blocks += [value] + (moved if last else moved[: inner - 1])
         value, arrived = moved[-1], moved
-    return blocks
+    return blocks if stop is None else (blocks, value)
 
 
 def row_move(parts, a, axis):
@@ -693,6 +693,10 @@
 
     inverse_seq = jnp.argsort(seq_order)
     o_heads = reorder(o_heads, inverse_seq, axis=0)
+    g_blocks, g_next = ring_gather(
+        after(cotangent, packed), "seq", (lambda _: qkv, lambda _: o_heads), True, stop=2
+    )
+    o_heads = after(o_heads, g_next)
     o_back = lax.all_to_all(o_heads, "seq", split_axis=0, concat_axis=0, tiled=True)
     o_rows = jnp.moveaxis(o_back, 0, 2).reshape(tokens, D)
 
@@ -732,44 +736,28 @@
     def combined(acts, banks, h, scaled, ties=()):
         return combine(acts, banks, slot_columns, slots, weights, h, ns // 2, scaled, ties)
 
-    pair = local_experts // 2
-
-    def take_work(first):
-        def work(ties):
-            before = done.get("takes", ())
-            done["takes"] = dispatch(
-                h_blocks, slots, weights, w_gate, capacity, False, ties, first, pair, before
-            )
-            return done["takes"][0]
-
-        return work
-
-    g_blocks = ring_gather(
-        after(cotangent, h_blocks[-1]), "seq", (None, None, take_work(0), take_work(pair)), True
-    )
-    taken, gate_act = done["takes"]
+    g_blocks = ring_gather(after(g_next, h_blocks[-1]), "seq", (), True, g_blocks)
 
     def grad_work(_):
         grad_rows, grad_hidden = dispatch(g_blocks, slots, weights, w_down, capacity, True)
         return keep(grad_rows=grad_rows, grad_hidden=grad_hidden)
 
-    def act_work(ties):
-        acts = activate(taken, gate_act, done["grad_hidden"], w_up, ties)
-        return keep(tail=acts[0], acts=acts)
-
-    def first_work(ties):
-        first = combined(done["acts"][1:], (w_gate, w_up), 0, False, ties)
-        return keep(tail=first[0], first=first)
+    def take_work(_):
+        taken, gate_act = dispatch(
+            h_blocks, slots, weights, w_gate, capacity, False, (done["grad_rows"],)
+        )
+        return keep(taken=taken, gate_act=gate_act)
 
     o_all = ring_gather(
-        after(o_heads.reshape(group * micro, width), g_blocks[-1]),
-        "seq",
-        (grad_work, None, act_work, first_work),
-    )
-    first = done["first"]
-    grad_rows = done["grad_rows"]
-    hidden, grad_gate_act, grad_up_act = done["acts"]
-    second = combined((grad_gate_act, grad_up_act), (w_gate, w_up), 1, False, (first[0], o_all[-1]))
+        after(o_heads.reshape(group * micro, width), g_blocks[-1]), "seq", (grad_work, take_work), True
+    )
+    o_all = o_all[:-2] + [jnp.concatenate(o_all[-2:], axis=0)] if len(o_all) > ns else o_all
+    grad_rows, taken = done["grad_rows"], done["taken"]
+    hidden, grad_gate_act, grad_up_act = activate(
+        taken, done["gate_act"], done["grad_hidden"], w_up, (o_all[-1],)
+    )
+    first = combined((grad_gate_act, grad_up_act), (w_gate, w_up), 0, False)
+    second = combined((grad_gate_act, grad_up_act), (w_gate, w_up), 1, False, (first[0],))
 
     def down_work(ties):
         return keep(whole_down=bank_grad(grad_rows, hidden, ties))

time: 1010 us -> 1010 us (level)
  local copies, waits for them, and re-layouts: 115 us -> 102 us
    unnamed x266 -> x184, local copies, waits for them, and re-layouts: 67.7 us -> 46.2 us
    pallas_call x12 -> x11, Pallas kernels: 289 us -> 284 us  [call(): pl.pallas_call(run, grid=grid, in_specs=[spec for _, spec in ins] + [pl.B...]
    ppermute x55 -> x56, starting transfers between devices: 56.9 us -> 52.3 us  [shift(): return lax.ppermute(value, axis, pairs)]
    ppermute x55 -> x56, waiting for transfers between devices: 278 us -> 278 us  [shift(): return lax.ppermute(value, axis, pairs)]
  transfers between devices with their start and end apart: 71 -> 72, of which waited for: 29 -> 32; matrix products, arithmetic and copies ran while one was open for 15% -> 17% of each run, Pallas kernels for 36% -> 29%
where the time goes in v7:
time: 1010 us; the launch traced here: 999 us
  Pallas kernels  354 us (35%)
  waiting for transfers between devices  316 us (31%)
  local copies, waits for them, and re-layouts  102 us (10%)
  other arithmetic  88.9 us (9%)
  starting transfers between devices  72.6 us (7%)
  blocking collectives  27.7 us (3%)
  matrix products  20.9 us (2%)
  between operations  15.9 us (2%)
    pallas_call x11, Pallas kernels, call(): pl.pallas_call(run, grid=grid, in_specs=[spec for _, spec in ins] + [pl.B...  284 us
    ppermute x56, waiting for transfers between devices, shift(): return lax.ppermute(value, axis, pairs)  278 us
    ppermute x56, starting transfers between devices, shift(): return lax.ppermute(value, axis, pairs)  52.3 us
    unnamed x184, local copies, waits for them, and re-layouts  46.2 us
    pallas_call x1, Pallas kernels, attend_back(): pl.pallas_call(lambda *refs: attend_back_kernel(tile, *refs[:7], *refs[-2...  33.3 us
    all_to_all x1, blocking collectives, body(): lax.all_to_all(o_heads, 'seq', split_axis=0, concat_axis=0, tiled=True)  27.7 us
    reduce_scatter x3, waiting for transfers between devices, bank_sum(): lax.psum_scatter(whole, 'fsdp', scatter_dimension=1, tiled=True).astype(f32)  22.8 us
    pallas_call x1, Pallas kernels, proj_grads(): pl.pallas_call(run, grid_spec=pltpu.PrefetchScalarGridSpec(num_scalar_pre...  20.8 us
  transfers between devices with their start and end apart: 72, of which 32 were waited for; matrix products, arithmetic and copies ran while one was open for 17% of the time, Pallas kernels for 29%

profile of v7, /device:TPU:0, one launch (start us, length us, event | category | flops | bytes accessed | tf_op | source)
XLA Modules:
  0.0 998.7 jit_solution(634458815875493529)
XLA Ops:
  17.0 3.0 collective-permute-start.1
  21.5 25.3 %collective-permute-done.1 = bf16[2,128,2176]{2,1,0:T(8,128)(2,1)S(1)} collective-permute-done((bf16[2,128,2176]{2,1,0:T(8,128)(2,1)}, bf16[2,128,2176]{2,1,0:T(8,128)(2,1)S(1)}, u32[]{:S(2)}, u32[]{:S(2)}) %collective-permute-start.1) | collective-permute-done | bytes 1114144 | tf_op jit(solution)/shard_map/ppermute | solution.py:31
  51.6 22.7 %collective-permute-done.3 = bf16[2,128,2176]{2,1,0:T(8,128)(2,1)S(1)} collective-permute-done((bf16[2,128,2176]{2,1,0:T(8,128)(2,1)S(1)}, bf16[2,128,2176]{2,1,0:T(8,128)(2,1)S(1)}, u32[]{:S(2)}, u32[]{:S(2)}) %collective-permute-start.3) | collective-permute-done | bytes 1114144 | tf_op jit(solution)/shard_map/ppermute | solution.py:31
  80.1 21.6 %collective-permute-done.5 = bf16[2,128,2176]{2,1,0:T(8,128)(2,1)S(1)} collective-permute-done((bf16[2,128,2176]{2,1,0:T(8,128)(2,1)S(1)}, bf16[2,128,2176]{2,1,0:T(8,128)(2,1)S(1)}, u32[]{:S(2)}, u32[]{:S(2)}) %collective-permute-start.5) | collective-permute-done | bytes 1114144 | tf_op jit(solution)/shard_map/ppermute | solution.py:31
  105.2 8.1 collective-permute-done.6
  117.7 6.5 fusion
  126.2 5.3 fusion.2
  131.5 8.0 fusion.4.refs_0_.refs_1_
  149.9 16.5 %attend.1 = bf16[8,2,128,256]{3,2,1,0:T(8,128)(2,1)S(1)} custom-call(bf16[8,2,128,768]{3,2,1,0:T(8,128)(2,1)S(1)} %copy-done.2, f32[1024,128]{1,0:T(8,128)S(1)} %get-tuple-element.112.refs_1_.refs_2_, f32[1024,128]{1,0:T(8,128)S(1)} %get-tuple-element.111.refs_2_.refs_3_, s32[2,1,1024]{2,1,0:T(1,128)S(1)} %bitcast.192, s32[2,1024,1]{2,1,0:T(8,128)S(1)} %copy-done.4, ...), custom_call_target="tpu_custom_call" | custom-call | flops 1 | bytes 1 | tf_op jit(solution)/shard_map/attend/pallas_call | solution.py:281
  169.0 2.8 gather_fusion.1
  171.8 27.7 %all_to_all.20 = bf16[8,2,128,256]{3,2,1,0:T(8,128)(2,1)S(1)} all-to-all(bf16[8,2,128,256]{3,2,1,0:T(8,128)(2,1)} %after.76), channel_id=1, replica_groups=mesh['fsdp'=4,'seq'=8] {'seq'}, dimensions={0} | all-to-all | bytes 2097152 | tf_op jit(solution)/shard_map/all_to_all | solution.py:700
  201.4 6.4 multiply_reduce_fusion.3
  211.4 20.6 %collective-permute-done.12.refs_0_ = bf16[2,128,2048]{2,1,0:T(8,128)(2,1)} collective-permute-done((bf16[2,128,2048]{2,1,0:T(8,128)(2,1)S(1)}, bf16[2,128,2048]{2,1,0:T(8,128)(2,1)}, u32[]{:S(2)}, u32[]{:S(2)}) %collective-permute-start.12) | collective-permute-done | bytes 1048608 | tf_op jit(solution)/shard_map/ppermute | solution.py:31
  232.1 3.2 collective-permute-done.13.refs_1_.refs_0_
  236.4 20.7 %collective-permute-done.14.refs_0_ = bf16[2,128,2048]{2,1,0:T(8,128)(2,1)} collective-permute-done((bf16[2,128,2048]{2,1,0:T(8,128)(2,1)}, bf16[2,128,2048]{2,1,0:T(8,128)(2,1)}, u32[]{:S(2)}, u32[]{:S(2)}) %collective-permute-start.14) | collective-permute-done | bytes 1048608 | tf_op jit(solution)/shard_map/ppermute | solution.py:31
  257.1 3.0 collective-permute-done.15.refs_1_.refs_0_
  260.6 20.3 %collective-permute-done.16.refs_0_ = bf16[2,128,2048]{2,1,0:T(8,128)(2,1)} collective-permute-done((bf16[2,128,2048]{2,1,0:T(8,128)(2,1)}, bf16[2,128,2048]{2,1,0:T(8,128)(2,1)}, u32[]{:S(2)}, u32[]{:S(2)}) %collective-permute-start.16) | collective-permute-done | bytes 1048608 | tf_op jit(solution)/shard_map/ppermute | solution.py:31
  286.8 8.7 collective-permute-done.18.refs_0_
  295.4 4.7 collective-permute-done.19.refs_1_.refs_0_
  300.1 16.7 %collective-permute-done.20.refs_0_ = bf16[2,128,2048]{2,1,0:T(8,128)(2,1)} collective-permute-done((bf16[2,128,2048]{2,1,0:T(8,128)(2,1)}, bf16[2,128,2048]{2,1,0:T(8,128)(2,1)}, u32[]{:S(2)}, u32[]{:S(2)}) %collective-permute-start.20) | collective-permute-done | bytes 1048608 | tf_op jit(solution)/shard_map/ppermute | solution.py:31
  316.8 3.5 collective-permute-done.21.refs_1_.refs_0_
  329.3 8.0 collective-permute-done.22.refs_0_
  342.9 3.1 slice_add_fusion
  349.0 34.1 %dispatch.2 = (bf16[4,2,384,2048]{3,2,1,0:T(8,128)(2,1)}, f32[4,2,384,1024]{3,2,1,0:T(8,128)}) custom-call(bf16[256,2048]{1,0:T(8,128)(2,1)} %bitcast.206, bf16[256,2048]{1,0:T(8,128)(2,1)} %bitcast.205, bf16[256,2048]{1,0:T(8,128)(2,1)} %bitcast.204, bf16[256,2048]{1,0:T(8,128)(2,1)} %bitcast.35.refs_3_, bf16[256,2048]{1,0:T(8,128)(2,1)} %bitcast.36.refs_4_, ...), custom_call_target="tpu_custom_call" | custom-call | flops 1 | bytes 1 | tf_op jit(solution)/shard_map/dispatch/pallas_call | solution.py:427
  383.6 33.0 %dispatch.3 = (bf16[4,2,384,2048]{3,2,1,0:T(8,128)(2,1)}, f32[4,2,384,1024]{3,2,1,0:T(8,128)}) custom-call(bf16[256,2048]{1,0:T(8,128)(2,1)} %copy-done.50, bf16[256,2048]{1,0:T(8,128)(2,1)} %bitcast.17.refs_1_, bf16[256,2048]{1,0:T(8,128)(2,1)} %bitcast.18.refs_2_, bf16[256,2048]{1,0:T(8,128)(2,1)} %bitcast.19.refs_3_, bf16[256,2048]{1,0:T(8,128)(2,1)} %bitcast.20.refs_4_, ...), custom_call_target="tpu_custom_call" | custom-call | flops 1 | bytes 1 | tf_op jit(solution)/shard_map/dispatch/pallas_call | solution.py:427
  419.2 18.6 %collective-permute-done.28.refs_1_.refs_0_ = bf16[2048,256]{1,0:T(8,128)(2,1)} collective-permute-done((bf16[2048,256]{1,0:T(8,128)(2,1)}, bf16[2048,256]{1,0:T(8,128)(2,1)}, u32[]{:S(2)}, u32[]{:S(2)}) %collective-permute-start.28) | collective-permute-done | bytes 1048608 | tf_op jit(solution)/shard_map/ppermute | solution.py:31
  442.6 3.8 collective-permute-start.31
  446.4 3.5 collective-permute-done.30.refs_0_
  449.9 4.0 collective-permute-done.31.refs_1_.refs_0_
  453.8 2.6 copy.268.refs_4_.refs_2_
  458.7 32.2 %activate.1 = (bf16[4,2,384,1024]{3,2,1,0:T(8,128)(2,1)}, bf16[4,2,384,1024]{3,2,1,0:T(8,128)(2,1)}, bf16[4,2,384,1024]{3,2,1,0:T(8,128)(2,1)}) custom-call(bf16[4,2,384,2048]{3,2,1,0:T(8,128)(2,1)} %get-tuple-element.53.refs_1_.refs_0_, f32[4,2,384,1024]{3,2,1,0:T(8,128)} %get-tuple-element.54.refs_1_, f32[4,2,384,1024]{3,2,1,0:T(8,128)} %get-tuple-element.55.refs_2_, ...), custom_call_target="tpu_custom_call" | custom-call | flops 1 | bytes 1 | tf_op jit(solution)/shard_map/activate/pallas_call | solution.py:427
  490.9 27.7 %combine.4 = (bf16[256,2048]{1,0:T(8,128)(2,1)}, bf16[256,2048]{1,0:T(8,128)(2,1)}, bf16[256,2048]{1,0:T(8,128)(2,1)}, bf16[256,2048]{1,0:T(8,128)(2,1)}) custom-call(bf16[4,2,384,1024]{3,2,1,0:T(8,128)(2,1)} %get-tuple-element.57.refs_0_.refs_1_, bf16[4,2,384,1024]{3,2,1,0:T(8,128)(2,1)} %get-tuple-element.58.refs_1_, ...), custom_call_target="tpu_custom_call" | custom-call | flops 1 | bytes 1 | tf_op jit(solution)/shard_map/combine/pallas_call | solution.py:427
  518.7 27.9 %combine.5 = (bf16[256,2048]{1,0:T(8,128)(2,1)}, bf16[256,2048]{1,0:T(8,128)(2,1)}, bf16[256,2048]{1,0:T(8,128)(2,1)}, bf16[256,2048]{1,0:T(8,128)(2,1)}) custom-call(bf16[4,2,384,1024]{3,2,1,0:T(8,128)(2,1)} %get-tuple-element.57.refs_0_.refs_1_, bf16[4,2,384,1024]{3,2,1,0:T(8,128)(2,1)} %get-tuple-element.58.refs_1_, ...), custom_call_target="tpu_custom_call" | custom-call | flops 1 | bytes 1 | tf_op jit(solution)/shard_map/combine/pallas_call | solution.py:427
  552.4 24.1 %bank_grad.3.refs_1_.refs_0_ = bf16[4,2048,1024]{2,1,0:T(8,128)(2,1)} custom-call(bf16[4,2,384,2048]{3,2,1,0:T(8,128)(2,1)} %get-tuple-element.52.refs_12_.refs_1_.refs_0_, bf16[4,2,384,1024]{3,2,1,0:T(8,128)(2,1)} %get-tuple-element.56.refs_1_.refs_0_, bf16[2,128,2048]{2,1,0:T(8,128)(2,1)} %after.99.refs_2_), custom_call_target="tpu_custom_call" | custom-call | flops 1 | bytes 1 | tf_op jit(solution)/shard_map/bank_grad/pallas_call | solution.py:427
  579.6 21.2 %combine.6 = (bf16[256,2048]{1,0:T(8,128)(2,1)}, bf16[256,2048]{1,0:T(8,128)(2,1)}, bf16[256,2048]{1,0:T(8,128)(2,1)}, bf16[256,2048]{1,0:T(8,128)(2,1)}) custom-call(bf16[4,2,384,1024]{3,2,1,0:T(8,128)(2,1)} %get-tuple-element.56.refs_1_.refs_0_, bf16[4,2048,1024]{2,1,0:T(8,128)(2,1)} %all-gather.12.cloned.1.call-done.refs_11_.refs_1_, ...), custom_call_target="tpu_custom_call" | custom-call | flops 1 | bytes 1 | tf_op jit(solution)/shard_map/combine/pallas_call | solution.py:427
  605.0 21.1 %combine.7 = (bf16[256,2048]{1,0:T(8,128)(2,1)}, bf16[256,2048]{1,0:T(8,128)(2,1)}, bf16[256,2048]{1,0:T(8,128)(2,1)}, bf16[256,2048]{1,0:T(8,128)(2,1)}) custom-call(bf16[4,2,384,1024]{3,2,1,0:T(8,128)(2,1)} %get-tuple-element.56.refs_1_.refs_0_, bf16[4,2048,1024]{2,1,0:T(8,128)(2,1)} %all-gather.12.cloned.1.call-done.refs_11_.refs_1_, ...), custom_call_target="tpu_custom_call" | custom-call | flops 1 | bytes 1 | tf_op jit(solution)/shard_map/combine/pallas_call | solution.py:427
  631.5 6.3 convolution_convert_fusion.refs_2_
  639.3 6.0 all-to-all-start.1
  645.3 24.9 %bank_grad.4.refs_1_.refs_0_ = bf16[4,2048,1024]{2,1,0:T(8,128)(2,1)} custom-call(bf16[4,2,384,2048]{3,2,1,0:T(8,128)(2,1)} %get-tuple-element.53.refs_1_.refs_0_, bf16[4,2,384,1024]{3,2,1,0:T(8,128)(2,1)} %get-tuple-element.57.refs_0_.refs_1_, bf16[256,2048]{1,0:T(8,128)(2,1)} %copy-done.51), custom_call_target="tpu_custom_call" | custom-call | flops 1 | bytes 1 | tf_op jit(solution)/shard_map/bank_grad/pallas_call | solution.py:427
  673.0 5.6 all-to-all-start.2
  682.1 2.9 gather_fusion.2
  690.2 33.3 %attend_back.1 = (bf16[8,2,128,768]{3,2,1,0:T(8,128)(2,1)S(1)}, f32[4,2,128]{2,1,0:T(2,128)S(1)}) custom-call(bf16[8,2,128,768]{3,2,1,0:T(8,128)(2,1)S(1)} %copy-done.2, bf16[8,2,128,256]{3,2,1,0:T(8,128)(2,1)S(1)} %copy-done.10, f32[1024,128]{1,0:T(8,128)S(1)} %copy-done.9, f32[1024,128]{1,0:T(8,128)S(1)} %copy-done.7, s32[2,1,1024]{2,1,0:T(1,128)S(1)} %bitcast.193, ...), custom_call_target="tpu_custom_call" | custom-call | flops 1 | bytes 1 | tf_op jit(solution)/shard_map/attend_back/pallas_call | solution.py:298
  726.0 13.2 %part_grads.1 = (bf16[256,2048]{1,0:T(8,128)(2,1)}, bf16[256,2048]{1,0:T(8,128)(2,1)}, bf16[256,2048]{1,0:T(8,128)(2,1)}, bf16[256,2048]{1,0:T(8,128)(2,1)}, bf1...) custom-call(bf16[2048,768]{1,0:T(8,128)(2,1)} %bitcast.190, ...), custom_call_target="tpu_custom_call" | custom-call | flops 1 | bytes 1 | tf_op jit(solution)/shard_map/part_grads/pallas_call | solution.py:427
  740.5 2.6 fusion.12
  750.5 20.8 %proj_grads.1 = (bf16[512,1152]{1,0:T(8,128)(2,1)}, bf16[512,1152]{1,0:T(8,128)(2,1)}, bf16[512,1152]{1,0:T(8,128)(2,1)}, bf16[512,1152]{1,0:T(8,128)(2,1)}) custom-call(s32[4]{0:T(128)} %fusion.41.refs_0_, s32[8]{0:T(128)} %copy-done.82, bf16[2048,2048]{1,0:T(8,128)(2,1)} %bitcast.200, bf16[2048,768]{1,0:T(8,128)(2,1)} %bitcast.191, ...), custom_call_target="tpu_custom_call" | custom-call | flops 1 | bytes 1 | tf_op jit(solution)/shard_map/proj_grads/pallas_call | solution.py:388
  779.0 2.9 add_convert_fusion.6
  786.3 24.2 %bank_grad.5.refs_1_.refs_0_ = bf16[4,2048,1024]{2,1,0:T(8,128)(2,1)} custom-call(bf16[4,2,384,2048]{3,2,1,0:T(8,128)(2,1)} %get-tuple-element.53.refs_1_.refs_0_, bf16[4,2,384,1024]{3,2,1,0:T(8,128)(2,1)} %get-tuple-element.58.refs_1_, bf16[2,128,2048]{2,1,0:T(8,128)(2,1)} %after.115.refs_1_.refs_2_.refs_4_), custom_call_target="tpu_custom_call" | custom-call | flops 1 | bytes 1 | tf_op jit(solution)/shard_map/bank_grad/pallas_call | solution.py:427
  810.5 21.9 %collective-permute-done.47.refs_2_.refs_0_ = bf16[512,1152]{1,0:T(8,128)(2,1)} collective-permute-done((bf16[512,1152]{1,0:T(8,128)(2,1)}, bf16[512,1152]{1,0:T(8,128)(2,1)}, u32[]{:S(2)}, u32[]{:S(2)}) %collective-permute-start.47) | collective-permute-done | bytes 1179680 | tf_op jit(solution)/shard_map/ppermute | solution.py:31
  833.7 3.1 add_convert_fusion.refs_5_.refs_0_
  838.2 4.4 all-to-all-start.3
  844.7 3.1 add_convert_fusion.5
  849.8 6.7 convert_element_type.430.refs_1_
  856.5 22.9 %collective-permute-done.53.refs_2_.refs_0_ = bf16[2,128,2048]{2,1,0:T(8,128)(2,1)S(1)} collective-permute-done((bf16[2,128,2048]{2,1,0:T(8,128)(2,1)}, bf16[2,128,2048]{2,1,0:T(8,128)(2,1)S(1)}, u32[]{:S(2)}, u32[]{:S(2)}) %collective-permute-start.53) | collective-permute-done | bytes 1048608 | tf_op jit(solution)/shard_map/ppermute | solution.py:31
  879.5 8.2 collective-permute-done.52.refs_0_
  887.7 5.5 all-to-all-done.3.refs_4_.refs_0_
  895.8 2.7 add_convert_fusion.3
  900.6 3.6 add_convert_fusion.4
  909.1 3.7 reshape.571
  915.7 5.6 fusion.63
  929.5 6.6 convert_element_type.438.refs_1_
  936.2 7.0 collective-permute-done.58.refs_3_.refs_0_
  958.4 2.9 fusion.19
  961.9 22.8 %reduce-scatter.8.cloned.1.call-done = bf16[4,512,1024]{2,1,0:T(8,128)(2,1)} async-done(((bf16[4,2048,1024]{2,1,0:T(8,128)(2,1)}), bf16[4,512,1024]{2,1,0:T(8,128)(2,1)}) %reduce-scatter.8.cloned.1.call-update) | async-done | bytes 4194320 | tf_op jit(solution)/shard_map/reduce_scatter | solution.py:788
  984.7 6.8 convert_element_type.467
  (480 shorter events, 182.4 us)
Async XLA Ops:
  7.2 117.1 %all-gather.6.cloned.1.call-start = ((), (), s32[]{:S(2)}) async-start(), calls=%async_computation.7 | async-start | bytes 4587520 | tf_op jit(solution)/shard_map/all_gather | solution.py:646
  11.1 190.3 %all-gather.8.cloned.1.call-start = ((), (), s32[]{:S(2)}) async-start(), calls=%async_computation.8 | async-start | bytes 10485760 | tf_op jit(solution)/shard_map/all_gather | solution.py:646
  11.8 337.2 %all-gather.12.cloned.1.call-start = ((), (), s32[]{:S(2)}) async-start(), calls=%async_computation.10 | async-start | bytes 20971520 | tf_op jit(solution)/shard_map/all_gather | solution.py:646
  12.5 371.1 %all-gather.10.cloned.1.call-start = ((), (), s32[]{:S(2)}) async-start(), calls=%async_computation.9 | async-start | bytes 20971520 | tf_op jit(solution)/shard_map/all_gather | solution.py:646
  13.2 445.5 %all-gather.14.cloned.1.call-start = ((), (), s32[]{:S(2)}) async-start(), calls=%async_computation.11 | async-start | bytes 20971520 | tf_op jit(solution)/shard_map/all_gather | solution.py:646
  13.7 836.1 %reduce-scatter.4.cloned.1.call-start = ((), (), s32[]{:S(2)}) async-start(), calls=%async_computation.12 | async-start | bytes 20971520 | tf_op jit(solution)/shard_map/reduce_scatter | solution.py:788
  17.0 29.8 %collective-permute-start.1 = (bf16[2,128,2176]{2,1,0:T(8,128)(2,1)}, bf16[2,128,2176]{2,1,0:T(8,128)(2,1)S(1)}, u32[]{:S(2)}, u32[]{:S(2)}) collective-permute-start(bf16[2,128,2176]{2,1,0:T(8,128)(2,1)} %get-tuple-element.107), channel_id=1, source_target_pairs={{0,2},{1,3},{2,4},{3,5},{4,6},{5,7},{6,0},{7,1},{8,10},{9,11},{10,... | collective-permute-start | bytes 3342344 | tf_op jit(solution)/shard_map/ppermute | solution.py:31
  20.0 29.3 %collective-permute-start = (bf16[2,128,2176]{2,1,0:T(8,128)(2,1)}, bf16[2,128,2176]{2,1,0:T(8,128)(2,1)}, u32[]{:S(2)}, u32[]{:S(2)}) collective-permute-start(bf16[2,128,2176]{2,1,0:T(8,128)(2,1)} %get-tuple-element.107), channel_id=1, source_target_pairs={{0,1},{1,0},{2,3},{3,2},{4,5},{5,4},{6,7},{7,6},{8,9},{9,8},{10,11... | collective-permute-start | bytes 3342344 | tf_op jit(solution)/shard_map/ppermute | solution.py:31
  46.8 27.5 %collective-permute-start.3 = (bf16[2,128,2176]{2,1,0:T(8,128)(2,1)S(1)}, bf16[2,128,2176]{2,1,0:T(8,128)(2,1)S(1)}, u32[]{:S(2)}, u32[]{:S(2)}) collective-permute-start(bf16[2,128,2176]{2,1,0:T(8,128)(2,1)S(1)} %collective-permute-done.1), channel_id=1, source_target_pairs={{0,2},{1,3},{2,4},{3,5},{4,6},{5,7},{6,0},{7,1},{8,10},{9,11},{10,... | collective-permute-start | bytes 3342344 | tf_op jit(solution)/shard_map/ppermute | solution.py:31
  46.8 29.9 %collective-permute-start.2 = (bf16[2,128,2176]{2,1,0:T(8,128)(2,1)S(1)}, bf16[2,128,2176]{2,1,0:T(8,128)(2,1)}, u32[]{:S(2)}, u32[]{:S(2)}) collective-permute-start(bf16[2,128,2176]{2,1,0:T(8,128)(2,1)S(1)} %collective-permute-done.1), channel_id=1, source_target_pairs={{0,1},{1,0},{2,3},{3,2},{4,5},{5,4},{6,7},{7,6},{8,9},{9,8},{10,11... | collective-permute-start | bytes 3342344 | tf_op jit(solution)/shard_map/ppermute | solution.py:31
  74.3 28.5 %collective-permute-start.4 = (bf16[2,128,2176]{2,1,0:T(8,128)(2,1)S(1)}, bf16[2,128,2176]{2,1,0:T(8,128)(2,1)S(1)}, u32[]{:S(2)}, u32[]{:S(2)}) collective-permute-start(bf16[2,128,2176]{2,1,0:T(8,128)(2,1)S(1)} %collective-permute-done.3), channel_id=1, source_target_pairs={{0,1},{1,0},{2,3},{3,2},{4,5},{5,4},{6,7},{7,6},{8,9},{9,8},{10,11... | collective-permute-start | bytes 3342344 | tf_op jit(solution)/shard_map/ppermute | solution.py:31
  75.6 26.1 %collective-permute-start.5 = (bf16[2,128,2176]{2,1,0:T(8,128)(2,1)S(1)}, bf16[2,128,2176]{2,1,0:T(8,128)(2,1)S(1)}, u32[]{:S(2)}, u32[]{:S(2)}) collective-permute-start(bf16[2,128,2176]{2,1,0:T(8,128)(2,1)S(1)} %collective-permute-done.3), channel_id=1, source_target_pairs={{0,2},{1,3},{2,4},{3,5},{4,6},{5,7},{6,0},{7,1},{8,10},{9,11},{10,... | collective-permute-start | bytes 3342344 | tf_op jit(solution)/shard_map/ppermute | solution.py:31
  102.9 13.3 %collective-permute-start.7 = (bf16[1,128,2176]{2,1,0:T(8,128)(2,1)S(1)}, bf16[1,128,2176]{2,1,0:T(8,128)(2,1)S(1)}, u32[]{:S(2)}, u32[]{:S(2)}) collective-permute-start(bf16[1,128,2176]{2,1,0:T(8,128)(2,1)S(1)} %slice.103), channel_id=1, source_target_pairs={{0,2},{1,3},{2,4},{3,5},{4,6},{5,7},{6,0},{7,1},{8,10},{9,11},{10,... | collective-permute-start | bytes 1671176 | tf_op jit(solution)/shard_map/ppermute | solution.py:31
  117.0 23.0 %collective-permute-start.8 = (bf16[2,128,2048]{2,1,0:T(8,128)(2,1)}, bf16[2,128,2048]{2,1,0:T(8,128)(2,1)S(1)}, u32[]{:S(2)}, u32[]{:S(2)}) collective-permute-start(bf16[2,128,2048]{2,1,0:T(8,128)(2,1)} %after.71), channel_id=1, source_target_pairs={{0,2},{1,3},{2,4},{3,5},{4,6},{5,7},{6,0},{7,1},{8,10},{9,11},{10,... | collective-permute-start | bytes 3145736 | tf_op jit(solution)/shard_map/ppermute | solution.py:31
  117.0 23.0 %collective-permute-start.9 = (bf16[2,128,2048]{2,1,0:T(8,128)(2,1)}, bf16[2,128,2048]{2,1,0:T(8,128)(2,1)S(1)}, u32[]{:S(2)}, u32[]{:S(2)}) collective-permute-start(bf16[2,128,2048]{2,1,0:T(8,128)(2,1)} %after.71), channel_id=1, source_target_pairs={{0,1},{1,0},{2,3},{3,2},{4,5},{5,4},{6,7},{7,6},{8,9},{9,8},{10,11... | collective-permute-start | bytes 3145736 | tf_op jit(solution)/shard_map/ppermute | solution.py:31
  142.1 29.7 %collective-permute-start.10 = (bf16[2,128,2048]{2,1,0:T(8,128)(2,1)}, bf16[2,128,2048]{2,1,0:T(8,128)(2,1)}, u32[]{:S(2)}, u32[]{:S(2)}) collective-permute-start(bf16[2,128,2048]{2,1,0:T(8,128)(2,1)} %after.73), channel_id=1, source_target_pairs={{0,2},{1,3},{2,4},{3,5},{4,6},{5,7},{6,0},{7,1},{8,10},{9,11},{10,... | collective-permute-start | bytes 3145736 | tf_op jit(solution)/shard_map/ppermute | solution.py:31
  142.3 29.5 %collective-permute-start.11 = (bf16[2,128,2048]{2,1,0:T(8,128)(2,1)}, bf16[2,128,2048]{2,1,0:T(8,128)(2,1)}, u32[]{:S(2)}, u32[]{:S(2)}) collective-permute-start(bf16[2,128,2048]{2,1,0:T(8,128)(2,1)} %after.73), channel_id=1, source_target_pairs={{0,1},{1,0},{2,3},{3,2},{4,5},{5,4},{6,7},{7,6},{8,9},{9,8},{10,11... | collective-permute-start | bytes 3145736 | tf_op jit(solution)/shard_map/ppermute | solution.py:31
  209.3 22.7 %collective-permute-start.12 = (bf16[2,128,2048]{2,1,0:T(8,128)(2,1)S(1)}, bf16[2,128,2048]{2,1,0:T(8,128)(2,1)}, u32[]{:S(2)}, u32[]{:S(2)}) collective-permute-start(bf16[2,128,2048]{2,1,0:T(8,128)(2,1)S(1)} %bitcast.211), channel_id=1, source_target_pairs={{0,1},{1,0},{2,3},{3,2},{4,5},{5,4},{6,7},{7,6},{8,9},{9,8},{10,11... | collective-permute-start | bytes 3145736 | tf_op jit(solution)/shard_map/ppermute | solution.py:31
  210.9 24.4 %collective-permute-start.13 = (bf16[2,128,2048]{2,1,0:T(8,128)(2,1)S(1)}, bf16[2,128,2048]{2,1,0:T(8,128)(2,1)}, u32[]{:S(2)}, u32[]{:S(2)}) collective-permute-start(bf16[2,128,2048]{2,1,0:T(8,128)(2,1)S(1)} %bitcast.212), channel_id=1, source_target_pairs={{0,2},{1,3},{2,4},{3,5},{4,6},{5,7},{6,0},{7,1},{8,10},{9,11},{10,... | collective-permute-start | bytes 3145736 | tf_op jit(solution)/shard_map/ppermute | solution.py:31
  235.2 21.8 %collective-permute-start.14 = (bf16[2,128,2048]{2,1,0:T(8,128)(2,1)}, bf16[2,128,2048]{2,1,0:T(8,128)(2,1)}, u32[]{:S(2)}, u32[]{:S(2)}) collective-permute-start(bf16[2,128,2048]{2,1,0:T(8,128)(2,1)} %after.78), channel_id=1, source_target_pairs={{0,1},{1,0},{2,3},{3,2},{4,5},{5,4},{6,7},{7,6},{8,9},{9,8},{10,11... | collective-permute-start | bytes 3145736 | tf_op jit(solution)/shard_map/ppermute | solution.py:31
  236.4 23.6 %collective-permute-start.15 = (bf16[2,128,2048]{2,1,0:T(8,128)(2,1)}, bf16[2,128,2048]{2,1,0:T(8,128)(2,1)}, u32[]{:S(2)}, u32[]{:S(2)}) collective-permute-start(bf16[2,128,2048]{2,1,0:T(8,128)(2,1)} %after.78), channel_id=1, source_target_pairs={{0,2},{1,3},{2,4},{3,5},{4,6},{5,7},{6,0},{7,1},{8,10},{9,11},{10,... | collective-permute-start | bytes 3145736 | tf_op jit(solution)/shard_map/ppermute | solution.py:31
  260.1 20.9 %collective-permute-start.16 = (bf16[2,128,2048]{2,1,0:T(8,128)(2,1)}, bf16[2,128,2048]{2,1,0:T(8,128)(2,1)}, u32[]{:S(2)}, u32[]{:S(2)}) collective-permute-start(bf16[2,128,2048]{2,1,0:T(8,128)(2,1)} %after.80), channel_id=1, source_target_pairs={{0,1},{1,0},{2,3},{3,2},{4,5},{5,4},{6,7},{7,6},{8,9},{9,8},{10,11... | collective-permute-start | bytes 3145736 | tf_op jit(solution)/shard_map/ppermute | solution.py:31
  260.6 22.2 %collective-permute-start.17 = (bf16[2,128,2048]{2,1,0:T(8,128)(2,1)}, bf16[2,128,2048]{2,1,0:T(8,128)(2,1)}, u32[]{:S(2)}, u32[]{:S(2)}) collective-permute-start(bf16[2,128,2048]{2,1,0:T(8,128)(2,1)} %after.80), channel_id=1, source_target_pairs={{0,2},{1,3},{2,4},{3,5},{4,6},{5,7},{6,0},{7,1},{8,10},{9,11},{10,... | collective-permute-start | bytes 3145736 | tf_op jit(solution)/shard_map/ppermute | solution.py:31
  286.8 13.3 %collective-permute-start.19 = (bf16[1,128,2048]{2,1,0:T(8,128)(2,1)S(1)}, bf16[1,128,2048]{2,1,0:T(8,128)(2,1)}, u32[]{:S(2)}, u32[]{:S(2)}) collective-permute-start(bf16[1,128,2048]{2,1,0:T(8,128)(2,1)S(1)} %slice.109), channel_id=1, source_target_pairs={{0,2},{1,3},{2,4},{3,5},{4,6},{5,7},{6,0},{7,1},{8,10},{9,11},{10,... | collective-permute-start | bytes 1572872 | tf_op jit(solution)/shard_map/ppermute | solution.py:31
  300.1 16.7 %collective-permute-start.20 = (bf16[2,128,2048]{2,1,0:T(8,128)(2,1)}, bf16[2,128,2048]{2,1,0:T(8,128)(2,1)}, u32[]{:S(2)}, u32[]{:S(2)}) collective-permute-start(bf16[2,128,2048]{2,1,0:T(8,128)(2,1)} %after.85), channel_id=1, source_target_pairs={{0,1},{1,0},{2,3},{3,2},{4,5},{5,4},{6,7},{7,6},{8,9},{9,8},{10,11... | collective-permute-start | bytes 3145736 | tf_op jit(solution)/shard_map/ppermute | solution.py:31
  300.1 20.2 %collective-permute-start.21 = (bf16[2,128,2048]{2,1,0:T(8,128)(2,1)}, bf16[2,128,2048]{2,1,0:T(8,128)(2,1)}, u32[]{:S(2)}, u32[]{:S(2)}) collective-permute-start(bf16[2,128,2048]{2,1,0:T(8,128)(2,1)} %after.85), channel_id=1, source_target_pairs={{0,2},{1,3},{2,4},{3,5},{4,6},{5,7},{6,0},{7,1},{8,10},{9,11},{10,... | collective-permute-start | bytes 3145736 | tf_op jit(solution)/shard_map/ppermute | solution.py:31
  324.1 13.2 %collective-permute-start.22 = (bf16[1,128,2048]{2,1,0:T(8,128)(2,1)}, bf16[1,128,2048]{2,1,0:T(8,128)(2,1)}, u32[]{:S(2)}, u32[]{:S(2)}) collective-permute-start(bf16[1,128,2048]{2,1,0:T(8,128)(2,1)} %slice.114), channel_id=1, source_target_pairs={{0,1},{1,0},{2,3},{3,2},{4,5},{5,4},{6,7},{7,6},{8,9},{9,8},{10,11... | collective-permute-start | bytes 1572872 | tf_op jit(solution)/shard_map/ppermute | solution.py:31
  324.4 15.3 %collective-permute-start.23 = (bf16[1,128,2048]{2,1,0:T(8,128)(2,1)}, bf16[1,128,2048]{2,1,0:T(8,128)(2,1)}, u32[]{:S(2)}, u32[]{:S(2)}) collective-permute-start(bf16[1,128,2048]{2,1,0:T(8,128)(2,1)} %slice.115), channel_id=1, source_target_pairs={{0,2},{1,3},{2,4},{3,5},{4,6},{5,7},{6,0},{7,1},{8,10},{9,11},{10,... | collective-permute-start | bytes 1572872 | tf_op jit(solution)/shard_map/ppermute | solution.py:31
  339.8 43.4 %collective-permute-start.24 = (bf16[2048,256]{1,0:T(8,128)(2,1)}, bf16[2048,256]{1,0:T(8,128)(2,1)}, u32[]{:S(2)}, u32[]{:S(2)}) collective-permute-start(bf16[2048,256]{1,0:T(8,128)(2,1)} %after.90.refs_6_), channel_id=1, source_target_pairs={{0,2},{1,3},{2,4},{3,5},{4,6},{5,7},{6,0},{7,1},{8,10},{9,11},{10,... | collective-permute-start | bytes 3145736 | tf_op jit(solution)/shard_map/ppermute | solution.py:31
  340.2 42.9 %collective-permute-start.25 = (bf16[2048,256]{1,0:T(8,128)(2,1)}, bf16[2048,256]{1,0:T(8,128)(2,1)}, u32[]{:S(2)}, u32[]{:S(2)}) collective-permute-start(bf16[2048,256]{1,0:T(8,128)(2,1)} %after.90.refs_6_), channel_id=1, source_target_pairs={{0,1},{1,0},{2,3},{3,2},{4,5},{5,4},{6,7},{7,6},{8,9},{9,8},{10,11... | collective-permute-start | bytes 3145736 | tf_op jit(solution)/shard_map/ppermute | solution.py:31
  383.2 33.5 %collective-permute-start.26 = (bf16[2048,256]{1,0:T(8,128)(2,1)}, bf16[2048,256]{1,0:T(8,128)(2,1)}, u32[]{:S(2)}, u32[]{:S(2)}) collective-permute-start(bf16[2048,256]{1,0:T(8,128)(2,1)} %after.92.refs_8_), channel_id=1, source_target_pairs={{0,2},{1,3},{2,4},{3,5},{4,6},{5,7},{6,0},{7,1},{8,10},{9,11},{10,... | collective-permute-start | bytes 3145736 | tf_op jit(solution)/shard_map/ppermute | solution.py:31
  383.2 33.4 %collective-permute-start.27 = (bf16[2048,256]{1,0:T(8,128)(2,1)}, bf16[2048,256]{1,0:T(8,128)(2,1)}, u32[]{:S(2)}, u32[]{:S(2)}) collective-permute-start(bf16[2048,256]{1,0:T(8,128)(2,1)} %after.92.refs_8_), channel_id=1, source_target_pairs={{0,1},{1,0},{2,3},{3,2},{4,5},{5,4},{6,7},{7,6},{8,9},{9,8},{10,11... | collective-permute-start | bytes 3145736 | tf_op jit(solution)/shard_map/ppermute | solution.py:31
  416.7 21.1 %collective-permute-start.28 = (bf16[2048,256]{1,0:T(8,128)(2,1)}, bf16[2048,256]{1,0:T(8,128)(2,1)}, u32[]{:S(2)}, u32[]{:S(2)}) collective-permute-start(bf16[2048,256]{1,0:T(8,128)(2,1)} %after.94.refs_10_), channel_id=1, source_target_pairs={{0,2},{1,3},{2,4},{3,5},{4,6},{5,7},{6,0},{7,1},{8,10},{9,11},{10,... | collective-permute-start | bytes 3145736 | tf_op jit(solution)/shard_map/ppermute | solution.py:31
  417.5 20.7 %collective-permute-start.29 = (bf16[2048,256]{1,0:T(8,128)(2,1)}, bf16[2048,256]{1,0:T(8,128)(2,1)}, u32[]{:S(2)}, u32[]{:S(2)}) collective-permute-start(bf16[2048,256]{1,0:T(8,128)(2,1)} %after.94.refs_10_), channel_id=1, source_target_pairs={{0,1},{1,0},{2,3},{3,2},{4,5},{5,4},{6,7},{7,6},{8,9},{9,8},{10,11... | collective-permute-start | bytes 3145736 | tf_op jit(solution)/shard_map/ppermute | solution.py:31
  518.6 30.0 %collective-permute-start.33 = (bf16[2,128,2048]{2,1,0:T(8,128)(2,1)}, bf16[2,128,2048]{2,1,0:T(8,128)(2,1)}, u32[]{:S(2)}, u32[]{:S(2)}) collective-permute-start(bf16[2,128,2048]{2,1,0:T(8,128)(2,1)} %bitcast.264), channel_id=1, source_target_pairs={{0,1},{1,0},{2,3},{3,2},{4,5},{5,4},{6,7},{7,6},{8,9},{9,8},{10,11... | collective-permute-start | bytes 3145736 | tf_op jit(solution)/shard_map/ppermute | solution.py:31
  546.6 29.9 %collective-permute-start.32 = (bf16[2,128,2048]{2,1,0:T(8,128)(2,1)}, bf16[2,128,2048]{2,1,0:T(8,128)(2,1)}, u32[]{:S(2)}, u32[]{:S(2)}) collective-permute-start(bf16[2,128,2048]{2,1,0:T(8,128)(2,1)} %bitcast.263), channel_id=1, source_target_pairs={{0,1},{1,0},{2,3},{3,2},{4,5},{5,4},{6,7},{7,6},{8,9},{9,8},{10,11... | collective-permute-start | bytes 3145736 | tf_op jit(solution)/shard_map/ppermute | solution.py:31
  550.5 26.0 %collective-permute-start.34 = (bf16[2,128,2048]{2,1,0:T(8,128)(2,1)S(1)}, bf16[2,128,2048]{2,1,0:T(8,128)(2,1)}, u32[]{:S(2)}, u32[]{:S(2)}) collective-permute-start(bf16[2,128,2048]{2,1,0:T(8,128)(2,1)S(1)} %fusion.16), channel_id=1, source_target_pairs={{0,2},{1,3},{2,4},{3,5},{4,6},{5,7},{6,0},{7,1},{8,10},{9,11},{10,... | collective-permute-start | bytes 3145736 | tf_op jit(solution)/shard_map/ppermute | solution.py:31
  576.6 24.2 %collective-permute-start.36 = (bf16[2,128,2048]{2,1,0:T(8,128)(2,1)}, bf16[2,128,2048]{2,1,0:T(8,128)(2,1)}, u32[]{:S(2)}, u32[]{:S(2)}) collective-permute-start(bf16[2,128,2048]{2,1,0:T(8,128)(2,1)} %bitcast.262), channel_id=1, source_target_pairs={{0,1},{1,0},{2,3},{3,2},{4,5},{5,4},{6,7},{7,6},{8,9},{9,8},{10,11... | collective-permute-start | bytes 3145736 | tf_op jit(solution)/shard_map/ppermute | solution.py:31
  579.4 21.4 %collective-permute-start.37 = (bf16[2,128,2048]{2,1,0:T(8,128)(2,1)S(1)}, bf16[2,128,2048]{2,1,0:T(8,128)(2,1)}, u32[]{:S(2)}, u32[]{:S(2)}) collective-permute-start(bf16[2,128,2048]{2,1,0:T(8,128)(2,1)S(1)} %add_convert_fusion.8), channel_id=1, source_target_pairs={{0,2},{1,3},{2,4},{3,5},{4,6},{5,7},{6,0},{7,1},{8,10},{9,11},{10,... | collective-permute-start | bytes 3145736 | tf_op jit(solution)/shard_map/ppermute | solution.py:31
  600.8 25.3 %collective-permute-start.35 = (bf16[2,128,2048]{2,1,0:T(8,128)(2,1)}, bf16[2,128,2048]{2,1,0:T(8,128)(2,1)}, u32[]{:S(2)}, u32[]{:S(2)}) collective-permute-start(bf16[2,128,2048]{2,1,0:T(8,128)(2,1)} %bitcast.261), channel_id=1, source_target_pairs={{0,1},{1,0},{2,3},{3,2},{4,5},{5,4},{6,7},{7,6},{8,9},{9,8},{10,11... | collective-permute-start | bytes 3145736 | tf_op jit(solution)/shard_map/ppermute | solution.py:31
  605.0 21.1 %collective-permute-start.38 = (bf16[2,128,2048]{2,1,0:T(8,128)(2,1)S(1)}, bf16[2,128,2048]{2,1,0:T(8,128)(2,1)}, u32[]{:S(2)}, u32[]{:S(2)}) collective-permute-start(bf16[2,128,2048]{2,1,0:T(8,128)(2,1)S(1)} %add_convert_fusion.7), channel_id=1, source_target_pairs={{0,2},{1,3},{2,4},{3,5},{4,6},{5,7},{6,0},{7,1},{8,10},{9,11},{10,... | collective-permute-start | bytes 3145736 | tf_op jit(solution)/shard_map/ppermute | solution.py:31
  639.3 30.9 %all-to-all-start.1 = ((bf16[8,2,128,256]{3,2,1,0:T(8,128)(2,1)}), bf16[8,2,128,256]{3,2,1,0:T(8,128)(2,1)}, u32[]{:S(2)}, u32[]{:S(2)}) async-start(bf16[8,2,128,256]{3,2,1,0:T(8,128)(2,1)} %bitcast.216), calls=%async_computation.1 | async-start | bytes 2097152 | tf_op jit(solution)/shard_map/all_to_all | solution.py:802
  645.3 284.2 %reduce-scatter.6.cloned.1.call-start = ((), (), s32[]{:S(2)}) async-start(), calls=%async_computation.13 | async-start | bytes 20971520 | tf_op jit(solution)/shard_map/reduce_scatter | solution.py:788
  673.0 66.3 %all-to-all-start.2 = ((bf16[8,2,128,256]{3,2,1,0:T(8,128)(2,1)}), bf16[8,2,128,256]{3,2,1,0:T(8,128)(2,1)}, u32[]{:S(2)}, u32[]{:S(2)}) async-start(bf16[8,2,128,256]{3,2,1,0:T(8,128)(2,1)} %bitcast.215), calls=%async_computation.2 | async-start | bytes 2097152 | tf_op jit(solution)/shard_map/all_to_all | solution.py:802
  678.6 306.0 %reduce-scatter.8.cloned.1.call-start = ((), (), s32[]{:S(2)}) async-start(), calls=%async_computation.14 | async-start | bytes 20971520 | tf_op jit(solution)/shard_map/reduce_scatter | solution.py:788
  678.7 60.6 %collective-permute-start.39 = (bf16[2,128,2048]{2,1,0:T(8,128)(2,1)}, bf16[2,128,2048]{2,1,0:T(8,128)(2,1)}, u32[]{:S(2)}, u32[]{:S(2)}) collective-permute-start(bf16[2,128,2048]{2,1,0:T(8,128)(2,1)} %after.108), channel_id=1, source_target_pairs={{0,1},{1,0},{2,3},{3,2},{4,5},{5,4},{6,7},{7,6},{8,9},{9,8},{10,11... | collective-permute-start | bytes 3145736 | tf_op jit(solution)/shard_map/ppermute | solution.py:31
  685.0 86.3 %collective-permute-start.42 = (bf16[2,128,2048]{2,1,0:T(8,128)(2,1)}, bf16[2,128,2048]{2,1,0:T(8,128)(2,1)}, u32[]{:S(2)}, u32[]{:S(2)}) collective-permute-start(bf16[2,128,2048]{2,1,0:T(8,128)(2,1)} %bitcast.259), channel_id=1, source_target_pairs={{0,1},{1,0},{2,3},{3,2},{4,5},{5,4},{6,7},{7,6},{8,9},{9,8},{10,11... | collective-permute-start | bytes 3145736 | tf_op jit(solution)/shard_map/ppermute | solution.py:31
  743.1 28.3 %collective-permute-start.41 = (bf16[2,128,2048]{2,1,0:T(8,128)(2,1)}, bf16[2,128,2048]{2,1,0:T(8,128)(2,1)S(1)}, u32[]{:S(2)}, u32[]{:S(2)}) collective-permute-start(bf16[2,128,2048]{2,1,0:T(8,128)(2,1)} %fusion.12), channel_id=1, source_target_pairs={{0,2},{1,3},{2,4},{3,5},{4,6},{5,7},{6,0},{7,1},{8,10},{9,11},{10,... | collective-permute-start | bytes 3145736 | tf_op jit(solution)/shard_map/ppermute | solution.py:31
  744.6 26.8 %collective-permute-start.40 = (bf16[2,128,2048]{2,1,0:T(8,128)(2,1)}, bf16[2,128,2048]{2,1,0:T(8,128)(2,1)S(1)}, u32[]{:S(2)}, u32[]{:S(2)}) collective-permute-start(bf16[2,128,2048]{2,1,0:T(8,128)(2,1)} %after.111), channel_id=1, source_target_pairs={{0,1},{1,0},{2,3},{3,2},{4,5},{5,4},{6,7},{7,6},{8,9},{9,8},{10,11... | collective-permute-start | bytes 3145736 | tf_op jit(solution)/shard_map/ppermute | solution.py:31
  747.9 23.4 %collective-permute-start.44 = (f32[2,128]{1,0:T(2,128)S(1)}, f32[2,128]{1,0:T(2,128)S(1)}, u32[]{:S(2)}, u32[]{:S(2)}) collective-permute-start(f32[2,128]{1,0:T(2,128)S(1)} %add.371), channel_id=1, source_target_pairs={{0,16},{8,24},{16,0},{24,8},{1,17},{9,25},{17,1},{25,9},{2,18},{10... | collective-permute-start | bytes 3080 | tf_op jit(solution)/shard_map/ppermute | solution.py:839
  772.7 64.1 %collective-permute-start.50 = (bf16[2,128,2048]{2,1,0:T(8,128)(2,1)}, bf16[2,128,2048]{2,1,0:T(8,128)(2,1)S(1)}, u32[]{:S(2)}, u32[]{:S(2)}) collective-permute-start(bf16[2,128,2048]{2,1,0:T(8,128)(2,1)} %bitcast.72), channel_id=1, source_target_pairs={{0,1},{1,0},{2,3},{3,2},{4,5},{5,4},{6,7},{7,6},{8,9},{9,8},{10,11... | collective-permute-start | bytes 3145736 | tf_op jit(solution)/shard_map/ppermute | solution.py:31
  773.4 63.4 %collective-permute-start.51 = (bf16[2,128,2048]{2,1,0:T(8,128)(2,1)}, bf16[2,128,2048]{2,1,0:T(8,128)(2,1)S(1)}, u32[]{:S(2)}, u32[]{:S(2)}) collective-permute-start(bf16[2,128,2048]{2,1,0:T(8,128)(2,1)} %bitcast.260), channel_id=1, source_target_pairs={{0,1},{1,0},{2,3},{3,2},{4,5},{5,4},{6,7},{7,6},{8,9},{9,8},{10,11... | collective-permute-start | bytes 3145736 | tf_op jit(solution)/shard_map/ppermute | solution.py:31
  778.3 54.1 %collective-permute-start.47 = (bf16[512,1152]{1,0:T(8,128)(2,1)}, bf16[512,1152]{1,0:T(8,128)(2,1)}, u32[]{:S(2)}, u32[]{:S(2)}) collective-permute-start(bf16[512,1152]{1,0:T(8,128)(2,1)} %add_convert_fusion.2), channel_id=1, source_target_pairs={{0,16},{8,24},{16,0},{24,8},{1,17},{9,25},{17,1},{25,9},{2,18},{10... | collective-permute-start | bytes 3538952 | tf_op jit(solution)/shard_map/ppermute | solution.py:31
  781.9 55.0 %collective-permute-start.48 = (bf16[2,128,2048]{2,1,0:T(8,128)(2,1)}, bf16[2,128,2048]{2,1,0:T(8,128)(2,1)}, u32[]{:S(2)}, u32[]{:S(2)}) collective-permute-start(bf16[2,128,2048]{2,1,0:T(8,128)(2,1)} %add_convert_fusion.6), channel_id=1, source_target_pairs={{0,2},{1,3},{2,4},{3,5},{4,6},{5,7},{6,0},{7,1},{8,10},{9,11},{10,... | collective-permute-start | bytes 3145736 | tf_op jit(solution)/shard_map/ppermute | solution.py:31
  784.8 52.0 %collective-permute-start.49 = (bf16[2,128,2048]{2,1,0:T(8,128)(2,1)}, bf16[2,128,2048]{2,1,0:T(8,128)(2,1)}, u32[]{:S(2)}, u32[]{:S(2)}) collective-permute-start(bf16[2,128,2048]{2,1,0:T(8,128)(2,1)} %fusion.10), channel_id=1, source_target_pairs={{0,2},{1,3},{2,4},{3,5},{4,6},{5,7},{6,0},{7,1},{8,10},{9,11},{10,... | collective-permute-start | bytes 3145736 | tf_op jit(solution)/shard_map/ppermute | solution.py:31
  838.2 55.0 %all-to-all-start.3 = ((bf16[8,64,1152]{2,1,0:T(8,128)(2,1)}), bf16[8,64,1152]{2,1,0:T(8,128)(2,1)S(1)}, u32[]{:S(2)}, u32[]{:S(2)}) async-start(bf16[8,64,1152]{2,1,0:T(8,128)(2,1)} %bitcast.74), calls=%async_computation.3 | async-start | bytes 2359296 | tf_op jit(solution)/shard_map/all_to_all | solution.py:867
  842.6 36.9 %collective-permute-start.53 = (bf16[2,128,2048]{2,1,0:T(8,128)(2,1)}, bf16[2,128,2048]{2,1,0:T(8,128)(2,1)S(1)}, u32[]{:S(2)}, u32[]{:S(2)}) collective-permute-start(bf16[2,128,2048]{2,1,0:T(8,128)(2,1)} %bitcast.258), channel_id=1, source_target_pairs={{0,1},{1,0},{2,3},{3,2},{4,5},{5,4},{6,7},{7,6},{8,9},{9,8},{10,11... | collective-permute-start | bytes 3145736 | tf_op jit(solution)/shard_map/ppermute | solution.py:31
  847.7 40.0 %collective-permute-start.52 = (bf16[2,128,2048]{2,1,0:T(8,128)(2,1)}, bf16[2,128,2048]{2,1,0:T(8,128)(2,1)S(1)}, u32[]{:S(2)}, u32[]{:S(2)}) collective-permute-start(bf16[2,128,2048]{2,1,0:T(8,128)(2,1)} %add_convert_fusion.5), channel_id=1, source_target_pairs={{0,2},{1,3},{2,4},{3,5},{4,6},{5,7},{6,0},{7,1},{8,10},{9,11},{10,... | collective-permute-start | bytes 3145736 | tf_op jit(solution)/shard_map/ppermute | solution.py:31
  849.2 30.3 %collective-permute-start.54 = (f32[2,128]{1,0:T(2,128)S(1)}, f32[2,128]{1,0:T(2,128)S(1)}, u32[]{:S(2)}, u32[]{:S(2)}) collective-permute-start(f32[2,128]{1,0:T(2,128)S(1)} %add.380), channel_id=1, source_target_pairs={{0,1},{1,0},{2,3},{3,2},{4,5},{5,4},{6,7},{7,6},{8,9},{9,8},{10,11... | collective-permute-start | bytes 3080 | tf_op jit(solution)/shard_map/ppermute | solution.py:839
  898.5 37.6 %collective-permute-start.59 = (bf16[2,128,2048]{2,1,0:T(8,128)(2,1)}, bf16[2,128,2048]{2,1,0:T(8,128)(2,1)S(1)}, u32[]{:S(2)}, u32[]{:S(2)}) collective-permute-start(bf16[2,128,2048]{2,1,0:T(8,128)(2,1)} %add_convert_fusion.3), channel_id=1, source_target_pairs={{0,2},{1,3},{2,4},{3,5},{4,6},{5,7},{6,0},{7,1},{8,10},{9,11},{10,... | collective-permute-start | bytes 3145736 | tf_op jit(solution)/shard_map/ppermute | solution.py:31
  898.5 44.6 %collective-permute-start.55 = (bf16[2,128,2048]{2,1,0:T(8,128)(2,1)}, bf16[2,128,2048]{2,1,0:T(8,128)(2,1)S(1)}, u32[]{:S(2)}, u32[]{:S(2)}) collective-permute-start(bf16[2,128,2048]{2,1,0:T(8,128)(2,1)} %after.133), channel_id=1, source_target_pairs={{0,1},{1,0},{2,3},{3,2},{4,5},{5,4},{6,7},{7,6},{8,9},{9,8},{10,11... | collective-permute-start | bytes 3145736 | tf_op jit(solution)/shard_map/ppermute | solution.py:31
  899.8 45.6 %collective-permute-start.57 = (bf16[2,128,2048]{2,1,0:T(8,128)(2,1)}, bf16[2,128,2048]{2,1,0:T(8,128)(2,1)S(1)}, u32[]{:S(2)}, u32[]{:S(2)}) collective-permute-start(bf16[2,128,2048]{2,1,0:T(8,128)(2,1)} %after.135), channel_id=1, source_target_pairs={{0,1},{1,0},{2,3},{3,2},{4,5},{5,4},{6,7},{7,6},{8,9},{9,8},{10,11... | collective-permute-start | bytes 3145736 | tf_op jit(solution)/shard_map/ppermute | solution.py:31
  904.2 42.1 %collective-permute-start.56 = (bf16[2,128,2048]{2,1,0:T(8,128)(2,1)}, bf16[2,128,2048]{2,1,0:T(8,128)(2,1)}, u32[]{:S(2)}, u32[]{:S(2)}) collective-permute-start(bf16[2,128,2048]{2,1,0:T(8,128)(2,1)} %add_convert_fusion.4), channel_id=1, source_target_pairs={{0,2},{1,3},{2,4},{3,5},{4,6},{5,7},{6,0},{7,1},{8,10},{9,11},{10,... | collective-permute-start | bytes 3145736 | tf_op jit(solution)/shard_map/ppermute | solution.py:31
  909.0 34.2 %collective-permute-start.58 = (f32[2,128]{1,0:T(2,128)S(1)}, f32[2,128]{1,0:T(2,128)S(1)}, u32[]{:S(2)}, u32[]{:S(2)}) collective-permute-start(f32[2,128]{1,0:T(2,128)S(1)} %add.383), channel_id=1, source_target_pairs={{0,2},{1,3},{2,0},{3,1},{4,6},{5,7},{6,4},{7,5},{8,10},{9,11},{10,... | collective-permute-start | bytes 3080 | tf_op jit(solution)/shard_map/ppermute | solution.py:839
  (92 other events, 438.1 us)
Sparse Core Ops, SparseCore 0:
  11.2 34.1 all-gather.5
  47.0 58.2 all-gather.7
  106.9 105.9 all-gather.11
  214.2 105.9 all-gather.9
  321.6 105.9 all-gather.13
  576.7 124.9 reduce-scatter.3
  704.5 151.4 reduce-scatter.5
  858.5 126.0 reduce-scatter.7

commit v8 on v7

--- a/solution.py
+++ b/solution.py
@@ -539,16 +539,17 @@
     out_ref[0] = dot(left, right, 0, 0).astype(bf16)
 
 
-def bank_grad(left, right, ties=()):
-    count, _, capacity, _ = left.shape
+def bank_grad(left, right, ties=(), first=0, count=None):
+    capacity = left.shape[2]
+    count = count or left.shape[0]
     result = jax.ShapeDtypeStruct((count, D, FFE), bf16)
     return call(
         bank_kernel,
         "bank_grad",
         (count, D // part),
         [
-            (left, pl.BlockSpec((1, 2, capacity, part), lambda e, d: (e, 0, 0, d))),
-            (right, pl.BlockSpec((1, 2, capacity, FFE), lambda e, d: (e, 0, 0, 0))),
+            (left, pl.BlockSpec((1, 2, capacity, part), lambda e, d: (first + e, 0, 0, d))),
+            (right, pl.BlockSpec((1, 2, capacity, FFE), lambda e, d: (first + e, 0, 0, 0))),
         ],
         [(result, pl.BlockSpec((1, part, FFE), lambda e, d: (e, d, 0)))],
         ties=ties,
@@ -691,10 +692,9 @@
     )
     o_heads = attend(qkv, tables)
 
-    inverse_seq = jnp.argsort(seq_order)
-    o_heads = reorder(o_heads, inverse_seq, axis=0)
+    o_heads = reorder(o_heads, seq_order, axis=0)
     g_blocks, g_next = ring_gather(
-        after(cotangent, packed), "seq", (lambda _: qkv, lambda _: o_heads), True, stop=2
+        after(cotangent, packed, *tables), "seq", (lambda _: qkv, lambda _: o_heads), True, stop=2
     )
     o_heads = after(o_heads, g_next)
     o_back = lax.all_to_all(o_heads, "seq", split_axis=0, concat_axis=0, tiled=True)
@@ -742,52 +742,72 @@
         grad_rows, grad_hidden = dispatch(g_blocks, slots, weights, w_down, capacity, True)
         return keep(grad_rows=grad_rows, grad_hidden=grad_hidden)
 
-    def take_work(_):
-        taken, gate_act = dispatch(
-            h_blocks, slots, weights, w_gate, capacity, False, (done["grad_rows"],)
-        )
-        return keep(taken=taken, gate_act=gate_act)
+    pair = local_experts // 2
+
+    def take_work(first):
+        def work(ties):
+            takes = dispatch(
+                h_blocks,
+                slots,
+                weights,
+                w_gate,
+                capacity,
+                False,
+                tuple(ties) + (done["grad_rows"],),
+                first,
+                local_experts - pair if first else pair,
+                done.get("takes", ()),
+            )
+            return keep(taken=takes[0], gate_act=takes[1], takes=takes)
+
+        return work
+
+    def act_work(_):
+        acts = activate(done["taken"], done["gate_act"], done["grad_hidden"], w_up)
+        return keep(tail=acts[0], acts=acts)
 
     o_all = ring_gather(
-        after(o_heads.reshape(group * micro, width), g_blocks[-1]), "seq", (grad_work, take_work), True
+        after(o_heads.reshape(group * micro, width), g_blocks[-1]),
+        "seq",
+        (grad_work, take_work(0), take_work(pair), act_work),
+        True,
     )
     o_all = o_all[:-2] + [jnp.concatenate(o_all[-2:], axis=0)] if len(o_all) > ns else o_all
     grad_rows, taken = done["grad_rows"], done["taken"]
-    hidden, grad_gate_act, grad_up_act = activate(
-        taken, done["gate_act"], done["grad_hidden"], w_up, (o_all[-1],)
-    )
-    first = combined((grad_gate_act, grad_up_act), (w_gate, w_up), 0, False)
-    second = combined((grad_gate_act, grad_up_act), (w_gate, w_up), 1, False, (first[0],))
-
-    def down_work(ties):
-        return keep(whole_down=bank_grad(grad_rows, hidden, ties))
-
-    def down_then(moved):
-        keep(sum_down=after(done["whole_down"], *moved))
+    hidden, grad_gate_act, grad_up_act = done["acts"]
+    first = combined((grad_gate_act, grad_up_act), (w_gate, w_up), 0, False, (o_all[-1],))
+    whole_down = [bank_grad(grad_rows, hidden, (first[0],), 0, pair)]
+    second = combined(
+        (grad_gate_act, grad_up_act), (w_gate, w_up), 1, False, (whole_down[0],)
+    )
 
     def mixed_work(h):
         def work(ties):
+            if h == 0:
+                whole_down.append(bank_grad(grad_rows, hidden, ties, pair, local_experts - pair))
+                ties = (whole_down[1],)
             mixed = combined((hidden,), (w_down,), h, True, ties)
             done.setdefault("mixed", []).extend(mixed)
             return mixed[0]
 
         return work
+
+    def gate_work(ties):
+        return keep(whole_gate=bank_grad(taken, grad_gate_act, ties))
 
     parts = [v.reshape(micro, rows, D) for v in list(first) + list(second)]
     grad_h_two = ring_scatter(
         parts,
         "seq",
-        (lambda _: second[0], down_work, mixed_work(0), mixed_work(1)),
-        {
-            1: down_then,
-            3: lambda moved: keep(last=moved),
-        },
+        (lambda _: second[0], mixed_work(0), mixed_work(1), gate_work),
+        {3: lambda moved: keep(sum_gate=after(done["whole_gate"], *moved))},
     ).reshape(tokens, D)
 
     def bank_sum(whole):
         return lax.psum_scatter(whole, "fsdp", scatter_dimension=1, tiled=True).astype(f32)
 
-    grad_down = bank_sum(done["sum_down"])
+    grad_down = jnp.concatenate([bank_sum(v) for v in whole_down], axis=0)
+    grad_gate = bank_sum(done["sum_gate"])
 
     grad_gain_two = jnp.sum(grad_h_two * normed_two, axis=0)
     grad_unit = grad_h_two * gain_two
@@ -803,9 +823,9 @@
             jnp.moveaxis(cut, 2, 0), "seq", split_axis=0, concat_axis=0, tiled=True
         )
 
-    whole_gate = bank_grad(taken, grad_gate_act, (grad_o,))
-    (do_blocks,) = together((whole_gate,), to_heads(grad_o))
-    grad_gate = bank_sum(after(whole_gate, do_blocks))
+    whole_up = bank_grad(taken, grad_up_act, (grad_o,))
+    (do_blocks,) = together((whole_up,), to_heads(grad_o))
+    grad_up = bank_sum(after(whole_up, do_blocks))
     do_heads = reorder(do_blocks, seq_order)
 
     mixed = [v.reshape(micro, rows, D) for v in done["mixed"]]
@@ -828,7 +848,7 @@
         columns.reshape(micro * group, width),
         gains,
         relative_order("fsdp"),
-        inverse_seq,
+        seq_order,
         (total,),
     )
     left = exchanges()
@@ -849,21 +869,19 @@
     )
     head = head + moved
 
-    whole_up = bank_grad(taken, grad_up_act, (one,))
     whole = [after(v, one) for v in whole]
-    owned = ring_scatter(whole, "fsdp", (None, lambda _: whole_up)).astype(bf16)
+    owned = ring_scatter(whole, "fsdp").astype(bf16)
 
     total = ahead(add(row_sum(two, mixed, 2, "seq"), total).astype(bf16), "seq")
     grad_total = ahead(row_sum(one, part_h_one, 1, "seq"), "seq")
     total, grad_total, three, two, owned = together(
-        (whole_up,),
+        (),
         total,
         grad_total,
         row_move(mixed, 3, "seq"),
         row_move(part_h_one, 2, "seq"),
         owned,
     )
-    grad_up = bank_sum(after(whole_up, owned))
     owned = lax.all_to_all(
         owned.reshape(ns, share, -1), "seq", split_axis=0, concat_axis=0, tiled=True
     )

time: 1010 us -> 985 us (0.975)
  waiting for transfers between devices: 316 us -> 287 us
    reduce_scatter x3 -> x4, waiting for transfers between devices: 22.8 us -> 0.01 us  [bank_sum(): lax.psum_scatter(whole, 'fsdp', scatter_dimension=1, tiled=True).astype(f32)]
    pallas_call x11 -> x13, Pallas kernels: 284 us -> 290 us  [call(): pl.pallas_call(run, grid=grid, in_specs=[spec for _, spec in ins] + [pl.B...]
    unnamed x184 -> x166, local copies, waits for them, and re-layouts: 46.2 us -> 43.3 us
  transfers between devices with their start and end apart: 72 -> 73, of which waited for: 32 -> 35; matrix products, arithmetic and copies ran while one was open for 17% -> 17% of each run, Pallas kernels for 29% -> 33%
where the time goes in v8:
time: 985 us; the launch traced here: 974 us
  Pallas kernels  361 us (37%)
  waiting for transfers between devices  287 us (29%)
  local copies, waits for them, and re-layouts  98.9 us (10%)
  other arithmetic  91.8 us (9%)
  starting transfers between devices  71.2 us (7%)
  blocking collectives  28.1 us (3%)
  matrix products  20.9 us (2%)
  between operations  15.5 us (2%)
    pallas_call x13, Pallas kernels, call(): pl.pallas_call(run, grid=grid, in_specs=[spec for _, spec in ins] + [pl.B...  290 us
    ppermute x56, waiting for transfers between devices, shift(): return lax.ppermute(value, axis, pairs)  269 us
    ppermute x56, starting transfers between devices, shift(): return lax.ppermute(value, axis, pairs)  51.5 us
    unnamed x166, local copies, waits for them, and re-layouts  43.3 us
    pallas_call x1, Pallas kernels, attend_back(): pl.pallas_call(lambda *refs: attend_back_kernel(tile, *refs[:7], *refs[-2...  33.1 us
    all_to_all x1, blocking collectives, body(): lax.all_to_all(o_heads, 'seq', split_axis=0, concat_axis=0, tiled=True)  28.1 us
    pallas_call x1, Pallas kernels, proj_grads(): pl.pallas_call(run, grid_spec=pltpu.PrefetchScalarGridSpec(num_scalar_pre...  20.7 us
  transfers between devices with their start and end apart: 73, of which 35 were waited for; matrix products, arithmetic and copies ran while one was open for 17% of the time, Pallas kernels for 33%

profile of v8, /device:TPU:0, one launch (start us, length us, event | category | flops | bytes accessed | tf_op | source)
XLA Modules:
  0.0 974.3 jit_solution(11061999521554490568)
XLA Ops:
  17.6 3.0 collective-permute-start.1
  22.1 25.0 %collective-permute-done.1 = bf16[2,128,2176]{2,1,0:T(8,128)(2,1)S(1)} collective-permute-done((bf16[2,128,2176]{2,1,0:T(8,128)(2,1)S(1)}, bf16[2,128,2176]{2,1,0:T(8,128)(2,1)S(1)}, u32[]{:S(2)}, u32[]{:S(2)}) %collective-permute-start.1) | collective-permute-done | bytes 1114144 | tf_op jit(solution)/shard_map/ppermute | solution.py:31
  53.4 3.1 fusion.27
  58.9 15.9 %collective-permute-done.3 = bf16[2,128,2176]{2,1,0:T(8,128)(2,1)} collective-permute-done((bf16[2,128,2176]{2,1,0:T(8,128)(2,1)S(1)}, bf16[2,128,2176]{2,1,0:T(8,128)(2,1)}, u32[]{:S(2)}, u32[]{:S(2)}) %collective-permute-start.3) | collective-permute-done | bytes 1114144 | tf_op jit(solution)/shard_map/ppermute | solution.py:31
  82.6 19.8 %collective-permute-done.5 = bf16[2,128,2176]{2,1,0:T(8,128)(2,1)S(1)} collective-permute-done((bf16[2,128,2176]{2,1,0:T(8,128)(2,1)}, bf16[2,128,2176]{2,1,0:T(8,128)(2,1)S(1)}, u32[]{:S(2)}, u32[]{:S(2)}) %collective-permute-start.5) | collective-permute-done | bytes 1114144 | tf_op jit(solution)/shard_map/ppermute | solution.py:31
  105.9 8.1 collective-permute-done.6
  118.5 6.5 fusion
  126.9 5.3 fusion.2
  132.2 8.0 fusion.4.refs_0_.refs_1_
  148.0 16.5 %attend.1 = bf16[8,2,128,256]{3,2,1,0:T(8,128)(2,1)S(1)} custom-call(bf16[8,2,128,768]{3,2,1,0:T(8,128)(2,1)S(1)} %copy-done.2, f32[1024,128]{1,0:T(8,128)S(1)} %copy-done.8, f32[1024,128]{1,0:T(8,128)S(1)} %copy-done.6, s32[2,1,1024]{2,1,0:T(1,128)S(1)} %bitcast.193, s32[2,1024,1]{2,1,0:T(8,128)S(1)} %copy-done.3, f32[2,128]{1,0:T(2,128)S(1)} %copy-done.14), custom_call_target="tpu_custom_call" | custom-call | flops 1 | bytes 1 | tf_op jit(solution)/shard_map/attend/pallas_call | solution.py:281
  165.5 2.8 gather_fusion.1
  168.3 28.1 %all_to_all.20 = bf16[8,2,128,256]{3,2,1,0:T(8,128)(2,1)S(1)} all-to-all(bf16[8,2,128,256]{3,2,1,0:T(8,128)(2,1)} %after.75), channel_id=1, replica_groups=mesh['fsdp'=4,'seq'=8] {'seq'}, dimensions={0} | all-to-all | bytes 2097152 | tf_op jit(solution)/shard_map/all_to_all | solution.py:700
  198.3 6.5 multiply_reduce_fusion.3
  208.4 21.0 %collective-permute-done.12.refs_0_ = bf16[2,128,2048]{2,1,0:T(8,128)(2,1)} collective-permute-done((bf16[2,128,2048]{2,1,0:T(8,128)(2,1)S(1)}, bf16[2,128,2048]{2,1,0:T(8,128)(2,1)}, u32[]{:S(2)}, u32[]{:S(2)}) %collective-permute-start.12) | collective-permute-done | bytes 1048608 | tf_op jit(solution)/shard_map/ppermute | solution.py:31
  229.3 2.8 collective-permute-done.13.refs_1_.refs_0_
  233.3 20.5 %collective-permute-done.14.refs_0_ = bf16[2,128,2048]{2,1,0:T(8,128)(2,1)} collective-permute-done((bf16[2,128,2048]{2,1,0:T(8,128)(2,1)}, bf16[2,128,2048]{2,1,0:T(8,128)(2,1)}, u32[]{:S(2)}, u32[]{:S(2)}) %collective-permute-start.14) | collective-permute-done | bytes 1048608 | tf_op jit(solution)/shard_map/ppermute | solution.py:31
  253.7 3.0 collective-permute-done.15.refs_1_.refs_0_
  257.3 20.1 %collective-permute-done.16.refs_0_ = bf16[2,128,2048]{2,1,0:T(8,128)(2,1)} collective-permute-done((bf16[2,128,2048]{2,1,0:T(8,128)(2,1)}, bf16[2,128,2048]{2,1,0:T(8,128)(2,1)}, u32[]{:S(2)}, u32[]{:S(2)}) %collective-permute-start.16) | collective-permute-done | bytes 1048608 | tf_op jit(solution)/shard_map/ppermute | solution.py:31
  283.2 8.8 collective-permute-done.18.refs_0_
  292.0 4.7 collective-permute-done.19.refs_1_.refs_0_
  296.7 16.5 %collective-permute-done.20.refs_0_ = bf16[2,128,2048]{2,1,0:T(8,128)(2,1)} collective-permute-done((bf16[2,128,2048]{2,1,0:T(8,128)(2,1)}, bf16[2,128,2048]{2,1,0:T(8,128)(2,1)}, u32[]{:S(2)}, u32[]{:S(2)}) %collective-permute-start.20) | collective-permute-done | bytes 1048608 | tf_op jit(solution)/shard_map/ppermute | solution.py:31
  313.2 4.9 collective-permute-done.21.refs_1_.refs_0_
  328.7 6.4 collective-permute-done.22.refs_1_.refs_0_
  340.5 3.3 slice_add_fusion
  346.8 34.2 %dispatch.3 = (bf16[4,2,384,2048]{3,2,1,0:T(8,128)(2,1)}, f32[4,2,384,1024]{3,2,1,0:T(8,128)}) custom-call(bf16[256,2048]{1,0:T(8,128)(2,1)} %bitcast.206, bf16[256,2048]{1,0:T(8,128)(2,1)} %bitcast.210, bf16[256,2048]{1,0:T(8,128)(2,1)} %bitcast.209, bf16[256,2048]{1,0:T(8,128)(2,1)} %bitcast.37.refs_3_, bf16[256,2048]{1,0:T(8,128)(2,1)} %bitcast.38.refs_4_, ...), custom_call_target="tpu_custom_call" | custom-call | flops 1 | bytes 1 | tf_op jit(solution)/shard_map/dispatch/pallas_call | solution.py:427
  381.8 19.8 %dispatch.4 = (bf16[4,2,384,2048]{3,2,1,0:T(8,128)(2,1)}, f32[4,2,384,1024]{3,2,1,0:T(8,128)}) custom-call(bf16[256,2048]{1,0:T(8,128)(2,1)} %copy-done.40, bf16[256,2048]{1,0:T(8,128)(2,1)} %bitcast.18.refs_1_, bf16[256,2048]{1,0:T(8,128)(2,1)} %bitcast.19.refs_2_, bf16[256,2048]{1,0:T(8,128)(2,1)} %bitcast.20.refs_3_, bf16[256,2048]{1,0:T(8,128)(2,1)} %bitcast.21.refs_4_, ...), custom_call_target="tpu_custom_call" | custom-call | flops 1 | bytes 1 | tf_op jit(solution)/shard_map/dispatch/pallas_call | solution.py:427
  407.9 19.7 %dispatch.5 = (bf16[4,2,384,2048]{3,2,1,0:T(8,128)(2,1)}, f32[4,2,384,1024]{3,2,1,0:T(8,128)}) custom-call(bf16[256,2048]{1,0:T(8,128)(2,1)} %copy-done.40, bf16[256,2048]{1,0:T(8,128)(2,1)} %bitcast.18.refs_1_, bf16[256,2048]{1,0:T(8,128)(2,1)} %bitcast.19.refs_2_, ...), custom_call_target="tpu_custom_call", output_to_operand_aliasing={{0}: (12, {}), {1}: (13, {})} | custom-call | flops 1 | bytes 1 | tf_op jit(solution)/shard_map/dispatch/pallas_call | solution.py:427
  433.0 32.2 %activate.1 = (bf16[4,2,384,1024]{3,2,1,0:T(8,128)(2,1)}, bf16[4,2,384,1024]{3,2,1,0:T(8,128)(2,1)}, bf16[4,2,384,1024]{3,2,1,0:T(8,128)(2,1)}) custom-call(bf16[4,2,384,2048]{3,2,1,0:T(8,128)(2,1)} %get-tuple-element.55.refs_0_.refs_1_, f32[4,2,384,1024]{3,2,1,0:T(8,128)} %get-tuple-element.56.refs_1_, f32[4,2,384,1024]{3,2,1,0:T(8,128)} %get-tuple-element.57.refs_2_, ...), custom_call_target="tpu_custom_call" | custom-call | flops 1 | bytes 1 | tf_op jit(solution)/shard_map/activate/pallas_call | solution.py:427
  470.1 27.7 %combine.4 = (bf16[256,2048]{1,0:T(8,128)(2,1)}, bf16[256,2048]{1,0:T(8,128)(2,1)}, bf16[256,2048]{1,0:T(8,128)(2,1)}, bf16[256,2048]{1,0:T(8,128)(2,1)}) custom-call(bf16[4,2,384,1024]{3,2,1,0:T(8,128)(2,1)} %get-tuple-element.59.refs_0_.refs_1_, bf16[4,2,384,1024]{3,2,1,0:T(8,128)(2,1)} %get-tuple-element.60.refs_1_, ...), custom_call_target="tpu_custom_call" | custom-call | flops 1 | bytes 1 | tf_op jit(solution)/shard_map/combine/pallas_call | solution.py:427
  497.8 12.9 %bank_grad.4.refs_7_ = bf16[2,2048,1024]{2,1,0:T(8,128)(2,1)} custom-call(bf16[4,2,384,2048]{3,2,1,0:T(8,128)(2,1)} %get-tuple-element.52.refs_1_.refs_14_.refs_16_.refs_0_, bf16[4,2,384,1024]{3,2,1,0:T(8,128)(2,1)} %get-tuple-element.58.refs_1_.refs_0_, bf16[256,2048]{1,0:T(8,128)(2,1)} %get-tuple-element.62.refs_2_), custom_call_target="tpu_custom_call" | custom-call | flops 1 | bytes 1 | tf_op jit(solution)/shard_map/bank_grad/pallas_call | solution.py:427
  512.9 28.5 %combine.5 = (bf16[256,2048]{1,0:T(8,128)(2,1)}, bf16[256,2048]{1,0:T(8,128)(2,1)}, bf16[256,2048]{1,0:T(8,128)(2,1)}, bf16[256,2048]{1,0:T(8,128)(2,1)}) custom-call(bf16[4,2,384,1024]{3,2,1,0:T(8,128)(2,1)} %get-tuple-element.59.refs_0_.refs_1_, bf16[4,2,384,1024]{3,2,1,0:T(8,128)(2,1)} %get-tuple-element.60.refs_1_, ...), custom_call_target="tpu_custom_call" | custom-call | flops 1 | bytes 1 | tf_op jit(solution)/shard_map/combine/pallas_call | solution.py:427
  541.5 12.9 %bank_grad.5.refs_5_ = bf16[2,2048,1024]{2,1,0:T(8,128)(2,1)} custom-call(bf16[4,2,384,2048]{3,2,1,0:T(8,128)(2,1)} %get-tuple-element.52.refs_1_.refs_14_.refs_16_.refs_0_, bf16[4,2,384,1024]{3,2,1,0:T(8,128)(2,1)} %get-tuple-element.58.refs_1_.refs_0_, bf16[2,128,2048]{2,1,0:T(8,128)(2,1)} %after.98.refs_2_), custom_call_target="tpu_custom_call" | custom-call | flops 1 | bytes 1 | tf_op jit(solution)/shard_map/bank_grad/pallas_call | solution.py:427
  558.3 20.2 %combine.6 = (bf16[256,2048]{1,0:T(8,128)(2,1)}, bf16[256,2048]{1,0:T(8,128)(2,1)}, bf16[256,2048]{1,0:T(8,128)(2,1)}, bf16[256,2048]{1,0:T(8,128)(2,1)}) custom-call(bf16[4,2,384,1024]{3,2,1,0:T(8,128)(2,1)} %get-tuple-element.58.refs_1_.refs_0_, bf16[4,2048,1024]{2,1,0:T(8,128)(2,1)} %all-gather.12.cloned.1.call-done.refs_11_.refs_1_, ...), custom_call_target="tpu_custom_call" | custom-call | flops 1 | bytes 1 | tf_op jit(solution)/shard_map/combine/pallas_call | solution.py:427
  583.0 20.0 %combine.7 = (bf16[256,2048]{1,0:T(8,128)(2,1)}, bf16[256,2048]{1,0:T(8,128)(2,1)}, bf16[256,2048]{1,0:T(8,128)(2,1)}, bf16[256,2048]{1,0:T(8,128)(2,1)}) custom-call(bf16[4,2,384,1024]{3,2,1,0:T(8,128)(2,1)} %get-tuple-element.58.refs_1_.refs_0_, bf16[4,2048,1024]{2,1,0:T(8,128)(2,1)} %all-gather.12.cloned.1.call-done.refs_11_.refs_1_, ...), custom_call_target="tpu_custom_call" | custom-call | flops 1 | bytes 1 | tf_op jit(solution)/shard_map/combine/pallas_call | solution.py:427
  608.9 24.7 %bank_grad.6.refs_1_.refs_0_ = bf16[4,2048,1024]{2,1,0:T(8,128)(2,1)} custom-call(bf16[4,2,384,2048]{3,2,1,0:T(8,128)(2,1)} %get-tuple-element.55.refs_0_.refs_1_, bf16[4,2,384,1024]{3,2,1,0:T(8,128)(2,1)} %get-tuple-element.59.refs_0_.refs_1_, bf16[2,128,2048]{2,1,0:T(8,128)(2,1)} %after.101.refs_2_, bf16[2,128,2048]{2,1,0:T(8,128)(2,1)} %after.102.refs_3_), custom_call_target="tpu_custom_call" | custom-call | flops 1 | bytes 1 | tf_op jit(solution)/shard_map/bank_grad/pallas_call | solution.py:427
  639.0 6.2 convolution_convert_fusion.refs_2_
  646.8 4.3 all-to-all-start.1
  651.1 25.3 %bank_grad.7.refs_1_.refs_0_ = bf16[4,2048,1024]{2,1,0:T(8,128)(2,1)} custom-call(bf16[4,2,384,2048]{3,2,1,0:T(8,128)(2,1)} %get-tuple-element.55.refs_0_.refs_1_, bf16[4,2,384,1024]{3,2,1,0:T(8,128)(2,1)} %get-tuple-element.60.refs_1_, bf16[256,2048]{1,0:T(8,128)(2,1)} %copy-done.50), custom_call_target="tpu_custom_call" | custom-call | flops 1 | bytes 1 | tf_op jit(solution)/shard_map/bank_grad/pallas_call | solution.py:427
  679.4 6.5 all-to-all-start.2
  689.4 2.9 gather_fusion.2
  697.7 33.1 %attend_back.1 = (bf16[8,2,128,768]{3,2,1,0:T(8,128)(2,1)S(1)}, f32[4,2,128]{2,1,0:T(2,128)S(1)}) custom-call(bf16[8,2,128,768]{3,2,1,0:T(8,128)(2,1)S(1)} %copy-done.2, bf16[8,2,128,256]{3,2,1,0:T(8,128)(2,1)S(1)} %copy-done.10, f32[1024,128]{1,0:T(8,128)S(1)} %copy-done.9, f32[1024,128]{1,0:T(8,128)S(1)} %copy-done.7, s32[2,1,1024]{2,1,0:T(1,128)S(1)} %bitcast.194, ...), custom_call_target="tpu_custom_call" | custom-call | flops 1 | bytes 1 | tf_op jit(solution)/shard_map/attend_back/pallas_call | solution.py:298
  733.1 12.3 %part_grads.1 = (bf16[256,2048]{1,0:T(8,128)(2,1)}, bf16[256,2048]{1,0:T(8,128)(2,1)}, bf16[256,2048]{1,0:T(8,128)(2,1)}, bf16[256,2048]{1,0:T(8,128)(2,1)}, bf1...) custom-call(bf16[2048,768]{1,0:T(8,128)(2,1)} %bitcast.190, ...), custom_call_target="tpu_custom_call" | custom-call | flops 1 | bytes 1 | tf_op jit(solution)/shard_map/part_grads/pallas_call | solution.py:427
  755.1 20.7 %proj_grads.1 = (bf16[512,1152]{1,0:T(8,128)(2,1)}, bf16[512,1152]{1,0:T(8,128)(2,1)}, bf16[512,1152]{1,0:T(8,128)(2,1)}, bf16[512,1152]{1,0:T(8,128)(2,1)}) custom-call(s32[4]{0:T(128)} %fusion.41.refs_0_, s32[8]{0:T(128)} %get-tuple-element.101.refs_1_, bf16[2048,2048]{1,0:T(8,128)(2,1)} %bitcast.202, bf16[2048,768]{1,0:T(8,128)(2,1)} %bitcast.191, ...), custom_call_target="tpu_custom_call" | custom-call | flops 1 | bytes 1 | tf_op jit(solution)/shard_map/proj_grads/pallas_call | solution.py:388
  780.4 3.0 add_convert_fusion.2
  787.4 2.7 add_convert_fusion.6
  791.6 20.1 %collective-permute-done.47.refs_1_.refs_0_ = bf16[512,1152]{1,0:T(8,128)(2,1)} collective-permute-done((bf16[512,1152]{1,0:T(8,128)(2,1)}, bf16[512,1152]{1,0:T(8,128)(2,1)}, u32[]{:S(2)}, u32[]{:S(2)}) %collective-permute-start.47) | collective-permute-done | bytes 1179680 | tf_op jit(solution)/shard_map/ppermute | solution.py:31
  813.2 3.6 add_convert_fusion.refs_4_.refs_0_
  816.8 8.6 collective-permute-done.51.refs_3_.refs_0_
  825.4 10.0 %collective-permute-done.48.refs_0_ = bf16[2,128,2048]{2,1,0:T(8,128)(2,1)} collective-permute-done((bf16[2,128,2048]{2,1,0:T(8,128)(2,1)}, bf16[2,128,2048]{2,1,0:T(8,128)(2,1)}, u32[]{:S(2)}, u32[]{:S(2)}) %collective-permute-start.48) | collective-permute-done | bytes 1048608 | tf_op jit(solution)/shard_map/ppermute | solution.py:31
  835.5 4.0 all-to-all-start.3
  841.5 3.1 add_convert_fusion.5
  846.6 6.2 maximum_convert_fusion.refs_1_
  852.8 23.5 %collective-permute-done.53.refs_2_.refs_0_ = bf16[2,128,2048]{2,1,0:T(8,128)(2,1)S(1)} collective-permute-done((bf16[2,128,2048]{2,1,0:T(8,128)(2,1)}, bf16[2,128,2048]{2,1,0:T(8,128)(2,1)S(1)}, u32[]{:S(2)}, u32[]{:S(2)}) %collective-permute-start.53) | collective-permute-done | bytes 1048608 | tf_op jit(solution)/shard_map/ppermute | solution.py:31
  876.3 8.3 collective-permute-done.52.refs_0_
  884.6 5.4 all-to-all-done.3.refs_4_.refs_0_
  891.0 3.1 add_convert_fusion.3
  905.9 3.7 reshape.579
  911.6 5.4 fusion.63
  921.6 6.6 convert_element_type.436.refs_1_
  928.3 9.5 collective-permute-done.58.refs_3_.refs_0_
  937.7 4.0 collective-permute-done.56.refs_0_
  941.7 3.2 collective-permute-done.55.refs_4_.refs_0_
  957.0 2.9 fusion.19
  960.5 6.8 convert_element_type.465
  (462 shorter events, 190.6 us)
Async XLA Ops:
  7.2 117.8 %all-gather.6.cloned.1.call-start = ((), (), s32[]{:S(2)}) async-start(), calls=%async_computation.8 | async-start | bytes 4587520 | tf_op jit(solution)/shard_map/all_gather | solution.py:647
  12.0 186.3 %all-gather.8.cloned.1.call-start = ((), (), s32[]{:S(2)}) async-start(), calls=%async_computation.9 | async-start | bytes 10485760 | tf_op jit(solution)/shard_map/all_gather | solution.py:647
  12.7 334.0 %all-gather.12.cloned.1.call-start = ((), (), s32[]{:S(2)}) async-start(), calls=%async_computation.11 | async-start | bytes 20971520 | tf_op jit(solution)/shard_map/all_gather | solution.py:647
  13.5 368.3 %all-gather.10.cloned.1.call-start = ((), (), s32[]{:S(2)}) async-start(), calls=%async_computation.10 | async-start | bytes 20971520 | tf_op jit(solution)/shard_map/all_gather | solution.py:647
  14.1 418.9 %all-gather.14.cloned.1.call-start = ((), (), s32[]{:S(2)}) async-start(), calls=%async_computation.12 | async-start | bytes 20971520 | tf_op jit(solution)/shard_map/all_gather | solution.py:647
  14.7 831.9 %reduce-scatter.5.cloned.1.call-start = ((), (), s32[]{:S(2)}) async-start(), calls=%async_computation.13 | async-start | bytes 10485760 | tf_op jit(solution)/shard_map/reduce_scatter | solution.py:807
  17.6 29.6 %collective-permute-start.1 = (bf16[2,128,2176]{2,1,0:T(8,128)(2,1)S(1)}, bf16[2,128,2176]{2,1,0:T(8,128)(2,1)S(1)}, u32[]{:S(2)}, u32[]{:S(2)}) collective-permute-start(bf16[2,128,2176]{2,1,0:T(8,128)(2,1)S(1)} %get-tuple-element.109), channel_id=1, source_target_pairs={{0,2},{1,3},{2,4},{3,5},{4,6},{5,7},{6,0},{7,1},{8,10},{9,11},{10,... | collective-permute-start | bytes 3342344 | tf_op jit(solution)/shard_map/ppermute | solution.py:31
  20.6 35.9 %collective-permute-start = (bf16[2,128,2176]{2,1,0:T(8,128)(2,1)S(1)}, bf16[2,128,2176]{2,1,0:T(8,128)(2,1)}, u32[]{:S(2)}, u32[]{:S(2)}) collective-permute-start(bf16[2,128,2176]{2,1,0:T(8,128)(2,1)S(1)} %get-tuple-element.109), channel_id=1, source_target_pairs={{0,1},{1,0},{2,3},{3,2},{4,5},{5,4},{6,7},{7,6},{8,9},{9,8},{10,11... | collective-permute-start | bytes 3342344 | tf_op jit(solution)/shard_map/ppermute | solution.py:31
  47.2 27.7 %collective-permute-start.3 = (bf16[2,128,2176]{2,1,0:T(8,128)(2,1)S(1)}, bf16[2,128,2176]{2,1,0:T(8,128)(2,1)}, u32[]{:S(2)}, u32[]{:S(2)}) collective-permute-start(bf16[2,128,2176]{2,1,0:T(8,128)(2,1)S(1)} %collective-permute-done.1), channel_id=1, source_target_pairs={{0,2},{1,3},{2,4},{3,5},{4,6},{5,7},{6,0},{7,1},{8,10},{9,11},{10,... | collective-permute-start | bytes 3342344 | tf_op jit(solution)/shard_map/ppermute | solution.py:31
  51.9 27.3 %collective-permute-start.2 = (bf16[2,128,2176]{2,1,0:T(8,128)(2,1)S(1)}, bf16[2,128,2176]{2,1,0:T(8,128)(2,1)S(1)}, u32[]{:S(2)}, u32[]{:S(2)}) collective-permute-start(bf16[2,128,2176]{2,1,0:T(8,128)(2,1)S(1)} %collective-permute-done.1), channel_id=1, source_target_pairs={{0,1},{1,0},{2,3},{3,2},{4,5},{5,4},{6,7},{7,6},{8,9},{9,8},{10,11... | collective-permute-start | bytes 3342344 | tf_op jit(solution)/shard_map/ppermute | solution.py:31
  74.8 28.7 %collective-permute-start.4 = (bf16[2,128,2176]{2,1,0:T(8,128)(2,1)}, bf16[2,128,2176]{2,1,0:T(8,128)(2,1)S(1)}, u32[]{:S(2)}, u32[]{:S(2)}) collective-permute-start(bf16[2,128,2176]{2,1,0:T(8,128)(2,1)} %collective-permute-done.3), channel_id=1, source_target_pairs={{0,1},{1,0},{2,3},{3,2},{4,5},{5,4},{6,7},{7,6},{8,9},{9,8},{10,11... | collective-permute-start | bytes 3342344 | tf_op jit(solution)/shard_map/ppermute | solution.py:31
  76.1 26.3 %collective-permute-start.5 = (bf16[2,128,2176]{2,1,0:T(8,128)(2,1)}, bf16[2,128,2176]{2,1,0:T(8,128)(2,1)S(1)}, u32[]{:S(2)}, u32[]{:S(2)}) collective-permute-start(bf16[2,128,2176]{2,1,0:T(8,128)(2,1)} %collective-permute-done.3), channel_id=1, source_target_pairs={{0,2},{1,3},{2,4},{3,5},{4,6},{5,7},{6,0},{7,1},{8,10},{9,11},{10,... | collective-permute-start | bytes 3342344 | tf_op jit(solution)/shard_map/ppermute | solution.py:31
  117.7 23.0 %collective-permute-start.8 = (bf16[2,128,2048]{2,1,0:T(8,128)(2,1)}, bf16[2,128,2048]{2,1,0:T(8,128)(2,1)S(1)}, u32[]{:S(2)}, u32[]{:S(2)}) collective-permute-start(bf16[2,128,2048]{2,1,0:T(8,128)(2,1)} %after.70), channel_id=1, source_target_pairs={{0,2},{1,3},{2,4},{3,5},{4,6},{5,7},{6,0},{7,1},{8,10},{9,11},{10,... | collective-permute-start | bytes 3145736 | tf_op jit(solution)/shard_map/ppermute | solution.py:31
  117.7 23.0 %collective-permute-start.9 = (bf16[2,128,2048]{2,1,0:T(8,128)(2,1)}, bf16[2,128,2048]{2,1,0:T(8,128)(2,1)S(1)}, u32[]{:S(2)}, u32[]{:S(2)}) collective-permute-start(bf16[2,128,2048]{2,1,0:T(8,128)(2,1)} %after.70), channel_id=1, source_target_pairs={{0,1},{1,0},{2,3},{3,2},{4,5},{5,4},{6,7},{7,6},{8,9},{9,8},{10,11... | collective-permute-start | bytes 3145736 | tf_op jit(solution)/shard_map/ppermute | solution.py:31
  142.8 25.6 %collective-permute-start.10 = (bf16[2,128,2048]{2,1,0:T(8,128)(2,1)}, bf16[2,128,2048]{2,1,0:T(8,128)(2,1)}, u32[]{:S(2)}, u32[]{:S(2)}) collective-permute-start(bf16[2,128,2048]{2,1,0:T(8,128)(2,1)} %after.72), channel_id=1, source_target_pairs={{0,2},{1,3},{2,4},{3,5},{4,6},{5,7},{6,0},{7,1},{8,10},{9,11},{10,... | collective-permute-start | bytes 3145736 | tf_op jit(solution)/shard_map/ppermute | solution.py:31
  143.4 24.9 %collective-permute-start.11 = (bf16[2,128,2048]{2,1,0:T(8,128)(2,1)}, bf16[2,128,2048]{2,1,0:T(8,128)(2,1)}, u32[]{:S(2)}, u32[]{:S(2)}) collective-permute-start(bf16[2,128,2048]{2,1,0:T(8,128)(2,1)} %after.72), channel_id=1, source_target_pairs={{0,1},{1,0},{2,3},{3,2},{4,5},{5,4},{6,7},{7,6},{8,9},{9,8},{10,11... | collective-permute-start | bytes 3145736 | tf_op jit(solution)/shard_map/ppermute | solution.py:31
  206.4 22.9 %collective-permute-start.12 = (bf16[2,128,2048]{2,1,0:T(8,128)(2,1)S(1)}, bf16[2,128,2048]{2,1,0:T(8,128)(2,1)}, u32[]{:S(2)}, u32[]{:S(2)}) collective-permute-start(bf16[2,128,2048]{2,1,0:T(8,128)(2,1)S(1)} %bitcast.204), channel_id=1, source_target_pairs={{0,1},{1,0},{2,3},{3,2},{4,5},{5,4},{6,7},{7,6},{8,9},{9,8},{10,11... | collective-permute-start | bytes 3145736 | tf_op jit(solution)/shard_map/ppermute | solution.py:31
  207.9 24.2 %collective-permute-start.13 = (bf16[2,128,2048]{2,1,0:T(8,128)(2,1)S(1)}, bf16[2,128,2048]{2,1,0:T(8,128)(2,1)}, u32[]{:S(2)}, u32[]{:S(2)}) collective-permute-start(bf16[2,128,2048]{2,1,0:T(8,128)(2,1)S(1)} %bitcast.205), channel_id=1, source_target_pairs={{0,2},{1,3},{2,4},{3,5},{4,6},{5,7},{6,0},{7,1},{8,10},{9,11},{10,... | collective-permute-start | bytes 3145736 | tf_op jit(solution)/shard_map/ppermute | solution.py:31
  232.1 21.6 %collective-permute-start.14 = (bf16[2,128,2048]{2,1,0:T(8,128)(2,1)}, bf16[2,128,2048]{2,1,0:T(8,128)(2,1)}, u32[]{:S(2)}, u32[]{:S(2)}) collective-permute-start(bf16[2,128,2048]{2,1,0:T(8,128)(2,1)} %after.77), channel_id=1, source_target_pairs={{0,1},{1,0},{2,3},{3,2},{4,5},{5,4},{6,7},{7,6},{8,9},{9,8},{10,11... | collective-permute-start | bytes 3145736 | tf_op jit(solution)/shard_map/ppermute | solution.py:31
  233.3 23.4 %collective-permute-start.15 = (bf16[2,128,2048]{2,1,0:T(8,128)(2,1)}, bf16[2,128,2048]{2,1,0:T(8,128)(2,1)}, u32[]{:S(2)}, u32[]{:S(2)}) collective-permute-start(bf16[2,128,2048]{2,1,0:T(8,128)(2,1)} %after.77), channel_id=1, source_target_pairs={{0,2},{1,3},{2,4},{3,5},{4,6},{5,7},{6,0},{7,1},{8,10},{9,11},{10,... | collective-permute-start | bytes 3145736 | tf_op jit(solution)/shard_map/ppermute | solution.py:31
  256.7 20.7 %collective-permute-start.16 = (bf16[2,128,2048]{2,1,0:T(8,128)(2,1)}, bf16[2,128,2048]{2,1,0:T(8,128)(2,1)}, u32[]{:S(2)}, u32[]{:S(2)}) collective-permute-start(bf16[2,128,2048]{2,1,0:T(8,128)(2,1)} %after.79), channel_id=1, source_target_pairs={{0,1},{1,0},{2,3},{3,2},{4,5},{5,4},{6,7},{7,6},{8,9},{9,8},{10,11... | collective-permute-start | bytes 3145736 | tf_op jit(solution)/shard_map/ppermute | solution.py:31
  257.3 22.0 %collective-permute-start.17 = (bf16[2,128,2048]{2,1,0:T(8,128)(2,1)}, bf16[2,128,2048]{2,1,0:T(8,128)(2,1)}, u32[]{:S(2)}, u32[]{:S(2)}) collective-permute-start(bf16[2,128,2048]{2,1,0:T(8,128)(2,1)} %after.79), channel_id=1, source_target_pairs={{0,2},{1,3},{2,4},{3,5},{4,6},{5,7},{6,0},{7,1},{8,10},{9,11},{10,... | collective-permute-start | bytes 3145736 | tf_op jit(solution)/shard_map/ppermute | solution.py:31
  296.7 16.5 %collective-permute-start.20 = (bf16[2,128,2048]{2,1,0:T(8,128)(2,1)}, bf16[2,128,2048]{2,1,0:T(8,128)(2,1)}, u32[]{:S(2)}, u32[]{:S(2)}) collective-permute-start(bf16[2,128,2048]{2,1,0:T(8,128)(2,1)} %after.84), channel_id=1, source_target_pairs={{0,1},{1,0},{2,3},{3,2},{4,5},{5,4},{6,7},{7,6},{8,9},{9,8},{10,11... | collective-permute-start | bytes 3145736 | tf_op jit(solution)/shard_map/ppermute | solution.py:31
  296.7 21.4 %collective-permute-start.21 = (bf16[2,128,2048]{2,1,0:T(8,128)(2,1)}, bf16[2,128,2048]{2,1,0:T(8,128)(2,1)}, u32[]{:S(2)}, u32[]{:S(2)}) collective-permute-start(bf16[2,128,2048]{2,1,0:T(8,128)(2,1)} %after.84), channel_id=1, source_target_pairs={{0,2},{1,3},{2,4},{3,5},{4,6},{5,7},{6,0},{7,1},{8,10},{9,11},{10,... | collective-permute-start | bytes 3145736 | tf_op jit(solution)/shard_map/ppermute | solution.py:31
  321.9 15.1 %collective-permute-start.23 = (bf16[1,128,2048]{2,1,0:T(8,128)(2,1)}, bf16[1,128,2048]{2,1,0:T(8,128)(2,1)}, u32[]{:S(2)}, u32[]{:S(2)}) collective-permute-start(bf16[1,128,2048]{2,1,0:T(8,128)(2,1)} %slice.115), channel_id=1, source_target_pairs={{0,1},{1,0},{2,3},{3,2},{4,5},{5,4},{6,7},{7,6},{8,9},{9,8},{10,11... | collective-permute-start | bytes 1572872 | tf_op jit(solution)/shard_map/ppermute | solution.py:31
  337.0 43.9 %collective-permute-start.24 = (bf16[2048,256]{1,0:T(8,128)(2,1)}, bf16[2048,256]{1,0:T(8,128)(2,1)}, u32[]{:S(2)}, u32[]{:S(2)}) collective-permute-start(bf16[2048,256]{1,0:T(8,128)(2,1)} %after.89.refs_6_), channel_id=1, source_target_pairs={{0,1},{1,0},{2,3},{3,2},{4,5},{5,4},{6,7},{7,6},{8,9},{9,8},{10,11... | collective-permute-start | bytes 3145736 | tf_op jit(solution)/shard_map/ppermute | solution.py:31
  339.2 41.8 %collective-permute-start.25 = (bf16[2048,256]{1,0:T(8,128)(2,1)}, bf16[2048,256]{1,0:T(8,128)(2,1)}, u32[]{:S(2)}, u32[]{:S(2)}) collective-permute-start(bf16[2048,256]{1,0:T(8,128)(2,1)} %after.89.refs_6_), channel_id=1, source_target_pairs={{0,2},{1,3},{2,4},{3,5},{4,6},{5,7},{6,0},{7,1},{8,10},{9,11},{10,... | collective-permute-start | bytes 3145736 | tf_op jit(solution)/shard_map/ppermute | solution.py:31
  381.0 20.9 %collective-permute-start.26 = (bf16[2048,256]{1,0:T(8,128)(2,1)}, bf16[2048,256]{1,0:T(8,128)(2,1)}, u32[]{:S(2)}, u32[]{:S(2)}) collective-permute-start(bf16[2048,256]{1,0:T(8,128)(2,1)} %after.91.refs_13_.refs_8_), channel_id=1, source_target_pairs={{0,1},{1,0},{2,3},{3,2},{4,5},{5,4},{6,7},{7,6},{8,9},{9,8},{10,11... | collective-permute-start | bytes 3145736 | tf_op jit(solution)/shard_map/ppermute | solution.py:31
  381.2 22.5 %collective-permute-start.27 = (bf16[2048,256]{1,0:T(8,128)(2,1)}, bf16[2048,256]{1,0:T(8,128)(2,1)}, u32[]{:S(2)}, u32[]{:S(2)}) collective-permute-start(bf16[2048,256]{1,0:T(8,128)(2,1)} %after.91.refs_13_.refs_8_), channel_id=1, source_target_pairs={{0,2},{1,3},{2,4},{3,5},{4,6},{5,7},{6,0},{7,1},{8,10},{9,11},{10,... | collective-permute-start | bytes 3145736 | tf_op jit(solution)/shard_map/ppermute | solution.py:31
  403.7 23.9 %collective-permute-start.29 = (bf16[2048,256]{1,0:T(8,128)(2,1)}, bf16[2048,256]{1,0:T(8,128)(2,1)}, u32[]{:S(2)}, u32[]{:S(2)}) collective-permute-start(bf16[2048,256]{1,0:T(8,128)(2,1)} %after.93.refs_15_.refs_10_), channel_id=1, source_target_pairs={{0,1},{1,0},{2,3},{3,2},{4,5},{5,4},{6,7},{7,6},{8,9},{9,8},{10,11... | collective-permute-start | bytes 3145736 | tf_op jit(solution)/shard_map/ppermute | solution.py:31
  405.9 22.7 %collective-permute-start.28 = (bf16[2048,256]{1,0:T(8,128)(2,1)}, bf16[2048,256]{1,0:T(8,128)(2,1)}, u32[]{:S(2)}, u32[]{:S(2)}) collective-permute-start(bf16[2048,256]{1,0:T(8,128)(2,1)} %after.93.refs_15_.refs_10_), channel_id=1, source_target_pairs={{0,2},{1,3},{2,4},{3,5},{4,6},{5,7},{6,0},{7,1},{8,10},{9,11},{10,... | collective-permute-start | bytes 3145736 | tf_op jit(solution)/shard_map/ppermute | solution.py:31
  430.4 34.7 %collective-permute-start.31 = (bf16[1024,256]{1,0:T(8,128)(2,1)}, bf16[1024,256]{1,0:T(8,128)(2,1)}, u32[]{:S(2)}, u32[]{:S(2)}) collective-permute-start(bf16[1024,256]{1,0:T(8,128)(2,1)} %slice.117), channel_id=1, source_target_pairs={{0,2},{1,3},{2,4},{3,5},{4,6},{5,7},{6,0},{7,1},{8,10},{9,11},{10,... | collective-permute-start | bytes 1572872 | tf_op jit(solution)/shard_map/ppermute | solution.py:31
  432.8 32.3 %collective-permute-start.30 = (bf16[1024,256]{1,0:T(8,128)(2,1)}, bf16[1024,256]{1,0:T(8,128)(2,1)}, u32[]{:S(2)}, u32[]{:S(2)}) collective-permute-start(bf16[1024,256]{1,0:T(8,128)(2,1)} %slice.116), channel_id=1, source_target_pairs={{0,1},{1,0},{2,3},{3,2},{4,5},{5,4},{6,7},{7,6},{8,9},{9,8},{10,11... | collective-permute-start | bytes 1572872 | tf_op jit(solution)/shard_map/ppermute | solution.py:31
  510.7 335.9 %reduce-scatter.7.cloned.1.call-start = ((), (), s32[]{:S(2)}) async-start(), calls=%async_computation.14 | async-start | bytes 10485760 | tf_op jit(solution)/shard_map/reduce_scatter | solution.py:807
  511.0 30.5 %collective-permute-start.32 = (bf16[2,128,2048]{2,1,0:T(8,128)(2,1)}, bf16[2,128,2048]{2,1,0:T(8,128)(2,1)}, u32[]{:S(2)}, u32[]{:S(2)}) collective-permute-start(bf16[2,128,2048]{2,1,0:T(8,128)(2,1)} %bitcast.266), channel_id=1, source_target_pairs={{0,1},{1,0},{2,3},{3,2},{4,5},{5,4},{6,7},{7,6},{8,9},{9,8},{10,11... | collective-permute-start | bytes 3145736 | tf_op jit(solution)/shard_map/ppermute | solution.py:31
  554.4 367.2 %reduce-scatter.9.cloned.1.call-start = ((), (), s32[]{:S(2)}) async-start(), calls=%async_computation.15 | async-start | bytes 20971520 | tf_op jit(solution)/shard_map/reduce_scatter | solution.py:807
  554.5 24.0 %collective-permute-start.35 = (bf16[2,128,2048]{2,1,0:T(8,128)(2,1)}, bf16[2,128,2048]{2,1,0:T(8,128)(2,1)}, u32[]{:S(2)}, u32[]{:S(2)}) collective-permute-start(bf16[2,128,2048]{2,1,0:T(8,128)(2,1)} %bitcast.265), channel_id=1, source_target_pairs={{0,1},{1,0},{2,3},{3,2},{4,5},{5,4},{6,7},{7,6},{8,9},{9,8},{10,11... | collective-permute-start | bytes 3145736 | tf_op jit(solution)/shard_map/ppermute | solution.py:31
  556.7 22.2 %collective-permute-start.36 = (bf16[2,128,2048]{2,1,0:T(8,128)(2,1)S(1)}, bf16[2,128,2048]{2,1,0:T(8,128)(2,1)}, u32[]{:S(2)}, u32[]{:S(2)}) collective-permute-start(bf16[2,128,2048]{2,1,0:T(8,128)(2,1)S(1)} %fusion.16), channel_id=1, source_target_pairs={{0,2},{1,3},{2,4},{3,5},{4,6},{5,7},{6,0},{7,1},{8,10},{9,11},{10,... | collective-permute-start | bytes 3145736 | tf_op jit(solution)/shard_map/ppermute | solution.py:31
  578.8 24.2 %collective-permute-start.34 = (bf16[2,128,2048]{2,1,0:T(8,128)(2,1)}, bf16[2,128,2048]{2,1,0:T(8,128)(2,1)}, u32[]{:S(2)}, u32[]{:S(2)}) collective-permute-start(bf16[2,128,2048]{2,1,0:T(8,128)(2,1)} %bitcast.264), channel_id=1, source_target_pairs={{0,1},{1,0},{2,3},{3,2},{4,5},{5,4},{6,7},{7,6},{8,9},{9,8},{10,11... | collective-permute-start | bytes 3145736 | tf_op jit(solution)/shard_map/ppermute | solution.py:31
  582.5 21.7 %collective-permute-start.37 = (bf16[2,128,2048]{2,1,0:T(8,128)(2,1)S(1)}, bf16[2,128,2048]{2,1,0:T(8,128)(2,1)}, u32[]{:S(2)}, u32[]{:S(2)}) collective-permute-start(bf16[2,128,2048]{2,1,0:T(8,128)(2,1)S(1)} %add_convert_fusion.8), channel_id=1, source_target_pairs={{0,2},{1,3},{2,4},{3,5},{4,6},{5,7},{6,0},{7,1},{8,10},{9,11},{10,... | collective-permute-start | bytes 3145736 | tf_op jit(solution)/shard_map/ppermute | solution.py:31
  604.2 29.4 %collective-permute-start.33 = (bf16[2,128,2048]{2,1,0:T(8,128)(2,1)}, bf16[2,128,2048]{2,1,0:T(8,128)(2,1)}, u32[]{:S(2)}, u32[]{:S(2)}) collective-permute-start(bf16[2,128,2048]{2,1,0:T(8,128)(2,1)} %bitcast.263), channel_id=1, source_target_pairs={{0,1},{1,0},{2,3},{3,2},{4,5},{5,4},{6,7},{7,6},{8,9},{9,8},{10,11... | collective-permute-start | bytes 3145736 | tf_op jit(solution)/shard_map/ppermute | solution.py:31
  607.5 26.1 %collective-permute-start.38 = (bf16[2,128,2048]{2,1,0:T(8,128)(2,1)S(1)}, bf16[2,128,2048]{2,1,0:T(8,128)(2,1)}, u32[]{:S(2)}, u32[]{:S(2)}) collective-permute-start(bf16[2,128,2048]{2,1,0:T(8,128)(2,1)S(1)} %add_convert_fusion.7), channel_id=1, source_target_pairs={{0,2},{1,3},{2,4},{3,5},{4,6},{5,7},{6,0},{7,1},{8,10},{9,11},{10,... | collective-permute-start | bytes 3145736 | tf_op jit(solution)/shard_map/ppermute | solution.py:31
  646.8 29.6 %all-to-all-start.1 = ((bf16[8,2,128,256]{3,2,1,0:T(8,128)(2,1)}), bf16[8,2,128,256]{3,2,1,0:T(8,128)(2,1)}, u32[]{:S(2)}, u32[]{:S(2)}) async-start(bf16[8,2,128,256]{3,2,1,0:T(8,128)(2,1)} %bitcast.218), calls=%async_computation.1 | async-start | bytes 2097152 | tf_op jit(solution)/shard_map/all_to_all | solution.py:822
  651.0 309.5 %reduce-scatter.11.cloned.1.call-start = ((), (), s32[]{:S(2)}) async-start(), calls=%async_computation.16 | async-start | bytes 20971520 | tf_op jit(solution)/shard_map/reduce_scatter | solution.py:807
  679.4 66.0 %all-to-all-start.2 = ((bf16[8,2,128,256]{3,2,1,0:T(8,128)(2,1)}), bf16[8,2,128,256]{3,2,1,0:T(8,128)(2,1)}, u32[]{:S(2)}, u32[]{:S(2)}) async-start(bf16[8,2,128,256]{3,2,1,0:T(8,128)(2,1)} %bitcast.217), calls=%async_computation.2 | async-start | bytes 2097152 | tf_op jit(solution)/shard_map/all_to_all | solution.py:822
  685.9 59.5 %collective-permute-start.39 = (bf16[2,128,2048]{2,1,0:T(8,128)(2,1)}, bf16[2,128,2048]{2,1,0:T(8,128)(2,1)}, u32[]{:S(2)}, u32[]{:S(2)}) collective-permute-start(bf16[2,128,2048]{2,1,0:T(8,128)(2,1)} %after.107), channel_id=1, source_target_pairs={{0,1},{1,0},{2,3},{3,2},{4,5},{5,4},{6,7},{7,6},{8,9},{9,8},{10,11... | collective-permute-start | bytes 3145736 | tf_op jit(solution)/shard_map/ppermute | solution.py:31
  692.3 83.5 %collective-permute-start.42 = (bf16[2,128,2048]{2,1,0:T(8,128)(2,1)}, bf16[2,128,2048]{2,1,0:T(8,128)(2,1)}, u32[]{:S(2)}, u32[]{:S(2)}) collective-permute-start(bf16[2,128,2048]{2,1,0:T(8,128)(2,1)} %bitcast.262), channel_id=1, source_target_pairs={{0,1},{1,0},{2,3},{3,2},{4,5},{5,4},{6,7},{7,6},{8,9},{9,8},{10,11... | collective-permute-start | bytes 3145736 | tf_op jit(solution)/shard_map/ppermute | solution.py:31
  745.4 30.4 %collective-permute-start.40 = (bf16[2,128,2048]{2,1,0:T(8,128)(2,1)}, bf16[2,128,2048]{2,1,0:T(8,128)(2,1)S(1)}, u32[]{:S(2)}, u32[]{:S(2)}) collective-permute-start(bf16[2,128,2048]{2,1,0:T(8,128)(2,1)} %after.110), channel_id=1, source_target_pairs={{0,1},{1,0},{2,3},{3,2},{4,5},{5,4},{6,7},{7,6},{8,9},{9,8},{10,11... | collective-permute-start | bytes 3145736 | tf_op jit(solution)/shard_map/ppermute | solution.py:31
  749.4 26.5 %collective-permute-start.41 = (bf16[2,128,2048]{2,1,0:T(8,128)(2,1)}, bf16[2,128,2048]{2,1,0:T(8,128)(2,1)S(1)}, u32[]{:S(2)}, u32[]{:S(2)}) collective-permute-start(bf16[2,128,2048]{2,1,0:T(8,128)(2,1)} %fusion.12), channel_id=1, source_target_pairs={{0,2},{1,3},{2,4},{3,5},{4,6},{5,7},{6,0},{7,1},{8,10},{9,11},{10,... | collective-permute-start | bytes 3145736 | tf_op jit(solution)/shard_map/ppermute | solution.py:31
  752.9 22.9 %collective-permute-start.44 = (f32[2,128]{1,0:T(2,128)S(1)}, f32[2,128]{1,0:T(2,128)S(1)}, u32[]{:S(2)}, u32[]{:S(2)}) collective-permute-start(f32[2,128]{1,0:T(2,128)S(1)} %add.360), channel_id=1, source_target_pairs={{0,16},{8,24},{16,0},{24,8},{1,17},{9,25},{17,1},{25,9},{2,18},{10... | collective-permute-start | bytes 3080 | tf_op jit(solution)/shard_map/ppermute | solution.py:859
  777.2 39.6 %collective-permute-start.50 = (bf16[2,128,2048]{2,1,0:T(8,128)(2,1)}, bf16[2,128,2048]{2,1,0:T(8,128)(2,1)S(1)}, u32[]{:S(2)}, u32[]{:S(2)}) collective-permute-start(bf16[2,128,2048]{2,1,0:T(8,128)(2,1)} %bitcast.72), channel_id=1, source_target_pairs={{0,1},{1,0},{2,3},{3,2},{4,5},{5,4},{6,7},{7,6},{8,9},{9,8},{10,11... | collective-permute-start | bytes 3145736 | tf_op jit(solution)/shard_map/ppermute | solution.py:31
  778.3 47.2 %collective-permute-start.51 = (bf16[2,128,2048]{2,1,0:T(8,128)(2,1)}, bf16[2,128,2048]{2,1,0:T(8,128)(2,1)S(1)}, u32[]{:S(2)}, u32[]{:S(2)}) collective-permute-start(bf16[2,128,2048]{2,1,0:T(8,128)(2,1)} %bitcast.73), channel_id=1, source_target_pairs={{0,1},{1,0},{2,3},{3,2},{4,5},{5,4},{6,7},{7,6},{8,9},{9,8},{10,11... | collective-permute-start | bytes 3145736 | tf_op jit(solution)/shard_map/ppermute | solution.py:31
  783.3 28.4 %collective-permute-start.47 = (bf16[512,1152]{1,0:T(8,128)(2,1)}, bf16[512,1152]{1,0:T(8,128)(2,1)}, u32[]{:S(2)}, u32[]{:S(2)}) collective-permute-start(bf16[512,1152]{1,0:T(8,128)(2,1)} %add_convert_fusion.2), channel_id=1, source_target_pairs={{0,16},{8,24},{16,0},{24,8},{1,17},{9,25},{17,1},{25,9},{2,18},{10... | collective-permute-start | bytes 3538952 | tf_op jit(solution)/shard_map/ppermute | solution.py:31
  785.9 39.5 %collective-permute-start.49 = (bf16[2,128,2048]{2,1,0:T(8,128)(2,1)}, bf16[2,128,2048]{2,1,0:T(8,128)(2,1)}, u32[]{:S(2)}, u32[]{:S(2)}) collective-permute-start(bf16[2,128,2048]{2,1,0:T(8,128)(2,1)} %fusion.10), channel_id=1, source_target_pairs={{0,2},{1,3},{2,4},{3,5},{4,6},{5,7},{6,0},{7,1},{8,10},{9,11},{10,... | collective-permute-start | bytes 3145736 | tf_op jit(solution)/shard_map/ppermute | solution.py:31
  790.2 45.3 %collective-permute-start.48 = (bf16[2,128,2048]{2,1,0:T(8,128)(2,1)}, bf16[2,128,2048]{2,1,0:T(8,128)(2,1)}, u32[]{:S(2)}, u32[]{:S(2)}) collective-permute-start(bf16[2,128,2048]{2,1,0:T(8,128)(2,1)} %add_convert_fusion.6), channel_id=1, source_target_pairs={{0,2},{1,3},{2,4},{3,5},{4,6},{5,7},{6,0},{7,1},{8,10},{9,11},{10,... | collective-permute-start | bytes 3145736 | tf_op jit(solution)/shard_map/ppermute | solution.py:31
  835.5 54.5 %all-to-all-start.3 = ((bf16[8,64,1152]{2,1,0:T(8,128)(2,1)}), bf16[8,64,1152]{2,1,0:T(8,128)(2,1)S(1)}, u32[]{:S(2)}, u32[]{:S(2)}) async-start(bf16[8,64,1152]{2,1,0:T(8,128)(2,1)} %bitcast.200), calls=%async_computation.3 | async-start | bytes 2359296 | tf_op jit(solution)/shard_map/all_to_all | solution.py:885
  839.5 36.8 %collective-permute-start.53 = (bf16[2,128,2048]{2,1,0:T(8,128)(2,1)}, bf16[2,128,2048]{2,1,0:T(8,128)(2,1)S(1)}, u32[]{:S(2)}, u32[]{:S(2)}) collective-permute-start(bf16[2,128,2048]{2,1,0:T(8,128)(2,1)} %bitcast.261), channel_id=1, source_target_pairs={{0,1},{1,0},{2,3},{3,2},{4,5},{5,4},{6,7},{7,6},{8,9},{9,8},{10,11... | collective-permute-start | bytes 3145736 | tf_op jit(solution)/shard_map/ppermute | solution.py:31
  844.5 40.1 %collective-permute-start.52 = (bf16[2,128,2048]{2,1,0:T(8,128)(2,1)}, bf16[2,128,2048]{2,1,0:T(8,128)(2,1)}, u32[]{:S(2)}, u32[]{:S(2)}) collective-permute-start(bf16[2,128,2048]{2,1,0:T(8,128)(2,1)} %add_convert_fusion.5), channel_id=1, source_target_pairs={{0,2},{1,3},{2,4},{3,5},{4,6},{5,7},{6,0},{7,1},{8,10},{9,11},{10,... | collective-permute-start | bytes 3145736 | tf_op jit(solution)/shard_map/ppermute | solution.py:31
  846.0 30.2 %collective-permute-start.54 = (f32[2,128]{1,0:T(2,128)S(1)}, f32[2,128]{1,0:T(2,128)S(1)}, u32[]{:S(2)}, u32[]{:S(2)}) collective-permute-start(f32[2,128]{1,0:T(2,128)S(1)} %add.369), channel_id=1, source_target_pairs={{0,1},{1,0},{2,3},{3,2},{4,5},{5,4},{6,7},{7,6},{8,9},{9,8},{10,11... | collective-permute-start | bytes 3080 | tf_op jit(solution)/shard_map/ppermute | solution.py:859
  894.1 34.2 %collective-permute-start.59 = (bf16[2,128,2048]{2,1,0:T(8,128)(2,1)}, bf16[2,128,2048]{2,1,0:T(8,128)(2,1)S(1)}, u32[]{:S(2)}, u32[]{:S(2)}) collective-permute-start(bf16[2,128,2048]{2,1,0:T(8,128)(2,1)} %add_convert_fusion.3), channel_id=1, source_target_pairs={{0,2},{1,3},{2,4},{3,5},{4,6},{5,7},{6,0},{7,1},{8,10},{9,11},{10,... | collective-permute-start | bytes 3145736 | tf_op jit(solution)/shard_map/ppermute | solution.py:31
  898.5 43.2 %collective-permute-start.56 = (bf16[2,128,2048]{2,1,0:T(8,128)(2,1)}, bf16[2,128,2048]{2,1,0:T(8,128)(2,1)}, u32[]{:S(2)}, u32[]{:S(2)}) collective-permute-start(bf16[2,128,2048]{2,1,0:T(8,128)(2,1)} %add_convert_fusion.4), channel_id=1, source_target_pairs={{0,2},{1,3},{2,4},{3,5},{4,6},{5,7},{6,0},{7,1},{8,10},{9,11},{10,... | collective-permute-start | bytes 3145736 | tf_op jit(solution)/shard_map/ppermute | solution.py:31
  898.5 43.2 %collective-permute-start.57 = (bf16[2,128,2048]{2,1,0:T(8,128)(2,1)}, bf16[2,128,2048]{2,1,0:T(8,128)(2,1)}, u32[]{:S(2)}, u32[]{:S(2)}) collective-permute-start(bf16[2,128,2048]{2,1,0:T(8,128)(2,1)} %after.133), channel_id=1, source_target_pairs={{0,1},{1,0},{2,3},{3,2},{4,5},{5,4},{6,7},{7,6},{8,9},{9,8},{10,11... | collective-permute-start | bytes 3145736 | tf_op jit(solution)/shard_map/ppermute | solution.py:31
  899.8 45.1 %collective-permute-start.55 = (bf16[2,128,2048]{2,1,0:T(8,128)(2,1)}, bf16[2,128,2048]{2,1,0:T(8,128)(2,1)S(1)}, u32[]{:S(2)}, u32[]{:S(2)}) collective-permute-start(bf16[2,128,2048]{2,1,0:T(8,128)(2,1)} %after.131), channel_id=1, source_target_pairs={{0,1},{1,0},{2,3},{3,2},{4,5},{5,4},{6,7},{7,6},{8,9},{9,8},{10,11... | collective-permute-start | bytes 3145736 | tf_op jit(solution)/shard_map/ppermute | solution.py:31
  905.0 32.8 %collective-permute-start.58 = (f32[2,128]{1,0:T(2,128)S(1)}, f32[2,128]{1,0:T(2,128)S(1)}, u32[]{:S(2)}, u32[]{:S(2)}) collective-permute-start(f32[2,128]{1,0:T(2,128)S(1)} %add.372), channel_id=1, source_target_pairs={{0,2},{1,3},{2,0},{3,1},{4,6},{5,7},{6,4},{7,5},{8,10},{9,11},{10,... | collective-permute-start | bytes 3080 | tf_op jit(solution)/shard_map/ppermute | solution.py:859
  (84 other events, 679.5 us)
Sparse Core Ops, SparseCore 0:
  12.1 34.1 all-gather.5
  47.9 58.2 all-gather.7
  107.8 105.9 all-gather.11
  215.2 105.9 all-gather.9
  322.5 105.9 all-gather.13
  510.8 72.3 reduce-scatter.4
  586.6 71.7 reduce-scatter.6
  660.9 126.1 reduce-scatter.8
  789.9 126.9 reduce-scatter.10

commit v9 on v8

--- a/solution.py
+++ b/solution.py
@@ -105,7 +105,7 @@
     return one.astype(f32) + other.astype(f32)
 
 
-def ring_scatter(parts, axis, work=(), then={}):
+def ring_scatter(parts, axis, work=(), then={}, beside={}):
     outer, _ = sizes(axis)
     total, arrived = None, []
     for step in range(outer):
@@ -113,6 +113,7 @@
         moved = [row_move(parts, a, axis)]
         if step:
             moved.append(ahead(total, axis))
+        moved += beside.get(step, [])
         moved = together([f(arrived) for f in work[step : step + 1] if f], *moved)
         if step in then:
             then[step](moved)
@@ -777,36 +778,39 @@
     hidden, grad_gate_act, grad_up_act = done["acts"]
     first = combined((grad_gate_act, grad_up_act), (w_gate, w_up), 0, False, (o_all[-1],))
     whole_down = [bank_grad(grad_rows, hidden, (first[0],), 0, pair)]
-    second = combined(
-        (grad_gate_act, grad_up_act), (w_gate, w_up), 1, False, (whole_down[0],)
-    )
-
-    def mixed_work(h):
-        def work(ties):
-            if h == 0:
-                whole_down.append(bank_grad(grad_rows, hidden, ties, pair, local_experts - pair))
-                ties = (whole_down[1],)
-            mixed = combined((hidden,), (w_down,), h, True, ties)
-            done.setdefault("mixed", []).extend(mixed)
-            return mixed[0]
-
-        return work
+    mixed = combined((hidden,), (w_down,), 0, True, (whole_down[0],))
+    second = combined((grad_gate_act, grad_up_act), (w_gate, w_up), 1, False, (mixed[0],))
+
+    def down_work(ties):
+        whole_down.append(bank_grad(grad_rows, hidden, ties, pair, local_experts - pair))
+        return whole_down[1]
+
+    def mixed_work(ties):
+        found = combined((hidden,), (w_down,), 1, True, ties)
+        return keep(tail=found[0], mixed=found)
 
     def gate_work(ties):
         return keep(whole_gate=bank_grad(taken, grad_gate_act, ties))
 
     parts = [v.reshape(micro, rows, D) for v in list(first) + list(second)]
+    mixed = [v.reshape(micro, rows, D) for v in mixed]
     grad_h_two = ring_scatter(
         parts,
         "seq",
-        (lambda _: second[0], mixed_work(0), mixed_work(1), gate_work),
-        {3: lambda moved: keep(sum_gate=after(done["whole_gate"], *moved))},
+        (lambda _: second[0], down_work, mixed_work, gate_work),
+        {
+            0: lambda moved: keep(mixed_one=moved[-1]),
+            1: lambda moved: keep(sum_down=after(whole_down[1], *moved)),
+            3: lambda moved: keep(sum_gate=after(done["whole_gate"], *moved)),
+        },
+        {0: [row_move(mixed, 1, "seq")]},
     ).reshape(tokens, D)
+    mixed += [v.reshape(micro, rows, D) for v in done["mixed"]]
 
     def bank_sum(whole):
         return lax.psum_scatter(whole, "fsdp", scatter_dimension=1, tiled=True).astype(f32)
 
-    grad_down = jnp.concatenate([bank_sum(v) for v in whole_down], axis=0)
+    grad_down = jnp.concatenate([bank_sum(whole_down[0]), bank_sum(done["sum_down"])], axis=0)
     grad_gate = bank_sum(done["sum_gate"])
 
     grad_gain_two = jnp.sum(grad_h_two * normed_two, axis=0)
@@ -828,18 +832,22 @@
     grad_up = bank_sum(after(whole_up, do_blocks))
     do_heads = reorder(do_blocks, seq_order)
 
-    mixed = [v.reshape(micro, rows, D) for v in done["mixed"]]
-    k = sizes("seq")[1] + 1 % sizes("seq")[1]
-    mixed[k] = after(mixed[k], do_blocks)
+    inner = sizes("seq")[1]
+    one = 1 % inner
+    total = row_sum(after(done["mixed_one"], do_blocks), mixed, 1, "seq")
+    mixed[2 * inner + one] = after(mixed[2 * inner + one], do_blocks)
     grad_qkv, grad_head = attend_back(qkv, do_heads, tables)
     part_h_one, grad_gain_one = part_grads(grad_qkv, w_first, x_all, inv_all)
-    one, columns = together(
-        (grad_gain_one,), row_move(mixed, 1, "seq"), to_heads(after(grad_attn, do_blocks))
-    )
-
-    total = one
+    total, two, columns = together(
+        (grad_gain_one,),
+        ahead(total, "seq"),
+        row_move(mixed, 2, "seq"),
+        to_heads(after(grad_attn, do_blocks)),
+    )
+
     part_h_one = [v.reshape(micro, rows, D) for v in part_h_one]
-    part_h_one[k] = after(part_h_one[k], total)
+    part_h_one[inner + one] = after(part_h_one[inner + one], total)
+    mixed[3 * inner + one] = after(mixed[3 * inner + one], total)
     gains = jnp.pad(jnp.stack([grad_gain_one, grad_gain_two], axis=1), ((0, 0), (0, HD - 2)))
     whole = proj_grads(
         h_one,
@@ -858,36 +866,39 @@
         axis, pairs = left.pop(0)
         return lax.ppermute(head, axis, pairs)
 
-    total = ahead(row_sum(total, mixed, 1, "seq"), "seq")
+    total = ahead(add(row_sum(two, mixed, 2, "seq"), total).astype(bf16), "seq")
     head = head + exchange(head)
-    total, two, one, moved = together(
+    total, three, grad_one, moved = together(
         (whole[0],),
         total,
-        row_move(mixed, 2, "seq"),
+        row_move(mixed, 3, "seq"),
         row_move(part_h_one, 1, "seq"),
         exchange(head),
     )
     head = head + moved
 
-    whole = [after(v, one) for v in whole]
+    whole = [after(v, grad_one) for v in whole]
     owned = ring_scatter(whole, "fsdp").astype(bf16)
 
-    total = ahead(add(row_sum(two, mixed, 2, "seq"), total).astype(bf16), "seq")
-    grad_total = ahead(row_sum(one, part_h_one, 1, "seq"), "seq")
-    total, grad_total, three, two, owned = together(
+    mixed[one] = after(mixed[one], grad_one)
+    part_h_one[2 * inner + one] = after(part_h_one[2 * inner + one], grad_one)
+    total = ahead(add(row_sum(three, mixed, 3, "seq"), total).astype(bf16), "seq")
+    grad_total = ahead(row_sum(grad_one, part_h_one, 1, "seq"), "seq")
+    total, grad_total, grad_two, zero, owned = together(
         (),
         total,
         grad_total,
-        row_move(mixed, 3, "seq"),
         row_move(part_h_one, 2, "seq"),
+        row_move(mixed, 0, "seq"),
         owned,
     )
     owned = lax.all_to_all(
         owned.reshape(ns, share, -1), "seq", split_axis=0, concat_axis=0, tiled=True
     )
 
-    grad_total = add(row_sum(two, part_h_one, 2, "seq"), grad_total).astype(bf16)
-    grad_total, zero, moved, owned = together(
+    part_h_one[3 * inner + one] = after(part_h_one[3 * inner + one], grad_total)
+    grad_total = add(row_sum(grad_two, part_h_one, 2, "seq"), grad_total).astype(bf16)
+    grad_total, grad_three, moved, owned = together(
         (grad_down,),
         ahead(grad_total, "seq"),
         row_move(part_h_one, 3, "seq"),
@@ -895,22 +906,18 @@
         owned,
     )
     head = head + moved
-
-    k = 1 % sizes("seq")[1]
-    mixed[k], part_h_one[k] = after(mixed[k], owned), after(part_h_one[k], owned)
-    total = ahead(add(row_sum(three, mixed, 3, "seq"), total).astype(bf16), "seq")
-    grad_total = add(row_sum(zero, part_h_one, 3, "seq"), grad_total).astype(bf16)
-    grad_total, zero, moved, last, total = together(
+    mixed = add(row_sum(zero, mixed, 0, "seq"), total).reshape(tokens, D)
+    layer_output = (middle + mixed).astype(bf16).reshape(micro, rows, D)
+
+    part_h_one[one] = after(part_h_one[one], owned)
+    grad_total = add(row_sum(grad_three, part_h_one, 3, "seq"), grad_total).astype(bf16)
+    grad_total, zero, moved = together(
         (grad_gate,),
         ahead(grad_total, "seq"),
         row_move(part_h_one, 0, "seq"),
         exchange(head),
-        row_move(mixed, 0, "seq"),
-        total,
     )
     head = head + moved
-    mixed = add(row_sum(last, mixed, 0, "seq"), total).reshape(tokens, D)
-    layer_output = (middle + mixed).astype(bf16).reshape(micro, rows, D)
     while left:
         head = head + exchange(head)
     grad_head_gains = head

time: 985 us -> 992 us (level)
    ppermute x56, waiting for transfers between devices: 269 us -> 254 us  [shift(): return lax.ppermute(value, axis, pairs)]
    ppermute x5, waiting for transfers between devices: 10.1 us -> 24.8 us  [exchange(): return lax.ppermute(head, axis, pairs)]
    unnamed x166 -> x172, local copies, waits for them, and re-layouts: 43.3 us -> 42.1 us
  transfers between devices with their start and end apart: 73 -> 73, of which waited for: 35 -> 33; matrix products, arithmetic and copies ran while one was open for 17% -> 18% of each run, Pallas kernels for 33% -> 33%
where the time goes in v9:
time: 992 us; the launch traced here: 982 us
  Pallas kernels  363 us (37%)
  waiting for transfers between devices  286 us (29%)
  local copies, waits for them, and re-layouts  100 us (10%)
  other arithmetic  93.3 us (9%)
  starting transfers between devices  74.5 us (8%)
  blocking collectives  28.1 us (3%)
  matrix products  20.8 us (2%)
  between operations  15.5 us (2%)
    pallas_call x13, Pallas kernels, call(): pl.pallas_call(run, grid=grid, in_specs=[spec for _, spec in ins] + [pl.B...  293 us
    ppermute x56, waiting for transfers between devices, shift(): return lax.ppermute(value, axis, pairs)  254 us
    ppermute x56, starting transfers between devices, shift(): return lax.ppermute(value, axis, pairs)  51.9 us
    unnamed x172, local copies, waits for them, and re-layouts  42.1 us
    pallas_call x1, Pallas kernels, attend_back(): pl.pallas_call(lambda *refs: attend_back_kernel(tile, *refs[:7], *refs[-2...  33.1 us
    all_to_all x1, blocking collectives, body(): lax.all_to_all(o_heads, 'seq', split_axis=0, concat_axis=0, tiled=True)  28.1 us
    ppermute x5, waiting for transfers between devices, exchange(): return lax.ppermute(head, axis, pairs)  24.8 us
    pallas_call x1, Pallas kernels, proj_grads(): pl.pallas_call(run, grid_spec=pltpu.PrefetchScalarGridSpec(num_scalar_pre...  20.5 us
  transfers between devices with their start and end apart: 73, of which 33 were waited for; matrix products, arithmetic and copies ran while one was open for 18% of the time, Pallas kernels for 33%

profile of v9, /device:TPU:0, one launch (start us, length us, event | category | flops | bytes accessed | tf_op | source)
XLA Modules:
  0.0 981.7 jit_solution(10103481446117388850)
XLA Ops:
  17.6 3.0 collective-permute-start.1
  22.1 25.0 %collective-permute-done.1 = bf16[2,128,2176]{2,1,0:T(8,128)(2,1)S(1)} collective-permute-done((bf16[2,128,2176]{2,1,0:T(8,128)(2,1)S(1)}, bf16[2,128,2176]{2,1,0:T(8,128)(2,1)S(1)}, u32[]{:S(2)}, u32[]{:S(2)}) %collective-permute-start.1) | collective-permute-done | bytes 1114144 | tf_op jit(solution)/shard_map/ppermute | solution.py:31
  53.4 3.1 fusion.27
  58.9 15.9 %collective-permute-done.3 = bf16[2,128,2176]{2,1,0:T(8,128)(2,1)} collective-permute-done((bf16[2,128,2176]{2,1,0:T(8,128)(2,1)S(1)}, bf16[2,128,2176]{2,1,0:T(8,128)(2,1)}, u32[]{:S(2)}, u32[]{:S(2)}) %collective-permute-start.3) | collective-permute-done | bytes 1114144 | tf_op jit(solution)/shard_map/ppermute | solution.py:31
  82.6 19.8 %collective-permute-done.5 = bf16[2,128,2176]{2,1,0:T(8,128)(2,1)S(1)} collective-permute-done((bf16[2,128,2176]{2,1,0:T(8,128)(2,1)}, bf16[2,128,2176]{2,1,0:T(8,128)(2,1)S(1)}, u32[]{:S(2)}, u32[]{:S(2)}) %collective-permute-start.5) | collective-permute-done | bytes 1114144 | tf_op jit(solution)/shard_map/ppermute | solution.py:31
  105.9 8.1 collective-permute-done.6
  118.5 6.5 fusion
  126.9 5.3 fusion.2
  132.2 8.0 fusion.4.refs_0_.refs_1_
  148.0 16.5 %attend.1 = bf16[8,2,128,256]{3,2,1,0:T(8,128)(2,1)S(1)} custom-call(bf16[8,2,128,768]{3,2,1,0:T(8,128)(2,1)S(1)} %copy-done.2, f32[1024,128]{1,0:T(8,128)S(1)} %copy-done.8, f32[1024,128]{1,0:T(8,128)S(1)} %copy-done.6, s32[2,1,1024]{2,1,0:T(1,128)S(1)} %bitcast.193, s32[2,1024,1]{2,1,0:T(8,128)S(1)} %copy-done.3, f32[2,128]{1,0:T(2,128)S(1)} %copy-done.14), custom_call_target="tpu_custom_call" | custom-call | flops 1 | bytes 1 | tf_op jit(solution)/shard_map/attend/pallas_call | solution.py:282
  165.5 2.8 gather_fusion.1
  168.3 28.1 %all_to_all.20 = bf16[8,2,128,256]{3,2,1,0:T(8,128)(2,1)S(1)} all-to-all(bf16[8,2,128,256]{3,2,1,0:T(8,128)(2,1)} %after.80), channel_id=1, replica_groups=mesh['fsdp'=4,'seq'=8] {'seq'}, dimensions={0} | all-to-all | bytes 2097152 | tf_op jit(solution)/shard_map/all_to_all | solution.py:701
  198.3 6.5 multiply_reduce_fusion.3
  208.3 21.0 %collective-permute-done.12.refs_0_ = bf16[2,128,2048]{2,1,0:T(8,128)(2,1)} collective-permute-done((bf16[2,128,2048]{2,1,0:T(8,128)(2,1)S(1)}, bf16[2,128,2048]{2,1,0:T(8,128)(2,1)}, u32[]{:S(2)}, u32[]{:S(2)}) %collective-permute-start.12) | collective-permute-done | bytes 1048608 | tf_op jit(solution)/shard_map/ppermute | solution.py:31
  229.3 2.7 collective-permute-done.13.refs_1_.refs_0_
  233.2 20.5 %collective-permute-done.14.refs_0_ = bf16[2,128,2048]{2,1,0:T(8,128)(2,1)} collective-permute-done((bf16[2,128,2048]{2,1,0:T(8,128)(2,1)}, bf16[2,128,2048]{2,1,0:T(8,128)(2,1)}, u32[]{:S(2)}, u32[]{:S(2)}) %collective-permute-start.14) | collective-permute-done | bytes 1048608 | tf_op jit(solution)/shard_map/ppermute | solution.py:31
  253.7 3.0 collective-permute-done.15.refs_1_.refs_0_
  257.2 20.1 %collective-permute-done.16.refs_0_ = bf16[2,128,2048]{2,1,0:T(8,128)(2,1)} collective-permute-done((bf16[2,128,2048]{2,1,0:T(8,128)(2,1)}, bf16[2,128,2048]{2,1,0:T(8,128)(2,1)}, u32[]{:S(2)}, u32[]{:S(2)}) %collective-permute-start.16) | collective-permute-done | bytes 1048608 | tf_op jit(solution)/shard_map/ppermute | solution.py:31
  283.1 8.8 collective-permute-done.18.refs_0_
  292.0 4.7 collective-permute-done.19.refs_1_.refs_0_
  296.6 16.5 %collective-permute-done.20.refs_0_ = bf16[2,128,2048]{2,1,0:T(8,128)(2,1)} collective-permute-done((bf16[2,128,2048]{2,1,0:T(8,128)(2,1)}, bf16[2,128,2048]{2,1,0:T(8,128)(2,1)}, u32[]{:S(2)}, u32[]{:S(2)}) %collective-permute-start.20) | collective-permute-done | bytes 1048608 | tf_op jit(solution)/shard_map/ppermute | solution.py:31
  313.1 4.9 collective-permute-done.21.refs_1_.refs_0_
  328.7 6.3 collective-permute-done.22.refs_1_.refs_0_
  340.4 3.3 slice_add_fusion
  346.7 34.2 %dispatch.3 = (bf16[4,2,384,2048]{3,2,1,0:T(8,128)(2,1)}, f32[4,2,384,1024]{3,2,1,0:T(8,128)}) custom-call(bf16[256,2048]{1,0:T(8,128)(2,1)} %bitcast.206, bf16[256,2048]{1,0:T(8,128)(2,1)} %bitcast.209, bf16[256,2048]{1,0:T(8,128)(2,1)} %bitcast.208, bf16[256,2048]{1,0:T(8,128)(2,1)} %bitcast.37.refs_3_, bf16[256,2048]{1,0:T(8,128)(2,1)} %bitcast.38.refs_4_, ...), custom_call_target="tpu_custom_call" | custom-call | flops 1 | bytes 1 | tf_op jit(solution)/shard_map/dispatch/pallas_call | solution.py:428
  381.8 19.8 %dispatch.4 = (bf16[4,2,384,2048]{3,2,1,0:T(8,128)(2,1)}, f32[4,2,384,1024]{3,2,1,0:T(8,128)}) custom-call(bf16[256,2048]{1,0:T(8,128)(2,1)} %copy-done.44, bf16[256,2048]{1,0:T(8,128)(2,1)} %bitcast.18.refs_1_, bf16[256,2048]{1,0:T(8,128)(2,1)} %bitcast.19.refs_2_, bf16[256,2048]{1,0:T(8,128)(2,1)} %bitcast.20.refs_3_, bf16[256,2048]{1,0:T(8,128)(2,1)} %bitcast.21.refs_4_, ...), custom_call_target="tpu_custom_call" | custom-call | flops 1 | bytes 1 | tf_op jit(solution)/shard_map/dispatch/pallas_call | solution.py:428
  407.8 19.6 %dispatch.5 = (bf16[4,2,384,2048]{3,2,1,0:T(8,128)(2,1)}, f32[4,2,384,1024]{3,2,1,0:T(8,128)}) custom-call(bf16[256,2048]{1,0:T(8,128)(2,1)} %copy-done.44, bf16[256,2048]{1,0:T(8,128)(2,1)} %bitcast.18.refs_1_, bf16[256,2048]{1,0:T(8,128)(2,1)} %bitcast.19.refs_2_, ...), custom_call_target="tpu_custom_call", output_to_operand_aliasing={{0}: (12, {}), {1}: (13, {})} | custom-call | flops 1 | bytes 1 | tf_op jit(solution)/shard_map/dispatch/pallas_call | solution.py:428
  432.8 32.2 %activate.1 = (bf16[4,2,384,1024]{3,2,1,0:T(8,128)(2,1)}, bf16[4,2,384,1024]{3,2,1,0:T(8,128)(2,1)}, bf16[4,2,384,1024]{3,2,1,0:T(8,128)(2,1)}) custom-call(bf16[4,2,384,2048]{3,2,1,0:T(8,128)(2,1)} %get-tuple-element.55.refs_0_.refs_1_, f32[4,2,384,1024]{3,2,1,0:T(8,128)} %get-tuple-element.56.refs_1_, f32[4,2,384,1024]{3,2,1,0:T(8,128)} %get-tuple-element.57.refs_2_, ...), custom_call_target="tpu_custom_call" | custom-call | flops 1 | bytes 1 | tf_op jit(solution)/shard_map/activate/pallas_call | solution.py:428
  469.9 27.8 %combine.4 = (bf16[256,2048]{1,0:T(8,128)(2,1)}, bf16[256,2048]{1,0:T(8,128)(2,1)}, bf16[256,2048]{1,0:T(8,128)(2,1)}, bf16[256,2048]{1,0:T(8,128)(2,1)}) custom-call(bf16[4,2,384,1024]{3,2,1,0:T(8,128)(2,1)} %get-tuple-element.59.refs_0_.refs_1_, bf16[4,2,384,1024]{3,2,1,0:T(8,128)(2,1)} %get-tuple-element.60.refs_1_, ...), custom_call_target="tpu_custom_call" | custom-call | flops 1 | bytes 1 | tf_op jit(solution)/shard_map/combine/pallas_call | solution.py:428
  497.7 12.9 %bank_grad.4.refs_5_ = bf16[2,2048,1024]{2,1,0:T(8,128)(2,1)} custom-call(bf16[4,2,384,2048]{3,2,1,0:T(8,128)(2,1)} %get-tuple-element.52.refs_1_.refs_14_.refs_16_.refs_0_, bf16[4,2,384,1024]{3,2,1,0:T(8,128)(2,1)} %get-tuple-element.58.refs_1_.refs_0_, bf16[256,2048]{1,0:T(8,128)(2,1)} %get-tuple-element.61.refs_2_), custom_call_target="tpu_custom_call" | custom-call | flops 1 | bytes 1 | tf_op jit(solution)/shard_map/bank_grad/pallas_call | solution.py:428
  512.9 20.0 %combine.5 = (bf16[256,2048]{1,0:T(8,128)(2,1)}, bf16[256,2048]{1,0:T(8,128)(2,1)}, bf16[256,2048]{1,0:T(8,128)(2,1)}, bf16[256,2048]{1,0:T(8,128)(2,1)}) custom-call(bf16[4,2,384,1024]{3,2,1,0:T(8,128)(2,1)} %get-tuple-element.58.refs_1_.refs_0_, bf16[4,2048,1024]{2,1,0:T(8,128)(2,1)} %all-gather.12.cloned.1.call-done.refs_11_.refs_1_, ...), custom_call_target="tpu_custom_call" | custom-call | flops 1 | bytes 1 | tf_op jit(solution)/shard_map/combine/pallas_call | solution.py:428
  533.0 28.4 %combine.6 = (bf16[256,2048]{1,0:T(8,128)(2,1)}, bf16[256,2048]{1,0:T(8,128)(2,1)}, bf16[256,2048]{1,0:T(8,128)(2,1)}, bf16[256,2048]{1,0:T(8,128)(2,1)}) custom-call(bf16[4,2,384,1024]{3,2,1,0:T(8,128)(2,1)} %get-tuple-element.59.refs_0_.refs_1_, bf16[4,2,384,1024]{3,2,1,0:T(8,128)(2,1)} %get-tuple-element.60.refs_1_, ...), custom_call_target="tpu_custom_call" | custom-call | flops 1 | bytes 1 | tf_op jit(solution)/shard_map/combine/pallas_call | solution.py:428
  563.4 2.9 fusion.16
  567.4 12.9 %bank_grad.5.refs_1_.refs_0_ = bf16[2,2048,1024]{2,1,0:T(8,128)(2,1)} custom-call(bf16[4,2,384,2048]{3,2,1,0:T(8,128)(2,1)} %get-tuple-element.52.refs_1_.refs_14_.refs_16_.refs_0_, bf16[4,2,384,1024]{3,2,1,0:T(8,128)(2,1)} %get-tuple-element.58.refs_1_.refs_0_, bf16[2,128,2048]{2,1,0:T(8,128)(2,1)} %after.103.refs_2_, ...), custom_call_target="tpu_custom_call" | custom-call | flops 1 | bytes 1 | tf_op jit(solution)/shard_map/bank_grad/pallas_call | solution.py:428
  581.4 5.9 collective-permute-done.37.refs_2_.refs_0_
  590.9 21.5 %combine.7 = (bf16[256,2048]{1,0:T(8,128)(2,1)}, bf16[256,2048]{1,0:T(8,128)(2,1)}, bf16[256,2048]{1,0:T(8,128)(2,1)}, bf16[256,2048]{1,0:T(8,128)(2,1)}) custom-call(bf16[4,2,384,1024]{3,2,1,0:T(8,128)(2,1)} %get-tuple-element.58.refs_1_.refs_0_, bf16[4,2048,1024]{2,1,0:T(8,128)(2,1)} %all-gather.12.cloned.1.call-done.refs_11_.refs_1_, ...), custom_call_target="tpu_custom_call" | custom-call | flops 1 | bytes 1 | tf_op jit(solution)/shard_map/combine/pallas_call | solution.py:428
  617.2 24.1 %bank_grad.6.refs_1_.refs_0_ = bf16[4,2048,1024]{2,1,0:T(8,128)(2,1)} custom-call(bf16[4,2,384,2048]{3,2,1,0:T(8,128)(2,1)} %get-tuple-element.55.refs_0_.refs_1_, bf16[4,2,384,1024]{3,2,1,0:T(8,128)(2,1)} %get-tuple-element.59.refs_0_.refs_1_, bf16[2,128,2048]{2,1,0:T(8,128)(2,1)} %after.107.refs_2_, bf16[2,128,2048]{2,1,0:T(8,128)(2,1)} %after.108.refs_3_), custom_call_target="tpu_custom_call" | custom-call | flops 1 | bytes 1 | tf_op jit(solution)/shard_map/bank_grad/pallas_call | solution.py:428
  646.7 6.1 convolution_convert_fusion.refs_2_
  654.4 6.0 all-to-all-start.1
  660.4 26.8 %bank_grad.7.refs_1_.refs_0_ = bf16[4,2048,1024]{2,1,0:T(8,128)(2,1)} custom-call(bf16[4,2,384,2048]{3,2,1,0:T(8,128)(2,1)} %get-tuple-element.55.refs_0_.refs_1_, bf16[4,2,384,1024]{3,2,1,0:T(8,128)(2,1)} %get-tuple-element.60.refs_1_, bf16[256,2048]{1,0:T(8,128)(2,1)} %copy-done.54), custom_call_target="tpu_custom_call" | custom-call | flops 1 | bytes 1 | tf_op jit(solution)/shard_map/bank_grad/pallas_call | solution.py:428
  690.0 6.0 all-to-all-start.2
  696.0 2.9 fusion.12
  702.4 3.0 gather_fusion.2
  711.5 33.1 %attend_back.1 = (bf16[8,2,128,768]{3,2,1,0:T(8,128)(2,1)S(1)}, f32[4,2,128]{2,1,0:T(2,128)S(1)}) custom-call(bf16[8,2,128,768]{3,2,1,0:T(8,128)(2,1)S(1)} %copy-done.2, bf16[8,2,128,256]{3,2,1,0:T(8,128)(2,1)S(1)} %copy-done.10, f32[1024,128]{1,0:T(8,128)S(1)} %copy-done.9, f32[1024,128]{1,0:T(8,128)S(1)} %copy-done.7, s32[2,1,1024]{2,1,0:T(1,128)S(1)} %bitcast.194, ...), custom_call_target="tpu_custom_call" | custom-call | flops 1 | bytes 1 | tf_op jit(solution)/shard_map/attend_back/pallas_call | solution.py:299
  746.8 12.6 %part_grads.1 = (bf16[256,2048]{1,0:T(8,128)(2,1)}, bf16[256,2048]{1,0:T(8,128)(2,1)}, bf16[256,2048]{1,0:T(8,128)(2,1)}, bf16[256,2048]{1,0:T(8,128)(2,1)}, bf1...) custom-call(bf16[2048,768]{1,0:T(8,128)(2,1)} %bitcast.190, ...), custom_call_target="tpu_custom_call" | custom-call | flops 1 | bytes 1 | tf_op jit(solution)/shard_map/part_grads/pallas_call | solution.py:428
  760.7 3.1 add_convert_fusion.6
  772.6 20.5 %proj_grads.1 = (bf16[512,1152]{1,0:T(8,128)(2,1)}, bf16[512,1152]{1,0:T(8,128)(2,1)}, bf16[512,1152]{1,0:T(8,128)(2,1)}, bf16[512,1152]{1,0:T(8,128)(2,1)}) custom-call(s32[4]{0:T(128)} %fusion.41.refs_0_, s32[8]{0:T(128)} %get-tuple-element.101.refs_1_, bf16[2048,2048]{1,0:T(8,128)(2,1)} %bitcast.202, bf16[2048,768]{1,0:T(8,128)(2,1)} %bitcast.191, ...), custom_call_target="tpu_custom_call" | custom-call | flops 1 | bytes 1 | tf_op jit(solution)/shard_map/proj_grads/pallas_call | solution.py:389
  793.1 2.9 collective-permute-done.44.refs_2_.refs_0_
  797.7 5.8 collective-permute-done.52
  812.7 27.3 %collective-permute-done.53.refs_1_.refs_0_ = bf16[512,1152]{1,0:T(8,128)(2,1)} collective-permute-done((bf16[512,1152]{1,0:T(8,128)(2,1)}, bf16[512,1152]{1,0:T(8,128)(2,1)}, u32[]{:S(2)}, u32[]{:S(2)}) %collective-permute-start.53) | collective-permute-done | bytes 1179680 | tf_op jit(solution)/shard_map/ppermute | solution.py:31
  841.3 3.1 add_convert_fusion.refs_4_.refs_0_
  844.5 11.4 %collective-permute-done.48.refs_0_ = bf16[2,128,2048]{2,1,0:T(8,128)(2,1)S(1)} collective-permute-done((bf16[2,128,2048]{2,1,0:T(8,128)(2,1)}, bf16[2,128,2048]{2,1,0:T(8,128)(2,1)S(1)}, u32[]{:S(2)}, u32[]{:S(2)}) %collective-permute-start.48) | collective-permute-done | bytes 1048608 | tf_op jit(solution)/shard_map/ppermute | solution.py:31
  858.4 4.2 all-to-all-start.3
  862.6 2.8 add_convert_fusion.4
  869.4 6.2 maximum_convert_fusion.refs_1_
  875.6 24.1 %collective-permute-done.56.refs_3_.refs_0_ = f32[2,128]{1,0:T(2,128)S(1)} collective-permute-done((f32[2,128]{1,0:T(2,128)S(1)}, f32[2,128]{1,0:T(2,128)S(1)}, u32[]{:S(2)}, u32[]{:S(2)}) %collective-permute-start.56) | collective-permute-done | bytes 1056 | tf_op jit(solution)/shard_map/ppermute | solution.py:867
  899.7 7.9 collective-permute-done.54.refs_0_
  907.7 5.5 all-to-all-done.3.refs_4_.refs_0_
  920.4 3.5 convert_add_fusion.14
  929.2 3.7 reshape.579
  935.0 5.4 fusion.63
  946.2 6.6 convert_element_type.450.refs_1_
  962.5 4.8 fusion.19
  967.9 6.8 convert_element_type.465
  (473 shorter events, 191.3 us)
Async XLA Ops:
  7.2 117.8 %all-gather.6.cloned.1.call-start = ((), (), s32[]{:S(2)}) async-start(), calls=%async_computation.8 | async-start | bytes 4587520 | tf_op jit(solution)/shard_map/all_gather | solution.py:648
  12.0 186.3 %all-gather.8.cloned.1.call-start = ((), (), s32[]{:S(2)}) async-start(), calls=%async_computation.9 | async-start | bytes 10485760 | tf_op jit(solution)/shard_map/all_gather | solution.py:648
  12.7 334.0 %all-gather.12.cloned.1.call-start = ((), (), s32[]{:S(2)}) async-start(), calls=%async_computation.11 | async-start | bytes 20971520 | tf_op jit(solution)/shard_map/all_gather | solution.py:648
  13.5 368.3 %all-gather.10.cloned.1.call-start = ((), (), s32[]{:S(2)}) async-start(), calls=%async_computation.10 | async-start | bytes 20971520 | tf_op jit(solution)/shard_map/all_gather | solution.py:648
  14.1 418.7 %all-gather.14.cloned.1.call-start = ((), (), s32[]{:S(2)}) async-start(), calls=%async_computation.12 | async-start | bytes 20971520 | tf_op jit(solution)/shard_map/all_gather | solution.py:648
  14.7 854.8 %reduce-scatter.5.cloned.1.call-start = ((), (), s32[]{:S(2)}) async-start(), calls=%async_computation.13 | async-start | bytes 10485760 | tf_op jit(solution)/shard_map/reduce_scatter | solution.py:811
  17.6 29.6 %collective-permute-start.1 = (bf16[2,128,2176]{2,1,0:T(8,128)(2,1)S(1)}, bf16[2,128,2176]{2,1,0:T(8,128)(2,1)S(1)}, u32[]{:S(2)}, u32[]{:S(2)}) collective-permute-start(bf16[2,128,2176]{2,1,0:T(8,128)(2,1)S(1)} %get-tuple-element.109), channel_id=1, source_target_pairs={{0,2},{1,3},{2,4},{3,5},{4,6},{5,7},{6,0},{7,1},{8,10},{9,11},{10,... | collective-permute-start | bytes 3342344 | tf_op jit(solution)/shard_map/ppermute | solution.py:31
  20.6 35.9 %collective-permute-start = (bf16[2,128,2176]{2,1,0:T(8,128)(2,1)S(1)}, bf16[2,128,2176]{2,1,0:T(8,128)(2,1)}, u32[]{:S(2)}, u32[]{:S(2)}) collective-permute-start(bf16[2,128,2176]{2,1,0:T(8,128)(2,1)S(1)} %get-tuple-element.109), channel_id=1, source_target_pairs={{0,1},{1,0},{2,3},{3,2},{4,5},{5,4},{6,7},{7,6},{8,9},{9,8},{10,11... | collective-permute-start | bytes 3342344 | tf_op jit(solution)/shard_map/ppermute | solution.py:31
  47.2 27.7 %collective-permute-start.3 = (bf16[2,128,2176]{2,1,0:T(8,128)(2,1)S(1)}, bf16[2,128,2176]{2,1,0:T(8,128)(2,1)}, u32[]{:S(2)}, u32[]{:S(2)}) collective-permute-start(bf16[2,128,2176]{2,1,0:T(8,128)(2,1)S(1)} %collective-permute-done.1), channel_id=1, source_target_pairs={{0,2},{1,3},{2,4},{3,5},{4,6},{5,7},{6,0},{7,1},{8,10},{9,11},{10,... | collective-permute-start | bytes 3342344 | tf_op jit(solution)/shard_map/ppermute | solution.py:31
  51.9 27.3 %collective-permute-start.2 = (bf16[2,128,2176]{2,1,0:T(8,128)(2,1)S(1)}, bf16[2,128,2176]{2,1,0:T(8,128)(2,1)S(1)}, u32[]{:S(2)}, u32[]{:S(2)}) collective-permute-start(bf16[2,128,2176]{2,1,0:T(8,128)(2,1)S(1)} %collective-permute-done.1), channel_id=1, source_target_pairs={{0,1},{1,0},{2,3},{3,2},{4,5},{5,4},{6,7},{7,6},{8,9},{9,8},{10,11... | collective-permute-start | bytes 3342344 | tf_op jit(solution)/shard_map/ppermute | solution.py:31
  74.8 28.7 %collective-permute-start.4 = (bf16[2,128,2176]{2,1,0:T(8,128)(2,1)}, bf16[2,128,2176]{2,1,0:T(8,128)(2,1)S(1)}, u32[]{:S(2)}, u32[]{:S(2)}) collective-permute-start(bf16[2,128,2176]{2,1,0:T(8,128)(2,1)} %collective-permute-done.3), channel_id=1, source_target_pairs={{0,1},{1,0},{2,3},{3,2},{4,5},{5,4},{6,7},{7,6},{8,9},{9,8},{10,11... | collective-permute-start | bytes 3342344 | tf_op jit(solution)/shard_map/ppermute | solution.py:31
  76.1 26.3 %collective-permute-start.5 = (bf16[2,128,2176]{2,1,0:T(8,128)(2,1)}, bf16[2,128,2176]{2,1,0:T(8,128)(2,1)S(1)}, u32[]{:S(2)}, u32[]{:S(2)}) collective-permute-start(bf16[2,128,2176]{2,1,0:T(8,128)(2,1)} %collective-permute-done.3), channel_id=1, source_target_pairs={{0,2},{1,3},{2,4},{3,5},{4,6},{5,7},{6,0},{7,1},{8,10},{9,11},{10,... | collective-permute-start | bytes 3342344 | tf_op jit(solution)/shard_map/ppermute | solution.py:31
  117.7 23.0 %collective-permute-start.8 = (bf16[2,128,2048]{2,1,0:T(8,128)(2,1)}, bf16[2,128,2048]{2,1,0:T(8,128)(2,1)S(1)}, u32[]{:S(2)}, u32[]{:S(2)}) collective-permute-start(bf16[2,128,2048]{2,1,0:T(8,128)(2,1)} %after.75), channel_id=1, source_target_pairs={{0,2},{1,3},{2,4},{3,5},{4,6},{5,7},{6,0},{7,1},{8,10},{9,11},{10,... | collective-permute-start | bytes 3145736 | tf_op jit(solution)/shard_map/ppermute | solution.py:31
  117.7 23.0 %collective-permute-start.9 = (bf16[2,128,2048]{2,1,0:T(8,128)(2,1)}, bf16[2,128,2048]{2,1,0:T(8,128)(2,1)S(1)}, u32[]{:S(2)}, u32[]{:S(2)}) collective-permute-start(bf16[2,128,2048]{2,1,0:T(8,128)(2,1)} %after.75), channel_id=1, source_target_pairs={{0,1},{1,0},{2,3},{3,2},{4,5},{5,4},{6,7},{7,6},{8,9},{9,8},{10,11... | collective-permute-start | bytes 3145736 | tf_op jit(solution)/shard_map/ppermute | solution.py:31
  142.8 25.5 %collective-permute-start.10 = (bf16[2,128,2048]{2,1,0:T(8,128)(2,1)}, bf16[2,128,2048]{2,1,0:T(8,128)(2,1)}, u32[]{:S(2)}, u32[]{:S(2)}) collective-permute-start(bf16[2,128,2048]{2,1,0:T(8,128)(2,1)} %after.77), channel_id=1, source_target_pairs={{0,2},{1,3},{2,4},{3,5},{4,6},{5,7},{6,0},{7,1},{8,10},{9,11},{10,... | collective-permute-start | bytes 3145736 | tf_op jit(solution)/shard_map/ppermute | solution.py:31
  143.4 24.9 %collective-permute-start.11 = (bf16[2,128,2048]{2,1,0:T(8,128)(2,1)}, bf16[2,128,2048]{2,1,0:T(8,128)(2,1)}, u32[]{:S(2)}, u32[]{:S(2)}) collective-permute-start(bf16[2,128,2048]{2,1,0:T(8,128)(2,1)} %after.77), channel_id=1, source_target_pairs={{0,1},{1,0},{2,3},{3,2},{4,5},{5,4},{6,7},{7,6},{8,9},{9,8},{10,11... | collective-permute-start | bytes 3145736 | tf_op jit(solution)/shard_map/ppermute | solution.py:31
  206.4 22.9 %collective-permute-start.12 = (bf16[2,128,2048]{2,1,0:T(8,128)(2,1)S(1)}, bf16[2,128,2048]{2,1,0:T(8,128)(2,1)}, u32[]{:S(2)}, u32[]{:S(2)}) collective-permute-start(bf16[2,128,2048]{2,1,0:T(8,128)(2,1)S(1)} %bitcast.204), channel_id=1, source_target_pairs={{0,1},{1,0},{2,3},{3,2},{4,5},{5,4},{6,7},{7,6},{8,9},{9,8},{10,11... | collective-permute-start | bytes 3145736 | tf_op jit(solution)/shard_map/ppermute | solution.py:31
  207.9 24.1 %collective-permute-start.13 = (bf16[2,128,2048]{2,1,0:T(8,128)(2,1)S(1)}, bf16[2,128,2048]{2,1,0:T(8,128)(2,1)}, u32[]{:S(2)}, u32[]{:S(2)}) collective-permute-start(bf16[2,128,2048]{2,1,0:T(8,128)(2,1)S(1)} %bitcast.205), channel_id=1, source_target_pairs={{0,2},{1,3},{2,4},{3,5},{4,6},{5,7},{6,0},{7,1},{8,10},{9,11},{10,... | collective-permute-start | bytes 3145736 | tf_op jit(solution)/shard_map/ppermute | solution.py:31
  232.0 21.6 %collective-permute-start.14 = (bf16[2,128,2048]{2,1,0:T(8,128)(2,1)}, bf16[2,128,2048]{2,1,0:T(8,128)(2,1)}, u32[]{:S(2)}, u32[]{:S(2)}) collective-permute-start(bf16[2,128,2048]{2,1,0:T(8,128)(2,1)} %after.82), channel_id=1, source_target_pairs={{0,1},{1,0},{2,3},{3,2},{4,5},{5,4},{6,7},{7,6},{8,9},{9,8},{10,11... | collective-permute-start | bytes 3145736 | tf_op jit(solution)/shard_map/ppermute | solution.py:31
  233.2 23.4 %collective-permute-start.15 = (bf16[2,128,2048]{2,1,0:T(8,128)(2,1)}, bf16[2,128,2048]{2,1,0:T(8,128)(2,1)}, u32[]{:S(2)}, u32[]{:S(2)}) collective-permute-start(bf16[2,128,2048]{2,1,0:T(8,128)(2,1)} %after.82), channel_id=1, source_target_pairs={{0,2},{1,3},{2,4},{3,5},{4,6},{5,7},{6,0},{7,1},{8,10},{9,11},{10,... | collective-permute-start | bytes 3145736 | tf_op jit(solution)/shard_map/ppermute | solution.py:31
  256.6 20.7 %collective-permute-start.16 = (bf16[2,128,2048]{2,1,0:T(8,128)(2,1)}, bf16[2,128,2048]{2,1,0:T(8,128)(2,1)}, u32[]{:S(2)}, u32[]{:S(2)}) collective-permute-start(bf16[2,128,2048]{2,1,0:T(8,128)(2,1)} %after.84), channel_id=1, source_target_pairs={{0,1},{1,0},{2,3},{3,2},{4,5},{5,4},{6,7},{7,6},{8,9},{9,8},{10,11... | collective-permute-start | bytes 3145736 | tf_op jit(solution)/shard_map/ppermute | solution.py:31
  257.2 21.9 %collective-permute-start.17 = (bf16[2,128,2048]{2,1,0:T(8,128)(2,1)}, bf16[2,128,2048]{2,1,0:T(8,128)(2,1)}, u32[]{:S(2)}, u32[]{:S(2)}) collective-permute-start(bf16[2,128,2048]{2,1,0:T(8,128)(2,1)} %after.84), channel_id=1, source_target_pairs={{0,2},{1,3},{2,4},{3,5},{4,6},{5,7},{6,0},{7,1},{8,10},{9,11},{10,... | collective-permute-start | bytes 3145736 | tf_op jit(solution)/shard_map/ppermute | solution.py:31
  296.6 16.5 %collective-permute-start.20 = (bf16[2,128,2048]{2,1,0:T(8,128)(2,1)}, bf16[2,128,2048]{2,1,0:T(8,128)(2,1)}, u32[]{:S(2)}, u32[]{:S(2)}) collective-permute-start(bf16[2,128,2048]{2,1,0:T(8,128)(2,1)} %after.89), channel_id=1, source_target_pairs={{0,1},{1,0},{2,3},{3,2},{4,5},{5,4},{6,7},{7,6},{8,9},{9,8},{10,11... | collective-permute-start | bytes 3145736 | tf_op jit(solution)/shard_map/ppermute | solution.py:31
  296.6 21.4 %collective-permute-start.21 = (bf16[2,128,2048]{2,1,0:T(8,128)(2,1)}, bf16[2,128,2048]{2,1,0:T(8,128)(2,1)}, u32[]{:S(2)}, u32[]{:S(2)}) collective-permute-start(bf16[2,128,2048]{2,1,0:T(8,128)(2,1)} %after.89), channel_id=1, source_target_pairs={{0,2},{1,3},{2,4},{3,5},{4,6},{5,7},{6,0},{7,1},{8,10},{9,11},{10,... | collective-permute-start | bytes 3145736 | tf_op jit(solution)/shard_map/ppermute | solution.py:31
  321.9 15.1 %collective-permute-start.23 = (bf16[1,128,2048]{2,1,0:T(8,128)(2,1)}, bf16[1,128,2048]{2,1,0:T(8,128)(2,1)}, u32[]{:S(2)}, u32[]{:S(2)}) collective-permute-start(bf16[1,128,2048]{2,1,0:T(8,128)(2,1)} %slice.115), channel_id=1, source_target_pairs={{0,1},{1,0},{2,3},{3,2},{4,5},{5,4},{6,7},{7,6},{8,9},{9,8},{10,11... | collective-permute-start | bytes 1572872 | tf_op jit(solution)/shard_map/ppermute | solution.py:31
  337.0 43.9 %collective-permute-start.24 = (bf16[2048,256]{1,0:T(8,128)(2,1)}, bf16[2048,256]{1,0:T(8,128)(2,1)}, u32[]{:S(2)}, u32[]{:S(2)}) collective-permute-start(bf16[2048,256]{1,0:T(8,128)(2,1)} %after.94.refs_6_), channel_id=1, source_target_pairs={{0,1},{1,0},{2,3},{3,2},{4,5},{5,4},{6,7},{7,6},{8,9},{9,8},{10,11... | collective-permute-start | bytes 3145736 | tf_op jit(solution)/shard_map/ppermute | solution.py:31
  339.1 41.8 %collective-permute-start.25 = (bf16[2048,256]{1,0:T(8,128)(2,1)}, bf16[2048,256]{1,0:T(8,128)(2,1)}, u32[]{:S(2)}, u32[]{:S(2)}) collective-permute-start(bf16[2048,256]{1,0:T(8,128)(2,1)} %after.94.refs_6_), channel_id=1, source_target_pairs={{0,2},{1,3},{2,4},{3,5},{4,6},{5,7},{6,0},{7,1},{8,10},{9,11},{10,... | collective-permute-start | bytes 3145736 | tf_op jit(solution)/shard_map/ppermute | solution.py:31
  380.9 20.9 %collective-permute-start.26 = (bf16[2048,256]{1,0:T(8,128)(2,1)}, bf16[2048,256]{1,0:T(8,128)(2,1)}, u32[]{:S(2)}, u32[]{:S(2)}) collective-permute-start(bf16[2048,256]{1,0:T(8,128)(2,1)} %after.96.refs_13_.refs_8_), channel_id=1, source_target_pairs={{0,1},{1,0},{2,3},{3,2},{4,5},{5,4},{6,7},{7,6},{8,9},{9,8},{10,11... | collective-permute-start | bytes 3145736 | tf_op jit(solution)/shard_map/ppermute | solution.py:31
  381.1 22.5 %collective-permute-start.27 = (bf16[2048,256]{1,0:T(8,128)(2,1)}, bf16[2048,256]{1,0:T(8,128)(2,1)}, u32[]{:S(2)}, u32[]{:S(2)}) collective-permute-start(bf16[2048,256]{1,0:T(8,128)(2,1)} %after.96.refs_13_.refs_8_), channel_id=1, source_target_pairs={{0,2},{1,3},{2,4},{3,5},{4,6},{5,7},{6,0},{7,1},{8,10},{9,11},{10,... | collective-permute-start | bytes 3145736 | tf_op jit(solution)/shard_map/ppermute | solution.py:31
  403.6 23.8 %collective-permute-start.29 = (bf16[2048,256]{1,0:T(8,128)(2,1)}, bf16[2048,256]{1,0:T(8,128)(2,1)}, u32[]{:S(2)}, u32[]{:S(2)}) collective-permute-start(bf16[2048,256]{1,0:T(8,128)(2,1)} %after.98.refs_15_.refs_10_), channel_id=1, source_target_pairs={{0,1},{1,0},{2,3},{3,2},{4,5},{5,4},{6,7},{7,6},{8,9},{9,8},{10,11... | collective-permute-start | bytes 3145736 | tf_op jit(solution)/shard_map/ppermute | solution.py:31
  405.9 22.7 %collective-permute-start.28 = (bf16[2048,256]{1,0:T(8,128)(2,1)}, bf16[2048,256]{1,0:T(8,128)(2,1)}, u32[]{:S(2)}, u32[]{:S(2)}) collective-permute-start(bf16[2048,256]{1,0:T(8,128)(2,1)} %after.98.refs_15_.refs_10_), channel_id=1, source_target_pairs={{0,2},{1,3},{2,4},{3,5},{4,6},{5,7},{6,0},{7,1},{8,10},{9,11},{10,... | collective-permute-start | bytes 3145736 | tf_op jit(solution)/shard_map/ppermute | solution.py:31
  430.4 34.6 %collective-permute-start.31 = (bf16[1024,256]{1,0:T(8,128)(2,1)}, bf16[1024,256]{1,0:T(8,128)(2,1)}, u32[]{:S(2)}, u32[]{:S(2)}) collective-permute-start(bf16[1024,256]{1,0:T(8,128)(2,1)} %slice.117), channel_id=1, source_target_pairs={{0,2},{1,3},{2,4},{3,5},{4,6},{5,7},{6,0},{7,1},{8,10},{9,11},{10,... | collective-permute-start | bytes 1572872 | tf_op jit(solution)/shard_map/ppermute | solution.py:31
  432.8 32.2 %collective-permute-start.30 = (bf16[1024,256]{1,0:T(8,128)(2,1)}, bf16[1024,256]{1,0:T(8,128)(2,1)}, u32[]{:S(2)}, u32[]{:S(2)}) collective-permute-start(bf16[1024,256]{1,0:T(8,128)(2,1)} %slice.116), channel_id=1, source_target_pairs={{0,1},{1,0},{2,3},{3,2},{4,5},{5,4},{6,7},{7,6},{8,9},{9,8},{10,11... | collective-permute-start | bytes 1572872 | tf_op jit(solution)/shard_map/ppermute | solution.py:31
  510.6 358.8 %reduce-scatter.7.cloned.1.call-start = ((), (), s32[]{:S(2)}) async-start(), calls=%async_computation.14 | async-start | bytes 10485760 | tf_op jit(solution)/shard_map/reduce_scatter | solution.py:811
  510.9 52.5 %collective-permute-start.35 = (bf16[2,128,2048]{2,1,0:T(8,128)(2,1)}, bf16[2,128,2048]{2,1,0:T(8,128)(2,1)}, u32[]{:S(2)}, u32[]{:S(2)}) collective-permute-start(bf16[2,128,2048]{2,1,0:T(8,128)(2,1)} %bitcast.267), channel_id=1, source_target_pairs={{0,1},{1,0},{2,3},{3,2},{4,5},{5,4},{6,7},{7,6},{8,9},{9,8},{10,11... | collective-permute-start | bytes 3145736 | tf_op jit(solution)/shard_map/ppermute | solution.py:31
  532.9 30.4 %collective-permute-start.36 = (bf16[2,128,2048]{2,1,0:T(8,128)(2,1)}, bf16[2,128,2048]{2,1,0:T(8,128)(2,1)}, u32[]{:S(2)}, u32[]{:S(2)}) collective-permute-start(bf16[2,128,2048]{2,1,0:T(8,128)(2,1)} %bitcast.269), channel_id=1, source_target_pairs={{0,1},{1,0},{2,3},{3,2},{4,5},{5,4},{6,7},{7,6},{8,9},{9,8},{10,11... | collective-permute-start | bytes 3145736 | tf_op jit(solution)/shard_map/ppermute | solution.py:31
  561.4 20.0 %collective-permute-start.34 = (bf16[2,128,2048]{2,1,0:T(8,128)(2,1)}, bf16[2,128,2048]{2,1,0:T(8,128)(2,1)}, u32[]{:S(2)}, u32[]{:S(2)}) collective-permute-start(bf16[2,128,2048]{2,1,0:T(8,128)(2,1)} %bitcast.268), channel_id=1, source_target_pairs={{0,1},{1,0},{2,3},{3,2},{4,5},{5,4},{6,7},{7,6},{8,9},{9,8},{10,11... | collective-permute-start | bytes 3145736 | tf_op jit(solution)/shard_map/ppermute | solution.py:31
  566.3 21.0 %collective-permute-start.37 = (bf16[2,128,2048]{2,1,0:T(8,128)(2,1)}, bf16[2,128,2048]{2,1,0:T(8,128)(2,1)}, u32[]{:S(2)}, u32[]{:S(2)}) collective-permute-start(bf16[2,128,2048]{2,1,0:T(8,128)(2,1)} %fusion.16), channel_id=1, source_target_pairs={{0,2},{1,3},{2,4},{3,5},{4,6},{5,7},{6,0},{7,1},{8,10},{9,11},{10,... | collective-permute-start | bytes 3145736 | tf_op jit(solution)/shard_map/ppermute | solution.py:31
  587.3 358.9 %reduce-scatter.9.cloned.1.call-start = ((), (), s32[]{:S(2)}) async-start(), calls=%async_computation.15 | async-start | bytes 20971520 | tf_op jit(solution)/shard_map/reduce_scatter | solution.py:811
  587.4 25.0 %collective-permute-start.33 = (bf16[2,128,2048]{2,1,0:T(8,128)(2,1)}, bf16[2,128,2048]{2,1,0:T(8,128)(2,1)}, u32[]{:S(2)}, u32[]{:S(2)}) collective-permute-start(bf16[2,128,2048]{2,1,0:T(8,128)(2,1)} %bitcast.266), channel_id=1, source_target_pairs={{0,1},{1,0},{2,3},{3,2},{4,5},{5,4},{6,7},{7,6},{8,9},{9,8},{10,11... | collective-permute-start | bytes 3145736 | tf_op jit(solution)/shard_map/ppermute | solution.py:31
  590.4 22.0 %collective-permute-start.38 = (bf16[2,128,2048]{2,1,0:T(8,128)(2,1)S(1)}, bf16[2,128,2048]{2,1,0:T(8,128)(2,1)}, u32[]{:S(2)}, u32[]{:S(2)}) collective-permute-start(bf16[2,128,2048]{2,1,0:T(8,128)(2,1)S(1)} %add_convert_fusion.8), channel_id=1, source_target_pairs={{0,2},{1,3},{2,4},{3,5},{4,6},{5,7},{6,0},{7,1},{8,10},{9,11},{10,... | collective-permute-start | bytes 3145736 | tf_op jit(solution)/shard_map/ppermute | solution.py:31
  612.4 28.9 %collective-permute-start.32 = (bf16[2,128,2048]{2,1,0:T(8,128)(2,1)}, bf16[2,128,2048]{2,1,0:T(8,128)(2,1)}, u32[]{:S(2)}, u32[]{:S(2)}) collective-permute-start(bf16[2,128,2048]{2,1,0:T(8,128)(2,1)} %bitcast.265), channel_id=1, source_target_pairs={{0,1},{1,0},{2,3},{3,2},{4,5},{5,4},{6,7},{7,6},{8,9},{9,8},{10,11... | collective-permute-start | bytes 3145736 | tf_op jit(solution)/shard_map/ppermute | solution.py:31
  616.3 25.0 %collective-permute-start.39 = (bf16[2,128,2048]{2,1,0:T(8,128)(2,1)S(1)}, bf16[2,128,2048]{2,1,0:T(8,128)(2,1)}, u32[]{:S(2)}, u32[]{:S(2)}) collective-permute-start(bf16[2,128,2048]{2,1,0:T(8,128)(2,1)S(1)} %add_convert_fusion.7), channel_id=1, source_target_pairs={{0,2},{1,3},{2,4},{3,5},{4,6},{5,7},{6,0},{7,1},{8,10},{9,11},{10,... | collective-permute-start | bytes 3145736 | tf_op jit(solution)/shard_map/ppermute | solution.py:31
  654.4 32.9 %all-to-all-start.1 = ((bf16[8,2,128,256]{3,2,1,0:T(8,128)(2,1)}), bf16[8,2,128,256]{3,2,1,0:T(8,128)(2,1)}, u32[]{:S(2)}, u32[]{:S(2)}) async-start(bf16[8,2,128,256]{3,2,1,0:T(8,128)(2,1)} %bitcast.218), calls=%async_computation.1 | async-start | bytes 2097152 | tf_op jit(solution)/shard_map/all_to_all | solution.py:826
  660.3 307.6 %reduce-scatter.11.cloned.1.call-start = ((), (), s32[]{:S(2)}) async-start(), calls=%async_computation.16 | async-start | bytes 20971520 | tf_op jit(solution)/shard_map/reduce_scatter | solution.py:811
  690.0 69.4 %all-to-all-start.2 = ((bf16[8,2,128,256]{3,2,1,0:T(8,128)(2,1)}), bf16[8,2,128,256]{3,2,1,0:T(8,128)(2,1)}, u32[]{:S(2)}, u32[]{:S(2)}) async-start(bf16[8,2,128,256]{3,2,1,0:T(8,128)(2,1)} %bitcast.217), calls=%async_computation.2 | async-start | bytes 2097152 | tf_op jit(solution)/shard_map/all_to_all | solution.py:826
  699.0 60.5 %collective-permute-start.40 = (bf16[2,128,2048]{2,1,0:T(8,128)(2,1)}, bf16[2,128,2048]{2,1,0:T(8,128)(2,1)}, u32[]{:S(2)}, u32[]{:S(2)}) collective-permute-start(bf16[2,128,2048]{2,1,0:T(8,128)(2,1)} %fusion.12), channel_id=1, source_target_pairs={{0,2},{1,3},{2,4},{3,5},{4,6},{5,7},{6,0},{7,1},{8,10},{9,11},{10,... | collective-permute-start | bytes 3145736 | tf_op jit(solution)/shard_map/ppermute | solution.py:31
  701.0 58.5 %collective-permute-start.41 = (bf16[2,128,2048]{2,1,0:T(8,128)(2,1)}, bf16[2,128,2048]{2,1,0:T(8,128)(2,1)}, u32[]{:S(2)}, u32[]{:S(2)}) collective-permute-start(bf16[2,128,2048]{2,1,0:T(8,128)(2,1)} %after.113), channel_id=1, source_target_pairs={{0,1},{1,0},{2,3},{3,2},{4,5},{5,4},{6,7},{7,6},{8,9},{9,8},{10,11... | collective-permute-start | bytes 3145736 | tf_op jit(solution)/shard_map/ppermute | solution.py:31
  759.5 33.6 %collective-permute-start.42 = (bf16[2,128,2048]{2,1,0:T(8,128)(2,1)}, bf16[2,128,2048]{2,1,0:T(8,128)(2,1)S(1)}, u32[]{:S(2)}, u32[]{:S(2)}) collective-permute-start(bf16[2,128,2048]{2,1,0:T(8,128)(2,1)} %after.116), channel_id=1, source_target_pairs={{0,1},{1,0},{2,3},{3,2},{4,5},{5,4},{6,7},{7,6},{8,9},{9,8},{10,11... | collective-permute-start | bytes 3145736 | tf_op jit(solution)/shard_map/ppermute | solution.py:31
  763.8 29.3 %collective-permute-start.43 = (bf16[2,128,2048]{2,1,0:T(8,128)(2,1)}, bf16[2,128,2048]{2,1,0:T(8,128)(2,1)S(1)}, u32[]{:S(2)}, u32[]{:S(2)}) collective-permute-start(bf16[2,128,2048]{2,1,0:T(8,128)(2,1)} %add_convert_fusion.6), channel_id=1, source_target_pairs={{0,2},{1,3},{2,4},{3,5},{4,6},{5,7},{6,0},{7,1},{8,10},{9,11},{10,... | collective-permute-start | bytes 3145736 | tf_op jit(solution)/shard_map/ppermute | solution.py:31
  765.4 30.6 %collective-permute-start.44 = (bf16[2,128,2048]{2,1,0:T(8,128)(2,1)}, bf16[2,128,2048]{2,1,0:T(8,128)(2,1)S(1)}, u32[]{:S(2)}, u32[]{:S(2)}) collective-permute-start(bf16[2,128,2048]{2,1,0:T(8,128)(2,1)} %after.119), channel_id=1, source_target_pairs={{0,1},{1,0},{2,3},{3,2},{4,5},{5,4},{6,7},{7,6},{8,9},{9,8},{10,11... | collective-permute-start | bytes 3145736 | tf_op jit(solution)/shard_map/ppermute | solution.py:31
  768.2 24.9 %collective-permute-start.46 = (f32[2,128]{1,0:T(2,128)S(1)}, f32[2,128]{1,0:T(2,128)S(1)}, u32[]{:S(2)}, u32[]{:S(2)}) collective-permute-start(f32[2,128]{1,0:T(2,128)S(1)} %add.362), channel_id=1, source_target_pairs={{0,16},{8,24},{16,0},{24,8},{1,17},{9,25},{17,1},{25,9},{2,18},{10... | collective-permute-start | bytes 3080 | tf_op jit(solution)/shard_map/ppermute | solution.py:867
  804.8 35.3 %collective-permute-start.53 = (bf16[512,1152]{1,0:T(8,128)(2,1)}, bf16[512,1152]{1,0:T(8,128)(2,1)}, u32[]{:S(2)}, u32[]{:S(2)}) collective-permute-start(bf16[512,1152]{1,0:T(8,128)(2,1)} %add_convert_fusion.2), channel_id=1, source_target_pairs={{0,16},{8,24},{16,0},{24,8},{1,17},{9,25},{17,1},{25,9},{2,18},{10... | collective-permute-start | bytes 3538952 | tf_op jit(solution)/shard_map/ppermute | solution.py:31
  806.2 38.3 %collective-permute-start.49 = (bf16[2,128,2048]{2,1,0:T(8,128)(2,1)}, bf16[2,128,2048]{2,1,0:T(8,128)(2,1)S(1)}, u32[]{:S(2)}, u32[]{:S(2)}) collective-permute-start(bf16[2,128,2048]{2,1,0:T(8,128)(2,1)} %fusion.9), channel_id=1, source_target_pairs={{0,2},{1,3},{2,4},{3,5},{4,6},{5,7},{6,0},{7,1},{8,10},{9,11},{10,... | collective-permute-start | bytes 3145736 | tf_op jit(solution)/shard_map/ppermute | solution.py:31
  809.2 46.7 %collective-permute-start.48 = (bf16[2,128,2048]{2,1,0:T(8,128)(2,1)}, bf16[2,128,2048]{2,1,0:T(8,128)(2,1)S(1)}, u32[]{:S(2)}, u32[]{:S(2)}) collective-permute-start(bf16[2,128,2048]{2,1,0:T(8,128)(2,1)} %add_convert_fusion.5), channel_id=1, source_target_pairs={{0,2},{1,3},{2,4},{3,5},{4,6},{5,7},{6,0},{7,1},{8,10},{9,11},{10,... | collective-permute-start | bytes 3145736 | tf_op jit(solution)/shard_map/ppermute | solution.py:31
  810.7 45.1 %collective-permute-start.50 = (bf16[2,128,2048]{2,1,0:T(8,128)(2,1)}, bf16[2,128,2048]{2,1,0:T(8,128)(2,1)}, u32[]{:S(2)}, u32[]{:S(2)}) collective-permute-start(bf16[2,128,2048]{2,1,0:T(8,128)(2,1)} %after.125), channel_id=1, source_target_pairs={{0,1},{1,0},{2,3},{3,2},{4,5},{5,4},{6,7},{7,6},{8,9},{9,8},{10,11... | collective-permute-start | bytes 3145736 | tf_op jit(solution)/shard_map/ppermute | solution.py:31
  811.4 46.9 %collective-permute-start.47 = (bf16[2,128,2048]{2,1,0:T(8,128)(2,1)}, bf16[2,128,2048]{2,1,0:T(8,128)(2,1)}, u32[]{:S(2)}, u32[]{:S(2)}) collective-permute-start(bf16[2,128,2048]{2,1,0:T(8,128)(2,1)} %after.124), channel_id=1, source_target_pairs={{0,1},{1,0},{2,3},{3,2},{4,5},{5,4},{6,7},{7,6},{8,9},{9,8},{10,11... | collective-permute-start | bytes 3145736 | tf_op jit(solution)/shard_map/ppermute | solution.py:31
  858.4 54.7 %all-to-all-start.3 = ((bf16[8,64,1152]{2,1,0:T(8,128)(2,1)}), bf16[8,64,1152]{2,1,0:T(8,128)(2,1)S(1)}, u32[]{:S(2)}, u32[]{:S(2)}) async-start(bf16[8,64,1152]{2,1,0:T(8,128)(2,1)} %bitcast.200), calls=%async_computation.3 | async-start | bytes 2359296 | tf_op jit(solution)/shard_map/all_to_all | solution.py:895
  865.4 42.3 %collective-permute-start.54 = (bf16[2,128,2048]{2,1,0:T(8,128)(2,1)}, bf16[2,128,2048]{2,1,0:T(8,128)(2,1)S(1)}, u32[]{:S(2)}, u32[]{:S(2)}) collective-permute-start(bf16[2,128,2048]{2,1,0:T(8,128)(2,1)} %add_convert_fusion.4), channel_id=1, source_target_pairs={{0,2},{1,3},{2,4},{3,5},{4,6},{5,7},{6,0},{7,1},{8,10},{9,11},{10,... | collective-permute-start | bytes 3145736 | tf_op jit(solution)/shard_map/ppermute | solution.py:31
  867.4 40.3 %collective-permute-start.55 = (bf16[2,128,2048]{2,1,0:T(8,128)(2,1)}, bf16[2,128,2048]{2,1,0:T(8,128)(2,1)S(1)}, u32[]{:S(2)}, u32[]{:S(2)}) collective-permute-start(bf16[2,128,2048]{2,1,0:T(8,128)(2,1)} %after.138), channel_id=1, source_target_pairs={{0,1},{1,0},{2,3},{3,2},{4,5},{5,4},{6,7},{7,6},{8,9},{9,8},{10,11... | collective-permute-start | bytes 3145736 | tf_op jit(solution)/shard_map/ppermute | solution.py:31
  868.9 30.9 %collective-permute-start.56 = (f32[2,128]{1,0:T(2,128)S(1)}, f32[2,128]{1,0:T(2,128)S(1)}, u32[]{:S(2)}, u32[]{:S(2)}) collective-permute-start(f32[2,128]{1,0:T(2,128)S(1)} %add.375), channel_id=1, source_target_pairs={{0,1},{1,0},{2,3},{3,2},{4,5},{5,4},{6,7},{7,6},{8,9},{9,8},{10,11... | collective-permute-start | bytes 3080 | tf_op jit(solution)/shard_map/ppermute | solution.py:867
  919.1 33.8 %collective-permute-start.58 = (bf16[2,128,2048]{2,1,0:T(8,128)(2,1)}, bf16[2,128,2048]{2,1,0:T(8,128)(2,1)S(1)}, u32[]{:S(2)}, u32[]{:S(2)}) collective-permute-start(bf16[2,128,2048]{2,1,0:T(8,128)(2,1)} %add_convert_fusion.3), channel_id=1, source_target_pairs={{0,2},{1,3},{2,4},{3,5},{4,6},{5,7},{6,0},{7,1},{8,10},{9,11},{10,... | collective-permute-start | bytes 3145736 | tf_op jit(solution)/shard_map/ppermute | solution.py:31
  919.1 33.8 %collective-permute-start.57 = (bf16[2,128,2048]{2,1,0:T(8,128)(2,1)}, bf16[2,128,2048]{2,1,0:T(8,128)(2,1)S(1)}, u32[]{:S(2)}, u32[]{:S(2)}) collective-permute-start(bf16[2,128,2048]{2,1,0:T(8,128)(2,1)} %after.144), channel_id=1, source_target_pairs={{0,1},{1,0},{2,3},{3,2},{4,5},{5,4},{6,7},{7,6},{8,9},{9,8},{10,11... | collective-permute-start | bytes 3145736 | tf_op jit(solution)/shard_map/ppermute | solution.py:31
  926.8 26.1 %collective-permute-start.59 = (f32[2,128]{1,0:T(2,128)S(1)}, f32[2,128]{1,0:T(2,128)S(1)}, u32[]{:S(2)}, u32[]{:S(2)}) collective-permute-start(f32[2,128]{1,0:T(2,128)S(1)} %add.378), channel_id=1, source_target_pairs={{0,2},{1,3},{2,0},{3,1},{4,6},{5,7},{6,4},{7,5},{8,10},{9,11},{10,... | collective-permute-start | bytes 3080 | tf_op jit(solution)/shard_map/ppermute | solution.py:867
  (87 other events, 631.0 us)
Sparse Core Ops, SparseCore 0:
  12.1 34.1 all-gather.5
  47.9 58.2 all-gather.7
  107.8 105.9 all-gather.11
  215.2 105.9 all-gather.9
  322.5 105.9 all-gather.13
  510.7 72.4 reduce-scatter.4
  587.4 70.7 reduce-scatter.6
  660.8 126.0 reduce-scatter.8
  789.7 134.4 reduce-scatter.10

commit v10 on v9

--- a/solution.py
+++ b/solution.py
@@ -847,7 +847,6 @@
 
     part_h_one = [v.reshape(micro, rows, D) for v in part_h_one]
     part_h_one[inner + one] = after(part_h_one[inner + one], total)
-    mixed[3 * inner + one] = after(mixed[3 * inner + one], total)
     gains = jnp.pad(jnp.stack([grad_gain_one, grad_gain_two], axis=1), ((0, 0), (0, HD - 2)))
     whole = proj_grads(
         h_one,
@@ -880,8 +879,6 @@
     whole = [after(v, grad_one) for v in whole]
     owned = ring_scatter(whole, "fsdp").astype(bf16)
 
-    mixed[one] = after(mixed[one], grad_one)
-    part_h_one[2 * inner + one] = after(part_h_one[2 * inner + one], grad_one)
     total = ahead(add(row_sum(three, mixed, 3, "seq"), total).astype(bf16), "seq")
     grad_total = ahead(row_sum(grad_one, part_h_one, 1, "seq"), "seq")
     total, grad_total, grad_two, zero, owned = together(

time: 992 us -> 984 us (level)
    unnamed x172 -> x168, local copies, waits for them, and re-layouts: 42.1 us -> 42.1 us
  transfers between devices with their start and end apart: 73 -> 73, of which waited for: 33 -> 32; matrix products, arithmetic and copies ran while one was open for 18% -> 18% of each run, Pallas kernels for 33% -> 33%
where the time goes in v10:
time: 984 us; the launch traced here: 973 us
  Pallas kernels  363 us (37%)
  waiting for transfers between devices  277 us (28%)
  local copies, waits for them, and re-layouts  97.8 us (10%)
  other arithmetic  96.5 us (10%)
  starting transfers between devices  74.3 us (8%)
  blocking collectives  28.1 us (3%)
  matrix products  20.8 us (2%)
  between operations  15.5 us (2%)
    pallas_call x13, Pallas kernels, call(): pl.pallas_call(run, grid=grid, in_specs=[spec for _, spec in ins] + [pl.B...  293 us
    ppermute x56, waiting for transfers between devices, shift(): return lax.ppermute(value, axis, pairs)  245 us
    ppermute x56, starting transfers between devices, shift(): return lax.ppermute(value, axis, pairs)  52.2 us
    unnamed x168, local copies, waits for them, and re-layouts  42.1 us
    pallas_call x1, Pallas kernels, attend_back(): pl.pallas_call(lambda *refs: attend_back_kernel(tile, *refs[:7], *refs[-2...  33.1 us
    all_to_all x1, blocking collectives, body(): lax.all_to_all(o_heads, 'seq', split_axis=0, concat_axis=0, tiled=True)  28.1 us
    ppermute x5, waiting for transfers between devices, exchange(): return lax.ppermute(head, axis, pairs)  24.3 us
    pallas_call x1, Pallas kernels, proj_grads(): pl.pallas_call(run, grid_spec=pltpu.PrefetchScalarGridSpec(num_scalar_pre...  20.4 us
  transfers between devices with their start and end apart: 73, of which 32 were waited for; matrix products, arithmetic and copies ran while one was open for 18% of the time, Pallas kernels for 33%

profile of v10, /device:TPU:0, one launch (start us, length us, event | category | flops | bytes accessed | tf_op | source)
XLA Modules:
  0.0 972.9 jit_solution(14961912311426018724)
XLA Ops:
  17.6 3.0 collective-permute-start.1
  22.1 25.0 %collective-permute-done.1 = bf16[2,128,2176]{2,1,0:T(8,128)(2,1)S(1)} collective-permute-done((bf16[2,128,2176]{2,1,0:T(8,128)(2,1)S(1)}, bf16[2,128,2176]{2,1,0:T(8,128)(2,1)S(1)}, u32[]{:S(2)}, u32[]{:S(2)}) %collective-permute-start.1) | collective-permute-done | bytes 1114144 | tf_op jit(solution)/shard_map/ppermute | solution.py:31
  53.4 3.1 fusion.27
  58.9 15.9 %collective-permute-done.3 = bf16[2,128,2176]{2,1,0:T(8,128)(2,1)} collective-permute-done((bf16[2,128,2176]{2,1,0:T(8,128)(2,1)S(1)}, bf16[2,128,2176]{2,1,0:T(8,128)(2,1)}, u32[]{:S(2)}, u32[]{:S(2)}) %collective-permute-start.3) | collective-permute-done | bytes 1114144 | tf_op jit(solution)/shard_map/ppermute | solution.py:31
  82.6 19.8 %collective-permute-done.5 = bf16[2,128,2176]{2,1,0:T(8,128)(2,1)S(1)} collective-permute-done((bf16[2,128,2176]{2,1,0:T(8,128)(2,1)}, bf16[2,128,2176]{2,1,0:T(8,128)(2,1)S(1)}, u32[]{:S(2)}, u32[]{:S(2)}) %collective-permute-start.5) | collective-permute-done | bytes 1114144 | tf_op jit(solution)/shard_map/ppermute | solution.py:31
  105.9 8.1 collective-permute-done.6
  118.5 6.5 fusion
  126.9 5.3 fusion.2
  132.2 8.0 fusion.4.refs_0_.refs_1_
  148.0 16.5 %attend.1 = bf16[8,2,128,256]{3,2,1,0:T(8,128)(2,1)S(1)} custom-call(bf16[8,2,128,768]{3,2,1,0:T(8,128)(2,1)S(1)} %copy-done.2, f32[1024,128]{1,0:T(8,128)S(1)} %copy-done.8, f32[1024,128]{1,0:T(8,128)S(1)} %copy-done.6, s32[2,1,1024]{2,1,0:T(1,128)S(1)} %bitcast.193, s32[2,1024,1]{2,1,0:T(8,128)S(1)} %copy-done.3, f32[2,128]{1,0:T(2,128)S(1)} %copy-done.14), custom_call_target="tpu_custom_call" | custom-call | flops 1 | bytes 1 | tf_op jit(solution)/shard_map/attend/pallas_call | solution.py:282
  165.5 2.8 gather_fusion.1
  168.3 28.1 %all_to_all.20 = bf16[8,2,128,256]{3,2,1,0:T(8,128)(2,1)S(1)} all-to-all(bf16[8,2,128,256]{3,2,1,0:T(8,128)(2,1)} %after.77), channel_id=1, replica_groups=mesh['fsdp'=4,'seq'=8] {'seq'}, dimensions={0} | all-to-all | bytes 2097152 | tf_op jit(solution)/shard_map/all_to_all | solution.py:701
  198.3 6.5 multiply_reduce_fusion.3
  208.4 20.9 %collective-permute-done.12.refs_0_ = bf16[2,128,2048]{2,1,0:T(8,128)(2,1)} collective-permute-done((bf16[2,128,2048]{2,1,0:T(8,128)(2,1)S(1)}, bf16[2,128,2048]{2,1,0:T(8,128)(2,1)}, u32[]{:S(2)}, u32[]{:S(2)}) %collective-permute-start.12) | collective-permute-done | bytes 1048608 | tf_op jit(solution)/shard_map/ppermute | solution.py:31
  229.3 2.7 collective-permute-done.13.refs_1_.refs_0_
  233.2 20.4 %collective-permute-done.14.refs_0_ = bf16[2,128,2048]{2,1,0:T(8,128)(2,1)} collective-permute-done((bf16[2,128,2048]{2,1,0:T(8,128)(2,1)}, bf16[2,128,2048]{2,1,0:T(8,128)(2,1)}, u32[]{:S(2)}, u32[]{:S(2)}) %collective-permute-start.14) | collective-permute-done | bytes 1048608 | tf_op jit(solution)/shard_map/ppermute | solution.py:31
  253.7 3.0 collective-permute-done.15.refs_1_.refs_0_
  257.2 20.1 %collective-permute-done.16.refs_0_ = bf16[2,128,2048]{2,1,0:T(8,128)(2,1)} collective-permute-done((bf16[2,128,2048]{2,1,0:T(8,128)(2,1)}, bf16[2,128,2048]{2,1,0:T(8,128)(2,1)}, u32[]{:S(2)}, u32[]{:S(2)}) %collective-permute-start.16) | collective-permute-done | bytes 1048608 | tf_op jit(solution)/shard_map/ppermute | solution.py:31
  283.1 8.8 collective-permute-done.18.refs_0_
  291.9 4.7 collective-permute-done.19.refs_1_.refs_0_
  296.6 16.5 %collective-permute-done.20.refs_0_ = bf16[2,128,2048]{2,1,0:T(8,128)(2,1)} collective-permute-done((bf16[2,128,2048]{2,1,0:T(8,128)(2,1)}, bf16[2,128,2048]{2,1,0:T(8,128)(2,1)}, u32[]{:S(2)}, u32[]{:S(2)}) %collective-permute-start.20) | collective-permute-done | bytes 1048608 | tf_op jit(solution)/shard_map/ppermute | solution.py:31
  313.1 4.9 collective-permute-done.21.refs_1_.refs_0_
  328.6 6.3 collective-permute-done.22.refs_1_.refs_0_
  340.4 3.3 slice_add_fusion
  346.7 34.2 %dispatch.3 = (bf16[4,2,384,2048]{3,2,1,0:T(8,128)(2,1)}, f32[4,2,384,1024]{3,2,1,0:T(8,128)}) custom-call(bf16[256,2048]{1,0:T(8,128)(2,1)} %bitcast.206, bf16[256,2048]{1,0:T(8,128)(2,1)} %bitcast.209, bf16[256,2048]{1,0:T(8,128)(2,1)} %bitcast.208, bf16[256,2048]{1,0:T(8,128)(2,1)} %bitcast.37.refs_3_, bf16[256,2048]{1,0:T(8,128)(2,1)} %bitcast.38.refs_4_, ...), custom_call_target="tpu_custom_call" | custom-call | flops 1 | bytes 1 | tf_op jit(solution)/shard_map/dispatch/pallas_call | solution.py:428
  381.8 19.8 %dispatch.4 = (bf16[4,2,384,2048]{3,2,1,0:T(8,128)(2,1)}, f32[4,2,384,1024]{3,2,1,0:T(8,128)}) custom-call(bf16[256,2048]{1,0:T(8,128)(2,1)} %copy-done.42, bf16[256,2048]{1,0:T(8,128)(2,1)} %bitcast.18.refs_1_, bf16[256,2048]{1,0:T(8,128)(2,1)} %bitcast.19.refs_2_, bf16[256,2048]{1,0:T(8,128)(2,1)} %bitcast.20.refs_3_, bf16[256,2048]{1,0:T(8,128)(2,1)} %bitcast.21.refs_4_, ...), custom_call_target="tpu_custom_call" | custom-call | flops 1 | bytes 1 | tf_op jit(solution)/shard_map/dispatch/pallas_call | solution.py:428
  407.7 19.6 %dispatch.5 = (bf16[4,2,384,2048]{3,2,1,0:T(8,128)(2,1)}, f32[4,2,384,1024]{3,2,1,0:T(8,128)}) custom-call(bf16[256,2048]{1,0:T(8,128)(2,1)} %copy-done.42, bf16[256,2048]{1,0:T(8,128)(2,1)} %bitcast.18.refs_1_, bf16[256,2048]{1,0:T(8,128)(2,1)} %bitcast.19.refs_2_, ...), custom_call_target="tpu_custom_call", output_to_operand_aliasing={{0}: (12, {}), {1}: (13, {})} | custom-call | flops 1 | bytes 1 | tf_op jit(solution)/shard_map/dispatch/pallas_call | solution.py:428
  432.8 32.2 %activate.1 = (bf16[4,2,384,1024]{3,2,1,0:T(8,128)(2,1)}, bf16[4,2,384,1024]{3,2,1,0:T(8,128)(2,1)}, bf16[4,2,384,1024]{3,2,1,0:T(8,128)(2,1)}) custom-call(bf16[4,2,384,2048]{3,2,1,0:T(8,128)(2,1)} %get-tuple-element.55.refs_0_.refs_1_, f32[4,2,384,1024]{3,2,1,0:T(8,128)} %get-tuple-element.56.refs_1_, f32[4,2,384,1024]{3,2,1,0:T(8,128)} %get-tuple-element.57.refs_2_, ...), custom_call_target="tpu_custom_call" | custom-call | flops 1 | bytes 1 | tf_op jit(solution)/shard_map/activate/pallas_call | solution.py:428
  469.9 27.8 %combine.4 = (bf16[256,2048]{1,0:T(8,128)(2,1)}, bf16[256,2048]{1,0:T(8,128)(2,1)}, bf16[256,2048]{1,0:T(8,128)(2,1)}, bf16[256,2048]{1,0:T(8,128)(2,1)}) custom-call(bf16[4,2,384,1024]{3,2,1,0:T(8,128)(2,1)} %get-tuple-element.59.refs_0_.refs_1_, bf16[4,2,384,1024]{3,2,1,0:T(8,128)(2,1)} %get-tuple-element.60.refs_1_, ...), custom_call_target="tpu_custom_call" | custom-call | flops 1 | bytes 1 | tf_op jit(solution)/shard_map/combine/pallas_call | solution.py:428
  497.6 12.9 %bank_grad.4.refs_5_ = bf16[2,2048,1024]{2,1,0:T(8,128)(2,1)} custom-call(bf16[4,2,384,2048]{3,2,1,0:T(8,128)(2,1)} %get-tuple-element.52.refs_1_.refs_14_.refs_16_.refs_0_, bf16[4,2,384,1024]{3,2,1,0:T(8,128)(2,1)} %get-tuple-element.58.refs_1_.refs_0_, bf16[256,2048]{1,0:T(8,128)(2,1)} %get-tuple-element.61.refs_2_), custom_call_target="tpu_custom_call" | custom-call | flops 1 | bytes 1 | tf_op jit(solution)/shard_map/bank_grad/pallas_call | solution.py:428
  512.8 20.0 %combine.5 = (bf16[256,2048]{1,0:T(8,128)(2,1)}, bf16[256,2048]{1,0:T(8,128)(2,1)}, bf16[256,2048]{1,0:T(8,128)(2,1)}, bf16[256,2048]{1,0:T(8,128)(2,1)}) custom-call(bf16[4,2,384,1024]{3,2,1,0:T(8,128)(2,1)} %get-tuple-element.58.refs_1_.refs_0_, bf16[4,2048,1024]{2,1,0:T(8,128)(2,1)} %all-gather.12.cloned.1.call-done.refs_11_.refs_1_, ...), custom_call_target="tpu_custom_call" | custom-call | flops 1 | bytes 1 | tf_op jit(solution)/shard_map/combine/pallas_call | solution.py:428
  532.9 28.4 %combine.6 = (bf16[256,2048]{1,0:T(8,128)(2,1)}, bf16[256,2048]{1,0:T(8,128)(2,1)}, bf16[256,2048]{1,0:T(8,128)(2,1)}, bf16[256,2048]{1,0:T(8,128)(2,1)}) custom-call(bf16[4,2,384,1024]{3,2,1,0:T(8,128)(2,1)} %get-tuple-element.59.refs_0_.refs_1_, bf16[4,2,384,1024]{3,2,1,0:T(8,128)(2,1)} %get-tuple-element.60.refs_1_, ...), custom_call_target="tpu_custom_call" | custom-call | flops 1 | bytes 1 | tf_op jit(solution)/shard_map/combine/pallas_call | solution.py:428
  563.2 2.9 fusion.16
  567.2 12.9 %bank_grad.5.refs_1_.refs_0_ = bf16[2,2048,1024]{2,1,0:T(8,128)(2,1)} custom-call(bf16[4,2,384,2048]{3,2,1,0:T(8,128)(2,1)} %get-tuple-element.52.refs_1_.refs_14_.refs_16_.refs_0_, bf16[4,2,384,1024]{3,2,1,0:T(8,128)(2,1)} %get-tuple-element.58.refs_1_.refs_0_, bf16[2,128,2048]{2,1,0:T(8,128)(2,1)} %after.100.refs_2_, ...), custom_call_target="tpu_custom_call" | custom-call | flops 1 | bytes 1 | tf_op jit(solution)/shard_map/bank_grad/pallas_call | solution.py:428
  581.4 5.9 collective-permute-done.36.refs_2_.refs_0_
  590.9 21.5 %combine.7 = (bf16[256,2048]{1,0:T(8,128)(2,1)}, bf16[256,2048]{1,0:T(8,128)(2,1)}, bf16[256,2048]{1,0:T(8,128)(2,1)}, bf16[256,2048]{1,0:T(8,128)(2,1)}) custom-call(bf16[4,2,384,1024]{3,2,1,0:T(8,128)(2,1)} %get-tuple-element.58.refs_1_.refs_0_, bf16[4,2048,1024]{2,1,0:T(8,128)(2,1)} %all-gather.12.cloned.1.call-done.refs_11_.refs_1_, ...), custom_call_target="tpu_custom_call" | custom-call | flops 1 | bytes 1 | tf_op jit(solution)/shard_map/combine/pallas_call | solution.py:428
  617.2 24.1 %bank_grad.6.refs_1_.refs_0_ = bf16[4,2048,1024]{2,1,0:T(8,128)(2,1)} custom-call(bf16[4,2,384,2048]{3,2,1,0:T(8,128)(2,1)} %get-tuple-element.55.refs_0_.refs_1_, bf16[4,2,384,1024]{3,2,1,0:T(8,128)(2,1)} %get-tuple-element.59.refs_0_.refs_1_, bf16[2,128,2048]{2,1,0:T(8,128)(2,1)} %after.104.refs_2_, bf16[2,128,2048]{2,1,0:T(8,128)(2,1)} %after.105.refs_3_), custom_call_target="tpu_custom_call" | custom-call | flops 1 | bytes 1 | tf_op jit(solution)/shard_map/bank_grad/pallas_call | solution.py:428
  646.7 6.1 convolution_convert_fusion.refs_2_
  654.4 6.1 all-to-all-start.1
  660.5 26.8 %bank_grad.7.refs_1_.refs_0_ = bf16[4,2048,1024]{2,1,0:T(8,128)(2,1)} custom-call(bf16[4,2,384,2048]{3,2,1,0:T(8,128)(2,1)} %get-tuple-element.55.refs_0_.refs_1_, bf16[4,2,384,1024]{3,2,1,0:T(8,128)(2,1)} %get-tuple-element.60.refs_1_, bf16[256,2048]{1,0:T(8,128)(2,1)} %copy-done.52), custom_call_target="tpu_custom_call" | custom-call | flops 1 | bytes 1 | tf_op jit(solution)/shard_map/bank_grad/pallas_call | solution.py:428
  690.0 6.0 all-to-all-start.2
  696.1 2.9 fusion.12
  703.9 2.9 gather_fusion.2
  712.1 33.1 %attend_back.1 = (bf16[8,2,128,768]{3,2,1,0:T(8,128)(2,1)S(1)}, f32[4,2,128]{2,1,0:T(2,128)S(1)}) custom-call(bf16[8,2,128,768]{3,2,1,0:T(8,128)(2,1)S(1)} %copy-done.2, bf16[8,2,128,256]{3,2,1,0:T(8,128)(2,1)S(1)} %copy-done.10, f32[1024,128]{1,0:T(8,128)S(1)} %copy-done.9, f32[1024,128]{1,0:T(8,128)S(1)} %copy-done.7, s32[2,1,1024]{2,1,0:T(1,128)S(1)} %bitcast.194, ...), custom_call_target="tpu_custom_call" | custom-call | flops 1 | bytes 1 | tf_op jit(solution)/shard_map/attend_back/pallas_call | solution.py:299
  747.4 12.4 %part_grads.1 = (bf16[256,2048]{1,0:T(8,128)(2,1)}, bf16[256,2048]{1,0:T(8,128)(2,1)}, bf16[256,2048]{1,0:T(8,128)(2,1)}, bf16[256,2048]{1,0:T(8,128)(2,1)}, bf1...) custom-call(bf16[2048,768]{1,0:T(8,128)(2,1)} %bitcast.190, ...), custom_call_target="tpu_custom_call" | custom-call | flops 1 | bytes 1 | tf_op jit(solution)/shard_map/part_grads/pallas_call | solution.py:428
  761.4 3.1 add_convert_fusion.6
  770.4 20.4 %proj_grads.1 = (bf16[512,1152]{1,0:T(8,128)(2,1)}, bf16[512,1152]{1,0:T(8,128)(2,1)}, bf16[512,1152]{1,0:T(8,128)(2,1)}, bf16[512,1152]{1,0:T(8,128)(2,1)}) custom-call(s32[4]{0:T(128)} %fusion.41.refs_0_, s32[8]{0:T(128)} %get-tuple-element.101.refs_1_, bf16[2048,2048]{1,0:T(8,128)(2,1)} %bitcast.202, bf16[2048,768]{1,0:T(8,128)(2,1)} %bitcast.191, ...), custom_call_target="tpu_custom_call" | custom-call | flops 1 | bytes 1 | tf_op jit(solution)/shard_map/proj_grads/pallas_call | solution.py:389
  802.4 3.0 add_convert_fusion.5
  805.8 23.4 %collective-permute-done.53.refs_1_.refs_0_ = bf16[512,1152]{1,0:T(8,128)(2,1)} collective-permute-done((bf16[512,1152]{1,0:T(8,128)(2,1)}, bf16[512,1152]{1,0:T(8,128)(2,1)}, u32[]{:S(2)}, u32[]{:S(2)}) %collective-permute-start.53) | collective-permute-done | bytes 1179680 | tf_op jit(solution)/shard_map/ppermute | solution.py:31
  830.5 3.1 add_convert_fusion.refs_4_.refs_0_
  833.6 6.9 collective-permute-done.50.refs_2_.refs_0_
  840.5 9.7 %collective-permute-done.48.refs_0_ = bf16[2,128,2048]{2,1,0:T(8,128)(2,1)} collective-permute-done((bf16[2,128,2048]{2,1,0:T(8,128)(2,1)}, bf16[2,128,2048]{2,1,0:T(8,128)(2,1)}, u32[]{:S(2)}, u32[]{:S(2)}) %collective-permute-start.48) | collective-permute-done | bytes 1048608 | tf_op jit(solution)/shard_map/ppermute | solution.py:31
  850.3 3.7 all-to-all-start.3
  854.1 2.7 add_convert_fusion.4
  861.0 6.3 maximum_convert_fusion.refs_1_
  867.4 23.7 %collective-permute-done.56.refs_3_.refs_0_ = f32[2,128]{1,0:T(2,128)S(1)} collective-permute-done((f32[2,128]{1,0:T(2,128)S(1)}, f32[2,128]{1,0:T(2,128)S(1)}, u32[]{:S(2)}, u32[]{:S(2)}) %collective-permute-start.56) | collective-permute-done | bytes 1056 | tf_op jit(solution)/shard_map/ppermute | solution.py:866
  891.0 7.9 collective-permute-done.54.refs_0_
  899.0 5.4 all-to-all-done.3.refs_4_.refs_0_
  911.8 3.5 convert_add_fusion.14
  920.5 3.7 reshape.579
  926.2 5.4 fusion.63
  937.4 6.6 convert_element_type.450.refs_1_
  953.7 4.8 fusion.19
  959.1 6.8 convert_element_type.465
  (466 shorter events, 188.1 us)
Async XLA Ops:
  7.2 117.8 %all-gather.6.cloned.1.call-start = ((), (), s32[]{:S(2)}) async-start(), calls=%async_computation.8 | async-start | bytes 4587520 | tf_op jit(solution)/shard_map/all_gather | solution.py:648
  12.0 186.3 %all-gather.8.cloned.1.call-start = ((), (), s32[]{:S(2)}) async-start(), calls=%async_computation.9 | async-start | bytes 10485760 | tf_op jit(solution)/shard_map/all_gather | solution.py:648
  12.7 334.0 %all-gather.12.cloned.1.call-start = ((), (), s32[]{:S(2)}) async-start(), calls=%async_computation.11 | async-start | bytes 20971520 | tf_op jit(solution)/shard_map/all_gather | solution.py:648
  13.5 368.3 %all-gather.10.cloned.1.call-start = ((), (), s32[]{:S(2)}) async-start(), calls=%async_computation.10 | async-start | bytes 20971520 | tf_op jit(solution)/shard_map/all_gather | solution.py:648
  14.1 418.7 %all-gather.14.cloned.1.call-start = ((), (), s32[]{:S(2)}) async-start(), calls=%async_computation.12 | async-start | bytes 20971520 | tf_op jit(solution)/shard_map/all_gather | solution.py:648
  14.7 846.3 %reduce-scatter.5.cloned.1.call-start = ((), (), s32[]{:S(2)}) async-start(), calls=%async_computation.13 | async-start | bytes 10485760 | tf_op jit(solution)/shard_map/reduce_scatter | solution.py:811
  17.6 29.6 %collective-permute-start.1 = (bf16[2,128,2176]{2,1,0:T(8,128)(2,1)S(1)}, bf16[2,128,2176]{2,1,0:T(8,128)(2,1)S(1)}, u32[]{:S(2)}, u32[]{:S(2)}) collective-permute-start(bf16[2,128,2176]{2,1,0:T(8,128)(2,1)S(1)} %get-tuple-element.109), channel_id=1, source_target_pairs={{0,2},{1,3},{2,4},{3,5},{4,6},{5,7},{6,0},{7,1},{8,10},{9,11},{10,... | collective-permute-start | bytes 3342344 | tf_op jit(solution)/shard_map/ppermute | solution.py:31
  20.6 35.9 %collective-permute-start = (bf16[2,128,2176]{2,1,0:T(8,128)(2,1)S(1)}, bf16[2,128,2176]{2,1,0:T(8,128)(2,1)}, u32[]{:S(2)}, u32[]{:S(2)}) collective-permute-start(bf16[2,128,2176]{2,1,0:T(8,128)(2,1)S(1)} %get-tuple-element.109), channel_id=1, source_target_pairs={{0,1},{1,0},{2,3},{3,2},{4,5},{5,4},{6,7},{7,6},{8,9},{9,8},{10,11... | collective-permute-start | bytes 3342344 | tf_op jit(solution)/shard_map/ppermute | solution.py:31
  47.2 27.7 %collective-permute-start.3 = (bf16[2,128,2176]{2,1,0:T(8,128)(2,1)S(1)}, bf16[2,128,2176]{2,1,0:T(8,128)(2,1)}, u32[]{:S(2)}, u32[]{:S(2)}) collective-permute-start(bf16[2,128,2176]{2,1,0:T(8,128)(2,1)S(1)} %collective-permute-done.1), channel_id=1, source_target_pairs={{0,2},{1,3},{2,4},{3,5},{4,6},{5,7},{6,0},{7,1},{8,10},{9,11},{10,... | collective-permute-start | bytes 3342344 | tf_op jit(solution)/shard_map/ppermute | solution.py:31
  51.9 27.3 %collective-permute-start.2 = (bf16[2,128,2176]{2,1,0:T(8,128)(2,1)S(1)}, bf16[2,128,2176]{2,1,0:T(8,128)(2,1)S(1)}, u32[]{:S(2)}, u32[]{:S(2)}) collective-permute-start(bf16[2,128,2176]{2,1,0:T(8,128)(2,1)S(1)} %collective-permute-done.1), channel_id=1, source_target_pairs={{0,1},{1,0},{2,3},{3,2},{4,5},{5,4},{6,7},{7,6},{8,9},{9,8},{10,11... | collective-permute-start | bytes 3342344 | tf_op jit(solution)/shard_map/ppermute | solution.py:31
  74.8 28.7 %collective-permute-start.4 = (bf16[2,128,2176]{2,1,0:T(8,128)(2,1)}, bf16[2,128,2176]{2,1,0:T(8,128)(2,1)S(1)}, u32[]{:S(2)}, u32[]{:S(2)}) collective-permute-start(bf16[2,128,2176]{2,1,0:T(8,128)(2,1)} %collective-permute-done.3), channel_id=1, source_target_pairs={{0,1},{1,0},{2,3},{3,2},{4,5},{5,4},{6,7},{7,6},{8,9},{9,8},{10,11... | collective-permute-start | bytes 3342344 | tf_op jit(solution)/shard_map/ppermute | solution.py:31
  76.1 26.3 %collective-permute-start.5 = (bf16[2,128,2176]{2,1,0:T(8,128)(2,1)}, bf16[2,128,2176]{2,1,0:T(8,128)(2,1)S(1)}, u32[]{:S(2)}, u32[]{:S(2)}) collective-permute-start(bf16[2,128,2176]{2,1,0:T(8,128)(2,1)} %collective-permute-done.3), channel_id=1, source_target_pairs={{0,2},{1,3},{2,4},{3,5},{4,6},{5,7},{6,0},{7,1},{8,10},{9,11},{10,... | collective-permute-start | bytes 3342344 | tf_op jit(solution)/shard_map/ppermute | solution.py:31
  117.7 23.0 %collective-permute-start.8 = (bf16[2,128,2048]{2,1,0:T(8,128)(2,1)}, bf16[2,128,2048]{2,1,0:T(8,128)(2,1)S(1)}, u32[]{:S(2)}, u32[]{:S(2)}) collective-permute-start(bf16[2,128,2048]{2,1,0:T(8,128)(2,1)} %after.72), channel_id=1, source_target_pairs={{0,2},{1,3},{2,4},{3,5},{4,6},{5,7},{6,0},{7,1},{8,10},{9,11},{10,... | collective-permute-start | bytes 3145736 | tf_op jit(solution)/shard_map/ppermute | solution.py:31
  117.7 23.0 %collective-permute-start.9 = (bf16[2,128,2048]{2,1,0:T(8,128)(2,1)}, bf16[2,128,2048]{2,1,0:T(8,128)(2,1)S(1)}, u32[]{:S(2)}, u32[]{:S(2)}) collective-permute-start(bf16[2,128,2048]{2,1,0:T(8,128)(2,1)} %after.72), channel_id=1, source_target_pairs={{0,1},{1,0},{2,3},{3,2},{4,5},{5,4},{6,7},{7,6},{8,9},{9,8},{10,11... | collective-permute-start | bytes 3145736 | tf_op jit(solution)/shard_map/ppermute | solution.py:31
  142.8 25.6 %collective-permute-start.10 = (bf16[2,128,2048]{2,1,0:T(8,128)(2,1)}, bf16[2,128,2048]{2,1,0:T(8,128)(2,1)}, u32[]{:S(2)}, u32[]{:S(2)}) collective-permute-start(bf16[2,128,2048]{2,1,0:T(8,128)(2,1)} %after.74), channel_id=1, source_target_pairs={{0,2},{1,3},{2,4},{3,5},{4,6},{5,7},{6,0},{7,1},{8,10},{9,11},{10,... | collective-permute-start | bytes 3145736 | tf_op jit(solution)/shard_map/ppermute | solution.py:31
  143.4 24.9 %collective-permute-start.11 = (bf16[2,128,2048]{2,1,0:T(8,128)(2,1)}, bf16[2,128,2048]{2,1,0:T(8,128)(2,1)}, u32[]{:S(2)}, u32[]{:S(2)}) collective-permute-start(bf16[2,128,2048]{2,1,0:T(8,128)(2,1)} %after.74), channel_id=1, source_target_pairs={{0,1},{1,0},{2,3},{3,2},{4,5},{5,4},{6,7},{7,6},{8,9},{9,8},{10,11... | collective-permute-start | bytes 3145736 | tf_op jit(solution)/shard_map/ppermute | solution.py:31
  206.4 22.9 %collective-permute-start.12 = (bf16[2,128,2048]{2,1,0:T(8,128)(2,1)S(1)}, bf16[2,128,2048]{2,1,0:T(8,128)(2,1)}, u32[]{:S(2)}, u32[]{:S(2)}) collective-permute-start(bf16[2,128,2048]{2,1,0:T(8,128)(2,1)S(1)} %bitcast.204), channel_id=1, source_target_pairs={{0,1},{1,0},{2,3},{3,2},{4,5},{5,4},{6,7},{7,6},{8,9},{9,8},{10,11... | collective-permute-start | bytes 3145736 | tf_op jit(solution)/shard_map/ppermute | solution.py:31
  207.9 24.1 %collective-permute-start.13 = (bf16[2,128,2048]{2,1,0:T(8,128)(2,1)S(1)}, bf16[2,128,2048]{2,1,0:T(8,128)(2,1)}, u32[]{:S(2)}, u32[]{:S(2)}) collective-permute-start(bf16[2,128,2048]{2,1,0:T(8,128)(2,1)S(1)} %bitcast.205), channel_id=1, source_target_pairs={{0,2},{1,3},{2,4},{3,5},{4,6},{5,7},{6,0},{7,1},{8,10},{9,11},{10,... | collective-permute-start | bytes 3145736 | tf_op jit(solution)/shard_map/ppermute | solution.py:31
  232.0 21.6 %collective-permute-start.14 = (bf16[2,128,2048]{2,1,0:T(8,128)(2,1)}, bf16[2,128,2048]{2,1,0:T(8,128)(2,1)}, u32[]{:S(2)}, u32[]{:S(2)}) collective-permute-start(bf16[2,128,2048]{2,1,0:T(8,128)(2,1)} %after.79), channel_id=1, source_target_pairs={{0,1},{1,0},{2,3},{3,2},{4,5},{5,4},{6,7},{7,6},{8,9},{9,8},{10,11... | collective-permute-start | bytes 3145736 | tf_op jit(solution)/shard_map/ppermute | solution.py:31
  233.2 23.4 %collective-permute-start.15 = (bf16[2,128,2048]{2,1,0:T(8,128)(2,1)}, bf16[2,128,2048]{2,1,0:T(8,128)(2,1)}, u32[]{:S(2)}, u32[]{:S(2)}) collective-permute-start(bf16[2,128,2048]{2,1,0:T(8,128)(2,1)} %after.79), channel_id=1, source_target_pairs={{0,2},{1,3},{2,4},{3,5},{4,6},{5,7},{6,0},{7,1},{8,10},{9,11},{10,... | collective-permute-start | bytes 3145736 | tf_op jit(solution)/shard_map/ppermute | solution.py:31
  256.6 20.7 %collective-permute-start.16 = (bf16[2,128,2048]{2,1,0:T(8,128)(2,1)}, bf16[2,128,2048]{2,1,0:T(8,128)(2,1)}, u32[]{:S(2)}, u32[]{:S(2)}) collective-permute-start(bf16[2,128,2048]{2,1,0:T(8,128)(2,1)} %after.81), channel_id=1, source_target_pairs={{0,1},{1,0},{2,3},{3,2},{4,5},{5,4},{6,7},{7,6},{8,9},{9,8},{10,11... | collective-permute-start | bytes 3145736 | tf_op jit(solution)/shard_map/ppermute | solution.py:31
  257.2 21.9 %collective-permute-start.17 = (bf16[2,128,2048]{2,1,0:T(8,128)(2,1)}, bf16[2,128,2048]{2,1,0:T(8,128)(2,1)}, u32[]{:S(2)}, u32[]{:S(2)}) collective-permute-start(bf16[2,128,2048]{2,1,0:T(8,128)(2,1)} %after.81), channel_id=1, source_target_pairs={{0,2},{1,3},{2,4},{3,5},{4,6},{5,7},{6,0},{7,1},{8,10},{9,11},{10,... | collective-permute-start | bytes 3145736 | tf_op jit(solution)/shard_map/ppermute | solution.py:31
  296.6 16.5 %collective-permute-start.20 = (bf16[2,128,2048]{2,1,0:T(8,128)(2,1)}, bf16[2,128,2048]{2,1,0:T(8,128)(2,1)}, u32[]{:S(2)}, u32[]{:S(2)}) collective-permute-start(bf16[2,128,2048]{2,1,0:T(8,128)(2,1)} %after.86), channel_id=1, source_target_pairs={{0,1},{1,0},{2,3},{3,2},{4,5},{5,4},{6,7},{7,6},{8,9},{9,8},{10,11... | collective-permute-start | bytes 3145736 | tf_op jit(solution)/shard_map/ppermute | solution.py:31
  296.6 21.4 %collective-permute-start.21 = (bf16[2,128,2048]{2,1,0:T(8,128)(2,1)}, bf16[2,128,2048]{2,1,0:T(8,128)(2,1)}, u32[]{:S(2)}, u32[]{:S(2)}) collective-permute-start(bf16[2,128,2048]{2,1,0:T(8,128)(2,1)} %after.86), channel_id=1, source_target_pairs={{0,2},{1,3},{2,4},{3,5},{4,6},{5,7},{6,0},{7,1},{8,10},{9,11},{10,... | collective-permute-start | bytes 3145736 | tf_op jit(solution)/shard_map/ppermute | solution.py:31
  319.9 15.1 %collective-permute-start.22 = (bf16[1,128,2048]{2,1,0:T(8,128)(2,1)}, bf16[1,128,2048]{2,1,0:T(8,128)(2,1)}, u32[]{:S(2)}, u32[]{:S(2)}) collective-permute-start(bf16[1,128,2048]{2,1,0:T(8,128)(2,1)} %slice.114), channel_id=1, source_target_pairs={{0,2},{1,3},{2,4},{3,5},{4,6},{5,7},{6,0},{7,1},{8,10},{9,11},{10,... | collective-permute-start | bytes 1572872 | tf_op jit(solution)/shard_map/ppermute | solution.py:31
  336.9 43.9 %collective-permute-start.24 = (bf16[2048,256]{1,0:T(8,128)(2,1)}, bf16[2048,256]{1,0:T(8,128)(2,1)}, u32[]{:S(2)}, u32[]{:S(2)}) collective-permute-start(bf16[2048,256]{1,0:T(8,128)(2,1)} %after.91.refs_6_), channel_id=1, source_target_pairs={{0,1},{1,0},{2,3},{3,2},{4,5},{5,4},{6,7},{7,6},{8,9},{9,8},{10,11... | collective-permute-start | bytes 3145736 | tf_op jit(solution)/shard_map/ppermute | solution.py:31
  339.1 41.8 %collective-permute-start.25 = (bf16[2048,256]{1,0:T(8,128)(2,1)}, bf16[2048,256]{1,0:T(8,128)(2,1)}, u32[]{:S(2)}, u32[]{:S(2)}) collective-permute-start(bf16[2048,256]{1,0:T(8,128)(2,1)} %after.91.refs_6_), channel_id=1, source_target_pairs={{0,2},{1,3},{2,4},{3,5},{4,6},{5,7},{6,0},{7,1},{8,10},{9,11},{10,... | collective-permute-start | bytes 3145736 | tf_op jit(solution)/shard_map/ppermute | solution.py:31
  380.9 20.9 %collective-permute-start.26 = (bf16[2048,256]{1,0:T(8,128)(2,1)}, bf16[2048,256]{1,0:T(8,128)(2,1)}, u32[]{:S(2)}, u32[]{:S(2)}) collective-permute-start(bf16[2048,256]{1,0:T(8,128)(2,1)} %after.93.refs_13_.refs_8_), channel_id=1, source_target_pairs={{0,1},{1,0},{2,3},{3,2},{4,5},{5,4},{6,7},{7,6},{8,9},{9,8},{10,11... | collective-permute-start | bytes 3145736 | tf_op jit(solution)/shard_map/ppermute | solution.py:31
  381.1 22.5 %collective-permute-start.27 = (bf16[2048,256]{1,0:T(8,128)(2,1)}, bf16[2048,256]{1,0:T(8,128)(2,1)}, u32[]{:S(2)}, u32[]{:S(2)}) collective-permute-start(bf16[2048,256]{1,0:T(8,128)(2,1)} %after.93.refs_13_.refs_8_), channel_id=1, source_target_pairs={{0,2},{1,3},{2,4},{3,5},{4,6},{5,7},{6,0},{7,1},{8,10},{9,11},{10,... | collective-permute-start | bytes 3145736 | tf_op jit(solution)/shard_map/ppermute | solution.py:31
  403.6 23.7 %collective-permute-start.29 = (bf16[2048,256]{1,0:T(8,128)(2,1)}, bf16[2048,256]{1,0:T(8,128)(2,1)}, u32[]{:S(2)}, u32[]{:S(2)}) collective-permute-start(bf16[2048,256]{1,0:T(8,128)(2,1)} %after.95.refs_15_.refs_10_), channel_id=1, source_target_pairs={{0,1},{1,0},{2,3},{3,2},{4,5},{5,4},{6,7},{7,6},{8,9},{9,8},{10,11... | collective-permute-start | bytes 3145736 | tf_op jit(solution)/shard_map/ppermute | solution.py:31
  405.9 22.7 %collective-permute-start.28 = (bf16[2048,256]{1,0:T(8,128)(2,1)}, bf16[2048,256]{1,0:T(8,128)(2,1)}, u32[]{:S(2)}, u32[]{:S(2)}) collective-permute-start(bf16[2048,256]{1,0:T(8,128)(2,1)} %after.95.refs_15_.refs_10_), channel_id=1, source_target_pairs={{0,2},{1,3},{2,4},{3,5},{4,6},{5,7},{6,0},{7,1},{8,10},{9,11},{10,... | collective-permute-start | bytes 3145736 | tf_op jit(solution)/shard_map/ppermute | solution.py:31
  430.4 34.6 %collective-permute-start.31 = (bf16[1024,256]{1,0:T(8,128)(2,1)}, bf16[1024,256]{1,0:T(8,128)(2,1)}, u32[]{:S(2)}, u32[]{:S(2)}) collective-permute-start(bf16[1024,256]{1,0:T(8,128)(2,1)} %slice.117), channel_id=1, source_target_pairs={{0,2},{1,3},{2,4},{3,5},{4,6},{5,7},{6,0},{7,1},{8,10},{9,11},{10,... | collective-permute-start | bytes 1572872 | tf_op jit(solution)/shard_map/ppermute | solution.py:31
  432.7 32.3 %collective-permute-start.30 = (bf16[1024,256]{1,0:T(8,128)(2,1)}, bf16[1024,256]{1,0:T(8,128)(2,1)}, u32[]{:S(2)}, u32[]{:S(2)}) collective-permute-start(bf16[1024,256]{1,0:T(8,128)(2,1)} %slice.116), channel_id=1, source_target_pairs={{0,1},{1,0},{2,3},{3,2},{4,5},{5,4},{6,7},{7,6},{8,9},{9,8},{10,11... | collective-permute-start | bytes 1572872 | tf_op jit(solution)/shard_map/ppermute | solution.py:31
  510.5 350.5 %reduce-scatter.7.cloned.1.call-start = ((), (), s32[]{:S(2)}) async-start(), calls=%async_computation.14 | async-start | bytes 10485760 | tf_op jit(solution)/shard_map/reduce_scatter | solution.py:811
  510.8 52.4 %collective-permute-start.34 = (bf16[2,128,2048]{2,1,0:T(8,128)(2,1)}, bf16[2,128,2048]{2,1,0:T(8,128)(2,1)}, u32[]{:S(2)}, u32[]{:S(2)}) collective-permute-start(bf16[2,128,2048]{2,1,0:T(8,128)(2,1)} %bitcast.265), channel_id=1, source_target_pairs={{0,1},{1,0},{2,3},{3,2},{4,5},{5,4},{6,7},{7,6},{8,9},{9,8},{10,11... | collective-permute-start | bytes 3145736 | tf_op jit(solution)/shard_map/ppermute | solution.py:31
  532.7 30.4 %collective-permute-start.35 = (bf16[2,128,2048]{2,1,0:T(8,128)(2,1)}, bf16[2,128,2048]{2,1,0:T(8,128)(2,1)}, u32[]{:S(2)}, u32[]{:S(2)}) collective-permute-start(bf16[2,128,2048]{2,1,0:T(8,128)(2,1)} %bitcast.267), channel_id=1, source_target_pairs={{0,1},{1,0},{2,3},{3,2},{4,5},{5,4},{6,7},{7,6},{8,9},{9,8},{10,11... | collective-permute-start | bytes 3145736 | tf_op jit(solution)/shard_map/ppermute | solution.py:31
  561.3 20.1 %collective-permute-start.33 = (bf16[2,128,2048]{2,1,0:T(8,128)(2,1)}, bf16[2,128,2048]{2,1,0:T(8,128)(2,1)}, u32[]{:S(2)}, u32[]{:S(2)}) collective-permute-start(bf16[2,128,2048]{2,1,0:T(8,128)(2,1)} %bitcast.266), channel_id=1, source_target_pairs={{0,1},{1,0},{2,3},{3,2},{4,5},{5,4},{6,7},{7,6},{8,9},{9,8},{10,11... | collective-permute-start | bytes 3145736 | tf_op jit(solution)/shard_map/ppermute | solution.py:31
  566.1 21.2 %collective-permute-start.36 = (bf16[2,128,2048]{2,1,0:T(8,128)(2,1)}, bf16[2,128,2048]{2,1,0:T(8,128)(2,1)}, u32[]{:S(2)}, u32[]{:S(2)}) collective-permute-start(bf16[2,128,2048]{2,1,0:T(8,128)(2,1)} %fusion.16), channel_id=1, source_target_pairs={{0,2},{1,3},{2,4},{3,5},{4,6},{5,7},{6,0},{7,1},{8,10},{9,11},{10,... | collective-permute-start | bytes 3145736 | tf_op jit(solution)/shard_map/ppermute | solution.py:31
  587.3 350.1 %reduce-scatter.9.cloned.1.call-start = ((), (), s32[]{:S(2)}) async-start(), calls=%async_computation.15 | async-start | bytes 20971520 | tf_op jit(solution)/shard_map/reduce_scatter | solution.py:811
  587.3 25.1 %collective-permute-start.39 = (bf16[2,128,2048]{2,1,0:T(8,128)(2,1)}, bf16[2,128,2048]{2,1,0:T(8,128)(2,1)}, u32[]{:S(2)}, u32[]{:S(2)}) collective-permute-start(bf16[2,128,2048]{2,1,0:T(8,128)(2,1)} %bitcast.264), channel_id=1, source_target_pairs={{0,1},{1,0},{2,3},{3,2},{4,5},{5,4},{6,7},{7,6},{8,9},{9,8},{10,11... | collective-permute-start | bytes 3145736 | tf_op jit(solution)/shard_map/ppermute | solution.py:31
  590.4 22.0 %collective-permute-start.40 = (bf16[2,128,2048]{2,1,0:T(8,128)(2,1)S(1)}, bf16[2,128,2048]{2,1,0:T(8,128)(2,1)}, u32[]{:S(2)}, u32[]{:S(2)}) collective-permute-start(bf16[2,128,2048]{2,1,0:T(8,128)(2,1)S(1)} %add_convert_fusion.8), channel_id=1, source_target_pairs={{0,2},{1,3},{2,4},{3,5},{4,6},{5,7},{6,0},{7,1},{8,10},{9,11},{10,... | collective-permute-start | bytes 3145736 | tf_op jit(solution)/shard_map/ppermute | solution.py:31
  612.4 28.9 %collective-permute-start.38 = (bf16[2,128,2048]{2,1,0:T(8,128)(2,1)}, bf16[2,128,2048]{2,1,0:T(8,128)(2,1)}, u32[]{:S(2)}, u32[]{:S(2)}) collective-permute-start(bf16[2,128,2048]{2,1,0:T(8,128)(2,1)} %bitcast.263), channel_id=1, source_target_pairs={{0,1},{1,0},{2,3},{3,2},{4,5},{5,4},{6,7},{7,6},{8,9},{9,8},{10,11... | collective-permute-start | bytes 3145736 | tf_op jit(solution)/shard_map/ppermute | solution.py:31
  616.2 25.1 %collective-permute-start.41 = (bf16[2,128,2048]{2,1,0:T(8,128)(2,1)S(1)}, bf16[2,128,2048]{2,1,0:T(8,128)(2,1)}, u32[]{:S(2)}, u32[]{:S(2)}) collective-permute-start(bf16[2,128,2048]{2,1,0:T(8,128)(2,1)S(1)} %add_convert_fusion.7), channel_id=1, source_target_pairs={{0,2},{1,3},{2,4},{3,5},{4,6},{5,7},{6,0},{7,1},{8,10},{9,11},{10,... | collective-permute-start | bytes 3145736 | tf_op jit(solution)/shard_map/ppermute | solution.py:31
  654.4 32.9 %all-to-all-start.1 = ((bf16[8,2,128,256]{3,2,1,0:T(8,128)(2,1)}), bf16[8,2,128,256]{3,2,1,0:T(8,128)(2,1)}, u32[]{:S(2)}, u32[]{:S(2)}) async-start(bf16[8,2,128,256]{3,2,1,0:T(8,128)(2,1)} %bitcast.218), calls=%async_computation.1 | async-start | bytes 2097152 | tf_op jit(solution)/shard_map/all_to_all | solution.py:826
  660.4 298.7 %reduce-scatter.11.cloned.1.call-start = ((), (), s32[]{:S(2)}) async-start(), calls=%async_computation.16 | async-start | bytes 20971520 | tf_op jit(solution)/shard_map/reduce_scatter | solution.py:811
  690.0 69.8 %all-to-all-start.2 = ((bf16[8,2,128,256]{3,2,1,0:T(8,128)(2,1)}), bf16[8,2,128,256]{3,2,1,0:T(8,128)(2,1)}, u32[]{:S(2)}, u32[]{:S(2)}) async-start(bf16[8,2,128,256]{3,2,1,0:T(8,128)(2,1)} %bitcast.217), calls=%async_computation.2 | async-start | bytes 2097152 | tf_op jit(solution)/shard_map/all_to_all | solution.py:826
  699.0 60.8 %collective-permute-start.42 = (bf16[2,128,2048]{2,1,0:T(8,128)(2,1)}, bf16[2,128,2048]{2,1,0:T(8,128)(2,1)}, u32[]{:S(2)}, u32[]{:S(2)}) collective-permute-start(bf16[2,128,2048]{2,1,0:T(8,128)(2,1)} %fusion.12), channel_id=1, source_target_pairs={{0,2},{1,3},{2,4},{3,5},{4,6},{5,7},{6,0},{7,1},{8,10},{9,11},{10,... | collective-permute-start | bytes 3145736 | tf_op jit(solution)/shard_map/ppermute | solution.py:31
  701.0 58.8 %collective-permute-start.43 = (bf16[2,128,2048]{2,1,0:T(8,128)(2,1)}, bf16[2,128,2048]{2,1,0:T(8,128)(2,1)}, u32[]{:S(2)}, u32[]{:S(2)}) collective-permute-start(bf16[2,128,2048]{2,1,0:T(8,128)(2,1)} %after.111), channel_id=1, source_target_pairs={{0,1},{1,0},{2,3},{3,2},{4,5},{5,4},{6,7},{7,6},{8,9},{9,8},{10,11... | collective-permute-start | bytes 3145736 | tf_op jit(solution)/shard_map/ppermute | solution.py:31
  706.9 83.9 %collective-permute-start.37 = (bf16[2,128,2048]{2,1,0:T(8,128)(2,1)}, bf16[2,128,2048]{2,1,0:T(8,128)(2,1)}, u32[]{:S(2)}, u32[]{:S(2)}) collective-permute-start(bf16[2,128,2048]{2,1,0:T(8,128)(2,1)} %bitcast.262), channel_id=1, source_target_pairs={{0,1},{1,0},{2,3},{3,2},{4,5},{5,4},{6,7},{7,6},{8,9},{9,8},{10,11... | collective-permute-start | bytes 3145736 | tf_op jit(solution)/shard_map/ppermute | solution.py:31
  759.9 31.0 %collective-permute-start.45 = (bf16[2,128,2048]{2,1,0:T(8,128)(2,1)}, bf16[2,128,2048]{2,1,0:T(8,128)(2,1)S(1)}, u32[]{:S(2)}, u32[]{:S(2)}) collective-permute-start(bf16[2,128,2048]{2,1,0:T(8,128)(2,1)} %after.115), channel_id=1, source_target_pairs={{0,1},{1,0},{2,3},{3,2},{4,5},{5,4},{6,7},{7,6},{8,9},{9,8},{10,11... | collective-permute-start | bytes 3145736 | tf_op jit(solution)/shard_map/ppermute | solution.py:31
  764.5 26.4 %collective-permute-start.44 = (bf16[2,128,2048]{2,1,0:T(8,128)(2,1)}, bf16[2,128,2048]{2,1,0:T(8,128)(2,1)S(1)}, u32[]{:S(2)}, u32[]{:S(2)}) collective-permute-start(bf16[2,128,2048]{2,1,0:T(8,128)(2,1)} %add_convert_fusion.6), channel_id=1, source_target_pairs={{0,2},{1,3},{2,4},{3,5},{4,6},{5,7},{6,0},{7,1},{8,10},{9,11},{10,... | collective-permute-start | bytes 3145736 | tf_op jit(solution)/shard_map/ppermute | solution.py:31
  768.0 22.8 %collective-permute-start.47 = (f32[2,128]{1,0:T(2,128)S(1)}, f32[2,128]{1,0:T(2,128)S(1)}, u32[]{:S(2)}, u32[]{:S(2)}) collective-permute-start(f32[2,128]{1,0:T(2,128)S(1)} %add.362), channel_id=1, source_target_pairs={{0,16},{8,24},{16,0},{24,8},{1,17},{9,25},{17,1},{25,9},{2,18},{10... | collective-permute-start | bytes 3080 | tf_op jit(solution)/shard_map/ppermute | solution.py:866
  792.2 41.5 %collective-permute-start.32 = (bf16[2,128,2048]{2,1,0:T(8,128)(2,1)}, bf16[2,128,2048]{2,1,0:T(8,128)(2,1)S(1)}, u32[]{:S(2)}, u32[]{:S(2)}) collective-permute-start(bf16[2,128,2048]{2,1,0:T(8,128)(2,1)} %bitcast.45), channel_id=1, source_target_pairs={{0,1},{1,0},{2,3},{3,2},{4,5},{5,4},{6,7},{7,6},{8,9},{9,8},{10,11... | collective-permute-start | bytes 3145736 | tf_op jit(solution)/shard_map/ppermute | solution.py:31
  793.3 47.2 %collective-permute-start.50 = (bf16[2,128,2048]{2,1,0:T(8,128)(2,1)}, bf16[2,128,2048]{2,1,0:T(8,128)(2,1)}, u32[]{:S(2)}, u32[]{:S(2)}) collective-permute-start(bf16[2,128,2048]{2,1,0:T(8,128)(2,1)} %bitcast.74), channel_id=1, source_target_pairs={{0,1},{1,0},{2,3},{3,2},{4,5},{5,4},{6,7},{7,6},{8,9},{9,8},{10,11... | collective-permute-start | bytes 3145736 | tf_op jit(solution)/shard_map/ppermute | solution.py:31
  798.4 30.8 %collective-permute-start.53 = (bf16[512,1152]{1,0:T(8,128)(2,1)}, bf16[512,1152]{1,0:T(8,128)(2,1)}, u32[]{:S(2)}, u32[]{:S(2)}) collective-permute-start(bf16[512,1152]{1,0:T(8,128)(2,1)} %add_convert_fusion.2), channel_id=1, source_target_pairs={{0,16},{8,24},{16,0},{24,8},{1,17},{9,25},{17,1},{25,9},{2,18},{10... | collective-permute-start | bytes 3538952 | tf_op jit(solution)/shard_map/ppermute | solution.py:31
  800.9 39.6 %collective-permute-start.49 = (bf16[2,128,2048]{2,1,0:T(8,128)(2,1)}, bf16[2,128,2048]{2,1,0:T(8,128)(2,1)S(1)}, u32[]{:S(2)}, u32[]{:S(2)}) collective-permute-start(bf16[2,128,2048]{2,1,0:T(8,128)(2,1)} %fusion.9), channel_id=1, source_target_pairs={{0,2},{1,3},{2,4},{3,5},{4,6},{5,7},{6,0},{7,1},{8,10},{9,11},{10,... | collective-permute-start | bytes 3145736 | tf_op jit(solution)/shard_map/ppermute | solution.py:31
  805.4 44.9 %collective-permute-start.48 = (bf16[2,128,2048]{2,1,0:T(8,128)(2,1)}, bf16[2,128,2048]{2,1,0:T(8,128)(2,1)}, u32[]{:S(2)}, u32[]{:S(2)}) collective-permute-start(bf16[2,128,2048]{2,1,0:T(8,128)(2,1)} %add_convert_fusion.5), channel_id=1, source_target_pairs={{0,2},{1,3},{2,4},{3,5},{4,6},{5,7},{6,0},{7,1},{8,10},{9,11},{10,... | collective-permute-start | bytes 3145736 | tf_op jit(solution)/shard_map/ppermute | solution.py:31
  850.3 54.1 %all-to-all-start.3 = ((bf16[8,64,1152]{2,1,0:T(8,128)(2,1)}), bf16[8,64,1152]{2,1,0:T(8,128)(2,1)S(1)}, u32[]{:S(2)}, u32[]{:S(2)}) async-start(bf16[8,64,1152]{2,1,0:T(8,128)(2,1)} %bitcast.200), calls=%async_computation.3 | async-start | bytes 2359296 | tf_op jit(solution)/shard_map/all_to_all | solution.py:892
  856.8 42.2 %collective-permute-start.54 = (bf16[2,128,2048]{2,1,0:T(8,128)(2,1)}, bf16[2,128,2048]{2,1,0:T(8,128)(2,1)S(1)}, u32[]{:S(2)}, u32[]{:S(2)}) collective-permute-start(bf16[2,128,2048]{2,1,0:T(8,128)(2,1)} %add_convert_fusion.4), channel_id=1, source_target_pairs={{0,2},{1,3},{2,4},{3,5},{4,6},{5,7},{6,0},{7,1},{8,10},{9,11},{10,... | collective-permute-start | bytes 3145736 | tf_op jit(solution)/shard_map/ppermute | solution.py:31
  859.0 40.0 %collective-permute-start.55 = (bf16[2,128,2048]{2,1,0:T(8,128)(2,1)}, bf16[2,128,2048]{2,1,0:T(8,128)(2,1)S(1)}, u32[]{:S(2)}, u32[]{:S(2)}) collective-permute-start(bf16[2,128,2048]{2,1,0:T(8,128)(2,1)} %after.132), channel_id=1, source_target_pairs={{0,1},{1,0},{2,3},{3,2},{4,5},{5,4},{6,7},{7,6},{8,9},{9,8},{10,11... | collective-permute-start | bytes 3145736 | tf_op jit(solution)/shard_map/ppermute | solution.py:31
  860.5 30.5 %collective-permute-start.56 = (f32[2,128]{1,0:T(2,128)S(1)}, f32[2,128]{1,0:T(2,128)S(1)}, u32[]{:S(2)}, u32[]{:S(2)}) collective-permute-start(f32[2,128]{1,0:T(2,128)S(1)} %add.375), channel_id=1, source_target_pairs={{0,1},{1,0},{2,3},{3,2},{4,5},{5,4},{6,7},{7,6},{8,9},{9,8},{10,11... | collective-permute-start | bytes 3080 | tf_op jit(solution)/shard_map/ppermute | solution.py:866
  910.4 33.7 %collective-permute-start.58 = (bf16[2,128,2048]{2,1,0:T(8,128)(2,1)}, bf16[2,128,2048]{2,1,0:T(8,128)(2,1)S(1)}, u32[]{:S(2)}, u32[]{:S(2)}) collective-permute-start(bf16[2,128,2048]{2,1,0:T(8,128)(2,1)} %add_convert_fusion.3), channel_id=1, source_target_pairs={{0,2},{1,3},{2,4},{3,5},{4,6},{5,7},{6,0},{7,1},{8,10},{9,11},{10,... | collective-permute-start | bytes 3145736 | tf_op jit(solution)/shard_map/ppermute | solution.py:31
  910.4 33.7 %collective-permute-start.57 = (bf16[2,128,2048]{2,1,0:T(8,128)(2,1)}, bf16[2,128,2048]{2,1,0:T(8,128)(2,1)S(1)}, u32[]{:S(2)}, u32[]{:S(2)}) collective-permute-start(bf16[2,128,2048]{2,1,0:T(8,128)(2,1)} %after.138), channel_id=1, source_target_pairs={{0,1},{1,0},{2,3},{3,2},{4,5},{5,4},{6,7},{7,6},{8,9},{9,8},{10,11... | collective-permute-start | bytes 3145736 | tf_op jit(solution)/shard_map/ppermute | solution.py:31
  918.1 25.9 %collective-permute-start.59 = (f32[2,128]{1,0:T(2,128)S(1)}, f32[2,128]{1,0:T(2,128)S(1)}, u32[]{:S(2)}, u32[]{:S(2)}) collective-permute-start(f32[2,128]{1,0:T(2,128)S(1)} %add.378), channel_id=1, source_target_pairs={{0,2},{1,3},{2,0},{3,1},{4,6},{5,7},{6,4},{7,5},{8,10},{9,11},{10,... | collective-permute-start | bytes 3080 | tf_op jit(solution)/shard_map/ppermute | solution.py:866
  (85 other events, 620.2 us)
Sparse Core Ops, SparseCore 0:
  12.1 34.1 all-gather.5
  47.9 58.2 all-gather.7
  107.8 105.9 all-gather.11
  215.2 105.9 all-gather.9
  322.5 105.9 all-gather.13
  510.7 72.4 reduce-scatter.4
  587.4 70.8 reduce-scatter.6
  660.8 126.1 reduce-scatter.8
  789.8 127.8 reduce-scatter.10

commit v11 on v10

--- a/solution.py
+++ b/solution.py
@@ -195,6 +195,7 @@
     tile,
     qkv_ref,
     do_ref,
+    order_ref,
     cos_ref,
     sin_ref,
     seg_row_ref,
@@ -233,7 +234,7 @@
 
     queries, keys = turned(0), turned(1)
     values = qkv_ref[:, 0, :, 2 * HD : 3 * HD].reshape(group, HD)
-    grad_out = do_ref[:, 0, :, :].reshape(group, HD)
+    grad_out = jnp.concatenate([do_ref[order_ref[k], 0] for k in range(blocks)], axis=0)
     seg_row = seg_row_ref[0]
     grad_query = []
     grad_key = jnp.zeros((group, HD), f32)
@@ -291,15 +292,15 @@
     )(qkv, *tables)
 
 
-def attend_back(qkv, grad_out, tables, ties=()):
+def attend_back(qkv, grad_out, order, tables):
     ns, micro, rows, width = qkv.shape
     heads = width // (3 * HD)
     tile, wide, narrow, shared = attention_specs(ns, micro, rows, heads)
     group = ns * rows
     return pl.pallas_call(
-        lambda *refs: attend_back_kernel(tile, *refs[:7], *refs[-2:]),
+        lambda *refs: attend_back_kernel(tile, *refs),
         grid=(micro, heads),
-        in_specs=[wide, narrow] + shared + [pl.BlockSpec(memory_space=pl.ANY)] * len(ties),
+        in_specs=[wide, narrow, pl.BlockSpec(memory_space=pltpu.SMEM)] + shared,
         out_specs=[wide, pl.BlockSpec((1, 2, HD), lambda m, h: (m * heads + h, 0, 0))],
         out_shape=[
             jax.ShapeDtypeStruct((ns, micro, rows, width), bf16),
@@ -308,7 +309,7 @@
         compiler_params=pltpu.CompilerParams(vmem_limit_bytes=40 * 2**20),
         cost_estimate=little,
         name="attend_back",
-    )(qkv, grad_out, *tables, *ties)
+    )(qkv, grad_out, order, *tables)
 
 
 def part_kernel(grad_ref, w_ref, x_ref, inv_ref, *out_refs):
@@ -830,13 +831,12 @@
     whole_up = bank_grad(taken, grad_up_act, (grad_o,))
     (do_blocks,) = together((whole_up,), to_heads(grad_o))
     grad_up = bank_sum(after(whole_up, do_blocks))
-    do_heads = reorder(do_blocks, seq_order)
 
     inner = sizes("seq")[1]
     one = 1 % inner
-    total = row_sum(after(done["mixed_one"], do_blocks), mixed, 1, "seq")
+    total = after(row_sum(done["mixed_one"], mixed, 1, "seq"), do_blocks)
     mixed[2 * inner + one] = after(mixed[2 * inner + one], do_blocks)
-    grad_qkv, grad_head = attend_back(qkv, do_heads, tables)
+    grad_qkv, grad_head = attend_back(qkv, do_blocks, seq_order, tables)
     part_h_one, grad_gain_one = part_grads(grad_qkv, w_first, x_all, inv_all)
     total, two, columns = together(
         (grad_gain_one,),
@@ -881,14 +881,16 @@
 
     total = ahead(add(row_sum(three, mixed, 3, "seq"), total).astype(bf16), "seq")
     grad_total = ahead(row_sum(grad_one, part_h_one, 1, "seq"), "seq")
-    total, grad_total, grad_two, zero, owned = together(
+    total, grad_total, grad_two, zero, moved, owned = together(
         (),
         total,
         grad_total,
         row_move(part_h_one, 2, "seq"),
         row_move(mixed, 0, "seq"),
+        exchange(head),
         owned,
     )
+    head = head + moved
     owned = lax.all_to_all(
         owned.reshape(ns, share, -1), "seq", split_axis=0, concat_axis=0, tiled=True
     )
@@ -909,7 +911,7 @@
     part_h_one[one] = after(part_h_one[one], owned)
     grad_total = add(row_sum(grad_three, part_h_one, 3, "seq"), grad_total).astype(bf16)
     grad_total, zero, moved = together(
-        (grad_gate,),
+        (grad_gate, grad_up),
         ahead(grad_total, "seq"),
         row_move(part_h_one, 0, "seq"),
         exchange(head),

time: 984 us -> 981 us (level)
  local copies, waits for them, and re-layouts: 97.8 us -> 110 us
    unnamed x168 -> x258, local copies, waits for them, and re-layouts: 42.1 us -> 66.8 us
  transfers between devices with their start and end apart: 73 -> 73, of which waited for: 32 -> 28; matrix products, arithmetic and copies ran while one was open for 18% -> 15% of each run, Pallas kernels for 33% -> 33%
where the time goes in v11:
time: 981 us; the launch traced here: 970 us
  Pallas kernels  363 us (37%)
  waiting for transfers between devices  273 us (28%)
  local copies, waits for them, and re-layouts  110 us (11%)
  other arithmetic  88.6 us (9%)
  starting transfers between devices  72.3 us (7%)
  blocking collectives  27.7 us (3%)
  matrix products  20.2 us (2%)
  between operations  15.6 us (2%)
    pallas_call x13, Pallas kernels, call(): pl.pallas_call(run, grid=grid, in_specs=[spec for _, spec in ins] + [pl.B...  293 us
    ppermute x56, waiting for transfers between devices, shift(): return lax.ppermute(value, axis, pairs)  237 us
    unnamed x258, local copies, waits for them, and re-layouts  66.8 us
    ppermute x56, starting transfers between devices, shift(): return lax.ppermute(value, axis, pairs)  50.6 us
    pallas_call x1, Pallas kernels, attend_back(): pl.pallas_call(lambda *refs: attend_back_kernel(tile, *refs), grid=(micro...  33.6 us
    ppermute x5, waiting for transfers between devices, exchange(): return lax.ppermute(head, axis, pairs)  27.8 us
    all_to_all x1, blocking collectives, body(): lax.all_to_all(o_heads, 'seq', split_axis=0, concat_axis=0, tiled=True)  27.7 us
    pallas_call x1, Pallas kernels, proj_grads(): pl.pallas_call(run, grid_spec=pltpu.PrefetchScalarGridSpec(num_scalar_pre...  20.6 us
  transfers between devices with their start and end apart: 73, of which 28 were waited for; matrix products, arithmetic and copies ran while one was open for 15% of the time, Pallas kernels for 33%

profile of v11, /device:TPU:0, one launch (start us, length us, event | category | flops | bytes accessed | tf_op | source)
XLA Modules:
  0.0 970.2 jit_solution(5664551652210271813)
XLA Ops:
  17.9 3.0 collective-permute-start.1
  22.5 25.3 %collective-permute-done.1 = bf16[2,128,2176]{2,1,0:T(8,128)(2,1)S(1)} collective-permute-done((bf16[2,128,2176]{2,1,0:T(8,128)(2,1)}, bf16[2,128,2176]{2,1,0:T(8,128)(2,1)S(1)}, u32[]{:S(2)}, u32[]{:S(2)}) %collective-permute-start.1) | collective-permute-done | bytes 1114144 | tf_op jit(solution)/shard_map/ppermute | solution.py:31
  53.4 3.1 fusion.27
  59.0 16.4 %collective-permute-done.3 = bf16[2,128,2176]{2,1,0:T(8,128)(2,1)} collective-permute-done((bf16[2,128,2176]{2,1,0:T(8,128)(2,1)S(1)}, bf16[2,128,2176]{2,1,0:T(8,128)(2,1)}, u32[]{:S(2)}, u32[]{:S(2)}) %collective-permute-start.3) | collective-permute-done | bytes 1114144 | tf_op jit(solution)/shard_map/ppermute | solution.py:31
  82.1 20.8 %collective-permute-done.5 = bf16[2,128,2176]{2,1,0:T(8,128)(2,1)S(1)} collective-permute-done((bf16[2,128,2176]{2,1,0:T(8,128)(2,1)}, bf16[2,128,2176]{2,1,0:T(8,128)(2,1)S(1)}, u32[]{:S(2)}, u32[]{:S(2)}) %collective-permute-start.5) | collective-permute-done | bytes 1114144 | tf_op jit(solution)/shard_map/ppermute | solution.py:31
  106.4 8.1 collective-permute-done.6
  119.0 6.7 fusion
  127.6 5.3 fusion.2
  132.9 8.0 fusion.4.refs_0_.refs_1_
  148.5 16.5 %attend.1 = bf16[8,2,128,256]{3,2,1,0:T(8,128)(2,1)S(1)} custom-call(bf16[8,2,128,768]{3,2,1,0:T(8,128)(2,1)S(1)} %copy-done.4, f32[1024,128]{1,0:T(8,128)S(1)} %copy-done.11, f32[1024,128]{1,0:T(8,128)S(1)} %copy-done.9, s32[2,1,1024]{2,1,0:T(1,128)S(1)} %bitcast.193, s32[2,1024,1]{2,1,0:T(8,128)S(1)} %copy-done.6, f32[2,128]{1,0:T(2,128)S(1)} %copy-done.16), custom_call_target="tpu_custom_call" | custom-call | flops 1 | bytes 1 | tf_op jit(solution)/shard_map/attend/pallas_call | solution.py:283
  166.0 2.8 gather_fusion.1
  168.8 27.7 %all_to_all.20 = bf16[8,2,128,256]{3,2,1,0:T(8,128)(2,1)S(1)} all-to-all(bf16[8,2,128,256]{3,2,1,0:T(8,128)(2,1)} %after.78), channel_id=1, replica_groups=mesh['fsdp'=4,'seq'=8] {'seq'}, dimensions={0} | all-to-all | bytes 2097152 | tf_op jit(solution)/shard_map/all_to_all | solution.py:702
  197.8 5.8 multiply_reduce_fusion.3
  206.7 21.4 %collective-permute-done.12.refs_0_ = bf16[2,128,2048]{2,1,0:T(8,128)(2,1)S(1)} collective-permute-done((bf16[2,128,2048]{2,1,0:T(8,128)(2,1)S(1)}, bf16[2,128,2048]{2,1,0:T(8,128)(2,1)S(1)}, u32[]{:S(2)}, u32[]{:S(2)}) %collective-permute-start.12) | collective-permute-done | bytes 1048608 | tf_op jit(solution)/shard_map/ppermute | solution.py:31
  228.1 2.7 collective-permute-done.13.refs_1_.refs_0_
  232.7 20.7 %collective-permute-done.14.refs_0_ = bf16[2,128,2048]{2,1,0:T(8,128)(2,1)S(1)} collective-permute-done((bf16[2,128,2048]{2,1,0:T(8,128)(2,1)}, bf16[2,128,2048]{2,1,0:T(8,128)(2,1)S(1)}, u32[]{:S(2)}, u32[]{:S(2)}) %collective-permute-start.14) | collective-permute-done | bytes 1048608 | tf_op jit(solution)/shard_map/ppermute | solution.py:31
  253.4 2.7 collective-permute-done.15.refs_1_.refs_0_
  257.9 19.8 %collective-permute-done.16.refs_0_ = bf16[2,128,2048]{2,1,0:T(8,128)(2,1)S(1)} collective-permute-done((bf16[2,128,2048]{2,1,0:T(8,128)(2,1)}, bf16[2,128,2048]{2,1,0:T(8,128)(2,1)S(1)}, u32[]{:S(2)}, u32[]{:S(2)}) %collective-permute-start.16) | collective-permute-done | bytes 1048608 | tf_op jit(solution)/shard_map/ppermute | solution.py:31
  284.6 8.1 collective-permute-done.18.refs_0_
  292.7 4.6 collective-permute-done.19.refs_1_.refs_0_
  298.1 16.7 %collective-permute-done.20.refs_0_ = bf16[2,128,2048]{2,1,0:T(8,128)(2,1)S(1)} collective-permute-done((bf16[2,128,2048]{2,1,0:T(8,128)(2,1)}, bf16[2,128,2048]{2,1,0:T(8,128)(2,1)S(1)}, u32[]{:S(2)}, u32[]{:S(2)}) %collective-permute-start.20) | collective-permute-done | bytes 1048608 | tf_op jit(solution)/shard_map/ppermute | solution.py:31
  314.8 4.7 collective-permute-done.21.refs_1_.refs_0_
  329.3 5.3 collective-permute-done.22.refs_1_.refs_0_
  334.7 3.3 collective-permute-done.23.refs_0_
  347.1 34.2 %dispatch.3 = (bf16[4,2,384,2048]{3,2,1,0:T(8,128)(2,1)}, f32[4,2,384,1024]{3,2,1,0:T(8,128)}) custom-call(bf16[256,2048]{1,0:T(8,128)(2,1)} %bitcast.222, bf16[256,2048]{1,0:T(8,128)(2,1)} %bitcast.225, bf16[256,2048]{1,0:T(8,128)(2,1)} %bitcast.224, bf16[256,2048]{1,0:T(8,128)(2,1)} %bitcast.37.refs_3_, bf16[256,2048]{1,0:T(8,128)(2,1)} %bitcast.38.refs_4_, ...), custom_call_target="tpu_custom_call" | custom-call | flops 1 | bytes 1 | tf_op jit(solution)/shard_map/dispatch/pallas_call | solution.py:429
  383.6 19.9 %dispatch.4 = (bf16[4,2,384,2048]{3,2,1,0:T(8,128)(2,1)}, f32[4,2,384,1024]{3,2,1,0:T(8,128)}) custom-call(bf16[256,2048]{1,0:T(8,128)(2,1)} %copy-done.73, bf16[256,2048]{1,0:T(8,128)(2,1)} %bitcast.207, bf16[256,2048]{1,0:T(8,128)(2,1)} %bitcast.211, bf16[256,2048]{1,0:T(8,128)(2,1)} %bitcast.209, bf16[256,2048]{1,0:T(8,128)(2,1)} %bitcast.213, ...), custom_call_target="tpu_custom_call" | custom-call | flops 1 | bytes 1 | tf_op jit(solution)/shard_map/dispatch/pallas_call | solution.py:429
  406.7 4.1 collective-permute-start.28
  410.9 19.9 %dispatch.5 = (bf16[4,2,384,2048]{3,2,1,0:T(8,128)(2,1)}, f32[4,2,384,1024]{3,2,1,0:T(8,128)}) custom-call(bf16[256,2048]{1,0:T(8,128)(2,1)} %copy-done.73, bf16[256,2048]{1,0:T(8,128)(2,1)} %bitcast.208, bf16[256,2048]{1,0:T(8,128)(2,1)} %bitcast.212, bf16[256,2048]{1,0:T(8,128)(2,1)} %bitcast.210, ...), custom_call_target="tpu_custom_call", output_to_operand_aliasing={{0}: (12, {}), {1}: (13, {})} | custom-call | flops 1 | bytes 1 | tf_op jit(solution)/shard_map/dispatch/pallas_call | solution.py:429
  434.8 32.2 %activate.1 = (bf16[4,2,384,1024]{3,2,1,0:T(8,128)(2,1)}, bf16[4,2,384,1024]{3,2,1,0:T(8,128)(2,1)}, bf16[4,2,384,1024]{3,2,1,0:T(8,128)(2,1)}) custom-call(bf16[4,2,384,2048]{3,2,1,0:T(8,128)(2,1)} %get-tuple-element.55.refs_0_.refs_1_, f32[4,2,384,1024]{3,2,1,0:T(8,128)} %get-tuple-element.56.refs_1_, f32[4,2,384,1024]{3,2,1,0:T(8,128)} %get-tuple-element.57.refs_2_, ...), custom_call_target="tpu_custom_call" | custom-call | flops 1 | bytes 1 | tf_op jit(solution)/shard_map/activate/pallas_call | solution.py:429
  468.0 2.7 copy.277.refs_4_.refs_2_
  473.8 27.7 %combine.4 = (bf16[256,2048]{1,0:T(8,128)(2,1)}, bf16[256,2048]{1,0:T(8,128)(2,1)}, bf16[256,2048]{1,0:T(8,128)(2,1)}, bf16[256,2048]{1,0:T(8,128)(2,1)}) custom-call(bf16[4,2,384,1024]{3,2,1,0:T(8,128)(2,1)} %get-tuple-element.59.refs_0_.refs_1_, bf16[4,2,384,1024]{3,2,1,0:T(8,128)(2,1)} %get-tuple-element.60.refs_1_, ...), custom_call_target="tpu_custom_call" | custom-call | flops 1 | bytes 1 | tf_op jit(solution)/shard_map/combine/pallas_call | solution.py:429
  501.5 12.9 %bank_grad.4.refs_5_ = bf16[2,2048,1024]{2,1,0:T(8,128)(2,1)} custom-call(bf16[4,2,384,2048]{3,2,1,0:T(8,128)(2,1)} %get-tuple-element.52.refs_1_.refs_14_.refs_16_.refs_0_, bf16[4,2,384,1024]{3,2,1,0:T(8,128)(2,1)} %get-tuple-element.58.refs_1_.refs_0_, bf16[256,2048]{1,0:T(8,128)(2,1)} %get-tuple-element.61.refs_2_), custom_call_target="tpu_custom_call" | custom-call | flops 1 | bytes 1 | tf_op jit(solution)/shard_map/bank_grad/pallas_call | solution.py:429
  516.5 20.0 %combine.5 = (bf16[256,2048]{1,0:T(8,128)(2,1)}, bf16[256,2048]{1,0:T(8,128)(2,1)}, bf16[256,2048]{1,0:T(8,128)(2,1)}, bf16[256,2048]{1,0:T(8,128)(2,1)}) custom-call(bf16[4,2,384,1024]{3,2,1,0:T(8,128)(2,1)} %get-tuple-element.58.refs_1_.refs_0_, bf16[4,2048,1024]{2,1,0:T(8,128)(2,1)} %all-gather.12.cloned.1.call-done.refs_11_.refs_1_, ...), custom_call_target="tpu_custom_call" | custom-call | flops 1 | bytes 1 | tf_op jit(solution)/shard_map/combine/pallas_call | solution.py:429
  536.7 28.4 %combine.6 = (bf16[256,2048]{1,0:T(8,128)(2,1)}, bf16[256,2048]{1,0:T(8,128)(2,1)}, bf16[256,2048]{1,0:T(8,128)(2,1)}, bf16[256,2048]{1,0:T(8,128)(2,1)}) custom-call(bf16[4,2,384,1024]{3,2,1,0:T(8,128)(2,1)} %get-tuple-element.59.refs_0_.refs_1_, bf16[4,2,384,1024]{3,2,1,0:T(8,128)(2,1)} %get-tuple-element.60.refs_1_, ...), custom_call_target="tpu_custom_call" | custom-call | flops 1 | bytes 1 | tf_op jit(solution)/shard_map/combine/pallas_call | solution.py:429
  570.4 12.9 %bank_grad.5.refs_1_.refs_0_ = bf16[2,2048,1024]{2,1,0:T(8,128)(2,1)} custom-call(bf16[4,2,384,2048]{3,2,1,0:T(8,128)(2,1)} %get-tuple-element.52.refs_1_.refs_14_.refs_16_.refs_0_, bf16[4,2,384,1024]{3,2,1,0:T(8,128)(2,1)} %get-tuple-element.58.refs_1_.refs_0_, bf16[2,128,2048]{2,1,0:T(8,128)(2,1)} %after.101.refs_2_, bf16[2,128,2048]{2,1,0:T(8,128)(2,1)} %after.102.refs_3_), custom_call_target="tpu_custom_call" | custom-call | flops 1 | bytes 1 | tf_op jit(solution)/shard_map/bank_grad/pallas_call | solution.py:429
  583.3 6.5 collective-permute-done.36.refs_2_.refs_0_
  593.7 20.8 %combine.7 = (bf16[256,2048]{1,0:T(8,128)(2,1)}, bf16[256,2048]{1,0:T(8,128)(2,1)}, bf16[256,2048]{1,0:T(8,128)(2,1)}, bf16[256,2048]{1,0:T(8,128)(2,1)}) custom-call(bf16[4,2,384,1024]{3,2,1,0:T(8,128)(2,1)} %get-tuple-element.58.refs_1_.refs_0_, bf16[4,2048,1024]{2,1,0:T(8,128)(2,1)} %all-gather.12.cloned.1.call-done.refs_11_.refs_1_, ...), custom_call_target="tpu_custom_call" | custom-call | flops 1 | bytes 1 | tf_op jit(solution)/shard_map/combine/pallas_call | solution.py:429
  620.5 24.1 %bank_grad.6.refs_1_.refs_0_ = bf16[4,2048,1024]{2,1,0:T(8,128)(2,1)} custom-call(bf16[4,2,384,2048]{3,2,1,0:T(8,128)(2,1)} %get-tuple-element.55.refs_0_.refs_1_, bf16[4,2,384,1024]{3,2,1,0:T(8,128)(2,1)} %get-tuple-element.59.refs_0_.refs_1_, bf16[2,128,2048]{2,1,0:T(8,128)(2,1)} %after.105.refs_2_, bf16[2,128,2048]{2,1,0:T(8,128)(2,1)} %after.106.refs_3_), custom_call_target="tpu_custom_call" | custom-call | flops 1 | bytes 1 | tf_op jit(solution)/shard_map/bank_grad/pallas_call | solution.py:429
  652.8 6.1 convolution_convert_fusion.refs_2_
  660.4 6.4 all-to-all-start.1
  666.9 27.1 %bank_grad.7.refs_1_.refs_0_ = bf16[4,2048,1024]{2,1,0:T(8,128)(2,1)} custom-call(bf16[4,2,384,2048]{3,2,1,0:T(8,128)(2,1)} %get-tuple-element.55.refs_0_.refs_1_, bf16[4,2,384,1024]{3,2,1,0:T(8,128)(2,1)} %get-tuple-element.60.refs_1_, bf16[256,2048]{1,0:T(8,128)(2,1)} %copy-done.90), custom_call_target="tpu_custom_call" | custom-call | flops 1 | bytes 1 | tf_op jit(solution)/shard_map/bank_grad/pallas_call | solution.py:429
  697.8 6.3 all-to-all-start.2
  713.1 33.6 %attend_back.1 = (bf16[8,2,128,768]{3,2,1,0:T(8,128)(2,1)S(1)}, f32[4,2,128]{2,1,0:T(2,128)S(1)}) custom-call(bf16[8,2,128,768]{3,2,1,0:T(8,128)(2,1)S(1)} %copy-done.5, bf16[8,2,128,256]{3,2,1,0:T(8,128)(2,1)S(1)} %copy-done.3, s32[8]{0:T(128)S(1)} %get-tuple-element.101.refs_2_.refs_1_, f32[1024,128]{1,0:T(8,128)S(1)} %copy-done.12, ...), custom_call_target="tpu_custom_call" | custom-call | flops 1 | bytes 1 | tf_op jit(solution)/shard_map/attend_back/pallas_call | solution.py:300
  748.9 12.5 %part_grads.1 = (bf16[256,2048]{1,0:T(8,128)(2,1)}, bf16[256,2048]{1,0:T(8,128)(2,1)}, bf16[256,2048]{1,0:T(8,128)(2,1)}, bf16[256,2048]{1,0:T(8,128)(2,1)}, bf1...) custom-call(bf16[2048,768]{1,0:T(8,128)(2,1)} %bitcast.190, ...), custom_call_target="tpu_custom_call" | custom-call | flops 1 | bytes 1 | tf_op jit(solution)/shard_map/part_grads/pallas_call | solution.py:429
  763.0 3.1 add_convert_fusion.6
  771.2 20.6 %proj_grads.1 = (bf16[512,1152]{1,0:T(8,128)(2,1)}, bf16[512,1152]{1,0:T(8,128)(2,1)}, bf16[512,1152]{1,0:T(8,128)(2,1)}, bf16[512,1152]{1,0:T(8,128)(2,1)}) custom-call(s32[4]{0:T(128)} %fusion.41.refs_0_, s32[8]{0:T(128)} %copy-done.17, bf16[2048,2048]{1,0:T(8,128)(2,1)} %bitcast.202, bf16[2048,768]{1,0:T(8,128)(2,1)} %bitcast.191, ...), custom_call_target="tpu_custom_call" | custom-call | flops 1 | bytes 1 | tf_op jit(solution)/shard_map/proj_grads/pallas_call | solution.py:390
  796.4 2.6 add_convert_fusion.2
  803.7 3.0 add_convert_fusion.5
  807.5 19.7 %collective-permute-done.54.refs_1_.refs_0_ = bf16[512,1152]{1,0:T(8,128)(2,1)} collective-permute-done((bf16[512,1152]{1,0:T(8,128)(2,1)}, bf16[512,1152]{1,0:T(8,128)(2,1)}, u32[]{:S(2)}, u32[]{:S(2)}) %collective-permute-start.54) | collective-permute-done | bytes 1179680 | tf_op jit(solution)/shard_map/ppermute | solution.py:31
  828.5 3.4 add_convert_fusion.refs_5_.refs_0_
  832.0 9.5 collective-permute-done.50.refs_2_.refs_0_
  841.5 9.9 %collective-permute-done.48.refs_0_ = bf16[2,128,2048]{2,1,0:T(8,128)(2,1)S(1)} collective-permute-done((bf16[2,128,2048]{2,1,0:T(8,128)(2,1)}, bf16[2,128,2048]{2,1,0:T(8,128)(2,1)S(1)}, u32[]{:S(2)}, u32[]{:S(2)}) %collective-permute-start.48) | collective-permute-done | bytes 1048608 | tf_op jit(solution)/shard_map/ppermute | solution.py:31
  852.5 4.0 all-to-all-start.3
  856.4 2.7 add_convert_fusion.4
  864.1 6.2 maximum_convert_fusion.refs_1_
  870.3 27.2 %collective-permute-done.57.refs_3_.refs_0_ = f32[2,128]{1,0:T(2,128)S(1)} collective-permute-done((f32[2,128]{1,0:T(2,128)S(1)}, f32[2,128]{1,0:T(2,128)S(1)}, u32[]{:S(2)}, u32[]{:S(2)}) %collective-permute-start.57) | collective-permute-done | bytes 1056 | tf_op jit(solution)/shard_map/ppermute | solution.py:866
  897.5 4.0 collective-permute-done.55.refs_0_
  901.5 5.5 all-to-all-done.3.refs_4_.refs_0_
  914.6 3.1 convert_add_fusion.14
  922.2 2.6 reshape.579
  934.7 6.6 convert_element_type.450.refs_1_
  941.3 6.7 convert_element_type.451.refs_2_
  952.0 3.3 multiply_reduce_fusion
  956.5 6.6 fusion.19
  (556 shorter events, 186.4 us)
Async XLA Ops:
  7.2 118.5 %all-gather.6.cloned.1.call-start = ((), (), s32[]{:S(2)}) async-start(), calls=%async_computation.8 | async-start | bytes 4587520 | tf_op jit(solution)/shard_map/all_gather | solution.py:649
  12.0 185.5 %all-gather.8.cloned.1.call-start = ((), (), s32[]{:S(2)}) async-start(), calls=%async_computation.9 | async-start | bytes 10485760 | tf_op jit(solution)/shard_map/all_gather | solution.py:649
  12.7 334.4 %all-gather.12.cloned.1.call-start = ((), (), s32[]{:S(2)}) async-start(), calls=%async_computation.11 | async-start | bytes 20971520 | tf_op jit(solution)/shard_map/all_gather | solution.py:649
  13.5 370.1 %all-gather.10.cloned.1.call-start = ((), (), s32[]{:S(2)}) async-start(), calls=%async_computation.10 | async-start | bytes 20971520 | tf_op jit(solution)/shard_map/all_gather | solution.py:649
  14.1 420.7 %all-gather.14.cloned.1.call-start = ((), (), s32[]{:S(2)}) async-start(), calls=%async_computation.12 | async-start | bytes 20971520 | tf_op jit(solution)/shard_map/all_gather | solution.py:649
  14.7 849.5 %reduce-scatter.5.cloned.1.call-start = ((), (), s32[]{:S(2)}) async-start(), calls=%async_computation.13 | async-start | bytes 10485760 | tf_op jit(solution)/shard_map/reduce_scatter | solution.py:812
  17.9 29.8 %collective-permute-start.1 = (bf16[2,128,2176]{2,1,0:T(8,128)(2,1)}, bf16[2,128,2176]{2,1,0:T(8,128)(2,1)S(1)}, u32[]{:S(2)}, u32[]{:S(2)}) collective-permute-start(bf16[2,128,2176]{2,1,0:T(8,128)(2,1)} %get-tuple-element.109), channel_id=1, source_target_pairs={{0,2},{1,3},{2,4},{3,5},{4,6},{5,7},{6,0},{7,1},{8,10},{9,11},{10,... | collective-permute-start | bytes 3342344 | tf_op jit(solution)/shard_map/ppermute | solution.py:31
  20.9 35.6 %collective-permute-start = (bf16[2,128,2176]{2,1,0:T(8,128)(2,1)}, bf16[2,128,2176]{2,1,0:T(8,128)(2,1)}, u32[]{:S(2)}, u32[]{:S(2)}) collective-permute-start(bf16[2,128,2176]{2,1,0:T(8,128)(2,1)} %get-tuple-element.109), channel_id=1, source_target_pairs={{0,1},{1,0},{2,3},{3,2},{4,5},{5,4},{6,7},{7,6},{8,9},{9,8},{10,11... | collective-permute-start | bytes 3342344 | tf_op jit(solution)/shard_map/ppermute | solution.py:31
  47.7 27.7 %collective-permute-start.3 = (bf16[2,128,2176]{2,1,0:T(8,128)(2,1)S(1)}, bf16[2,128,2176]{2,1,0:T(8,128)(2,1)}, u32[]{:S(2)}, u32[]{:S(2)}) collective-permute-start(bf16[2,128,2176]{2,1,0:T(8,128)(2,1)S(1)} %collective-permute-done.1), channel_id=1, source_target_pairs={{0,2},{1,3},{2,4},{3,5},{4,6},{5,7},{6,0},{7,1},{8,10},{9,11},{10,... | collective-permute-start | bytes 3342344 | tf_op jit(solution)/shard_map/ppermute | solution.py:31
  51.9 26.8 %collective-permute-start.2 = (bf16[2,128,2176]{2,1,0:T(8,128)(2,1)S(1)}, bf16[2,128,2176]{2,1,0:T(8,128)(2,1)S(1)}, u32[]{:S(2)}, u32[]{:S(2)}) collective-permute-start(bf16[2,128,2176]{2,1,0:T(8,128)(2,1)S(1)} %collective-permute-done.1), channel_id=1, source_target_pairs={{0,1},{1,0},{2,3},{3,2},{4,5},{5,4},{6,7},{7,6},{8,9},{9,8},{10,11... | collective-permute-start | bytes 3342344 | tf_op jit(solution)/shard_map/ppermute | solution.py:31
  75.4 28.7 %collective-permute-start.4 = (bf16[2,128,2176]{2,1,0:T(8,128)(2,1)}, bf16[2,128,2176]{2,1,0:T(8,128)(2,1)S(1)}, u32[]{:S(2)}, u32[]{:S(2)}) collective-permute-start(bf16[2,128,2176]{2,1,0:T(8,128)(2,1)} %collective-permute-done.3), channel_id=1, source_target_pairs={{0,1},{1,0},{2,3},{3,2},{4,5},{5,4},{6,7},{7,6},{8,9},{9,8},{10,11... | collective-permute-start | bytes 3342344 | tf_op jit(solution)/shard_map/ppermute | solution.py:31
  76.6 26.3 %collective-permute-start.5 = (bf16[2,128,2176]{2,1,0:T(8,128)(2,1)}, bf16[2,128,2176]{2,1,0:T(8,128)(2,1)S(1)}, u32[]{:S(2)}, u32[]{:S(2)}) collective-permute-start(bf16[2,128,2176]{2,1,0:T(8,128)(2,1)} %collective-permute-done.3), channel_id=1, source_target_pairs={{0,2},{1,3},{2,4},{3,5},{4,6},{5,7},{6,0},{7,1},{8,10},{9,11},{10,... | collective-permute-start | bytes 3342344 | tf_op jit(solution)/shard_map/ppermute | solution.py:31
  118.2 23.0 %collective-permute-start.8 = (bf16[2,128,2048]{2,1,0:T(8,128)(2,1)}, bf16[2,128,2048]{2,1,0:T(8,128)(2,1)S(1)}, u32[]{:S(2)}, u32[]{:S(2)}) collective-permute-start(bf16[2,128,2048]{2,1,0:T(8,128)(2,1)} %after.73), channel_id=1, source_target_pairs={{0,2},{1,3},{2,4},{3,5},{4,6},{5,7},{6,0},{7,1},{8,10},{9,11},{10,... | collective-permute-start | bytes 3145736 | tf_op jit(solution)/shard_map/ppermute | solution.py:31
  118.2 23.0 %collective-permute-start.9 = (bf16[2,128,2048]{2,1,0:T(8,128)(2,1)}, bf16[2,128,2048]{2,1,0:T(8,128)(2,1)S(1)}, u32[]{:S(2)}, u32[]{:S(2)}) collective-permute-start(bf16[2,128,2048]{2,1,0:T(8,128)(2,1)} %after.73), channel_id=1, source_target_pairs={{0,1},{1,0},{2,3},{3,2},{4,5},{5,4},{6,7},{7,6},{8,9},{9,8},{10,11... | collective-permute-start | bytes 3145736 | tf_op jit(solution)/shard_map/ppermute | solution.py:31
  143.2 25.6 %collective-permute-start.10 = (bf16[2,128,2048]{2,1,0:T(8,128)(2,1)}, bf16[2,128,2048]{2,1,0:T(8,128)(2,1)}, u32[]{:S(2)}, u32[]{:S(2)}) collective-permute-start(bf16[2,128,2048]{2,1,0:T(8,128)(2,1)} %after.75), channel_id=1, source_target_pairs={{0,2},{1,3},{2,4},{3,5},{4,6},{5,7},{6,0},{7,1},{8,10},{9,11},{10,... | collective-permute-start | bytes 3145736 | tf_op jit(solution)/shard_map/ppermute | solution.py:31
  143.5 25.3 %collective-permute-start.11 = (bf16[2,128,2048]{2,1,0:T(8,128)(2,1)}, bf16[2,128,2048]{2,1,0:T(8,128)(2,1)}, u32[]{:S(2)}, u32[]{:S(2)}) collective-permute-start(bf16[2,128,2048]{2,1,0:T(8,128)(2,1)} %after.75), channel_id=1, source_target_pairs={{0,1},{1,0},{2,3},{3,2},{4,5},{5,4},{6,7},{7,6},{8,9},{9,8},{10,11... | collective-permute-start | bytes 3145736 | tf_op jit(solution)/shard_map/ppermute | solution.py:31
  205.2 22.9 %collective-permute-start.12 = (bf16[2,128,2048]{2,1,0:T(8,128)(2,1)S(1)}, bf16[2,128,2048]{2,1,0:T(8,128)(2,1)S(1)}, u32[]{:S(2)}, u32[]{:S(2)}) collective-permute-start(bf16[2,128,2048]{2,1,0:T(8,128)(2,1)S(1)} %bitcast.220), channel_id=1, source_target_pairs={{0,1},{1,0},{2,3},{3,2},{4,5},{5,4},{6,7},{7,6},{8,9},{9,8},{10,11... | collective-permute-start | bytes 3145736 | tf_op jit(solution)/shard_map/ppermute | solution.py:31
  206.7 24.1 %collective-permute-start.13 = (bf16[2,128,2048]{2,1,0:T(8,128)(2,1)S(1)}, bf16[2,128,2048]{2,1,0:T(8,128)(2,1)S(1)}, u32[]{:S(2)}, u32[]{:S(2)}) collective-permute-start(bf16[2,128,2048]{2,1,0:T(8,128)(2,1)S(1)} %bitcast.221), channel_id=1, source_target_pairs={{0,2},{1,3},{2,4},{3,5},{4,6},{5,7},{6,0},{7,1},{8,10},{9,11},{10,... | collective-permute-start | bytes 3145736 | tf_op jit(solution)/shard_map/ppermute | solution.py:31
  231.8 21.6 %collective-permute-start.14 = (bf16[2,128,2048]{2,1,0:T(8,128)(2,1)}, bf16[2,128,2048]{2,1,0:T(8,128)(2,1)S(1)}, u32[]{:S(2)}, u32[]{:S(2)}) collective-permute-start(bf16[2,128,2048]{2,1,0:T(8,128)(2,1)} %after.80), channel_id=1, source_target_pairs={{0,1},{1,0},{2,3},{3,2},{4,5},{5,4},{6,7},{7,6},{8,9},{9,8},{10,11... | collective-permute-start | bytes 3145736 | tf_op jit(solution)/shard_map/ppermute | solution.py:31
  232.7 23.4 %collective-permute-start.15 = (bf16[2,128,2048]{2,1,0:T(8,128)(2,1)}, bf16[2,128,2048]{2,1,0:T(8,128)(2,1)S(1)}, u32[]{:S(2)}, u32[]{:S(2)}) collective-permute-start(bf16[2,128,2048]{2,1,0:T(8,128)(2,1)} %after.80), channel_id=1, source_target_pairs={{0,2},{1,3},{2,4},{3,5},{4,6},{5,7},{6,0},{7,1},{8,10},{9,11},{10,... | collective-permute-start | bytes 3145736 | tf_op jit(solution)/shard_map/ppermute | solution.py:31
  257.0 20.7 %collective-permute-start.16 = (bf16[2,128,2048]{2,1,0:T(8,128)(2,1)}, bf16[2,128,2048]{2,1,0:T(8,128)(2,1)S(1)}, u32[]{:S(2)}, u32[]{:S(2)}) collective-permute-start(bf16[2,128,2048]{2,1,0:T(8,128)(2,1)} %after.82), channel_id=1, source_target_pairs={{0,1},{1,0},{2,3},{3,2},{4,5},{5,4},{6,7},{7,6},{8,9},{9,8},{10,11... | collective-permute-start | bytes 3145736 | tf_op jit(solution)/shard_map/ppermute | solution.py:31
  257.9 21.9 %collective-permute-start.17 = (bf16[2,128,2048]{2,1,0:T(8,128)(2,1)}, bf16[2,128,2048]{2,1,0:T(8,128)(2,1)S(1)}, u32[]{:S(2)}, u32[]{:S(2)}) collective-permute-start(bf16[2,128,2048]{2,1,0:T(8,128)(2,1)} %after.82), channel_id=1, source_target_pairs={{0,2},{1,3},{2,4},{3,5},{4,6},{5,7},{6,0},{7,1},{8,10},{9,11},{10,... | collective-permute-start | bytes 3145736 | tf_op jit(solution)/shard_map/ppermute | solution.py:31
  298.1 16.7 %collective-permute-start.20 = (bf16[2,128,2048]{2,1,0:T(8,128)(2,1)}, bf16[2,128,2048]{2,1,0:T(8,128)(2,1)S(1)}, u32[]{:S(2)}, u32[]{:S(2)}) collective-permute-start(bf16[2,128,2048]{2,1,0:T(8,128)(2,1)} %after.87), channel_id=1, source_target_pairs={{0,1},{1,0},{2,3},{3,2},{4,5},{5,4},{6,7},{7,6},{8,9},{9,8},{10,11... | collective-permute-start | bytes 3145736 | tf_op jit(solution)/shard_map/ppermute | solution.py:31
  298.1 21.4 %collective-permute-start.21 = (bf16[2,128,2048]{2,1,0:T(8,128)(2,1)}, bf16[2,128,2048]{2,1,0:T(8,128)(2,1)S(1)}, u32[]{:S(2)}, u32[]{:S(2)}) collective-permute-start(bf16[2,128,2048]{2,1,0:T(8,128)(2,1)} %after.87), channel_id=1, source_target_pairs={{0,2},{1,3},{2,4},{3,5},{4,6},{5,7},{6,0},{7,1},{8,10},{9,11},{10,... | collective-permute-start | bytes 3145736 | tf_op jit(solution)/shard_map/ppermute | solution.py:31
  323.6 14.4 %collective-permute-start.23 = (bf16[1,128,2048]{2,1,0:T(8,128)(2,1)}, bf16[1,128,2048]{2,1,0:T(8,128)(2,1)S(1)}, u32[]{:S(2)}, u32[]{:S(2)}) collective-permute-start(bf16[1,128,2048]{2,1,0:T(8,128)(2,1)} %slice.113), channel_id=1, source_target_pairs={{0,1},{1,0},{2,3},{3,2},{4,5},{5,4},{6,7},{7,6},{8,9},{9,8},{10,11... | collective-permute-start | bytes 1572872 | tf_op jit(solution)/shard_map/ppermute | solution.py:31
  338.8 42.5 %collective-permute-start.24 = (bf16[2048,256]{1,0:T(8,128)(2,1)}, bf16[2048,256]{1,0:T(8,128)(2,1)S(1)}, u32[]{:S(2)}, u32[]{:S(2)}) collective-permute-start(bf16[2048,256]{1,0:T(8,128)(2,1)} %after.92.refs_6_), channel_id=1, source_target_pairs={{0,1},{1,0},{2,3},{3,2},{4,5},{5,4},{6,7},{7,6},{8,9},{9,8},{10,11... | collective-permute-start | bytes 3145736 | tf_op jit(solution)/shard_map/ppermute | solution.py:31
  341.2 40.1 %collective-permute-start.25 = (bf16[2048,256]{1,0:T(8,128)(2,1)}, bf16[2048,256]{1,0:T(8,128)(2,1)S(1)}, u32[]{:S(2)}, u32[]{:S(2)}) collective-permute-start(bf16[2048,256]{1,0:T(8,128)(2,1)} %after.92.refs_6_), channel_id=1, source_target_pairs={{0,2},{1,3},{2,4},{3,5},{4,6},{5,7},{6,0},{7,1},{8,10},{9,11},{10,... | collective-permute-start | bytes 3145736 | tf_op jit(solution)/shard_map/ppermute | solution.py:31
  382.6 20.8 %collective-permute-start.26 = (bf16[2048,256]{1,0:T(8,128)(2,1)}, bf16[2048,256]{1,0:T(8,128)(2,1)S(1)}, u32[]{:S(2)}, u32[]{:S(2)}) collective-permute-start(bf16[2048,256]{1,0:T(8,128)(2,1)} %after.94.refs_13_.refs_8_), channel_id=1, source_target_pairs={{0,1},{1,0},{2,3},{3,2},{4,5},{5,4},{6,7},{7,6},{8,9},{9,8},{10,11... | collective-permute-start | bytes 3145736 | tf_op jit(solution)/shard_map/ppermute | solution.py:31
  382.8 20.7 %collective-permute-start.27 = (bf16[2048,256]{1,0:T(8,128)(2,1)}, bf16[2048,256]{1,0:T(8,128)(2,1)S(1)}, u32[]{:S(2)}, u32[]{:S(2)}) collective-permute-start(bf16[2048,256]{1,0:T(8,128)(2,1)} %after.94.refs_13_.refs_8_), channel_id=1, source_target_pairs={{0,2},{1,3},{2,4},{3,5},{4,6},{5,7},{6,0},{7,1},{8,10},{9,11},{10,... | collective-permute-start | bytes 3145736 | tf_op jit(solution)/shard_map/ppermute | solution.py:31
  404.8 25.9 %collective-permute-start.29 = (bf16[2048,256]{1,0:T(8,128)(2,1)}, bf16[2048,256]{1,0:T(8,128)(2,1)S(1)}, u32[]{:S(2)}, u32[]{:S(2)}) collective-permute-start(bf16[2048,256]{1,0:T(8,128)(2,1)} %after.96.refs_15_.refs_10_), channel_id=1, source_target_pairs={{0,1},{1,0},{2,3},{3,2},{4,5},{5,4},{6,7},{7,6},{8,9},{9,8},{10,11... | collective-permute-start | bytes 3145736 | tf_op jit(solution)/shard_map/ppermute | solution.py:31
  406.7 24.0 %collective-permute-start.28 = (bf16[2048,256]{1,0:T(8,128)(2,1)}, bf16[2048,256]{1,0:T(8,128)(2,1)S(1)}, u32[]{:S(2)}, u32[]{:S(2)}) collective-permute-start(bf16[2048,256]{1,0:T(8,128)(2,1)} %after.96.refs_15_.refs_10_), channel_id=1, source_target_pairs={{0,2},{1,3},{2,4},{3,5},{4,6},{5,7},{6,0},{7,1},{8,10},{9,11},{10,... | collective-permute-start | bytes 3145736 | tf_op jit(solution)/shard_map/ppermute | solution.py:31
  433.2 33.8 %collective-permute-start.31 = (bf16[1024,256]{1,0:T(8,128)(2,1)S(1)}, bf16[1024,256]{1,0:T(8,128)(2,1)S(1)}, u32[]{:S(2)}, u32[]{:S(2)}) collective-permute-start(bf16[1024,256]{1,0:T(8,128)(2,1)S(1)} %slice.115), channel_id=1, source_target_pairs={{0,2},{1,3},{2,4},{3,5},{4,6},{5,7},{6,0},{7,1},{8,10},{9,11},{10,... | collective-permute-start | bytes 1572872 | tf_op jit(solution)/shard_map/ppermute | solution.py:31
  434.5 32.5 %collective-permute-start.30 = (bf16[1024,256]{1,0:T(8,128)(2,1)S(1)}, bf16[1024,256]{1,0:T(8,128)(2,1)S(1)}, u32[]{:S(2)}, u32[]{:S(2)}) collective-permute-start(bf16[1024,256]{1,0:T(8,128)(2,1)S(1)} %slice.114), channel_id=1, source_target_pairs={{0,1},{1,0},{2,3},{3,2},{4,5},{5,4},{6,7},{7,6},{8,9},{9,8},{10,11... | collective-permute-start | bytes 1572872 | tf_op jit(solution)/shard_map/ppermute | solution.py:31
  514.4 349.8 %reduce-scatter.7.cloned.1.call-start = ((), (), s32[]{:S(2)}) async-start(), calls=%async_computation.14 | async-start | bytes 10485760 | tf_op jit(solution)/shard_map/reduce_scatter | solution.py:812
  514.6 52.3 %collective-permute-start.34 = (bf16[2,128,2048]{2,1,0:T(8,128)(2,1)}, bf16[2,128,2048]{2,1,0:T(8,128)(2,1)S(1)}, u32[]{:S(2)}, u32[]{:S(2)}) collective-permute-start(bf16[2,128,2048]{2,1,0:T(8,128)(2,1)} %bitcast.47), channel_id=1, source_target_pairs={{0,1},{1,0},{2,3},{3,2},{4,5},{5,4},{6,7},{7,6},{8,9},{9,8},{10,11... | collective-permute-start | bytes 3145736 | tf_op jit(solution)/shard_map/ppermute | solution.py:31
  536.5 30.4 %collective-permute-start.35 = (bf16[2,128,2048]{2,1,0:T(8,128)(2,1)}, bf16[2,128,2048]{2,1,0:T(8,128)(2,1)S(1)}, u32[]{:S(2)}, u32[]{:S(2)}) collective-permute-start(bf16[2,128,2048]{2,1,0:T(8,128)(2,1)} %bitcast.284), channel_id=1, source_target_pairs={{0,1},{1,0},{2,3},{3,2},{4,5},{5,4},{6,7},{7,6},{8,9},{9,8},{10,11... | collective-permute-start | bytes 3145736 | tf_op jit(solution)/shard_map/ppermute | solution.py:31
  565.2 18.1 %collective-permute-start.33 = (bf16[2,128,2048]{2,1,0:T(8,128)(2,1)}, bf16[2,128,2048]{2,1,0:T(8,128)(2,1)S(1)}, u32[]{:S(2)}, u32[]{:S(2)}) collective-permute-start(bf16[2,128,2048]{2,1,0:T(8,128)(2,1)} %bitcast.283), channel_id=1, source_target_pairs={{0,1},{1,0},{2,3},{3,2},{4,5},{5,4},{6,7},{7,6},{8,9},{9,8},{10,11... | collective-permute-start | bytes 3145736 | tf_op jit(solution)/shard_map/ppermute | solution.py:31
  570.3 19.6 %collective-permute-start.36 = (bf16[2,128,2048]{2,1,0:T(8,128)(2,1)S(1)}, bf16[2,128,2048]{2,1,0:T(8,128)(2,1)S(1)}, u32[]{:S(2)}, u32[]{:S(2)}) collective-permute-start(bf16[2,128,2048]{2,1,0:T(8,128)(2,1)S(1)} %fusion.16), channel_id=1, source_target_pairs={{0,2},{1,3},{2,4},{3,5},{4,6},{5,7},{6,0},{7,1},{8,10},{9,11},{10,... | collective-permute-start | bytes 3145736 | tf_op jit(solution)/shard_map/ppermute | solution.py:31
  590.8 343.8 %reduce-scatter.9.cloned.1.call-start = ((), (), s32[]{:S(2)}) async-start(), calls=%async_computation.15 | async-start | bytes 20971520 | tf_op jit(solution)/shard_map/reduce_scatter | solution.py:812
  590.9 23.6 %collective-permute-start.39 = (bf16[2,128,2048]{2,1,0:T(8,128)(2,1)}, bf16[2,128,2048]{2,1,0:T(8,128)(2,1)S(1)}, u32[]{:S(2)}, u32[]{:S(2)}) collective-permute-start(bf16[2,128,2048]{2,1,0:T(8,128)(2,1)} %bitcast.282), channel_id=1, source_target_pairs={{0,1},{1,0},{2,3},{3,2},{4,5},{5,4},{6,7},{7,6},{8,9},{9,8},{10,11... | collective-permute-start | bytes 3145736 | tf_op jit(solution)/shard_map/ppermute | solution.py:31
  593.2 21.3 %collective-permute-start.40 = (bf16[2,128,2048]{2,1,0:T(8,128)(2,1)S(1)}, bf16[2,128,2048]{2,1,0:T(8,128)(2,1)S(1)}, u32[]{:S(2)}, u32[]{:S(2)}) collective-permute-start(bf16[2,128,2048]{2,1,0:T(8,128)(2,1)S(1)} %add_convert_fusion.8), channel_id=1, source_target_pairs={{0,2},{1,3},{2,4},{3,5},{4,6},{5,7},{6,0},{7,1},{8,10},{9,11},{10,... | collective-permute-start | bytes 3145736 | tf_op jit(solution)/shard_map/ppermute | solution.py:31
  616.4 28.1 %collective-permute-start.38 = (bf16[2,128,2048]{2,1,0:T(8,128)(2,1)}, bf16[2,128,2048]{2,1,0:T(8,128)(2,1)S(1)}, u32[]{:S(2)}, u32[]{:S(2)}) collective-permute-start(bf16[2,128,2048]{2,1,0:T(8,128)(2,1)} %bitcast.281), channel_id=1, source_target_pairs={{0,1},{1,0},{2,3},{3,2},{4,5},{5,4},{6,7},{7,6},{8,9},{9,8},{10,11... | collective-permute-start | bytes 3145736 | tf_op jit(solution)/shard_map/ppermute | solution.py:31
  619.7 24.9 %collective-permute-start.41 = (bf16[2,128,2048]{2,1,0:T(8,128)(2,1)S(1)}, bf16[2,128,2048]{2,1,0:T(8,128)(2,1)S(1)}, u32[]{:S(2)}, u32[]{:S(2)}) collective-permute-start(bf16[2,128,2048]{2,1,0:T(8,128)(2,1)S(1)} %add_convert_fusion.7), channel_id=1, source_target_pairs={{0,2},{1,3},{2,4},{3,5},{4,6},{5,7},{6,0},{7,1},{8,10},{9,11},{10,... | collective-permute-start | bytes 3145736 | tf_op jit(solution)/shard_map/ppermute | solution.py:31
  660.4 33.6 %all-to-all-start.1 = ((bf16[8,2,128,256]{3,2,1,0:T(8,128)(2,1)}), bf16[8,2,128,256]{3,2,1,0:T(8,128)(2,1)S(1)}, u32[]{:S(2)}, u32[]{:S(2)}) async-start(bf16[8,2,128,256]{3,2,1,0:T(8,128)(2,1)} %bitcast.188), calls=%async_computation.1 | async-start | bytes 2097152 | tf_op jit(solution)/shard_map/all_to_all | solution.py:827
  666.8 274.5 %reduce-scatter.11.cloned.1.call-start = ((), (), s32[]{:S(2)}) async-start(), calls=%async_computation.16 | async-start | bytes 20971520 | tf_op jit(solution)/shard_map/reduce_scatter | solution.py:812
  697.8 63.6 %all-to-all-start.2 = ((bf16[8,2,128,256]{3,2,1,0:T(8,128)(2,1)}), bf16[8,2,128,256]{3,2,1,0:T(8,128)(2,1)}, u32[]{:S(2)}, u32[]{:S(2)}) async-start(bf16[8,2,128,256]{3,2,1,0:T(8,128)(2,1)} %bitcast.187), calls=%async_computation.2 | async-start | bytes 2097152 | tf_op jit(solution)/shard_map/all_to_all | solution.py:827
  705.5 55.9 %collective-permute-start.42 = (bf16[2,128,2048]{2,1,0:T(8,128)(2,1)}, bf16[2,128,2048]{2,1,0:T(8,128)(2,1)}, u32[]{:S(2)}, u32[]{:S(2)}) collective-permute-start(bf16[2,128,2048]{2,1,0:T(8,128)(2,1)} %after.111), channel_id=1, source_target_pairs={{0,2},{1,3},{2,4},{3,5},{4,6},{5,7},{6,0},{7,1},{8,10},{9,11},{10,... | collective-permute-start | bytes 3145736 | tf_op jit(solution)/shard_map/ppermute | solution.py:31
  707.5 53.9 %collective-permute-start.43 = (bf16[2,128,2048]{2,1,0:T(8,128)(2,1)}, bf16[2,128,2048]{2,1,0:T(8,128)(2,1)}, u32[]{:S(2)}, u32[]{:S(2)}) collective-permute-start(bf16[2,128,2048]{2,1,0:T(8,128)(2,1)} %after.112), channel_id=1, source_target_pairs={{0,1},{1,0},{2,3},{3,2},{4,5},{5,4},{6,7},{7,6},{8,9},{9,8},{10,11... | collective-permute-start | bytes 3145736 | tf_op jit(solution)/shard_map/ppermute | solution.py:31
  710.4 81.4 %collective-permute-start.37 = (bf16[2,128,2048]{2,1,0:T(8,128)(2,1)}, bf16[2,128,2048]{2,1,0:T(8,128)(2,1)}, u32[]{:S(2)}, u32[]{:S(2)}) collective-permute-start(bf16[2,128,2048]{2,1,0:T(8,128)(2,1)} %bitcast.280), channel_id=1, source_target_pairs={{0,1},{1,0},{2,3},{3,2},{4,5},{5,4},{6,7},{7,6},{8,9},{9,8},{10,11... | collective-permute-start | bytes 3145736 | tf_op jit(solution)/shard_map/ppermute | solution.py:31
  761.5 30.4 %collective-permute-start.45 = (bf16[2,128,2048]{2,1,0:T(8,128)(2,1)}, bf16[2,128,2048]{2,1,0:T(8,128)(2,1)S(1)}, u32[]{:S(2)}, u32[]{:S(2)}) collective-permute-start(bf16[2,128,2048]{2,1,0:T(8,128)(2,1)} %after.116), channel_id=1, source_target_pairs={{0,1},{1,0},{2,3},{3,2},{4,5},{5,4},{6,7},{7,6},{8,9},{9,8},{10,11... | collective-permute-start | bytes 3145736 | tf_op jit(solution)/shard_map/ppermute | solution.py:31
  766.1 25.7 %collective-permute-start.44 = (bf16[2,128,2048]{2,1,0:T(8,128)(2,1)}, bf16[2,128,2048]{2,1,0:T(8,128)(2,1)S(1)}, u32[]{:S(2)}, u32[]{:S(2)}) collective-permute-start(bf16[2,128,2048]{2,1,0:T(8,128)(2,1)} %add_convert_fusion.6), channel_id=1, source_target_pairs={{0,2},{1,3},{2,4},{3,5},{4,6},{5,7},{6,0},{7,1},{8,10},{9,11},{10,... | collective-permute-start | bytes 3145736 | tf_op jit(solution)/shard_map/ppermute | solution.py:31
  769.6 22.2 %collective-permute-start.47 = (f32[2,128]{1,0:T(2,128)S(1)}, f32[2,128]{1,0:T(2,128)S(1)}, u32[]{:S(2)}, u32[]{:S(2)}) collective-permute-start(f32[2,128]{1,0:T(2,128)S(1)} %add.361), channel_id=1, source_target_pairs={{0,16},{8,24},{16,0},{24,8},{1,17},{9,25},{17,1},{25,9},{2,18},{10... | collective-permute-start | bytes 3080 | tf_op jit(solution)/shard_map/ppermute | solution.py:866
  793.1 38.8 %collective-permute-start.32 = (bf16[2,128,2048]{2,1,0:T(8,128)(2,1)}, bf16[2,128,2048]{2,1,0:T(8,128)(2,1)S(1)}, u32[]{:S(2)}, u32[]{:S(2)}) collective-permute-start(bf16[2,128,2048]{2,1,0:T(8,128)(2,1)} %bitcast.45), channel_id=1, source_target_pairs={{0,1},{1,0},{2,3},{3,2},{4,5},{5,4},{6,7},{7,6},{8,9},{9,8},{10,11... | collective-permute-start | bytes 3145736 | tf_op jit(solution)/shard_map/ppermute | solution.py:31
  794.4 47.1 %collective-permute-start.50 = (bf16[2,128,2048]{2,1,0:T(8,128)(2,1)}, bf16[2,128,2048]{2,1,0:T(8,128)(2,1)}, u32[]{:S(2)}, u32[]{:S(2)}) collective-permute-start(bf16[2,128,2048]{2,1,0:T(8,128)(2,1)} %bitcast.74), channel_id=1, source_target_pairs={{0,1},{1,0},{2,3},{3,2},{4,5},{5,4},{6,7},{7,6},{8,9},{9,8},{10,11... | collective-permute-start | bytes 3145736 | tf_op jit(solution)/shard_map/ppermute | solution.py:31
  799.0 28.2 %collective-permute-start.54 = (bf16[512,1152]{1,0:T(8,128)(2,1)}, bf16[512,1152]{1,0:T(8,128)(2,1)}, u32[]{:S(2)}, u32[]{:S(2)}) collective-permute-start(bf16[512,1152]{1,0:T(8,128)(2,1)} %add_convert_fusion.2), channel_id=1, source_target_pairs={{0,16},{8,24},{16,0},{24,8},{1,17},{9,25},{17,1},{25,9},{2,18},{10... | collective-permute-start | bytes 3538952 | tf_op jit(solution)/shard_map/ppermute | solution.py:31
  802.2 39.3 %collective-permute-start.49 = (bf16[2,128,2048]{2,1,0:T(8,128)(2,1)}, bf16[2,128,2048]{2,1,0:T(8,128)(2,1)S(1)}, u32[]{:S(2)}, u32[]{:S(2)}) collective-permute-start(bf16[2,128,2048]{2,1,0:T(8,128)(2,1)} %fusion.9), channel_id=1, source_target_pairs={{0,2},{1,3},{2,4},{3,5},{4,6},{5,7},{6,0},{7,1},{8,10},{9,11},{10,... | collective-permute-start | bytes 3145736 | tf_op jit(solution)/shard_map/ppermute | solution.py:31
  806.7 44.7 %collective-permute-start.48 = (bf16[2,128,2048]{2,1,0:T(8,128)(2,1)}, bf16[2,128,2048]{2,1,0:T(8,128)(2,1)S(1)}, u32[]{:S(2)}, u32[]{:S(2)}) collective-permute-start(bf16[2,128,2048]{2,1,0:T(8,128)(2,1)} %add_convert_fusion.5), channel_id=1, source_target_pairs={{0,2},{1,3},{2,4},{3,5},{4,6},{5,7},{6,0},{7,1},{8,10},{9,11},{10,... | collective-permute-start | bytes 3145736 | tf_op jit(solution)/shard_map/ppermute | solution.py:31
  852.5 54.5 %all-to-all-start.3 = ((bf16[8,64,1152]{2,1,0:T(8,128)(2,1)}), bf16[8,64,1152]{2,1,0:T(8,128)(2,1)S(1)}, u32[]{:S(2)}, u32[]{:S(2)}) async-start(bf16[8,64,1152]{2,1,0:T(8,128)(2,1)} %bitcast.200), calls=%async_computation.3 | async-start | bytes 2359296 | tf_op jit(solution)/shard_map/all_to_all | solution.py:894
  859.2 42.3 %collective-permute-start.55 = (bf16[2,128,2048]{2,1,0:T(8,128)(2,1)}, bf16[2,128,2048]{2,1,0:T(8,128)(2,1)S(1)}, u32[]{:S(2)}, u32[]{:S(2)}) collective-permute-start(bf16[2,128,2048]{2,1,0:T(8,128)(2,1)} %add_convert_fusion.4), channel_id=1, source_target_pairs={{0,2},{1,3},{2,4},{3,5},{4,6},{5,7},{6,0},{7,1},{8,10},{9,11},{10,... | collective-permute-start | bytes 3145736 | tf_op jit(solution)/shard_map/ppermute | solution.py:31
  861.2 40.3 %collective-permute-start.56 = (bf16[2,128,2048]{2,1,0:T(8,128)(2,1)}, bf16[2,128,2048]{2,1,0:T(8,128)(2,1)S(1)}, u32[]{:S(2)}, u32[]{:S(2)}) collective-permute-start(bf16[2,128,2048]{2,1,0:T(8,128)(2,1)} %after.135), channel_id=1, source_target_pairs={{0,1},{1,0},{2,3},{3,2},{4,5},{5,4},{6,7},{7,6},{8,9},{9,8},{10,11... | collective-permute-start | bytes 3145736 | tf_op jit(solution)/shard_map/ppermute | solution.py:31
  862.7 34.9 %collective-permute-start.57 = (f32[2,128]{1,0:T(2,128)S(1)}, f32[2,128]{1,0:T(2,128)S(1)}, u32[]{:S(2)}, u32[]{:S(2)}) collective-permute-start(f32[2,128]{1,0:T(2,128)S(1)} %add.375), channel_id=1, source_target_pairs={{0,2},{1,3},{2,0},{3,1},{4,6},{5,7},{6,4},{7,5},{8,10},{9,11},{10,... | collective-permute-start | bytes 3080 | tf_op jit(solution)/shard_map/ppermute | solution.py:866
  913.0 35.0 %collective-permute-start.59 = (bf16[2,128,2048]{2,1,0:T(8,128)(2,1)}, bf16[2,128,2048]{2,1,0:T(8,128)(2,1)S(1)}, u32[]{:S(2)}, u32[]{:S(2)}) collective-permute-start(bf16[2,128,2048]{2,1,0:T(8,128)(2,1)} %add_convert_fusion.3), channel_id=1, source_target_pairs={{0,2},{1,3},{2,4},{3,5},{4,6},{5,7},{6,0},{7,1},{8,10},{9,11},{10,... | collective-permute-start | bytes 3145736 | tf_op jit(solution)/shard_map/ppermute | solution.py:31
  913.0 35.0 %collective-permute-start.58 = (bf16[2,128,2048]{2,1,0:T(8,128)(2,1)}, bf16[2,128,2048]{2,1,0:T(8,128)(2,1)}, u32[]{:S(2)}, u32[]{:S(2)}) collective-permute-start(bf16[2,128,2048]{2,1,0:T(8,128)(2,1)} %after.140), channel_id=1, source_target_pairs={{0,1},{1,0},{2,3},{3,2},{4,5},{5,4},{6,7},{7,6},{8,9},{9,8},{10,11... | collective-permute-start | bytes 3145736 | tf_op jit(solution)/shard_map/ppermute | solution.py:31
  920.6 27.4 %collective-permute-start.60 = (f32[2,128]{1,0:T(2,128)S(1)}, f32[2,128]{1,0:T(2,128)S(1)}, u32[]{:S(2)}, u32[]{:S(2)}) collective-permute-start(f32[2,128]{1,0:T(2,128)S(1)} %add.378), channel_id=1, source_target_pairs={{0,4},{1,5},{2,6},{3,7},{4,0},{5,1},{6,2},{7,3},{8,12},{9,13},{10,... | collective-permute-start | bytes 3080 | tf_op jit(solution)/shard_map/ppermute | solution.py:866
  (130 other events, 1257.2 us)
Sparse Core Ops, SparseCore 0:
  12.1 34.1 all-gather.5
  47.9 58.2 all-gather.7
  107.8 105.9 all-gather.11
  215.2 105.9 all-gather.9
  322.5 105.9 all-gather.13
  514.5 72.3 reduce-scatter.4
  591.0 70.9 reduce-scatter.6
  664.5 126.1 reduce-scatter.8
  793.5 126.1 reduce-scatter.10

commit v12 on v8

--- a/solution.py
+++ b/solution.py
@@ -194,6 +194,7 @@
     tile,
     qkv_ref,
     do_ref,
+    order_ref,
     cos_ref,
     sin_ref,
     seg_row_ref,
@@ -232,7 +233,7 @@
 
     queries, keys = turned(0), turned(1)
     values = qkv_ref[:, 0, :, 2 * HD : 3 * HD].reshape(group, HD)
-    grad_out = do_ref[:, 0, :, :].reshape(group, HD)
+    grad_out = jnp.concatenate([do_ref[order_ref[k], 0] for k in range(blocks)], axis=0)
     seg_row = seg_row_ref[0]
     grad_query = []
     grad_key = jnp.zeros((group, HD), f32)
@@ -290,15 +291,15 @@
     )(qkv, *tables)
 
 
-def attend_back(qkv, grad_out, tables, ties=()):
+def attend_back(qkv, grad_out, order, tables):
     ns, micro, rows, width = qkv.shape
     heads = width // (3 * HD)
     tile, wide, narrow, shared = attention_specs(ns, micro, rows, heads)
     group = ns * rows
     return pl.pallas_call(
-        lambda *refs: attend_back_kernel(tile, *refs[:7], *refs[-2:]),
+        lambda *refs: attend_back_kernel(tile, *refs),
         grid=(micro, heads),
-        in_specs=[wide, narrow] + shared + [pl.BlockSpec(memory_space=pl.ANY)] * len(ties),
+        in_specs=[wide, narrow, pl.BlockSpec(memory_space=pltpu.SMEM)] + shared,
         out_specs=[wide, pl.BlockSpec((1, 2, HD), lambda m, h: (m * heads + h, 0, 0))],
         out_shape=[
             jax.ShapeDtypeStruct((ns, micro, rows, width), bf16),
@@ -307,7 +308,7 @@
         compiler_params=pltpu.CompilerParams(vmem_limit_bytes=40 * 2**20),
         cost_estimate=little,
         name="attend_back",
-    )(qkv, grad_out, *tables, *ties)
+    )(qkv, grad_out, order, *tables)
 
 
 def part_kernel(grad_ref, w_ref, x_ref, inv_ref, *out_refs):
@@ -783,31 +784,28 @@
 
     def mixed_work(h):
         def work(ties):
-            if h == 0:
-                whole_down.append(bank_grad(grad_rows, hidden, ties, pair, local_experts - pair))
-                ties = (whole_down[1],)
             mixed = combined((hidden,), (w_down,), h, True, ties)
             done.setdefault("mixed", []).extend(mixed)
             return mixed[0]
 
         return work
 
-    def gate_work(ties):
-        return keep(whole_gate=bank_grad(taken, grad_gate_act, ties))
+    def down_work(ties):
+        whole_down.append(bank_grad(grad_rows, hidden, ties, pair, local_experts - pair))
+        return whole_down[1]
 
     parts = [v.reshape(micro, rows, D) for v in list(first) + list(second)]
     grad_h_two = ring_scatter(
         parts,
         "seq",
-        (lambda _: second[0], mixed_work(0), mixed_work(1), gate_work),
-        {3: lambda moved: keep(sum_gate=after(done["whole_gate"], *moved))},
+        (lambda _: second[0], down_work, mixed_work(0), mixed_work(1)),
+        {1: lambda moved: keep(sum_down=after(whole_down[1], *moved))},
     ).reshape(tokens, D)
 
     def bank_sum(whole):
         return lax.psum_scatter(whole, "fsdp", scatter_dimension=1, tiled=True).astype(f32)
 
-    grad_down = jnp.concatenate([bank_sum(v) for v in whole_down], axis=0)
-    grad_gate = bank_sum(done["sum_gate"])
+    grad_down = jnp.concatenate([bank_sum(whole_down[0]), bank_sum(done["sum_down"])], axis=0)
 
     grad_gain_two = jnp.sum(grad_h_two * normed_two, axis=0)
     grad_unit = grad_h_two * gain_two
@@ -823,15 +821,14 @@
             jnp.moveaxis(cut, 2, 0), "seq", split_axis=0, concat_axis=0, tiled=True
         )
 
-    whole_up = bank_grad(taken, grad_up_act, (grad_o,))
-    (do_blocks,) = together((whole_up,), to_heads(grad_o))
-    grad_up = bank_sum(after(whole_up, do_blocks))
-    do_heads = reorder(do_blocks, seq_order)
+    whole_gate = bank_grad(taken, grad_gate_act, (grad_o,))
+    (do_blocks,) = together((whole_gate,), to_heads(grad_o))
+    grad_gate = bank_sum(after(whole_gate, do_blocks))
 
     mixed = [v.reshape(micro, rows, D) for v in done["mixed"]]
     k = sizes("seq")[1] + 1 % sizes("seq")[1]
     mixed[k] = after(mixed[k], do_blocks)
-    grad_qkv, grad_head = attend_back(qkv, do_heads, tables)
+    grad_qkv, grad_head = attend_back(qkv, do_blocks, seq_order, tables)
     part_h_one, grad_gain_one = part_grads(grad_qkv, w_first, x_all, inv_all)
     one, columns = together(
         (grad_gain_one,), row_move(mixed, 1, "seq"), to_heads(after(grad_attn, do_blocks))
@@ -870,18 +867,20 @@
     head = head + moved
 
     whole = [after(v, one) for v in whole]
-    owned = ring_scatter(whole, "fsdp").astype(bf16)
+    whole_up = bank_grad(taken, grad_up_act, (one,))
+    owned = ring_scatter(whole, "fsdp", (None, lambda _: whole_up)).astype(bf16)
 
     total = ahead(add(row_sum(two, mixed, 2, "seq"), total).astype(bf16), "seq")
     grad_total = ahead(row_sum(one, part_h_one, 1, "seq"), "seq")
     total, grad_total, three, two, owned = together(
-        (),
+        (whole_up,),
         total,
         grad_total,
         row_move(mixed, 3, "seq"),
         row_move(part_h_one, 2, "seq"),
         owned,
     )
+    grad_up = bank_sum(after(whole_up, owned))
     owned = lax.all_to_all(
         owned.reshape(ns, share, -1), "seq", split_axis=0, concat_axis=0, tiled=True
     )

time: 985 us -> 969 us (0.984)
  waiting for transfers between devices: 287 us -> 268 us
    ppermute x56, waiting for transfers between devices: 269 us -> 250 us  [shift(): return lax.ppermute(value, axis, pairs)]
    unnamed x166 -> x172, local copies, waits for them, and re-layouts: 43.3 us -> 43.3 us
  transfers between devices with their start and end apart: 73 -> 73, of which waited for: 35 -> 33; matrix products, arithmetic and copies ran while one was open for 17% -> 18% of each run, Pallas kernels for 33% -> 34%
where the time goes in v12:
time: 969 us; the launch traced here: 958 us
  Pallas kernels  363 us (37%)
  waiting for transfers between devices  268 us (28%)
  local copies, waits for them, and re-layouts  96.3 us (10%)
  other arithmetic  94 us (10%)
  starting transfers between devices  73.1 us (8%)
  blocking collectives  27.7 us (3%)
  matrix products  21 us (2%)
  between operations  15.5 us (2%)
    pallas_call x13, Pallas kernels, call(): pl.pallas_call(run, grid=grid, in_specs=[spec for _, spec in ins] + [pl.B...  292 us
    ppermute x56, waiting for transfers between devices, shift(): return lax.ppermute(value, axis, pairs)  250 us
    ppermute x56, starting transfers between devices, shift(): return lax.ppermute(value, axis, pairs)  51.1 us
    unnamed x172, local copies, waits for them, and re-layouts  43.3 us
    pallas_call x1, Pallas kernels, attend_back(): pl.pallas_call(lambda *refs: attend_back_kernel(tile, *refs), grid=(micro...  33.9 us
    all_to_all x1, blocking collectives, body(): lax.all_to_all(o_heads, 'seq', split_axis=0, concat_axis=0, tiled=True)  27.7 us
    pallas_call x1, Pallas kernels, proj_grads(): pl.pallas_call(run, grid_spec=pltpu.PrefetchScalarGridSpec(num_scalar_pre...  20.7 us
  transfers between devices with their start and end apart: 73, of which 33 were waited for; matrix products, arithmetic and copies ran while one was open for 18% of the time, Pallas kernels for 34%

profile of v12, /device:TPU:0, one launch (start us, length us, event | category | flops | bytes accessed | tf_op | source)
XLA Modules:
  0.0 958.5 jit_solution(5316361646080862615)
XLA Ops:
  17.9 3.0 collective-permute-start.1
  22.5 25.3 %collective-permute-done.1 = bf16[2,128,2176]{2,1,0:T(8,128)(2,1)S(1)} collective-permute-done((bf16[2,128,2176]{2,1,0:T(8,128)(2,1)}, bf16[2,128,2176]{2,1,0:T(8,128)(2,1)S(1)}, u32[]{:S(2)}, u32[]{:S(2)}) %collective-permute-start.1) | collective-permute-done | bytes 1114144 | tf_op jit(solution)/shard_map/ppermute | solution.py:31
  53.5 3.1 fusion.27
  59.0 16.4 %collective-permute-done.3 = bf16[2,128,2176]{2,1,0:T(8,128)(2,1)} collective-permute-done((bf16[2,128,2176]{2,1,0:T(8,128)(2,1)S(1)}, bf16[2,128,2176]{2,1,0:T(8,128)(2,1)}, u32[]{:S(2)}, u32[]{:S(2)}) %collective-permute-start.3) | collective-permute-done | bytes 1114144 | tf_op jit(solution)/shard_map/ppermute | solution.py:31
  82.1 20.8 %collective-permute-done.5 = bf16[2,128,2176]{2,1,0:T(8,128)(2,1)S(1)} collective-permute-done((bf16[2,128,2176]{2,1,0:T(8,128)(2,1)}, bf16[2,128,2176]{2,1,0:T(8,128)(2,1)S(1)}, u32[]{:S(2)}, u32[]{:S(2)}) %collective-permute-start.5) | collective-permute-done | bytes 1114144 | tf_op jit(solution)/shard_map/ppermute | solution.py:31
  106.4 8.1 collective-permute-done.6
  119.0 6.7 fusion
  127.7 5.3 fusion.2
  133.0 8.0 fusion.4.refs_0_.refs_1_
  148.6 16.5 %attend.1 = bf16[8,2,128,256]{3,2,1,0:T(8,128)(2,1)S(1)} custom-call(bf16[8,2,128,768]{3,2,1,0:T(8,128)(2,1)S(1)} %copy-done.2, f32[1024,128]{1,0:T(8,128)S(1)} %copy-done.8, f32[1024,128]{1,0:T(8,128)S(1)} %copy-done.6, s32[2,1,1024]{2,1,0:T(1,128)S(1)} %bitcast.193, s32[2,1024,1]{2,1,0:T(8,128)S(1)} %copy-done.3, f32[2,128]{1,0:T(2,128)S(1)} %copy-done.13), custom_call_target="tpu_custom_call" | custom-call | flops 1 | bytes 1 | tf_op jit(solution)/shard_map/attend/pallas_call | solution.py:282
  166.0 2.9 gather_fusion.1
  168.9 27.7 %all_to_all.20 = bf16[8,2,128,256]{3,2,1,0:T(8,128)(2,1)S(1)} all-to-all(bf16[8,2,128,256]{3,2,1,0:T(8,128)(2,1)} %after.76), channel_id=1, replica_groups=mesh['fsdp'=4,'seq'=8] {'seq'}, dimensions={0} | all-to-all | bytes 2097152 | tf_op jit(solution)/shard_map/all_to_all | solution.py:701
  198.5 6.5 multiply_reduce_fusion.3
  208.7 21.0 %collective-permute-done.12.refs_0_ = bf16[2,128,2048]{2,1,0:T(8,128)(2,1)} collective-permute-done((bf16[2,128,2048]{2,1,0:T(8,128)(2,1)S(1)}, bf16[2,128,2048]{2,1,0:T(8,128)(2,1)}, u32[]{:S(2)}, u32[]{:S(2)}) %collective-permute-start.12) | collective-permute-done | bytes 1048608 | tf_op jit(solution)/shard_map/ppermute | solution.py:31
  229.6 2.7 collective-permute-done.13.refs_1_.refs_0_
  233.5 20.5 %collective-permute-done.14.refs_0_ = bf16[2,128,2048]{2,1,0:T(8,128)(2,1)} collective-permute-done((bf16[2,128,2048]{2,1,0:T(8,128)(2,1)}, bf16[2,128,2048]{2,1,0:T(8,128)(2,1)}, u32[]{:S(2)}, u32[]{:S(2)}) %collective-permute-start.14) | collective-permute-done | bytes 1048608 | tf_op jit(solution)/shard_map/ppermute | solution.py:31
  254.0 3.0 collective-permute-done.15.refs_1_.refs_0_
  257.6 20.2 %collective-permute-done.16.refs_0_ = bf16[2,128,2048]{2,1,0:T(8,128)(2,1)} collective-permute-done((bf16[2,128,2048]{2,1,0:T(8,128)(2,1)}, bf16[2,128,2048]{2,1,0:T(8,128)(2,1)}, u32[]{:S(2)}, u32[]{:S(2)}) %collective-permute-start.16) | collective-permute-done | bytes 1048608 | tf_op jit(solution)/shard_map/ppermute | solution.py:31
  283.5 8.8 collective-permute-done.18.refs_0_
  292.3 4.7 collective-permute-done.19.refs_1_.refs_0_
  297.0 16.5 %collective-permute-done.20.refs_0_ = bf16[2,128,2048]{2,1,0:T(8,128)(2,1)} collective-permute-done((bf16[2,128,2048]{2,1,0:T(8,128)(2,1)}, bf16[2,128,2048]{2,1,0:T(8,128)(2,1)}, u32[]{:S(2)}, u32[]{:S(2)}) %collective-permute-start.20) | collective-permute-done | bytes 1048608 | tf_op jit(solution)/shard_map/ppermute | solution.py:31
  313.6 4.9 collective-permute-done.21.refs_1_.refs_0_
  329.2 6.3 collective-permute-done.22.refs_1_.refs_0_
  340.8 3.3 slice_add_fusion
  347.1 34.2 %dispatch.3 = (bf16[4,2,384,2048]{3,2,1,0:T(8,128)(2,1)}, f32[4,2,384,1024]{3,2,1,0:T(8,128)}) custom-call(bf16[256,2048]{1,0:T(8,128)(2,1)} %bitcast.205, bf16[256,2048]{1,0:T(8,128)(2,1)} %bitcast.209, bf16[256,2048]{1,0:T(8,128)(2,1)} %bitcast.208, bf16[256,2048]{1,0:T(8,128)(2,1)} %bitcast.37.refs_3_, bf16[256,2048]{1,0:T(8,128)(2,1)} %bitcast.38.refs_4_, ...), custom_call_target="tpu_custom_call" | custom-call | flops 1 | bytes 1 | tf_op jit(solution)/shard_map/dispatch/pallas_call | solution.py:428
  382.1 19.8 %dispatch.4 = (bf16[4,2,384,2048]{3,2,1,0:T(8,128)(2,1)}, f32[4,2,384,1024]{3,2,1,0:T(8,128)}) custom-call(bf16[256,2048]{1,0:T(8,128)(2,1)} %copy-done.40, bf16[256,2048]{1,0:T(8,128)(2,1)} %bitcast.18.refs_1_, bf16[256,2048]{1,0:T(8,128)(2,1)} %bitcast.19.refs_2_, bf16[256,2048]{1,0:T(8,128)(2,1)} %bitcast.20.refs_3_, bf16[256,2048]{1,0:T(8,128)(2,1)} %bitcast.21.refs_4_, ...), custom_call_target="tpu_custom_call" | custom-call | flops 1 | bytes 1 | tf_op jit(solution)/shard_map/dispatch/pallas_call | solution.py:428
  408.0 19.6 %dispatch.5 = (bf16[4,2,384,2048]{3,2,1,0:T(8,128)(2,1)}, f32[4,2,384,1024]{3,2,1,0:T(8,128)}) custom-call(bf16[256,2048]{1,0:T(8,128)(2,1)} %copy-done.40, bf16[256,2048]{1,0:T(8,128)(2,1)} %bitcast.18.refs_1_, bf16[256,2048]{1,0:T(8,128)(2,1)} %bitcast.19.refs_2_, ...), custom_call_target="tpu_custom_call", output_to_operand_aliasing={{0}: (12, {}), {1}: (13, {})} | custom-call | flops 1 | bytes 1 | tf_op jit(solution)/shard_map/dispatch/pallas_call | solution.py:428
  433.3 32.2 %activate.1 = (bf16[4,2,384,1024]{3,2,1,0:T(8,128)(2,1)}, bf16[4,2,384,1024]{3,2,1,0:T(8,128)(2,1)}, bf16[4,2,384,1024]{3,2,1,0:T(8,128)(2,1)}) custom-call(bf16[4,2,384,2048]{3,2,1,0:T(8,128)(2,1)} %get-tuple-element.55.refs_0_.refs_1_, f32[4,2,384,1024]{3,2,1,0:T(8,128)} %get-tuple-element.56.refs_1_, f32[4,2,384,1024]{3,2,1,0:T(8,128)} %get-tuple-element.57.refs_2_, ...), custom_call_target="tpu_custom_call" | custom-call | flops 1 | bytes 1 | tf_op jit(solution)/shard_map/activate/pallas_call | solution.py:428
  470.4 27.7 %combine.4 = (bf16[256,2048]{1,0:T(8,128)(2,1)}, bf16[256,2048]{1,0:T(8,128)(2,1)}, bf16[256,2048]{1,0:T(8,128)(2,1)}, bf16[256,2048]{1,0:T(8,128)(2,1)}) custom-call(bf16[4,2,384,1024]{3,2,1,0:T(8,128)(2,1)} %get-tuple-element.59.refs_0_.refs_1_, bf16[4,2,384,1024]{3,2,1,0:T(8,128)(2,1)} %get-tuple-element.60.refs_1_, ...), custom_call_target="tpu_custom_call" | custom-call | flops 1 | bytes 1 | tf_op jit(solution)/shard_map/combine/pallas_call | solution.py:428
  498.2 12.9 %bank_grad.4.refs_7_ = bf16[2,2048,1024]{2,1,0:T(8,128)(2,1)} custom-call(bf16[4,2,384,2048]{3,2,1,0:T(8,128)(2,1)} %get-tuple-element.52.refs_1_.refs_14_.refs_16_.refs_0_, bf16[4,2,384,1024]{3,2,1,0:T(8,128)(2,1)} %get-tuple-element.58.refs_1_.refs_0_, bf16[256,2048]{1,0:T(8,128)(2,1)} %get-tuple-element.61.refs_2_), custom_call_target="tpu_custom_call" | custom-call | flops 1 | bytes 1 | tf_op jit(solution)/shard_map/bank_grad/pallas_call | solution.py:428
  513.1 28.5 %combine.5 = (bf16[256,2048]{1,0:T(8,128)(2,1)}, bf16[256,2048]{1,0:T(8,128)(2,1)}, bf16[256,2048]{1,0:T(8,128)(2,1)}, bf16[256,2048]{1,0:T(8,128)(2,1)}) custom-call(bf16[4,2,384,1024]{3,2,1,0:T(8,128)(2,1)} %get-tuple-element.59.refs_0_.refs_1_, bf16[4,2,384,1024]{3,2,1,0:T(8,128)(2,1)} %get-tuple-element.60.refs_1_, ...), custom_call_target="tpu_custom_call" | custom-call | flops 1 | bytes 1 | tf_op jit(solution)/shard_map/combine/pallas_call | solution.py:428
  545.4 13.0 %bank_grad.5.refs_1_.refs_0_ = bf16[2,2048,1024]{2,1,0:T(8,128)(2,1)} custom-call(bf16[4,2,384,2048]{3,2,1,0:T(8,128)(2,1)} %get-tuple-element.52.refs_1_.refs_14_.refs_16_.refs_0_, bf16[4,2,384,1024]{3,2,1,0:T(8,128)(2,1)} %get-tuple-element.58.refs_1_.refs_0_, bf16[2,128,2048]{2,1,0:T(8,128)(2,1)} %after.99.refs_2_), custom_call_target="tpu_custom_call" | custom-call | flops 1 | bytes 1 | tf_op jit(solution)/shard_map/bank_grad/pallas_call | solution.py:428
  558.4 3.1 collective-permute-done.32.refs_0_
  561.5 3.6 collective-permute-done.34.refs_2_.refs_0_
  569.8 20.1 %combine.6 = (bf16[256,2048]{1,0:T(8,128)(2,1)}, bf16[256,2048]{1,0:T(8,128)(2,1)}, bf16[256,2048]{1,0:T(8,128)(2,1)}, bf16[256,2048]{1,0:T(8,128)(2,1)}) custom-call(bf16[4,2,384,1024]{3,2,1,0:T(8,128)(2,1)} %get-tuple-element.58.refs_1_.refs_0_, bf16[4,2048,1024]{2,1,0:T(8,128)(2,1)} %all-gather.12.cloned.1.call-done.refs_11_.refs_1_, ...), custom_call_target="tpu_custom_call" | custom-call | flops 1 | bytes 1 | tf_op jit(solution)/shard_map/combine/pallas_call | solution.py:428
  594.1 22.2 %combine.7 = (bf16[256,2048]{1,0:T(8,128)(2,1)}, bf16[256,2048]{1,0:T(8,128)(2,1)}, bf16[256,2048]{1,0:T(8,128)(2,1)}, bf16[256,2048]{1,0:T(8,128)(2,1)}) custom-call(bf16[4,2,384,1024]{3,2,1,0:T(8,128)(2,1)} %get-tuple-element.58.refs_1_.refs_0_, bf16[4,2048,1024]{2,1,0:T(8,128)(2,1)} %all-gather.12.cloned.1.call-done.refs_11_.refs_1_, ...), custom_call_target="tpu_custom_call" | custom-call | flops 1 | bytes 1 | tf_op jit(solution)/shard_map/combine/pallas_call | solution.py:428
  621.7 6.2 convolution_convert_fusion.refs_2_
  629.4 5.6 all-to-all-start.1
  635.1 24.9 %bank_grad.6.refs_1_.refs_0_ = bf16[4,2048,1024]{2,1,0:T(8,128)(2,1)} custom-call(bf16[4,2,384,2048]{3,2,1,0:T(8,128)(2,1)} %get-tuple-element.55.refs_0_.refs_1_, bf16[4,2,384,1024]{3,2,1,0:T(8,128)(2,1)} %get-tuple-element.59.refs_0_.refs_1_, bf16[256,2048]{1,0:T(8,128)(2,1)} %copy-done.50), custom_call_target="tpu_custom_call" | custom-call | flops 1 | bytes 1 | tf_op jit(solution)/shard_map/bank_grad/pallas_call | solution.py:428
  662.8 5.7 all-to-all-start.2
  676.1 33.9 %attend_back.1 = (bf16[8,2,128,768]{3,2,1,0:T(8,128)(2,1)S(1)}, f32[4,2,128]{2,1,0:T(2,128)S(1)}) custom-call(bf16[8,2,128,768]{3,2,1,0:T(8,128)(2,1)S(1)} %copy-done.2, bf16[8,2,128,256]{3,2,1,0:T(8,128)(2,1)} %after.106.refs_1_, s32[8]{0:T(128)S(1)} %get-tuple-element.101.refs_2_.refs_1_, f32[1024,128]{1,0:T(8,128)S(1)} %copy-done.9, ...), custom_call_target="tpu_custom_call" | custom-call | flops 1 | bytes 1 | tf_op jit(solution)/shard_map/attend_back/pallas_call | solution.py:299
  712.2 12.6 %part_grads.1 = (bf16[256,2048]{1,0:T(8,128)(2,1)}, bf16[256,2048]{1,0:T(8,128)(2,1)}, bf16[256,2048]{1,0:T(8,128)(2,1)}, bf16[256,2048]{1,0:T(8,128)(2,1)}, bf1...) custom-call(bf16[2048,768]{1,0:T(8,128)(2,1)} %bitcast.190, ...), custom_call_target="tpu_custom_call" | custom-call | flops 1 | bytes 1 | tf_op jit(solution)/shard_map/part_grads/pallas_call | solution.py:428
  735.0 20.7 %proj_grads.1 = (bf16[512,1152]{1,0:T(8,128)(2,1)}, bf16[512,1152]{1,0:T(8,128)(2,1)}, bf16[512,1152]{1,0:T(8,128)(2,1)}, bf16[512,1152]{1,0:T(8,128)(2,1)}) custom-call(s32[4]{0:T(128)} %fusion.41.refs_0_, s32[8]{0:T(128)} %copy-done.14, bf16[2048,2048]{1,0:T(8,128)(2,1)} %bitcast.201, bf16[2048,768]{1,0:T(8,128)(2,1)} %bitcast.191, ...), custom_call_target="tpu_custom_call" | custom-call | flops 1 | bytes 1 | tf_op jit(solution)/shard_map/proj_grads/pallas_call | solution.py:389
  760.3 2.9 add_convert_fusion.2
  767.3 2.7 add_convert_fusion.6
  771.5 24.1 %bank_grad.7.refs_1_.refs_0_ = bf16[4,2048,1024]{2,1,0:T(8,128)(2,1)} custom-call(bf16[4,2,384,2048]{3,2,1,0:T(8,128)(2,1)} %get-tuple-element.55.refs_0_.refs_1_, bf16[4,2,384,1024]{3,2,1,0:T(8,128)(2,1)} %get-tuple-element.60.refs_1_, bf16[2,128,2048]{2,1,0:T(8,128)(2,1)} %after.115.refs_1_.refs_2_.refs_4_), custom_call_target="tpu_custom_call" | custom-call | flops 1 | bytes 1 | tf_op jit(solution)/shard_map/bank_grad/pallas_call | solution.py:428
  795.6 15.7 %collective-permute-done.47.refs_2_.refs_0_ = bf16[512,1152]{1,0:T(8,128)(2,1)} collective-permute-done((bf16[512,1152]{1,0:T(8,128)(2,1)}, bf16[512,1152]{1,0:T(8,128)(2,1)}, u32[]{:S(2)}, u32[]{:S(2)}) %collective-permute-start.47) | collective-permute-done | bytes 1179680 | tf_op jit(solution)/shard_map/ppermute | solution.py:31
  812.6 3.1 add_convert_fusion.refs_5_.refs_0_
  817.0 5.9 all-to-all-start.3
  825.0 3.7 add_convert_fusion.5
  830.5 8.8 maximum_convert_fusion.refs_1_
  839.2 21.2 %collective-permute-done.53.refs_2_.refs_0_ = bf16[2,128,2048]{2,1,0:T(8,128)(2,1)S(1)} collective-permute-done((bf16[2,128,2048]{2,1,0:T(8,128)(2,1)}, bf16[2,128,2048]{2,1,0:T(8,128)(2,1)S(1)}, u32[]{:S(2)}, u32[]{:S(2)}) %collective-permute-start.53) | collective-permute-done | bytes 1048608 | tf_op jit(solution)/shard_map/ppermute | solution.py:31
  860.5 8.2 collective-permute-done.52.refs_0_
  868.7 5.3 all-to-all-done.3.refs_4_.refs_0_
  875.0 3.2 add_convert_fusion.3
  879.8 2.8 add_convert_fusion.4
  890.1 3.7 reshape.579
  895.8 5.4 fusion.63
  905.8 6.6 convert_element_type.436.refs_1_
  912.5 9.9 %collective-permute-done.58.refs_3_.refs_0_ = f32[2,128]{1,0:T(2,128)S(1)} collective-permute-done((f32[2,128]{1,0:T(2,128)S(1)}, f32[2,128]{1,0:T(2,128)S(1)}, u32[]{:S(2)}, u32[]{:S(2)}) %collective-permute-start.58) | collective-permute-done | bytes 1056 | tf_op jit(solution)/shard_map/ppermute | solution.py:856
  922.4 4.0 collective-permute-done.56.refs_0_
  926.4 2.9 collective-permute-done.55.refs_4_.refs_0_
  941.3 2.9 fusion.19
  944.7 6.8 convert_element_type.465
  (468 shorter events, 184.6 us)
Async XLA Ops:
  7.2 118.6 %all-gather.6.cloned.1.call-start = ((), (), s32[]{:S(2)}) async-start(), calls=%async_computation.8 | async-start | bytes 4587520 | tf_op jit(solution)/shard_map/all_gather | solution.py:648
  12.0 186.5 %all-gather.8.cloned.1.call-start = ((), (), s32[]{:S(2)}) async-start(), calls=%async_computation.9 | async-start | bytes 10485760 | tf_op jit(solution)/shard_map/all_gather | solution.py:648
  12.7 334.3 %all-gather.12.cloned.1.call-start = ((), (), s32[]{:S(2)}) async-start(), calls=%async_computation.11 | async-start | bytes 20971520 | tf_op jit(solution)/shard_map/all_gather | solution.py:648
  13.5 368.7 %all-gather.10.cloned.1.call-start = ((), (), s32[]{:S(2)}) async-start(), calls=%async_computation.10 | async-start | bytes 20971520 | tf_op jit(solution)/shard_map/all_gather | solution.py:648
  14.1 419.2 %all-gather.14.cloned.1.call-start = ((), (), s32[]{:S(2)}) async-start(), calls=%async_computation.12 | async-start | bytes 20971520 | tf_op jit(solution)/shard_map/all_gather | solution.py:648
  14.7 815.8 %reduce-scatter.5.cloned.1.call-start = ((), (), s32[]{:S(2)}) async-start(), calls=%async_computation.13 | async-start | bytes 10485760 | tf_op jit(solution)/shard_map/reduce_scatter | solution.py:806
  17.9 29.8 %collective-permute-start.1 = (bf16[2,128,2176]{2,1,0:T(8,128)(2,1)}, bf16[2,128,2176]{2,1,0:T(8,128)(2,1)S(1)}, u32[]{:S(2)}, u32[]{:S(2)}) collective-permute-start(bf16[2,128,2176]{2,1,0:T(8,128)(2,1)} %get-tuple-element.109), channel_id=1, source_target_pairs={{0,2},{1,3},{2,4},{3,5},{4,6},{5,7},{6,0},{7,1},{8,10},{9,11},{10,... | collective-permute-start | bytes 3342344 | tf_op jit(solution)/shard_map/ppermute | solution.py:31
  20.9 35.6 %collective-permute-start = (bf16[2,128,2176]{2,1,0:T(8,128)(2,1)}, bf16[2,128,2176]{2,1,0:T(8,128)(2,1)}, u32[]{:S(2)}, u32[]{:S(2)}) collective-permute-start(bf16[2,128,2176]{2,1,0:T(8,128)(2,1)} %get-tuple-element.109), channel_id=1, source_target_pairs={{0,1},{1,0},{2,3},{3,2},{4,5},{5,4},{6,7},{7,6},{8,9},{9,8},{10,11... | collective-permute-start | bytes 3342344 | tf_op jit(solution)/shard_map/ppermute | solution.py:31
  47.7 27.7 %collective-permute-start.3 = (bf16[2,128,2176]{2,1,0:T(8,128)(2,1)S(1)}, bf16[2,128,2176]{2,1,0:T(8,128)(2,1)}, u32[]{:S(2)}, u32[]{:S(2)}) collective-permute-start(bf16[2,128,2176]{2,1,0:T(8,128)(2,1)S(1)} %collective-permute-done.1), channel_id=1, source_target_pairs={{0,2},{1,3},{2,4},{3,5},{4,6},{5,7},{6,0},{7,1},{8,10},{9,11},{10,... | collective-permute-start | bytes 3342344 | tf_op jit(solution)/shard_map/ppermute | solution.py:31
  51.9 26.8 %collective-permute-start.2 = (bf16[2,128,2176]{2,1,0:T(8,128)(2,1)S(1)}, bf16[2,128,2176]{2,1,0:T(8,128)(2,1)S(1)}, u32[]{:S(2)}, u32[]{:S(2)}) collective-permute-start(bf16[2,128,2176]{2,1,0:T(8,128)(2,1)S(1)} %collective-permute-done.1), channel_id=1, source_target_pairs={{0,1},{1,0},{2,3},{3,2},{4,5},{5,4},{6,7},{7,6},{8,9},{9,8},{10,11... | collective-permute-start | bytes 3342344 | tf_op jit(solution)/shard_map/ppermute | solution.py:31
  75.4 28.7 %collective-permute-start.4 = (bf16[2,128,2176]{2,1,0:T(8,128)(2,1)}, bf16[2,128,2176]{2,1,0:T(8,128)(2,1)S(1)}, u32[]{:S(2)}, u32[]{:S(2)}) collective-permute-start(bf16[2,128,2176]{2,1,0:T(8,128)(2,1)} %collective-permute-done.3), channel_id=1, source_target_pairs={{0,1},{1,0},{2,3},{3,2},{4,5},{5,4},{6,7},{7,6},{8,9},{9,8},{10,11... | collective-permute-start | bytes 3342344 | tf_op jit(solution)/shard_map/ppermute | solution.py:31
  76.7 26.3 %collective-permute-start.5 = (bf16[2,128,2176]{2,1,0:T(8,128)(2,1)}, bf16[2,128,2176]{2,1,0:T(8,128)(2,1)S(1)}, u32[]{:S(2)}, u32[]{:S(2)}) collective-permute-start(bf16[2,128,2176]{2,1,0:T(8,128)(2,1)} %collective-permute-done.3), channel_id=1, source_target_pairs={{0,2},{1,3},{2,4},{3,5},{4,6},{5,7},{6,0},{7,1},{8,10},{9,11},{10,... | collective-permute-start | bytes 3342344 | tf_op jit(solution)/shard_map/ppermute | solution.py:31
  118.3 23.0 %collective-permute-start.8 = (bf16[2,128,2048]{2,1,0:T(8,128)(2,1)}, bf16[2,128,2048]{2,1,0:T(8,128)(2,1)S(1)}, u32[]{:S(2)}, u32[]{:S(2)}) collective-permute-start(bf16[2,128,2048]{2,1,0:T(8,128)(2,1)} %after.71), channel_id=1, source_target_pairs={{0,2},{1,3},{2,4},{3,5},{4,6},{5,7},{6,0},{7,1},{8,10},{9,11},{10,... | collective-permute-start | bytes 3145736 | tf_op jit(solution)/shard_map/ppermute | solution.py:31
  118.3 23.0 %collective-permute-start.9 = (bf16[2,128,2048]{2,1,0:T(8,128)(2,1)}, bf16[2,128,2048]{2,1,0:T(8,128)(2,1)S(1)}, u32[]{:S(2)}, u32[]{:S(2)}) collective-permute-start(bf16[2,128,2048]{2,1,0:T(8,128)(2,1)} %after.71), channel_id=1, source_target_pairs={{0,1},{1,0},{2,3},{3,2},{4,5},{5,4},{6,7},{7,6},{8,9},{9,8},{10,11... | collective-permute-start | bytes 3145736 | tf_op jit(solution)/shard_map/ppermute | solution.py:31
  143.3 25.6 %collective-permute-start.10 = (bf16[2,128,2048]{2,1,0:T(8,128)(2,1)}, bf16[2,128,2048]{2,1,0:T(8,128)(2,1)}, u32[]{:S(2)}, u32[]{:S(2)}) collective-permute-start(bf16[2,128,2048]{2,1,0:T(8,128)(2,1)} %after.73), channel_id=1, source_target_pairs={{0,2},{1,3},{2,4},{3,5},{4,6},{5,7},{6,0},{7,1},{8,10},{9,11},{10,... | collective-permute-start | bytes 3145736 | tf_op jit(solution)/shard_map/ppermute | solution.py:31
  143.6 25.4 %collective-permute-start.11 = (bf16[2,128,2048]{2,1,0:T(8,128)(2,1)}, bf16[2,128,2048]{2,1,0:T(8,128)(2,1)}, u32[]{:S(2)}, u32[]{:S(2)}) collective-permute-start(bf16[2,128,2048]{2,1,0:T(8,128)(2,1)} %after.73), channel_id=1, source_target_pairs={{0,1},{1,0},{2,3},{3,2},{4,5},{5,4},{6,7},{7,6},{8,9},{9,8},{10,11... | collective-permute-start | bytes 3145736 | tf_op jit(solution)/shard_map/ppermute | solution.py:31
  206.6 23.0 %collective-permute-start.12 = (bf16[2,128,2048]{2,1,0:T(8,128)(2,1)S(1)}, bf16[2,128,2048]{2,1,0:T(8,128)(2,1)}, u32[]{:S(2)}, u32[]{:S(2)}) collective-permute-start(bf16[2,128,2048]{2,1,0:T(8,128)(2,1)S(1)} %bitcast.203), channel_id=1, source_target_pairs={{0,1},{1,0},{2,3},{3,2},{4,5},{5,4},{6,7},{7,6},{8,9},{9,8},{10,11... | collective-permute-start | bytes 3145736 | tf_op jit(solution)/shard_map/ppermute | solution.py:31
  208.1 24.2 %collective-permute-start.13 = (bf16[2,128,2048]{2,1,0:T(8,128)(2,1)S(1)}, bf16[2,128,2048]{2,1,0:T(8,128)(2,1)}, u32[]{:S(2)}, u32[]{:S(2)}) collective-permute-start(bf16[2,128,2048]{2,1,0:T(8,128)(2,1)S(1)} %bitcast.204), channel_id=1, source_target_pairs={{0,2},{1,3},{2,4},{3,5},{4,6},{5,7},{6,0},{7,1},{8,10},{9,11},{10,... | collective-permute-start | bytes 3145736 | tf_op jit(solution)/shard_map/ppermute | solution.py:31
  232.3 21.7 %collective-permute-start.14 = (bf16[2,128,2048]{2,1,0:T(8,128)(2,1)}, bf16[2,128,2048]{2,1,0:T(8,128)(2,1)}, u32[]{:S(2)}, u32[]{:S(2)}) collective-permute-start(bf16[2,128,2048]{2,1,0:T(8,128)(2,1)} %after.78), channel_id=1, source_target_pairs={{0,1},{1,0},{2,3},{3,2},{4,5},{5,4},{6,7},{7,6},{8,9},{9,8},{10,11... | collective-permute-start | bytes 3145736 | tf_op jit(solution)/shard_map/ppermute | solution.py:31
  233.5 23.5 %collective-permute-start.15 = (bf16[2,128,2048]{2,1,0:T(8,128)(2,1)}, bf16[2,128,2048]{2,1,0:T(8,128)(2,1)}, u32[]{:S(2)}, u32[]{:S(2)}) collective-permute-start(bf16[2,128,2048]{2,1,0:T(8,128)(2,1)} %after.78), channel_id=1, source_target_pairs={{0,2},{1,3},{2,4},{3,5},{4,6},{5,7},{6,0},{7,1},{8,10},{9,11},{10,... | collective-permute-start | bytes 3145736 | tf_op jit(solution)/shard_map/ppermute | solution.py:31
  257.0 20.8 %collective-permute-start.16 = (bf16[2,128,2048]{2,1,0:T(8,128)(2,1)}, bf16[2,128,2048]{2,1,0:T(8,128)(2,1)}, u32[]{:S(2)}, u32[]{:S(2)}) collective-permute-start(bf16[2,128,2048]{2,1,0:T(8,128)(2,1)} %after.80), channel_id=1, source_target_pairs={{0,1},{1,0},{2,3},{3,2},{4,5},{5,4},{6,7},{7,6},{8,9},{9,8},{10,11... | collective-permute-start | bytes 3145736 | tf_op jit(solution)/shard_map/ppermute | solution.py:31
  257.6 22.0 %collective-permute-start.17 = (bf16[2,128,2048]{2,1,0:T(8,128)(2,1)}, bf16[2,128,2048]{2,1,0:T(8,128)(2,1)}, u32[]{:S(2)}, u32[]{:S(2)}) collective-permute-start(bf16[2,128,2048]{2,1,0:T(8,128)(2,1)} %after.80), channel_id=1, source_target_pairs={{0,2},{1,3},{2,4},{3,5},{4,6},{5,7},{6,0},{7,1},{8,10},{9,11},{10,... | collective-permute-start | bytes 3145736 | tf_op jit(solution)/shard_map/ppermute | solution.py:31
  297.0 16.6 %collective-permute-start.20 = (bf16[2,128,2048]{2,1,0:T(8,128)(2,1)}, bf16[2,128,2048]{2,1,0:T(8,128)(2,1)}, u32[]{:S(2)}, u32[]{:S(2)}) collective-permute-start(bf16[2,128,2048]{2,1,0:T(8,128)(2,1)} %after.85), channel_id=1, source_target_pairs={{0,1},{1,0},{2,3},{3,2},{4,5},{5,4},{6,7},{7,6},{8,9},{9,8},{10,11... | collective-permute-start | bytes 3145736 | tf_op jit(solution)/shard_map/ppermute | solution.py:31
  297.0 21.4 %collective-permute-start.21 = (bf16[2,128,2048]{2,1,0:T(8,128)(2,1)}, bf16[2,128,2048]{2,1,0:T(8,128)(2,1)}, u32[]{:S(2)}, u32[]{:S(2)}) collective-permute-start(bf16[2,128,2048]{2,1,0:T(8,128)(2,1)} %after.85), channel_id=1, source_target_pairs={{0,2},{1,3},{2,4},{3,5},{4,6},{5,7},{6,0},{7,1},{8,10},{9,11},{10,... | collective-permute-start | bytes 3145736 | tf_op jit(solution)/shard_map/ppermute | solution.py:31
  320.3 15.1 %collective-permute-start.22 = (bf16[1,128,2048]{2,1,0:T(8,128)(2,1)}, bf16[1,128,2048]{2,1,0:T(8,128)(2,1)}, u32[]{:S(2)}, u32[]{:S(2)}) collective-permute-start(bf16[1,128,2048]{2,1,0:T(8,128)(2,1)} %slice.112), channel_id=1, source_target_pairs={{0,2},{1,3},{2,4},{3,5},{4,6},{5,7},{6,0},{7,1},{8,10},{9,11},{10,... | collective-permute-start | bytes 1572872 | tf_op jit(solution)/shard_map/ppermute | solution.py:31
  337.3 44.0 %collective-permute-start.24 = (bf16[2048,256]{1,0:T(8,128)(2,1)}, bf16[2048,256]{1,0:T(8,128)(2,1)}, u32[]{:S(2)}, u32[]{:S(2)}) collective-permute-start(bf16[2048,256]{1,0:T(8,128)(2,1)} %after.90.refs_6_), channel_id=1, source_target_pairs={{0,1},{1,0},{2,3},{3,2},{4,5},{5,4},{6,7},{7,6},{8,9},{9,8},{10,11... | collective-permute-start | bytes 3145736 | tf_op jit(solution)/shard_map/ppermute | solution.py:31
  339.5 41.8 %collective-permute-start.25 = (bf16[2048,256]{1,0:T(8,128)(2,1)}, bf16[2048,256]{1,0:T(8,128)(2,1)}, u32[]{:S(2)}, u32[]{:S(2)}) collective-permute-start(bf16[2048,256]{1,0:T(8,128)(2,1)} %after.90.refs_6_), channel_id=1, source_target_pairs={{0,2},{1,3},{2,4},{3,5},{4,6},{5,7},{6,0},{7,1},{8,10},{9,11},{10,... | collective-permute-start | bytes 3145736 | tf_op jit(solution)/shard_map/ppermute | solution.py:31
  381.3 21.0 %collective-permute-start.26 = (bf16[2048,256]{1,0:T(8,128)(2,1)}, bf16[2048,256]{1,0:T(8,128)(2,1)}, u32[]{:S(2)}, u32[]{:S(2)}) collective-permute-start(bf16[2048,256]{1,0:T(8,128)(2,1)} %after.92.refs_13_.refs_8_), channel_id=1, source_target_pairs={{0,1},{1,0},{2,3},{3,2},{4,5},{5,4},{6,7},{7,6},{8,9},{9,8},{10,11... | collective-permute-start | bytes 3145736 | tf_op jit(solution)/shard_map/ppermute | solution.py:31
  381.5 22.7 %collective-permute-start.27 = (bf16[2048,256]{1,0:T(8,128)(2,1)}, bf16[2048,256]{1,0:T(8,128)(2,1)}, u32[]{:S(2)}, u32[]{:S(2)}) collective-permute-start(bf16[2048,256]{1,0:T(8,128)(2,1)} %after.92.refs_13_.refs_8_), channel_id=1, source_target_pairs={{0,2},{1,3},{2,4},{3,5},{4,6},{5,7},{6,0},{7,1},{8,10},{9,11},{10,... | collective-permute-start | bytes 3145736 | tf_op jit(solution)/shard_map/ppermute | solution.py:31
  404.1 23.5 %collective-permute-start.29 = (bf16[2048,256]{1,0:T(8,128)(2,1)}, bf16[2048,256]{1,0:T(8,128)(2,1)}, u32[]{:S(2)}, u32[]{:S(2)}) collective-permute-start(bf16[2048,256]{1,0:T(8,128)(2,1)} %after.94.refs_15_.refs_10_), channel_id=1, source_target_pairs={{0,1},{1,0},{2,3},{3,2},{4,5},{5,4},{6,7},{7,6},{8,9},{9,8},{10,11... | collective-permute-start | bytes 3145736 | tf_op jit(solution)/shard_map/ppermute | solution.py:31
  406.3 22.7 %collective-permute-start.28 = (bf16[2048,256]{1,0:T(8,128)(2,1)}, bf16[2048,256]{1,0:T(8,128)(2,1)}, u32[]{:S(2)}, u32[]{:S(2)}) collective-permute-start(bf16[2048,256]{1,0:T(8,128)(2,1)} %after.94.refs_15_.refs_10_), channel_id=1, source_target_pairs={{0,2},{1,3},{2,4},{3,5},{4,6},{5,7},{6,0},{7,1},{8,10},{9,11},{10,... | collective-permute-start | bytes 3145736 | tf_op jit(solution)/shard_map/ppermute | solution.py:31
  430.9 34.7 %collective-permute-start.31 = (bf16[1024,256]{1,0:T(8,128)(2,1)}, bf16[1024,256]{1,0:T(8,128)(2,1)}, u32[]{:S(2)}, u32[]{:S(2)}) collective-permute-start(bf16[1024,256]{1,0:T(8,128)(2,1)} %slice.115), channel_id=1, source_target_pairs={{0,2},{1,3},{2,4},{3,5},{4,6},{5,7},{6,0},{7,1},{8,10},{9,11},{10,... | collective-permute-start | bytes 1572872 | tf_op jit(solution)/shard_map/ppermute | solution.py:31
  433.0 32.5 %collective-permute-start.30 = (bf16[1024,256]{1,0:T(8,128)(2,1)}, bf16[1024,256]{1,0:T(8,128)(2,1)}, u32[]{:S(2)}, u32[]{:S(2)}) collective-permute-start(bf16[1024,256]{1,0:T(8,128)(2,1)} %slice.114), channel_id=1, source_target_pairs={{0,1},{1,0},{2,3},{3,2},{4,5},{5,4},{6,7},{7,6},{8,9},{9,8},{10,11... | collective-permute-start | bytes 1572872 | tf_op jit(solution)/shard_map/ppermute | solution.py:31
  511.1 319.4 %reduce-scatter.7.cloned.1.call-start = ((), (), s32[]{:S(2)}) async-start(), calls=%async_computation.14 | async-start | bytes 10485760 | tf_op jit(solution)/shard_map/reduce_scatter | solution.py:806
  511.3 30.2 %collective-permute-start.33 = (bf16[2,128,2048]{2,1,0:T(8,128)(2,1)}, bf16[2,128,2048]{2,1,0:T(8,128)(2,1)}, u32[]{:S(2)}, u32[]{:S(2)}) collective-permute-start(bf16[2,128,2048]{2,1,0:T(8,128)(2,1)} %bitcast.264), channel_id=1, source_target_pairs={{0,1},{1,0},{2,3},{3,2},{4,5},{5,4},{6,7},{7,6},{8,9},{9,8},{10,11... | collective-permute-start | bytes 3145736 | tf_op jit(solution)/shard_map/ppermute | solution.py:31
  541.6 20.0 %collective-permute-start.32 = (bf16[2,128,2048]{2,1,0:T(8,128)(2,1)}, bf16[2,128,2048]{2,1,0:T(8,128)(2,1)}, u32[]{:S(2)}, u32[]{:S(2)}) collective-permute-start(bf16[2,128,2048]{2,1,0:T(8,128)(2,1)} %bitcast.265), channel_id=1, source_target_pairs={{0,1},{1,0},{2,3},{3,2},{4,5},{5,4},{6,7},{7,6},{8,9},{9,8},{10,11... | collective-permute-start | bytes 3145736 | tf_op jit(solution)/shard_map/ppermute | solution.py:31
  543.5 21.6 %collective-permute-start.34 = (bf16[2,128,2048]{2,1,0:T(8,128)(2,1)S(1)}, bf16[2,128,2048]{2,1,0:T(8,128)(2,1)}, u32[]{:S(2)}, u32[]{:S(2)}) collective-permute-start(bf16[2,128,2048]{2,1,0:T(8,128)(2,1)S(1)} %fusion.16), channel_id=1, source_target_pairs={{0,2},{1,3},{2,4},{3,5},{4,6},{5,7},{6,0},{7,1},{8,10},{9,11},{10,... | collective-permute-start | bytes 3145736 | tf_op jit(solution)/shard_map/ppermute | solution.py:31
  565.2 24.7 %collective-permute-start.36 = (bf16[2,128,2048]{2,1,0:T(8,128)(2,1)}, bf16[2,128,2048]{2,1,0:T(8,128)(2,1)}, u32[]{:S(2)}, u32[]{:S(2)}) collective-permute-start(bf16[2,128,2048]{2,1,0:T(8,128)(2,1)} %bitcast.263), channel_id=1, source_target_pairs={{0,1},{1,0},{2,3},{3,2},{4,5},{5,4},{6,7},{7,6},{8,9},{9,8},{10,11... | collective-permute-start | bytes 3145736 | tf_op jit(solution)/shard_map/ppermute | solution.py:31
  569.4 20.5 %collective-permute-start.37 = (bf16[2,128,2048]{2,1,0:T(8,128)(2,1)S(1)}, bf16[2,128,2048]{2,1,0:T(8,128)(2,1)}, u32[]{:S(2)}, u32[]{:S(2)}) collective-permute-start(bf16[2,128,2048]{2,1,0:T(8,128)(2,1)S(1)} %add_convert_fusion.8), channel_id=1, source_target_pairs={{0,2},{1,3},{2,4},{3,5},{4,6},{5,7},{6,0},{7,1},{8,10},{9,11},{10,... | collective-permute-start | bytes 3145736 | tf_op jit(solution)/shard_map/ppermute | solution.py:31
  590.0 26.4 %collective-permute-start.35 = (bf16[2,128,2048]{2,1,0:T(8,128)(2,1)}, bf16[2,128,2048]{2,1,0:T(8,128)(2,1)}, u32[]{:S(2)}, u32[]{:S(2)}) collective-permute-start(bf16[2,128,2048]{2,1,0:T(8,128)(2,1)} %bitcast.262), channel_id=1, source_target_pairs={{0,1},{1,0},{2,3},{3,2},{4,5},{5,4},{6,7},{7,6},{8,9},{9,8},{10,11... | collective-permute-start | bytes 3145736 | tf_op jit(solution)/shard_map/ppermute | solution.py:31
  592.6 23.7 %collective-permute-start.38 = (bf16[2,128,2048]{2,1,0:T(8,128)(2,1)S(1)}, bf16[2,128,2048]{2,1,0:T(8,128)(2,1)}, u32[]{:S(2)}, u32[]{:S(2)}) collective-permute-start(bf16[2,128,2048]{2,1,0:T(8,128)(2,1)S(1)} %add_convert_fusion.7), channel_id=1, source_target_pairs={{0,2},{1,3},{2,4},{3,5},{4,6},{5,7},{6,0},{7,1},{8,10},{9,11},{10,... | collective-permute-start | bytes 3145736 | tf_op jit(solution)/shard_map/ppermute | solution.py:31
  629.4 30.6 %all-to-all-start.1 = ((bf16[8,2,128,256]{3,2,1,0:T(8,128)(2,1)}), bf16[8,2,128,256]{3,2,1,0:T(8,128)(2,1)}, u32[]{:S(2)}, u32[]{:S(2)}) async-start(bf16[8,2,128,256]{3,2,1,0:T(8,128)(2,1)} %bitcast.217), calls=%async_computation.1 | async-start | bytes 2097152 | tf_op jit(solution)/shard_map/all_to_all | solution.py:820
  635.0 270.8 %reduce-scatter.9.cloned.1.call-start = ((), (), s32[]{:S(2)}) async-start(), calls=%async_computation.15 | async-start | bytes 20971520 | tf_op jit(solution)/shard_map/reduce_scatter | solution.py:806
  662.8 62.1 %all-to-all-start.2 = ((bf16[8,2,128,256]{3,2,1,0:T(8,128)(2,1)}), bf16[8,2,128,256]{3,2,1,0:T(8,128)(2,1)}, u32[]{:S(2)}, u32[]{:S(2)}) async-start(bf16[8,2,128,256]{3,2,1,0:T(8,128)(2,1)} %bitcast.216), calls=%async_computation.2 | async-start | bytes 2097152 | tf_op jit(solution)/shard_map/all_to_all | solution.py:820
  668.5 276.3 %reduce-scatter.11.cloned.1.call-start = ((), (), s32[]{:S(2)}) async-start(), calls=%async_computation.16 | async-start | bytes 20971520 | tf_op jit(solution)/shard_map/reduce_scatter | solution.py:806
  668.7 56.2 %collective-permute-start.39 = (bf16[2,128,2048]{2,1,0:T(8,128)(2,1)}, bf16[2,128,2048]{2,1,0:T(8,128)(2,1)}, u32[]{:S(2)}, u32[]{:S(2)}) collective-permute-start(bf16[2,128,2048]{2,1,0:T(8,128)(2,1)} %after.108), channel_id=1, source_target_pairs={{0,1},{1,0},{2,3},{3,2},{4,5},{5,4},{6,7},{7,6},{8,9},{9,8},{10,11... | collective-permute-start | bytes 3145736 | tf_op jit(solution)/shard_map/ppermute | solution.py:31
  672.1 83.6 %collective-permute-start.42 = (bf16[2,128,2048]{2,1,0:T(8,128)(2,1)}, bf16[2,128,2048]{2,1,0:T(8,128)(2,1)}, u32[]{:S(2)}, u32[]{:S(2)}) collective-permute-start(bf16[2,128,2048]{2,1,0:T(8,128)(2,1)} %bitcast.261), channel_id=1, source_target_pairs={{0,1},{1,0},{2,3},{3,2},{4,5},{5,4},{6,7},{7,6},{8,9},{9,8},{10,11... | collective-permute-start | bytes 3145736 | tf_op jit(solution)/shard_map/ppermute | solution.py:31
  724.9 30.8 %collective-permute-start.40 = (bf16[2,128,2048]{2,1,0:T(8,128)(2,1)}, bf16[2,128,2048]{2,1,0:T(8,128)(2,1)S(1)}, u32[]{:S(2)}, u32[]{:S(2)}) collective-permute-start(bf16[2,128,2048]{2,1,0:T(8,128)(2,1)} %after.111), channel_id=1, source_target_pairs={{0,1},{1,0},{2,3},{3,2},{4,5},{5,4},{6,7},{7,6},{8,9},{9,8},{10,11... | collective-permute-start | bytes 3145736 | tf_op jit(solution)/shard_map/ppermute | solution.py:31
  729.4 26.4 %collective-permute-start.41 = (bf16[2,128,2048]{2,1,0:T(8,128)(2,1)}, bf16[2,128,2048]{2,1,0:T(8,128)(2,1)S(1)}, u32[]{:S(2)}, u32[]{:S(2)}) collective-permute-start(bf16[2,128,2048]{2,1,0:T(8,128)(2,1)} %fusion.12), channel_id=1, source_target_pairs={{0,2},{1,3},{2,4},{3,5},{4,6},{5,7},{6,0},{7,1},{8,10},{9,11},{10,... | collective-permute-start | bytes 3145736 | tf_op jit(solution)/shard_map/ppermute | solution.py:31
  732.9 22.8 %collective-permute-start.44 = (f32[2,128]{1,0:T(2,128)S(1)}, f32[2,128]{1,0:T(2,128)S(1)}, u32[]{:S(2)}, u32[]{:S(2)}) collective-permute-start(f32[2,128]{1,0:T(2,128)S(1)} %add.359), channel_id=1, source_target_pairs={{0,16},{8,24},{16,0},{24,8},{1,17},{9,25},{17,1},{25,9},{2,18},{10... | collective-permute-start | bytes 3080 | tf_op jit(solution)/shard_map/ppermute | solution.py:856
  757.1 58.6 %collective-permute-start.50 = (bf16[2,128,2048]{2,1,0:T(8,128)(2,1)}, bf16[2,128,2048]{2,1,0:T(8,128)(2,1)S(1)}, u32[]{:S(2)}, u32[]{:S(2)}) collective-permute-start(bf16[2,128,2048]{2,1,0:T(8,128)(2,1)} %bitcast.72), channel_id=1, source_target_pairs={{0,1},{1,0},{2,3},{3,2},{4,5},{5,4},{6,7},{7,6},{8,9},{9,8},{10,11... | collective-permute-start | bytes 3145736 | tf_op jit(solution)/shard_map/ppermute | solution.py:31
  758.3 57.3 %collective-permute-start.51 = (bf16[2,128,2048]{2,1,0:T(8,128)(2,1)}, bf16[2,128,2048]{2,1,0:T(8,128)(2,1)S(1)}, u32[]{:S(2)}, u32[]{:S(2)}) collective-permute-start(bf16[2,128,2048]{2,1,0:T(8,128)(2,1)} %bitcast.73), channel_id=1, source_target_pairs={{0,1},{1,0},{2,3},{3,2},{4,5},{5,4},{6,7},{7,6},{8,9},{9,8},{10,11... | collective-permute-start | bytes 3145736 | tf_op jit(solution)/shard_map/ppermute | solution.py:31
  763.2 48.1 %collective-permute-start.47 = (bf16[512,1152]{1,0:T(8,128)(2,1)}, bf16[512,1152]{1,0:T(8,128)(2,1)}, u32[]{:S(2)}, u32[]{:S(2)}) collective-permute-start(bf16[512,1152]{1,0:T(8,128)(2,1)} %add_convert_fusion.2), channel_id=1, source_target_pairs={{0,16},{8,24},{16,0},{24,8},{1,17},{9,25},{17,1},{25,9},{2,18},{10... | collective-permute-start | bytes 3538952 | tf_op jit(solution)/shard_map/ppermute | solution.py:31
  765.7 50.0 %collective-permute-start.49 = (bf16[2,128,2048]{2,1,0:T(8,128)(2,1)}, bf16[2,128,2048]{2,1,0:T(8,128)(2,1)}, u32[]{:S(2)}, u32[]{:S(2)}) collective-permute-start(bf16[2,128,2048]{2,1,0:T(8,128)(2,1)} %fusion.10), channel_id=1, source_target_pairs={{0,2},{1,3},{2,4},{3,5},{4,6},{5,7},{6,0},{7,1},{8,10},{9,11},{10,... | collective-permute-start | bytes 3145736 | tf_op jit(solution)/shard_map/ppermute | solution.py:31
  770.0 45.7 %collective-permute-start.48 = (bf16[2,128,2048]{2,1,0:T(8,128)(2,1)}, bf16[2,128,2048]{2,1,0:T(8,128)(2,1)}, u32[]{:S(2)}, u32[]{:S(2)}) collective-permute-start(bf16[2,128,2048]{2,1,0:T(8,128)(2,1)} %add_convert_fusion.6), channel_id=1, source_target_pairs={{0,2},{1,3},{2,4},{3,5},{4,6},{5,7},{6,0},{7,1},{8,10},{9,11},{10,... | collective-permute-start | bytes 3145736 | tf_op jit(solution)/shard_map/ppermute | solution.py:31
  817.0 56.9 %all-to-all-start.3 = ((bf16[8,64,1152]{2,1,0:T(8,128)(2,1)}), bf16[8,64,1152]{2,1,0:T(8,128)(2,1)S(1)}, u32[]{:S(2)}, u32[]{:S(2)}) async-start(bf16[8,64,1152]{2,1,0:T(8,128)(2,1)} %bitcast.74), calls=%async_computation.3 | async-start | bytes 2359296 | tf_op jit(solution)/shard_map/all_to_all | solution.py:884
  822.9 37.5 %collective-permute-start.53 = (bf16[2,128,2048]{2,1,0:T(8,128)(2,1)}, bf16[2,128,2048]{2,1,0:T(8,128)(2,1)S(1)}, u32[]{:S(2)}, u32[]{:S(2)}) collective-permute-start(bf16[2,128,2048]{2,1,0:T(8,128)(2,1)} %bitcast.260), channel_id=1, source_target_pairs={{0,1},{1,0},{2,3},{3,2},{4,5},{5,4},{6,7},{7,6},{8,9},{9,8},{10,11... | collective-permute-start | bytes 3145736 | tf_op jit(solution)/shard_map/ppermute | solution.py:31
  828.7 40.0 %collective-permute-start.52 = (bf16[2,128,2048]{2,1,0:T(8,128)(2,1)}, bf16[2,128,2048]{2,1,0:T(8,128)(2,1)}, u32[]{:S(2)}, u32[]{:S(2)}) collective-permute-start(bf16[2,128,2048]{2,1,0:T(8,128)(2,1)} %add_convert_fusion.5), channel_id=1, source_target_pairs={{0,2},{1,3},{2,4},{3,5},{4,6},{5,7},{6,0},{7,1},{8,10},{9,11},{10,... | collective-permute-start | bytes 3145736 | tf_op jit(solution)/shard_map/ppermute | solution.py:31
  830.1 30.4 %collective-permute-start.54 = (f32[2,128]{1,0:T(2,128)S(1)}, f32[2,128]{1,0:T(2,128)S(1)}, u32[]{:S(2)}, u32[]{:S(2)}) collective-permute-start(f32[2,128]{1,0:T(2,128)S(1)} %add.368), channel_id=1, source_target_pairs={{0,1},{1,0},{2,3},{3,2},{4,5},{5,4},{6,7},{7,6},{8,9},{9,8},{10,11... | collective-permute-start | bytes 3080 | tf_op jit(solution)/shard_map/ppermute | solution.py:856
  878.2 34.3 %collective-permute-start.59 = (bf16[2,128,2048]{2,1,0:T(8,128)(2,1)}, bf16[2,128,2048]{2,1,0:T(8,128)(2,1)S(1)}, u32[]{:S(2)}, u32[]{:S(2)}) collective-permute-start(bf16[2,128,2048]{2,1,0:T(8,128)(2,1)} %add_convert_fusion.3), channel_id=1, source_target_pairs={{0,2},{1,3},{2,4},{3,5},{4,6},{5,7},{6,0},{7,1},{8,10},{9,11},{10,... | collective-permute-start | bytes 3145736 | tf_op jit(solution)/shard_map/ppermute | solution.py:31
  882.6 43.8 %collective-permute-start.56 = (bf16[2,128,2048]{2,1,0:T(8,128)(2,1)}, bf16[2,128,2048]{2,1,0:T(8,128)(2,1)}, u32[]{:S(2)}, u32[]{:S(2)}) collective-permute-start(bf16[2,128,2048]{2,1,0:T(8,128)(2,1)} %add_convert_fusion.4), channel_id=1, source_target_pairs={{0,2},{1,3},{2,4},{3,5},{4,6},{5,7},{6,0},{7,1},{8,10},{9,11},{10,... | collective-permute-start | bytes 3145736 | tf_op jit(solution)/shard_map/ppermute | solution.py:31
  882.6 43.8 %collective-permute-start.57 = (bf16[2,128,2048]{2,1,0:T(8,128)(2,1)}, bf16[2,128,2048]{2,1,0:T(8,128)(2,1)}, u32[]{:S(2)}, u32[]{:S(2)}) collective-permute-start(bf16[2,128,2048]{2,1,0:T(8,128)(2,1)} %after.135), channel_id=1, source_target_pairs={{0,1},{1,0},{2,3},{3,2},{4,5},{5,4},{6,7},{7,6},{8,9},{9,8},{10,11... | collective-permute-start | bytes 3145736 | tf_op jit(solution)/shard_map/ppermute | solution.py:31
  884.0 45.4 %collective-permute-start.55 = (bf16[2,128,2048]{2,1,0:T(8,128)(2,1)}, bf16[2,128,2048]{2,1,0:T(8,128)(2,1)S(1)}, u32[]{:S(2)}, u32[]{:S(2)}) collective-permute-start(bf16[2,128,2048]{2,1,0:T(8,128)(2,1)} %after.133), channel_id=1, source_target_pairs={{0,1},{1,0},{2,3},{3,2},{4,5},{5,4},{6,7},{7,6},{8,9},{9,8},{10,11... | collective-permute-start | bytes 3145736 | tf_op jit(solution)/shard_map/ppermute | solution.py:31
  889.0 33.4 %collective-permute-start.58 = (f32[2,128]{1,0:T(2,128)S(1)}, f32[2,128]{1,0:T(2,128)S(1)}, u32[]{:S(2)}, u32[]{:S(2)}) collective-permute-start(f32[2,128]{1,0:T(2,128)S(1)} %add.371), channel_id=1, source_target_pairs={{0,2},{1,3},{2,0},{3,1},{4,6},{5,7},{6,4},{7,5},{8,10},{9,11},{10,... | collective-permute-start | bytes 3080 | tf_op jit(solution)/shard_map/ppermute | solution.py:856
  (87 other events, 1163.5 us)
Sparse Core Ops, SparseCore 0:
  12.1 34.1 all-gather.5
  47.9 58.2 all-gather.7
  107.8 105.9 all-gather.11
  215.2 105.9 all-gather.9
  322.5 105.9 all-gather.13
  511.2 72.2 reduce-scatter.4
  586.8 71.6 reduce-scatter.6
  661.2 145.9 reduce-scatter.8
  817.1 126.1 reduce-scatter.10
